TPU v7x, 32 devices: a whole 2x2x4 slice. The times are simulated.
32 devices in a mesh: dp: 16 (over z, y, core), tensor: 2 (over x).
Axes of the slice: x: 2, y: 2, z: 4, core: 2. Of those that a mesh axis runs over, the one named last changes fastest.
Arguments:
- inputs: bfloat16 [256, 64, 512], P(('dp', 'tensor')), may hold values from -6 to 6
- cotangent: bfloat16 [256, 64, 512], P(('dp', 'tensor')), may hold values from -6 to 6
- attention_mask: int32 [256, 64], P(('dp', 'tensor')), may hold values from 0 to 1, as said below
- patch_valid: int32 [256, 64], P(('dp', 'tensor')), may hold values 0 or 1
- buckets: int32 [64, 64], replicated, may hold values from 0 to 31
- mask_embed: float32 [512], replicated, may hold values from -6 to 6
- w_query: bfloat16 [2, 512, 384], P(None, ('dp', 'tensor')), may hold values from -0.125 to 0.125
- w_key: bfloat16 [2, 512, 384], P(None, ('dp', 'tensor')), may hold values from -0.125 to 0.125
- w_value: bfloat16 [2, 512, 384], P(None, ('dp', 'tensor')), may hold values from -0.25 to 0.25
- w_output: bfloat16 [2, 384, 512], P(None, None, ('dp', 'tensor')), may hold values from -0.875 to 0.875
- w_gate: bfloat16 [2, 512, 1024], P(None, None, 'tensor'), may hold values from -0.25 to 0.25
- w_up: bfloat16 [2, 512, 1024], P(None, None, 'tensor'), may hold values from -0.25 to 0.25
- w_down: bfloat16 [2, 1024, 512], P(None, 'tensor'), may hold values from -0.25 to 0.25
- gain_attn: float32 [2, 512], replicated, may hold values from 0.5 to 1.5
- gain_ff: float32 [2, 512], replicated, may hold values from 0.5 to 1.5
- bias_table: float32 [32, 6], replicated, may hold values from -6 to 6
Outputs:
- outputs: bfloat16 [256, 64, 512], P(('dp', 'tensor'))
- grad_inputs: float32 [256, 64, 512], P(('dp', 'tensor'))
- grad_query: float32 [2, 512, 384], P(None, ('dp', 'tensor'))
- grad_key: float32 [2, 512, 384], P(None, ('dp', 'tensor'))
- grad_value: float32 [2, 512, 384], P(None, ('dp', 'tensor'))
- grad_output: float32 [2, 384, 512], P(None, None, ('dp', 'tensor'))
- grad_gate: float32 [2, 512, 1024], P(None, None, 'tensor')
- grad_up: float32 [2, 512, 1024], P(None, None, 'tensor')
- grad_down: float32 [2, 1024, 512], P(None, 'tensor')
- grad_gain_attn: float32 [2, 512], replicated
- grad_gain_ff: float32 [2, 512], replicated
- grad_bias_table: float32 [32, 6], replicated
- grad_mask_embed: float32 [512], replicated
Inputs may be any that keep to these rules, and one draw needn't show every extreme that they name: In each series the ones of attention_mask are the last of its 64 slots, one or more of them.
All inputs are finite; a program needn't handle non-finite values. No bound on the sum of `patch_valid` on one device may be relied on, other than what follows from the above.
Results may differ from a plain program's by a relative error of at most 0.03.
The roundings to bfloat16 on the way count: a program that leaves them out, or rounds other values in their place, can miss the bound.
Values may be sent and summed in bfloat16 or wider, within the bound.
No kernel may reach another device: no remote copies, remote signals or barrier semaphores. Data moves between devices by JAX's collectives and lax.ppermute only.
A program may use at most 128 MiB of HBM per device.

v0:
```python
import jax
import jax.numpy as jnp
from jax import lax
from jax.sharding import PartitionSpec as P

norm_eps = 1e-06
masked_score = -1e30
precise = lax.Precision.HIGHEST


def rms_norm(values, gain):
    return values * lax.rsqrt(jnp.mean(values * values, axis=-1, keepdims=True) + norm_eps) * gain


def gelu_mix(gate_act, up_act):
    inner = 0.7978845608028654 * (gate_act + 0.044715 * gate_act * gate_act * gate_act)
    return 0.5 * gate_act * (1.0 + jnp.tanh(inner)) * up_act


def product(left, right):
    return jnp.dot(left, right, preferred_element_type=jnp.float32)


def block_scores(query_rows, key_rows, key_mask, score_bias):
    scores = (
        jnp.einsum("bqhe,bkhe->bhqk", query_rows, key_rows, preferred_element_type=jnp.float32)
        + score_bias[None]
    )
    return jnp.where(key_mask[:, None, None, :] == 1, scores, masked_score)


def attend_block(pieces, score_bias):
    query_rows, key_rows, value_rows, key_mask = pieces
    scores = block_scores(query_rows, key_rows, key_mask, score_bias)
    row_max = jnp.max(scores, axis=-1, keepdims=True)
    exp_scores = jnp.exp(scores - row_max)
    row_sum = jnp.sum(exp_scores, axis=-1, keepdims=True)
    probs = exp_scores / row_sum
    attended = jnp.einsum(
        "bhqk,bkhe->bqhe",
        probs.astype(jnp.bfloat16),
        value_rows,
        preferred_element_type=jnp.float32,
    )
    return (attended.astype(jnp.bfloat16), row_max + jnp.log(row_sum))


def attend_back(pieces, score_bias):
    query_rows, key_rows, value_rows, key_mask, log_total, grad_out = pieces
    scores = block_scores(query_rows, key_rows, key_mask, score_bias)
    probs = jnp.exp(scores - log_total)
    grad_probs = jnp.einsum(
        "bqhe,bkhe->bhqk", grad_out, value_rows, preferred_element_type=jnp.float32
    )
    inner = jnp.sum(probs * grad_probs, axis=-1, keepdims=True)
    grad_scores = (probs * (grad_probs - inner)).astype(jnp.bfloat16)
    grad_query = jnp.einsum(
        "bhqk,bkhe->bqhe", grad_scores, key_rows, preferred_element_type=jnp.float32
    )
    grad_key = jnp.einsum(
        "bhqk,bqhe->bkhe", grad_scores, query_rows, preferred_element_type=jnp.float32
    )
    grad_value = jnp.einsum(
        "bhqk,bqhe->bkhe", probs.astype(jnp.bfloat16), grad_out, preferred_element_type=jnp.float32
    )
    grad_bias = jnp.sum(grad_scores.astype(jnp.float32), axis=0)
    return (
        grad_query.astype(jnp.bfloat16),
        grad_key.astype(jnp.bfloat16),
        grad_value.astype(jnp.bfloat16),
        grad_bias,
    )


def on_device(
    inputs,
    cotangent,
    attention_mask,
    patch_valid,
    buckets,
    mask_embed,
    w_query,
    w_key,
    w_value,
    w_output,
    w_gate,
    w_up,
    w_down,
    gain_attn,
    gain_ff,
    bias_table,
):
    series_count, slot_count, model_width = inputs.shape
    head_count = bias_table.shape[1]
    inner_width = w_query.shape[2]
    head_size = inner_width // head_count
    layer_count = w_query.shape[0]
    row_count = series_count * slot_count
    block_ser = min(8, series_count)
    block_count = series_count // block_ser
    onehot = (
        buckets[:, :, None] == jnp.arange(bias_table.shape[0], dtype=jnp.int32)[None, None, :]
    ).astype(jnp.float32)
    score_bias = jnp.einsum("qkn,nh->hqk", onehot, bias_table, precision=precise)
    valid_rows = patch_valid.reshape(row_count, 1) == 1
    residual = jnp.where(
        valid_rows, inputs.reshape(row_count, model_width).astype(jnp.float32), mask_embed[None, :]
    )
    mask_blocks = attention_mask.reshape(block_count, block_ser, slot_count)

    def split_heads(flat_rows):
        return flat_rows.reshape(block_count, block_ser, slot_count, head_count, head_size)

    def join_heads(blocked):
        return blocked.reshape(row_count, inner_width)

    def forward_block(pieces):
        return attend_block(pieces, score_bias)

    def backward_block(pieces):
        return attend_back(pieces, score_bias)

    stored = []
    for layer_idx in range(layer_count):
        query_weight, key_weight, value_weight, out_weight = (
            lax.all_gather(w_query[layer_idx], ("dp", "tensor"), axis=0, tiled=True),
            lax.all_gather(w_key[layer_idx], ("dp", "tensor"), axis=0, tiled=True),
            lax.all_gather(w_value[layer_idx], ("dp", "tensor"), axis=0, tiled=True),
            lax.all_gather(w_output[layer_idx], ("dp", "tensor"), axis=1, tiled=True),
        )
        normed = rms_norm(residual, gain_attn[layer_idx]).astype(jnp.bfloat16)
        query_rows = product(normed, query_weight).astype(jnp.bfloat16)
        key_rows = product(normed, key_weight).astype(jnp.bfloat16)
        value_rows = product(normed, value_weight).astype(jnp.bfloat16)
        attended, log_total = lax.map(
            forward_block,
            (split_heads(query_rows), split_heads(key_rows), split_heads(value_rows), mask_blocks),
        )
        attended = join_heads(attended)
        middle = residual + product(attended, out_weight)
        ff_input = rms_norm(middle, gain_ff[layer_idx]).astype(jnp.bfloat16)
        ff_rows = lax.all_gather(ff_input, "tensor", axis=0, tiled=True)
        ff_full = None
        gate_act = product(ff_rows, w_gate[layer_idx])
        up_act = product(ff_rows, w_up[layer_idx])
        hidden = gelu_mix(gate_act, up_act).astype(jnp.bfloat16)
        down_weight = w_down[layer_idx]
        ff_out = lax.psum_scatter(
            product(hidden, down_weight).astype(jnp.bfloat16),
            "tensor",
            scatter_dimension=0,
            tiled=True,
        ).astype(jnp.float32)
        kept_weights = None
        stored.append(
            (
                residual,
                normed,
                query_rows,
                key_rows,
                value_rows,
                log_total,
                attended,
                middle,
                ff_rows,
                gate_act,
                up_act,
                hidden,
                ff_full,
                kept_weights,
            )
        )
        residual = middle + ff_out
    outputs = residual.reshape(series_count, slot_count, model_width).astype(jnp.bfloat16)
    gradient = cotangent.reshape(row_count, model_width).astype(jnp.float32)
    bias_grad = jnp.zeros((head_count, slot_count, slot_count), jnp.float32)
    attn_list = []
    ff_list = []
    gains_attn = []
    gains_ff = []
    for layer_idx in reversed(range(layer_count)):
        (
            layer_in,
            normed,
            query_rows,
            key_rows,
            value_rows,
            log_total,
            attended,
            middle,
            ff_rows,
            gate_act,
            up_act,
            hidden,
            ff_full,
            kept_weights,
        ) = stored[layer_idx]
        ff_grad = gradient.astype(jnp.bfloat16)
        cot_rows = lax.all_gather(ff_grad, "tensor", axis=0, tiled=True)
        gate_weight = w_gate[layer_idx]
        up_weight = w_up[layer_idx]
        down_weight = w_down[layer_idx]
        grad_hidden = jnp.einsum(
            "rd,fd->rf", cot_rows, down_weight, preferred_element_type=jnp.float32
        )
        unused_mix, pull_mix = jax.vjp(gelu_mix, gate_act, up_act)
        grad_gate, grad_up = pull_mix(grad_hidden)
        grad_gate = grad_gate.astype(jnp.bfloat16)
        grad_up = grad_up.astype(jnp.bfloat16)
        down_grad = jnp.einsum("rf,rd->fd", hidden, cot_rows, preferred_element_type=jnp.float32)
        gate_grad = jnp.einsum("rd,rf->df", ff_rows, grad_gate, preferred_element_type=jnp.float32)
        up_grad = jnp.einsum("rd,rf->df", ff_rows, grad_up, preferred_element_type=jnp.float32)
        ff_in_grad = lax.psum_scatter(
            (
                jnp.einsum("rf,df->rd", grad_gate, gate_weight, preferred_element_type=jnp.float32)
                + jnp.einsum("rf,df->rd", grad_up, up_weight, preferred_element_type=jnp.float32)
            ).astype(jnp.bfloat16),
            "tensor",
            scatter_dimension=0,
            tiled=True,
        ).astype(jnp.float32)
        ff_list.append(lax.psum((gate_grad, up_grad, down_grad), "dp"))
        unused_norm, pull_norm = jax.vjp(rms_norm, middle, gain_ff[layer_idx])
        grad_mid, gain_part = pull_norm(ff_in_grad)
        gains_ff.append(gain_part)
        gradient = gradient + grad_mid
        query_weight, key_weight, value_weight, out_weight = (
            lax.all_gather(w_query[layer_idx], ("dp", "tensor"), axis=0, tiled=True),
            lax.all_gather(w_key[layer_idx], ("dp", "tensor"), axis=0, tiled=True),
            lax.all_gather(w_value[layer_idx], ("dp", "tensor"), axis=0, tiled=True),
            lax.all_gather(w_output[layer_idx], ("dp", "tensor"), axis=1, tiled=True),
        )
        branch_grad = gradient.astype(jnp.bfloat16)
        grad_attended = jnp.einsum(
            "re,de->rd", branch_grad, out_weight, preferred_element_type=jnp.float32
        ).astype(jnp.bfloat16)
        out_grad = jnp.einsum(
            "rd,re->de", attended, branch_grad, preferred_element_type=jnp.float32
        )
        grad_q, grad_k, grad_v, block_bias = lax.map(
            backward_block,
            (
                split_heads(query_rows),
                split_heads(key_rows),
                split_heads(value_rows),
                mask_blocks,
                log_total,
                split_heads(grad_attended),
            ),
        )
        bias_grad = bias_grad + jnp.sum(block_bias, axis=0)
        grad_q = join_heads(grad_q)
        grad_k = join_heads(grad_k)
        grad_v = join_heads(grad_v)
        query_grad = jnp.einsum("rd,re->de", normed, grad_q, preferred_element_type=jnp.float32)
        key_grad = jnp.einsum("rd,re->de", normed, grad_k, preferred_element_type=jnp.float32)
        value_grad = jnp.einsum("rd,re->de", normed, grad_v, preferred_element_type=jnp.float32)
        grad_normed = (
            jnp.einsum("re,de->rd", grad_q, query_weight, preferred_element_type=jnp.float32)
            + jnp.einsum("re,de->rd", grad_k, key_weight, preferred_element_type=jnp.float32)
            + jnp.einsum("re,de->rd", grad_v, value_weight, preferred_element_type=jnp.float32)
        )
        unused_attn, pull_attn = jax.vjp(rms_norm, layer_in, gain_attn[layer_idx])
        grad_in, gain_part = pull_attn(grad_normed)
        gains_attn.append(gain_part)
        gradient = gradient + grad_in
        attn_list.append(
            (
                lax.psum_scatter(query_grad, ("dp", "tensor"), scatter_dimension=0, tiled=True),
                lax.psum_scatter(key_grad, ("dp", "tensor"), scatter_dimension=0, tiled=True),
                lax.psum_scatter(value_grad, ("dp", "tensor"), scatter_dimension=0, tiled=True),
                lax.psum_scatter(out_grad, ("dp", "tensor"), scatter_dimension=1, tiled=True),
            )
        )
    attn_list = attn_list[::-1]
    ff_list = ff_list[::-1]
    grad_inputs = jnp.where(valid_rows, gradient, 0.0).reshape(
        series_count, slot_count, model_width
    )
    mask_grad = jnp.sum(jnp.where(valid_rows, 0.0, gradient), axis=0)
    table_grad = jnp.einsum("hqk,qkn->nh", bias_grad, onehot, precision=precise)
    gain_a, gain_f, table_grad, mask_grad = lax.psum(
        (jnp.stack(gains_attn[::-1]), jnp.stack(gains_ff[::-1]), table_grad, mask_grad),
        ("dp", "tensor"),
    )
    return (
        outputs,
        grad_inputs,
        jnp.stack([entry[0] for entry in attn_list]),
        jnp.stack([entry[1] for entry in attn_list]),
        jnp.stack([entry[2] for entry in attn_list]),
        jnp.stack([entry[3] for entry in attn_list]),
        jnp.stack([entry[0] for entry in ff_list]),
        jnp.stack([entry[1] for entry in ff_list]),
        jnp.stack([entry[2] for entry in ff_list]),
        gain_a,
        gain_f,
        table_grad,
        mask_grad,
    )


def solution(mesh):
    placed = (
        P(("dp", "tensor"), None, None),
        P(("dp", "tensor"), None, None),
        P(("dp", "tensor"), None),
        P(("dp", "tensor"), None),
        P(),
        P(),
        P(None, ("dp", "tensor"), None),
        P(None, ("dp", "tensor"), None),
        P(None, ("dp", "tensor"), None),
        P(None, None, ("dp", "tensor")),
        P(None, None, "tensor"),
        P(None, None, "tensor"),
        P(None, "tensor", None),
        P(),
        P(),
        P(),
    )
    return jax.shard_map(
        on_device,
        mesh=mesh,
        in_specs=placed,
        out_specs=(
            P(("dp", "tensor"), None, None),
            P(("dp", "tensor"), None, None),
            P(None, ("dp", "tensor"), None),
            P(None, ("dp", "tensor"), None),
            P(None, ("dp", "tensor"), None),
            P(None, None, ("dp", "tensor")),
            P(None, None, "tensor"),
            P(None, None, "tensor"),
            P(None, "tensor", None),
            P(),
            P(),
            P(),
            P(),
        ),
        check_vma=False,
    )
```

profile of v0, /device:TPU:0, one launch (start us, length us, event | category | flops | bytes accessed | tf_op | source)
XLA Modules:
  0.0 1772.3 jit_solution(9656636095467020904)
XLA Ops:
  12.1 71.9 %all-gather.2 = bf16[1,512,384]{2,1,0:T(8,128)(2,1)S(1)} all-gather(bf16[1,16,384]{2,1,0:T(8,128)(2,1)S(1)} %get-tuple-element.175), channel_id=4, replica_groups=mesh['dp'=16,'tensor'=2] {'dp','tensor'}, dimensions={1}, use_global_device_ids=true | all-gather | bytes 405504 | tf_op jit(solution)/shard_map/all_gather | solution.py:127
  88.9 65.4 %all-gather.1 = bf16[1,512,384]{2,1,0:T(8,128)(2,1)S(1)} all-gather(bf16[1,16,384]{2,1,0:T(8,128)(2,1)S(1)} %get-tuple-element.177), channel_id=3, replica_groups=mesh['dp'=16,'tensor'=2] {'dp','tensor'}, dimensions={1}, use_global_device_ids=true | all-gather | bytes 405504 | tf_op jit(solution)/shard_map/all_gather | solution.py:126
  160.1 67.8 %all-gather = bf16[1,512,384]{2,1,0:T(8,128)(2,1)S(1)} all-gather(bf16[1,16,384]{2,1,0:T(8,128)(2,1)S(1)} %get-tuple-element.173), channel_id=2, replica_groups=mesh['dp'=16,'tensor'=2] {'dp','tensor'}, dimensions={1}, use_global_device_ids=true | all-gather | bytes 405504 | tf_op jit(solution)/shard_map/all_gather | solution.py:128
  233.1 65.4 %all-gather.3 = bf16[1,384,512]{1,2,0:T(8,128)(2,1)S(1)} all-gather(bf16[1,384,16]{1,2,0:T(8,128)(2,1)S(1)} %get-tuple-element.171), channel_id=5, replica_groups=mesh['dp'=16,'tensor'=2] {'dp','tensor'}, dimensions={2}, use_global_device_ids=true | all-gather | bytes 405504 | tf_op jit(solution)/shard_map/all_gather | solution.py:129
  302.6 19.5 %all-gather.13.cloned.1.call-done = bf16[1024,512]{1,0:T(8,128)(2,1)} async-done(((bf16[512,512]{1,0:T(8,128)(2,1)}), bf16[1024,512]{1,0:T(8,128)(2,1)}) %all-gather.13.cloned.1.call-update) | async-done | bytes 1048592 | tf_op jit(solution)/shard_map/all_gather | solution.py:142
  329.4 69.7 %all-gather.6 = bf16[1,512,384]{2,1,0:T(8,128)(2,1)S(1)} all-gather(bf16[1,16,384]{2,1,0:T(8,128)(2,1)S(1)} %get-tuple-element.174), channel_id=8, replica_groups=mesh['dp'=16,'tensor'=2] {'dp','tensor'}, dimensions={1}, use_global_device_ids=true | all-gather | bytes 405504 | tf_op jit(solution)/shard_map/all_gather | solution.py:127
  399.1 70.8 %all-gather.5 = bf16[1,512,384]{2,1,0:T(8,128)(2,1)} all-gather(bf16[1,16,384]{2,1,0:T(8,128)(2,1)S(1)} %copy-done.79), channel_id=7, replica_groups=mesh['dp'=16,'tensor'=2] {'dp','tensor'}, dimensions={1}, use_global_device_ids=true | all-gather | bytes 405504 | tf_op jit(solution)/shard_map/all_gather | solution.py:126
  469.9 72.9 %all-gather.4 = bf16[1,512,384]{2,1,0:T(8,128)(2,1)} all-gather(bf16[1,16,384]{2,1,0:T(8,128)(2,1)S(1)} %copy-done.80), channel_id=6, replica_groups=mesh['dp'=16,'tensor'=2] {'dp','tensor'}, dimensions={1}, use_global_device_ids=true | all-gather | bytes 405504 | tf_op jit(solution)/shard_map/all_gather | solution.py:128
  542.8 71.0 %all-gather.7 = bf16[1,384,512]{1,2,0:T(8,128)(2,1)} all-gather(bf16[1,384,16]{1,2,0:T(8,128)(2,1)S(1)} %get-tuple-element.170), channel_id=9, replica_groups=mesh['dp'=16,'tensor'=2] {'dp','tensor'}, dimensions={2}, use_global_device_ids=true | all-gather | bytes 405504 | tf_op jit(solution)/shard_map/all_gather | solution.py:129
  640.0 18.2 %all-gather.15.cloned.1.call-done = bf16[1024,512]{1,0:T(8,128)(2,1)} async-done(((bf16[512,512]{1,0:T(8,128)(2,1)}), bf16[1024,512]{1,0:T(8,128)(2,1)}) %all-gather.15.cloned.1.call-update) | async-done | bytes 1048592 | tf_op jit(solution)/shard_map/all_gather | solution.py:142
  663.8 17.3 all-gather.17.cloned.1.call-done
  696.0 15.7 reduce-scatter.17.cloned.1.call-done
  714.7 20.1 %reduce-scatter.15.cloned.1.call-done = bf16[512,512]{1,0:T(8,128)(2,1)} async-done(((bf16[1024,512]{1,0:T(8,128)(2,1)}), bf16[512,512]{1,0:T(8,128)(2,1)}) %reduce-scatter.15.cloned.1.call-update) | async-done | bytes 524304 | tf_op jit(solution)/shard_map/reduce_scatter | solution.py:148
  763.8 21.2 %all-gather.19.cloned.1.call-done = bf16[1024,512]{1,0:T(8,128)(2,1)} async-done(((bf16[512,512]{1,0:T(8,128)(2,1)}), bf16[1024,512]{1,0:T(8,128)(2,1)}) %all-gather.19.cloned.1.call-update) | async-done | bytes 1048592 | tf_op jit(solution)/shard_map/all_gather | solution.py:199
  796.1 17.6 reduce-scatter.19.cloned.1.call-done
  880.2 39.6 %all-reduce = (f32[2,512]{1,0:T(2,128)}, f32[2,512]{1,0:T(2,128)}, f32[32,6]{0,1:T(8,128)}, f32[512]{0:T(512)}) all-reduce(f32[2,512]{1,0:T(2,128)S(1)} %get-tuple-element.202, f32[2,512]{1,0:T(2,128)S(1)} %get-tuple-element.203, f32[32,6]{0,1:T(8,128)S(1)} %convolution_bitcast_fusion.7, ...), channel_id=1, replica_groups=mesh['dp'=16,'tensor'=2] {'dp','tensor'}, use_global_device_ids=true, to_apply=%region_34.35 | all-reduce | flops 2752 | bytes 22016 | tf_op jit(solution)/shard_map/psum | solution.py:282
  922.1 91.8 %reduce-scatter.33.cloned.1.call-done = f32[384,16]{0,1:T(8,128)} async-done(((f32[384,512]{0,1:T(8,128)}), f32[384,16]{0,1:T(8,128)}) %reduce-scatter.33.cloned.1.call-update) | async-done | bytes 24592 | tf_op jit(solution)/shard_map/reduce_scatter | solution.py:272
  1015.3 98.3 %reduce-scatter.31.cloned.1.call-done = f32[16,384]{1,0:T(8,128)} async-done(((f32[512,384]{1,0:T(8,128)}), f32[16,384]{1,0:T(8,128)}) %reduce-scatter.31.cloned.1.call-update) | async-done | bytes 24592 | tf_op jit(solution)/shard_map/reduce_scatter | solution.py:271
  1113.6 99.6 %reduce-scatter.29.cloned.1.call-done = f32[16,384]{1,0:T(8,128)} async-done(((f32[512,384]{1,0:T(8,128)}), f32[16,384]{1,0:T(8,128)}) %reduce-scatter.29.cloned.1.call-update) | async-done | bytes 24592 | tf_op jit(solution)/shard_map/reduce_scatter | solution.py:271
  1214.6 98.4 %reduce-scatter.27.cloned.1.call-done = f32[16,384]{1,0:T(8,128)} async-done(((f32[512,384]{1,0:T(8,128)}), f32[16,384]{1,0:T(8,128)}) %reduce-scatter.27.cloned.1.call-update) | async-done | bytes 24592 | tf_op jit(solution)/shard_map/reduce_scatter | solution.py:270
  1312.9 99.6 %reduce-scatter.25.cloned.1.call-done = f32[16,384]{1,0:T(8,128)} async-done(((f32[512,384]{1,0:T(8,128)}), f32[16,384]{1,0:T(8,128)}) %reduce-scatter.25.cloned.1.call-update) | async-done | bytes 24592 | tf_op jit(solution)/shard_map/reduce_scatter | solution.py:270
  1413.9 144.0 %all-reduce.4.cloned.1.call-done = (f32[1,512,512]{2,1,0:T(8,128)}, f32[1,512,512]{2,1,0:T(8,128)}, f32[1,512,512]{2,1,0:T(8,128)}, f32[1,512,512]{2,1,0:T(8,128...) async-done(((f32[1,512,512]{2,1,0:T(8,128)}, f32[1,512,512]{2,1,0:T(8,128)}, f32[1,512,512]{2,1,0:T(8,128)}, f32[1,512,512]{2,1,0:T(8,128)}, f32[1,512,512]{2,1,0:T(8,128)}, ...) | async-done | bytes 6291472 | tf_op jit(solution)/shard_map/psum | solution.py:222
  1561.1 98.8 %reduce-scatter.23.cloned.1.call-done = f32[16,384]{1,0:T(8,128)} async-done(((f32[512,384]{1,0:T(8,128)}), f32[16,384]{1,0:T(8,128)}) %reduce-scatter.23.cloned.1.call-update) | async-done | bytes 24592 | tf_op jit(solution)/shard_map/reduce_scatter | solution.py:269
  1659.9 100.4 %reduce-scatter.21.cloned.1.call-done = f32[16,384]{1,0:T(8,128)} async-done(((f32[512,384]{1,0:T(8,128)}), f32[16,384]{1,0:T(8,128)}) %reduce-scatter.21.cloned.1.call-update) | async-done | bytes 24592 | tf_op jit(solution)/shard_map/reduce_scatter | solution.py:269
  (417 shorter events, 201.6 us)
Async XLA Ops:
  7.2 151.8 %copy-start = (f32[32,6]{0,1:T(8,128)S(1)}, f32[32,6]{0,1:T(8,128)}, u32[]{:S(2)}) copy-start(f32[32,6]{0,1:T(8,128)} %param.31) | copy-start | bytes 2308
  7.2 314.8 %all-gather.13.cloned.1.call-start = ((), (), s32[]{:S(2)}) async-start(), calls=%async_computation.12 | async-start | bytes 1572864 | tf_op jit(solution)/shard_map/all_gather | solution.py:142
  300.3 313.4 %copy-start.4 = (f32[512,512]{1,0:T(8,128)}, f32[512,512]{1,0:T(8,128)S(1)}, u32[]{:S(2)}) copy-start(f32[512,512]{1,0:T(8,128)S(1)} %get-tuple-element.187) | copy-start | bytes 3145732
  302.5 311.3 %reduce-scatter.13.cloned.1.call-start = ((), (), s32[]{:S(2)}) async-start(), calls=%async_computation.13 | async-start | bytes 1572864 | tf_op jit(solution)/shard_map/reduce_scatter | solution.py:148
  329.3 328.9 %all-gather.15.cloned.1.call-start = ((), (), s32[]{:S(2)}) async-start(), calls=%async_computation.14 | async-start | bytes 1572864 | tf_op jit(solution)/shard_map/all_gather | solution.py:142
  329.4 286.6 %copy-start.81 = (f32[1,512]{1,0:T(1,128)S(1)}, f32[1,512]{1,0:T(1,128)}, u32[]{:S(2)}) copy-start(f32[1,512]{1,0:T(1,128)} %get-tuple-element.182) | copy-start | bytes 6148
  399.1 217.1 %copy-start.40 = (bf16[1,512,384]{2,1,0:T(8,128)(2,1)}, bf16[1,512,384]{2,1,0:T(8,128)(2,1)S(1)}, u32[]{:S(2)}) copy-start(bf16[1,512,384]{2,1,0:T(8,128)(2,1)S(1)} %all-gather.6) | copy-start | bytes 1179652
  639.4 41.7 %all-gather.17.cloned.1.call-start = ((), (), s32[]{:S(2)}) async-start(), calls=%async_computation.16 | async-start | bytes 1572864 | tf_op jit(solution)/shard_map/all_gather | solution.py:199
  640.0 71.7 %reduce-scatter.17.cloned.1.call-start = ((), (), s32[]{:S(2)}) async-start(), calls=%async_computation.17 | async-start | bytes 1572864 | tf_op jit(solution)/shard_map/reduce_scatter | solution.py:213
  691.2 43.5 %reduce-scatter.15.cloned.1.call-start = ((), (), s32[]{:S(2)}) async-start(), calls=%async_computation.15 | async-start | bytes 1572864 | tf_op jit(solution)/shard_map/reduce_scatter | solution.py:148
  694.5 90.5 %all-gather.19.cloned.1.call-start = ((), (), s32[]{:S(2)}) async-start(), calls=%async_computation.18 | async-start | bytes 1572864 | tf_op jit(solution)/shard_map/all_gather | solution.py:199
  763.6 50.2 %reduce-scatter.19.cloned.1.call-start = ((), (), s32[]{:S(2)}) async-start(), calls=%async_computation.19 | async-start | bytes 1572864 | tf_op jit(solution)/shard_map/reduce_scatter | solution.py:213
  793.3 128.9 %reduce-scatter.35.cloned.1.call-start = ((), (), s32[]{:S(2)}) async-start(), calls=%async_computation.27 | async-start | bytes 811008 | tf_op jit(solution)/shard_map/reduce_scatter | solution.py:272
  796.0 217.9 %reduce-scatter.33.cloned.1.call-start = ((), (), s32[]{:S(2)}) async-start(), calls=%async_computation.26 | async-start | bytes 811008 | tf_op jit(solution)/shard_map/reduce_scatter | solution.py:272
  819.7 293.9 %reduce-scatter.31.cloned.1.call-start = ((), (), s32[]{:S(2)}) async-start(), calls=%async_computation.25 | async-start | bytes 811008 | tf_op jit(solution)/shard_map/reduce_scatter | solution.py:271
  824.4 388.8 %reduce-scatter.29.cloned.1.call-start = ((), (), s32[]{:S(2)}) async-start(), calls=%async_computation.24 | async-start | bytes 811008 | tf_op jit(solution)/shard_map/reduce_scatter | solution.py:271
  839.2 473.8 %reduce-scatter.27.cloned.1.call-start = ((), (), s32[]{:S(2)}) async-start(), calls=%async_computation.23 | async-start | bytes 811008 | tf_op jit(solution)/shard_map/reduce_scatter | solution.py:270
  843.9 568.6 %reduce-scatter.25.cloned.1.call-start = ((), (), s32[]{:S(2)}) async-start(), calls=%async_computation.22 | async-start | bytes 811008 | tf_op jit(solution)/shard_map/reduce_scatter | solution.py:270
  852.8 705.1 %all-reduce.4.cloned.1.call-start = ((), (), s32[]{:S(2)}) async-start(), calls=%async_computation.28 | async-start | bytes 12582912 | tf_op jit(solution)/shard_map/psum | solution.py:222
  863.3 796.6 %reduce-scatter.23.cloned.1.call-start = ((), (), s32[]{:S(2)}) async-start(), calls=%async_computation.21 | async-start | bytes 811008 | tf_op jit(solution)/shard_map/reduce_scatter | solution.py:269
  865.7 894.6 %reduce-scatter.21.cloned.1.call-start = ((), (), s32[]{:S(2)}) async-start(), calls=%async_computation.20 | async-start | bytes 811008 | tf_op jit(solution)/shard_map/reduce_scatter | solution.py:269
  1557.9 203.7 %copy-start.67 = (f32[1,512,512]{2,1,0:T(8,128)S(1)}, f32[1,512,512]{2,1,0:T(8,128)}, u32[]{:S(2)}) copy-start(f32[1,512,512]{2,1,0:T(8,128)} %get-tuple-element.121) | copy-start | bytes 3145732
  1557.9 203.7 %copy-start.68 = (f32[1,512,512]{2,1,0:T(8,128)S(1)}, f32[1,512,512]{2,1,0:T(8,128)}, u32[]{:S(2)}) copy-start(f32[1,512,512]{2,1,0:T(8,128)} %get-tuple-element.122) | copy-start | bytes 3145732
  1558.0 203.8 %copy-start.69 = (f32[1,512,512]{2,1,0:T(8,128)S(1)}, f32[1,512,512]{2,1,0:T(8,128)}, u32[]{:S(2)}) copy-start(f32[1,512,512]{2,1,0:T(8,128)} %get-tuple-element.123) | copy-start | bytes 3145732
  (115 other events, 1390.4 us)
Sparse Core Ops, SparseCore 0:
  302.6 19.3 all-gather.12
  329.5 21.8 reduce-scatter.12
  639.5 18.6 all-gather.14
  659.8 21.2 all-gather.16
  691.4 20.3 reduce-scatter.16
  714.4 20.3 reduce-scatter.14
  763.7 21.3 all-gather.18
  793.4 20.3 reduce-scatter.18
  818.8 95.5 reduce-scatter.34
  919.3 94.5 reduce-scatter.32
  1019.1 94.5 reduce-scatter.30
  1118.6 94.5 reduce-scatter.28
  1218.3 94.5 reduce-scatter.26
  1317.9 94.5 reduce-scatter.24
  1417.8 140.0 all-reduce.3
  1564.3 95.5 reduce-scatter.22
  1665.7 94.5 reduce-scatter.20
where the time goes:
time: 1780 us; the launch traced here: 1770 us
  waiting for transfers between devices  961 us (54%)
  blocking collectives  594 us (33%)
  matrix products  92.3 us (5%)
  local copies, waits for them, and re-layouts  61.2 us (3%)
  other arithmetic  46 us (3%)
    reduce_scatter x2, waiting for transfers between devices, on_device(): lax.psum_scatter(query_grad, ('dp', 'tensor'), scatter_dimension=0, tiled...  199 us
    reduce_scatter x2, waiting for transfers between devices, on_device(): lax.psum_scatter(key_grad, ('dp', 'tensor'), scatter_dimension=0, tiled=T...  198 us
    reduce_scatter x2, waiting for transfers between devices, on_device(): lax.psum_scatter(value_grad, ('dp', 'tensor'), scatter_dimension=0, tiled...  198 us
    psum x1, waiting for transfers between devices, on_device(): ff_list.append(lax.psum((gate_grad, up_grad, down_grad), 'dp'))  144 us
    all_gather x2, blocking collectives, on_device(): lax.all_gather(w_key[layer_idx], ('dp', 'tensor'), axis=0, tiled=True)  142 us
    all_gather x2, blocking collectives, on_device(): lax.all_gather(w_value[layer_idx], ('dp', 'tensor'), axis=0, tiled=True)  141 us
    all_gather x2, blocking collectives, on_device(): lax.all_gather(w_output[layer_idx], ('dp', 'tensor'), axis=1, tiled=True)  136 us
    all_gather x2, blocking collectives, on_device(): lax.all_gather(w_query[layer_idx], ('dp', 'tensor'), axis=0, tiled=True)  136 us
  transfers between devices with their start and end apart: 17, of which 15 were waited for; matrix products, arithmetic and copies ran while one was open for 5% of the time, Pallas kernels for 0%

commit v1 on v0

v1 whole, which is shorter than its diff:
```python
import functools
import types

import jax
import jax.numpy as jnp
from jax import lax
from jax.experimental import pallas as pl
from jax.experimental.pallas import tpu as pltpu
from jax.sharding import PartitionSpec as P

norm_eps = 1e-06
masked_score = -1e30
bf16 = jnp.bfloat16
f32 = jnp.float32
axes = ("dp", "tensor")
vmem_bytes = 56 * 1024 * 1024


def dot_nn(left, right):
    return lax.dot_general(left, right, (((1,), (0,)), ((), ())), preferred_element_type=f32)


def dot_nt(left, right):
    return lax.dot_general(left, right, (((1,), (1,)), ((), ())), preferred_element_type=f32)


def dot_tn(left, right):
    return lax.dot_general(left, right, (((0,), (0,)), ((), ())), preferred_element_type=f32)


def inverse_rms(values):
    return lax.rsqrt(jnp.mean(values * values, axis=-1, keepdims=True) + norm_eps)


def norm_back(values, gain, grad_out):
    scale = inverse_rms(values)
    pulled = grad_out * gain
    mean_part = jnp.mean(pulled * values, axis=-1, keepdims=True)
    grad_in = scale * pulled - values * (scale * scale * scale) * mean_part
    return grad_in, jnp.sum(grad_out * values * scale, axis=0, keepdims=True)


def gelu_terms(gate_act):
    square = gate_act * gate_act
    bent = jnp.tanh(0.7978845608028654 * gate_act * (1.0 + 0.044715 * square))
    half = 0.5 * (1.0 + bent)
    slope = half + 0.5 * gate_act * (1.0 - bent * bent) * (
        0.7978845608028654 * (1.0 + 3.0 * 0.044715 * square)
    )
    return gate_act * half, slope


def run(body, name, ins, outs, scratch, flops=0):
    names = list(ins) + list(outs) + list(scratch)

    def kernel(*refs):
        body(types.SimpleNamespace(**dict(zip(names, refs))))

    moved = sum(a.size * a.dtype.itemsize for a, _ in ins.values())
    results = pl.pallas_call(
        kernel,
        name=name,
        in_specs=[pl.BlockSpec(memory_space=space) for _, space in ins.values()],
        out_specs=[pl.BlockSpec(memory_space=pltpu.VMEM) for _ in outs],
        out_shape=[jax.ShapeDtypeStruct(shape, kind) for shape, kind in outs.values()],
        scratch_shapes=list(scratch.values()),
        compiler_params=pltpu.CompilerParams(vmem_limit_bytes=vmem_bytes),
        cost_estimate=pl.CostEstimate(flops=flops, bytes_accessed=moved, transcendentals=0),
    )(*[a for a, _ in ins.values()])
    return types.SimpleNamespace(**dict(zip(outs, results)))


def chunks(extent, size):
    size = min(size, extent)
    return [slice(start, start + size) for start in range(0, extent, size)]


def attention_copies(r, masks, rows):
    copies = []
    for idx, mask in enumerate(masks):
        half, at = divmod(idx, max(1, len(masks) // 2))
        source = (r.attn_near if half == 0 else r.attn_far).at[pl.ds(at * rows, rows)]
        place = (r.place[0] ^ mask) * rows if len(masks) > 1 else 0
        target = r.attn_w.at[pl.ds(pl.multiple_of(place, rows), rows)]
        copies.append(pltpu.make_async_copy(source, target, r.attn_sem))
    return copies


def ff_copies(r, layer_idx):
    copies = []
    for k, own in enumerate((r.w_gate, r.w_up, r.w_down)):
        copies.append(pltpu.make_async_copy(own.at[layer_idx], r.ff_w.at[0, k], r.ff_sem))
    part = r.ff_near.shape[1]
    core = r.place[1]
    for source, which in ((r.ff_near, core), (r.ff_far, 1 - core)):
        for k in range(3):
            target = r.ff_w.at[1, k, pl.ds(pl.multiple_of(which * part, part), part)]
            copies.append(pltpu.make_async_copy(source.at[k], target, r.ff_sem))
    return copies


def start_all(copies):
    for copy in copies:
        copy.start()


def wait_all(whole, sem):
    pltpu.make_async_copy(whole, whole, sem).wait()


def lane_low(rows):
    return lax.broadcasted_iota(jnp.int32, (rows, 128), 1) < 64


def pair_blocks(rows, low, high):
    return jnp.concatenate([rows * low, rows * high], axis=0)


def half_sums(values, is_low):
    first = jnp.sum(jnp.where(is_low, values, 0.0), axis=1, keepdims=True)
    second = jnp.sum(jnp.where(is_low, 0.0, values), axis=1, keepdims=True)
    return jnp.where(is_low, first, second)


def attention_forward(r, x_ref, a_ref, gain_ref, series, slots, inner):
    rows = series * slots
    for part in chunks(rows, 256):
        r.qkv[part, :] = dot_nn(a_ref[part, :], r.attn_w[:, : 3 * inner]).astype(bf16)
    is_low = lane_low(slots)
    low = lane_low(1).astype(f32).astype(bf16)
    high = (1.0 - low.astype(f32)).astype(bf16)

    def one(s):
        here = pl.ds(pl.multiple_of(s * slots, slots), slots)
        keep = r.mask[pl.ds(s, 1), :] == 1
        for start in range(0, inner, 128):
            at = slice(start, start + 128)
            query = r.qkv[here, at]
            keys = r.qkv[here, inner + start : inner + start + 128]
            values = r.qkv[here, 2 * inner + start : 2 * inner + start + 128]
            scores = dot_nt(query, pair_blocks(keys, low, high)) + r.bias[:, at]
            scores = jnp.where(keep, scores, masked_score)
            top_low = jnp.max(jnp.where(is_low, scores, -jnp.inf), axis=1, keepdims=True)
            top_high = jnp.max(jnp.where(is_low, -jnp.inf, scores), axis=1, keepdims=True)
            exps = jnp.exp(scores - jnp.where(is_low, top_low, top_high))
            probs = exps / half_sums(exps, is_low)
            r.probs[here, at] = probs
            r.heads[here, at] = dot_nn(
                probs.astype(bf16), pair_blocks(values, low, high)
            ).astype(bf16)

    @pl.loop(0, series // 2)
    def _(step):
        one(2 * step)
        one(2 * step + 1)

    for part in chunks(rows, 256):
        middle = x_ref[part, :] + dot_nt(r.heads[part, :], r.attn_w[:, 3 * inner :])
        r.middle[part, :] = middle
        r.ff_in[part, :] = (middle * inverse_rms(middle) * gain_ref[...]).astype(bf16)


def ff_forward(r, part):
    total = None
    for half in range(2):
        rows = r.ff_in[part, :]
        gate_act = dot_nn(rows, r.ff_w[half, 0])
        up_act = dot_nn(rows, r.ff_w[half, 1])
        hidden = (gelu_terms(gate_act)[0] * up_act).astype(bf16)
        term = dot_nn(hidden, r.ff_w[half, 2])
        total = term if total is None else total + term
    return total


def prepare_body(r):
    x = jnp.where(r.valid[...] == 1, r.inputs[...].astype(f32), r.embed[...])
    r.x[...] = x
    r.a[...] = (x * inverse_rms(x) * r.gain[...]).astype(bf16)
    buckets = r.buckets[...]
    bias = jnp.zeros(buckets.shape, f32)
    for idx in range(r.table.shape[0]):
        bias = jnp.where(buckets == idx, r.table[idx : idx + 1, :], bias)
    r.bias[...] = bias


def first_body(r, sizes, masks, grain):
    attn = attention_copies(r, masks, grain)
    start_all(attn)
    ff = ff_copies(r, 0)
    start_all(ff)
    wait_all(r.attn_w, r.attn_sem)
    attention_forward(r, r.x, r.a, r.gain_ff, *sizes)
    wait_all(r.ff_w, r.ff_sem)
    for part in chunks(r.x.shape[0], 256):
        x_next = r.middle[part, :] + ff_forward(r, part)
        r.x_next[part, :] = x_next
        r.a_next[part, :] = (x_next * inverse_rms(x_next) * r.gain_next[...]).astype(bf16)


def second_body(r, sizes, masks, grain):
    attn = attention_copies(r, masks, grain)
    start_all(attn)
    wait_all(r.attn_w, r.attn_sem)
    attention_forward(r, r.x, r.a, r.gain_ff, *sizes)


def backward_body(r, sizes, masks, grain, layer_idx, last, piece_masks):
    series, slots, inner = sizes
    rows = series * slots
    attn = attention_copies(r, masks, grain)
    ff = ff_copies(r, layer_idx)
    start_all(ff)
    start_all(attn)
    wait_all(r.ff_w, r.ff_sem)
    r.grad_gain_ff[...] = jnp.zeros(r.grad_gain_ff.shape, f32)
    r.grad_gain_attn[...] = jnp.zeros(r.grad_gain_attn.shape, f32)
    for part in chunks(rows, 256):
        grad = r.grad[part, :].astype(f32)
        rounded = grad.astype(bf16)
        ff_rows = r.ff_in[part, :]
        back = None
        total = None
        for half in range(2):
            gate_act = dot_nn(ff_rows, r.ff_w[half, 0])
            up_act = dot_nn(ff_rows, r.ff_w[half, 1])
            grad_hidden = dot_nt(rounded, r.ff_w[half, 2])
            mixed, slope = gelu_terms(gate_act)
            grad_gate = (grad_hidden * up_act * slope).astype(bf16)
            grad_up = (grad_hidden * mixed).astype(bf16)
            hidden = (mixed * up_act).astype(bf16)
            if half == 0:
                r.hidden[part, :] = hidden
                r.grad_gate[part, :] = grad_gate
                r.grad_up[part, :] = grad_up
            if last:
                term = dot_nn(hidden, r.ff_w[half, 2])
                total = term if total is None else total + term
            term = dot_nt(grad_gate, r.ff_w[half, 0]) + dot_nt(grad_up, r.ff_w[half, 1])
            back = term if back is None else back + term
        middle = r.middle[part, :]
        if last:
            r.outputs[part, :] = (middle + total).astype(bf16)
        grad_mid, gain_part = norm_back(middle, r.gain_ff[...], back)
        r.grad_gain_ff[...] += gain_part
        grad_mid = grad + grad_mid
        r.grad_mid[part, :] = grad_mid
        r.branch[part, :] = grad_mid.astype(bf16)
    wait_all(r.attn_w, r.attn_sem)
    for part in chunks(rows, 256):
        r.grad_heads[part, :] = dot_nn(r.branch[part, :], r.attn_w[:, 3 * inner :]).astype(bf16)
    is_low = lane_low(slots)
    low = lane_low(1).astype(f32).astype(bf16)
    high = (1.0 - low.astype(f32)).astype(bf16)
    if last:
        r.bias_acc[...] = jnp.zeros(r.bias_acc.shape, f32)
    else:
        r.bias_acc[...] = r.bias_before[...]

    def one(s):
        here = pl.ds(pl.multiple_of(s * slots, slots), slots)
        for start in range(0, inner, 128):
            at = slice(start, start + 128)
            key_at = slice(inner + start, inner + start + 128)
            value_at = slice(2 * inner + start, 2 * inner + start + 128)
            query = r.qkv[here, at]
            probs = r.probs[here, at]
            grad_out = r.grad_heads[here, at]
            grad_probs = dot_nt(grad_out, pair_blocks(r.qkv[here, value_at], low, high))
            inner_sum = half_sums(probs * grad_probs, is_low)
            grad_scores = (probs * (grad_probs - inner_sum)).astype(bf16)
            r.bias_acc[:, at] += grad_scores.astype(f32)
            r.grad_qkv[here, at] = dot_nn(
                grad_scores, pair_blocks(r.qkv[here, key_at], low, high)
            ).astype(bf16)
            both = dot_tn(grad_scores, query)
            r.grad_qkv[here, key_at] = jnp.where(is_low, both[:slots], both[slots:]).astype(bf16)
            both = dot_tn(probs.astype(bf16), grad_out)
            r.grad_qkv[here, value_at] = jnp.where(is_low, both[:slots], both[slots:]).astype(bf16)

    @pl.loop(0, series // 2)
    def _(step):
        one(2 * step)
        one(2 * step + 1)

    for at in chunks(3 * inner, inner):
        r.attn_grad[:, at] = dot_tn(r.a[...], r.grad_qkv[:, at])
    r.attn_grad[:, 3 * inner :] = dot_tn(r.branch[...], r.heads[...])
    scatter_pieces(r, r.attn_grad, r.attn_keep, r.attn_send, piece_masks, r.place[2])
    if not last:
        r.grad_embed[...] = jnp.zeros(r.grad_embed.shape, f32)
    for part in chunks(rows, 256):
        grad_normed = dot_nt(r.grad_qkv[part, :], r.attn_w[:, : 3 * inner])
        grad_in, gain_part = norm_back(r.x[part, :], r.gain_attn[...], grad_normed)
        r.grad_gain_attn[...] += gain_part
        grad_in = r.grad_mid[part, :] + grad_in
        if last:
            r.grad_next[part, :] = grad_in
            r.grad_next_low[part, :] = grad_in.astype(bf16)
        else:
            seen = r.valid[part, :] == 1
            r.grad_next[part, :] = jnp.where(seen, grad_in, 0.0)
            r.grad_embed[...] += jnp.sum(jnp.where(seen, 0.0, grad_in), axis=0, keepdims=True)
    if not last:
        head_size = r.bias_acc.shape[1] // r.head_count
        for idx in range(r.table_rows.shape[0]):
            chosen = jnp.where(r.buckets[...] == idx, r.bias_acc[...], 0.0)
            r.table_rows[idx : idx + 1, :] = jnp.sum(chosen, axis=0, keepdims=True)
        lane = lax.broadcasted_iota(jnp.int32, r.grad_table.shape, 1)
        table = jnp.zeros(r.grad_table.shape, f32)
        for head in range(r.head_count):
            cut = r.table_rows[:, head * head_size : (head + 1) * head_size]
            table = jnp.where(lane == head, jnp.sum(cut, axis=1, keepdims=True), table)
        r.grad_table[...] = table


def scatter_pieces(r, whole, keep, send, masks, place):
    count = len(masks)
    grain = whole.shape[-2] // count
    for idx, mask in enumerate(masks):
        target = keep if idx < count // 2 else send
        at = idx % (count // 2)
        source = pl.ds(pl.multiple_of((place ^ mask) * grain, grain), grain)
        if len(whole.shape) == 2:
            target[at] = whole[source, :].astype(bf16)
        else:
            for k in range(whole.shape[0]):
                target[at, k] = whole[k, source, :].astype(bf16)


def weight_body(r, layer_idx, piece_masks):
    copies = [
        pltpu.make_async_copy(own.at[layer_idx], r.ff_w.at[k], r.ff_sem)
        for k, own in enumerate((r.w_gate, r.w_up, r.w_down))
    ]
    start_all(copies)
    wait_all(r.ff_w, r.ff_sem)
    for part in chunks(r.peer_in.shape[0], 256):
        rows = r.peer_in[part, :]
        gate_act = dot_nn(rows, r.ff_w[0])
        up_act = dot_nn(rows, r.ff_w[1])
        grad_hidden = dot_nt(r.peer_grad[part, :], r.ff_w[2])
        mixed, slope = gelu_terms(gate_act)
        r.peer_gate[part, :] = (grad_hidden * up_act * slope).astype(bf16)
        r.peer_up[part, :] = (grad_hidden * mixed).astype(bf16)
        r.peer_hidden[part, :] = (mixed * up_act).astype(bf16)
    r.ff_grad[0] = dot_tn(r.ff_in[...], r.grad_gate[...]) + dot_tn(r.peer_in[...], r.peer_gate[...])
    r.ff_grad[1] = dot_tn(r.ff_in[...], r.grad_up[...]) + dot_tn(r.peer_in[...], r.peer_up[...])
    r.ff_grad[2] = dot_tn(r.hidden[...], r.grad[...]) + dot_tn(r.peer_hidden[...], r.peer_grad[...])
    scatter_pieces(r, r.ff_grad, r.ff_keep, r.ff_send, piece_masks, r.place[3])


def finish_body(r, masks):
    count = len(masks)
    grain = r.near0.shape[2]
    for layer_idx, (near, far) in enumerate(((r.near0, r.far0), (r.near1, r.far1))):
        for idx, mask in enumerate(masks):
            half, at = divmod(idx, count // 2)
            source = far if half else near
            target = pl.ds(pl.multiple_of((r.place[3] ^ mask) * grain, grain), grain)
            for k, out in enumerate((r.gate, r.up, r.down)):
                out[layer_idx, target, :] = source[at, k].astype(f32)


def order_masks(hops):
    masks = [0]
    for hop in reversed(hops):
        masks = masks + [mask ^ hop for mask in masks]
    return masks


def on_device(
    inputs,
    cotangent,
    attention_mask,
    patch_valid,
    buckets,
    mask_embed,
    w_query,
    w_key,
    w_value,
    w_output,
    w_gate,
    w_up,
    w_down,
    gain_attn,
    gain_ff,
    bias_table,
    dp_size,
):
    series, slots, width = inputs.shape
    heads = bias_table.shape[1]
    inner = w_query.shape[2]
    rows = series * slots
    sizes = (series, slots, inner)
    devices = 2 * dp_size
    dp_at = lax.axis_index("dp")
    device_at = 2 * dp_at + lax.axis_index("tensor")
    core_at = lax.rem(dp_at, 2)
    VMEM, ANY, SMEM = pltpu.VMEM, pl.ANY, pltpu.SMEM

    def swap(array, mask):
        return lax.ppermute(array, axes, [(n, n ^ mask) for n in range(devices)])

    bits = [1 << k for k in range(devices.bit_length() - 1)]
    far_first = bits[4:] + bits[2:4][::-1] + bits[:1] + bits[1:2]

    packed = jnp.concatenate(
        [w_query, w_key, w_value, jnp.swapaxes(w_output, 1, 2)], axis=2
    )
    own_rows = packed.shape[1]
    direct = own_rows % 16 == 0

    def gather_attention(block, hops):
        if not direct:
            return lax.all_gather(block, axes, axis=0, tiled=True), None, [0]
        masks = [0]
        for hop in hops[:-1]:
            block = jnp.concatenate([block, swap(block, hop)], axis=0)
            masks = masks + [mask ^ hop for mask in masks]
        return block, swap(block, hops[-1]), masks + [mask ^ hops[-1] for mask in masks]

    def gather_ff(layer_idx):
        part = width // 2
        blocks = [
            lax.dynamic_slice_in_dim(w[layer_idx], core_at * part, part, axis=0)
            for w in (w_gate, w_up, w_down)
        ]
        near = swap(jnp.stack(blocks), 1)
        return near, swap(near, 2)

    attn_pieces = []
    ff_pieces = []
    for layer_idx in range(2):
        attn_pieces.append(gather_attention(packed[layer_idx], far_first))
        ff_pieces.append(gather_ff(layer_idx))
    peer_cotangent = swap(cotangent.reshape(rows, width), 1)

    attn_grain = max(16, width // devices)
    attn_count = width // attn_grain
    ff_grain = max(16, width // dp_size)
    ff_count = width // ff_grain
    place = jnp.stack(
        [
            device_at,
            core_at,
            device_at // (devices // attn_count),
            lax.rem(dp_at, ff_count),
        ]
    ).astype(jnp.int32)

    wide_buckets = jnp.tile(buckets, (1, heads))
    wide_table = jnp.repeat(bias_table, slots, axis=1)
    wide_mask = jnp.tile(attention_mask, (1, 2))
    valid = patch_valid.reshape(rows, 1)
    matrix = (rows, width)

    start = run(
        prepare_body,
        "prepare",
        dict(
            inputs=(inputs.reshape(matrix), VMEM),
            valid=(valid, VMEM),
            embed=(mask_embed[None, :], VMEM),
            gain=(gain_attn[0:1], VMEM),
            buckets=(wide_buckets, VMEM),
            table=(wide_table, VMEM),
        ),
        dict(x=(matrix, f32), a=(matrix, bf16), bias=((slots, heads * slots), f32)),
        {},
    )

    def attn_ins(layer_idx):
        near, far, masks = attn_pieces[layer_idx]
        return dict(attn_near=(near, ANY), attn_far=(near if far is None else far, ANY)), masks

    def ff_ins(layer_idx):
        near, far = ff_pieces[layer_idx]
        return dict(
            w_gate=(w_gate, ANY),
            w_up=(w_up, ANY),
            w_down=(w_down, ANY),
            ff_near=(near, ANY),
            ff_far=(far, ANY),
        )

    attn_scratch = dict(
        attn_w=pltpu.VMEM((width, 4 * inner), bf16), attn_sem=pltpu.SemaphoreType.DMA
    )
    ff_scratch = dict(
        ff_w=pltpu.VMEM((2, 3, width, width), bf16), ff_sem=pltpu.SemaphoreType.DMA
    )
    grain = own_rows if direct else width
    attn_outs = dict(
        qkv=((rows, 3 * inner), bf16),
        probs=((rows, heads * slots), f32),
        heads=((rows, inner), bf16),
        middle=(matrix, f32),
        ff_in=(matrix, bf16),
    )
    attn_flops = 2 * rows * width * 4 * inner
    ff_flops = 2 * rows * width * 6 * width

    pieces, masks = attn_ins(0)
    first = run(
        functools.partial(first_body, sizes=sizes, masks=masks, grain=grain),
        "layer_0_forward",
        dict(
            place=(place, SMEM),
            x=(start.x, VMEM),
            a=(start.a, VMEM),
            bias=(start.bias, VMEM),
            mask=(wide_mask, VMEM),
            gain_ff=(gain_ff[0:1], VMEM),
            gain_next=(gain_attn[1:2], VMEM),
            **pieces,
            **ff_ins(0),
        ),
        dict(**attn_outs, x_next=(matrix, f32), a_next=(matrix, bf16)),
        dict(**attn_scratch, **ff_scratch),
        flops=attn_flops + ff_flops,
    )
    peer_in_0 = swap(first.ff_in, 1)
    pieces, masks = attn_ins(1)
    second = run(
        functools.partial(second_body, sizes=sizes, masks=masks, grain=grain),
        "layer_1_attention",
        dict(
            place=(place, SMEM),
            x=(first.x_next, VMEM),
            a=(first.a_next, VMEM),
            bias=(start.bias, VMEM),
            mask=(wide_mask, VMEM),
            gain_ff=(gain_ff[1:2], VMEM),
            **pieces,
        ),
        attn_outs,
        attn_scratch,
        flops=attn_flops,
    )
    peer_in_1 = swap(second.ff_in, 1)

    attn_hops = [2, 1] + bits[2:]
    attn_low = devices // attn_count
    attn_split = [hop for hop in attn_hops if hop >= attn_low]
    attn_whole = [hop for hop in attn_hops if hop < attn_low]
    ff_hops = bits[1:]
    ff_split = [hop for hop in ff_hops if hop // 2 < ff_count]
    ff_whole = [hop for hop in ff_hops if hop // 2 >= ff_count]
    attn_masks = [mask // attn_low for mask in order_masks(attn_split)]
    ff_masks = [mask // 2 for mask in order_masks(ff_split)]
    attn_half = (attn_count // 2, attn_grain, 4 * inner)
    ff_half = (ff_count // 2, 3, ff_grain, width)

    def backward(layer_idx, kept, x, a, grad, extra_ins, extra_outs, extra_scratch):
        last = layer_idx == 1
        pieces, masks = attn_ins(layer_idx)

        def body(r):
            r.head_count = heads
            backward_body(r, sizes, masks, grain, layer_idx, last, attn_masks)

        return run(
            body,
            "layer_%d_backward" % layer_idx,
            dict(
                place=(place, SMEM),
                x=(x, VMEM),
                a=(a, VMEM),
                grad=(grad, VMEM),
                gain_attn=(gain_attn[layer_idx : layer_idx + 1], VMEM),
                gain_ff=(gain_ff[layer_idx : layer_idx + 1], VMEM),
                qkv=(kept.qkv, VMEM),
                probs=(kept.probs, VMEM),
                heads=(kept.heads, VMEM),
                middle=(kept.middle, VMEM),
                ff_in=(kept.ff_in, VMEM),
                **pieces,
                **ff_ins(layer_idx),
                **extra_ins,
            ),
            dict(
                grad_next=(matrix, f32),
                hidden=(matrix, bf16),
                grad_gate=(matrix, bf16),
                grad_up=(matrix, bf16),
                grad_gain_attn=((1, width), f32),
                grad_gain_ff=((1, width), f32),
                attn_keep=(attn_half, bf16),
                attn_send=(attn_half, bf16),
                **extra_outs,
            ),
            dict(
                grad_mid=pltpu.VMEM(matrix, f32),
                branch=pltpu.VMEM(matrix, bf16),
                grad_heads=pltpu.VMEM((rows, inner), bf16),
                grad_qkv=pltpu.VMEM((rows, 3 * inner), bf16),
                attn_grad=pltpu.VMEM((width, 4 * inner), f32),
                **attn_scratch,
                **ff_scratch,
                **extra_scratch,
            ),
            flops=2 * (attn_flops + ff_flops),
        )

    def weight_grads(layer_idx, kept, back, grad, peer_in, peer_grad):
        return run(
            functools.partial(weight_body, layer_idx=layer_idx, piece_masks=ff_masks),
            "layer_%d_weight_grads" % layer_idx,
            dict(
                place=(place, SMEM),
                ff_in=(kept.ff_in, VMEM),
                grad=(grad, VMEM),
                hidden=(back.hidden, VMEM),
                grad_gate=(back.grad_gate, VMEM),
                grad_up=(back.grad_up, VMEM),
                peer_in=(peer_in, VMEM),
                peer_grad=(peer_grad, VMEM),
                w_gate=(w_gate, ANY),
                w_up=(w_up, ANY),
                w_down=(w_down, ANY),
            ),
            dict(ff_keep=(ff_half, bf16), ff_send=(ff_half, bf16)),
            dict(
                peer_gate=pltpu.VMEM(matrix, bf16),
                peer_up=pltpu.VMEM(matrix, bf16),
                peer_hidden=pltpu.VMEM(matrix, bf16),
                ff_grad=pltpu.VMEM((3, width, width), f32),
                ff_w=pltpu.VMEM((3, width, width), bf16),
                ff_sem=pltpu.SemaphoreType.DMA,
            ),
            flops=ff_flops,
        )

    def add(left, right):
        return (left.astype(f32) + right.astype(f32)).astype(bf16)

    def halve(keep, send, hops):
        for step, hop in enumerate(hops):
            got = swap(send, hop)
            if step + 1 < len(hops):
                cut = keep.shape[0] // 2
                send = add(keep[cut:], got[cut:])
                keep = add(keep[:cut], got[:cut])
            else:
                keep = add(keep, got)
        return keep

    def share(piece, hops):
        for hop in hops[:-1]:
            piece = jnp.concatenate([piece, swap(piece, hop)], axis=0)
        return piece, swap(piece, hops[-1])

    def whole_sum(piece, hops):
        for hop in hops:
            piece = add(piece, swap(piece, hop))
        return piece

    def reduce_ff(part):
        piece = whole_sum(halve(part.ff_keep, part.ff_send, ff_split), ff_whole)
        return share(piece, ff_split[::-1])

    def reduce_attn(part):
        piece = whole_sum(halve(part.attn_keep, part.attn_send, attn_split), attn_whole)[0]
        if own_rows < attn_grain:
            first_row = lax.rem(device_at, attn_low) * own_rows
            piece = lax.dynamic_slice_in_dim(piece, first_row, own_rows, axis=0)
        return piece.astype(f32)

    back_1 = backward(
        1,
        second,
        first.x_next,
        first.a_next,
        cotangent.reshape(matrix),
        {},
        dict(
            outputs=(matrix, bf16),
            grad_next_low=(matrix, bf16),
            bias_acc=((slots, heads * slots), f32),
        ),
        {},
    )
    peer_grad_0 = swap(back_1.grad_next_low, 1)
    part_1 = weight_grads(
        1, second, back_1, cotangent.reshape(matrix), peer_in_1, peer_cotangent
    )
    back_0 = backward(
        0,
        first,
        start.x,
        start.a,
        back_1.grad_next,
        dict(bias_before=(back_1.bias_acc, VMEM), valid=(valid, VMEM), buckets=(wide_buckets, VMEM)),
        dict(grad_embed=((1, width), f32), grad_table=((bias_table.shape[0], 128), f32)),
        dict(
            bias_acc=pltpu.VMEM((slots, heads * slots), f32),
            table_rows=pltpu.VMEM((bias_table.shape[0], heads * slots), f32),
        ),
    )
    part_0 = weight_grads(0, first, back_0, back_1.grad_next_low, peer_in_0, peer_grad_0)

    attn_1 = reduce_attn(back_1)
    ff_1 = reduce_ff(part_1)
    attn_0 = reduce_attn(back_0)
    ff_0 = reduce_ff(part_0)

    small = jnp.concatenate(
        [
            back_0.grad_gain_attn,
            back_1.grad_gain_attn,
            back_0.grad_gain_ff,
            back_1.grad_gain_ff,
            back_0.grad_embed,
            back_0.grad_table[:, :heads].reshape(1, -1),
        ],
        axis=1,
    ).reshape(-1, 1)
    small = jnp.pad(small, ((0, -small.shape[0] % 1024), (0, 0))).reshape(-1, 128)
    for hop in attn_hops:
        small = small + swap(small, hop)
    small = small.reshape(-1)

    done = run(
        functools.partial(
            finish_body,
            masks=[mask // 2 for mask in order_masks(ff_split)],
        ),
        "finish",
        dict(
            place=(place, SMEM),
            near0=(ff_0[0], VMEM),
            far0=(ff_0[1], VMEM),
            near1=(ff_1[0], VMEM),
            far1=(ff_1[1], VMEM),
        ),
        dict(
            gate=((2, width, width), f32),
            up=((2, width, width), f32),
            down=((2, width, width), f32),
        ),
        {},
    )
    attn_grads = jnp.stack([attn_0, attn_1])
    table_size = bias_table.size
    return (
        back_1.outputs.reshape(inputs.shape),
        back_0.grad_next.reshape(inputs.shape),
        attn_grads[:, :, :inner],
        attn_grads[:, :, inner : 2 * inner],
        attn_grads[:, :, 2 * inner : 3 * inner],
        jnp.swapaxes(attn_grads[:, :, 3 * inner :], 1, 2),
        done.gate,
        done.up,
        done.down,
        small[: 2 * width].reshape(2, width),
        small[2 * width : 4 * width].reshape(2, width),
        small[5 * width : 5 * width + table_size].reshape(bias_table.shape),
        small[4 * width : 5 * width],
    )


def solution(mesh):
    placed = (
        P(("dp", "tensor"), None, None),
        P(("dp", "tensor"), None, None),
        P(("dp", "tensor"), None),
        P(("dp", "tensor"), None),
        P(),
        P(),
        P(None, ("dp", "tensor"), None),
        P(None, ("dp", "tensor"), None),
        P(None, ("dp", "tensor"), None),
        P(None, None, ("dp", "tensor")),
        P(None, None, "tensor"),
        P(None, None, "tensor"),
        P(None, "tensor", None),
        P(),
        P(),
        P(),
    )
    return jax.shard_map(
        functools.partial(on_device, dp_size=mesh.shape["dp"]),
        mesh=mesh,
        in_specs=placed,
        out_specs=(
            P(("dp", "tensor"), None, None),
            P(("dp", "tensor"), None, None),
            P(None, ("dp", "tensor"), None),
            P(None, ("dp", "tensor"), None),
            P(None, ("dp", "tensor"), None),
            P(None, None, ("dp", "tensor")),
            P(None, None, "tensor"),
            P(None, None, "tensor"),
            P(None, "tensor", None),
            P(),
            P(),
            P(),
            P(),
        ),
        check_vma=False,
    )
```

time: 1780 us -> 299 us (0.17)
  waiting for transfers between devices: 961 us -> 126 us
  blocking collectives: 594 us -> 0 us
  Pallas kernels: 0 us -> 97.9 us
  matrix products: 92.3 us -> 0 us
  starting transfers between devices: 1.34 us -> 47.6 us
  other arithmetic: 46 us -> 2.93 us
  local copies, waits for them, and re-layouts: 61.2 us -> 22.1 us
    reduce_scatter x12 -> x0, waiting for transfers between devices: 740 us -> none  [the longest x2 199 us: on_device(): lax.psum_scatter(query_grad, ('dp', 'tensor'), scatter_dimension=0, tiled...]
    all_gather x8 -> x0, blocking collectives: 555 us -> none  [the longest x2 142 us: on_device(): lax.all_gather(w_key[layer_idx], ('dp', 'tensor'), axis=0, tiled=True)]
    psum x1 -> x0, waiting for transfers between devices: 144 us -> none  [on_device(): ff_list.append(lax.psum((gate_grad, up_grad, down_grad), 'dp'))]
    ppermute x0 -> x49, waiting for transfers between devices: none -> 126 us  [swap(): return lax.ppermute(array, axes, [(n, n ^ mask) for n in range(devices)])]
    pallas_call x0 -> x8, Pallas kernels: none -> 97.9 us  [run(): pl.pallas_call(kernel, name=name, in_specs=[pl.BlockSpec(memory_space=spa...]
    dot_general x56 -> x0, matrix products: 92.3 us -> none  [the longest x14 24.7 us: product(): return jnp.dot(left, right, preferred_element_type=jnp.float32)]
    all_gather x4 -> x0, waiting for transfers between devices: 76.2 us -> none  [the longest x2 38.5 us: on_device(): cot_rows = lax.all_gather(ff_grad, 'tensor', axis=0, tiled=True)]
    ppermute x0 -> x49, starting transfers between devices: none -> 47.6 us  [swap(): return lax.ppermute(array, axes, [(n, n ^ mask) for n in range(devices)])]
  transfers between devices with their start and end apart: 17 -> 49, of which waited for: 15 -> 27; matrix products, arithmetic and copies ran while one was open for 5% -> 6% of each run, Pallas kernels for 0% -> 31%
where the time goes in v1:
time: 299 us; the launch traced here: 298 us
  waiting for transfers between devices  126 us (42%)
  Pallas kernels  97.9 us (33%)
  starting transfers between devices  47.6 us (16%)
  local copies, waits for them, and re-layouts  22.1 us (7%)
    ppermute x49, waiting for transfers between devices, swap(): return lax.ppermute(array, axes, [(n, n ^ mask) for n in range(devices)])  126 us
    pallas_call x8, Pallas kernels, run(): pl.pallas_call(kernel, name=name, in_specs=[pl.BlockSpec(memory_space=spa...  97.9 us
    ppermute x49, starting transfers between devices, swap(): return lax.ppermute(array, axes, [(n, n ^ mask) for n in range(devices)])  47.6 us
    unnamed x78, local copies, waits for them, and re-layouts  11.7 us
  transfers between devices with their start and end apart: 49, of which 27 were waited for; matrix products, arithmetic and copies ran while one was open for 6% of the time, Pallas kernels for 31%

profile of v1, /device:TPU:0, one launch (start us, length us, event | category | flops | bytes accessed | tf_op | source)
XLA Modules:
  0.0 298.1 jit_solution(12467771810840548363)
XLA Ops:
  2.8 3.0 %collective-permute-start.5 = (bf16[3,256,512]{2,1,0:T(8,128)(2,1)S(1)}, bf16[3,256,512]{2,1,0:T(8,128)(2,1)}, u32[]{:S(2)}, u32[]{:S(2)}) collective-permute-start(bf16[3,256,512]{2,1,0:T(8,128)(2,1)S(1)} %pad_maximum_fusion), channel_id=1, source_target_pairs={{0,1},{1,0},{2,3},{3,2},{4,5},{5,4},{6,7},{7,6},{8,9},{9,8},{10,11... | collective-permute-start | bytes 2359304 | tf_op jit(solution)/shard_map/ppermute | solution.py:402
  5.9 2.7 collective-permute-start
  23.6 2.8 collective-permute-done.2
  30.1 30.6 %collective-permute-done.3 = bf16[128,1536]{1,0:T(8,128)(2,1)S(1)} collective-permute-done((bf16[128,1536]{1,0:T(8,128)(2,1)S(1)}, bf16[128,1536]{1,0:T(8,128)(2,1)S(1)}, u32[]{:S(2)}, u32[]{:S(2)}) %collective-permute-start.3) | collective-permute-done | bytes 393248 | tf_op jit(solution)/shard_map/ppermute | solution.py:402
  62.0 6.3 %collective-permute-done.10 = bf16[128,1536]{1,0:T(8,128)(2,1)S(1)} collective-permute-done((bf16[128,1536]{1,0:T(8,128)(2,1)S(1)}, bf16[128,1536]{1,0:T(8,128)(2,1)S(1)}, u32[]{:S(2)}, u32[]{:S(2)}) %collective-permute-start.10) | collective-permute-done | bytes 393248 | tf_op jit(solution)/shard_map/ppermute | solution.py:402
  74.5 17.0 %layer_0_forward.1 = (bf16[512,1152]{1,0:T(8,128)(2,1)}, f32[512,384]{1,0:T(8,128)}, bf16[512,384]{1,0:T(8,128)(2,1)}, f32[512,512]{1,0:T(8,128)}, bf16[512,512]...) custom-call(s32[4]{0:T(128)} %pad_add_fusion.refs_0_, f32[512,512]{1,0:T(8,128)} %get-tuple-element.56.refs_1_, ...), custom_call_target="tpu_custom_call" | custom-call | flops 2415919104 | bytes 7970832 | tf_op jit(solution)/shard_map/layer_0_forward/pallas_call | solution.py:60
  92.4 13.9 %layer_1_attention.1 = (bf16[512,1152]{1,0:T(8,128)(2,1)}, f32[512,384]{1,0:T(8,128)}, bf16[512,384]{1,0:T(8,128)(2,1)}, f32[512,512]{1,0:T(8,128)}, bf16[512,512]{1,0:T(8,128)(2,1)}) custom-call(s32[4]{0:T(128)} %pad_add_fusion.refs_0_, f32[512,512]{1,0:T(8,128)} %get-tuple-element.59.refs_1_, bf16[512,512]{1,0:T(8,128)(2,1)} %get-tuple-element.60.refs_2_, ...), custom_call_target="tpu_custom_call" | custom-call | flops 805306368 | bytes 3250192 | tf_op jit(solution)/shard_map/layer_1_attention/pallas_call | solution.py:60
  109.1 21.9 %layer_1_backward.1 = (f32[512,512]{1,0:T(8,128)}, bf16[512,512]{1,0:T(8,128)(2,1)}, bf16[512,512]{1,0:T(8,128)(2,1)}, bf16[512,512]{1,0:T(8,128)(2,1)}, f32[1,5...) custom-call(s32[4]{0:T(128)} %pad_add_fusion.refs_0_, ...), custom_call_target="tpu_custom_call" | custom-call | flops 4831838208 | bytes 12324880 | tf_op jit(solution)/shard_map/layer_1_backward/pallas_call | solution.py:60
  131.0 22.2 %layer_0_backward.1 = (f32[512,512]{1,0:T(8,128)}, bf16[512,512]{1,0:T(8,128)(2,1)}, bf16[512,512]{1,0:T(8,128)(2,1)}, bf16[512,512]{1,0:T(8,128)(2,1)}, f32[1,5...) custom-call(s32[4]{0:T(128)} %pad_add_fusion.refs_0_, ...), custom_call_target="tpu_custom_call" | custom-call | flops 4831838208 | bytes 13047824 | tf_op jit(solution)/shard_map/layer_0_backward/pallas_call | solution.py:60
  157.7 3.4 %collective-permute-done.45 = f32[24,128]{1,0:T(8,128)S(1)} collective-permute-done((f32[24,128]{1,0:T(8,128)S(1)}, f32[24,128]{1,0:T(8,128)S(1)}, u32[]{:S(2)}, u32[]{:S(2)}) %collective-permute-start.45) | collective-permute-done | bytes 12320 | tf_op jit(solution)/shard_map/ppermute | solution.py:402
  176.8 7.6 %layer_1_weight_grads.1 = (bf16[8,3,32,512]{3,2,1,0:T(8,128)(2,1)}, bf16[8,3,32,512]{3,2,1,0:T(8,128)(2,1)}) custom-call(s32[4]{0:T(128)} %pad_add_fusion.refs_0_, bf16[512,512]{1,0:T(8,128)(2,1)} %get-tuple-element.65.refs_10_.refs_1_, bf16[512,512]{1,0:T(8,128)(2,1)} %bitcast.7.refs_3_.refs_2_, bf16[512,512]{1,0:T(8,128)(2,1)} %get-tuple-element.85.refs_3_, ...), custom_call_target="tpu_custom_call" | custom-call | flops 1610612736 | bytes 6815760 | tf_op jit(solution)/shard_map/layer_1_weight_grads/pallas_call | solution.py:60
  185.0 8.1 %collective-permute-done.25.refs_7_ = bf16[512,512]{1,0:T(8,128)(2,1)S(1)} collective-permute-done((bf16[512,512]{1,0:T(8,128)(2,1)S(1)}, bf16[512,512]{1,0:T(8,128)(2,1)S(1)}, u32[]{:S(2)}, u32[]{:S(2)}) %collective-permute-start.25) | collective-permute-done | bytes 524320 | tf_op jit(solution)/shard_map/ppermute | solution.py:402
  194.1 7.7 %layer_0_weight_grads.1 = (bf16[8,3,32,512]{3,2,1,0:T(8,128)(2,1)}, bf16[8,3,32,512]{3,2,1,0:T(8,128)(2,1)}) custom-call(s32[4]{0:T(128)} %pad_add_fusion.refs_0_, bf16[512,512]{1,0:T(8,128)(2,1)} %get-tuple-element.72.refs_10_.refs_1_, bf16[512,512]{1,0:T(8,128)(2,1)} %get-tuple-element.79.refs_2_, bf16[512,512]{1,0:T(8,128)(2,1)} %get-tuple-element.80.refs_3_, ...), custom_call_target="tpu_custom_call" | custom-call | flops 1610612736 | bytes 6815760 | tf_op jit(solution)/shard_map/layer_0_weight_grads/pallas_call | solution.py:60
  204.6 9.6 %collective-permute-done.15 = bf16[8,16,1536]{2,1,0:T(8,128)(2,1)S(1)} collective-permute-done((bf16[8,16,1536]{2,1,0:T(8,128)(2,1)S(1)}, bf16[8,16,1536]{2,1,0:T(8,128)(2,1)S(1)}, u32[]{:S(2)}, u32[]{:S(2)}) %collective-permute-start.15) | collective-permute-done | bytes 393248 | tf_op jit(solution)/shard_map/ppermute | solution.py:402
  215.4 6.8 %collective-permute-done.20 = bf16[8,16,1536]{2,1,0:T(8,128)(2,1)S(1)} collective-permute-done((bf16[8,16,1536]{2,1,0:T(8,128)(2,1)S(1)}, bf16[8,16,1536]{2,1,0:T(8,128)(2,1)S(1)}, u32[]{:S(2)}, u32[]{:S(2)}) %collective-permute-start.20) | collective-permute-done | bytes 393248 | tf_op jit(solution)/shard_map/ppermute | solution.py:402
  232.3 6.3 %collective-permute-done.37 = bf16[4,3,32,512]{3,2,1,0:T(8,128)(2,1)S(1)} collective-permute-done((bf16[4,3,32,512]{3,2,1,0:T(8,128)(2,1)S(1)}, bf16[4,3,32,512]{3,2,1,0:T(8,128)(2,1)S(1)}, u32[]{:S(2)}, u32[]{:S(2)}) %collective-permute-start.37) | collective-permute-done | bytes 393248 | tf_op jit(solution)/shard_map/ppermute | solution.py:402
  240.4 5.4 %collective-permute-done.27 = bf16[4,3,32,512]{3,2,1,0:T(8,128)(2,1)S(1)} collective-permute-done((bf16[4,3,32,512]{3,2,1,0:T(8,128)(2,1)S(1)}, bf16[4,3,32,512]{3,2,1,0:T(8,128)(2,1)S(1)}, u32[]{:S(2)}, u32[]{:S(2)}) %collective-permute-start.27) | collective-permute-done | bytes 393248 | tf_op jit(solution)/shard_map/ppermute | solution.py:402
  247.9 5.2 %collective-permute-done.28 = bf16[2,3,32,512]{3,2,1,0:T(8,128)(2,1)S(1)} collective-permute-done((bf16[2,3,32,512]{3,2,1,0:T(8,128)(2,1)S(1)}, bf16[2,3,32,512]{3,2,1,0:T(8,128)(2,1)S(1)}, u32[]{:S(2)}, u32[]{:S(2)}) %collective-permute-start.28) | collective-permute-done | bytes 196640 | tf_op jit(solution)/shard_map/ppermute | solution.py:402
  257.4 4.6 %collective-permute-done.29 = bf16[1,3,32,512]{3,2,1,0:T(8,128)(2,1)S(1)} collective-permute-done((bf16[1,3,32,512]{3,2,1,0:T(8,128)(2,1)S(1)}, bf16[1,3,32,512]{3,2,1,0:T(8,128)(2,1)S(1)}, u32[]{:S(2)}, u32[]{:S(2)}) %collective-permute-start.29) | collective-permute-done | bytes 98336 | tf_op jit(solution)/shard_map/ppermute | solution.py:402
  265.3 3.3 %collective-permute-done.30 = bf16[1,3,32,512]{3,2,1,0:T(8,128)(2,1)S(1)} collective-permute-done((bf16[1,3,32,512]{3,2,1,0:T(8,128)(2,1)S(1)}, bf16[1,3,32,512]{3,2,1,0:T(8,128)(2,1)S(1)}, u32[]{:S(2)}, u32[]{:S(2)}) %collective-permute-start.30) | collective-permute-done | bytes 98336 | tf_op jit(solution)/shard_map/ppermute | solution.py:402
  268.7 2.7 collective-permute-start.23
  277.4 7.8 %collective-permute-done.42 = bf16[4,3,32,512]{3,2,1,0:T(8,128)(2,1)S(1)} collective-permute-done((bf16[4,3,32,512]{3,2,1,0:T(8,128)(2,1)S(1)}, bf16[4,3,32,512]{3,2,1,0:T(8,128)(2,1)S(1)}, u32[]{:S(2)}, u32[]{:S(2)}) %collective-permute-start.42) | collective-permute-done | bytes 393248 | tf_op jit(solution)/shard_map/ppermute | solution.py:402
  285.4 4.4 %collective-permute-done.32 = bf16[4,3,32,512]{3,2,1,0:T(8,128)(2,1)S(1)} collective-permute-done((bf16[4,3,32,512]{3,2,1,0:T(8,128)(2,1)S(1)}, bf16[4,3,32,512]{3,2,1,0:T(8,128)(2,1)S(1)}, u32[]{:S(2)}, u32[]{:S(2)}) %collective-permute-start.32) | collective-permute-done | bytes 393248 | tf_op jit(solution)/shard_map/ppermute | solution.py:402
  293.1 5.0 %finish.1 = (f32[2,512,512]{2,1,0:T(8,128)}, f32[2,512,512]{2,1,0:T(8,128)}, f32[2,512,512]{2,1,0:T(8,128)}) custom-call(s32[4]{0:T(128)} %pad_add_fusion.refs_0_, bf16[8,3,32,512]{3,2,1,0:T(8,128)(2,1)} %copy-done.3, bf16[8,3,32,512]{3,2,1,0:T(8,128)(2,1)} %copy-done.11, bf16[8,3,32,512]{3,2,1,0:T(8,128)(2,1)} %copy-done.2, bf16[8,3,32,512]{3,2,1,0:T(8,128)(2,1)} %copy-done.10), custom_call_target="tpu_custom_call" | custom-call | bytes 3145744 | tf_op jit(solution)/shard_map/finish/pallas_call | solution.py:60
  (229 shorter events, 88.5 us)
Async XLA Ops:
  2.8 58.7 %collective-permute-start.5 = (bf16[3,256,512]{2,1,0:T(8,128)(2,1)S(1)}, bf16[3,256,512]{2,1,0:T(8,128)(2,1)}, u32[]{:S(2)}, u32[]{:S(2)}) collective-permute-start(bf16[3,256,512]{2,1,0:T(8,128)(2,1)S(1)} %pad_maximum_fusion), channel_id=1, source_target_pairs={{0,1},{1,0},{2,3},{3,2},{4,5},{5,4},{6,7},{7,6},{8,9},{9,8},{10,11... | collective-permute-start | bytes 2359304 | tf_op jit(solution)/shard_map/ppermute | solution.py:402
  9.1 59.4 %collective-permute-start.12 = (bf16[3,256,512]{2,1,0:T(8,128)(2,1)S(1)}, bf16[3,256,512]{2,1,0:T(8,128)(2,1)}, u32[]{:S(2)}, u32[]{:S(2)}) collective-permute-start(bf16[3,256,512]{2,1,0:T(8,128)(2,1)S(1)} %pad_maximum_fusion.1), channel_id=1, source_target_pairs={{0,1},{1,0},{2,3},{3,2},{4,5},{5,4},{6,7},{7,6},{8,9},{9,8},{10,11... | collective-permute-start | bytes 2359304 | tf_op jit(solution)/shard_map/ppermute | solution.py:402
  9.6 166.4 %collective-permute-start.35 = (bf16[512,512]{1,0:T(8,128)(2,1)}, bf16[512,512]{1,0:T(8,128)(2,1)}, u32[]{:S(2)}, u32[]{:S(2)}) collective-permute-start(bf16[512,512]{1,0:T(8,128)(2,1)} %bitcast.7.refs_3_.refs_2_), channel_id=1, source_target_pairs={{0,1},{1,0},{2,3},{3,2},{4,5},{5,4},{6,7},{7,6},{8,9},{9,8},{10,11... | collective-permute-start | bytes 1572872 | tf_op jit(solution)/shard_map/ppermute | solution.py:402
  26.5 34.2 %collective-permute-start.3 = (bf16[128,1536]{1,0:T(8,128)(2,1)S(1)}, bf16[128,1536]{1,0:T(8,128)(2,1)S(1)}, u32[]{:S(2)}, u32[]{:S(2)}) collective-permute-start(bf16[128,1536]{1,0:T(8,128)(2,1)S(1)} %pad_maximum_fusion.4), channel_id=1, source_target_pairs={{0,1},{1,0},{2,3},{3,2},{4,5},{5,4},{6,7},{7,6},{8,9},{9,8},{10,11... | collective-permute-start | bytes 1179656 | tf_op jit(solution)/shard_map/ppermute | solution.py:402
  28.6 39.7 %collective-permute-start.10 = (bf16[128,1536]{1,0:T(8,128)(2,1)S(1)}, bf16[128,1536]{1,0:T(8,128)(2,1)S(1)}, u32[]{:S(2)}, u32[]{:S(2)}) collective-permute-start(bf16[128,1536]{1,0:T(8,128)(2,1)S(1)} %pad_maximum_fusion.5), channel_id=1, source_target_pairs={{0,1},{1,0},{2,3},{3,2},{4,5},{5,4},{6,7},{7,6},{8,9},{9,8},{10,11... | collective-permute-start | bytes 1179656 | tf_op jit(solution)/shard_map/ppermute | solution.py:402
  68.4 23.2 %collective-permute-start.11 = (bf16[256,1536]{1,0:T(8,128)(2,1)S(1)}, bf16[256,1536]{1,0:T(8,128)(2,1)S(1)}, u32[]{:S(2)}, u32[]{:S(2)}) collective-permute-start(bf16[256,1536]{1,0:T(8,128)(2,1)S(1)} %constant_dynamic-update-slice_fusion.5.refs_6_.refs_11_), channel_id=1, source_target_pairs={{0,2},{1,3},{2,0},{3,1},{4,6},{5,7},{6,4},{7,5},{8,10},{9,11},{10,... | collective-permute-start | bytes 2359304 | tf_op jit(solution)/shard_map/ppermute | solution.py:402
  68.4 39.7 %collective-permute-start.13 = (bf16[3,256,512]{2,1,0:T(8,128)(2,1)}, bf16[3,256,512]{2,1,0:T(8,128)(2,1)S(1)}, u32[]{:S(2)}, u32[]{:S(2)}) collective-permute-start(bf16[3,256,512]{2,1,0:T(8,128)(2,1)} %collective-permute-done.12.refs_16_), channel_id=1, source_target_pairs={{0,2},{1,3},{2,0},{3,1},{4,6},{5,7},{6,4},{7,5},{8,10},{9,11},{10,... | collective-permute-start | bytes 2359304 | tf_op jit(solution)/shard_map/ppermute | solution.py:402
  106.3 69.7 %collective-permute-start.34 = (bf16[512,512]{1,0:T(8,128)(2,1)}, bf16[512,512]{1,0:T(8,128)(2,1)S(1)}, u32[]{:S(2)}, u32[]{:S(2)}) collective-permute-start(bf16[512,512]{1,0:T(8,128)(2,1)} %get-tuple-element.65.refs_10_.refs_1_), channel_id=1, source_target_pairs={{0,1},{1,0},{2,3},{3,2},{4,5},{5,4},{6,7},{7,6},{8,9},{9,8},{10,11... | collective-permute-start | bytes 1572872 | tf_op jit(solution)/shard_map/ppermute | solution.py:402
  162.7 39.3 %collective-permute-start.14 = (bf16[16,16,1536]{2,1,0:T(8,128)(2,1)}, bf16[16,16,1536]{2,1,0:T(8,128)(2,1)S(1)}, u32[]{:S(2)}, u32[]{:S(2)}) collective-permute-start(bf16[16,16,1536]{2,1,0:T(8,128)(2,1)} %get-tuple-element.76), channel_id=1, source_target_pairs={{0,2},{1,3},{2,0},{3,1},{4,6},{5,7},{6,4},{7,5},{8,10},{9,11},{10,... | collective-permute-start | bytes 2359304 | tf_op jit(solution)/shard_map/ppermute | solution.py:402
  171.1 22.0 %collective-permute-start.24 = (bf16[512,512]{1,0:T(8,128)(2,1)S(1)}, bf16[512,512]{1,0:T(8,128)(2,1)S(1)}, u32[]{:S(2)}, u32[]{:S(2)}) collective-permute-start(bf16[512,512]{1,0:T(8,128)(2,1)S(1)} %copy-done.12), channel_id=1, source_target_pairs={{0,1},{1,0},{2,3},{3,2},{4,5},{5,4},{6,7},{7,6},{8,9},{9,8},{10,11... | collective-permute-start | bytes 1572872 | tf_op jit(solution)/shard_map/ppermute | solution.py:402
  173.1 20.0 %collective-permute-start.25 = (bf16[512,512]{1,0:T(8,128)(2,1)S(1)}, bf16[512,512]{1,0:T(8,128)(2,1)S(1)}, u32[]{:S(2)}, u32[]{:S(2)}) collective-permute-start(bf16[512,512]{1,0:T(8,128)(2,1)S(1)} %copy-done.13), channel_id=1, source_target_pairs={{0,1},{1,0},{2,3},{3,2},{4,5},{5,4},{6,7},{7,6},{8,9},{9,8},{10,11... | collective-permute-start | bytes 1572872 | tf_op jit(solution)/shard_map/ppermute | solution.py:402
  176.0 26.8 %collective-permute-start.19 = (bf16[16,16,1536]{2,1,0:T(8,128)(2,1)}, bf16[16,16,1536]{2,1,0:T(8,128)(2,1)S(1)}, u32[]{:S(2)}, u32[]{:S(2)}) collective-permute-start(bf16[16,16,1536]{2,1,0:T(8,128)(2,1)} %get-tuple-element.78), channel_id=1, source_target_pairs={{0,2},{1,3},{2,0},{3,1},{4,6},{5,7},{6,4},{7,5},{8,10},{9,11},{10,... | collective-permute-start | bytes 2359304 | tf_op jit(solution)/shard_map/ppermute | solution.py:402
  184.5 38.9 %collective-permute-start.36 = (bf16[8,3,32,512]{3,2,1,0:T(8,128)(2,1)}, bf16[8,3,32,512]{3,2,1,0:T(8,128)(2,1)S(1)}, u32[]{:S(2)}, u32[]{:S(2)}) collective-permute-start(bf16[8,3,32,512]{3,2,1,0:T(8,128)(2,1)} %get-tuple-element.89), channel_id=1, source_target_pairs={{0,2},{1,3},{2,0},{3,1},{4,6},{5,7},{6,4},{7,5},{8,10},{9,11},{10,... | collective-permute-start | bytes 2359304 | tf_op jit(solution)/shard_map/ppermute | solution.py:402
  201.8 22.9 %collective-permute-start.26 = (bf16[8,3,32,512]{3,2,1,0:T(8,128)(2,1)}, bf16[8,3,32,512]{3,2,1,0:T(8,128)(2,1)S(1)}, u32[]{:S(2)}, u32[]{:S(2)}) collective-permute-start(bf16[8,3,32,512]{3,2,1,0:T(8,128)(2,1)} %get-tuple-element.84), channel_id=1, source_target_pairs={{0,2},{1,3},{2,0},{3,1},{4,6},{5,7},{6,4},{7,5},{8,10},{9,11},{10,... | collective-permute-start | bytes 2359304 | tf_op jit(solution)/shard_map/ppermute | solution.py:402
  202.2 12.0 %collective-permute-start.15 = (bf16[8,16,1536]{2,1,0:T(8,128)(2,1)S(1)}, bf16[8,16,1536]{2,1,0:T(8,128)(2,1)S(1)}, u32[]{:S(2)}, u32[]{:S(2)}) collective-permute-start(bf16[8,16,1536]{2,1,0:T(8,128)(2,1)S(1)} %get-tuple-element.117), channel_id=1, source_target_pairs={{0,1},{1,0},{2,3},{3,2},{4,5},{5,4},{6,7},{7,6},{8,9},{9,8},{10,11... | collective-permute-start | bytes 1179656 | tf_op jit(solution)/shard_map/ppermute | solution.py:402
  203.2 19.0 %collective-permute-start.20 = (bf16[8,16,1536]{2,1,0:T(8,128)(2,1)S(1)}, bf16[8,16,1536]{2,1,0:T(8,128)(2,1)S(1)}, u32[]{:S(2)}, u32[]{:S(2)}) collective-permute-start(bf16[8,16,1536]{2,1,0:T(8,128)(2,1)S(1)} %get-tuple-element.119), channel_id=1, source_target_pairs={{0,1},{1,0},{2,3},{3,2},{4,5},{5,4},{6,7},{7,6},{8,9},{9,8},{10,11... | collective-permute-start | bytes 1179656 | tf_op jit(solution)/shard_map/ppermute | solution.py:402
  214.3 11.8 %collective-permute-start.16 = (bf16[4,16,1536]{2,1,0:T(8,128)(2,1)S(1)}, bf16[4,16,1536]{2,1,0:T(8,128)(2,1)S(1)}, u32[]{:S(2)}, u32[]{:S(2)}) collective-permute-start(bf16[4,16,1536]{2,1,0:T(8,128)(2,1)S(1)} %get-tuple-element.131), channel_id=1, source_target_pairs={{0,4},{1,5},{2,6},{3,7},{4,0},{5,1},{6,2},{7,3},{8,12},{9,13},{10,... | collective-permute-start | bytes 589832 | tf_op jit(solution)/shard_map/ppermute | solution.py:402
  223.7 14.9 %collective-permute-start.37 = (bf16[4,3,32,512]{3,2,1,0:T(8,128)(2,1)S(1)}, bf16[4,3,32,512]{3,2,1,0:T(8,128)(2,1)S(1)}, u32[]{:S(2)}, u32[]{:S(2)}) collective-permute-start(bf16[4,3,32,512]{3,2,1,0:T(8,128)(2,1)S(1)} %get-tuple-element.113), channel_id=1, source_target_pairs={{0,4},{1,5},{2,6},{3,7},{4,0},{5,1},{6,2},{7,3},{8,12},{9,13},{10,... | collective-permute-start | bytes 1179656 | tf_op jit(solution)/shard_map/ppermute | solution.py:402
  225.0 20.7 %collective-permute-start.27 = (bf16[4,3,32,512]{3,2,1,0:T(8,128)(2,1)S(1)}, bf16[4,3,32,512]{3,2,1,0:T(8,128)(2,1)S(1)}, u32[]{:S(2)}, u32[]{:S(2)}) collective-permute-start(bf16[4,3,32,512]{3,2,1,0:T(8,128)(2,1)S(1)} %get-tuple-element.115), channel_id=1, source_target_pairs={{0,4},{1,5},{2,6},{3,7},{4,0},{5,1},{6,2},{7,3},{8,12},{9,13},{10,... | collective-permute-start | bytes 1179656 | tf_op jit(solution)/shard_map/ppermute | solution.py:402
  230.2 38.5 %collective-permute-start.22 = (bf16[2,16,1536]{2,1,0:T(8,128)(2,1)S(1)}, bf16[2,16,1536]{2,1,0:T(8,128)(2,1)S(1)}, u32[]{:S(2)}, u32[]{:S(2)}) collective-permute-start(bf16[2,16,1536]{2,1,0:T(8,128)(2,1)S(1)} %get-tuple-element.137), channel_id=1, source_target_pairs={{0,8},{1,9},{2,10},{3,11},{4,12},{5,13},{6,14},{7,15},{8,0},{9,1},... | collective-permute-start | bytes 294920 | tf_op jit(solution)/shard_map/ppermute | solution.py:402
  231.9 45.5 %collective-permute-start.18 = (bf16[1,16,1536]{2,1,0:T(8,128)(2,1)S(1)}, bf16[1,16,1536]{2,1,0:T(8,128)(2,1)S(1)}, u32[]{:S(2)}, u32[]{:S(2)}) collective-permute-start(bf16[1,16,1536]{2,1,0:T(8,128)(2,1)S(1)} %add_convert_fusion.30), channel_id=1, source_target_pairs={{0,16},{1,17},{2,18},{3,19},{4,20},{5,21},{6,22},{7,23},{8,24},{9,... | collective-permute-start | bytes 147464 | tf_op jit(solution)/shard_map/ppermute | solution.py:402
  268.7 21.2 %collective-permute-start.23 = (bf16[1,16,1536]{2,1,0:T(8,128)(2,1)S(1)}, bf16[1,16,1536]{2,1,0:T(8,128)(2,1)S(1)}, u32[]{:S(2)}, u32[]{:S(2)}) collective-permute-start(bf16[1,16,1536]{2,1,0:T(8,128)(2,1)S(1)} %add_convert_fusion.27), channel_id=1, source_target_pairs={{0,16},{1,17},{2,18},{3,19},{4,20},{5,21},{6,22},{7,23},{8,24},{9,... | collective-permute-start | bytes 147464 | tf_op jit(solution)/shard_map/ppermute | solution.py:402
  273.1 12.1 %collective-permute-start.42 = (bf16[4,3,32,512]{3,2,1,0:T(8,128)(2,1)S(1)}, bf16[4,3,32,512]{3,2,1,0:T(8,128)(2,1)S(1)}, u32[]{:S(2)}, u32[]{:S(2)}) collective-permute-start(bf16[4,3,32,512]{3,2,1,0:T(8,128)(2,1)S(1)} %pad_maximum_fusion.7), channel_id=1, source_target_pairs={{0,4},{1,5},{2,6},{3,7},{4,0},{5,1},{6,2},{7,3},{8,12},{9,13},{10,... | collective-permute-start | bytes 1179656 | tf_op jit(solution)/shard_map/ppermute | solution.py:402
  276.3 13.5 %collective-permute-start.32 = (bf16[4,3,32,512]{3,2,1,0:T(8,128)(2,1)S(1)}, bf16[4,3,32,512]{3,2,1,0:T(8,128)(2,1)S(1)}, u32[]{:S(2)}, u32[]{:S(2)}) collective-permute-start(bf16[4,3,32,512]{3,2,1,0:T(8,128)(2,1)S(1)} %pad_maximum_fusion.6), channel_id=1, source_target_pairs={{0,4},{1,5},{2,6},{3,7},{4,0},{5,1},{6,2},{7,3},{8,12},{9,13},{10,... | collective-permute-start | bytes 1179656 | tf_op jit(solution)/shard_map/ppermute | solution.py:402
  (57 other events, 512.1 us)

commit v2 on v1

v2 whole, which is shorter than its diff:
```python
import functools
import types

import jax
import jax.numpy as jnp
from jax import lax
from jax.experimental import pallas as pl
from jax.experimental.pallas import tpu as pltpu
from jax.sharding import PartitionSpec as P

norm_eps = 1e-06
masked_score = -1e30
bf16 = jnp.bfloat16
f32 = jnp.float32
axes = ("dp", "tensor")
vmem_bytes = 56 * 1024 * 1024
raw_names = ("attn_near", "attn_far", "ff_near", "ff_far", "w_gate", "w_up", "w_down")


def dot_nn(left, right):
    return lax.dot_general(left, right, (((1,), (0,)), ((), ())), preferred_element_type=f32)


def dot_nt(left, right):
    return lax.dot_general(left, right, (((1,), (1,)), ((), ())), preferred_element_type=f32)


def dot_tn(left, right):
    return lax.dot_general(left, right, (((0,), (0,)), ((), ())), preferred_element_type=f32)


def inverse_rms(values):
    return lax.rsqrt(jnp.mean(values * values, axis=-1, keepdims=True) + norm_eps)


def norm_back(values, gain, grad_out):
    scale = inverse_rms(values)
    pulled = grad_out * gain
    mean_part = jnp.mean(pulled * values, axis=-1, keepdims=True)
    grad_in = scale * pulled - values * (scale * scale * scale) * mean_part
    return grad_in, jnp.sum(grad_out * values * scale, axis=0, keepdims=True)


def gelu_terms(gate_act):
    square = gate_act * gate_act
    bent = jnp.tanh(0.7978845608028654 * gate_act * (1.0 + 0.044715 * square))
    half = 0.5 * (1.0 + bent)
    slope = half + 0.5 * gate_act * (1.0 - bent * bent) * (
        0.7978845608028654 * (1.0 + 3.0 * 0.044715 * square)
    )
    return gate_act * half, slope


def run(body, name, ins, outs, scratch, after=(), flops=0):
    in_names, out_names, scratch_names = list(ins), list(outs), list(scratch)
    staged = [n for n in in_names if n != "place" and n not in raw_names]
    in_sems = {n: i for i, n in enumerate(staged)}
    out_sems = {n: i for i, n in enumerate(out_names)}

    def kernel(*refs):
        refs = list(refs)
        sources = dict(zip(in_names, refs))
        refs = refs[len(in_names) + len(after) :]
        targets = dict(zip(out_names, refs))
        refs = refs[len(out_names) :]
        space = dict(zip(scratch_names, refs))
        refs = refs[len(scratch_names) :]
        buffers = dict(zip(staged + out_names, refs))
        sems_in, sems_out = refs[len(staged) + len(out_names) :]
        r = types.SimpleNamespace(**space, **buffers)
        for n in in_names:
            if n == "place" or n in raw_names:
                setattr(r, n, sources[n])

        def copy_in(n):
            return pltpu.make_async_copy(sources[n], buffers[n], sems_in.at[in_sems[n]])

        def copy_out(n):
            return pltpu.make_async_copy(buffers[n], targets[n], sems_out.at[out_sems[n]])

        r.fetch = lambda *names: [copy_in(n).start() for n in names]
        r.need = lambda *names: [copy_in(n).wait() for n in names]
        r.write = lambda *names: [copy_out(n).start() for n in names]
        r.drain = lambda *names: [copy_out(n).wait() for n in names]
        body(r)

    moved = sum(a.size * a.dtype.itemsize for a in ins.values())
    results = pl.pallas_call(
        kernel,
        name=name,
        in_specs=[
            pl.BlockSpec(memory_space=pltpu.SMEM if n == "place" else pl.ANY) for n in in_names
        ]
        + [pl.BlockSpec(memory_space=pl.ANY) for _ in after],
        out_specs=[pl.BlockSpec(memory_space=pl.ANY) for _ in outs],
        out_shape=[jax.ShapeDtypeStruct(shape, kind) for shape, kind in outs.values()],
        scratch_shapes=list(scratch.values())
        + [pltpu.VMEM(ins[n].shape, ins[n].dtype) for n in staged]
        + [pltpu.VMEM(shape, kind) for shape, kind in outs.values()]
        + [pltpu.SemaphoreType.DMA((max(1, len(staged)),)), pltpu.SemaphoreType.DMA((len(outs),))],
        compiler_params=pltpu.CompilerParams(vmem_limit_bytes=vmem_bytes),
        cost_estimate=pl.CostEstimate(flops=flops, bytes_accessed=moved, transcendentals=0),
    )(*ins.values(), *after)
    return types.SimpleNamespace(**dict(zip(outs, results)))


def chunks(extent, size):
    size = min(size, extent)
    return [slice(start, start + size) for start in range(0, extent, size)]


def attention_copies(r, masks, rows):
    copies = []
    for idx, mask in enumerate(masks):
        half, at = divmod(idx, max(1, len(masks) // 2))
        source = (r.attn_near if half == 0 else r.attn_far).at[pl.ds(at * rows, rows)]
        place = (r.place[0] ^ mask) * rows if len(masks) > 1 else 0
        target = r.attn_w.at[pl.ds(pl.multiple_of(place, rows), rows)]
        copies.append(pltpu.make_async_copy(source, target, r.attn_sem))
    return copies


def ff_copies(r, layer_idx):
    width = r.ff_down.shape[-1]
    copies = []
    for k, own in enumerate((r.w_gate, r.w_up)):
        target = r.ff_gate_up.at[0, :, pl.ds(k * width, width)]
        copies.append(pltpu.make_async_copy(own.at[layer_idx], target, r.ff_sem))
    copies.append(pltpu.make_async_copy(r.w_down.at[layer_idx], r.ff_down.at[0], r.ff_sem))
    part = r.ff_near.shape[1]
    for source, base in ((r.ff_near, 0), (r.ff_far, 1)):
        for m in range(2):
            rows = pl.ds(pl.multiple_of((r.place[1] ^ (2 * m + base)) * part, part), part)
            for k in range(2):
                target = r.ff_gate_up.at[1, rows, pl.ds(k * width, width)]
                copies.append(pltpu.make_async_copy(source.at[3 * m + k], target, r.ff_sem))
            copies.append(
                pltpu.make_async_copy(source.at[3 * m + 2], r.ff_down.at[1, rows], r.ff_sem)
            )
    return copies


def start_all(copies):
    for copy in copies:
        copy.start()


def wait_all(sem, *buffers):
    for whole in buffers:
        pltpu.make_async_copy(whole, whole, sem).wait()


def lane_low(rows):
    return lax.broadcasted_iota(jnp.int32, (rows, 128), 1) < 64


def lane_halves():
    low = lane_low(1).astype(f32)
    return low.astype(bf16), (1.0 - low).astype(bf16)


def pair_blocks(rows, low, high):
    return jnp.concatenate([rows * low, rows * high], axis=0)


def own_blocks(both, is_low):
    half = both.shape[0] // 2
    return jnp.where(is_low, both[:half], both[half:]).astype(bf16)


def attention_forward(r, x_ref, a_ref, sizes):
    series, slots, inner = sizes
    rows = series * slots
    for part in chunks(rows, 256):
        r.qkv[part, :] = dot_nn(a_ref[part, :], r.attn_w[:, : 3 * inner]).astype(bf16)
    r.write("qkv")
    is_low = lane_low(slots)
    low, high = lane_halves()
    for s in range(series):
        here = slice(s * slots, (s + 1) * slots)
        keep = r.mask[here, :] == 1
        for start in range(0, inner, 128):
            at = slice(start, start + 128)
            query = r.qkv[here, at]
            keys = r.qkv[here, inner + start : inner + start + 128]
            scores = dot_nt(keys, pair_blocks(query, low, high)) + r.bias[:, at]
            scores = jnp.where(keep, scores, masked_score)
            exps = jnp.exp(scores - jnp.max(scores, axis=0, keepdims=True))
            r.probs[here, at] = exps / jnp.sum(exps, axis=0, keepdims=True)
    r.write("probs")
    for s in range(series):
        here = slice(s * slots, (s + 1) * slots)
        for start in range(0, inner, 128):
            at = slice(start, start + 128)
            values = r.qkv[here, 2 * inner + start : 2 * inner + start + 128]
            both = dot_tn(r.probs[here, at].astype(bf16), values)
            r.heads[here, at] = own_blocks(both, is_low)
    r.write("heads")
    for part in chunks(rows, 256):
        middle = x_ref[part, :] + dot_nt(r.heads[part, :], r.attn_w[:, 3 * inner :])
        r.middle[part, :] = middle
        r.ff_in[part, :] = (middle * inverse_rms(middle) * r.gain_ff[...]).astype(bf16)
    r.write("middle", "ff_in")


attn_out_names = ("qkv", "probs", "heads", "middle", "ff_in")


def prepare_body(r):
    r.fetch("inputs", "marks", "embed", "gain", "buckets", "table")
    r.need("inputs", "marks", "embed", "gain", "buckets", "table")
    x = jnp.where(r.marks[:, 0:1] == 1, r.inputs[...].astype(f32), r.embed[...])
    r.x[...] = x
    r.a[...] = (x * inverse_rms(x) * r.gain[...]).astype(bf16)
    buckets = r.buckets[...]
    bias = jnp.zeros(buckets.shape, f32)
    for idx in range(r.table.shape[0]):
        bias = jnp.where(buckets == idx, r.table[idx : idx + 1, :], bias)
    r.bias[...] = bias
    r.mask[...] = jnp.broadcast_to(r.marks[:, 1:2], r.mask.shape)
    r.write("x", "a", "bias", "mask")
    r.drain("x", "a", "bias", "mask")


def first_body(r, sizes, masks, grain):
    r.fetch("a")
    start_all(attention_copies(r, masks, grain))
    r.fetch("bias", "mask", "x", "gain_ff", "gain_next")
    start_all(ff_copies(r, 0))
    r.need("a")
    wait_all(r.attn_sem, r.attn_w)
    r.need("bias", "mask", "x", "gain_ff", "gain_next")
    attention_forward(r, r.x, r.a, sizes)
    wait_all(r.ff_sem, r.ff_gate_up, r.ff_down)
    width = r.x.shape[1]
    for part in chunks(r.x.shape[0], 256):
        x_next = r.middle[part, :]
        for half in range(2):
            both = dot_nn(r.ff_in[part, :], r.ff_gate_up[half])
            hidden = (gelu_terms(both[:, :width])[0] * both[:, width:]).astype(bf16)
            x_next = x_next + dot_nn(hidden, r.ff_down[half])
        r.x_next[part, :] = x_next
        r.a_next[part, :] = (x_next * inverse_rms(x_next) * r.gain_next[...]).astype(bf16)
    r.write("x_next", "a_next")
    r.drain(*attn_out_names, "x_next", "a_next")


def second_body(r, sizes, masks, grain):
    r.fetch("a")
    start_all(attention_copies(r, masks, grain))
    r.fetch("bias", "mask", "x", "gain_ff")
    r.need("a")
    wait_all(r.attn_sem, r.attn_w)
    r.need("bias", "mask", "x", "gain_ff")
    attention_forward(r, r.x, r.a, sizes)
    r.drain(*attn_out_names)


def backward_body(r, sizes, masks, grain, layer_idx, last, piece_masks, heads):
    series, slots, inner = sizes
    rows = series * slots
    width = r.x.shape[1]
    r.fetch("grad", "ff_in", "gain_ff", "gain_attn")
    start_all(ff_copies(r, layer_idx))
    r.fetch("middle")
    start_all(attention_copies(r, masks, grain))
    r.fetch("qkv", "probs", "heads", "a", "x")
    if not last:
        r.fetch("bias_before", "marks", "buckets", "small_before")
    r.need("grad", "ff_in", "gain_ff", "gain_attn")
    if not last:
        r.need("small_before")
        r.small[...] = r.small_before[...]
    wait_all(r.ff_sem, r.ff_gate_up, r.ff_down)
    r.need("middle")
    gain_total = jnp.zeros((1, width), f32)
    for part in chunks(rows, 256):
        grad = r.grad[part, :].astype(f32)
        rounded = grad.astype(bf16)
        ff_rows = r.ff_in[part, :]
        back = None
        middle = r.middle[part, :]
        total = middle
        for half in range(2):
            both = dot_nn(ff_rows, r.ff_gate_up[half])
            grad_hidden = dot_nt(rounded, r.ff_down[half])
            gate_act, up_act = both[:, :width], both[:, width:]
            mixed, slope = gelu_terms(gate_act)
            if half == 0:
                r.grad_gate_up[part, :width] = (grad_hidden * up_act * slope).astype(bf16)
                r.grad_gate_up[part, width:] = (grad_hidden * mixed).astype(bf16)
                pulled = r.grad_gate_up[part, :]
            else:
                r.pulled[:, :width] = (grad_hidden * up_act * slope).astype(bf16)
                r.pulled[:, width:] = (grad_hidden * mixed).astype(bf16)
                pulled = r.pulled[...]
            hidden = (mixed * up_act).astype(bf16)
            if half == 0:
                r.hidden[part, :] = hidden
            if last:
                total = total + dot_nn(hidden, r.ff_down[half])
            term = dot_nt(pulled, r.ff_gate_up[half])
            back = term if back is None else back + term
        if last:
            r.outputs[part, :] = total.astype(bf16)
        grad_mid, gain_part = norm_back(middle, r.gain_ff[...], back)
        gain_total += gain_part
        grad_mid = grad + grad_mid
        r.grad_mid[part, :] = grad_mid
        r.branch[part, :] = grad_mid.astype(bf16)
    if last:
        r.small[...] = jnp.zeros(r.small.shape, f32)
    put_row(r.small, 2 + layer_idx, gain_total)
    r.write("hidden", "grad_gate_up")
    if last:
        r.write("outputs")
    wait_all(r.attn_sem, r.attn_w)
    for part in chunks(rows, 256):
        r.grad_heads[part, :] = dot_nn(r.branch[part, :], r.attn_w[:, 3 * inner :]).astype(bf16)
    r.need("qkv", "probs", "heads", "a", "x")
    if not last:
        r.need("bias_before", "marks", "buckets")
    is_low = lane_low(slots)
    low, high = lane_halves()
    for start in range(0, inner, 128):
        at = slice(start, start + 128)
        bias_total = jnp.zeros((slots, 128), f32) if last else r.bias_before[:, at]
        for s in range(series):
            here = slice(s * slots, (s + 1) * slots)
            probs = r.probs[here, at]
            values = r.qkv[here, 2 * inner + start : 2 * inner + start + 128]
            grad_probs = dot_nt(values, pair_blocks(r.grad_heads[here, at], low, high))
            inner_sum = jnp.sum(probs * grad_probs, axis=0, keepdims=True)
            grad_scores = (probs * (grad_probs - inner_sum)).astype(bf16)
            r.grad_scores[here, at] = grad_scores
            bias_total = bias_total + grad_scores.astype(f32)
        r.bias_acc[:, at] = bias_total
    for s in range(series):
        here = slice(s * slots, (s + 1) * slots)
        for start in range(0, inner, 128):
            at = slice(start, start + 128)
            key_at = slice(inner + start, inner + start + 128)
            value_at = slice(2 * inner + start, 2 * inner + start + 128)
            grad_scores = r.grad_scores[here, at]
            r.grad_qkv[here, key_at] = dot_nn(
                grad_scores, pair_blocks(r.qkv[here, at], low, high)
            ).astype(bf16)
            r.grad_qkv[here, value_at] = dot_nn(
                r.probs[here, at].astype(bf16), pair_blocks(r.grad_heads[here, at], low, high)
            ).astype(bf16)
            r.grad_qkv[here, at] = own_blocks(dot_tn(grad_scores, r.qkv[here, key_at]), is_low)
    r.attn_grad[:, : 3 * inner] = dot_tn(r.a[...], r.grad_qkv[...])
    r.attn_grad[:, 3 * inner :] = dot_tn(r.branch[...], r.heads[...])
    scatter_pieces(r.attn_grad, r.attn_keep, r.attn_send, piece_masks, r.place[2])
    r.write("attn_send", "attn_keep")
    gain_total = jnp.zeros((1, width), f32)
    embed_total = jnp.zeros((1, width), f32)
    for part in chunks(rows, 256):
        grad_normed = dot_nt(r.grad_qkv[part, :], r.attn_w[:, : 3 * inner])
        grad_in, gain_part = norm_back(r.x[part, :], r.gain_attn[...], grad_normed)
        gain_total += gain_part
        grad_in = r.grad_mid[part, :] + grad_in
        if last:
            r.grad_next[part, :] = grad_in
            r.grad_next_low[part, :] = grad_in.astype(bf16)
        else:
            seen = r.marks[part, 0:1] == 1
            r.grad_next[part, :] = jnp.where(seen, grad_in, 0.0)
            embed_total += jnp.sum(jnp.where(seen, 0.0, grad_in), axis=0, keepdims=True)
    put_row(r.small, layer_idx, gain_total)
    r.write("grad_next")
    if last:
        r.write("grad_next_low", "bias_acc", "small")
    else:
        put_row(r.small, 4, embed_total)
        head_size = inner // heads
        for idx in range(r.table_rows.shape[0]):
            chosen = jnp.where(r.buckets[...] == idx, r.bias_acc[...], 0.0)
            r.table_rows[idx : idx + 1, :] = jnp.sum(chosen, axis=0, keepdims=True)
        lane = lax.broadcasted_iota(jnp.int32, (r.table_rows.shape[0], 128), 1)
        table = jnp.zeros(lane.shape, f32)
        for head in range(heads):
            cut = r.table_rows[:, head * head_size : (head + 1) * head_size]
            table = jnp.where(lane == head, jnp.sum(cut, axis=1, keepdims=True), table)
        r.small[small_rows(width) :, :] = table
        r.write("small")
    r.drain("hidden", "grad_gate_up", "attn_send", "attn_keep", "grad_next", "small")
    if last:
        r.drain("outputs", "grad_next_low", "bias_acc")


def small_rows(width):
    return -(-5 * width // 1024) * 8


def put_row(packed, which, row):
    lanes = row.shape[1] // 128
    for k in range(lanes):
        packed[which * lanes + k : which * lanes + k + 1, :] = row[:, k * 128 : (k + 1) * 128]


def scatter_pieces(whole, keep, send, masks, place):
    count = len(masks)
    grain = whole.shape[0] // count
    for idx, mask in enumerate(masks):
        target = keep if idx < count // 2 else send
        source = pl.ds(pl.multiple_of((place ^ mask) * grain, grain), grain)
        target[idx % (count // 2)] = whole[source, :].astype(bf16)


def weight_body(r, layer_idx, piece_masks):
    width = r.ff_in.shape[1]
    rows = r.ff_in.shape[0]
    r.fetch("peer_in", "peer_grad")
    copies = [
        pltpu.make_async_copy(
            own.at[layer_idx], r.ff_gate_up.at[:, pl.ds(k * width, width)], r.ff_sem
        )
        for k, own in enumerate((r.w_gate, r.w_up))
    ]
    copies.append(pltpu.make_async_copy(r.w_down.at[layer_idx], r.ff_down, r.ff_sem))
    start_all(copies)
    r.fetch("ff_in", "grad_gate_up", "hidden", "grad")
    r.need("peer_in", "peer_grad")
    wait_all(r.ff_sem, r.ff_gate_up, r.ff_down)
    for part in chunks(rows, 256):
        both = dot_nn(r.peer_in[part, :], r.ff_gate_up[...])
        grad_hidden = dot_nt(r.peer_grad[part, :], r.ff_down[...])
        gate_act, up_act = both[:, :width], both[:, width:]
        mixed, slope = gelu_terms(gate_act)
        r.peer_gate_up[part, :width] = (grad_hidden * up_act * slope).astype(bf16)
        r.peer_gate_up[part, width:] = (grad_hidden * mixed).astype(bf16)
        r.peer_hidden[part, :] = (mixed * up_act).astype(bf16)
    r.need("ff_in", "grad_gate_up", "hidden", "grad")
    r.ff_grad[:, : 2 * width] = dot_tn(r.ff_in[...], r.grad_gate_up[...]) + dot_tn(
        r.peer_in[...], r.peer_gate_up[...]
    )
    r.ff_grad[:, 2 * width :] = dot_tn(r.hidden[...], r.grad[...]) + dot_tn(
        r.peer_hidden[...], r.peer_grad[...]
    )
    scatter_pieces(r.ff_grad, r.ff_keep, r.ff_send, piece_masks, r.place[3])
    r.write("ff_send", "ff_keep")
    r.drain("ff_send", "ff_keep")


def finish(pieces, masks, layer_idx, place, shape, before=()):
    grain, width = pieces.shape[1], shape[-1]
    count = len(before)

    def kernel(place_ref, source, *refs):
        outs = refs[count : count + 3]
        held, stage, in_sem, out_sem = refs[count + 3 :]
        copy_in = pltpu.make_async_copy(source, held, in_sem)
        copy_in.start()
        copy_in.wait()
        for idx, mask in enumerate(masks):
            rows = pl.ds(pl.multiple_of((place_ref[3] ^ mask) * grain, grain), grain)
            for k, out in enumerate(outs):
                stage[k, idx] = held[idx, :, k * width : (k + 1) * width].astype(f32)
                pltpu.make_async_copy(stage.at[k, idx], out.at[layer_idx, rows], out_sem).start()
        pltpu.make_async_copy(stage, stage, out_sem).wait()

    return pl.pallas_call(
        kernel,
        name="layer_%d_ff_grads" % layer_idx,
        in_specs=[pl.BlockSpec(memory_space=pltpu.SMEM)]
        + [pl.BlockSpec(memory_space=pl.ANY)] * (1 + count),
        out_specs=[pl.BlockSpec(memory_space=pl.ANY)] * 3,
        out_shape=[jax.ShapeDtypeStruct(shape, f32)] * 3,
        input_output_aliases={2 + k: k for k in range(count)},
        scratch_shapes=[
            pltpu.VMEM(pieces.shape, bf16),
            pltpu.VMEM((3, len(masks), grain, width), f32),
            pltpu.SemaphoreType.DMA,
            pltpu.SemaphoreType.DMA,
        ],
        compiler_params=pltpu.CompilerParams(vmem_limit_bytes=vmem_bytes),
    )(place, pieces, *before)


def small_body(r):
    r.fetch("packed")
    r.need("packed")
    lanes = r.embed.shape[1] // 128
    for which in range(5):
        out, row = ((r.gain_attn, which), (r.gain_ff, which - 2), (r.embed, 0))[which // 2]
        for k in range(lanes):
            at = which * lanes + k
            out[row : row + 1, k * 128 : (k + 1) * 128] = r.packed[at : at + 1, :]
    r.table[...] = r.packed[small_rows(r.embed.shape[1]) :, : r.table.shape[1]]
    r.write("gain_attn", "gain_ff", "embed", "table")
    r.drain("gain_attn", "gain_ff", "embed", "table")


def order_masks(hops):
    masks = [0]
    for hop in reversed(hops):
        masks = masks + [mask ^ hop for mask in masks]
    return masks


def tie(value, *others):
    return lax.optimization_barrier((value, *others))[0]


def on_device(
    inputs,
    cotangent,
    attention_mask,
    patch_valid,
    buckets,
    mask_embed,
    w_query,
    w_key,
    w_value,
    w_output,
    w_gate,
    w_up,
    w_down,
    gain_attn,
    gain_ff,
    bias_table,
    dp_size,
):
    series, slots, width = inputs.shape
    heads = bias_table.shape[1]
    inner = w_query.shape[2]
    rows = series * slots
    sizes = (series, slots, inner)
    matrix = (rows, width)
    devices = 2 * dp_size
    dp_at = lax.axis_index("dp")
    device_at = 2 * dp_at + lax.axis_index("tensor")
    cotangent = cotangent.reshape(matrix)

    def swap(array, mask):
        return lax.ppermute(array, axes, [(n, n ^ mask) for n in range(devices)])

    def join(left, right):
        return jnp.concatenate([left, right], axis=0)

    bits = [1 << k for k in range(devices.bit_length() - 1)]

    attn_grain = max(16, width // devices)
    attn_count = width // attn_grain
    ff_grain = max(16, width // dp_size)
    ff_count = width // ff_grain
    quarter_at = lax.rem(dp_at, 4)
    place = jnp.stack(
        [
            device_at,
            quarter_at,
            device_at // (devices // attn_count),
            lax.rem(dp_at, ff_count),
        ]
    ).astype(jnp.int32)

    quarter = width // 4
    packed = jnp.concatenate([w_query, w_key, w_value, jnp.swapaxes(w_output, 1, 2)], axis=2)
    ff_blocks = jnp.concatenate(
        [
            lax.dynamic_slice_in_dim(tie(w, packed), quarter_at * quarter, quarter, axis=1)
            for w in (w_gate, w_up, w_down)
        ],
        axis=0,
    )
    ff_quarter = swap(ff_blocks, 1).reshape(3, 2, quarter, width)

    wide_buckets = jnp.tile(buckets.T, (1, heads))
    wide_table = jnp.repeat(bias_table, slots, axis=1)
    marks = jnp.stack([patch_valid.reshape(rows), attention_mask.reshape(rows)], axis=1)

    start = run(
        prepare_body,
        "prepare",
        dict(
            inputs=inputs.reshape(matrix),
            marks=marks,
            embed=mask_embed[None, :],
            gain=gain_attn[0:1],
            buckets=wide_buckets,
            table=wide_table,
        ),
        dict(
            x=(matrix, f32),
            a=(matrix, bf16),
            bias=((slots, heads * slots), f32),
            mask=((rows, 128), jnp.int32),
        ),
        {},
    )

    own_rows = packed.shape[1]
    direct = own_rows % 16 == 0
    far = bits[2:]
    if direct:
        hops_0 = far[1:][::-1] + far[:1] + [1, 2]
        hops_1 = [1] + far + [2]
        block_0, block_1 = packed[0], packed[1]
        got_0 = got_1 = None
        for step, (hop_0, hop_1) in enumerate(zip(hops_0, hops_1)):
            if step + 1 == len(hops_0):
                break
            got_0, got_1 = swap(block_0, hop_0), swap(block_1, hop_1)
            if step + 2 == len(hops_0):
                before_last = block_0
                got_0 = tie(got_0, start.a)
            block_0, block_1 = join(block_0, got_0), join(block_1, got_1)
        ff_0 = ff_quarter[:, 0]
        ff_0 = join(ff_0, swap(tie(ff_0, before_last), 4))
        ff_1 = tie(ff_quarter[:, 1], block_0)
        ff_1 = join(ff_1, swap(ff_1, 4))
        attn_pieces = [
            (block_0, swap(block_0, 2), order_masks(hops_0[::-1])),
            (block_1, swap(block_1, 2), order_masks(hops_1[::-1])),
        ]
    else:
        ff_0, ff_1 = (
            join(ff_quarter[:, layer_idx], swap(ff_quarter[:, layer_idx], 4))
            for layer_idx in range(2)
        )
        attn_pieces = []
        for layer_idx in range(2):
            whole = lax.all_gather(packed[layer_idx], axes, axis=0, tiled=True)
            attn_pieces.append((whole, whole, [0]))
    ff_pieces = [(ff_0, swap(ff_0, 2)), (ff_1, swap(ff_1, 2))]

    def attn_ins(layer_idx):
        near, far, masks = attn_pieces[layer_idx]
        return dict(attn_near=near, attn_far=far), masks

    def ff_ins(layer_idx):
        near, far = ff_pieces[layer_idx]
        return dict(w_gate=w_gate, w_up=w_up, w_down=w_down, ff_near=near, ff_far=far)

    attn_scratch = dict(
        attn_w=pltpu.VMEM((width, 4 * inner), bf16), attn_sem=pltpu.SemaphoreType.DMA
    )
    ff_scratch = dict(
        ff_gate_up=pltpu.VMEM((2, width, 2 * width), bf16),
        ff_down=pltpu.VMEM((2, width, width), bf16),
        ff_sem=pltpu.SemaphoreType.DMA,
    )
    grain = own_rows if direct else width
    attn_outs = dict(
        qkv=((rows, 3 * inner), bf16),
        probs=((rows, heads * slots), f32),
        heads=((rows, inner), bf16),
        middle=(matrix, f32),
        ff_in=(matrix, bf16),
    )
    attn_flops = 2 * rows * width * 4 * inner
    ff_flops = 2 * rows * width * 6 * width

    pieces, masks = attn_ins(0)
    first = run(
        functools.partial(first_body, sizes=sizes, masks=masks, grain=grain),
        "layer_0_forward",
        dict(
            place=place,
            x=start.x,
            a=start.a,
            bias=start.bias,
            mask=start.mask,
            gain_ff=gain_ff[0:1],
            gain_next=gain_attn[1:2],
            **pieces,
            **ff_ins(0),
        ),
        dict(**attn_outs, x_next=(matrix, f32), a_next=(matrix, bf16)),
        dict(**attn_scratch, **ff_scratch),
        flops=attn_flops + ff_flops,
    )
    peer_in_0 = swap(first.ff_in, 1)
    pieces, masks = attn_ins(1)
    second = run(
        functools.partial(second_body, sizes=sizes, masks=masks, grain=grain),
        "layer_1_attention",
        dict(
            place=place,
            x=first.x_next,
            a=first.a_next,
            bias=start.bias,
            mask=start.mask,
            gain_ff=gain_ff[1:2],
            **pieces,
        ),
        attn_outs,
        attn_scratch,
        flops=attn_flops,
    )
    peer_in_1 = swap(second.ff_in, 1)
    peer_cotangent = swap(tie(cotangent, second.ff_in), 1)

    attn_hops = [2, 1] + bits[2:]
    attn_low = devices // attn_count
    attn_split = [hop for hop in attn_hops if hop >= attn_low]
    attn_whole = [hop for hop in attn_hops if hop < attn_low]
    ff_hops = bits[1:]
    ff_split = [hop for hop in ff_hops if hop // 2 < ff_count]
    ff_whole = [hop for hop in ff_hops if hop // 2 >= ff_count]
    attn_masks = [mask // attn_low for mask in order_masks(attn_split)]
    ff_masks = [mask // 2 for mask in order_masks(ff_split)]
    attn_half = (attn_count // 2, attn_grain, 4 * inner)
    ff_half = (ff_count // 2, ff_grain, 3 * width)
    small_shape = (small_rows(width) + bias_table.shape[0], 128)

    def backward(layer_idx, kept, x, a, grad, extra_ins, extra_outs, extra_scratch, after=()):
        last = layer_idx == 1
        pieces, masks = attn_ins(layer_idx)
        return run(
            functools.partial(
                backward_body,
                sizes=sizes,
                masks=masks,
                grain=grain,
                layer_idx=layer_idx,
                last=last,
                piece_masks=attn_masks,
                heads=heads,
            ),
            "layer_%d_backward" % layer_idx,
            dict(
                place=place,
                x=x,
                a=a,
                grad=grad,
                gain_attn=gain_attn[layer_idx : layer_idx + 1],
                gain_ff=gain_ff[layer_idx : layer_idx + 1],
                qkv=kept.qkv,
                probs=kept.probs,
                heads=kept.heads,
                middle=kept.middle,
                ff_in=kept.ff_in,
                **pieces,
                **ff_ins(layer_idx),
                **extra_ins,
            ),
            dict(
                grad_next=(matrix, f32),
                hidden=(matrix, bf16),
                grad_gate_up=((rows, 2 * width), bf16),
                small=(small_shape, f32),
                attn_keep=(attn_half, bf16),
                attn_send=(attn_half, bf16),
                **extra_outs,
            ),
            dict(
                grad_mid=pltpu.VMEM(matrix, f32),
                branch=pltpu.VMEM(matrix, bf16),
                grad_heads=pltpu.VMEM((rows, inner), bf16),
                grad_qkv=pltpu.VMEM((rows, 3 * inner), bf16),
                grad_scores=pltpu.VMEM((rows, heads * slots), bf16),
                attn_grad=pltpu.VMEM((width, 4 * inner), f32),
                pulled=pltpu.VMEM((256, 2 * width), bf16),
                **attn_scratch,
                **ff_scratch,
                **extra_scratch,
            ),
            after=after,
            flops=2 * (attn_flops + ff_flops),
        )

    def weight_grads(layer_idx, kept, back, grad, peer_in, peer_grad, after=()):
        return run(
            functools.partial(weight_body, layer_idx=layer_idx, piece_masks=ff_masks),
            "layer_%d_weight_grads" % layer_idx,
            dict(
                place=place,
                ff_in=kept.ff_in,
                grad=grad,
                hidden=back.hidden,
                grad_gate_up=back.grad_gate_up,
                peer_in=peer_in,
                peer_grad=peer_grad,
                w_gate=w_gate,
                w_up=w_up,
                w_down=w_down,
            ),
            dict(ff_keep=(ff_half, bf16), ff_send=(ff_half, bf16)),
            dict(
                peer_gate_up=pltpu.VMEM((rows, 2 * width), bf16),
                peer_hidden=pltpu.VMEM(matrix, bf16),
                ff_grad=pltpu.VMEM((width, 3 * width), f32),
                ff_gate_up=pltpu.VMEM((width, 2 * width), bf16),
                ff_down=pltpu.VMEM((width, width), bf16),
                ff_sem=pltpu.SemaphoreType.DMA,
            ),
            after=after,
            flops=ff_flops,
        )

    def add(left, right):
        return (left.astype(f32) + right.astype(f32)).astype(bf16)

    def halving(keep, send, hops, out):
        for step, hop in enumerate(hops):
            got = yield swap(send, hop)
            if step + 1 < len(hops):
                cut = keep.shape[0] // 2
                send = add(keep[cut:], got[cut:])
                keep = add(keep[:cut], got[:cut])
                out["token"] = send
            else:
                out["token"] = keep = add(keep, got)
        out["piece"] = keep

    def summing(piece, hops, out):
        for hop in hops:
            got = yield swap(piece, hop)
            out["token"] = piece = add(piece, got) if piece.dtype == bf16 else piece + got
        out["piece"] = piece

    def sharing(piece, hops, out):
        for step, hop in enumerate(hops):
            got = yield swap(piece, hop)
            if step + 1 < len(hops):
                out["token"] = piece = join(piece, got)
            else:
                out["token"] = got
        out["near"], out["far"] = piece, got

    def attn_chain(part, out):
        yield from halving(part.attn_keep, part.attn_send, attn_split, out)
        yield from summing(out["piece"], attn_whole, out)
        piece = out["piece"][0]
        if own_rows < attn_grain:
            first_row = lax.rem(device_at, attn_low) * own_rows
            piece = lax.dynamic_slice_in_dim(piece, first_row, own_rows, axis=0)
        out["done"] = piece.astype(f32)

    def ff_chain(part, out):
        yield from halving(part.ff_keep, part.ff_send, ff_split, out)
        yield from summing(out["piece"], ff_whole, out)
        yield from sharing(out["piece"], ff_split[::-1], out)
        out["done"] = True

    class Chain:
        def __init__(self, steps, *args):
            self.out = {}
            self.steps = steps(*args, self.out)
            self.arriving = next(self.steps)

        def step(self, token):
            if self.arriving is not None:
                arrived = tie(self.arriving, token)
                self.arriving = None
                try:
                    self.arriving = self.steps.send(arrived)
                except StopIteration:
                    pass
                return self.out["token"]
            return token

    back_1 = backward(
        1,
        second,
        first.x_next,
        first.a_next,
        cotangent,
        {},
        dict(
            outputs=(matrix, bf16),
            grad_next_low=(matrix, bf16),
            bias_acc=((slots, heads * slots), f32),
        ),
        {},
    )
    peer_grad_0 = swap(back_1.grad_next_low, 1)
    part_1 = weight_grads(1, second, back_1, cotangent, peer_in_1, peer_cotangent)
    attn_1 = Chain(attn_chain, back_1)
    ff_1 = Chain(ff_chain, part_1)
    token = attn_1.step(part_1.ff_send)
    back_0 = backward(
        0,
        first,
        start.x,
        start.a,
        back_1.grad_next,
        dict(
            bias_before=back_1.bias_acc,
            marks=marks,
            buckets=wide_buckets,
            small_before=back_1.small,
        ),
        {},
        dict(
            bias_acc=pltpu.VMEM((slots, heads * slots), f32),
            table_rows=pltpu.VMEM((bias_table.shape[0], heads * slots), f32),
        ),
        after=(token,),
    )
    attn_0 = Chain(attn_chain, back_0)
    token = ff_1.step(back_0.attn_send)
    token = attn_1.step(token)
    part_0 = weight_grads(
        0, first, back_0, back_1.grad_next_low, peer_in_0, peer_grad_0, after=(token,)
    )
    ff_0 = Chain(ff_chain, part_0)
    small = Chain(summing, back_0.small, attn_hops)
    token = part_0.ff_send
    done_1 = None
    shape = (2, width, width)
    finish_masks = order_masks(ff_split)
    near_masks = [mask // 2 for mask in finish_masks[: ff_count // 2]]
    far_masks = [mask // 2 for mask in finish_masks[ff_count // 2 :]]
    chains = (ff_0, attn_0, ff_1, attn_1, small)
    while any(chain.arriving is not None for chain in chains):
        if "near" in ff_1.out and done_1 is None:
            pieces = join(ff_1.out["near"], ff_1.out["far"])
            done_1 = finish(pieces, near_masks + far_masks, 1, place, shape)
        for chain in chains:
            token = chain.step(token)
    if done_1 is None:
        pieces = join(ff_1.out["near"], ff_1.out["far"])
        done_1 = finish(pieces, near_masks + far_masks, 1, place, shape)
    near_0 = finish(ff_0.out["near"], near_masks, 0, place, shape, done_1)
    done = finish(ff_0.out["far"], far_masks, 0, place, shape, near_0)
    sums = run(
        small_body,
        "small_sums",
        dict(packed=small.out["piece"]),
        dict(
            gain_attn=((2, width), f32),
            gain_ff=((2, width), f32),
            embed=((1, width), f32),
            table=(bias_table.shape, f32),
        ),
        {},
    )
    attn_0, attn_1 = attn_0.out["done"], attn_1.out["done"]
    attn_grads = jnp.stack([attn_0, attn_1])
    return (
        back_1.outputs.reshape(inputs.shape),
        back_0.grad_next.reshape(inputs.shape),
        attn_grads[:, :, :inner],
        attn_grads[:, :, inner : 2 * inner],
        attn_grads[:, :, 2 * inner : 3 * inner],
        jnp.swapaxes(attn_grads[:, :, 3 * inner :], 1, 2),
        *done,
        sums.gain_attn,
        sums.gain_ff,
        sums.table,
        sums.embed[0],
    )


def solution(mesh):
    placed = (
        P(("dp", "tensor"), None, None),
        P(("dp", "tensor"), None, None),
        P(("dp", "tensor"), None),
        P(("dp", "tensor"), None),
        P(),
        P(),
        P(None, ("dp", "tensor"), None),
        P(None, ("dp", "tensor"), None),
        P(None, ("dp", "tensor"), None),
        P(None, None, ("dp", "tensor")),
        P(None, None, "tensor"),
        P(None, None, "tensor"),
        P(None, "tensor", None),
        P(),
        P(),
        P(),
    )
    return jax.shard_map(
        functools.partial(on_device, dp_size=mesh.shape["dp"]),
        mesh=mesh,
        in_specs=placed,
        out_specs=(
            P(("dp", "tensor"), None, None),
            P(("dp", "tensor"), None, None),
            P(None, ("dp", "tensor"), None),
            P(None, ("dp", "tensor"), None),
            P(None, ("dp", "tensor"), None),
            P(None, None, ("dp", "tensor")),
            P(None, None, "tensor"),
            P(None, None, "tensor"),
            P(None, "tensor", None),
            P(),
            P(),
            P(),
            P(),
        ),
        check_vma=False,
    )
```

time: 299 us -> 244 us (0.82)
  waiting for transfers between devices: 126 us -> 94.1 us
  Pallas kernels: 97.9 us -> 73.7 us
  local copies, waits for them, and re-layouts: 22.1 us -> 16.8 us
  other arithmetic: 2.93 us -> 6.89 us
    ppermute x49 -> x50, waiting for transfers between devices: 126 us -> 94.1 us  [swap(): return lax.ppermute(array, axes, [(n, n ^ mask) for n in range(devices)])]
    pallas_call x8 -> x11, Pallas kernels: 97.9 us -> 73.7 us  [the longest x8 64.1 us: run(): pl.pallas_call(kernel, name=name, in_specs=[pl.BlockSpec(memory_space=plt...]
    unnamed x78 -> x65, local copies, waits for them, and re-layouts: 11.7 us -> 8.05 us
    reshape x5 -> x0, local copies, waits for them, and re-layouts: 3.04 us -> none  [the longest x1 0.92 us: on_device(): valid = patch_valid.reshape(rows, 1)]
    ppermute x49 -> x50, starting transfers between devices: 47.6 us -> 50.1 us  [swap(): return lax.ppermute(array, axes, [(n, n ^ mask) for n in range(devices)])]
  transfers between devices with their start and end apart: 49 -> 50, of which waited for: 27 -> 26; matrix products, arithmetic and copies ran while one was open for 6% -> 7% of each run, Pallas kernels for 31% -> 20%
where the time goes in v2:
time: 244 us; the launch traced here: 243 us
  waiting for transfers between devices  94.1 us (39%)
  Pallas kernels  73.7 us (30%)
  starting transfers between devices  50.1 us (21%)
  local copies, waits for them, and re-layouts  16.8 us (7%)
  other arithmetic  6.89 us (3%)
    ppermute x50, waiting for transfers between devices, swap(): return lax.ppermute(array, axes, [(n, n ^ mask) for n in range(devices)])  94.1 us
    pallas_call x8, Pallas kernels, run(): pl.pallas_call(kernel, name=name, in_specs=[pl.BlockSpec(memory_space=plt...  64.1 us
    ppermute x50, starting transfers between devices, swap(): return lax.ppermute(array, axes, [(n, n ^ mask) for n in range(devices)])  50.1 us
    pallas_call x3, Pallas kernels, finish(): pl.pallas_call(kernel, name='layer_%d_ff_grads' % layer_idx, in_specs=[pl...  9.58 us
    unnamed x65, local copies, waits for them, and re-layouts  8.05 us
  transfers between devices with their start and end apart: 50, of which 26 were waited for; matrix products, arithmetic and copies ran while one was open for 7% of the time, Pallas kernels for 20%

profile of v2, /device:TPU:0, one launch (start us, length us, event | category | flops | bytes accessed | tf_op | source)
XLA Modules:
  0.0 243.2 jit_solution(3113094848794666286)
XLA Ops:
  3.7 3.0 %collective-permute-start.5 = (bf16[6,128,512]{2,1,0:T(8,128)(2,1)S(1)}, bf16[6,128,512]{2,1,0:T(8,128)(2,1)S(1)}, u32[]{:S(2)}, u32[]{:S(2)}) collective-permute-start(bf16[6,128,512]{2,1,0:T(8,128)(2,1)S(1)} %pad_maximum_fusion), channel_id=1, source_target_pairs={{0,1},{1,0},{2,3},{3,2},{4,5},{5,4},{6,7},{7,6},{8,9},{9,8},{10,11... | collective-permute-start | bytes 2359304 | tf_op jit(solution)/shard_map/ppermute | solution.py:537
  18.3 7.0 %collective-permute-done.8 = bf16[16,1536]{1,0:T(8,128)(2,1)S(1)} collective-permute-done((bf16[16,1536]{1,0:T(8,128)(2,1)S(1)}, bf16[16,1536]{1,0:T(8,128)(2,1)S(1)}, u32[]{:S(2)}, u32[]{:S(2)}) %collective-permute-start.8) | collective-permute-done | bytes 49184 | tf_op jit(solution)/shard_map/ppermute | solution.py:537
  36.6 3.1 %collective-permute-start.11 = (bf16[128,1536]{1,0:T(8,128)(2,1)S(1)}, bf16[128,1536]{1,0:T(8,128)(2,1)S(1)}, u32[]{:S(2)}, u32[]{:S(2)}) collective-permute-start(bf16[128,1536]{1,0:T(8,128)(2,1)S(1)} %pad_maximum_fusion.5), channel_id=1, source_target_pairs={{0,16},{1,17},{2,18},{3,19},{4,20},{5,21},{6,22},{7,23},{8,24},{9,... | collective-permute-start | bytes 1179656 | tf_op jit(solution)/shard_map/ppermute | solution.py:537
  40.5 3.3 %collective-permute-start.6 = (bf16[3,128,512]{2,1,0:T(8,128)(2,1)S(1)}, bf16[3,128,512]{2,1,0:T(8,128)(2,1)S(1)}, u32[]{:S(2)}, u32[]{:S(2)}) collective-permute-start(bf16[3,128,512]{2,1,0:T(8,128)(2,1)S(1)} %get-tuple-element.107), channel_id=1, source_target_pairs={{0,4},{1,5},{2,6},{3,7},{4,0},{5,1},{6,2},{7,3},{8,12},{9,13},{10,... | collective-permute-start | bytes 1179656 | tf_op jit(solution)/shard_map/ppermute | solution.py:537
  44.9 7.5 %collective-permute-done.6 = bf16[3,128,512]{2,1,0:T(8,128)(2,1)S(1)} collective-permute-done((bf16[3,128,512]{2,1,0:T(8,128)(2,1)S(1)}, bf16[3,128,512]{2,1,0:T(8,128)(2,1)S(1)}, u32[]{:S(2)}, u32[]{:S(2)}) %collective-permute-start.6) | collective-permute-done | bytes 393248 | tf_op jit(solution)/shard_map/ppermute | solution.py:537
  59.4 9.2 %layer_0_forward.1 = (bf16[512,1152]{1,0:T(8,128)(2,1)}, f32[512,384]{1,0:T(8,128)}, bf16[512,384]{1,0:T(8,128)(2,1)}, f32[512,512]{1,0:T(8,128)}, bf16[512,512]...) custom-call(s32[4]{0:T(128)} %pad_add_fusion.1.refs_0_.place_ref, ...), custom_call_target="tpu_custom_call" | custom-call | flops 2415919104 | bytes 8228880 | tf_op jit(solution)/shard_map/layer_0_forward/pallas_call | solution.py:88
  69.6 6.0 %layer_1_attention.1 = (bf16[512,1152]{1,0:T(8,128)(2,1)}, f32[512,384]{1,0:T(8,128)}, bf16[512,384]{1,0:T(8,128)(2,1)}, f32[512,512]{1,0:T(8,128)}, bf16[512,512]{1,0:T(8,128)(2,1)}) custom-call(s32[4]{0:T(128)} %pad_add_fusion.1.refs_0_.place_ref, f32[512,512]{1,0:T(8,128)} %get-tuple-element.108.refs_1_, bf16[512,512]{1,0:T(8,128)(2,1)} %get-tuple-element.109.refs_2_, ...), custom_call_target="tpu_custom_call" | custom-call | flops 805306368 | bytes 3508240 | tf_op jit(solution)/shard_map/layer_1_attention/pallas_call | solution.py:88
  75.6 14.2 %layer_1_backward.1 = (f32[512,512]{1,0:T(8,128)}, bf16[512,512]{1,0:T(8,128)(2,1)}, bf16[512,1024]{1,0:T(8,128)(2,1)}, f32[56,128]{1,0:T(8,128)}, bf16[16,16,15...) custom-call(s32[4]{0:T(128)} %pad_add_fusion.1.refs_0_.place_ref, ...), custom_call_target="tpu_custom_call" | custom-call | flops 4831838208 | bytes 12324880 | tf_op jit(solution)/shard_map/layer_1_backward/pallas_call | solution.py:88
  94.3 10.7 %collective-permute-done.17.refs_6_ = bf16[512,512]{1,0:T(8,128)(2,1)S(1)} collective-permute-done((bf16[512,512]{1,0:T(8,128)(2,1)S(1)}, bf16[512,512]{1,0:T(8,128)(2,1)S(1)}, u32[]{:S(2)}, u32[]{:S(2)}) %collective-permute-start.17) | collective-permute-done | bytes 524320 | tf_op jit(solution)/shard_map/ppermute | solution.py:537
  105.0 11.2 %collective-permute-done.16.refs_5_ = bf16[512,512]{1,0:T(8,128)(2,1)S(1)} collective-permute-done((bf16[512,512]{1,0:T(8,128)(2,1)S(1)}, bf16[512,512]{1,0:T(8,128)(2,1)S(1)}, u32[]{:S(2)}, u32[]{:S(2)}) %collective-permute-start.16) | collective-permute-done | bytes 524320 | tf_op jit(solution)/shard_map/ppermute | solution.py:537
  117.1 7.7 %layer_1_weight_grads.1 = (bf16[8,32,1536]{2,1,0:T(8,128)(2,1)}, bf16[8,32,1536]{2,1,0:T(8,128)(2,1)}) custom-call(s32[4]{0:T(128)} %pad_add_fusion.1.refs_0_.place_ref, bf16[512,512]{1,0:T(8,128)(2,1)} %get-tuple-element.114.refs_10_.refs_1_, bf16[512,512]{1,0:T(8,128)(2,1)} %bitcast.33, bf16[512,512]{1,0:T(8,128)(2,1)} %get-tuple-element.127.refs_3_, ...), custom_call_target="tpu_custom_call" | custom-call | flops 1610612736 | bytes 6815760 | tf_op jit(solution)/shard_map/layer_1_weight_grads/pallas_call | solution.py:88
  126.7 15.4 %layer_0_backward.1 = (f32[512,512]{1,0:T(8,128)}, bf16[512,512]{1,0:T(8,128)(2,1)}, bf16[512,1024]{1,0:T(8,128)(2,1)}, f32[56,128]{1,0:T(8,128)}, bf16[16,16,15...) custom-call(s32[4]{0:T(128)} %pad_add_fusion.1.refs_0_.place_ref, f32[512,512]{1,0:T(8,128)} %get-tuple-element.99.refs_1_, ...), custom_call_target="tpu_custom_call" | custom-call | flops 4831838208 | bytes 13078544 | tf_op jit(solution)/shard_map/layer_0_backward/pallas_call | solution.py:88
  142.3 4.0 %collective-permute-done.21 = bf16[8,16,1536]{2,1,0:T(8,128)(2,1)S(1)} collective-permute-done((bf16[8,16,1536]{2,1,0:T(8,128)(2,1)S(1)}, bf16[8,16,1536]{2,1,0:T(8,128)(2,1)S(1)}, u32[]{:S(2)}, u32[]{:S(2)}) %collective-permute-start.21) | collective-permute-done | bytes 393248 | tf_op jit(solution)/shard_map/ppermute | solution.py:537
  148.1 7.6 %layer_0_weight_grads.1 = (bf16[8,32,1536]{2,1,0:T(8,128)(2,1)}, bf16[8,32,1536]{2,1,0:T(8,128)(2,1)}) custom-call(s32[4]{0:T(128)} %pad_add_fusion.1.refs_0_.place_ref, bf16[512,512]{1,0:T(8,128)(2,1)} %get-tuple-element.122.refs_10_.refs_1_, bf16[512,512]{1,0:T(8,128)(2,1)} %get-tuple-element.135.refs_2_, bf16[512,512]{1,0:T(8,128)(2,1)} %get-tuple-element.136.refs_3_, ...), custom_call_target="tpu_custom_call" | custom-call | flops 1610612736 | bytes 6815760 | tf_op jit(solution)/shard_map/layer_0_weight_grads/pallas_call | solution.py:88
  163.7 4.6 %collective-permute-done.28 = bf16[4,32,1536]{2,1,0:T(8,128)(2,1)S(1)} collective-permute-done((bf16[4,32,1536]{2,1,0:T(8,128)(2,1)S(1)}, bf16[4,32,1536]{2,1,0:T(8,128)(2,1)S(1)}, u32[]{:S(2)}, u32[]{:S(2)}) %collective-permute-start.28) | collective-permute-done | bytes 393248 | tf_op jit(solution)/shard_map/ppermute | solution.py:537
  169.2 3.3 %collective-permute-done.27 = bf16[4,16,1536]{2,1,0:T(8,128)(2,1)S(1)} collective-permute-done((bf16[4,16,1536]{2,1,0:T(8,128)(2,1)S(1)}, bf16[4,16,1536]{2,1,0:T(8,128)(2,1)S(1)}, u32[]{:S(2)}, u32[]{:S(2)}) %collective-permute-start.27) | collective-permute-done | bytes 196640 | tf_op jit(solution)/shard_map/ppermute | solution.py:537
  174.6 6.1 %collective-permute-done.25 = bf16[4,32,1536]{2,1,0:T(8,128)(2,1)S(1)} collective-permute-done((bf16[4,32,1536]{2,1,0:T(8,128)(2,1)S(1)}, bf16[4,32,1536]{2,1,0:T(8,128)(2,1)S(1)}, u32[]{:S(2)}, u32[]{:S(2)}) %collective-permute-start.25) | collective-permute-done | bytes 393248 | tf_op jit(solution)/shard_map/ppermute | solution.py:537
  199.7 3.0 %collective-permute-start.39 = (bf16[1,16,1536]{2,1,0:T(8,128)(2,1)S(1)}, bf16[1,16,1536]{2,1,0:T(8,128)(2,1)S(1)}, u32[]{:S(2)}, u32[]{:S(2)}) collective-permute-start(bf16[1,16,1536]{2,1,0:T(8,128)(2,1)S(1)} %add_convert_fusion.27), channel_id=1, source_target_pairs={{0,16},{1,17},{2,18},{3,19},{4,20},{5,21},{6,22},{7,23},{8,24},{9,... | collective-permute-start | bytes 147464 | tf_op jit(solution)/shard_map/ppermute | solution.py:537
  207.7 4.5 %collective-permute-done.45 = bf16[2,32,1536]{2,1,0:T(8,128)(2,1)S(1)} collective-permute-done((bf16[2,32,1536]{2,1,0:T(8,128)(2,1)S(1)}, bf16[2,32,1536]{2,1,0:T(8,128)(2,1)S(1)}, u32[]{:S(2)}, u32[]{:S(2)}) %collective-permute-start.45) | collective-permute-done | bytes 196640 | tf_op jit(solution)/shard_map/ppermute | solution.py:537
  215.0 8.0 %collective-permute-done.47 = bf16[4,32,1536]{2,1,0:T(8,128)(2,1)S(1)} collective-permute-done((bf16[4,32,1536]{2,1,0:T(8,128)(2,1)S(1)}, bf16[4,32,1536]{2,1,0:T(8,128)(2,1)S(1)}, u32[]{:S(2)}, u32[]{:S(2)}) %collective-permute-start.47) | collective-permute-done | bytes 393248 | tf_op jit(solution)/shard_map/ppermute | solution.py:537
  224.0 3.3 %collective-permute-done.46 = bf16[4,32,1536]{2,1,0:T(8,128)(2,1)S(1)} collective-permute-done((bf16[4,32,1536]{2,1,0:T(8,128)(2,1)S(1)}, bf16[4,32,1536]{2,1,0:T(8,128)(2,1)S(1)}, u32[]{:S(2)}, u32[]{:S(2)}) %collective-permute-start.46) | collective-permute-done | bytes 393248 | tf_op jit(solution)/shard_map/ppermute | solution.py:537
  233.4 3.7 %layer_1_ff_grads.1 = (f32[2,512,512]{2,1,0:T(8,128)}, f32[2,512,512]{2,1,0:T(8,128)}, f32[2,512,512]{2,1,0:T(8,128)}) custom-call(s32[4]{0:T(128)} %pad_add_fusion.1.refs_0_.place_ref, bf16[16,32,1536]{2,1,0:T(8,128)(2,1)} %copy-done.1), custom_call_target="tpu_custom_call" | custom-call | tf_op jit(solution)/shard_map/layer_1_ff_grads/pallas_call | solution.py:463
  237.2 2.9 %layer_0_ff_grads.2 = (f32[2,512,512]{2,1,0:T(8,128)}, f32[2,512,512]{2,1,0:T(8,128)}, f32[2,512,512]{2,1,0:T(8,128)}) custom-call(s32[4]{0:T(128)} %pad_add_fusion.1.refs_0_.place_ref, bf16[8,32,1536]{2,1,0:T(8,128)(2,1)} %copy-done, f32[2,512,512]{2,1,0:T(8,128)} %get-tuple-element.172.refs_0_, ...), custom_call_target="tpu_custom_call", output_to_operand_aliasing={{0}: (2, {}), {1}: (3, {}), {2}: (4, {})} | custom-call | tf_op jit(solution)/shard_map/layer_0_ff_grads/pallas_call | solution.py:463
  240.1 2.9 %layer_0_ff_grads.3 = (f32[2,512,512]{2,1,0:T(8,128)}, f32[2,512,512]{2,1,0:T(8,128)}, f32[2,512,512]{2,1,0:T(8,128)}) custom-call(s32[4]{0:T(128)} %pad_add_fusion.1.refs_0_.place_ref, bf16[8,32,1536]{2,1,0:T(8,128)(2,1)} %collective-permute-done.48.source, ...), custom_call_target="tpu_custom_call", output_to_operand_aliasing={{0}: (2, {}), {1}: (3, {}), {2}: (4, {})} | custom-call | tf_op jit(solution)/shard_map/layer_0_ff_grads/pallas_call | solution.py:463
  (212 shorter events, 89.4 us)
Async XLA Ops:
  3.7 36.7 %collective-permute-start.5 = (bf16[6,128,512]{2,1,0:T(8,128)(2,1)S(1)}, bf16[6,128,512]{2,1,0:T(8,128)(2,1)S(1)}, u32[]{:S(2)}, u32[]{:S(2)}) collective-permute-start(bf16[6,128,512]{2,1,0:T(8,128)(2,1)S(1)} %pad_maximum_fusion), channel_id=1, source_target_pairs={{0,1},{1,0},{2,3},{3,2},{4,5},{5,4},{6,7},{7,6},{8,9},{9,8},{10,11... | collective-permute-start | bytes 2359304 | tf_op jit(solution)/shard_map/ppermute | solution.py:537
  9.4 15.9 %collective-permute-start.8 = (bf16[16,1536]{1,0:T(8,128)(2,1)S(1)}, bf16[16,1536]{1,0:T(8,128)(2,1)S(1)}, u32[]{:S(2)}, u32[]{:S(2)}) collective-permute-start(bf16[16,1536]{1,0:T(8,128)(2,1)S(1)} %get-tuple-element.252), channel_id=1, source_target_pairs={{0,1},{1,0},{2,3},{3,2},{4,5},{5,4},{6,7},{7,6},{8,9},{9,8},{10,11... | collective-permute-start | bytes 147464 | tf_op jit(solution)/shard_map/ppermute | solution.py:537
  36.6 18.3 %collective-permute-start.11 = (bf16[128,1536]{1,0:T(8,128)(2,1)S(1)}, bf16[128,1536]{1,0:T(8,128)(2,1)S(1)}, u32[]{:S(2)}, u32[]{:S(2)}) collective-permute-start(bf16[128,1536]{1,0:T(8,128)(2,1)S(1)} %pad_maximum_fusion.5), channel_id=1, source_target_pairs={{0,16},{1,17},{2,18},{3,19},{4,20},{5,21},{6,22},{7,23},{8,24},{9,... | collective-permute-start | bytes 1179656 | tf_op jit(solution)/shard_map/ppermute | solution.py:537
  44.8 14.5 %collective-permute-start.4 = (bf16[256,1536]{1,0:T(8,128)(2,1)}, bf16[256,1536]{1,0:T(8,128)(2,1)}, u32[]{:S(2)}, u32[]{:S(2)}) collective-permute-start(bf16[256,1536]{1,0:T(8,128)(2,1)} %constant_dynamic-update-slice_fusion.refs_7_.refs_11_), channel_id=1, source_target_pairs={{0,2},{1,3},{2,0},{3,1},{4,6},{5,7},{6,4},{7,5},{8,10},{9,11},{10,... | collective-permute-start | bytes 2359304 | tf_op jit(solution)/shard_map/ppermute | solution.py:537
  44.8 13.1 %collective-permute-start.13 = (bf16[3,128,512]{2,1,0:T(8,128)(2,1)S(1)}, bf16[3,128,512]{2,1,0:T(8,128)(2,1)S(1)}, u32[]{:S(2)}, u32[]{:S(2)}) collective-permute-start(bf16[3,128,512]{2,1,0:T(8,128)(2,1)S(1)} %get-tuple-element.115), channel_id=1, source_target_pairs={{0,4},{1,5},{2,6},{3,7},{4,0},{5,1},{6,2},{7,3},{8,12},{9,13},{10,... | collective-permute-start | bytes 1179656 | tf_op jit(solution)/shard_map/ppermute | solution.py:537
  55.0 13.6 %collective-permute-start.12 = (bf16[256,1536]{1,0:T(8,128)(2,1)S(1)}, bf16[256,1536]{1,0:T(8,128)(2,1)S(1)}, u32[]{:S(2)}, u32[]{:S(2)}) collective-permute-start(bf16[256,1536]{1,0:T(8,128)(2,1)S(1)} %constant_dynamic-update-slice_fusion.5.refs_6_.refs_11_), channel_id=1, source_target_pairs={{0,2},{1,3},{2,0},{3,1},{4,6},{5,7},{6,4},{7,5},{8,10},{9,11},{10,... | collective-permute-start | bytes 2359304 | tf_op jit(solution)/shard_map/ppermute | solution.py:537
  58.0 17.5 %collective-permute-start.14 = (bf16[6,128,512]{2,1,0:T(8,128)(2,1)S(1)}, bf16[6,128,512]{2,1,0:T(8,128)(2,1)}, u32[]{:S(2)}, u32[]{:S(2)}) collective-permute-start(bf16[6,128,512]{2,1,0:T(8,128)(2,1)S(1)} %constant_dynamic-update-slice_fusion.10.refs_16_), channel_id=1, source_target_pairs={{0,2},{1,3},{2,0},{3,1},{4,6},{5,7},{6,4},{7,5},{8,10},{9,11},{10,... | collective-permute-start | bytes 2359304 | tf_op jit(solution)/shard_map/ppermute | solution.py:537
  89.8 35.0 %collective-permute-start.15 = (bf16[16,16,1536]{2,1,0:T(8,128)(2,1)}, bf16[16,16,1536]{2,1,0:T(8,128)(2,1)S(1)}, u32[]{:S(2)}, u32[]{:S(2)}) collective-permute-start(bf16[16,16,1536]{2,1,0:T(8,128)(2,1)} %get-tuple-element.126), channel_id=1, source_target_pairs={{0,2},{1,3},{2,0},{3,1},{4,6},{5,7},{6,4},{7,5},{8,10},{9,11},{10,... | collective-permute-start | bytes 2359304 | tf_op jit(solution)/shard_map/ppermute | solution.py:537
  90.2 14.8 %collective-permute-start.17 = (bf16[512,512]{1,0:T(8,128)(2,1)S(1)}, bf16[512,512]{1,0:T(8,128)(2,1)S(1)}, u32[]{:S(2)}, u32[]{:S(2)}) collective-permute-start(bf16[512,512]{1,0:T(8,128)(2,1)S(1)} %bitcast.34), channel_id=1, source_target_pairs={{0,1},{1,0},{2,3},{3,2},{4,5},{5,4},{6,7},{7,6},{8,9},{9,8},{10,11... | collective-permute-start | bytes 1572872 | tf_op jit(solution)/shard_map/ppermute | solution.py:537
  91.8 24.5 %collective-permute-start.16 = (bf16[512,512]{1,0:T(8,128)(2,1)S(1)}, bf16[512,512]{1,0:T(8,128)(2,1)S(1)}, u32[]{:S(2)}, u32[]{:S(2)}) collective-permute-start(bf16[512,512]{1,0:T(8,128)(2,1)S(1)} %copy-done.13), channel_id=1, source_target_pairs={{0,1},{1,0},{2,3},{3,2},{4,5},{5,4},{6,7},{7,6},{8,9},{9,8},{10,11... | collective-permute-start | bytes 1572872 | tf_op jit(solution)/shard_map/ppermute | solution.py:537
  92.3 54.8 %collective-permute-start.20 = (bf16[512,512]{1,0:T(8,128)(2,1)}, bf16[512,512]{1,0:T(8,128)(2,1)S(1)}, u32[]{:S(2)}, u32[]{:S(2)}) collective-permute-start(bf16[512,512]{1,0:T(8,128)(2,1)} %get-tuple-element.135.refs_2_), channel_id=1, source_target_pairs={{0,1},{1,0},{2,3},{3,2},{4,5},{5,4},{6,7},{7,6},{8,9},{9,8},{10,11... | collective-permute-start | bytes 1572872 | tf_op jit(solution)/shard_map/ppermute | solution.py:537
  93.8 53.3 %collective-permute-start.19 = (bf16[512,512]{1,0:T(8,128)(2,1)S(1)}, bf16[512,512]{1,0:T(8,128)(2,1)S(1)}, u32[]{:S(2)}, u32[]{:S(2)}) collective-permute-start(bf16[512,512]{1,0:T(8,128)(2,1)S(1)} %copy-done.10), channel_id=1, source_target_pairs={{0,1},{1,0},{2,3},{3,2},{4,5},{5,4},{6,7},{7,6},{8,9},{9,8},{10,11... | collective-permute-start | bytes 1572872 | tf_op jit(solution)/shard_map/ppermute | solution.py:537
  124.7 17.4 %collective-permute-start.22 = (bf16[8,32,1536]{2,1,0:T(8,128)(2,1)}, bf16[8,32,1536]{2,1,0:T(8,128)(2,1)S(1)}, u32[]{:S(2)}, u32[]{:S(2)}) collective-permute-start(bf16[8,32,1536]{2,1,0:T(8,128)(2,1)} %get-tuple-element.130), channel_id=1, source_target_pairs={{0,2},{1,3},{2,0},{3,1},{4,6},{5,7},{6,4},{7,5},{8,10},{9,11},{10,... | collective-permute-start | bytes 2359304 | tf_op jit(solution)/shard_map/ppermute | solution.py:537
  125.1 21.2 %collective-permute-start.21 = (bf16[8,16,1536]{2,1,0:T(8,128)(2,1)S(1)}, bf16[8,16,1536]{2,1,0:T(8,128)(2,1)S(1)}, u32[]{:S(2)}, u32[]{:S(2)}) collective-permute-start(bf16[8,16,1536]{2,1,0:T(8,128)(2,1)S(1)} %get-tuple-element.233.refs_22_), channel_id=1, source_target_pairs={{0,1},{1,0},{2,3},{3,2},{4,5},{5,4},{6,7},{7,6},{8,9},{9,8},{10,11... | collective-permute-start | bytes 1179656 | tf_op jit(solution)/shard_map/ppermute | solution.py:537
  156.2 17.2 %collective-permute-start.26 = (f32[56,128]{1,0:T(8,128)S(1)}, f32[56,128]{1,0:T(8,128)S(1)}, u32[]{:S(2)}, u32[]{:S(2)}) collective-permute-start(f32[56,128]{1,0:T(8,128)S(1)} %copy-done.19), channel_id=1, source_target_pairs={{0,2},{1,3},{2,0},{3,1},{4,6},{5,7},{6,4},{7,5},{8,10},{9,11},{10,... | collective-permute-start | bytes 86024 | tf_op jit(solution)/shard_map/ppermute | solution.py:537
  156.3 12.0 %collective-permute-start.28 = (bf16[4,32,1536]{2,1,0:T(8,128)(2,1)S(1)}, bf16[4,32,1536]{2,1,0:T(8,128)(2,1)S(1)}, u32[]{:S(2)}, u32[]{:S(2)}) collective-permute-start(bf16[4,32,1536]{2,1,0:T(8,128)(2,1)S(1)} %get-tuple-element.231), channel_id=1, source_target_pairs={{0,4},{1,5},{2,6},{3,7},{4,0},{5,1},{6,2},{7,3},{8,12},{9,13},{10,... | collective-permute-start | bytes 1179656 | tf_op jit(solution)/shard_map/ppermute | solution.py:537
  158.3 14.2 %collective-permute-start.27 = (bf16[4,16,1536]{2,1,0:T(8,128)(2,1)S(1)}, bf16[4,16,1536]{2,1,0:T(8,128)(2,1)S(1)}, u32[]{:S(2)}, u32[]{:S(2)}) collective-permute-start(bf16[4,16,1536]{2,1,0:T(8,128)(2,1)S(1)} %copy-done.3), channel_id=1, source_target_pairs={{0,4},{1,5},{2,6},{3,7},{4,0},{5,1},{6,2},{7,3},{8,12},{9,13},{10,... | collective-permute-start | bytes 589832 | tf_op jit(solution)/shard_map/ppermute | solution.py:537
  159.8 20.9 %collective-permute-start.25 = (bf16[4,32,1536]{2,1,0:T(8,128)(2,1)S(1)}, bf16[4,32,1536]{2,1,0:T(8,128)(2,1)S(1)}, u32[]{:S(2)}, u32[]{:S(2)}) collective-permute-start(bf16[4,32,1536]{2,1,0:T(8,128)(2,1)S(1)} %get-tuple-element.227), channel_id=1, source_target_pairs={{0,4},{1,5},{2,6},{3,7},{4,0},{5,1},{6,2},{7,3},{8,12},{9,13},{10,... | collective-permute-start | bytes 1179656 | tf_op jit(solution)/shard_map/ppermute | solution.py:537
  162.1 19.3 %collective-permute-start.24 = (bf16[8,16,1536]{2,1,0:T(8,128)(2,1)S(1)}, bf16[8,16,1536]{2,1,0:T(8,128)(2,1)S(1)}, u32[]{:S(2)}, u32[]{:S(2)}) collective-permute-start(bf16[8,16,1536]{2,1,0:T(8,128)(2,1)S(1)} %get-tuple-element.229), channel_id=1, source_target_pairs={{0,1},{1,0},{2,3},{3,2},{4,5},{5,4},{6,7},{7,6},{8,9},{9,8},{10,11... | collective-permute-start | bytes 1179656 | tf_op jit(solution)/shard_map/ppermute | solution.py:537
  168.4 14.7 %collective-permute-start.33 = (bf16[2,32,1536]{2,1,0:T(8,128)(2,1)S(1)}, bf16[2,32,1536]{2,1,0:T(8,128)(2,1)S(1)}, u32[]{:S(2)}, u32[]{:S(2)}) collective-permute-start(bf16[2,32,1536]{2,1,0:T(8,128)(2,1)S(1)} %get-tuple-element.239), channel_id=1, source_target_pairs={{0,8},{1,9},{2,10},{3,11},{4,12},{5,13},{6,14},{7,15},{8,0},{9,1},... | collective-permute-start | bytes 589832 | tf_op jit(solution)/shard_map/ppermute | solution.py:537
  173.4 12.9 %collective-permute-start.31 = (f32[56,128]{1,0:T(8,128)S(1)}, f32[56,128]{1,0:T(8,128)S(1)}, u32[]{:S(2)}, u32[]{:S(2)}) collective-permute-start(f32[56,128]{1,0:T(8,128)S(1)} %add.134), channel_id=1, source_target_pairs={{0,1},{1,0},{2,3},{3,2},{4,5},{5,4},{6,7},{7,6},{8,9},{9,8},{10,11... | collective-permute-start | bytes 86024 | tf_op jit(solution)/shard_map/ppermute | solution.py:537
  184.0 12.6 %collective-permute-start.37 = (bf16[1,16,1536]{2,1,0:T(8,128)(2,1)S(1)}, bf16[1,16,1536]{2,1,0:T(8,128)(2,1)S(1)}, u32[]{:S(2)}, u32[]{:S(2)}) collective-permute-start(bf16[1,16,1536]{2,1,0:T(8,128)(2,1)S(1)} %add_convert_fusion.31), channel_id=1, source_target_pairs={{0,16},{1,17},{2,18},{3,19},{4,20},{5,21},{6,22},{7,23},{8,24},{9,... | collective-permute-start | bytes 147464 | tf_op jit(solution)/shard_map/ppermute | solution.py:537
  214.3 13.0 %collective-permute-start.46 = (bf16[4,32,1536]{2,1,0:T(8,128)(2,1)S(1)}, bf16[4,32,1536]{2,1,0:T(8,128)(2,1)S(1)}, u32[]{:S(2)}, u32[]{:S(2)}) collective-permute-start(bf16[4,32,1536]{2,1,0:T(8,128)(2,1)S(1)} %pad_maximum_fusion.7), channel_id=1, source_target_pairs={{0,4},{1,5},{2,6},{3,7},{4,0},{5,1},{6,2},{7,3},{8,12},{9,13},{10,... | collective-permute-start | bytes 1179656 | tf_op jit(solution)/shard_map/ppermute | solution.py:537
  227.3 12.8 %collective-permute-start.48 = (bf16[8,32,1536]{2,1,0:T(8,128)(2,1)S(1)}, bf16[8,32,1536]{2,1,0:T(8,128)(2,1)}, u32[]{:S(2)}, u32[]{:S(2)}) collective-permute-start(bf16[8,32,1536]{2,1,0:T(8,128)(2,1)S(1)} %pad_maximum_fusion.3.source), channel_id=1, source_target_pairs={{0,2},{1,3},{2,0},{3,1},{4,6},{5,7},{6,4},{7,5},{8,10},{9,11},{10,... | collective-permute-start | bytes 2359304 | tf_op jit(solution)/shard_map/ppermute | solution.py:537
  (52 other events, 428.2 us)

commit v3 on v2

--- a/solution.py
+++ b/solution.py
@@ -51,7 +51,11 @@
     return gate_act * half, slope
 
 
-def run(body, name, ins, outs, scratch, after=(), flops=0):
+def cost(micros):
+    return pl.CostEstimate(flops=int(micros * 1.15e9), bytes_accessed=0, transcendentals=0)
+
+
+def run(body, name, ins, outs, scratch, after=(), micros=1):
     in_names, out_names, scratch_names = list(ins), list(outs), list(scratch)
     staged = [n for n in in_names if n != "place" and n not in raw_names]
     in_sems = {n: i for i, n in enumerate(staged)}
@@ -84,7 +88,6 @@
         r.drain = lambda *names: [copy_out(n).wait() for n in names]
         body(r)
 
-    moved = sum(a.size * a.dtype.itemsize for a in ins.values())
     results = pl.pallas_call(
         kernel,
         name=name,
@@ -99,7 +102,7 @@
         + [pltpu.VMEM(shape, kind) for shape, kind in outs.values()]
         + [pltpu.SemaphoreType.DMA((max(1, len(staged)),)), pltpu.SemaphoreType.DMA((len(outs),))],
         compiler_params=pltpu.CompilerParams(vmem_limit_bytes=vmem_bytes),
-        cost_estimate=pl.CostEstimate(flops=flops, bytes_accessed=moved, transcendentals=0),
+        cost_estimate=cost(micros),
     )(*ins.values(), *after)
     return types.SimpleNamespace(**dict(zip(outs, results)))
 
@@ -475,6 +478,7 @@
             pltpu.SemaphoreType.DMA,
         ],
         compiler_params=pltpu.CompilerParams(vmem_limit_bytes=vmem_bytes),
+        cost_estimate=cost(3),
     )(place, pieces, *before)
 
 
@@ -588,6 +592,7 @@
             mask=((rows, 128), jnp.int32),
         ),
         {},
+        micros=3,
     )
 
     own_rows = packed.shape[1]
@@ -595,21 +600,22 @@
     far = bits[2:]
     if direct:
         hops_0 = far[1:][::-1] + far[:1] + [1, 2]
-        hops_1 = [1] + far + [2]
+        hops_1 = far[:1] + far[1:][::-1] + [1, 2]
         block_0, block_1 = packed[0], packed[1]
-        got_0 = got_1 = None
-        for step, (hop_0, hop_1) in enumerate(zip(hops_0, hops_1)):
-            if step + 1 == len(hops_0):
-                break
+        for hop_0, hop_1 in zip(hops_0[:-2], hops_1[:-2]):
             got_0, got_1 = swap(block_0, hop_0), swap(block_1, hop_1)
-            if step + 2 == len(hops_0):
-                before_last = block_0
-                got_0 = tie(got_0, start.a)
-            block_0, block_1 = join(block_0, got_0), join(block_1, got_1)
-        ff_0 = ff_quarter[:, 0]
-        ff_0 = join(ff_0, swap(tie(ff_0, before_last), 4))
-        ff_1 = tie(ff_quarter[:, 1], block_0)
+            block_0 = join(block_0, got_0)
+            block_1 = join(block_1, tie(got_1, block_0))
+        got_0 = swap(block_0, 1)
+        ff_0 = tie(ff_quarter[:, 0], block_0)
+        got_ff_0 = swap(ff_0, 4)
+        block_0 = join(block_0, tie(got_0, start.a, ff_0))
+        block_1 = tie(block_1, block_0)
+        got_1 = swap(block_1, 1)
+        ff_0 = join(ff_0, tie(got_ff_0, block_0))
+        ff_1 = tie(ff_quarter[:, 1], ff_0)
         ff_1 = join(ff_1, swap(ff_1, 4))
+        block_1 = join(block_1, got_1)
         attn_pieces = [
             (block_0, swap(block_0, 2), order_masks(hops_0[::-1])),
             (block_1, swap(block_1, 2), order_masks(hops_1[::-1])),
@@ -649,8 +655,6 @@
         middle=(matrix, f32),
         ff_in=(matrix, bf16),
     )
-    attn_flops = 2 * rows * width * 4 * inner
-    ff_flops = 2 * rows * width * 6 * width
 
     pieces, masks = attn_ins(0)
     first = run(
@@ -669,9 +673,9 @@
         ),
         dict(**attn_outs, x_next=(matrix, f32), a_next=(matrix, bf16)),
         dict(**attn_scratch, **ff_scratch),
-        flops=attn_flops + ff_flops,
-    )
-    peer_in_0 = swap(first.ff_in, 1)
+        micros=9,
+    )
+    peer_cotangent = swap(tie(cotangent, first.ff_in), 1)
     pieces, masks = attn_ins(1)
     second = run(
         functools.partial(second_body, sizes=sizes, masks=masks, grain=grain),
@@ -687,10 +691,9 @@
         ),
         attn_outs,
         attn_scratch,
-        flops=attn_flops,
+        micros=6,
     )
     peer_in_1 = swap(second.ff_in, 1)
-    peer_cotangent = swap(tie(cotangent, second.ff_in), 1)
 
     attn_hops = [2, 1] + bits[2:]
     attn_low = devices // attn_count
@@ -758,7 +761,7 @@
                 **extra_scratch,
             ),
             after=after,
-            flops=2 * (attn_flops + ff_flops),
+            micros=14,
         )
 
     def weight_grads(layer_idx, kept, back, grad, peer_in, peer_grad, after=()):
@@ -787,7 +790,7 @@
                 ff_sem=pltpu.SemaphoreType.DMA,
             ),
             after=after,
-            flops=ff_flops,
+            micros=7,
         )
 
     def add(left, right):
@@ -865,12 +868,15 @@
             bias_acc=((slots, heads * slots), f32),
         ),
         {},
+        after=(peer_cotangent,),
     )
     peer_grad_0 = swap(back_1.grad_next_low, 1)
     part_1 = weight_grads(1, second, back_1, cotangent, peer_in_1, peer_cotangent)
     attn_1 = Chain(attn_chain, back_1)
     ff_1 = Chain(ff_chain, part_1)
     token = attn_1.step(part_1.ff_send)
+    token = ff_1.step(token)
+    peer_in_0 = swap(tie(first.ff_in, token), 1)
     back_0 = backward(
         0,
         first,
@@ -898,17 +904,20 @@
     )
     ff_0 = Chain(ff_chain, part_0)
     small = Chain(summing, back_0.small, attn_hops)
-    token = part_0.ff_send
+    token = attn_1.step(ff_1.step(part_0.ff_send))
+    token = ff_0.step(attn_0.step(token))
+    token = small.step(token)
     done_1 = None
     shape = (2, width, width)
     finish_masks = order_masks(ff_split)
     near_masks = [mask // 2 for mask in finish_masks[: ff_count // 2]]
     far_masks = [mask // 2 for mask in finish_masks[ff_count // 2 :]]
-    chains = (ff_0, attn_0, ff_1, attn_1, small)
+    chains = (ff_0, ff_1, attn_0, attn_1, small)
     while any(chain.arriving is not None for chain in chains):
         if "near" in ff_1.out and done_1 is None:
             pieces = join(ff_1.out["near"], ff_1.out["far"])
-            done_1 = finish(pieces, near_masks + far_masks, 1, place, shape)
+            done_1 = finish(tie(pieces, token), near_masks + far_masks, 1, place, shape)
+            token = done_1[0]
         for chain in chains:
             token = chain.step(token)
     if done_1 is None:

time: 244 us -> 208 us (0.85)
  waiting for transfers between devices: 94.1 us -> 77.7 us
  starting transfers between devices: 50.1 us -> 35.3 us
  other arithmetic: 6.89 us -> 4.16 us
    ppermute x50, waiting for transfers between devices: 94.1 us -> 77.7 us  [swap(): return lax.ppermute(array, axes, [(n, n ^ mask) for n in range(devices)])]
    ppermute x50, starting transfers between devices: 50.1 us -> 35.3 us  [swap(): return lax.ppermute(array, axes, [(n, n ^ mask) for n in range(devices)])]
    unnamed x65 -> x74, local copies, waits for them, and re-layouts: 8.05 us -> 8.45 us
  transfers between devices with their start and end apart: 50 -> 50, of which waited for: 26 -> 24; matrix products, arithmetic and copies ran while one was open for 7% -> 6% of each run, Pallas kernels for 20% -> 34%
where the time goes in v3:
time: 208 us
  waiting for transfers between devices  77.7 us (37%)
  Pallas kernels  73.6 us (35%)
  starting transfers between devices  35.3 us (17%)
  local copies, waits for them, and re-layouts  15.3 us (7%)
  other arithmetic  4.16 us (2%)
    ppermute x50, waiting for transfers between devices, swap(): return lax.ppermute(array, axes, [(n, n ^ mask) for n in range(devices)])  77.7 us
    pallas_call x8, Pallas kernels, run(): pl.pallas_call(kernel, name=name, in_specs=[pl.BlockSpec(memory_space=plt...  64.1 us
    ppermute x50, starting transfers between devices, swap(): return lax.ppermute(array, axes, [(n, n ^ mask) for n in range(devices)])  35.3 us
    pallas_call x3, Pallas kernels, finish(): pl.pallas_call(kernel, name='layer_%d_ff_grads' % layer_idx, in_specs=[pl...  9.57 us
    unnamed x74, local copies, waits for them, and re-layouts  8.45 us
  transfers between devices with their start and end apart: 50, of which 24 were waited for; matrix products, arithmetic and copies ran while one was open for 6% of the time, Pallas kernels for 34%

profile of v3, /device:TPU:0, one launch (start us, length us, event | category | flops | bytes accessed | tf_op | source)
XLA Modules:
  0.0 207.7 jit_solution(10396715976857335860)
XLA Ops:
  1.5 3.0 %collective-permute-start.8 = (bf16[16,1536]{1,0:T(8,128)(2,1)S(1)}, bf16[16,1536]{1,0:T(8,128)(2,1)S(1)}, u32[]{:S(2)}, u32[]{:S(2)}) collective-permute-start(bf16[16,1536]{1,0:T(8,128)(2,1)S(1)} %get-tuple-element.266), channel_id=1, source_target_pairs={{0,4},{1,5},{2,6},{3,7},{4,0},{5,1},{6,2},{7,3},{8,12},{9,13},{10,... | collective-permute-start | bytes 147464 | tf_op jit(solution)/shard_map/ppermute | solution.py:541
  4.5 2.6 %collective-permute-start = (bf16[16,1536]{1,0:T(8,128)(2,1)S(1)}, bf16[16,1536]{1,0:T(8,128)(2,1)S(1)}, u32[]{:S(2)}, u32[]{:S(2)}) collective-permute-start(bf16[16,1536]{1,0:T(8,128)(2,1)S(1)} %get-tuple-element.267), channel_id=1, source_target_pairs={{0,16},{1,17},{2,18},{3,19},{4,20},{5,21},{6,22},{7,23},{8,24},{9,... | collective-permute-start | bytes 147464 | tf_op jit(solution)/shard_map/ppermute | solution.py:541
  14.3 2.7 %prepare.1 = (f32[512,512]{1,0:T(8,128)}, bf16[512,512]{1,0:T(8,128)(2,1)}, f32[64,384]{1,0:T(8,128)}, s32[512,128]{1,0:T(8,128)}) custom-call(bf16[512,512]{1,0:T(8,128)(2,1)} %bitcast.31, s32[512,2]{1,0:T(8,128)} %copy.47.refs_1_.refs_19_, f32[1,512]{1,0:T(1,128)} %bitcast.35, f32[1,512]{1,0:T(1,128)} %get-tuple-element.271.refs_3_.refs_4_, ...), custom_call_target="tpu_custom_call" | custom-call | flops 3449999872 | tf_op jit(solution)/shard_map/prepare/pallas_call | solution.py:91
  19.7 3.3 %collective-permute-done.1 = bf16[32,1536]{1,0:T(8,128)(2,1)S(1)} collective-permute-done((bf16[32,1536]{1,0:T(8,128)(2,1)S(1)}, bf16[32,1536]{1,0:T(8,128)(2,1)S(1)}, u32[]{:S(2)}, u32[]{:S(2)}) %collective-permute-start.1) | collective-permute-done | bytes 98336 | tf_op jit(solution)/shard_map/ppermute | solution.py:541
  25.9 2.9 %collective-permute-done.2 = bf16[64,1536]{1,0:T(8,128)(2,1)S(1)} collective-permute-done((bf16[64,1536]{1,0:T(8,128)(2,1)S(1)}, bf16[64,1536]{1,0:T(8,128)(2,1)S(1)}, u32[]{:S(2)}, u32[]{:S(2)}) %collective-permute-start.2) | collective-permute-done | bytes 196640 | tf_op jit(solution)/shard_map/ppermute | solution.py:541
  32.2 4.4 %collective-permute-done.3 = bf16[128,1536]{1,0:T(8,128)(2,1)S(1)} collective-permute-done((bf16[128,1536]{1,0:T(8,128)(2,1)S(1)}, bf16[128,1536]{1,0:T(8,128)(2,1)S(1)}, u32[]{:S(2)}, u32[]{:S(2)}) %collective-permute-start.3) | collective-permute-done | bytes 393248 | tf_op jit(solution)/shard_map/ppermute | solution.py:541
  40.8 7.5 %collective-permute-done.11 = bf16[128,1536]{1,0:T(8,128)(2,1)S(1)} collective-permute-done((bf16[128,1536]{1,0:T(8,128)(2,1)S(1)}, bf16[128,1536]{1,0:T(8,128)(2,1)S(1)}, u32[]{:S(2)}, u32[]{:S(2)}) %collective-permute-start.11) | collective-permute-done | bytes 393248 | tf_op jit(solution)/shard_map/ppermute | solution.py:541
  48.5 3.3 %collective-permute-done.13 = bf16[3,128,512]{2,1,0:T(8,128)(2,1)S(1)} collective-permute-done((bf16[3,128,512]{2,1,0:T(8,128)(2,1)S(1)}, bf16[3,128,512]{2,1,0:T(8,128)(2,1)S(1)}, u32[]{:S(2)}, u32[]{:S(2)}) %collective-permute-start.13) | collective-permute-done | bytes 393248 | tf_op jit(solution)/shard_map/ppermute | solution.py:541
  53.2 9.3 %layer_0_forward.1 = (bf16[512,1152]{1,0:T(8,128)(2,1)}, f32[512,384]{1,0:T(8,128)}, bf16[512,384]{1,0:T(8,128)(2,1)}, f32[512,512]{1,0:T(8,128)}, bf16[512,512]...) custom-call(s32[4]{0:T(128)} %pad_add_fusion.1.refs_0_.place_ref, ...), custom_call_target="tpu_custom_call" | custom-call | flops 10350000128 | tf_op jit(solution)/shard_map/layer_0_forward/pallas_call | solution.py:91
  64.1 6.0 %layer_1_attention.1 = (bf16[512,1152]{1,0:T(8,128)(2,1)}, f32[512,384]{1,0:T(8,128)}, bf16[512,384]{1,0:T(8,128)(2,1)}, f32[512,512]{1,0:T(8,128)}, bf16[512,512]{1,0:T(8,128)(2,1)}) custom-call(s32[4]{0:T(128)} %pad_add_fusion.1.refs_0_.place_ref, f32[512,512]{1,0:T(8,128)} %get-tuple-element.116.refs_1_, bf16[512,512]{1,0:T(8,128)(2,1)} %get-tuple-element.117.refs_2_, ...), custom_call_target="tpu_custom_call" | custom-call | flops 6899999744 | tf_op jit(solution)/shard_map/layer_1_attention/pallas_call | solution.py:91
  71.6 5.7 %collective-permute-done.15.refs_18_.refs_6_ = bf16[512,512]{1,0:T(8,128)(2,1)S(1)} collective-permute-done((bf16[512,512]{1,0:T(8,128)(2,1)S(1)}, bf16[512,512]{1,0:T(8,128)(2,1)S(1)}, u32[]{:S(2)}, u32[]{:S(2)}) %collective-permute-start.15) | collective-permute-done | bytes 524320 | tf_op jit(solution)/shard_map/ppermute | solution.py:541
  78.1 14.1 %layer_1_backward.1 = (f32[512,512]{1,0:T(8,128)}, bf16[512,512]{1,0:T(8,128)(2,1)}, bf16[512,1024]{1,0:T(8,128)(2,1)}, f32[56,128]{1,0:T(8,128)}, bf16[16,16,15...) custom-call(s32[4]{0:T(128)} %pad_add_fusion.1.refs_0_.place_ref, ...), custom_call_target="tpu_custom_call" | custom-call | flops 16099999744 | tf_op jit(solution)/shard_map/layer_1_backward/pallas_call | solution.py:91
  93.2 7.6 %layer_1_weight_grads.1 = (bf16[8,32,1536]{2,1,0:T(8,128)(2,1)}, bf16[8,32,1536]{2,1,0:T(8,128)(2,1)}) custom-call(s32[4]{0:T(128)} %pad_add_fusion.1.refs_0_.place_ref, bf16[512,512]{1,0:T(8,128)(2,1)} %get-tuple-element.126.refs_10_.refs_1_, bf16[512,512]{1,0:T(8,128)(2,1)} %bitcast.33, bf16[512,512]{1,0:T(8,128)(2,1)} %get-tuple-element.138.refs_3_, ...), custom_call_target="tpu_custom_call" | custom-call | flops 8049999872 | tf_op jit(solution)/shard_map/layer_1_weight_grads/pallas_call | solution.py:91
  106.3 15.3 %layer_0_backward.1 = (f32[512,512]{1,0:T(8,128)}, bf16[512,512]{1,0:T(8,128)(2,1)}, bf16[512,1024]{1,0:T(8,128)(2,1)}, f32[56,128]{1,0:T(8,128)}, bf16[16,16,15...) custom-call(s32[4]{0:T(128)} %pad_add_fusion.1.refs_0_.place_ref, f32[512,512]{1,0:T(8,128)} %get-tuple-element.106.refs_1_, ...), custom_call_target="tpu_custom_call" | custom-call | flops 16099999744 | tf_op jit(solution)/shard_map/layer_0_backward/pallas_call | solution.py:91
  125.2 9.7 %collective-permute-done.24.refs_5_ = bf16[512,512]{1,0:T(8,128)(2,1)S(1)} collective-permute-done((bf16[512,512]{1,0:T(8,128)(2,1)S(1)}, bf16[512,512]{1,0:T(8,128)(2,1)S(1)}, u32[]{:S(2)}, u32[]{:S(2)}) %collective-permute-start.24) | collective-permute-done | bytes 524320 | tf_op jit(solution)/shard_map/ppermute | solution.py:541
  135.7 7.6 %layer_0_weight_grads.1 = (bf16[8,32,1536]{2,1,0:T(8,128)(2,1)}, bf16[8,32,1536]{2,1,0:T(8,128)(2,1)}) custom-call(s32[4]{0:T(128)} %pad_add_fusion.1.refs_0_.place_ref, bf16[512,512]{1,0:T(8,128)(2,1)} %get-tuple-element.154.refs_10_.refs_1_, bf16[512,512]{1,0:T(8,128)(2,1)} %get-tuple-element.151.refs_2_, bf16[512,512]{1,0:T(8,128)(2,1)} %get-tuple-element.152.refs_3_, ...), custom_call_target="tpu_custom_call" | custom-call | flops 8049999872 | tf_op jit(solution)/shard_map/layer_0_weight_grads/pallas_call | solution.py:91
  149.4 7.9 %collective-permute-done.29 = bf16[4,32,1536]{2,1,0:T(8,128)(2,1)S(1)} collective-permute-done((bf16[4,32,1536]{2,1,0:T(8,128)(2,1)S(1)}, bf16[4,32,1536]{2,1,0:T(8,128)(2,1)S(1)}, u32[]{:S(2)}, u32[]{:S(2)}) %collective-permute-start.29) | collective-permute-done | bytes 393248 | tf_op jit(solution)/shard_map/ppermute | solution.py:541
  160.3 2.7 %collective-permute-start.40 = (bf16[1,16,1536]{2,1,0:T(8,128)(2,1)S(1)}, bf16[1,16,1536]{2,1,0:T(8,128)(2,1)S(1)}, u32[]{:S(2)}, u32[]{:S(2)}) collective-permute-start(bf16[1,16,1536]{2,1,0:T(8,128)(2,1)S(1)} %add_convert_fusion.31), channel_id=1, source_target_pairs={{0,16},{1,17},{2,18},{3,19},{4,20},{5,21},{6,22},{7,23},{8,24},{9,... | collective-permute-start | bytes 147464 | tf_op jit(solution)/shard_map/ppermute | solution.py:541
  172.9 3.8 %collective-permute-done.37 = bf16[2,32,1536]{2,1,0:T(8,128)(2,1)S(1)} collective-permute-done((bf16[2,32,1536]{2,1,0:T(8,128)(2,1)S(1)}, bf16[2,32,1536]{2,1,0:T(8,128)(2,1)S(1)}, u32[]{:S(2)}, u32[]{:S(2)}) %collective-permute-start.37) | collective-permute-done | bytes 196640 | tf_op jit(solution)/shard_map/ppermute | solution.py:541
  179.1 2.8 %collective-permute-start.46 = (f32[56,128]{1,0:T(8,128)S(1)}, f32[56,128]{1,0:T(8,128)S(1)}, u32[]{:S(2)}, u32[]{:S(2)}) collective-permute-start(f32[56,128]{1,0:T(8,128)S(1)} %add.156), channel_id=1, source_target_pairs={{0,16},{1,17},{2,18},{3,19},{4,20},{5,21},{6,22},{7,23},{8,24},{9,... | collective-permute-start | bytes 86024 | tf_op jit(solution)/shard_map/ppermute | solution.py:541
  189.1 3.7 %layer_1_ff_grads.1 = (f32[2,512,512]{2,1,0:T(8,128)}, f32[2,512,512]{2,1,0:T(8,128)}, f32[2,512,512]{2,1,0:T(8,128)}) custom-call(s32[4]{0:T(128)} %pad_add_fusion.1.refs_0_.place_ref, bf16[16,32,1536]{2,1,0:T(8,128)(2,1)} %copy-done.12), custom_call_target="tpu_custom_call" | custom-call | flops 3449999872 | tf_op jit(solution)/shard_map/layer_1_ff_grads/pallas_call | solution.py:466
  192.8 4.3 %collective-permute-done.47 = bf16[4,32,1536]{2,1,0:T(8,128)(2,1)S(1)} collective-permute-done((bf16[4,32,1536]{2,1,0:T(8,128)(2,1)S(1)}, bf16[4,32,1536]{2,1,0:T(8,128)(2,1)S(1)}, u32[]{:S(2)}, u32[]{:S(2)}) %collective-permute-start.47) | collective-permute-done | bytes 393248 | tf_op jit(solution)/shard_map/ppermute | solution.py:541
  200.8 2.9 %layer_0_ff_grads.2 = (f32[2,512,512]{2,1,0:T(8,128)}, f32[2,512,512]{2,1,0:T(8,128)}, f32[2,512,512]{2,1,0:T(8,128)}) custom-call(s32[4]{0:T(128)} %pad_add_fusion.1.refs_0_.place_ref, bf16[8,32,1536]{2,1,0:T(8,128)(2,1)} %copy-done, f32[2,512,512]{2,1,0:T(8,128)} %get-tuple-element.184.refs_0_, ...), custom_call_target="tpu_custom_call", output_to_operand_aliasing={{0}: (2, {}), {1}: (3, {}), {2}: (4, {})} | custom-call | flops 3449999872 | tf_op jit(solution)/shard_map/layer_0_ff_grads/pallas_call | solution.py:466
  204.6 2.9 %layer_0_ff_grads.3 = (f32[2,512,512]{2,1,0:T(8,128)}, f32[2,512,512]{2,1,0:T(8,128)}, f32[2,512,512]{2,1,0:T(8,128)}) custom-call(s32[4]{0:T(128)} %pad_add_fusion.1.refs_0_.place_ref, bf16[8,32,1536]{2,1,0:T(8,128)(2,1)} %copy-done.23, f32[2,512,512]{2,1,0:T(8,128)} %get-tuple-element.189.refs_0_, ...), custom_call_target="tpu_custom_call", output_to_operand_aliasing={{0}: (2, {}), {1}: (3, {}), {2}: (4, {})} | custom-call | flops 3449999872 | tf_op jit(solution)/shard_map/layer_0_ff_grads/pallas_call | solution.py:466
  (221 shorter events, 70.2 us)
Async XLA Ops:
  1.5 17.8 %collective-permute-start.8 = (bf16[16,1536]{1,0:T(8,128)(2,1)S(1)}, bf16[16,1536]{1,0:T(8,128)(2,1)S(1)}, u32[]{:S(2)}, u32[]{:S(2)}) collective-permute-start(bf16[16,1536]{1,0:T(8,128)(2,1)S(1)} %get-tuple-element.266), channel_id=1, source_target_pairs={{0,4},{1,5},{2,6},{3,7},{4,0},{5,1},{6,2},{7,3},{8,12},{9,13},{10,... | collective-permute-start | bytes 147464 | tf_op jit(solution)/shard_map/ppermute | solution.py:541
  4.5 13.1 %collective-permute-start = (bf16[16,1536]{1,0:T(8,128)(2,1)S(1)}, bf16[16,1536]{1,0:T(8,128)(2,1)S(1)}, u32[]{:S(2)}, u32[]{:S(2)}) collective-permute-start(bf16[16,1536]{1,0:T(8,128)(2,1)S(1)} %get-tuple-element.267), channel_id=1, source_target_pairs={{0,16},{1,17},{2,18},{3,19},{4,20},{5,21},{6,22},{7,23},{8,24},{9,... | collective-permute-start | bytes 147464 | tf_op jit(solution)/shard_map/ppermute | solution.py:541
  9.3 22.3 %collective-permute-start.4 = (bf16[6,128,512]{2,1,0:T(8,128)(2,1)S(1)}, bf16[6,128,512]{2,1,0:T(8,128)(2,1)S(1)}, u32[]{:S(2)}, u32[]{:S(2)}) collective-permute-start(bf16[6,128,512]{2,1,0:T(8,128)(2,1)S(1)} %pad_maximum_fusion), channel_id=1, source_target_pairs={{0,1},{1,0},{2,3},{3,2},{4,5},{5,4},{6,7},{7,6},{8,9},{9,8},{10,11... | collective-permute-start | bytes 2359304 | tf_op jit(solution)/shard_map/ppermute | solution.py:541
  36.7 15.2 %collective-permute-start.5 = (bf16[256,1536]{1,0:T(8,128)(2,1)S(1)}, bf16[256,1536]{1,0:T(8,128)(2,1)S(1)}, u32[]{:S(2)}, u32[]{:S(2)}) collective-permute-start(bf16[256,1536]{1,0:T(8,128)(2,1)S(1)} %constant_dynamic-update-slice_fusion.refs_7_.refs_11_), channel_id=1, source_target_pairs={{0,2},{1,3},{2,0},{3,1},{4,6},{5,7},{6,4},{7,5},{8,10},{9,11},{10,... | collective-permute-start | bytes 2359304 | tf_op jit(solution)/shard_map/ppermute | solution.py:541
  36.8 11.5 %collective-permute-start.11 = (bf16[128,1536]{1,0:T(8,128)(2,1)S(1)}, bf16[128,1536]{1,0:T(8,128)(2,1)S(1)}, u32[]{:S(2)}, u32[]{:S(2)}) collective-permute-start(bf16[128,1536]{1,0:T(8,128)(2,1)S(1)} %pad_maximum_fusion.4), channel_id=1, source_target_pairs={{0,1},{1,0},{2,3},{3,2},{4,5},{5,4},{6,7},{7,6},{8,9},{9,8},{10,11... | collective-permute-start | bytes 1179656 | tf_op jit(solution)/shard_map/ppermute | solution.py:541
  39.5 12.4 %collective-permute-start.7 = (bf16[6,128,512]{2,1,0:T(8,128)(2,1)S(1)}, bf16[6,128,512]{2,1,0:T(8,128)(2,1)S(1)}, u32[]{:S(2)}, u32[]{:S(2)}) collective-permute-start(bf16[6,128,512]{2,1,0:T(8,128)(2,1)S(1)} %constant_dynamic-update-slice_fusion.5.refs_12_.refs_16_), channel_id=1, source_target_pairs={{0,2},{1,3},{2,0},{3,1},{4,6},{5,7},{6,4},{7,5},{8,10},{9,11},{10,... | collective-permute-start | bytes 2359304 | tf_op jit(solution)/shard_map/ppermute | solution.py:541
  40.3 11.4 %collective-permute-start.13 = (bf16[3,128,512]{2,1,0:T(8,128)(2,1)S(1)}, bf16[3,128,512]{2,1,0:T(8,128)(2,1)S(1)}, u32[]{:S(2)}, u32[]{:S(2)}) collective-permute-start(bf16[3,128,512]{2,1,0:T(8,128)(2,1)S(1)} %get-tuple-element.127), channel_id=1, source_target_pairs={{0,4},{1,5},{2,6},{3,7},{4,0},{5,1},{6,2},{7,3},{8,12},{9,13},{10,... | collective-permute-start | bytes 1179656 | tf_op jit(solution)/shard_map/ppermute | solution.py:541
  48.3 14.8 %collective-permute-start.12 = (bf16[256,1536]{1,0:T(8,128)(2,1)S(1)}, bf16[256,1536]{1,0:T(8,128)(2,1)S(1)}, u32[]{:S(2)}, u32[]{:S(2)}) collective-permute-start(bf16[256,1536]{1,0:T(8,128)(2,1)S(1)} %constant_dynamic-update-slice_fusion.7.refs_6_.refs_11_), channel_id=1, source_target_pairs={{0,2},{1,3},{2,0},{3,1},{4,6},{5,7},{6,4},{7,5},{8,10},{9,11},{10,... | collective-permute-start | bytes 2359304 | tf_op jit(solution)/shard_map/ppermute | solution.py:541
  51.8 19.9 %collective-permute-start.14 = (bf16[6,128,512]{2,1,0:T(8,128)(2,1)S(1)}, bf16[6,128,512]{2,1,0:T(8,128)(2,1)S(1)}, u32[]{:S(2)}, u32[]{:S(2)}) collective-permute-start(bf16[6,128,512]{2,1,0:T(8,128)(2,1)S(1)} %constant_dynamic-update-slice_fusion.9.refs_16_), channel_id=1, source_target_pairs={{0,2},{1,3},{2,0},{3,1},{4,6},{5,7},{6,4},{7,5},{8,10},{9,11},{10,... | collective-permute-start | bytes 2359304 | tf_op jit(solution)/shard_map/ppermute | solution.py:541
  62.5 14.8 %collective-permute-start.15 = (bf16[512,512]{1,0:T(8,128)(2,1)S(1)}, bf16[512,512]{1,0:T(8,128)(2,1)S(1)}, u32[]{:S(2)}, u32[]{:S(2)}) collective-permute-start(bf16[512,512]{1,0:T(8,128)(2,1)S(1)} %bitcast.34), channel_id=1, source_target_pairs={{0,1},{1,0},{2,3},{3,2},{4,5},{5,4},{6,7},{7,6},{8,9},{9,8},{10,11... | collective-permute-start | bytes 1572872 | tf_op jit(solution)/shard_map/ppermute | solution.py:541
  70.1 22.3 %collective-permute-start.16 = (bf16[512,512]{1,0:T(8,128)(2,1)}, bf16[512,512]{1,0:T(8,128)(2,1)S(1)}, u32[]{:S(2)}, u32[]{:S(2)}) collective-permute-start(bf16[512,512]{1,0:T(8,128)(2,1)} %get-tuple-element.126.refs_10_.refs_1_), channel_id=1, source_target_pairs={{0,1},{1,0},{2,3},{3,2},{4,5},{5,4},{6,7},{7,6},{8,9},{9,8},{10,11... | collective-permute-start | bytes 1572872 | tf_op jit(solution)/shard_map/ppermute | solution.py:541
  101.3 23.9 %collective-permute-start.25 = (bf16[512,512]{1,0:T(8,128)(2,1)S(1)}, bf16[512,512]{1,0:T(8,128)(2,1)S(1)}, u32[]{:S(2)}, u32[]{:S(2)}) collective-permute-start(bf16[512,512]{1,0:T(8,128)(2,1)S(1)} %copy-done.26), channel_id=1, source_target_pairs={{0,1},{1,0},{2,3},{3,2},{4,5},{5,4},{6,7},{7,6},{8,9},{9,8},{10,11... | collective-permute-start | bytes 1572872 | tf_op jit(solution)/shard_map/ppermute | solution.py:541
  103.6 18.0 %collective-permute-start.21 = (bf16[4,32,1536]{2,1,0:T(8,128)(2,1)S(1)}, bf16[4,32,1536]{2,1,0:T(8,128)(2,1)S(1)}, u32[]{:S(2)}, u32[]{:S(2)}) collective-permute-start(bf16[4,32,1536]{2,1,0:T(8,128)(2,1)S(1)} %get-tuple-element.245.refs_22_), channel_id=1, source_target_pairs={{0,4},{1,5},{2,6},{3,7},{4,0},{5,1},{6,2},{7,3},{8,12},{9,13},{10,... | collective-permute-start | bytes 1179656 | tf_op jit(solution)/shard_map/ppermute | solution.py:541
  104.2 20.3 %collective-permute-start.20 = (bf16[8,16,1536]{2,1,0:T(8,128)(2,1)S(1)}, bf16[8,16,1536]{2,1,0:T(8,128)(2,1)S(1)}, u32[]{:S(2)}, u32[]{:S(2)}) collective-permute-start(bf16[8,16,1536]{2,1,0:T(8,128)(2,1)S(1)} %get-tuple-element.247), channel_id=1, source_target_pairs={{0,1},{1,0},{2,3},{3,2},{4,5},{5,4},{6,7},{7,6},{8,9},{9,8},{10,11... | collective-permute-start | bytes 1179656 | tf_op jit(solution)/shard_map/ppermute | solution.py:541
  104.8 30.1 %collective-permute-start.24 = (bf16[512,512]{1,0:T(8,128)(2,1)S(1)}, bf16[512,512]{1,0:T(8,128)(2,1)S(1)}, u32[]{:S(2)}, u32[]{:S(2)}) collective-permute-start(bf16[512,512]{1,0:T(8,128)(2,1)S(1)} %copy-done.25), channel_id=1, source_target_pairs={{0,1},{1,0},{2,3},{3,2},{4,5},{5,4},{6,7},{7,6},{8,9},{9,8},{10,11... | collective-permute-start | bytes 1572872 | tf_op jit(solution)/shard_map/ppermute | solution.py:541
  121.6 21.9 %collective-permute-start.19 = (bf16[16,16,1536]{2,1,0:T(8,128)(2,1)}, bf16[16,16,1536]{2,1,0:T(8,128)(2,1)S(1)}, u32[]{:S(2)}, u32[]{:S(2)}) collective-permute-start(bf16[16,16,1536]{2,1,0:T(8,128)(2,1)} %get-tuple-element.148), channel_id=1, source_target_pairs={{0,2},{1,3},{2,0},{3,1},{4,6},{5,7},{6,4},{7,5},{8,10},{9,11},{10,... | collective-permute-start | bytes 2359304 | tf_op jit(solution)/shard_map/ppermute | solution.py:541
  121.8 21.6 %collective-permute-start.23 = (bf16[2,32,1536]{2,1,0:T(8,128)(2,1)S(1)}, bf16[2,32,1536]{2,1,0:T(8,128)(2,1)S(1)}, u32[]{:S(2)}, u32[]{:S(2)}) collective-permute-start(bf16[2,32,1536]{2,1,0:T(8,128)(2,1)S(1)} %get-tuple-element.253), channel_id=1, source_target_pairs={{0,8},{1,9},{2,10},{3,11},{4,12},{5,13},{6,14},{7,15},{8,0},{9,1},... | collective-permute-start | bytes 589832 | tf_op jit(solution)/shard_map/ppermute | solution.py:541
  124.6 18.8 %collective-permute-start.22 = (bf16[4,16,1536]{2,1,0:T(8,128)(2,1)S(1)}, bf16[4,16,1536]{2,1,0:T(8,128)(2,1)S(1)}, u32[]{:S(2)}, u32[]{:S(2)}) collective-permute-start(bf16[4,16,1536]{2,1,0:T(8,128)(2,1)S(1)} %get-tuple-element.254.refs_10_), channel_id=1, source_target_pairs={{0,4},{1,5},{2,6},{3,7},{4,0},{5,1},{6,2},{7,3},{8,12},{9,13},{10,... | collective-permute-start | bytes 589832 | tf_op jit(solution)/shard_map/ppermute | solution.py:541
  146.1 11.2 %collective-permute-start.29 = (bf16[4,32,1536]{2,1,0:T(8,128)(2,1)S(1)}, bf16[4,32,1536]{2,1,0:T(8,128)(2,1)S(1)}, u32[]{:S(2)}, u32[]{:S(2)}) collective-permute-start(bf16[4,32,1536]{2,1,0:T(8,128)(2,1)S(1)} %get-tuple-element.240), channel_id=1, source_target_pairs={{0,4},{1,5},{2,6},{3,7},{4,0},{5,1},{6,2},{7,3},{8,12},{9,13},{10,... | collective-permute-start | bytes 1179656 | tf_op jit(solution)/shard_map/ppermute | solution.py:541
  146.7 13.6 %collective-permute-start.35 = (bf16[2,16,1536]{2,1,0:T(8,128)(2,1)S(1)}, bf16[2,16,1536]{2,1,0:T(8,128)(2,1)S(1)}, u32[]{:S(2)}, u32[]{:S(2)}) collective-permute-start(bf16[2,16,1536]{2,1,0:T(8,128)(2,1)S(1)} %get-tuple-element.260), channel_id=1, source_target_pairs={{0,8},{1,9},{2,10},{3,11},{4,12},{5,13},{6,14},{7,15},{8,0},{9,1},... | collective-permute-start | bytes 294920 | tf_op jit(solution)/shard_map/ppermute | solution.py:541
  147.0 10.8 %collective-permute-start.27 = (bf16[1,32,1536]{2,1,0:T(8,128)(2,1)S(1)}, bf16[1,32,1536]{2,1,0:T(8,128)(2,1)S(1)}, u32[]{:S(2)}, u32[]{:S(2)}) collective-permute-start(bf16[1,32,1536]{2,1,0:T(8,128)(2,1)S(1)} %add_convert_fusion.25), channel_id=1, source_target_pairs={{0,16},{1,17},{2,18},{3,19},{4,20},{5,21},{6,22},{7,23},{8,24},{9,... | collective-permute-start | bytes 294920 | tf_op jit(solution)/shard_map/ppermute | solution.py:541
  147.3 11.3 %collective-permute-start.26 = (bf16[8,16,1536]{2,1,0:T(8,128)(2,1)S(1)}, bf16[8,16,1536]{2,1,0:T(8,128)(2,1)S(1)}, u32[]{:S(2)}, u32[]{:S(2)}) collective-permute-start(bf16[8,16,1536]{2,1,0:T(8,128)(2,1)S(1)} %get-tuple-element.242), channel_id=1, source_target_pairs={{0,1},{1,0},{2,3},{3,2},{4,5},{5,4},{6,7},{7,6},{8,9},{9,8},{10,11... | collective-permute-start | bytes 1179656 | tf_op jit(solution)/shard_map/ppermute | solution.py:541
  148.2 14.8 %collective-permute-start.34 = (f32[56,128]{1,0:T(8,128)S(1)}, f32[56,128]{1,0:T(8,128)S(1)}, u32[]{:S(2)}, u32[]{:S(2)}) collective-permute-start(f32[56,128]{1,0:T(8,128)S(1)} %add.137), channel_id=1, source_target_pairs={{0,1},{1,0},{2,3},{3,2},{4,5},{5,4},{6,7},{7,6},{8,9},{9,8},{10,11... | collective-permute-start | bytes 86024 | tf_op jit(solution)/shard_map/ppermute | solution.py:541
  168.1 10.8 %collective-permute-start.36 = (bf16[2,16,1536]{2,1,0:T(8,128)(2,1)S(1)}, bf16[2,16,1536]{2,1,0:T(8,128)(2,1)S(1)}, u32[]{:S(2)}, u32[]{:S(2)}) collective-permute-start(bf16[2,16,1536]{2,1,0:T(8,128)(2,1)S(1)} %get-tuple-element.259), channel_id=1, source_target_pairs={{0,8},{1,9},{2,10},{3,11},{4,12},{5,13},{6,14},{7,15},{8,0},{9,1},... | collective-permute-start | bytes 294920 | tf_op jit(solution)/shard_map/ppermute | solution.py:541
  (57 other events, 332.8 us)

commit v4 on v3

--- a/solution.py
+++ b/solution.py
@@ -13,7 +13,7 @@
 bf16 = jnp.bfloat16
 f32 = jnp.float32
 axes = ("dp", "tensor")
-vmem_bytes = 56 * 1024 * 1024
+vmem_bytes = 26 * 1024 * 1024
 raw_names = ("attn_near", "attn_far", "ff_near", "ff_far", "w_gate", "w_up", "w_down")
 
 
@@ -57,9 +57,11 @@
 
 def run(body, name, ins, outs, scratch, after=(), micros=1):
     in_names, out_names, scratch_names = list(ins), list(outs), list(scratch)
-    staged = [n for n in in_names if n != "place" and n not in raw_names]
+    direct = {n for n in in_names if n == "place" or n in raw_names or isinstance(ins[n], Kept)}
+    staged = [n for n in in_names if n not in direct]
+    copied = [n for n in out_names if not isinstance(outs[n], Kept)]
     in_sems = {n: i for i, n in enumerate(staged)}
-    out_sems = {n: i for i, n in enumerate(out_names)}
+    out_sems = {n: i for i, n in enumerate(copied)}
 
     def kernel(*refs):
         refs = list(refs)
@@ -69,12 +71,12 @@
         refs = refs[len(out_names) :]
         space = dict(zip(scratch_names, refs))
         refs = refs[len(scratch_names) :]
-        buffers = dict(zip(staged + out_names, refs))
-        sems_in, sems_out = refs[len(staged) + len(out_names) :]
-        r = types.SimpleNamespace(**space, **buffers)
-        for n in in_names:
-            if n == "place" or n in raw_names:
-                setattr(r, n, sources[n])
+        buffers = dict(zip(staged + copied, refs))
+        sems_in, sems_out = refs[len(staged) + len(copied) :]
+        kept = {n: ref for n, ref in targets.items() if n not in out_sems}
+        r = types.SimpleNamespace(**space, **buffers, **kept)
+        for n in direct:
+            setattr(r, n, sources[n])
 
         def copy_in(n):
             return pltpu.make_async_copy(sources[n], buffers[n], sems_in.at[in_sems[n]])
@@ -82,29 +84,58 @@
         def copy_out(n):
             return pltpu.make_async_copy(buffers[n], targets[n], sems_out.at[out_sems[n]])
 
-        r.fetch = lambda *names: [copy_in(n).start() for n in names]
-        r.need = lambda *names: [copy_in(n).wait() for n in names]
-        r.write = lambda *names: [copy_out(n).start() for n in names]
-        r.drain = lambda *names: [copy_out(n).wait() for n in names]
+        r.fetch = lambda *names: [copy_in(n).start() for n in names if n in in_sems]
+        r.need = lambda *names: [copy_in(n).wait() for n in names if n in in_sems]
+        r.write = lambda *names: [copy_out(n).start() for n in names if n in out_sems]
+        r.drain = lambda *names: [copy_out(n).wait() for n in names if n in out_sems]
         body(r)
+
+    def in_space(n):
+        if n == "place":
+            return pltpu.SMEM
+        return pltpu.VMEM if isinstance(ins[n], Kept) else pl.ANY
 
     results = pl.pallas_call(
         kernel,
         name=name,
-        in_specs=[
-            pl.BlockSpec(memory_space=pltpu.SMEM if n == "place" else pl.ANY) for n in in_names
-        ]
+        in_specs=[pl.BlockSpec(memory_space=in_space(n)) for n in in_names]
         + [pl.BlockSpec(memory_space=pl.ANY) for _ in after],
-        out_specs=[pl.BlockSpec(memory_space=pl.ANY) for _ in outs],
-        out_shape=[jax.ShapeDtypeStruct(shape, kind) for shape, kind in outs.values()],
+        out_specs=[
+            pl.BlockSpec(memory_space=pltpu.VMEM if isinstance(out, Kept) else pl.ANY)
+            for out in outs.values()
+        ],
+        out_shape=[
+            pltpu.VMEM(*out.what) if isinstance(out, Kept) else jax.ShapeDtypeStruct(*out)
+            for out in outs.values()
+        ],
         scratch_shapes=list(scratch.values())
         + [pltpu.VMEM(ins[n].shape, ins[n].dtype) for n in staged]
-        + [pltpu.VMEM(shape, kind) for shape, kind in outs.values()]
-        + [pltpu.SemaphoreType.DMA((max(1, len(staged)),)), pltpu.SemaphoreType.DMA((len(outs),))],
+        + [pltpu.VMEM(*outs[n]) for n in copied]
+        + [
+            pltpu.SemaphoreType.DMA((max(1, len(staged)),)),
+            pltpu.SemaphoreType.DMA((max(1, len(copied)),)),
+        ],
         compiler_params=pltpu.CompilerParams(vmem_limit_bytes=vmem_bytes),
         cost_estimate=cost(micros),
-    )(*ins.values(), *after)
+    )(
+        *[
+            pltpu.with_memory_space_constraint(value.what, pltpu.VMEM)
+            if isinstance(value, Kept)
+            else value
+            for value in ins.values()
+        ],
+        *after,
+    )
     return types.SimpleNamespace(**dict(zip(outs, results)))
+
+
+class Kept:
+    def __init__(self, *what):
+        self.what = what[0] if len(what) == 1 else what
+
+
+def keep_all(names):
+    return {name: Kept(value) for name, value in names.items()}
 
 
 def chunks(extent, size):
@@ -171,7 +202,7 @@
     return jnp.where(is_low, both[:half], both[half:]).astype(bf16)
 
 
-def attention_forward(r, x_ref, a_ref, sizes):
+def attention_forward(r, x_ref, a_ref, sizes, layer_idx):
     series, slots, inner = sizes
     rows = series * slots
     for part in chunks(rows, 256):
@@ -199,10 +230,11 @@
             both = dot_tn(r.probs[here, at].astype(bf16), values)
             r.heads[here, at] = own_blocks(both, is_low)
     r.write("heads")
+    gain = r.gain_ff[layer_idx : layer_idx + 1, :]
     for part in chunks(rows, 256):
         middle = x_ref[part, :] + dot_nt(r.heads[part, :], r.attn_w[:, 3 * inner :])
         r.middle[part, :] = middle
-        r.ff_in[part, :] = (middle * inverse_rms(middle) * r.gain_ff[...]).astype(bf16)
+        r.ff_in[part, :] = (middle * inverse_rms(middle) * gain).astype(bf16)
     r.write("middle", "ff_in")
 
 
@@ -210,11 +242,11 @@
 
 
 def prepare_body(r):
-    r.fetch("inputs", "marks", "embed", "gain", "buckets", "table")
-    r.need("inputs", "marks", "embed", "gain", "buckets", "table")
+    r.fetch("inputs", "marks", "embed", "gain_attn", "buckets", "table")
+    r.need("inputs", "marks", "embed", "gain_attn", "buckets", "table")
     x = jnp.where(r.marks[:, 0:1] == 1, r.inputs[...].astype(f32), r.embed[...])
     r.x[...] = x
-    r.a[...] = (x * inverse_rms(x) * r.gain[...]).astype(bf16)
+    r.a[...] = (x * inverse_rms(x) * r.gain_attn[0:1, :]).astype(bf16)
     buckets = r.buckets[...]
     bias = jnp.zeros(buckets.shape, f32)
     for idx in range(r.table.shape[0]):
@@ -228,12 +260,12 @@
 def first_body(r, sizes, masks, grain):
     r.fetch("a")
     start_all(attention_copies(r, masks, grain))
-    r.fetch("bias", "mask", "x", "gain_ff", "gain_next")
+    r.fetch("bias", "mask", "x", "gain_ff", "gain_attn")
     start_all(ff_copies(r, 0))
     r.need("a")
     wait_all(r.attn_sem, r.attn_w)
-    r.need("bias", "mask", "x", "gain_ff", "gain_next")
-    attention_forward(r, r.x, r.a, sizes)
+    r.need("bias", "mask", "x", "gain_ff", "gain_attn")
+    attention_forward(r, r.x, r.a, sizes, 0)
     wait_all(r.ff_sem, r.ff_gate_up, r.ff_down)
     width = r.x.shape[1]
     for part in chunks(r.x.shape[0], 256):
@@ -243,7 +275,7 @@
             hidden = (gelu_terms(both[:, :width])[0] * both[:, width:]).astype(bf16)
             x_next = x_next + dot_nn(hidden, r.ff_down[half])
         r.x_next[part, :] = x_next
-        r.a_next[part, :] = (x_next * inverse_rms(x_next) * r.gain_next[...]).astype(bf16)
+        r.a_next[part, :] = (x_next * inverse_rms(x_next) * r.gain_attn[1:2, :]).astype(bf16)
     r.write("x_next", "a_next")
     r.drain(*attn_out_names, "x_next", "a_next")
 
@@ -255,18 +287,18 @@
     r.need("a")
     wait_all(r.attn_sem, r.attn_w)
     r.need("bias", "mask", "x", "gain_ff")
-    attention_forward(r, r.x, r.a, sizes)
+    attention_forward(r, r.x, r.a, sizes, 1)
     r.drain(*attn_out_names)
 
 
-def backward_body(r, sizes, masks, grain, layer_idx, last, piece_masks, heads):
+def backward_body(r, sizes, layer_idx, last, piece_masks, heads):
     series, slots, inner = sizes
     rows = series * slots
     width = r.x.shape[1]
     r.fetch("grad", "ff_in", "gain_ff", "gain_attn")
-    start_all(ff_copies(r, layer_idx))
+    if last:
+        start_all(ff_copies(r, layer_idx))
     r.fetch("middle")
-    start_all(attention_copies(r, masks, grain))
     r.fetch("qkv", "probs", "heads", "a", "x")
     if not last:
         r.fetch("bias_before", "marks", "buckets", "small_before")
@@ -274,8 +306,11 @@
     if not last:
         r.need("small_before")
         r.small[...] = r.small_before[...]
-    wait_all(r.ff_sem, r.ff_gate_up, r.ff_down)
+    if last:
+        wait_all(r.ff_sem, r.ff_gate_up, r.ff_down)
     r.need("middle")
+    gain_ff = r.gain_ff[layer_idx : layer_idx + 1, :]
+    gain_attn = r.gain_attn[layer_idx : layer_idx + 1, :]
     gain_total = jnp.zeros((1, width), f32)
     for part in chunks(rows, 256):
         grad = r.grad[part, :].astype(f32)
@@ -306,7 +341,7 @@
             back = term if back is None else back + term
         if last:
             r.outputs[part, :] = total.astype(bf16)
-        grad_mid, gain_part = norm_back(middle, r.gain_ff[...], back)
+        grad_mid, gain_part = norm_back(middle, gain_ff, back)
         gain_total += gain_part
         grad_mid = grad + grad_mid
         r.grad_mid[part, :] = grad_mid
@@ -317,7 +352,6 @@
     r.write("hidden", "grad_gate_up")
     if last:
         r.write("outputs")
-    wait_all(r.attn_sem, r.attn_w)
     for part in chunks(rows, 256):
         r.grad_heads[part, :] = dot_nn(r.branch[part, :], r.attn_w[:, 3 * inner :]).astype(bf16)
     r.need("qkv", "probs", "heads", "a", "x")
@@ -360,7 +394,7 @@
     embed_total = jnp.zeros((1, width), f32)
     for part in chunks(rows, 256):
         grad_normed = dot_nt(r.grad_qkv[part, :], r.attn_w[:, : 3 * inner])
-        grad_in, gain_part = norm_back(r.x[part, :], r.gain_attn[...], grad_normed)
+        grad_in, gain_part = norm_back(r.x[part, :], gain_attn, grad_normed)
         gain_total += gain_part
         grad_in = r.grad_mid[part, :] + grad_in
         if last:
@@ -411,24 +445,15 @@
         target[idx % (count // 2)] = whole[source, :].astype(bf16)
 
 
-def weight_body(r, layer_idx, piece_masks):
+def weight_body(r, piece_masks):
     width = r.ff_in.shape[1]
     rows = r.ff_in.shape[0]
     r.fetch("peer_in", "peer_grad")
-    copies = [
-        pltpu.make_async_copy(
-            own.at[layer_idx], r.ff_gate_up.at[:, pl.ds(k * width, width)], r.ff_sem
-        )
-        for k, own in enumerate((r.w_gate, r.w_up))
-    ]
-    copies.append(pltpu.make_async_copy(r.w_down.at[layer_idx], r.ff_down, r.ff_sem))
-    start_all(copies)
     r.fetch("ff_in", "grad_gate_up", "hidden", "grad")
     r.need("peer_in", "peer_grad")
-    wait_all(r.ff_sem, r.ff_gate_up, r.ff_down)
     for part in chunks(rows, 256):
-        both = dot_nn(r.peer_in[part, :], r.ff_gate_up[...])
-        grad_hidden = dot_nt(r.peer_grad[part, :], r.ff_down[...])
+        both = dot_nn(r.peer_in[part, :], r.ff_gate_up[0])
+        grad_hidden = dot_nt(r.peer_grad[part, :], r.ff_down[0])
         gate_act, up_act = both[:, :width], both[:, width:]
         mixed, slope = gelu_terms(gate_act)
         r.peer_gate_up[part, :width] = (grad_hidden * up_act * slope).astype(bf16)
@@ -452,34 +477,32 @@
 
     def kernel(place_ref, source, *refs):
         outs = refs[count : count + 3]
-        held, stage, in_sem, out_sem = refs[count + 3 :]
-        copy_in = pltpu.make_async_copy(source, held, in_sem)
-        copy_in.start()
-        copy_in.wait()
+        stage, out_sem = refs[count + 3 :]
         for idx, mask in enumerate(masks):
             rows = pl.ds(pl.multiple_of((place_ref[3] ^ mask) * grain, grain), grain)
             for k, out in enumerate(outs):
-                stage[k, idx] = held[idx, :, k * width : (k + 1) * width].astype(f32)
+                stage[k, idx] = source[idx, :, k * width : (k + 1) * width].astype(f32)
                 pltpu.make_async_copy(stage.at[k, idx], out.at[layer_idx, rows], out_sem).start()
         pltpu.make_async_copy(stage, stage, out_sem).wait()
 
     return pl.pallas_call(
         kernel,
         name="layer_%d_ff_grads" % layer_idx,
-        in_specs=[pl.BlockSpec(memory_space=pltpu.SMEM)]
-        + [pl.BlockSpec(memory_space=pl.ANY)] * (1 + count),
+        in_specs=[
+            pl.BlockSpec(memory_space=pltpu.SMEM),
+            pl.BlockSpec(memory_space=pltpu.VMEM),
+        ]
+        + [pl.BlockSpec(memory_space=pl.ANY)] * count,
         out_specs=[pl.BlockSpec(memory_space=pl.ANY)] * 3,
         out_shape=[jax.ShapeDtypeStruct(shape, f32)] * 3,
         input_output_aliases={2 + k: k for k in range(count)},
         scratch_shapes=[
-            pltpu.VMEM(pieces.shape, bf16),
             pltpu.VMEM((3, len(masks), grain, width), f32),
-            pltpu.SemaphoreType.DMA,
             pltpu.SemaphoreType.DMA,
         ],
         compiler_params=pltpu.CompilerParams(vmem_limit_bytes=vmem_bytes),
         cost_estimate=cost(3),
-    )(place, pieces, *before)
+    )(place, pltpu.with_memory_space_constraint(pieces, pltpu.VMEM), *before)
 
 
 def small_body(r):
@@ -570,30 +593,34 @@
     )
     ff_quarter = swap(ff_blocks, 1).reshape(3, 2, quarter, width)
 
-    wide_buckets = jnp.tile(buckets.T, (1, heads))
-    wide_table = jnp.repeat(bias_table, slots, axis=1)
-    marks = jnp.stack([patch_valid.reshape(rows), attention_mask.reshape(rows)], axis=1)
-
-    start = run(
-        prepare_body,
-        "prepare",
-        dict(
-            inputs=inputs.reshape(matrix),
-            marks=marks,
-            embed=mask_embed[None, :],
-            gain=gain_attn[0:1],
-            buckets=wide_buckets,
-            table=wide_table,
-        ),
-        dict(
-            x=(matrix, f32),
-            a=(matrix, bf16),
-            bias=((slots, heads * slots), f32),
-            mask=((rows, 128), jnp.int32),
-        ),
-        {},
-        micros=3,
-    )
+    def prepare(token):
+        table, marked, kept, near = (
+            tie(array, token) for array in (bias_table, patch_valid, attention_mask, buckets)
+        )
+        wide_buckets = jnp.tile(near.T, (1, heads))
+        wide_table = jnp.repeat(table, slots, axis=1)
+        marks = jnp.stack([marked.reshape(rows), kept.reshape(rows)], axis=1)
+        result = run(
+            prepare_body,
+            "prepare",
+            dict(
+                inputs=inputs.reshape(matrix),
+                marks=marks,
+                embed=mask_embed[None, :],
+                gain_attn=gain_attn,
+                buckets=wide_buckets,
+                table=wide_table,
+            ),
+            dict(
+                x=Kept(matrix, f32),
+                a=Kept(matrix, bf16),
+                bias=Kept((slots, heads * slots), f32),
+                mask=Kept((rows, 128), jnp.int32),
+            ),
+            {},
+            micros=3,
+        )
+        return result, wide_buckets, marks
 
     own_rows = packed.shape[1]
     direct = own_rows % 16 == 0
@@ -606,6 +633,8 @@
             got_0, got_1 = swap(block_0, hop_0), swap(block_1, hop_1)
             block_0 = join(block_0, got_0)
             block_1 = join(block_1, tie(got_1, block_0))
+            if hop_0 == hops_0[0]:
+                start, wide_buckets, marks = prepare(block_1)
         got_0 = swap(block_0, 1)
         ff_0 = tie(ff_quarter[:, 0], block_0)
         got_ff_0 = swap(ff_0, 4)
@@ -613,47 +642,38 @@
         block_1 = tie(block_1, block_0)
         got_1 = swap(block_1, 1)
         ff_0 = join(ff_0, tie(got_ff_0, block_0))
-        ff_1 = tie(ff_quarter[:, 1], ff_0)
-        ff_1 = join(ff_1, swap(ff_1, 4))
-        block_1 = join(block_1, got_1)
-        attn_pieces = [
-            (block_0, swap(block_0, 2), order_masks(hops_0[::-1])),
-            (block_1, swap(block_1, 2), order_masks(hops_1[::-1])),
-        ]
+        got_ff_1 = swap(tie(ff_quarter[:, 1], ff_0), 4)
+        attn_pieces = [(block_0, swap(block_0, 2), order_masks(hops_0[::-1]))]
+        peer_cotangent = swap(tie(cotangent, got_1), 1)
     else:
-        ff_0, ff_1 = (
-            join(ff_quarter[:, layer_idx], swap(ff_quarter[:, layer_idx], 4))
-            for layer_idx in range(2)
-        )
-        attn_pieces = []
-        for layer_idx in range(2):
-            whole = lax.all_gather(packed[layer_idx], axes, axis=0, tiled=True)
-            attn_pieces.append((whole, whole, [0]))
-    ff_pieces = [(ff_0, swap(ff_0, 2)), (ff_1, swap(ff_1, 2))]
+        ff_0 = join(ff_quarter[:, 0], swap(ff_quarter[:, 0], 4))
+        start, wide_buckets, marks = prepare(packed)
+        whole = lax.all_gather(packed[0], axes, axis=0, tiled=True)
+        attn_pieces = [(whole, whole, [0])]
+        peer_cotangent = swap(cotangent, 1)
+    ff_pieces = [(ff_0, swap(ff_0, 2))]
 
     def attn_ins(layer_idx):
         near, far, masks = attn_pieces[layer_idx]
-        return dict(attn_near=near, attn_far=far), masks
+        return dict(attn_near=Kept(near), attn_far=Kept(far)), masks
 
     def ff_ins(layer_idx):
         near, far = ff_pieces[layer_idx]
-        return dict(w_gate=w_gate, w_up=w_up, w_down=w_down, ff_near=near, ff_far=far)
-
-    attn_scratch = dict(
-        attn_w=pltpu.VMEM((width, 4 * inner), bf16), attn_sem=pltpu.SemaphoreType.DMA
-    )
-    ff_scratch = dict(
-        ff_gate_up=pltpu.VMEM((2, width, 2 * width), bf16),
-        ff_down=pltpu.VMEM((2, width, width), bf16),
-        ff_sem=pltpu.SemaphoreType.DMA,
+        return dict(w_gate=w_gate, w_up=w_up, w_down=w_down, ff_near=Kept(near), ff_far=Kept(far))
+
+    attn_scratch = dict(attn_sem=pltpu.SemaphoreType.DMA)
+    ff_scratch = dict(ff_sem=pltpu.SemaphoreType.DMA)
+    ff_outs = dict(
+        ff_gate_up=Kept((2, width, 2 * width), bf16), ff_down=Kept((2, width, width), bf16)
     )
     grain = own_rows if direct else width
     attn_outs = dict(
-        qkv=((rows, 3 * inner), bf16),
-        probs=((rows, heads * slots), f32),
-        heads=((rows, inner), bf16),
-        middle=(matrix, f32),
-        ff_in=(matrix, bf16),
+        attn_w=Kept((width, 4 * inner), bf16),
+        qkv=Kept((rows, 3 * inner), bf16),
+        probs=Kept((rows, heads * slots), f32),
+        heads=Kept((rows, inner), bf16),
+        middle=Kept(matrix, f32),
+        ff_in=Kept(matrix, bf16),
     )
 
     pieces, masks = attn_ins(0)
@@ -662,31 +682,41 @@
         "layer_0_forward",
         dict(
             place=place,
-            x=start.x,
-            a=start.a,
-            bias=start.bias,
-            mask=start.mask,
-            gain_ff=gain_ff[0:1],
-            gain_next=gain_attn[1:2],
+            x=Kept(start.x),
+            a=Kept(start.a),
+            bias=Kept(start.bias),
+            mask=Kept(start.mask),
+            gain_ff=gain_ff,
+            gain_attn=gain_attn,
             **pieces,
             **ff_ins(0),
         ),
-        dict(**attn_outs, x_next=(matrix, f32), a_next=(matrix, bf16)),
+        dict(**attn_outs, **ff_outs, x_next=Kept(matrix, f32), a_next=Kept(matrix, bf16)),
         dict(**attn_scratch, **ff_scratch),
         micros=9,
     )
-    peer_cotangent = swap(tie(cotangent, first.ff_in), 1)
+    peer_in_0 = swap(first.ff_in, 1)
+    if direct:
+        block_1 = join(block_1, tie(got_1, first.ff_in))
+        attn_pieces.append((block_1, swap(block_1, 2), order_masks(hops_1[::-1])))
+        ff_1 = tie(ff_quarter[:, 1], ff_0)
+        ff_1 = join(ff_1, tie(got_ff_1, first.ff_in))
+    else:
+        whole = lax.all_gather(packed[1], axes, axis=0, tiled=True)
+        attn_pieces.append((whole, whole, [0]))
+        ff_1 = join(ff_quarter[:, 1], swap(ff_quarter[:, 1], 4))
+    ff_pieces.append((ff_1, swap(ff_1, 2)))
     pieces, masks = attn_ins(1)
     second = run(
         functools.partial(second_body, sizes=sizes, masks=masks, grain=grain),
         "layer_1_attention",
         dict(
             place=place,
-            x=first.x_next,
-            a=first.a_next,
-            bias=start.bias,
-            mask=start.mask,
-            gain_ff=gain_ff[1:2],
+            x=Kept(first.x_next),
+            a=Kept(first.a_next),
+            bias=Kept(start.bias),
+            mask=Kept(start.mask),
+            gain_ff=gain_ff,
             **pieces,
         ),
         attn_outs,
@@ -710,13 +740,13 @@
 
     def backward(layer_idx, kept, x, a, grad, extra_ins, extra_outs, extra_scratch, after=()):
         last = layer_idx == 1
-        pieces, masks = attn_ins(layer_idx)
+        ff_given = ff_ins(1) if last else keep_all(
+            dict(ff_gate_up=kept.ff_gate_up, ff_down=kept.ff_down)
+        )
         return run(
             functools.partial(
                 backward_body,
                 sizes=sizes,
-                masks=masks,
-                grain=grain,
                 layer_idx=layer_idx,
                 last=last,
                 piece_masks=attn_masks,
@@ -725,27 +755,27 @@
             "layer_%d_backward" % layer_idx,
             dict(
                 place=place,
-                x=x,
-                a=a,
+                x=Kept(x),
+                a=Kept(a),
                 grad=grad,
-                gain_attn=gain_attn[layer_idx : layer_idx + 1],
-                gain_ff=gain_ff[layer_idx : layer_idx + 1],
-                qkv=kept.qkv,
-                probs=kept.probs,
-                heads=kept.heads,
-                middle=kept.middle,
-                ff_in=kept.ff_in,
-                **pieces,
-                **ff_ins(layer_idx),
+                gain_attn=gain_attn,
+                gain_ff=gain_ff,
+                attn_w=Kept(kept.attn_w),
+                qkv=Kept(kept.qkv),
+                probs=Kept(kept.probs),
+                heads=Kept(kept.heads),
+                middle=Kept(kept.middle),
+                ff_in=Kept(kept.ff_in),
+                **ff_given,
                 **extra_ins,
             ),
             dict(
-                grad_next=(matrix, f32),
-                hidden=(matrix, bf16),
-                grad_gate_up=((rows, 2 * width), bf16),
-                small=(small_shape, f32),
-                attn_keep=(attn_half, bf16),
-                attn_send=(attn_half, bf16),
+                hidden=Kept(matrix, bf16),
+                grad_gate_up=Kept((rows, 2 * width), bf16),
+                small=Kept(small_shape, f32),
+                attn_keep=Kept(attn_half, bf16),
+                attn_send=Kept(attn_half, bf16),
+                **(ff_outs if last else {}),
                 **extra_outs,
             ),
             dict(
@@ -756,38 +786,33 @@
                 grad_scores=pltpu.VMEM((rows, heads * slots), bf16),
                 attn_grad=pltpu.VMEM((width, 4 * inner), f32),
                 pulled=pltpu.VMEM((256, 2 * width), bf16),
-                **attn_scratch,
-                **ff_scratch,
+                **(ff_scratch if last else {}),
                 **extra_scratch,
             ),
             after=after,
             micros=14,
         )
 
-    def weight_grads(layer_idx, kept, back, grad, peer_in, peer_grad, after=()):
+    def weight_grads(layer_idx, kept, weights, back, grad, peer_in, peer_grad, after=()):
         return run(
-            functools.partial(weight_body, layer_idx=layer_idx, piece_masks=ff_masks),
+            functools.partial(weight_body, piece_masks=ff_masks),
             "layer_%d_weight_grads" % layer_idx,
             dict(
                 place=place,
-                ff_in=kept.ff_in,
+                ff_in=Kept(kept.ff_in),
                 grad=grad,
-                hidden=back.hidden,
-                grad_gate_up=back.grad_gate_up,
-                peer_in=peer_in,
-                peer_grad=peer_grad,
-                w_gate=w_gate,
-                w_up=w_up,
-                w_down=w_down,
+                hidden=Kept(back.hidden),
+                grad_gate_up=Kept(back.grad_gate_up),
+                peer_in=Kept(peer_in),
+                peer_grad=Kept(peer_grad),
+                ff_gate_up=Kept(weights.ff_gate_up),
+                ff_down=Kept(weights.ff_down),
             ),
-            dict(ff_keep=(ff_half, bf16), ff_send=(ff_half, bf16)),
+            dict(ff_keep=Kept(ff_half, bf16), ff_send=Kept(ff_half, bf16)),
             dict(
                 peer_gate_up=pltpu.VMEM((rows, 2 * width), bf16),
                 peer_hidden=pltpu.VMEM(matrix, bf16),
                 ff_grad=pltpu.VMEM((width, 3 * width), f32),
-                ff_gate_up=pltpu.VMEM((width, 2 * width), bf16),
-                ff_down=pltpu.VMEM((width, width), bf16),
-                ff_sem=pltpu.SemaphoreType.DMA,
             ),
             after=after,
             micros=7,
@@ -864,32 +889,34 @@
         {},
         dict(
             outputs=(matrix, bf16),
-            grad_next_low=(matrix, bf16),
-            bias_acc=((slots, heads * slots), f32),
+            grad_next=Kept(matrix, f32),
+            grad_next_low=Kept(matrix, bf16),
+            bias_acc=Kept((slots, heads * slots), f32),
         ),
         {},
         after=(peer_cotangent,),
     )
     peer_grad_0 = swap(back_1.grad_next_low, 1)
-    part_1 = weight_grads(1, second, back_1, cotangent, peer_in_1, peer_cotangent)
+    part_1 = weight_grads(
+        1, second, back_1, back_1, cotangent, peer_in_1, peer_cotangent, after=(peer_in_0,)
+    )
     attn_1 = Chain(attn_chain, back_1)
     ff_1 = Chain(ff_chain, part_1)
     token = attn_1.step(part_1.ff_send)
     token = ff_1.step(token)
-    peer_in_0 = swap(tie(first.ff_in, token), 1)
     back_0 = backward(
         0,
         first,
         start.x,
         start.a,
-        back_1.grad_next,
+        Kept(back_1.grad_next),
         dict(
-            bias_before=back_1.bias_acc,
+            bias_before=Kept(back_1.bias_acc),
             marks=marks,
             buckets=wide_buckets,
-            small_before=back_1.small,
+            small_before=Kept(back_1.small),
         ),
-        {},
+        dict(grad_next=(matrix, f32)),
         dict(
             bias_acc=pltpu.VMEM((slots, heads * slots), f32),
             table_rows=pltpu.VMEM((bias_table.shape[0], heads * slots), f32),
@@ -900,7 +927,14 @@
     token = ff_1.step(back_0.attn_send)
     token = attn_1.step(token)
     part_0 = weight_grads(
-        0, first, back_0, back_1.grad_next_low, peer_in_0, peer_grad_0, after=(token,)
+        0,
+        first,
+        first,
+        back_0,
+        Kept(back_1.grad_next_low),
+        peer_in_0,
+        peer_grad_0,
+        after=(token,),
     )
     ff_0 = Chain(ff_chain, part_0)
     small = Chain(summing, back_0.small, attn_hops)
@@ -928,7 +962,7 @@
     sums = run(
         small_body,
         "small_sums",
-        dict(packed=small.out["piece"]),
+        dict(packed=Kept(small.out["piece"])),
         dict(
             gain_attn=((2, width), f32),
             gain_ff=((2, width), f32),

time: 208 us -> 199 us (0.957)
  Pallas kernels: 73.6 us -> 49.6 us
  starting transfers between devices: 35.3 us -> 57 us
  local copies, waits for them, and re-layouts: 15.3 us -> 11.3 us
  waiting for transfers between devices: 77.7 us -> 74.9 us
    ppermute x50, starting transfers between devices: 35.3 us -> 57 us  [swap(): return lax.ppermute(array, axes, [(n, n ^ mask) for n in range(devices)])]
    pallas_call x8, Pallas kernels: 64.1 us -> 44.1 us  [run(): pl.pallas_call(kernel, name=name, in_specs=[pl.BlockSpec(memory_space=in_...]
    pallas_call x3, Pallas kernels: 9.57 us -> 5.51 us  [finish(): pl.pallas_call(kernel, name='layer_%d_ff_grads' % layer_idx, in_specs=[pl...]
    ppermute x50, waiting for transfers between devices: 77.7 us -> 74.9 us  [swap(): return lax.ppermute(array, axes, [(n, n ^ mask) for n in range(devices)])]
    unnamed x74 -> x65, local copies, waits for them, and re-layouts: 8.45 us -> 6.06 us
  transfers between devices with their start and end apart: 50 -> 50, of which waited for: 24 -> 23; matrix products, arithmetic and copies ran while one was open for 6% -> 5% of each run, Pallas kernels for 34% -> 24%
where the time goes in v4:
time: 199 us
  waiting for transfers between devices  74.9 us (38%)
  starting transfers between devices  57 us (29%)
  Pallas kernels  49.6 us (25%)
  local copies, waits for them, and re-layouts  11.3 us (6%)
  other arithmetic  4.61 us (2%)
    ppermute x50, waiting for transfers between devices, swap(): return lax.ppermute(array, axes, [(n, n ^ mask) for n in range(devices)])  74.9 us
    ppermute x50, starting transfers between devices, swap(): return lax.ppermute(array, axes, [(n, n ^ mask) for n in range(devices)])  57 us
    pallas_call x8, Pallas kernels, run(): pl.pallas_call(kernel, name=name, in_specs=[pl.BlockSpec(memory_space=in_...  44.1 us
    unnamed x65, local copies, waits for them, and re-layouts  6.06 us
    pallas_call x3, Pallas kernels, finish(): pl.pallas_call(kernel, name='layer_%d_ff_grads' % layer_idx, in_specs=[pl...  5.51 us
  transfers between devices with their start and end apart: 50, of which 23 were waited for; matrix products, arithmetic and copies ran while one was open for 5% of the time, Pallas kernels for 24%

profile of v4, /device:TPU:0, one launch (start us, length us, event | category | flops | bytes accessed | tf_op | source)
XLA Modules:
  0.0 199.0 jit_solution(2634434837535492345)
XLA Ops:
  3.7 3.0 %collective-permute-start.5 = (bf16[6,128,512]{2,1,0:T(8,128)(2,1)S(1)}, bf16[6,128,512]{2,1,0:T(8,128)(2,1)S(1)}, u32[]{:S(2)}, u32[]{:S(2)}) collective-permute-start(bf16[6,128,512]{2,1,0:T(8,128)(2,1)S(1)} %pad_maximum_fusion), channel_id=1, source_target_pairs={{0,1},{1,0},{2,3},{3,2},{4,5},{5,4},{6,7},{7,6},{8,9},{9,8},{10,11... | collective-permute-start | bytes 2359304 | tf_op jit(solution)/shard_map/ppermute | solution.py:564
  6.7 2.7 %collective-permute-start.1 = (bf16[16,1536]{1,0:T(8,128)(2,1)S(1)}, bf16[16,1536]{1,0:T(8,128)(2,1)S(1)}, u32[]{:S(2)}, u32[]{:S(2)}) collective-permute-start(bf16[16,1536]{1,0:T(8,128)(2,1)S(1)} %get-tuple-element.288), channel_id=1, source_target_pairs={{0,16},{1,17},{2,18},{3,19},{4,20},{5,21},{6,22},{7,23},{8,24},{9,... | collective-permute-start | bytes 147464 | tf_op jit(solution)/shard_map/ppermute | solution.py:564
  13.5 3.0 %collective-permute-start.9 = (bf16[32,1536]{1,0:T(8,128)(2,1)S(1)}, bf16[32,1536]{1,0:T(8,128)(2,1)S(1)}, u32[]{:S(2)}, u32[]{:S(2)}) collective-permute-start(bf16[32,1536]{1,0:T(8,128)(2,1)S(1)} %pad_maximum_fusion.13), channel_id=1, source_target_pairs={{0,16},{1,17},{2,18},{3,19},{4,20},{5,21},{6,22},{7,23},{8,24},{9,... | collective-permute-start | bytes 294920 | tf_op jit(solution)/shard_map/ppermute | solution.py:564
  21.4 3.5 %collective-permute-done.3 = bf16[64,1536]{1,0:T(8,128)(2,1)S(1)} collective-permute-done((bf16[64,1536]{1,0:T(8,128)(2,1)S(1)}, bf16[64,1536]{1,0:T(8,128)(2,1)S(1)}, u32[]{:S(2)}, u32[]{:S(2)}) %collective-permute-start.3) | collective-permute-done | bytes 196640 | tf_op jit(solution)/shard_map/ppermute | solution.py:564
  28.6 4.4 %collective-permute-done.4 = bf16[128,1536]{1,0:T(8,128)(2,1)S(1)} collective-permute-done((bf16[128,1536]{1,0:T(8,128)(2,1)S(1)}, bf16[128,1536]{1,0:T(8,128)(2,1)S(1)}, u32[]{:S(2)}, u32[]{:S(2)}) %collective-permute-start.4) | collective-permute-done | bytes 393248 | tf_op jit(solution)/shard_map/ppermute | solution.py:564
  37.8 6.0 %collective-permute-done.10 = bf16[64,1536]{1,0:T(8,128)(2,1)} collective-permute-done((bf16[64,1536]{1,0:T(8,128)(2,1)}, bf16[64,1536]{1,0:T(8,128)(2,1)}, u32[]{:S(2)}, u32[]{:S(2)}) %collective-permute-start.10) | collective-permute-done | bytes 196640 | tf_op jit(solution)/shard_map/ppermute | solution.py:564
  48.9 9.4 %layer_0_forward.1 = (bf16[512,1536]{1,0:T(8,128)(2,1)S(1)}, bf16[512,1152]{1,0:T(8,128)(2,1)S(1)}, f32[512,384]{1,0:T(8,128)S(1)}, bf16[512,384]{1,0:T(8,128)(2...) custom-call(s32[4]{0:T(128)S(1)} %pad_add_fusion.1.refs_0_.place_ref, ...), custom_call_target="tpu_custom_call" | custom-call | flops 10350000128 | tf_op jit(solution)/shard_map/layer_0_forward/pallas_call | solution.py:98
  60.1 9.9 %collective-permute-done.13 = bf16[3,128,512]{2,1,0:T(8,128)(2,1)S(1)} collective-permute-done((bf16[3,128,512]{2,1,0:T(8,128)(2,1)S(1)}, bf16[3,128,512]{2,1,0:T(8,128)(2,1)S(1)}, u32[]{:S(2)}, u32[]{:S(2)}) %collective-permute-start.13) | collective-permute-done | bytes 393248 | tf_op jit(solution)/shard_map/ppermute | solution.py:564
  72.2 5.0 %layer_1_attention.1 = (bf16[512,1536]{1,0:T(8,128)(2,1)S(1)}, bf16[512,1152]{1,0:T(8,128)(2,1)S(1)}, f32[512,384]{1,0:T(8,128)S(1)}, bf16[512,384]{1,0:T(8,128)...) custom-call(s32[4]{0:T(128)S(1)} %pad_add_fusion.1.refs_0_.place_ref, ...), custom_call_target="tpu_custom_call" | custom-call | flops 6899999744 | tf_op jit(solution)/shard_map/layer_1_attention/pallas_call | solution.py:98
  77.9 7.0 %collective-permute-done.15.refs_17_.refs_6_ = bf16[512,512]{1,0:T(8,128)(2,1)S(1)} collective-permute-done((bf16[512,512]{1,0:T(8,128)(2,1)S(1)}, bf16[512,512]{1,0:T(8,128)(2,1)S(1)}, u32[]{:S(2)}, u32[]{:S(2)}) %collective-permute-start.15) | collective-permute-done | bytes 524320 | tf_op jit(solution)/shard_map/ppermute | solution.py:564
  84.9 9.6 %layer_1_backward.1 = (bf16[512,512]{1,0:T(8,128)(2,1)S(1)}, bf16[512,1024]{1,0:T(8,128)(2,1)S(1)}, f32[56,128]{1,0:T(8,128)S(1)}, bf16[16,16,1536]{2,1,0:T(8,12...) custom-call(s32[4]{0:T(128)S(1)} %pad_add_fusion.1.refs_0_.place_ref, ...), custom_call_target="tpu_custom_call" | custom-call | flops 16099999744 | tf_op jit(solution)/shard_map/layer_1_backward/pallas_call | solution.py:98
  96.1 10.8 %collective-permute-done.16.refs_5_ = bf16[512,512]{1,0:T(8,128)(2,1)S(1)} collective-permute-done((bf16[512,512]{1,0:T(8,128)(2,1)S(1)}, bf16[512,512]{1,0:T(8,128)(2,1)S(1)}, u32[]{:S(2)}, u32[]{:S(2)}) %collective-permute-start.16) | collective-permute-done | bytes 524320 | tf_op jit(solution)/shard_map/ppermute | solution.py:564
  106.9 3.9 %layer_1_weight_grads.1 = (bf16[8,32,1536]{2,1,0:T(8,128)(2,1)S(1)}, bf16[8,32,1536]{2,1,0:T(8,128)(2,1)S(1)}) custom-call(s32[4]{0:T(128)S(1)} %pad_add_fusion.1.refs_0_.place_ref, bf16[512,512]{1,0:T(8,128)(2,1)S(1)} %get-tuple-element.144.refs_11_.refs_1_, bf16[512,512]{1,0:T(8,128)(2,1)S(1)} %bitcast.31, ...), custom_call_target="tpu_custom_call" | custom-call | flops 8049999872 | tf_op jit(solution)/shard_map/layer_1_weight_grads/pallas_call | solution.py:98
  115.1 10.7 %layer_0_backward.1 = (bf16[512,512]{1,0:T(8,128)(2,1)S(1)}, bf16[512,1024]{1,0:T(8,128)(2,1)S(1)}, f32[56,128]{1,0:T(8,128)S(1)}, bf16[16,16,1536]{2,1,0:T(8,12...) custom-call(s32[4]{0:T(128)S(1)} %pad_add_fusion.1.refs_0_.place_ref, f32[512,512]{1,0:T(8,128)S(1)} %copy-done.11, ...), custom_call_target="tpu_custom_call" | custom-call | flops 16099999744 | tf_op jit(solution)/shard_map/layer_0_backward/pallas_call | solution.py:98
  127.6 6.0 %collective-permute-done.21 = bf16[8,16,1536]{2,1,0:T(8,128)(2,1)S(1)} collective-permute-done((bf16[8,16,1536]{2,1,0:T(8,128)(2,1)S(1)}, bf16[8,16,1536]{2,1,0:T(8,128)(2,1)S(1)}, u32[]{:S(2)}, u32[]{:S(2)}) %collective-permute-start.21) | collective-permute-done | bytes 393248 | tf_op jit(solution)/shard_map/ppermute | solution.py:564
  135.3 3.8 %layer_0_weight_grads.1 = (bf16[8,32,1536]{2,1,0:T(8,128)(2,1)S(1)}, bf16[8,32,1536]{2,1,0:T(8,128)(2,1)S(1)}) custom-call(s32[4]{0:T(128)S(1)} %pad_add_fusion.1.refs_0_.place_ref, bf16[512,512]{1,0:T(8,128)(2,1)S(1)} %get-tuple-element.137.refs_11_.refs_1_, bf16[512,512]{1,0:T(8,128)(2,1)S(1)} %get-tuple-element.174.refs_2_, ...), custom_call_target="tpu_custom_call" | custom-call | flops 8049999872 | tf_op jit(solution)/shard_map/layer_0_weight_grads/pallas_call | solution.py:98
  142.4 2.6 %collective-permute-start.27 = (bf16[1,32,1536]{2,1,0:T(8,128)(2,1)S(1)}, bf16[1,32,1536]{2,1,0:T(8,128)(2,1)S(1)}, u32[]{:S(2)}, u32[]{:S(2)}) collective-permute-start(bf16[1,32,1536]{2,1,0:T(8,128)(2,1)S(1)} %add_convert_fusion.25), channel_id=1, source_target_pairs={{0,16},{1,17},{2,18},{3,19},{4,20},{5,21},{6,22},{7,23},{8,24},{9,... | collective-permute-start | bytes 294920 | tf_op jit(solution)/shard_map/ppermute | solution.py:564
  148.6 4.3 %collective-permute-done.29 = bf16[4,32,1536]{2,1,0:T(8,128)(2,1)S(1)} collective-permute-done((bf16[4,32,1536]{2,1,0:T(8,128)(2,1)S(1)}, bf16[4,32,1536]{2,1,0:T(8,128)(2,1)S(1)}, u32[]{:S(2)}, u32[]{:S(2)}) %collective-permute-start.29) | collective-permute-done | bytes 393248 | tf_op jit(solution)/shard_map/ppermute | solution.py:564
  154.7 2.6 %collective-permute-start.32 = (bf16[1,32,1536]{2,1,0:T(8,128)(2,1)S(1)}, bf16[1,32,1536]{2,1,0:T(8,128)(2,1)S(1)}, u32[]{:S(2)}, u32[]{:S(2)}) collective-permute-start(bf16[1,32,1536]{2,1,0:T(8,128)(2,1)S(1)} %get-tuple-element.261), channel_id=1, source_target_pairs={{0,16},{1,17},{2,18},{3,19},{4,20},{5,21},{6,22},{7,23},{8,24},{9,... | collective-permute-start | bytes 294920 | tf_op jit(solution)/shard_map/ppermute | solution.py:564
  163.5 2.5 %collective-permute-start.37 = (bf16[2,32,1536]{2,1,0:T(8,128)(2,1)S(1)}, bf16[2,32,1536]{2,1,0:T(8,128)(2,1)S(1)}, u32[]{:S(2)}, u32[]{:S(2)}) collective-permute-start(bf16[2,32,1536]{2,1,0:T(8,128)(2,1)S(1)} %pad_maximum_fusion.9), channel_id=1, source_target_pairs={{0,8},{1,9},{2,10},{3,11},{4,12},{5,13},{6,14},{7,15},{8,0},{9,1},... | collective-permute-start | bytes 589832 | tf_op jit(solution)/shard_map/ppermute | solution.py:564
  170.2 3.3 %collective-permute-done.37 = bf16[2,32,1536]{2,1,0:T(8,128)(2,1)S(1)} collective-permute-done((bf16[2,32,1536]{2,1,0:T(8,128)(2,1)S(1)}, bf16[2,32,1536]{2,1,0:T(8,128)(2,1)S(1)}, u32[]{:S(2)}, u32[]{:S(2)}) %collective-permute-start.37) | collective-permute-done | bytes 196640 | tf_op jit(solution)/shard_map/ppermute | solution.py:564
  176.1 2.8 %collective-permute-start.46 = (f32[56,128]{1,0:T(8,128)S(1)}, f32[56,128]{1,0:T(8,128)S(1)}, u32[]{:S(2)}, u32[]{:S(2)}) collective-permute-start(f32[56,128]{1,0:T(8,128)S(1)} %add.156), channel_id=1, source_target_pairs={{0,16},{1,17},{2,18},{3,19},{4,20},{5,21},{6,22},{7,23},{8,24},{9,... | collective-permute-start | bytes 86024 | tf_op jit(solution)/shard_map/ppermute | solution.py:564
  181.7 3.0 %collective-permute-done.45 = bf16[2,32,1536]{2,1,0:T(8,128)(2,1)S(1)} collective-permute-done((bf16[2,32,1536]{2,1,0:T(8,128)(2,1)S(1)}, bf16[2,32,1536]{2,1,0:T(8,128)(2,1)S(1)}, u32[]{:S(2)}, u32[]{:S(2)}) %collective-permute-start.45) | collective-permute-done | bytes 196640 | tf_op jit(solution)/shard_map/ppermute | solution.py:564
  187.5 5.8 %collective-permute-done.47 = bf16[4,32,1536]{2,1,0:T(8,128)(2,1)S(1)} collective-permute-done((bf16[4,32,1536]{2,1,0:T(8,128)(2,1)S(1)}, bf16[4,32,1536]{2,1,0:T(8,128)(2,1)S(1)}, u32[]{:S(2)}, u32[]{:S(2)}) %collective-permute-start.47) | collective-permute-done | bytes 393248 | tf_op jit(solution)/shard_map/ppermute | solution.py:564
  (211 shorter events, 71.8 us)
Async XLA Ops:
  3.7 21.8 %collective-permute-start.5 = (bf16[6,128,512]{2,1,0:T(8,128)(2,1)S(1)}, bf16[6,128,512]{2,1,0:T(8,128)(2,1)S(1)}, u32[]{:S(2)}, u32[]{:S(2)}) collective-permute-start(bf16[6,128,512]{2,1,0:T(8,128)(2,1)S(1)} %pad_maximum_fusion), channel_id=1, source_target_pairs={{0,1},{1,0},{2,3},{3,2},{4,5},{5,4},{6,7},{7,6},{8,9},{9,8},{10,11... | collective-permute-start | bytes 2359304 | tf_op jit(solution)/shard_map/ppermute | solution.py:564
  33.8 12.6 %collective-permute-start.6 = (bf16[256,1536]{1,0:T(8,128)(2,1)}, bf16[256,1536]{1,0:T(8,128)(2,1)}, u32[]{:S(2)}, u32[]{:S(2)}) collective-permute-start(bf16[256,1536]{1,0:T(8,128)(2,1)} %constant_dynamic-update-slice_fusion.refs_7_), channel_id=1, source_target_pairs={{0,2},{1,3},{2,0},{3,1},{4,6},{5,7},{6,4},{7,5},{8,10},{9,11},{10,... | collective-permute-start | bytes 2359304 | tf_op jit(solution)/shard_map/ppermute | solution.py:564
  35.4 11.0 %collective-permute-start.8 = (bf16[6,128,512]{2,1,0:T(8,128)(2,1)S(1)}, bf16[6,128,512]{2,1,0:T(8,128)(2,1)}, u32[]{:S(2)}, u32[]{:S(2)}) collective-permute-start(bf16[6,128,512]{2,1,0:T(8,128)(2,1)S(1)} %constant_dynamic-update-slice_fusion.5.refs_12_), channel_id=1, source_target_pairs={{0,2},{1,3},{2,0},{3,1},{4,6},{5,7},{6,4},{7,5},{8,10},{9,11},{10,... | collective-permute-start | bytes 2359304 | tf_op jit(solution)/shard_map/ppermute | solution.py:564
  44.8 13.5 %collective-permute-start.11 = (bf16[128,1536]{1,0:T(8,128)(2,1)S(1)}, bf16[128,1536]{1,0:T(8,128)(2,1)S(1)}, u32[]{:S(2)}, u32[]{:S(2)}) collective-permute-start(bf16[128,1536]{1,0:T(8,128)(2,1)S(1)} %pad_maximum_fusion.4), channel_id=1, source_target_pairs={{0,1},{1,0},{2,3},{3,2},{4,5},{5,4},{6,7},{7,6},{8,9},{9,8},{10,11... | collective-permute-start | bytes 1179656 | tf_op jit(solution)/shard_map/ppermute | solution.py:564
  58.4 13.8 %collective-permute-start.12 = (bf16[256,1536]{1,0:T(8,128)(2,1)S(1)}, bf16[256,1536]{1,0:T(8,128)(2,1)S(1)}, u32[]{:S(2)}, u32[]{:S(2)}) collective-permute-start(bf16[256,1536]{1,0:T(8,128)(2,1)S(1)} %constant_dynamic-update-slice_fusion.7.refs_6_), channel_id=1, source_target_pairs={{0,2},{1,3},{2,0},{3,1},{4,6},{5,7},{6,4},{7,5},{8,10},{9,11},{10,... | collective-permute-start | bytes 2359304 | tf_op jit(solution)/shard_map/ppermute | solution.py:564
  58.4 11.5 %collective-permute-start.13 = (bf16[3,128,512]{2,1,0:T(8,128)(2,1)S(1)}, bf16[3,128,512]{2,1,0:T(8,128)(2,1)S(1)}, u32[]{:S(2)}, u32[]{:S(2)}) collective-permute-start(bf16[3,128,512]{2,1,0:T(8,128)(2,1)S(1)} %copy-done.16), channel_id=1, source_target_pairs={{0,4},{1,5},{2,6},{3,7},{4,0},{5,1},{6,2},{7,3},{8,12},{9,13},{10,... | collective-permute-start | bytes 1179656 | tf_op jit(solution)/shard_map/ppermute | solution.py:564
  70.0 14.9 %collective-permute-start.14 = (bf16[6,128,512]{2,1,0:T(8,128)(2,1)S(1)}, bf16[6,128,512]{2,1,0:T(8,128)(2,1)S(1)}, u32[]{:S(2)}, u32[]{:S(2)}) collective-permute-start(bf16[6,128,512]{2,1,0:T(8,128)(2,1)S(1)} %constant_dynamic-update-slice_fusion.9.refs_15_), channel_id=1, source_target_pairs={{0,2},{1,3},{2,0},{3,1},{4,6},{5,7},{6,4},{7,5},{8,10},{9,11},{10,... | collective-permute-start | bytes 2359304 | tf_op jit(solution)/shard_map/ppermute | solution.py:564
  70.1 14.8 %collective-permute-start.15 = (bf16[512,512]{1,0:T(8,128)(2,1)S(1)}, bf16[512,512]{1,0:T(8,128)(2,1)S(1)}, u32[]{:S(2)}, u32[]{:S(2)}) collective-permute-start(bf16[512,512]{1,0:T(8,128)(2,1)S(1)} %bitcast.29), channel_id=1, source_target_pairs={{0,1},{1,0},{2,3},{3,2},{4,5},{5,4},{6,7},{7,6},{8,9},{9,8},{10,11... | collective-permute-start | bytes 1572872 | tf_op jit(solution)/shard_map/ppermute | solution.py:564
  70.8 25.4 %collective-permute-start.17 = (bf16[512,512]{1,0:T(8,128)(2,1)S(1)}, bf16[512,512]{1,0:T(8,128)(2,1)S(1)}, u32[]{:S(2)}, u32[]{:S(2)}) collective-permute-start(bf16[512,512]{1,0:T(8,128)(2,1)S(1)} %get-tuple-element.137.refs_11_.refs_1_), channel_id=1, source_target_pairs={{0,1},{1,0},{2,3},{3,2},{4,5},{5,4},{6,7},{7,6},{8,9},{9,8},{10,11... | collective-permute-start | bytes 1572872 | tf_op jit(solution)/shard_map/ppermute | solution.py:564
  77.2 29.7 %collective-permute-start.16 = (bf16[512,512]{1,0:T(8,128)(2,1)S(1)}, bf16[512,512]{1,0:T(8,128)(2,1)S(1)}, u32[]{:S(2)}, u32[]{:S(2)}) collective-permute-start(bf16[512,512]{1,0:T(8,128)(2,1)S(1)} %get-tuple-element.144.refs_11_.refs_1_), channel_id=1, source_target_pairs={{0,1},{1,0},{2,3},{3,2},{4,5},{5,4},{6,7},{7,6},{8,9},{9,8},{10,11... | collective-permute-start | bytes 1572872 | tf_op jit(solution)/shard_map/ppermute | solution.py:564
  94.5 17.1 %collective-permute-start.19 = (bf16[16,16,1536]{2,1,0:T(8,128)(2,1)S(1)}, bf16[16,16,1536]{2,1,0:T(8,128)(2,1)S(1)}, u32[]{:S(2)}, u32[]{:S(2)}) collective-permute-start(bf16[16,16,1536]{2,1,0:T(8,128)(2,1)S(1)} %get-tuple-element.166), channel_id=1, source_target_pairs={{0,2},{1,3},{2,0},{3,1},{4,6},{5,7},{6,4},{7,5},{8,10},{9,11},{10,... | collective-permute-start | bytes 2359304 | tf_op jit(solution)/shard_map/ppermute | solution.py:564
  110.9 24.4 %collective-permute-start.25 = (bf16[512,512]{1,0:T(8,128)(2,1)S(1)}, bf16[512,512]{1,0:T(8,128)(2,1)S(1)}, u32[]{:S(2)}, u32[]{:S(2)}) collective-permute-start(bf16[512,512]{1,0:T(8,128)(2,1)S(1)} %get-tuple-element.174.refs_2_), channel_id=1, source_target_pairs={{0,1},{1,0},{2,3},{3,2},{4,5},{5,4},{6,7},{7,6},{8,9},{9,8},{10,11... | collective-permute-start | bytes 1572872 | tf_op jit(solution)/shard_map/ppermute | solution.py:564
  111.8 21.8 %collective-permute-start.21 = (bf16[8,16,1536]{2,1,0:T(8,128)(2,1)S(1)}, bf16[8,16,1536]{2,1,0:T(8,128)(2,1)S(1)}, u32[]{:S(2)}, u32[]{:S(2)}) collective-permute-start(bf16[8,16,1536]{2,1,0:T(8,128)(2,1)S(1)} %get-tuple-element.269), channel_id=1, source_target_pairs={{0,1},{1,0},{2,3},{3,2},{4,5},{5,4},{6,7},{7,6},{8,9},{9,8},{10,11... | collective-permute-start | bytes 1179656 | tf_op jit(solution)/shard_map/ppermute | solution.py:564
  113.5 12.3 %collective-permute-start.22 = (bf16[4,32,1536]{2,1,0:T(8,128)(2,1)S(1)}, bf16[4,32,1536]{2,1,0:T(8,128)(2,1)S(1)}, u32[]{:S(2)}, u32[]{:S(2)}) collective-permute-start(bf16[4,32,1536]{2,1,0:T(8,128)(2,1)S(1)} %get-tuple-element.267.refs_18_), channel_id=1, source_target_pairs={{0,4},{1,5},{2,6},{3,7},{4,0},{5,1},{6,2},{7,3},{8,12},{9,13},{10,... | collective-permute-start | bytes 1179656 | tf_op jit(solution)/shard_map/ppermute | solution.py:564
  125.8 14.6 %collective-permute-start.20 = (bf16[16,16,1536]{2,1,0:T(8,128)(2,1)S(1)}, bf16[16,16,1536]{2,1,0:T(8,128)(2,1)S(1)}, u32[]{:S(2)}, u32[]{:S(2)}) collective-permute-start(bf16[16,16,1536]{2,1,0:T(8,128)(2,1)S(1)} %get-tuple-element.171), channel_id=1, source_target_pairs={{0,2},{1,3},{2,0},{3,1},{4,6},{5,7},{6,4},{7,5},{8,10},{9,11},{10,... | collective-permute-start | bytes 2359304 | tf_op jit(solution)/shard_map/ppermute | solution.py:564
  126.0 13.3 %collective-permute-start.24 = (bf16[2,32,1536]{2,1,0:T(8,128)(2,1)S(1)}, bf16[2,32,1536]{2,1,0:T(8,128)(2,1)S(1)}, u32[]{:S(2)}, u32[]{:S(2)}) collective-permute-start(bf16[2,32,1536]{2,1,0:T(8,128)(2,1)S(1)} %get-tuple-element.275), channel_id=1, source_target_pairs={{0,8},{1,9},{2,10},{3,11},{4,12},{5,13},{6,14},{7,15},{8,0},{9,1},... | collective-permute-start | bytes 589832 | tf_op jit(solution)/shard_map/ppermute | solution.py:564
  141.7 11.2 %collective-permute-start.29 = (bf16[4,32,1536]{2,1,0:T(8,128)(2,1)S(1)}, bf16[4,32,1536]{2,1,0:T(8,128)(2,1)S(1)}, u32[]{:S(2)}, u32[]{:S(2)}) collective-permute-start(bf16[4,32,1536]{2,1,0:T(8,128)(2,1)S(1)} %get-tuple-element.262), channel_id=1, source_target_pairs={{0,4},{1,5},{2,6},{3,7},{4,0},{5,1},{6,2},{7,3},{8,12},{9,13},{10,... | collective-permute-start | bytes 1179656 | tf_op jit(solution)/shard_map/ppermute | solution.py:564
  142.4 12.3 %collective-permute-start.27 = (bf16[1,32,1536]{2,1,0:T(8,128)(2,1)S(1)}, bf16[1,32,1536]{2,1,0:T(8,128)(2,1)S(1)}, u32[]{:S(2)}, u32[]{:S(2)}) collective-permute-start(bf16[1,32,1536]{2,1,0:T(8,128)(2,1)S(1)} %add_convert_fusion.25), channel_id=1, source_target_pairs={{0,16},{1,17},{2,18},{3,19},{4,20},{5,21},{6,22},{7,23},{8,24},{9,... | collective-permute-start | bytes 294920 | tf_op jit(solution)/shard_map/ppermute | solution.py:564
  145.0 14.4 %collective-permute-start.35 = (bf16[2,16,1536]{2,1,0:T(8,128)(2,1)S(1)}, bf16[2,16,1536]{2,1,0:T(8,128)(2,1)S(1)}, u32[]{:S(2)}, u32[]{:S(2)}) collective-permute-start(bf16[2,16,1536]{2,1,0:T(8,128)(2,1)S(1)} %get-tuple-element.282), channel_id=1, source_target_pairs={{0,8},{1,9},{2,10},{3,11},{4,12},{5,13},{6,14},{7,15},{8,0},{9,1},... | collective-permute-start | bytes 294920 | tf_op jit(solution)/shard_map/ppermute | solution.py:564
  146.5 11.3 %collective-permute-start.26 = (bf16[8,16,1536]{2,1,0:T(8,128)(2,1)S(1)}, bf16[8,16,1536]{2,1,0:T(8,128)(2,1)S(1)}, u32[]{:S(2)}, u32[]{:S(2)}) collective-permute-start(bf16[8,16,1536]{2,1,0:T(8,128)(2,1)S(1)} %get-tuple-element.264), channel_id=1, source_target_pairs={{0,1},{1,0},{2,3},{3,2},{4,5},{5,4},{6,7},{7,6},{8,9},{9,8},{10,11... | collective-permute-start | bytes 1179656 | tf_op jit(solution)/shard_map/ppermute | solution.py:564
  147.1 12.7 %collective-permute-start.34 = (f32[56,128]{1,0:T(8,128)S(1)}, f32[56,128]{1,0:T(8,128)S(1)}, u32[]{:S(2)}, u32[]{:S(2)}) collective-permute-start(f32[56,128]{1,0:T(8,128)S(1)} %add.137), channel_id=1, source_target_pairs={{0,1},{1,0},{2,3},{3,2},{4,5},{5,4},{6,7},{7,6},{8,9},{9,8},{10,11... | collective-permute-start | bytes 86024 | tf_op jit(solution)/shard_map/ppermute | solution.py:564
  163.5 10.0 %collective-permute-start.37 = (bf16[2,32,1536]{2,1,0:T(8,128)(2,1)S(1)}, bf16[2,32,1536]{2,1,0:T(8,128)(2,1)S(1)}, u32[]{:S(2)}, u32[]{:S(2)}) collective-permute-start(bf16[2,32,1536]{2,1,0:T(8,128)(2,1)S(1)} %pad_maximum_fusion.9), channel_id=1, source_target_pairs={{0,8},{1,9},{2,10},{3,11},{4,12},{5,13},{6,14},{7,15},{8,0},{9,1},... | collective-permute-start | bytes 589832 | tf_op jit(solution)/shard_map/ppermute | solution.py:564
  166.1 9.7 %collective-permute-start.36 = (bf16[2,16,1536]{2,1,0:T(8,128)(2,1)S(1)}, bf16[2,16,1536]{2,1,0:T(8,128)(2,1)S(1)}, u32[]{:S(2)}, u32[]{:S(2)}) collective-permute-start(bf16[2,16,1536]{2,1,0:T(8,128)(2,1)S(1)} %get-tuple-element.281), channel_id=1, source_target_pairs={{0,8},{1,9},{2,10},{3,11},{4,12},{5,13},{6,14},{7,15},{8,0},{9,1},... | collective-permute-start | bytes 294920 | tf_op jit(solution)/shard_map/ppermute | solution.py:564
  168.9 10.0 %collective-permute-start.43 = (bf16[1,32,1536]{2,1,0:T(8,128)(2,1)S(1)}, bf16[1,32,1536]{2,1,0:T(8,128)(2,1)S(1)}, u32[]{:S(2)}, u32[]{:S(2)}) collective-permute-start(bf16[1,32,1536]{2,1,0:T(8,128)(2,1)S(1)} %add_convert_fusion.16), channel_id=1, source_target_pairs={{0,16},{1,17},{2,18},{3,19},{4,20},{5,21},{6,22},{7,23},{8,24},{9,... | collective-permute-start | bytes 294920 | tf_op jit(solution)/shard_map/ppermute | solution.py:564
  (53 other events, 436.6 us)

commit v5 on v4

--- a/solution.py
+++ b/solution.py
@@ -207,7 +207,6 @@
     rows = series * slots
     for part in chunks(rows, 256):
         r.qkv[part, :] = dot_nn(a_ref[part, :], r.attn_w[:, : 3 * inner]).astype(bf16)
-    r.write("qkv")
     is_low = lane_low(slots)
     low, high = lane_halves()
     for s in range(series):
@@ -221,7 +220,6 @@
             scores = jnp.where(keep, scores, masked_score)
             exps = jnp.exp(scores - jnp.max(scores, axis=0, keepdims=True))
             r.probs[here, at] = exps / jnp.sum(exps, axis=0, keepdims=True)
-    r.write("probs")
     for s in range(series):
         here = slice(s * slots, (s + 1) * slots)
         for start in range(0, inner, 128):
@@ -229,16 +227,11 @@
             values = r.qkv[here, 2 * inner + start : 2 * inner + start + 128]
             both = dot_tn(r.probs[here, at].astype(bf16), values)
             r.heads[here, at] = own_blocks(both, is_low)
-    r.write("heads")
     gain = r.gain_ff[layer_idx : layer_idx + 1, :]
     for part in chunks(rows, 256):
         middle = x_ref[part, :] + dot_nt(r.heads[part, :], r.attn_w[:, 3 * inner :])
         r.middle[part, :] = middle
         r.ff_in[part, :] = (middle * inverse_rms(middle) * gain).astype(bf16)
-    r.write("middle", "ff_in")
-
-
-attn_out_names = ("qkv", "probs", "heads", "middle", "ff_in")
 
 
 def prepare_body(r):
@@ -257,18 +250,21 @@
     r.drain("x", "a", "bias", "mask")
 
 
-def first_body(r, sizes, masks, grain):
-    r.fetch("a")
+def attention_body(r, sizes, masks, grain, layer_idx):
     start_all(attention_copies(r, masks, grain))
-    r.fetch("bias", "mask", "x", "gain_ff", "gain_attn")
+    r.fetch("gain_ff")
+    r.need("gain_ff")
+    wait_all(r.attn_sem, r.attn_w)
+    attention_forward(r, r.x, r.a, sizes, layer_idx)
+
+
+def ff_body(r):
     start_all(ff_copies(r, 0))
-    r.need("a")
-    wait_all(r.attn_sem, r.attn_w)
-    r.need("bias", "mask", "x", "gain_ff", "gain_attn")
-    attention_forward(r, r.x, r.a, sizes, 0)
+    r.fetch("gain_attn")
+    r.need("gain_attn")
     wait_all(r.ff_sem, r.ff_gate_up, r.ff_down)
-    width = r.x.shape[1]
-    for part in chunks(r.x.shape[0], 256):
+    width = r.middle.shape[1]
+    for part in chunks(r.middle.shape[0], 256):
         x_next = r.middle[part, :]
         for half in range(2):
             both = dot_nn(r.ff_in[part, :], r.ff_gate_up[half])
@@ -276,41 +272,17 @@
             x_next = x_next + dot_nn(hidden, r.ff_down[half])
         r.x_next[part, :] = x_next
         r.a_next[part, :] = (x_next * inverse_rms(x_next) * r.gain_attn[1:2, :]).astype(bf16)
-    r.write("x_next", "a_next")
-    r.drain(*attn_out_names, "x_next", "a_next")
-
-
-def second_body(r, sizes, masks, grain):
-    r.fetch("a")
-    start_all(attention_copies(r, masks, grain))
-    r.fetch("bias", "mask", "x", "gain_ff")
-    r.need("a")
-    wait_all(r.attn_sem, r.attn_w)
-    r.need("bias", "mask", "x", "gain_ff")
-    attention_forward(r, r.x, r.a, sizes, 1)
-    r.drain(*attn_out_names)
-
-
-def backward_body(r, sizes, layer_idx, last, piece_masks, heads):
-    series, slots, inner = sizes
-    rows = series * slots
-    width = r.x.shape[1]
-    r.fetch("grad", "ff_in", "gain_ff", "gain_attn")
+
+
+def ff_backward(r, layer_idx, last):
+    rows, width = r.middle.shape
+    r.fetch("grad", "gain_ff")
     if last:
         start_all(ff_copies(r, layer_idx))
-    r.fetch("middle")
-    r.fetch("qkv", "probs", "heads", "a", "x")
-    if not last:
-        r.fetch("bias_before", "marks", "buckets", "small_before")
-    r.need("grad", "ff_in", "gain_ff", "gain_attn")
-    if not last:
-        r.need("small_before")
-        r.small[...] = r.small_before[...]
+    r.need("grad", "gain_ff")
     if last:
         wait_all(r.ff_sem, r.ff_gate_up, r.ff_down)
-    r.need("middle")
     gain_ff = r.gain_ff[layer_idx : layer_idx + 1, :]
-    gain_attn = r.gain_attn[layer_idx : layer_idx + 1, :]
     gain_total = jnp.zeros((1, width), f32)
     for part in chunks(rows, 256):
         grad = r.grad[part, :].astype(f32)
@@ -347,16 +319,19 @@
         r.grad_mid[part, :] = grad_mid
         r.branch[part, :] = grad_mid.astype(bf16)
     if last:
-        r.small[...] = jnp.zeros(r.small.shape, f32)
-    put_row(r.small, 2 + layer_idx, gain_total)
-    r.write("hidden", "grad_gate_up")
-    if last:
         r.write("outputs")
+    return gain_total
+
+
+def attention_backward(r, sizes, layer_idx, last, piece_masks, heads):
+    series, slots, inner = sizes
+    rows = series * slots
+    width = r.x.shape[1]
+    r.fetch("gain_attn")
+    if not last:
+        r.fetch("marks", "buckets")
     for part in chunks(rows, 256):
         r.grad_heads[part, :] = dot_nn(r.branch[part, :], r.attn_w[:, 3 * inner :]).astype(bf16)
-    r.need("qkv", "probs", "heads", "a", "x")
-    if not last:
-        r.need("bias_before", "marks", "buckets")
     is_low = lane_low(slots)
     low, high = lane_halves()
     for start in range(0, inner, 128):
@@ -389,7 +364,10 @@
     r.attn_grad[:, : 3 * inner] = dot_tn(r.a[...], r.grad_qkv[...])
     r.attn_grad[:, 3 * inner :] = dot_tn(r.branch[...], r.heads[...])
     scatter_pieces(r.attn_grad, r.attn_keep, r.attn_send, piece_masks, r.place[2])
-    r.write("attn_send", "attn_keep")
+    r.need("gain_attn")
+    if not last:
+        r.need("marks", "buckets")
+    gain_attn = r.gain_attn[layer_idx : layer_idx + 1, :]
     gain_total = jnp.zeros((1, width), f32)
     embed_total = jnp.zeros((1, width), f32)
     for part in chunks(rows, 256):
@@ -404,11 +382,8 @@
             seen = r.marks[part, 0:1] == 1
             r.grad_next[part, :] = jnp.where(seen, grad_in, 0.0)
             embed_total += jnp.sum(jnp.where(seen, 0.0, grad_in), axis=0, keepdims=True)
-    put_row(r.small, layer_idx, gain_total)
     r.write("grad_next")
-    if last:
-        r.write("grad_next_low", "bias_acc", "small")
-    else:
+    if not last:
         put_row(r.small, 4, embed_total)
         head_size = inner // heads
         for idx in range(r.table_rows.shape[0]):
@@ -420,10 +395,25 @@
             cut = r.table_rows[:, head * head_size : (head + 1) * head_size]
             table = jnp.where(lane == head, jnp.sum(cut, axis=1, keepdims=True), table)
         r.small[small_rows(width) :, :] = table
-        r.write("small")
-    r.drain("hidden", "grad_gate_up", "attn_send", "attn_keep", "grad_next", "small")
-    if last:
-        r.drain("outputs", "grad_next_low", "bias_acc")
+    r.drain("grad_next")
+    return gain_total
+
+
+def last_backward_body(r, sizes, piece_masks, heads):
+    r.small[...] = jnp.zeros(r.small.shape, f32)
+    put_row(r.small, 3, ff_backward(r, 1, True))
+    put_row(r.small, 1, attention_backward(r, sizes, 1, True, piece_masks, heads))
+    r.drain("outputs")
+
+
+def ff_backward_body(r):
+    r.small[...] = r.small_before[...]
+    put_row(r.small, 2, ff_backward(r, 0, False))
+
+
+def attention_backward_body(r, sizes, piece_masks, heads):
+    r.small[...] = r.small_before[...]
+    put_row(r.small, 0, attention_backward(r, sizes, 0, False, piece_masks, heads))
 
 
 def small_rows(width):
@@ -591,7 +581,6 @@
         ],
         axis=0,
     )
-    ff_quarter = swap(ff_blocks, 1).reshape(3, 2, quarter, width)
 
     def prepare(token):
         table, marked, kept, near = (
@@ -626,30 +615,44 @@
     direct = own_rows % 16 == 0
     far = bits[2:]
     if direct:
-        hops_0 = far[1:][::-1] + far[:1] + [1, 2]
-        hops_1 = far[:1] + far[1:][::-1] + [1, 2]
+        hops_0 = [1] + far[2:] + far[:2] + [2]
+        hops_1 = far[2:] + far[:2] + [1, 2]
         block_0, block_1 = packed[0], packed[1]
-        for hop_0, hop_1 in zip(hops_0[:-2], hops_1[:-2]):
-            got_0, got_1 = swap(block_0, hop_0), swap(block_1, hop_1)
+        got_1 = swap(block_1, hops_1[0])
+        got_0 = swap(block_0, hops_0[0])
+        ff_quarter = swap(tie(ff_blocks, got_0), 1).reshape(3, 2, quarter, width)
+        block_0 = join(block_0, got_0)
+        block_1 = join(block_1, tie(got_1, block_0))
+        for hop_0, hop_1 in zip(hops_0[1:-2], hops_1[1:-2]):
+            got_1, got_0 = swap(block_1, hop_1), swap(block_0, hop_0)
+            if hop_1 == hops_1[1]:
+                start, wide_buckets, marks = prepare(block_1)
             block_0 = join(block_0, got_0)
             block_1 = join(block_1, tie(got_1, block_0))
-            if hop_0 == hops_0[0]:
-                start, wide_buckets, marks = prepare(block_1)
-        got_0 = swap(block_0, 1)
-        ff_0 = tie(ff_quarter[:, 0], block_0)
+        got_0 = swap(block_0, hops_0[-2])
+        got_1 = swap(block_1, hops_1[-2])
+        ff_0 = tie(ff_quarter[:, 0], block_1)
         got_ff_0 = swap(ff_0, 4)
-        block_0 = join(block_0, tie(got_0, start.a, ff_0))
-        block_1 = tie(block_1, block_0)
-        got_1 = swap(block_1, 1)
-        ff_0 = join(ff_0, tie(got_ff_0, block_0))
+        block_0 = join(block_0, tie(got_0, start.a, got_ff_0))
+        block_1 = join(block_1, tie(got_1, block_0))
+        ff_0 = join(ff_0, tie(got_ff_0, block_1))
         got_ff_1 = swap(tie(ff_quarter[:, 1], ff_0), 4)
-        attn_pieces = [(block_0, swap(block_0, 2), order_masks(hops_0[::-1]))]
-        peer_cotangent = swap(tie(cotangent, got_1), 1)
+        peer_cotangent = swap(tie(cotangent, ff_0), 1)
+        far_0 = swap(block_0, 2)
+        attn_pieces = [
+            (block_0, far_0, order_masks(hops_0[::-1])),
+            (block_1, swap(tie(block_1, far_0), 2), order_masks(hops_1[::-1])),
+        ]
+        after_first = (attn_pieces[1][1], peer_cotangent)
     else:
+        ff_quarter = swap(ff_blocks, 1).reshape(3, 2, quarter, width)
         ff_0 = join(ff_quarter[:, 0], swap(ff_quarter[:, 0], 4))
         start, wide_buckets, marks = prepare(packed)
         whole = lax.all_gather(packed[0], axes, axis=0, tiled=True)
         attn_pieces = [(whole, whole, [0])]
+        whole = lax.all_gather(packed[1], axes, axis=0, tiled=True)
+        attn_pieces.append((whole, whole, [0]))
+        after_first = ()
         peer_cotangent = swap(cotangent, 1)
     ff_pieces = [(ff_0, swap(ff_0, 2))]
 
@@ -676,126 +679,96 @@
         ff_in=Kept(matrix, bf16),
     )
 
-    pieces, masks = attn_ins(0)
-    first = run(
-        functools.partial(first_body, sizes=sizes, masks=masks, grain=grain),
-        "layer_0_forward",
-        dict(
-            place=place,
-            x=Kept(start.x),
-            a=Kept(start.a),
-            bias=Kept(start.bias),
-            mask=Kept(start.mask),
-            gain_ff=gain_ff,
-            gain_attn=gain_attn,
-            **pieces,
-            **ff_ins(0),
-        ),
-        dict(**attn_outs, **ff_outs, x_next=Kept(matrix, f32), a_next=Kept(matrix, bf16)),
-        dict(**attn_scratch, **ff_scratch),
-        micros=9,
-    )
-    peer_in_0 = swap(first.ff_in, 1)
-    if direct:
-        block_1 = join(block_1, tie(got_1, first.ff_in))
-        attn_pieces.append((block_1, swap(block_1, 2), order_masks(hops_1[::-1])))
-        ff_1 = tie(ff_quarter[:, 1], ff_0)
-        ff_1 = join(ff_1, tie(got_ff_1, first.ff_in))
-    else:
-        whole = lax.all_gather(packed[1], axes, axis=0, tiled=True)
-        attn_pieces.append((whole, whole, [0]))
-        ff_1 = join(ff_quarter[:, 1], swap(ff_quarter[:, 1], 4))
-    ff_pieces.append((ff_1, swap(ff_1, 2)))
-    pieces, masks = attn_ins(1)
-    second = run(
-        functools.partial(second_body, sizes=sizes, masks=masks, grain=grain),
-        "layer_1_attention",
-        dict(
-            place=place,
-            x=Kept(first.x_next),
-            a=Kept(first.a_next),
-            bias=Kept(start.bias),
-            mask=Kept(start.mask),
-            gain_ff=gain_ff,
-            **pieces,
-        ),
-        attn_outs,
-        attn_scratch,
-        micros=6,
-    )
-    peer_in_1 = swap(second.ff_in, 1)
-
-    attn_hops = [2, 1] + bits[2:]
-    attn_low = devices // attn_count
-    attn_split = [hop for hop in attn_hops if hop >= attn_low]
-    attn_whole = [hop for hop in attn_hops if hop < attn_low]
-    ff_hops = bits[1:]
-    ff_split = [hop for hop in ff_hops if hop // 2 < ff_count]
-    ff_whole = [hop for hop in ff_hops if hop // 2 >= ff_count]
-    attn_masks = [mask // attn_low for mask in order_masks(attn_split)]
-    ff_masks = [mask // 2 for mask in order_masks(ff_split)]
-    attn_half = (attn_count // 2, attn_grain, 4 * inner)
-    ff_half = (ff_count // 2, ff_grain, 3 * width)
-    small_shape = (small_rows(width) + bias_table.shape[0], 128)
-
-    def backward(layer_idx, kept, x, a, grad, extra_ins, extra_outs, extra_scratch, after=()):
-        last = layer_idx == 1
-        ff_given = ff_ins(1) if last else keep_all(
-            dict(ff_gate_up=kept.ff_gate_up, ff_down=kept.ff_down)
-        )
+    def attention(layer_idx, x, a, after=(), micros=5):
+        pieces, masks = attn_ins(layer_idx)
         return run(
             functools.partial(
-                backward_body,
-                sizes=sizes,
-                layer_idx=layer_idx,
-                last=last,
-                piece_masks=attn_masks,
-                heads=heads,
+                attention_body, sizes=sizes, masks=masks, grain=grain, layer_idx=layer_idx
             ),
-            "layer_%d_backward" % layer_idx,
+            "layer_%d_attention" % layer_idx,
             dict(
                 place=place,
                 x=Kept(x),
                 a=Kept(a),
-                grad=grad,
-                gain_attn=gain_attn,
+                bias=Kept(start.bias),
+                mask=Kept(start.mask),
                 gain_ff=gain_ff,
-                attn_w=Kept(kept.attn_w),
-                qkv=Kept(kept.qkv),
-                probs=Kept(kept.probs),
-                heads=Kept(kept.heads),
-                middle=Kept(kept.middle),
-                ff_in=Kept(kept.ff_in),
-                **ff_given,
-                **extra_ins,
+                **pieces,
             ),
-            dict(
-                hidden=Kept(matrix, bf16),
-                grad_gate_up=Kept((rows, 2 * width), bf16),
-                small=Kept(small_shape, f32),
-                attn_keep=Kept(attn_half, bf16),
-                attn_send=Kept(attn_half, bf16),
-                **(ff_outs if last else {}),
-                **extra_outs,
-            ),
-            dict(
-                grad_mid=pltpu.VMEM(matrix, f32),
-                branch=pltpu.VMEM(matrix, bf16),
-                grad_heads=pltpu.VMEM((rows, inner), bf16),
-                grad_qkv=pltpu.VMEM((rows, 3 * inner), bf16),
-                grad_scores=pltpu.VMEM((rows, heads * slots), bf16),
-                attn_grad=pltpu.VMEM((width, 4 * inner), f32),
-                pulled=pltpu.VMEM((256, 2 * width), bf16),
-                **(ff_scratch if last else {}),
-                **extra_scratch,
-            ),
+            attn_outs,
+            attn_scratch,
             after=after,
-            micros=14,
+            micros=micros,
         )
 
-    def weight_grads(layer_idx, kept, weights, back, grad, peer_in, peer_grad, after=()):
+    first = attention(0, start.x, start.a, micros=10)
+    peer_in_0 = swap(first.ff_in, 1)
+    first_ff = run(
+        ff_body,
+        "layer_0_ff",
+        dict(
+            place=place,
+            middle=Kept(first.middle),
+            ff_in=Kept(first.ff_in),
+            gain_attn=gain_attn,
+            **ff_ins(0),
+        ),
+        dict(**ff_outs, x_next=Kept(matrix, f32), a_next=Kept(matrix, bf16)),
+        ff_scratch,
+        after=after_first,
+        micros=0.1,
+    )
+    if direct:
+        ff_1 = join(ff_quarter[:, 1], tie(got_ff_1, first_ff.a_next))
+    else:
+        ff_1 = join(ff_quarter[:, 1], swap(ff_quarter[:, 1], 4))
+    ff_pieces.append((ff_1, swap(ff_1, 2)))
+    second = attention(1, first_ff.x_next, first_ff.a_next, micros=0.1)
+    peer_in_1 = swap(second.ff_in, 1)
+
+    attn_low = devices // attn_count
+    attn_hops = ([2, 1] + bits[2:], [2] + bits[3:] + bits[2:3] + [1])
+    attn_split = [[hop for hop in hops if hop >= attn_low] for hops in attn_hops]
+    attn_whole = [hop for hop in bits if hop < attn_low]
+    attn_masks = [[mask // attn_low for mask in order_masks(hops)] for hops in attn_split]
+    ff_hops = (bits[1:], [2] + bits[3:] + bits[2:3])
+    ff_split = [[hop for hop in hops if hop // 2 < ff_count] for hops in ff_hops]
+    ff_whole = [hop for hop in bits[1:] if hop // 2 >= ff_count]
+    ff_masks = [[mask // 2 for mask in order_masks(hops)] for hops in ff_split]
+    attn_half = (attn_count // 2, attn_grain, 4 * inner)
+    ff_half = (ff_count // 2, ff_grain, 3 * width)
+    small_shape = (small_rows(width) + bias_table.shape[0], 128)
+
+    ff_back_outs = dict(
+        hidden=Kept(matrix, bf16),
+        grad_gate_up=Kept((rows, 2 * width), bf16),
+        small=Kept(small_shape, f32),
+    )
+    attn_back_outs = dict(attn_keep=Kept(attn_half, bf16), attn_send=Kept(attn_half, bf16))
+    attn_back_scratch = dict(
+        grad_heads=pltpu.VMEM((rows, inner), bf16),
+        grad_qkv=pltpu.VMEM((rows, 3 * inner), bf16),
+        grad_scores=pltpu.VMEM((rows, heads * slots), bf16),
+        attn_grad=pltpu.VMEM((width, 4 * inner), f32),
+    )
+    mid_scratch = dict(grad_mid=pltpu.VMEM(matrix, f32), branch=pltpu.VMEM(matrix, bf16))
+    pulled_scratch = dict(pulled=pltpu.VMEM((256, 2 * width), bf16))
+    bias_shape = (slots, heads * slots)
+
+    def attn_back_ins(kept, x, a):
+        return dict(
+            x=Kept(x),
+            a=Kept(a),
+            gain_attn=gain_attn,
+            attn_w=Kept(kept.attn_w),
+            qkv=Kept(kept.qkv),
+            probs=Kept(kept.probs),
+            heads=Kept(kept.heads),
+        )
+
+    def weight_grads(layer_idx, kept, weights, back, grad, peer_in, peer_grad, after, micros):
         return run(
-            functools.partial(weight_body, piece_masks=ff_masks),
+            functools.partial(weight_body, piece_masks=ff_masks[layer_idx]),
             "layer_%d_weight_grads" % layer_idx,
             dict(
                 place=place,
@@ -815,7 +788,7 @@
                 ff_grad=pltpu.VMEM((width, 3 * width), f32),
             ),
             after=after,
-            micros=7,
+            micros=micros,
         )
 
     def add(left, right):
@@ -848,8 +821,8 @@
                 out["token"] = got
         out["near"], out["far"] = piece, got
 
-    def attn_chain(part, out):
-        yield from halving(part.attn_keep, part.attn_send, attn_split, out)
+    def attn_chain(part, split, out):
+        yield from halving(part.attn_keep, part.attn_send, split, out)
         yield from summing(out["piece"], attn_whole, out)
         piece = out["piece"][0]
         if own_rows < attn_grain:
@@ -857,10 +830,10 @@
             piece = lax.dynamic_slice_in_dim(piece, first_row, own_rows, axis=0)
         out["done"] = piece.astype(f32)
 
-    def ff_chain(part, out):
-        yield from halving(part.ff_keep, part.ff_send, ff_split, out)
+    def ff_chain(part, split, out):
+        yield from halving(part.ff_keep, part.ff_send, split, out)
         yield from summing(out["piece"], ff_whole, out)
-        yield from sharing(out["piece"], ff_split[::-1], out)
+        yield from sharing(out["piece"], split[::-1], out)
         out["done"] = True
 
     class Chain:
@@ -880,102 +853,133 @@
                 return self.out["token"]
             return token
 
-    back_1 = backward(
-        1,
-        second,
-        first.x_next,
-        first.a_next,
-        cotangent,
-        {},
+    back_1 = run(
+        functools.partial(
+            last_backward_body, sizes=sizes, piece_masks=attn_masks[1], heads=heads
+        ),
+        "layer_1_backward",
         dict(
+            place=place,
+            grad=cotangent,
+            gain_ff=gain_ff,
+            middle=Kept(second.middle),
+            ff_in=Kept(second.ff_in),
+            **ff_ins(1),
+            **attn_back_ins(second, first_ff.x_next, first_ff.a_next),
+        ),
+        dict(
+            **ff_outs,
+            **ff_back_outs,
+            **attn_back_outs,
             outputs=(matrix, bf16),
             grad_next=Kept(matrix, f32),
             grad_next_low=Kept(matrix, bf16),
-            bias_acc=Kept((slots, heads * slots), f32),
+            bias_acc=Kept(bias_shape, f32),
         ),
-        {},
-        after=(peer_cotangent,),
+        dict(**mid_scratch, **pulled_scratch, **attn_back_scratch, **ff_scratch),
+        micros=10,
     )
     peer_grad_0 = swap(back_1.grad_next_low, 1)
+    attn_1 = Chain(attn_chain, back_1, attn_split[1])
+    back_0 = run(
+        ff_backward_body,
+        "layer_0_ff_backward",
+        dict(
+            grad=Kept(back_1.grad_next),
+            gain_ff=gain_ff,
+            small_before=Kept(back_1.small),
+            middle=Kept(first.middle),
+            ff_in=Kept(first.ff_in),
+            ff_gate_up=Kept(first_ff.ff_gate_up),
+            ff_down=Kept(first_ff.ff_down),
+        ),
+        dict(**ff_back_outs, grad_mid=Kept(matrix, f32), branch=Kept(matrix, bf16)),
+        pulled_scratch,
+        after=(peer_in_0, peer_in_1),
+        micros=10,
+    )
+    token = attn_1.step(back_0.branch)
     part_1 = weight_grads(
-        1, second, back_1, back_1, cotangent, peer_in_1, peer_cotangent, after=(peer_in_0,)
-    )
-    attn_1 = Chain(attn_chain, back_1)
-    ff_1 = Chain(ff_chain, part_1)
-    token = attn_1.step(part_1.ff_send)
-    token = ff_1.step(token)
-    back_0 = backward(
-        0,
-        first,
-        start.x,
-        start.a,
-        Kept(back_1.grad_next),
-        dict(
-            bias_before=Kept(back_1.bias_acc),
-            marks=marks,
-            buckets=wide_buckets,
-            small_before=Kept(back_1.small),
-        ),
-        dict(grad_next=(matrix, f32)),
-        dict(
-            bias_acc=pltpu.VMEM((slots, heads * slots), f32),
-            table_rows=pltpu.VMEM((bias_table.shape[0], heads * slots), f32),
-        ),
-        after=(token,),
-    )
-    attn_0 = Chain(attn_chain, back_0)
-    token = ff_1.step(back_0.attn_send)
-    token = attn_1.step(token)
+        1, second, back_1, back_1, cotangent, peer_in_1, peer_cotangent, (token,), 0.1
+    )
+    ff_1 = Chain(ff_chain, part_1, ff_split[1])
     part_0 = weight_grads(
         0,
         first,
-        first,
+        first_ff,
         back_0,
         Kept(back_1.grad_next_low),
         peer_in_0,
         peer_grad_0,
+        (part_1.ff_send,),
+        4,
+    )
+    ff_0 = Chain(ff_chain, part_0, ff_split[0])
+    token = ff_1.step(part_0.ff_send)
+    token = attn_1.step(token)
+    token = ff_0.step(token)
+    back_attn_0 = run(
+        functools.partial(
+            attention_backward_body, sizes=sizes, piece_masks=attn_masks[0], heads=heads
+        ),
+        "layer_0_attention_backward",
+        dict(
+            place=place,
+            bias_before=Kept(back_1.bias_acc),
+            marks=marks,
+            buckets=wide_buckets,
+            small_before=Kept(back_0.small),
+            grad_mid=Kept(back_0.grad_mid),
+            branch=Kept(back_0.branch),
+            **attn_back_ins(first, start.x, start.a),
+        ),
+        dict(**attn_back_outs, small=Kept(small_shape, f32), grad_next=(matrix, f32)),
+        dict(
+            bias_acc=pltpu.VMEM(bias_shape, f32),
+            table_rows=pltpu.VMEM((bias_table.shape[0], heads * slots), f32),
+            **attn_back_scratch,
+        ),
         after=(token,),
-    )
-    ff_0 = Chain(ff_chain, part_0)
-    small = Chain(summing, back_0.small, attn_hops)
-    token = attn_1.step(ff_1.step(part_0.ff_send))
-    token = ff_0.step(attn_0.step(token))
-    token = small.step(token)
-    done_1 = None
+        micros=7,
+    )
+    attn_0 = Chain(attn_chain, back_attn_0, attn_split[0])
+    small = Chain(summing, back_attn_0.small, attn_hops[0])
+    token = back_attn_0.attn_send
     shape = (2, width, width)
-    finish_masks = order_masks(ff_split)
-    near_masks = [mask // 2 for mask in finish_masks[: ff_count // 2]]
-    far_masks = [mask // 2 for mask in finish_masks[ff_count // 2 :]]
-    chains = (ff_0, ff_1, attn_0, attn_1, small)
-    while any(chain.arriving is not None for chain in chains):
-        if "near" in ff_1.out and done_1 is None:
-            pieces = join(ff_1.out["near"], ff_1.out["far"])
-            done_1 = finish(tie(pieces, token), near_masks + far_masks, 1, place, shape)
+    near_masks = ff_masks[0][: ff_count // 2]
+    far_masks = ff_masks[0][ff_count // 2 :]
+    done_1 = sums = attn_grads = None
+    while True:
+        for chain in (ff_0, ff_1, attn_0, small, attn_1):
+            token = chain.step(token)
+        if sums is None and small.arriving is None:
+            sums = run(
+                small_body,
+                "small_sums",
+                dict(packed=Kept(tie(small.out["piece"], token))),
+                dict(
+                    gain_attn=((2, width), f32),
+                    gain_ff=((2, width), f32),
+                    embed=((1, width), f32),
+                    table=(bias_table.shape, f32),
+                ),
+                {},
+            )
+            token = sums.embed
+        if attn_grads is None and attn_0.arriving is None and attn_1.arriving is None:
+            attn_grads = jnp.stack([attn_0.out["done"], tie(attn_1.out["done"], token)])
+            token = attn_grads
+        if done_1 is None and ff_1.arriving is None:
+            pieces = tie(join(ff_1.out["near"], ff_1.out["far"]), token)
+            done_1 = finish(pieces, ff_masks[1], 1, place, shape)
             token = done_1[0]
-        for chain in chains:
-            token = chain.step(token)
-    if done_1 is None:
-        pieces = join(ff_1.out["near"], ff_1.out["far"])
-        done_1 = finish(pieces, near_masks + far_masks, 1, place, shape)
+        if ff_0.arriving is None:
+            break
     near_0 = finish(ff_0.out["near"], near_masks, 0, place, shape, done_1)
     done = finish(ff_0.out["far"], far_masks, 0, place, shape, near_0)
-    sums = run(
-        small_body,
-        "small_sums",
-        dict(packed=Kept(small.out["piece"])),
-        dict(
-            gain_attn=((2, width), f32),
-            gain_ff=((2, width), f32),
-            embed=((1, width), f32),
-            table=(bias_table.shape, f32),
-        ),
-        {},
-    )
-    attn_0, attn_1 = attn_0.out["done"], attn_1.out["done"]
-    attn_grads = jnp.stack([attn_0, attn_1])
     return (
         back_1.outputs.reshape(inputs.shape),
-        back_0.grad_next.reshape(inputs.shape),
+        back_attn_0.grad_next.reshape(inputs.shape),
         attn_grads[:, :, :inner],
         attn_grads[:, :, inner : 2 * inner],
         attn_grads[:, :, 2 * inner : 3 * inner],

time: 199 us -> 176 us (0.88)
  starting transfers between devices: 57 us -> 42.5 us
  waiting for transfers between devices: 74.9 us -> 68.9 us
  local copies, waits for them, and re-layouts: 11.3 us -> 6.13 us
    ppermute x50, starting transfers between devices: 57 us -> 42.5 us  [swap(): return lax.ppermute(array, axes, [(n, n ^ mask) for n in range(devices)])]
    ppermute x50, waiting for transfers between devices: 74.9 us -> 68.9 us  [swap(): return lax.ppermute(array, axes, [(n, n ^ mask) for n in range(devices)])]
    unnamed x65 -> x36, local copies, waits for them, and re-layouts: 6.06 us -> 0.88 us
    pallas_call x8 -> x10, Pallas kernels: 44.1 us -> 45.2 us  [run(): pl.pallas_call(kernel, name=name, in_specs=[pl.BlockSpec(memory_space=in_...]
  transfers between devices with their start and end apart: 50 -> 50, of which waited for: 23 -> 23; matrix products, arithmetic and copies ran while one was open for 5% -> 5% of each run, Pallas kernels for 24% -> 26%
where the time goes in v5:
time: 176 us
  waiting for transfers between devices  68.9 us (39%)
  Pallas kernels  51.3 us (29%)
  starting transfers between devices  42.5 us (24%)
  local copies, waits for them, and re-layouts  6.13 us (3%)
  other arithmetic  5.48 us (3%)
    ppermute x50, waiting for transfers between devices, swap(): return lax.ppermute(array, axes, [(n, n ^ mask) for n in range(devices)])  68.9 us
    pallas_call x10, Pallas kernels, run(): pl.pallas_call(kernel, name=name, in_specs=[pl.BlockSpec(memory_space=in_...  45.2 us
    ppermute x50, starting transfers between devices, swap(): return lax.ppermute(array, axes, [(n, n ^ mask) for n in range(devices)])  42.5 us
    pallas_call x3, Pallas kernels, finish(): pl.pallas_call(kernel, name='layer_%d_ff_grads' % layer_idx, in_specs=[pl...  6.12 us
  transfers between devices with their start and end apart: 50, of which 23 were waited for; matrix products, arithmetic and copies ran while one was open for 5% of the time, Pallas kernels for 26%

profile of v5, /device:TPU:0, one launch (start us, length us, event | category | flops | bytes accessed | tf_op | source)
XLA Modules:
  0.0 175.9 jit_solution(5713512664762573837)
XLA Ops:
  1.5 3.0 %collective-permute-start.1 = (bf16[16,1536]{1,0:T(8,128)(2,1)S(1)}, bf16[16,1536]{1,0:T(8,128)(2,1)S(1)}, u32[]{:S(2)}, u32[]{:S(2)}) collective-permute-start(bf16[16,1536]{1,0:T(8,128)(2,1)S(1)} %get-tuple-element.304), channel_id=1, source_target_pairs={{0,1},{1,0},{2,3},{3,2},{4,5},{5,4},{6,7},{7,6},{8,9},{9,8},{10,11... | collective-permute-start | bytes 147464 | tf_op jit(solution)/shard_map/ppermute | solution.py:554
  4.5 2.6 %collective-permute-start = (bf16[16,1536]{1,0:T(8,128)(2,1)S(1)}, bf16[16,1536]{1,0:T(8,128)(2,1)S(1)}, u32[]{:S(2)}, u32[]{:S(2)}) collective-permute-start(bf16[16,1536]{1,0:T(8,128)(2,1)S(1)} %get-tuple-element.305), channel_id=1, source_target_pairs={{0,16},{1,17},{2,18},{3,19},{4,20},{5,21},{6,22},{7,23},{8,24},{9,... | collective-permute-start | bytes 147464 | tf_op jit(solution)/shard_map/ppermute | solution.py:554
  14.7 2.9 %collective-permute-done.2 = bf16[32,1536]{1,0:T(8,128)(2,1)S(1)} collective-permute-done((bf16[32,1536]{1,0:T(8,128)(2,1)S(1)}, bf16[32,1536]{1,0:T(8,128)(2,1)S(1)}, u32[]{:S(2)}, u32[]{:S(2)}) %collective-permute-start.2) | collective-permute-done | bytes 98336 | tf_op jit(solution)/shard_map/ppermute | solution.py:554
  19.8 3.6 %collective-permute-done.3 = bf16[64,1536]{1,0:T(8,128)(2,1)S(1)} collective-permute-done((bf16[64,1536]{1,0:T(8,128)(2,1)S(1)}, bf16[64,1536]{1,0:T(8,128)(2,1)S(1)}, u32[]{:S(2)}, u32[]{:S(2)}) %collective-permute-start.3) | collective-permute-done | bytes 196640 | tf_op jit(solution)/shard_map/ppermute | solution.py:554
  23.9 3.2 %collective-permute-done.7 = bf16[64,1536]{1,0:T(8,128)(2,1)S(1)} collective-permute-done((bf16[64,1536]{1,0:T(8,128)(2,1)S(1)}, bf16[64,1536]{1,0:T(8,128)(2,1)S(1)}, u32[]{:S(2)}, u32[]{:S(2)}) %collective-permute-start.7) | collective-permute-done | bytes 196640 | tf_op jit(solution)/shard_map/ppermute | solution.py:554
  32.7 7.2 %collective-permute-done.8 = bf16[3,128,512]{2,1,0:T(8,128)(2,1)S(1)} collective-permute-done((bf16[3,128,512]{2,1,0:T(8,128)(2,1)S(1)}, bf16[3,128,512]{2,1,0:T(8,128)(2,1)S(1)}, u32[]{:S(2)}, u32[]{:S(2)}) %collective-permute-start.8) | collective-permute-done | bytes 393248 | tf_op jit(solution)/shard_map/ppermute | solution.py:554
  43.1 5.0 %layer_0_attention.1 = (bf16[512,1536]{1,0:T(8,128)(2,1)S(1)}, bf16[512,1152]{1,0:T(8,128)(2,1)S(1)}, f32[512,384]{1,0:T(8,128)S(1)}, bf16[512,384]{1,0:T(8,128)...) custom-call(s32[4]{0:T(128)S(1)} %pad_add_fusion.1.refs_0_.place_ref, ...), custom_call_target="tpu_custom_call" | custom-call | flops 11500000256 | tf_op jit(solution)/shard_map/layer_0_attention/pallas_call | solution.py:98
  48.1 7.6 %collective-permute-done.13.refs_10_.refs_6_ = bf16[512,512]{1,0:T(8,128)(2,1)S(1)} collective-permute-done((bf16[512,512]{1,0:T(8,128)(2,1)S(1)}, bf16[512,512]{1,0:T(8,128)(2,1)S(1)}, u32[]{:S(2)}, u32[]{:S(2)}) %collective-permute-start.13) | collective-permute-done | bytes 524320 | tf_op jit(solution)/shard_map/ppermute | solution.py:554
  55.7 3.9 %layer_0_ff.1 = (bf16[2,512,1024]{2,1,0:T(8,128)(2,1)S(1)}, bf16[2,512,512]{2,1,0:T(8,128)(2,1)S(1)}, f32[512,512]{1,0:T(8,128)S(1)}, bf16[512,512]{1,0:T(8,128)(2,1)S(1)}) custom-call(s32[4]{0:T(128)S(1)} %pad_add_fusion.1.refs_0_.place_ref, f32[512,512]{1,0:T(8,128)S(1)} %get-tuple-element.139.refs_1_.refs_3_, ...), custom_call_target="tpu_custom_call" | custom-call | flops 115000000 | tf_op jit(solution)/shard_map/layer_0_ff/pallas_call | solution.py:98
  60.4 5.0 %layer_1_attention.1 = (bf16[512,1536]{1,0:T(8,128)(2,1)S(1)}, bf16[512,1152]{1,0:T(8,128)(2,1)S(1)}, f32[512,384]{1,0:T(8,128)S(1)}, bf16[512,384]{1,0:T(8,128)...) custom-call(s32[4]{0:T(128)S(1)} %pad_add_fusion.1.refs_0_.place_ref, ...), custom_call_target="tpu_custom_call" | custom-call | flops 115000000 | tf_op jit(solution)/shard_map/layer_1_attention/pallas_call | solution.py:98
  67.1 10.7 %layer_1_backward.1 = (bf16[2,512,1024]{2,1,0:T(8,128)(2,1)S(1)}, bf16[2,512,512]{2,1,0:T(8,128)(2,1)S(1)}, bf16[512,512]{1,0:T(8,128)(2,1)S(1)}, bf16[512,1024]...) custom-call(s32[4]{0:T(128)S(1)} %pad_add_fusion.1.refs_0_.place_ref, ...), custom_call_target="tpu_custom_call" | custom-call | flops 11500000256 | tf_op jit(solution)/shard_map/layer_1_backward/pallas_call | solution.py:98
  78.5 7.4 %collective-permute-done.17.refs_8_.refs_5_ = bf16[512,512]{1,0:T(8,128)(2,1)S(1)} collective-permute-done((bf16[512,512]{1,0:T(8,128)(2,1)S(1)}, bf16[512,512]{1,0:T(8,128)(2,1)S(1)}, u32[]{:S(2)}, u32[]{:S(2)}) %collective-permute-start.17) | collective-permute-done | bytes 524320 | tf_op jit(solution)/shard_map/ppermute | solution.py:554
  85.9 4.5 %layer_0_ff_backward.1 = (bf16[512,512]{1,0:T(8,128)(2,1)S(1)}, bf16[512,1024]{1,0:T(8,128)(2,1)S(1)}, f32[56,128]{1,0:T(8,128)S(1)}, f32[512,512]{1,0:T(8,128)S(1)}, bf16[512,512]{1,0:T(8,128)(2,1)S(1)}) custom-call(f32[512,512]{1,0:T(8,128)S(1)} %get-tuple-element.157.refs_0_, f32[2,512]{1,0:T(2,128)S(1)} %copy-done.5, ...), custom_call_target="tpu_custom_call" | custom-call | flops 11500000256 | tf_op jit(solution)/shard_map/layer_0_ff_backward/pallas_call | solution.py:98
  90.7 4.2 %layer_1_weight_grads.1 = (bf16[8,32,1536]{2,1,0:T(8,128)(2,1)S(1)}, bf16[8,32,1536]{2,1,0:T(8,128)(2,1)S(1)}) custom-call(s32[4]{0:T(128)S(1)} %pad_add_fusion.1.refs_0_.place_ref, bf16[512,512]{1,0:T(8,128)(2,1)S(1)} %get-tuple-element.148.refs_4_.refs_1_, bf16[512,512]{1,0:T(8,128)(2,1)S(1)} %bitcast.36, bf16[512,512]{1,0:T(8,128)(2,1)S(1)} %get-tuple-element.171.refs_3_, ...), custom_call_target="tpu_custom_call" | custom-call | flops 115000000 | tf_op jit(solution)/shard_map/layer_1_weight_grads/pallas_call | solution.py:98
  96.7 3.8 %layer_0_weight_grads.1 = (bf16[8,32,1536]{2,1,0:T(8,128)(2,1)S(1)}, bf16[8,32,1536]{2,1,0:T(8,128)(2,1)S(1)}) custom-call(s32[4]{0:T(128)S(1)} %pad_add_fusion.1.refs_0_.place_ref, bf16[512,512]{1,0:T(8,128)(2,1)S(1)} %get-tuple-element.140.refs_2_.refs_4_.refs_1_, bf16[512,512]{1,0:T(8,128)(2,1)S(1)} %get-tuple-element.168.refs_2_, ...), custom_call_target="tpu_custom_call" | custom-call | flops 4600000000 | tf_op jit(solution)/shard_map/layer_0_weight_grads/pallas_call | solution.py:98
  102.4 4.5 %collective-permute-done.21 = bf16[8,16,1536]{2,1,0:T(8,128)(2,1)S(1)} collective-permute-done((bf16[8,16,1536]{2,1,0:T(8,128)(2,1)S(1)}, bf16[8,16,1536]{2,1,0:T(8,128)(2,1)S(1)}, u32[]{:S(2)}, u32[]{:S(2)}) %collective-permute-start.21) | collective-permute-done | bytes 393248 | tf_op jit(solution)/shard_map/ppermute | solution.py:554
  108.2 6.3 %layer_0_attention_backward.1 = (bf16[16,16,1536]{2,1,0:T(8,128)(2,1)S(1)}, bf16[16,16,1536]{2,1,0:T(8,128)(2,1)S(1)}, f32[56,128]{1,0:T(8,128)S(1)}, f32[512,512]{1,0:T(8,128)}) custom-call(s32[4]{0:T(128)S(1)} %pad_add_fusion.1.refs_0_.place_ref, f32[64,384]{1,0:T(8,128)S(1)} %get-tuple-element.156.refs_1_, s32[512,2]{1,0:T(8,128)S(1)} %copy.47.refs_1_.refs_2_, ...), custom_call_target="tpu_custom_call" | custom-call | flops 8049999872 | tf_op jit(solution)/shard_map/layer_0_attention_backward/pallas_call | solution.py:98
  125.2 3.0 %collective-permute-start.33 = (bf16[1,32,1536]{2,1,0:T(8,128)(2,1)S(1)}, bf16[1,32,1536]{2,1,0:T(8,128)(2,1)S(1)}, u32[]{:S(2)}, u32[]{:S(2)}) collective-permute-start(bf16[1,32,1536]{2,1,0:T(8,128)(2,1)S(1)} %add_convert_fusion.24), channel_id=1, source_target_pairs={{0,16},{1,17},{2,18},{3,19},{4,20},{5,21},{6,22},{7,23},{8,24},{9,... | collective-permute-start | bytes 294920 | tf_op jit(solution)/shard_map/ppermute | solution.py:554
  128.3 5.2 %collective-permute-done.27 = bf16[2,32,1536]{2,1,0:T(8,128)(2,1)S(1)} collective-permute-done((bf16[2,32,1536]{2,1,0:T(8,128)(2,1)S(1)}, bf16[2,32,1536]{2,1,0:T(8,128)(2,1)S(1)}, u32[]{:S(2)}, u32[]{:S(2)}) %collective-permute-start.27) | collective-permute-done | bytes 196640 | tf_op jit(solution)/shard_map/ppermute | solution.py:554
  140.4 2.6 %collective-permute-done.31 = bf16[4,16,1536]{2,1,0:T(8,128)(2,1)S(1)} collective-permute-done((bf16[4,16,1536]{2,1,0:T(8,128)(2,1)S(1)}, bf16[4,16,1536]{2,1,0:T(8,128)(2,1)S(1)}, u32[]{:S(2)}, u32[]{:S(2)}) %collective-permute-start.31) | collective-permute-done | bytes 196640 | tf_op jit(solution)/shard_map/ppermute | solution.py:554
  145.9 3.4 %collective-permute-done.36 = bf16[2,16,1536]{2,1,0:T(8,128)(2,1)S(1)} collective-permute-done((bf16[2,16,1536]{2,1,0:T(8,128)(2,1)S(1)}, bf16[2,16,1536]{2,1,0:T(8,128)(2,1)S(1)}, u32[]{:S(2)}, u32[]{:S(2)}) %collective-permute-start.36) | collective-permute-done | bytes 98336 | tf_op jit(solution)/shard_map/ppermute | solution.py:554
  149.9 2.8 %collective-permute-done.43 = bf16[2,32,1536]{2,1,0:T(8,128)(2,1)S(1)} collective-permute-done((bf16[2,32,1536]{2,1,0:T(8,128)(2,1)S(1)}, bf16[2,32,1536]{2,1,0:T(8,128)(2,1)S(1)}, u32[]{:S(2)}, u32[]{:S(2)}) %collective-permute-start.43) | collective-permute-done | bytes 196640 | tf_op jit(solution)/shard_map/ppermute | solution.py:554
  157.7 2.9 %collective-permute-done.46 = bf16[4,32,1536]{2,1,0:T(8,128)(2,1)S(1)} collective-permute-done((bf16[4,32,1536]{2,1,0:T(8,128)(2,1)S(1)}, bf16[4,32,1536]{2,1,0:T(8,128)(2,1)S(1)}, u32[]{:S(2)}, u32[]{:S(2)}) %collective-permute-start.46) | collective-permute-done | bytes 393248 | tf_op jit(solution)/shard_map/ppermute | solution.py:554
  160.8 4.0 %collective-permute-done.48 = bf16[4,32,1536]{2,1,0:T(8,128)(2,1)S(1)} collective-permute-done((bf16[4,32,1536]{2,1,0:T(8,128)(2,1)S(1)}, bf16[4,32,1536]{2,1,0:T(8,128)(2,1)S(1)}, u32[]{:S(2)}, u32[]{:S(2)}) %collective-permute-start.48) | collective-permute-done | bytes 393248 | tf_op jit(solution)/shard_map/ppermute | solution.py:554
  (183 shorter events, 64.8 us)
Async XLA Ops:
  1.5 8.8 %collective-permute-start.1 = (bf16[16,1536]{1,0:T(8,128)(2,1)S(1)}, bf16[16,1536]{1,0:T(8,128)(2,1)S(1)}, u32[]{:S(2)}, u32[]{:S(2)}) collective-permute-start(bf16[16,1536]{1,0:T(8,128)(2,1)S(1)} %get-tuple-element.304), channel_id=1, source_target_pairs={{0,1},{1,0},{2,3},{3,2},{4,5},{5,4},{6,7},{7,6},{8,9},{9,8},{10,11... | collective-permute-start | bytes 147464 | tf_op jit(solution)/shard_map/ppermute | solution.py:554
  10.3 19.0 %collective-permute-start.5 = (bf16[6,128,512]{2,1,0:T(8,128)(2,1)}, bf16[6,128,512]{2,1,0:T(8,128)(2,1)}, u32[]{:S(2)}, u32[]{:S(2)}) collective-permute-start(bf16[6,128,512]{2,1,0:T(8,128)(2,1)} %pad_maximum_fusion), channel_id=1, source_target_pairs={{0,1},{1,0},{2,3},{3,2},{4,5},{5,4},{6,7},{7,6},{8,9},{9,8},{10,11... | collective-permute-start | bytes 2359304 | tf_op jit(solution)/shard_map/ppermute | solution.py:554
  23.4 9.3 %collective-permute-start.4 = (bf16[128,1536]{1,0:T(8,128)(2,1)S(1)}, bf16[128,1536]{1,0:T(8,128)(2,1)S(1)}, u32[]{:S(2)}, u32[]{:S(2)}) collective-permute-start(bf16[128,1536]{1,0:T(8,128)(2,1)S(1)} %pad_maximum_fusion.4), channel_id=1, source_target_pairs={{0,8},{1,9},{2,10},{3,11},{4,12},{5,13},{6,14},{7,15},{8,0},{9,1},... | collective-permute-start | bytes 1179656 | tf_op jit(solution)/shard_map/ppermute | solution.py:554
  30.5 9.4 %collective-permute-start.8 = (bf16[3,128,512]{2,1,0:T(8,128)(2,1)S(1)}, bf16[3,128,512]{2,1,0:T(8,128)(2,1)S(1)}, u32[]{:S(2)}, u32[]{:S(2)}) collective-permute-start(bf16[3,128,512]{2,1,0:T(8,128)(2,1)S(1)} %get-tuple-element.137), channel_id=1, source_target_pairs={{0,4},{1,5},{2,6},{3,7},{4,0},{5,1},{6,2},{7,3},{8,12},{9,13},{10,... | collective-permute-start | bytes 1179656 | tf_op jit(solution)/shard_map/ppermute | solution.py:554
  32.1 9.1 %collective-permute-start.10 = (bf16[128,1536]{1,0:T(8,128)(2,1)S(1)}, bf16[128,1536]{1,0:T(8,128)(2,1)S(1)}, u32[]{:S(2)}, u32[]{:S(2)}) collective-permute-start(bf16[128,1536]{1,0:T(8,128)(2,1)S(1)} %pad_maximum_fusion.5), channel_id=1, source_target_pairs={{0,1},{1,0},{2,3},{3,2},{4,5},{5,4},{6,7},{7,6},{8,9},{9,8},{10,11... | collective-permute-start | bytes 1179656 | tf_op jit(solution)/shard_map/ppermute | solution.py:554
  41.3 14.4 %collective-permute-start.11 = (bf16[6,128,512]{2,1,0:T(8,128)(2,1)S(1)}, bf16[6,128,512]{2,1,0:T(8,128)(2,1)S(1)}, u32[]{:S(2)}, u32[]{:S(2)}) collective-permute-start(bf16[6,128,512]{2,1,0:T(8,128)(2,1)S(1)} %constant_dynamic-update-slice_fusion.10.refs_7_), channel_id=1, source_target_pairs={{0,2},{1,3},{2,0},{3,1},{4,6},{5,7},{6,4},{7,5},{8,10},{9,11},{10,... | collective-permute-start | bytes 2359304 | tf_op jit(solution)/shard_map/ppermute | solution.py:554
  41.4 14.3 %collective-permute-start.13 = (bf16[512,512]{1,0:T(8,128)(2,1)S(1)}, bf16[512,512]{1,0:T(8,128)(2,1)S(1)}, u32[]{:S(2)}, u32[]{:S(2)}) collective-permute-start(bf16[512,512]{1,0:T(8,128)(2,1)S(1)} %bitcast.34), channel_id=1, source_target_pairs={{0,1},{1,0},{2,3},{3,2},{4,5},{5,4},{6,7},{7,6},{8,9},{9,8},{10,11... | collective-permute-start | bytes 1572872 | tf_op jit(solution)/shard_map/ppermute | solution.py:554
  42.0 17.7 %collective-permute-start.14 = (bf16[3,128,512]{2,1,0:T(8,128)(2,1)S(1)}, bf16[3,128,512]{2,1,0:T(8,128)(2,1)S(1)}, u32[]{:S(2)}, u32[]{:S(2)}) collective-permute-start(bf16[3,128,512]{2,1,0:T(8,128)(2,1)S(1)} %get-tuple-element.149), channel_id=1, source_target_pairs={{0,4},{1,5},{2,6},{3,7},{4,0},{5,1},{6,2},{7,3},{8,12},{9,13},{10,... | collective-permute-start | bytes 1179656 | tf_op jit(solution)/shard_map/ppermute | solution.py:554
  43.0 12.7 %collective-permute-start.12 = (bf16[256,1536]{1,0:T(8,128)(2,1)S(1)}, bf16[256,1536]{1,0:T(8,128)(2,1)S(1)}, u32[]{:S(2)}, u32[]{:S(2)}) collective-permute-start(bf16[256,1536]{1,0:T(8,128)(2,1)S(1)} %constant_dynamic-update-slice_fusion.5.refs_6_), channel_id=1, source_target_pairs={{0,2},{1,3},{2,0},{3,1},{4,6},{5,7},{6,4},{7,5},{8,10},{9,11},{10,... | collective-permute-start | bytes 2359304 | tf_op jit(solution)/shard_map/ppermute | solution.py:554
  59.9 18.6 %collective-permute-start.16 = (bf16[512,512]{1,0:T(8,128)(2,1)S(1)}, bf16[512,512]{1,0:T(8,128)(2,1)S(1)}, u32[]{:S(2)}, u32[]{:S(2)}) collective-permute-start(bf16[512,512]{1,0:T(8,128)(2,1)S(1)} %get-tuple-element.140.refs_2_.refs_4_.refs_1_), channel_id=1, source_target_pairs={{0,1},{1,0},{2,3},{3,2},{4,5},{5,4},{6,7},{7,6},{8,9},{9,8},{10,11... | collective-permute-start | bytes 1572872 | tf_op jit(solution)/shard_map/ppermute | solution.py:554
  65.5 20.4 %collective-permute-start.17 = (bf16[512,512]{1,0:T(8,128)(2,1)S(1)}, bf16[512,512]{1,0:T(8,128)(2,1)S(1)}, u32[]{:S(2)}, u32[]{:S(2)}) collective-permute-start(bf16[512,512]{1,0:T(8,128)(2,1)S(1)} %get-tuple-element.148.refs_4_.refs_1_), channel_id=1, source_target_pairs={{0,1},{1,0},{2,3},{3,2},{4,5},{5,4},{6,7},{7,6},{8,9},{9,8},{10,11... | collective-permute-start | bytes 1572872 | tf_op jit(solution)/shard_map/ppermute | solution.py:554
  77.8 12.6 %collective-permute-start.19 = (bf16[16,16,1536]{2,1,0:T(8,128)(2,1)S(1)}, bf16[16,16,1536]{2,1,0:T(8,128)(2,1)S(1)}, u32[]{:S(2)}, u32[]{:S(2)}) collective-permute-start(bf16[16,16,1536]{2,1,0:T(8,128)(2,1)S(1)} %get-tuple-element.176), channel_id=1, source_target_pairs={{0,2},{1,3},{2,0},{3,1},{4,6},{5,7},{6,4},{7,5},{8,10},{9,11},{10,... | collective-permute-start | bytes 2359304 | tf_op jit(solution)/shard_map/ppermute | solution.py:554
  77.8 18.8 %collective-permute-start.18 = (bf16[512,512]{1,0:T(8,128)(2,1)S(1)}, bf16[512,512]{1,0:T(8,128)(2,1)S(1)}, u32[]{:S(2)}, u32[]{:S(2)}) collective-permute-start(bf16[512,512]{1,0:T(8,128)(2,1)S(1)} %get-tuple-element.168.refs_2_), channel_id=1, source_target_pairs={{0,1},{1,0},{2,3},{3,2},{4,5},{5,4},{6,7},{7,6},{8,9},{9,8},{10,11... | collective-permute-start | bytes 1572872 | tf_op jit(solution)/shard_map/ppermute | solution.py:554
  95.0 12.0 %collective-permute-start.21 = (bf16[8,16,1536]{2,1,0:T(8,128)(2,1)S(1)}, bf16[8,16,1536]{2,1,0:T(8,128)(2,1)S(1)}, u32[]{:S(2)}, u32[]{:S(2)}) collective-permute-start(bf16[8,16,1536]{2,1,0:T(8,128)(2,1)S(1)} %get-tuple-element.283.refs_9_), channel_id=1, source_target_pairs={{0,8},{1,9},{2,10},{3,11},{4,12},{5,13},{6,14},{7,15},{8,0},{9,1},... | collective-permute-start | bytes 1179656 | tf_op jit(solution)/shard_map/ppermute | solution.py:554
  100.9 18.7 %collective-permute-start.24 = (bf16[4,32,1536]{2,1,0:T(8,128)(2,1)S(1)}, bf16[4,32,1536]{2,1,0:T(8,128)(2,1)S(1)}, u32[]{:S(2)}, u32[]{:S(2)}) collective-permute-start(bf16[4,32,1536]{2,1,0:T(8,128)(2,1)S(1)} %get-tuple-element.281), channel_id=1, source_target_pairs={{0,8},{1,9},{2,10},{3,11},{4,12},{5,13},{6,14},{7,15},{8,0},{9,1},... | collective-permute-start | bytes 1179656 | tf_op jit(solution)/shard_map/ppermute | solution.py:554
  107.0 17.5 %collective-permute-start.29 = (bf16[4,16,1536]{2,1,0:T(8,128)(2,1)S(1)}, bf16[4,16,1536]{2,1,0:T(8,128)(2,1)S(1)}, u32[]{:S(2)}, u32[]{:S(2)}) collective-permute-start(bf16[4,16,1536]{2,1,0:T(8,128)(2,1)S(1)} %get-tuple-element.287), channel_id=1, source_target_pairs={{0,16},{1,17},{2,18},{3,19},{4,20},{5,21},{6,22},{7,23},{8,24},{9,... | collective-permute-start | bytes 589832 | tf_op jit(solution)/shard_map/ppermute | solution.py:554
  107.6 10.0 %collective-permute-start.25 = (bf16[4,32,1536]{2,1,0:T(8,128)(2,1)S(1)}, bf16[4,32,1536]{2,1,0:T(8,128)(2,1)S(1)}, u32[]{:S(2)}, u32[]{:S(2)}) collective-permute-start(bf16[4,32,1536]{2,1,0:T(8,128)(2,1)S(1)} %get-tuple-element.279.refs_14_), channel_id=1, source_target_pairs={{0,4},{1,5},{2,6},{3,7},{4,0},{5,1},{6,2},{7,3},{8,12},{9,13},{10,... | collective-permute-start | bytes 1179656 | tf_op jit(solution)/shard_map/ppermute | solution.py:554
  119.7 13.8 %collective-permute-start.27 = (bf16[2,32,1536]{2,1,0:T(8,128)(2,1)S(1)}, bf16[2,32,1536]{2,1,0:T(8,128)(2,1)S(1)}, u32[]{:S(2)}, u32[]{:S(2)}) collective-permute-start(bf16[2,32,1536]{2,1,0:T(8,128)(2,1)S(1)} %get-tuple-element.291), channel_id=1, source_target_pairs={{0,16},{1,17},{2,18},{3,19},{4,20},{5,21},{6,22},{7,23},{8,24},{9,... | collective-permute-start | bytes 589832 | tf_op jit(solution)/shard_map/ppermute | solution.py:554
  122.4 12.2 %collective-permute-start.26 = (bf16[8,16,1536]{2,1,0:T(8,128)(2,1)S(1)}, bf16[8,16,1536]{2,1,0:T(8,128)(2,1)S(1)}, u32[]{:S(2)}, u32[]{:S(2)}) collective-permute-start(bf16[8,16,1536]{2,1,0:T(8,128)(2,1)S(1)} %get-tuple-element.276), channel_id=1, source_target_pairs={{0,1},{1,0},{2,3},{3,2},{4,5},{5,4},{6,7},{7,6},{8,9},{9,8},{10,11... | collective-permute-start | bytes 1179656 | tf_op jit(solution)/shard_map/ppermute | solution.py:554
  123.0 12.8 %collective-permute-start.35 = (f32[56,128]{1,0:T(8,128)S(1)}, f32[56,128]{1,0:T(8,128)S(1)}, u32[]{:S(2)}, u32[]{:S(2)}) collective-permute-start(f32[56,128]{1,0:T(8,128)S(1)} %add.136), channel_id=1, source_target_pairs={{0,1},{1,0},{2,3},{3,2},{4,5},{5,4},{6,7},{7,6},{8,9},{9,8},{10,11... | collective-permute-start | bytes 86024 | tf_op jit(solution)/shard_map/ppermute | solution.py:554
  124.6 12.2 %collective-permute-start.34 = (bf16[2,16,1536]{2,1,0:T(8,128)(2,1)S(1)}, bf16[2,16,1536]{2,1,0:T(8,128)(2,1)S(1)}, u32[]{:S(2)}, u32[]{:S(2)}) collective-permute-start(bf16[2,16,1536]{2,1,0:T(8,128)(2,1)S(1)} %get-tuple-element.297), channel_id=1, source_target_pairs={{0,4},{1,5},{2,6},{3,7},{4,0},{5,1},{6,2},{7,3},{8,12},{9,13},{10,... | collective-permute-start | bytes 294920 | tf_op jit(solution)/shard_map/ppermute | solution.py:554
  125.2 12.2 %collective-permute-start.33 = (bf16[1,32,1536]{2,1,0:T(8,128)(2,1)S(1)}, bf16[1,32,1536]{2,1,0:T(8,128)(2,1)S(1)}, u32[]{:S(2)}, u32[]{:S(2)}) collective-permute-start(bf16[1,32,1536]{2,1,0:T(8,128)(2,1)S(1)} %add_convert_fusion.24), channel_id=1, source_target_pairs={{0,16},{1,17},{2,18},{3,19},{4,20},{5,21},{6,22},{7,23},{8,24},{9,... | collective-permute-start | bytes 294920 | tf_op jit(solution)/shard_map/ppermute | solution.py:554
  145.4 11.0 %collective-permute-start.42 = (bf16[2,32,1536]{2,1,0:T(8,128)(2,1)S(1)}, bf16[2,32,1536]{2,1,0:T(8,128)(2,1)S(1)}, u32[]{:S(2)}, u32[]{:S(2)}) collective-permute-start(bf16[2,32,1536]{2,1,0:T(8,128)(2,1)S(1)} %pad_maximum_fusion.12), channel_id=1, source_target_pairs={{0,16},{1,17},{2,18},{3,19},{4,20},{5,21},{6,22},{7,23},{8,24},{9,... | collective-permute-start | bytes 589832 | tf_op jit(solution)/shard_map/ppermute | solution.py:554
  156.5 9.3 %collective-permute-start.45 = (f32[56,128]{1,0:T(8,128)S(1)}, f32[56,128]{1,0:T(8,128)S(1)}, u32[]{:S(2)}, u32[]{:S(2)}) collective-permute-start(f32[56,128]{1,0:T(8,128)S(1)} %add.156), channel_id=1, source_target_pairs={{0,16},{1,17},{2,18},{3,19},{4,20},{5,21},{6,22},{7,23},{8,24},{9,... | collective-permute-start | bytes 86024 | tf_op jit(solution)/shard_map/ppermute | solution.py:554
  (38 other events, 254.8 us)

commit v6 on v5

--- a/solution.py
+++ b/solution.py
@@ -13,7 +13,7 @@
 bf16 = jnp.bfloat16
 f32 = jnp.float32
 axes = ("dp", "tensor")
-vmem_bytes = 26 * 1024 * 1024
+vmem_bytes = 32 * 1024 * 1024
 raw_names = ("attn_near", "attn_far", "ff_near", "ff_far", "w_gate", "w_up", "w_down")
 
 
@@ -296,17 +296,15 @@
             grad_hidden = dot_nt(rounded, r.ff_down[half])
             gate_act, up_act = both[:, :width], both[:, width:]
             mixed, slope = gelu_terms(gate_act)
-            if half == 0:
-                r.grad_gate_up[part, :width] = (grad_hidden * up_act * slope).astype(bf16)
-                r.grad_gate_up[part, width:] = (grad_hidden * mixed).astype(bf16)
-                pulled = r.grad_gate_up[part, :]
+            hidden = (mixed * up_act).astype(bf16)
+            if last or half == 0:
+                r.hidden[half, part, :] = hidden
+                held = r.grad_gate_up.at[half, part]
             else:
-                r.pulled[:, :width] = (grad_hidden * up_act * slope).astype(bf16)
-                r.pulled[:, width:] = (grad_hidden * mixed).astype(bf16)
-                pulled = r.pulled[...]
-            hidden = (mixed * up_act).astype(bf16)
-            if half == 0:
-                r.hidden[part, :] = hidden
+                held = r.pulled
+            held[:, :width] = (grad_hidden * up_act * slope).astype(bf16)
+            held[:, width:] = (grad_hidden * mixed).astype(bf16)
+            pulled = held[...]
             if last:
                 total = total + dot_nn(hidden, r.ff_down[half])
             term = dot_nt(pulled, r.ff_gate_up[half])
@@ -394,14 +392,29 @@
         for head in range(heads):
             cut = r.table_rows[:, head * head_size : (head + 1) * head_size]
             table = jnp.where(lane == head, jnp.sum(cut, axis=1, keepdims=True), table)
-        r.small[small_rows(width) :, :] = table
+        r.small[:heads, : table.shape[0]] = jnp.transpose(table)[:heads, :]
     r.drain("grad_next")
     return gain_total
 
 
-def last_backward_body(r, sizes, piece_masks, heads):
+def two_parts(values):
+    high = values.astype(bf16).astype(f32)
+    return high, (values - high).astype(bf16).astype(f32)
+
+
+def last_backward_body(r, sizes, piece_masks, ff_masks, heads):
     r.small[...] = jnp.zeros(r.small.shape, f32)
     put_row(r.small, 3, ff_backward(r, 1, True))
+    width = r.middle.shape[1]
+    for half in range(2):
+        r.ff_grad[half, :, : 2 * width] = dot_tn(r.ff_in[...], r.grad_gate_up[half])
+        r.ff_grad[half, :, 2 * width :] = dot_tn(r.hidden[half], r.grad[...])
+    count = len(ff_masks)
+    grain = r.ff_keep.shape[1]
+    for idx, mask in enumerate(ff_masks):
+        target = r.ff_keep if idx < count // 2 else r.ff_send
+        rows = pl.ds(pl.multiple_of((r.place[3] ^ (mask // 2)) * grain, grain), grain)
+        target[idx % (count // 2)] = r.ff_grad[mask % 2, rows, :].astype(bf16)
     put_row(r.small, 1, attention_backward(r, sizes, 1, True, piece_masks, heads))
     r.drain("outputs")
 
@@ -414,16 +427,16 @@
 def attention_backward_body(r, sizes, piece_masks, heads):
     r.small[...] = r.small_before[...]
     put_row(r.small, 0, attention_backward(r, sizes, 0, False, piece_masks, heads))
-
-
-def small_rows(width):
-    return -(-5 * width // 1024) * 8
+    high, low = two_parts(r.small[...])
+    last = r.attn_send.shape[0] - 1
+    r.attn_send[last] = jnp.concatenate([high, low], axis=0).astype(bf16)
+    r.small[...] = high + low
 
 
 def put_row(packed, which, row):
-    lanes = row.shape[1] // 128
-    for k in range(lanes):
-        packed[which * lanes + k : which * lanes + k + 1, :] = row[:, k * 128 : (k + 1) * 128]
+    first, width = packed.shape[0] - 2, row.shape[1]
+    at = which % 3 * width
+    packed[first + which // 3 : first + which // 3 + 1, at : at + width] = row
 
 
 def scatter_pieces(whole, keep, send, masks, place):
@@ -450,10 +463,10 @@
         r.peer_gate_up[part, width:] = (grad_hidden * mixed).astype(bf16)
         r.peer_hidden[part, :] = (mixed * up_act).astype(bf16)
     r.need("ff_in", "grad_gate_up", "hidden", "grad")
-    r.ff_grad[:, : 2 * width] = dot_tn(r.ff_in[...], r.grad_gate_up[...]) + dot_tn(
+    r.ff_grad[:, : 2 * width] = dot_tn(r.ff_in[...], r.grad_gate_up[0]) + dot_tn(
         r.peer_in[...], r.peer_gate_up[...]
     )
-    r.ff_grad[:, 2 * width :] = dot_tn(r.hidden[...], r.grad[...]) + dot_tn(
+    r.ff_grad[:, 2 * width :] = dot_tn(r.hidden[0], r.grad[...]) + dot_tn(
         r.peer_hidden[...], r.peer_grad[...]
     )
     scatter_pieces(r.ff_grad, r.ff_keep, r.ff_send, piece_masks, r.place[3])
@@ -496,17 +509,28 @@
 
 
 def small_body(r):
-    r.fetch("packed")
-    r.need("packed")
-    lanes = r.embed.shape[1] // 128
-    for which in range(5):
-        out, row = ((r.gain_attn, which), (r.gain_ff, which - 2), (r.embed, 0))[which // 2]
-        for k in range(lanes):
-            at = which * lanes + k
-            out[row : row + 1, k * 128 : (k + 1) * 128] = r.packed[at : at + 1, :]
-    r.table[...] = r.packed[small_rows(r.embed.shape[1]) :, : r.table.shape[1]]
+    width = r.embed.shape[1]
+    heads = r.table.shape[1]
+    outs = ((r.gain_attn, 0), (r.gain_attn, 1), (r.gain_ff, 0), (r.gain_ff, 1), (r.embed, 0))
+    for which, (out, row) in enumerate(outs):
+        first = r.packed.shape[0] - 2 + which // 3
+        at = which % 3 * width
+        out[row : row + 1, :] = r.packed[first : first + 1, at : at + width]
+    r.table[...] = jnp.transpose(r.packed[:, :128])[: r.table.shape[0], :heads]
     r.write("gain_attn", "gain_ff", "embed", "table")
     r.drain("gain_attn", "gain_ff", "embed", "table")
+
+
+def cut_body(r):
+    rows = r.quarters.shape[2]
+    at = pl.ds(pl.multiple_of(r.place[1] * rows, rows), rows)
+    copies = [
+        pltpu.make_async_copy(w.at[layer_idx, at], r.quarters.at[layer_idx, k], r.cut_sem)
+        for layer_idx in range(2)
+        for k, w in enumerate((r.w_gate, r.w_up, r.w_down))
+    ]
+    start_all(copies)
+    wait_all(r.cut_sem, r.quarters)
 
 
 def order_masks(hops):
@@ -574,13 +598,16 @@
 
     quarter = width // 4
     packed = jnp.concatenate([w_query, w_key, w_value, jnp.swapaxes(w_output, 1, 2)], axis=2)
-    ff_blocks = jnp.concatenate(
-        [
-            lax.dynamic_slice_in_dim(tie(w, packed), quarter_at * quarter, quarter, axis=1)
-            for w in (w_gate, w_up, w_down)
-        ],
-        axis=0,
-    )
+    ff_blocks = run(
+        cut_body,
+        "cut_quarters",
+        dict(place=place, w_gate=w_gate, w_up=w_up, w_down=w_down),
+        dict(quarters=Kept((2, 3, quarter, width), bf16)),
+        dict(cut_sem=pltpu.SemaphoreType.DMA),
+    ).quarters
+    own_rows = packed.shape[1]
+    direct = own_rows % 16 == 0
+    far = bits[2:]
 
     def prepare(token):
         table, marked, kept, near = (
@@ -611,16 +638,13 @@
         )
         return result, wide_buckets, marks
 
-    own_rows = packed.shape[1]
-    direct = own_rows % 16 == 0
-    far = bits[2:]
     if direct:
         hops_0 = [1] + far[2:] + far[:2] + [2]
         hops_1 = far[2:] + far[:2] + [1, 2]
         block_0, block_1 = packed[0], packed[1]
         got_1 = swap(block_1, hops_1[0])
         got_0 = swap(block_0, hops_0[0])
-        ff_quarter = swap(tie(ff_blocks, got_0), 1).reshape(3, 2, quarter, width)
+        ff_quarter = swap(tie(ff_blocks, got_0), 1)
         block_0 = join(block_0, got_0)
         block_1 = join(block_1, tie(got_1, block_0))
         for hop_0, hop_1 in zip(hops_0[1:-2], hops_1[1:-2]):
@@ -631,29 +655,27 @@
             block_1 = join(block_1, tie(got_1, block_0))
         got_0 = swap(block_0, hops_0[-2])
         got_1 = swap(block_1, hops_1[-2])
-        ff_0 = tie(ff_quarter[:, 0], block_1)
+        ff_0 = tie(ff_quarter[0], block_1)
         got_ff_0 = swap(ff_0, 4)
         block_0 = join(block_0, tie(got_0, start.a, got_ff_0))
         block_1 = join(block_1, tie(got_1, block_0))
         ff_0 = join(ff_0, tie(got_ff_0, block_1))
-        got_ff_1 = swap(tie(ff_quarter[:, 1], ff_0), 4)
-        peer_cotangent = swap(tie(cotangent, ff_0), 1)
+        got_ff_1 = swap(tie(ff_quarter[1], ff_0), 4)
         far_0 = swap(block_0, 2)
         attn_pieces = [
             (block_0, far_0, order_masks(hops_0[::-1])),
             (block_1, swap(tie(block_1, far_0), 2), order_masks(hops_1[::-1])),
         ]
-        after_first = (attn_pieces[1][1], peer_cotangent)
+        after_first = (attn_pieces[1][1],)
     else:
-        ff_quarter = swap(ff_blocks, 1).reshape(3, 2, quarter, width)
-        ff_0 = join(ff_quarter[:, 0], swap(ff_quarter[:, 0], 4))
+        ff_quarter = swap(ff_blocks, 1)
+        ff_0 = join(ff_quarter[0], swap(ff_quarter[0], 4))
         start, wide_buckets, marks = prepare(packed)
         whole = lax.all_gather(packed[0], axes, axis=0, tiled=True)
         attn_pieces = [(whole, whole, [0])]
         whole = lax.all_gather(packed[1], axes, axis=0, tiled=True)
         attn_pieces.append((whole, whole, [0]))
         after_first = ()
-        peer_cotangent = swap(cotangent, 1)
     ff_pieces = [(ff_0, swap(ff_0, 2))]
 
     def attn_ins(layer_idx):
@@ -719,31 +741,27 @@
         micros=0.1,
     )
     if direct:
-        ff_1 = join(ff_quarter[:, 1], tie(got_ff_1, first_ff.a_next))
+        ff_1 = join(ff_quarter[1], tie(got_ff_1, first_ff.a_next))
     else:
-        ff_1 = join(ff_quarter[:, 1], swap(ff_quarter[:, 1], 4))
+        ff_1 = join(ff_quarter[1], swap(ff_quarter[1], 4))
     ff_pieces.append((ff_1, swap(ff_1, 2)))
     second = attention(1, first_ff.x_next, first_ff.a_next, micros=0.1)
-    peer_in_1 = swap(second.ff_in, 1)
 
     attn_low = devices // attn_count
-    attn_hops = ([2, 1] + bits[2:], [2] + bits[3:] + bits[2:3] + [1])
+    attn_hops = ([2, 1] + bits[2:], [2, 1] + bits[2:])
     attn_split = [[hop for hop in hops if hop >= attn_low] for hops in attn_hops]
     attn_whole = [hop for hop in bits if hop < attn_low]
     attn_masks = [[mask // attn_low for mask in order_masks(hops)] for hops in attn_split]
-    ff_hops = (bits[1:], [2] + bits[3:] + bits[2:3])
+    ff_hops = ([2] + bits[3:] + bits[2:3], [2] + bits[2:3] + [1] + bits[3:])
     ff_split = [[hop for hop in hops if hop // 2 < ff_count] for hops in ff_hops]
     ff_whole = [hop for hop in bits[1:] if hop // 2 >= ff_count]
-    ff_masks = [[mask // 2 for mask in order_masks(hops)] for hops in ff_split]
+    ff_share = [[hop for hop in hops if hop > 1] for hops in ff_split]
+    ff_masks = [order_masks(hops) for hops in ff_split]
+    place_masks = [[mask // 2 for mask in order_masks(hops)] for hops in ff_share]
     attn_half = (attn_count // 2, attn_grain, 4 * inner)
     ff_half = (ff_count // 2, ff_grain, 3 * width)
-    small_shape = (small_rows(width) + bias_table.shape[0], 128)
-
-    ff_back_outs = dict(
-        hidden=Kept(matrix, bf16),
-        grad_gate_up=Kept((rows, 2 * width), bf16),
-        small=Kept(small_shape, f32),
-    )
+    small_shape = (heads + 2, 3 * width)
+
     attn_back_outs = dict(attn_keep=Kept(attn_half, bf16), attn_send=Kept(attn_half, bf16))
     attn_back_scratch = dict(
         grad_heads=pltpu.VMEM((rows, inner), bf16),
@@ -764,31 +782,6 @@
             qkv=Kept(kept.qkv),
             probs=Kept(kept.probs),
             heads=Kept(kept.heads),
-        )
-
-    def weight_grads(layer_idx, kept, weights, back, grad, peer_in, peer_grad, after, micros):
-        return run(
-            functools.partial(weight_body, piece_masks=ff_masks[layer_idx]),
-            "layer_%d_weight_grads" % layer_idx,
-            dict(
-                place=place,
-                ff_in=Kept(kept.ff_in),
-                grad=grad,
-                hidden=Kept(back.hidden),
-                grad_gate_up=Kept(back.grad_gate_up),
-                peer_in=Kept(peer_in),
-                peer_grad=Kept(peer_grad),
-                ff_gate_up=Kept(weights.ff_gate_up),
-                ff_down=Kept(weights.ff_down),
-            ),
-            dict(ff_keep=Kept(ff_half, bf16), ff_send=Kept(ff_half, bf16)),
-            dict(
-                peer_gate_up=pltpu.VMEM((rows, 2 * width), bf16),
-                peer_hidden=pltpu.VMEM(matrix, bf16),
-                ff_grad=pltpu.VMEM((width, 3 * width), f32),
-            ),
-            after=after,
-            micros=micros,
         )
 
     def add(left, right):
@@ -809,7 +802,7 @@
     def summing(piece, hops, out):
         for hop in hops:
             got = yield swap(piece, hop)
-            out["token"] = piece = add(piece, got) if piece.dtype == bf16 else piece + got
+            out["token"] = piece = add(piece, got)
         out["piece"] = piece
 
     def sharing(piece, hops, out):
@@ -821,20 +814,48 @@
                 out["token"] = got
         out["near"], out["far"] = piece, got
 
-    def attn_chain(part, split, out):
-        yield from halving(part.attn_keep, part.attn_send, split, out)
-        yield from summing(out["piece"], attn_whole, out)
-        piece = out["piece"][0]
+    def rounded(values):
+        return lax.reduce_precision(values, exponent_bits=8, mantissa_bits=7)
+
+    def with_small(pieces, small):
+        high = rounded(small)
+        low = rounded(small - high)
+        parts = join(high, low).astype(bf16)[None]
+        return join(pieces, parts), high + low
+
+    def add_small(small, got):
+        parts = got[-1].astype(f32)
+        return small + (parts[: small.shape[0]] + parts[small.shape[0] :])
+
+    def attn_chain(part, layer_idx, out):
+        small = part.small if layer_idx == 0 else None
+        keep, send = part.attn_keep, part.attn_send
+        hops = attn_split[layer_idx] + attn_whole
+        for step, hop in enumerate(hops):
+            got = yield swap(send, hop)
+            if small is not None:
+                small = add_small(small, got)
+                got = got[:-1]
+            if step + 1 < len(attn_split[layer_idx]):
+                half = keep.shape[0] // 2
+                send = add(keep[half:], got[half:])
+                keep = add(keep[:half], got[:half])
+            else:
+                send = keep = add(keep, got)
+            if small is not None and step + 1 < len(hops):
+                send, small = with_small(send, small)
+            out["token"] = send
+        piece = keep[0]
         if own_rows < attn_grain:
             first_row = lax.rem(device_at, attn_low) * own_rows
             piece = lax.dynamic_slice_in_dim(piece, first_row, own_rows, axis=0)
         out["done"] = piece.astype(f32)
-
-    def ff_chain(part, split, out):
-        yield from halving(part.ff_keep, part.ff_send, split, out)
+        out["small"] = small
+
+    def ff_chain(part, layer_idx, out):
+        yield from halving(part.ff_keep, part.ff_send, ff_split[layer_idx], out)
         yield from summing(out["piece"], ff_whole, out)
-        yield from sharing(out["piece"], split[::-1], out)
-        out["done"] = True
+        yield from sharing(out["piece"], ff_share[layer_idx][::-1], out)
 
     class Chain:
         def __init__(self, steps, *args):
@@ -842,9 +863,9 @@
             self.steps = steps(*args, self.out)
             self.arriving = next(self.steps)
 
-        def step(self, token):
+        def step(self, token, *others):
             if self.arriving is not None:
-                arrived = tie(self.arriving, token)
+                arrived = tie(self.arriving, token, *others)
                 self.arriving = None
                 try:
                     self.arriving = self.steps.send(arrived)
@@ -855,7 +876,11 @@
 
     back_1 = run(
         functools.partial(
-            last_backward_body, sizes=sizes, piece_masks=attn_masks[1], heads=heads
+            last_backward_body,
+            sizes=sizes,
+            piece_masks=attn_masks[1],
+            ff_masks=ff_masks[1],
+            heads=heads,
         ),
         "layer_1_backward",
         dict(
@@ -868,19 +893,29 @@
             **attn_back_ins(second, first_ff.x_next, first_ff.a_next),
         ),
         dict(
-            **ff_outs,
-            **ff_back_outs,
+            ff_keep=Kept((ff_count, ff_grain, 3 * width), bf16),
+            ff_send=Kept((ff_count, ff_grain, 3 * width), bf16),
+            small=Kept(small_shape, f32),
             **attn_back_outs,
             outputs=(matrix, bf16),
             grad_next=Kept(matrix, f32),
             grad_next_low=Kept(matrix, bf16),
             bias_acc=Kept(bias_shape, f32),
         ),
-        dict(**mid_scratch, **pulled_scratch, **attn_back_scratch, **ff_scratch),
+        dict(
+            ff_gate_up=pltpu.VMEM((2, width, 2 * width), bf16),
+            ff_down=pltpu.VMEM((2, width, width), bf16),
+            hidden=pltpu.VMEM((2, rows, width), bf16),
+            grad_gate_up=pltpu.VMEM((2, rows, 2 * width), bf16),
+            ff_grad=pltpu.VMEM((2, width, 3 * width), f32),
+            **mid_scratch,
+            **attn_back_scratch,
+            **ff_scratch,
+        ),
         micros=10,
     )
     peer_grad_0 = swap(back_1.grad_next_low, 1)
-    attn_1 = Chain(attn_chain, back_1, attn_split[1])
+    attn_1 = Chain(attn_chain, back_1, 1)
     back_0 = run(
         ff_backward_body,
         "layer_0_ff_backward",
@@ -893,31 +928,19 @@
             ff_gate_up=Kept(first_ff.ff_gate_up),
             ff_down=Kept(first_ff.ff_down),
         ),
-        dict(**ff_back_outs, grad_mid=Kept(matrix, f32), branch=Kept(matrix, bf16)),
+        dict(
+            hidden=Kept((1, rows, width), bf16),
+            grad_gate_up=Kept((1, rows, 2 * width), bf16),
+            small=Kept(small_shape, f32),
+            grad_mid=Kept(matrix, f32),
+            branch=Kept(matrix, bf16),
+        ),
         pulled_scratch,
-        after=(peer_in_0, peer_in_1),
+        after=(peer_in_0,),
         micros=10,
     )
-    token = attn_1.step(back_0.branch)
-    part_1 = weight_grads(
-        1, second, back_1, back_1, cotangent, peer_in_1, peer_cotangent, (token,), 0.1
-    )
-    ff_1 = Chain(ff_chain, part_1, ff_split[1])
-    part_0 = weight_grads(
-        0,
-        first,
-        first_ff,
-        back_0,
-        Kept(back_1.grad_next_low),
-        peer_in_0,
-        peer_grad_0,
-        (part_1.ff_send,),
-        4,
-    )
-    ff_0 = Chain(ff_chain, part_0, ff_split[0])
-    token = ff_1.step(part_0.ff_send)
-    token = attn_1.step(token)
-    token = ff_0.step(token)
+    ff_1 = Chain(ff_chain, back_1, 1)
+    token = ff_1.step(back_0.branch)
     back_attn_0 = run(
         functools.partial(
             attention_backward_body, sizes=sizes, piece_masks=attn_masks[0], heads=heads
@@ -933,7 +956,12 @@
             branch=Kept(back_0.branch),
             **attn_back_ins(first, start.x, start.a),
         ),
-        dict(**attn_back_outs, small=Kept(small_shape, f32), grad_next=(matrix, f32)),
+        dict(
+            attn_keep=Kept(attn_half, bf16),
+            attn_send=Kept((attn_count // 2 + 1, *attn_half[1:]), bf16),
+            small=Kept(small_shape, f32),
+            grad_next=(matrix, f32),
+        ),
         dict(
             bias_acc=pltpu.VMEM(bias_shape, f32),
             table_rows=pltpu.VMEM((bias_table.shape[0], heads * slots), f32),
@@ -942,21 +970,45 @@
         after=(token,),
         micros=7,
     )
-    attn_0 = Chain(attn_chain, back_attn_0, attn_split[0])
-    small = Chain(summing, back_attn_0.small, attn_hops[0])
-    token = back_attn_0.attn_send
+    attn_0 = Chain(attn_chain, back_attn_0, 0)
+    token = attn_1.step(back_attn_0.attn_send, peer_grad_0)
+    part_0 = run(
+        functools.partial(weight_body, piece_masks=place_masks[0]),
+        "layer_0_weight_grads",
+        dict(
+            place=place,
+            ff_in=Kept(first.ff_in),
+            grad=Kept(back_1.grad_next_low),
+            hidden=Kept(back_0.hidden),
+            grad_gate_up=Kept(back_0.grad_gate_up),
+            peer_in=Kept(peer_in_0),
+            peer_grad=Kept(peer_grad_0),
+            ff_gate_up=Kept(first_ff.ff_gate_up),
+            ff_down=Kept(first_ff.ff_down),
+        ),
+        dict(ff_keep=Kept(ff_half, bf16), ff_send=Kept(ff_half, bf16)),
+        dict(
+            peer_gate_up=pltpu.VMEM((rows, 2 * width), bf16),
+            peer_hidden=pltpu.VMEM(matrix, bf16),
+            ff_grad=pltpu.VMEM((width, 3 * width), f32),
+        ),
+        after=(token,),
+        micros=4,
+    )
+    ff_0 = Chain(ff_chain, part_0, 0)
+    token = part_0.ff_send
     shape = (2, width, width)
-    near_masks = ff_masks[0][: ff_count // 2]
-    far_masks = ff_masks[0][ff_count // 2 :]
+    near_masks = place_masks[0][: ff_count // 2]
+    far_masks = place_masks[0][ff_count // 2 :]
     done_1 = sums = attn_grads = None
     while True:
-        for chain in (ff_0, ff_1, attn_0, small, attn_1):
+        for chain in (ff_0, ff_1, attn_0, attn_1):
             token = chain.step(token)
-        if sums is None and small.arriving is None:
+        if sums is None and attn_0.arriving is None:
             sums = run(
                 small_body,
                 "small_sums",
-                dict(packed=Kept(tie(small.out["piece"], token))),
+                dict(packed=Kept(tie(attn_0.out["small"], token))),
                 dict(
                     gain_attn=((2, width), f32),
                     gain_ff=((2, width), f32),
@@ -971,7 +1023,7 @@
             token = attn_grads
         if done_1 is None and ff_1.arriving is None:
             pieces = tie(join(ff_1.out["near"], ff_1.out["far"]), token)
-            done_1 = finish(pieces, ff_masks[1], 1, place, shape)
+            done_1 = finish(pieces, place_masks[1], 1, place, shape)
             token = done_1[0]
         if ff_0.arriving is None:
             break

time: 176 us -> 188 us (1.068)
  local copies, waits for them, and re-layouts: 6.13 us -> 10.6 us
  starting transfers between devices: 42.5 us -> 46.6 us
  waiting for transfers between devices: 68.9 us -> 71 us
    unnamed x36 -> x52, local copies, waits for them, and re-layouts: 0.88 us -> 7.44 us
    ppermute x50 -> x44, starting transfers between devices: 42.5 us -> 46.6 us  [swap(): return lax.ppermute(array, axes, [(n, n ^ mask) for n in range(devices)])]
    ppermute x50 -> x44, waiting for transfers between devices: 68.9 us -> 71 us  [swap(): return lax.ppermute(array, axes, [(n, n ^ mask) for n in range(devices)])]
    dynamic_slice x2 -> x0, local copies, waits for them, and re-layouts: 2.05 us -> none  [on_device(): lax.dynamic_slice_in_dim(tie(w, packed), quarter_at * quarter, quarter, a...]
  transfers between devices with their start and end apart: 50 -> 44, of which waited for: 23 -> 18; matrix products, arithmetic and copies ran while one was open for 5% -> 5% of each run, Pallas kernels for 26% -> 22%
where the time goes in v6:
time: 188 us; the launch traced here: 187 us
  waiting for transfers between devices  71 us (38%)
  Pallas kernels  49.9 us (27%)
  starting transfers between devices  46.6 us (25%)
  local copies, waits for them, and re-layouts  10.6 us (6%)
  other arithmetic  7.28 us (4%)
    ppermute x44, waiting for transfers between devices, swap(): return lax.ppermute(array, axes, [(n, n ^ mask) for n in range(devices)])  71 us
    ppermute x44, starting transfers between devices, swap(): return lax.ppermute(array, axes, [(n, n ^ mask) for n in range(devices)])  46.6 us
    pallas_call x10, Pallas kernels, run(): pl.pallas_call(kernel, name=name, in_specs=[pl.BlockSpec(memory_space=in_...  44.4 us
    unnamed x52, local copies, waits for them, and re-layouts  7.44 us
    pallas_call x3, Pallas kernels, finish(): pl.pallas_call(kernel, name='layer_%d_ff_grads' % layer_idx, in_specs=[pl...  5.52 us
  transfers between devices with their start and end apart: 44, of which 18 were waited for; matrix products, arithmetic and copies ran while one was open for 5% of the time, Pallas kernels for 22%

profile of v6, /device:TPU:0, one launch (start us, length us, event | category | flops | bytes accessed | tf_op | source)
XLA Modules:
  0.0 187.0 jit_solution(11668026071186889704)
XLA Ops:
  1.5 3.0 %collective-permute-start.1 = (bf16[16,1536]{1,0:T(8,128)(2,1)S(1)}, bf16[16,1536]{1,0:T(8,128)(2,1)S(1)}, u32[]{:S(2)}, u32[]{:S(2)}) collective-permute-start(bf16[16,1536]{1,0:T(8,128)(2,1)S(1)} %get-tuple-element.292), channel_id=1, source_target_pairs={{0,1},{1,0},{2,3},{3,2},{4,5},{5,4},{6,7},{7,6},{8,9},{9,8},{10,11... | collective-permute-start | bytes 147464 | tf_op jit(solution)/shard_map/ppermute | solution.py:578
  4.5 2.6 %collective-permute-start = (bf16[16,1536]{1,0:T(8,128)(2,1)S(1)}, bf16[16,1536]{1,0:T(8,128)(2,1)S(1)}, u32[]{:S(2)}, u32[]{:S(2)}) collective-permute-start(bf16[16,1536]{1,0:T(8,128)(2,1)S(1)} %get-tuple-element.293), channel_id=1, source_target_pairs={{0,16},{1,17},{2,18},{3,19},{4,20},{5,21},{6,22},{7,23},{8,24},{9,... | collective-permute-start | bytes 147464 | tf_op jit(solution)/shard_map/ppermute | solution.py:578
  22.2 3.9 %collective-permute-done.3 = bf16[64,1536]{1,0:T(8,128)(2,1)S(1)} collective-permute-done((bf16[64,1536]{1,0:T(8,128)(2,1)S(1)}, bf16[64,1536]{1,0:T(8,128)(2,1)S(1)}, u32[]{:S(2)}, u32[]{:S(2)}) %collective-permute-start.3) | collective-permute-done | bytes 196640 | tf_op jit(solution)/shard_map/ppermute | solution.py:578
  26.4 3.4 %collective-permute-done.7 = bf16[64,1536]{1,0:T(8,128)(2,1)S(1)} collective-permute-done((bf16[64,1536]{1,0:T(8,128)(2,1)S(1)}, bf16[64,1536]{1,0:T(8,128)(2,1)S(1)}, u32[]{:S(2)}, u32[]{:S(2)}) %collective-permute-start.7) | collective-permute-done | bytes 196640 | tf_op jit(solution)/shard_map/ppermute | solution.py:578
  29.8 3.5 %collective-permute-done.5 = bf16[2,3,128,512]{3,2,1,0:T(8,128)(2,1)} collective-permute-done((bf16[2,3,128,512]{3,2,1,0:T(8,128)(2,1)S(1)}, bf16[2,3,128,512]{3,2,1,0:T(8,128)(2,1)}, u32[]{:S(2)}, u32[]{:S(2)}) %collective-permute-start.5) | collective-permute-done | bytes 786464 | tf_op jit(solution)/shard_map/ppermute | solution.py:578
  35.6 7.7 %collective-permute-done.8 = bf16[3,128,512]{2,1,0:T(8,128)(2,1)S(1)} collective-permute-done((bf16[3,128,512]{2,1,0:T(8,128)(2,1)S(1)}, bf16[3,128,512]{2,1,0:T(8,128)(2,1)S(1)}, u32[]{:S(2)}, u32[]{:S(2)}) %collective-permute-start.8) | collective-permute-done | bytes 393248 | tf_op jit(solution)/shard_map/ppermute | solution.py:578
  45.9 5.0 %layer_0_attention.1 = (bf16[512,1536]{1,0:T(8,128)(2,1)S(1)}, bf16[512,1152]{1,0:T(8,128)(2,1)S(1)}, f32[512,384]{1,0:T(8,128)S(1)}, bf16[512,384]{1,0:T(8,128)...) custom-call(s32[4]{0:T(128)S(1)} %pad_add_fusion.1.refs_0_.place_ref, ...), custom_call_target="tpu_custom_call" | custom-call | flops 11500000256 | tf_op jit(solution)/shard_map/layer_0_attention/pallas_call | solution.py:98
  51.0 3.9 %layer_0_ff.1 = (bf16[2,512,1024]{2,1,0:T(8,128)(2,1)S(1)}, bf16[2,512,512]{2,1,0:T(8,128)(2,1)S(1)}, f32[512,512]{1,0:T(8,128)S(1)}, bf16[512,512]{1,0:T(8,128)(2,1)S(1)}) custom-call(s32[4]{0:T(128)S(1)} %pad_add_fusion.1.refs_0_.place_ref, f32[512,512]{1,0:T(8,128)S(1)} %get-tuple-element.125.refs_1_.refs_3_, ...), custom_call_target="tpu_custom_call" | custom-call | flops 115000000 | tf_op jit(solution)/shard_map/layer_0_ff/pallas_call | solution.py:98
  56.3 5.0 %layer_1_attention.1 = (bf16[512,1536]{1,0:T(8,128)(2,1)S(1)}, bf16[512,1152]{1,0:T(8,128)(2,1)S(1)}, f32[512,384]{1,0:T(8,128)S(1)}, bf16[512,384]{1,0:T(8,128)...) custom-call(s32[4]{0:T(128)S(1)} %pad_add_fusion.1.refs_0_.place_ref, ...), custom_call_target="tpu_custom_call" | custom-call | flops 115000000 | tf_op jit(solution)/shard_map/layer_1_attention/pallas_call | solution.py:98
  61.3 12.5 %layer_1_backward.1 = (bf16[16,32,1536]{2,1,0:T(8,128)(2,1)S(1)}, bf16[16,32,1536]{2,1,0:T(8,128)(2,1)S(1)}, f32[8,1536]{1,0:T(8,128)S(1)}, bf16[16,16,1536]{2,1...) custom-call(s32[4]{0:T(128)S(1)} %pad_add_fusion.1.refs_0_.place_ref, ...), custom_call_target="tpu_custom_call" | custom-call | flops 11500000256 | tf_op jit(solution)/shard_map/layer_1_backward/pallas_call | solution.py:98
  75.7 4.6 %layer_0_ff_backward.1 = (bf16[1,512,512]{2,1,0:T(8,128)(2,1)S(1)}, bf16[1,512,1024]{2,1,0:T(8,128)(2,1)S(1)}, f32[8,1536]{1,0:T(8,128)S(1)}, f32[512,512]{1,0:T(8,128)S(1)}, bf16[512,512]{1,0:T(8,128)(2,1)S(1)}) custom-call(f32[512,512]{1,0:T(8,128)S(1)} %get-tuple-element.142.refs_0_, f32[2,512]{1,0:T(2,128)S(1)} %copy-done.6, ...), custom_call_target="tpu_custom_call" | custom-call | flops 11500000256 | tf_op jit(solution)/shard_map/layer_0_ff_backward/pallas_call | solution.py:98
  81.6 6.3 %layer_0_attention_backward.1 = (bf16[16,16,1536]{2,1,0:T(8,128)(2,1)S(1)}, bf16[17,16,1536]{2,1,0:T(8,128)(2,1)S(1)}, f32[8,1536]{1,0:T(8,128)S(1)}, f32[512,512]{1,0:T(8,128)}) custom-call(s32[4]{0:T(128)S(1)} %pad_add_fusion.1.refs_0_.place_ref, f32[64,384]{1,0:T(8,128)S(1)} %get-tuple-element.141.refs_1_, s32[512,2]{1,0:T(8,128)S(1)} %copy.45.refs_1_.refs_2_, ...), custom_call_target="tpu_custom_call" | custom-call | flops 8049999872 | tf_op jit(solution)/shard_map/layer_0_attention_backward/pallas_call | solution.py:98
  88.7 3.8 %layer_0_weight_grads.1 = (bf16[8,32,1536]{2,1,0:T(8,128)(2,1)S(1)}, bf16[8,32,1536]{2,1,0:T(8,128)(2,1)S(1)}) custom-call(s32[4]{0:T(128)S(1)} %pad_add_fusion.1.refs_0_.place_ref, bf16[512,512]{1,0:T(8,128)(2,1)S(1)} %get-tuple-element.126.refs_2_.refs_4_.refs_1_, bf16[512,512]{1,0:T(8,128)(2,1)S(1)} %get-tuple-element.159.refs_2_, ...), custom_call_target="tpu_custom_call" | custom-call | flops 4600000000 | tf_op jit(solution)/shard_map/layer_0_weight_grads/pallas_call | solution.py:98
  97.5 15.1 %collective-permute-done.18 = bf16[8,32,1536]{2,1,0:T(8,128)(2,1)S(1)} collective-permute-done((bf16[8,32,1536]{2,1,0:T(8,128)(2,1)S(1)}, bf16[8,32,1536]{2,1,0:T(8,128)(2,1)S(1)}, u32[]{:S(2)}, u32[]{:S(2)}) %collective-permute-start.18) | collective-permute-done | bytes 786464 | tf_op jit(solution)/shard_map/ppermute | solution.py:578
  116.8 2.7 %collective-permute-start.28 = (bf16[2,32,1536]{2,1,0:T(8,128)(2,1)S(1)}, bf16[2,32,1536]{2,1,0:T(8,128)(2,1)S(1)}, u32[]{:S(2)}, u32[]{:S(2)}) collective-permute-start(bf16[2,32,1536]{2,1,0:T(8,128)(2,1)S(1)} %get-tuple-element.277), channel_id=1, source_target_pairs={{0,16},{1,17},{2,18},{3,19},{4,20},{5,21},{6,22},{7,23},{8,24},{9,... | collective-permute-start | bytes 589832 | tf_op jit(solution)/shard_map/ppermute | solution.py:578
  119.5 5.4 %collective-permute-done.23 = bf16[4,32,1536]{2,1,0:T(8,128)(2,1)S(1)} collective-permute-done((bf16[4,32,1536]{2,1,0:T(8,128)(2,1)S(1)}, bf16[4,32,1536]{2,1,0:T(8,128)(2,1)S(1)}, u32[]{:S(2)}, u32[]{:S(2)}) %collective-permute-start.23) | collective-permute-done | bytes 393248 | tf_op jit(solution)/shard_map/ppermute | solution.py:578
  126.4 6.6 %collective-permute-done.22 = bf16[9,16,1536]{2,1,0:T(8,128)(2,1)S(1)} collective-permute-done((bf16[9,16,1536]{2,1,0:T(8,128)(2,1)S(1)}, bf16[9,16,1536]{2,1,0:T(8,128)(2,1)S(1)}, u32[]{:S(2)}, u32[]{:S(2)}) %collective-permute-start.22) | collective-permute-done | bytes 442400 | tf_op jit(solution)/shard_map/ppermute | solution.py:578
  136.9 2.6 %collective-permute-start.31 = (bf16[1,32,1536]{2,1,0:T(8,128)(2,1)S(1)}, bf16[1,32,1536]{2,1,0:T(8,128)(2,1)S(1)}, u32[]{:S(2)}, u32[]{:S(2)}) collective-permute-start(bf16[1,32,1536]{2,1,0:T(8,128)(2,1)S(1)} %add_convert_fusion.25), channel_id=1, source_target_pairs={{0,16},{1,17},{2,18},{3,19},{4,20},{5,21},{6,22},{7,23},{8,24},{9,... | collective-permute-start | bytes 294920 | tf_op jit(solution)/shard_map/ppermute | solution.py:578
  142.5 2.6 %collective-permute-start.37 = (bf16[1,16,1536]{2,1,0:T(8,128)(2,1)S(1)}, bf16[1,16,1536]{2,1,0:T(8,128)(2,1)S(1)}, u32[]{:S(2)}, u32[]{:S(2)}) collective-permute-start(bf16[1,16,1536]{2,1,0:T(8,128)(2,1)S(1)} %add_convert_fusion.33), channel_id=1, source_target_pairs={{0,16},{1,17},{2,18},{3,19},{4,20},{5,21},{6,22},{7,23},{8,24},{9,... | collective-permute-start | bytes 147464 | tf_op jit(solution)/shard_map/ppermute | solution.py:578
  147.3 3.0 %collective-permute-start.34 = (bf16[2,16,1536]{2,1,0:T(8,128)(2,1)S(1)}, bf16[2,16,1536]{2,1,0:T(8,128)(2,1)S(1)}, u32[]{:S(2)}, u32[]{:S(2)}) collective-permute-start(bf16[2,16,1536]{2,1,0:T(8,128)(2,1)S(1)} %maximum_maximum_fusion.3), channel_id=1, source_target_pairs={{0,16},{1,17},{2,18},{3,19},{4,20},{5,21},{6,22},{7,23},{8,24},{9,... | collective-permute-start | bytes 294920 | tf_op jit(solution)/shard_map/ppermute | solution.py:578
  151.1 5.7 %collective-permute-done.35 = bf16[1,32,1536]{2,1,0:T(8,128)(2,1)S(1)} collective-permute-done((bf16[1,32,1536]{2,1,0:T(8,128)(2,1)S(1)}, bf16[1,32,1536]{2,1,0:T(8,128)(2,1)S(1)}, u32[]{:S(2)}, u32[]{:S(2)}) %collective-permute-start.35) | collective-permute-done | bytes 98336 | tf_op jit(solution)/shard_map/ppermute | solution.py:578
  157.0 4.2 %collective-permute-done.34 = bf16[2,16,1536]{2,1,0:T(8,128)(2,1)S(1)} collective-permute-done((bf16[2,16,1536]{2,1,0:T(8,128)(2,1)S(1)}, bf16[2,16,1536]{2,1,0:T(8,128)(2,1)S(1)}, u32[]{:S(2)}, u32[]{:S(2)}) %collective-permute-start.34) | collective-permute-done | bytes 98336 | tf_op jit(solution)/shard_map/ppermute | solution.py:578
  161.8 2.4 %collective-permute-done.38 = bf16[2,32,1536]{2,1,0:T(8,128)(2,1)S(1)} collective-permute-done((bf16[2,32,1536]{2,1,0:T(8,128)(2,1)S(1)}, bf16[2,32,1536]{2,1,0:T(8,128)(2,1)S(1)}, u32[]{:S(2)}, u32[]{:S(2)}) %collective-permute-start.38) | collective-permute-done | bytes 196640 | tf_op jit(solution)/shard_map/ppermute | solution.py:578
  167.9 6.6 %collective-permute-done.39 = bf16[4,32,1536]{2,1,0:T(8,128)(2,1)S(1)} collective-permute-done((bf16[4,32,1536]{2,1,0:T(8,128)(2,1)S(1)}, bf16[4,32,1536]{2,1,0:T(8,128)(2,1)S(1)}, u32[]{:S(2)}, u32[]{:S(2)}) %collective-permute-start.39) | collective-permute-done | bytes 393248 | tf_op jit(solution)/shard_map/ppermute | solution.py:578
  (198 shorter events, 63.2 us)
Async XLA Ops:
  1.5 11.0 %collective-permute-start.1 = (bf16[16,1536]{1,0:T(8,128)(2,1)S(1)}, bf16[16,1536]{1,0:T(8,128)(2,1)S(1)}, u32[]{:S(2)}, u32[]{:S(2)}) collective-permute-start(bf16[16,1536]{1,0:T(8,128)(2,1)S(1)} %get-tuple-element.292), channel_id=1, source_target_pairs={{0,1},{1,0},{2,3},{3,2},{4,5},{5,4},{6,7},{7,6},{8,9},{9,8},{10,11... | collective-permute-start | bytes 147464 | tf_op jit(solution)/shard_map/ppermute | solution.py:578
  4.5 9.0 %collective-permute-start = (bf16[16,1536]{1,0:T(8,128)(2,1)S(1)}, bf16[16,1536]{1,0:T(8,128)(2,1)S(1)}, u32[]{:S(2)}, u32[]{:S(2)}) collective-permute-start(bf16[16,1536]{1,0:T(8,128)(2,1)S(1)} %get-tuple-element.293), channel_id=1, source_target_pairs={{0,16},{1,17},{2,18},{3,19},{4,20},{5,21},{6,22},{7,23},{8,24},{9,... | collective-permute-start | bytes 147464 | tf_op jit(solution)/shard_map/ppermute | solution.py:578
  15.1 18.3 %collective-permute-start.5 = (bf16[2,3,128,512]{3,2,1,0:T(8,128)(2,1)S(1)}, bf16[2,3,128,512]{3,2,1,0:T(8,128)(2,1)}, u32[]{:S(2)}, u32[]{:S(2)}) collective-permute-start(bf16[2,3,128,512]{3,2,1,0:T(8,128)(2,1)S(1)} %cut_quarters.1), channel_id=1, source_target_pairs={{0,1},{1,0},{2,3},{3,2},{4,5},{5,4},{6,7},{7,6},{8,9},{9,8},{10,11... | collective-permute-start | bytes 2359304 | tf_op jit(solution)/shard_map/ppermute | solution.py:578
  26.1 9.6 %collective-permute-start.4 = (bf16[128,1536]{1,0:T(8,128)(2,1)S(1)}, bf16[128,1536]{1,0:T(8,128)(2,1)S(1)}, u32[]{:S(2)}, u32[]{:S(2)}) collective-permute-start(bf16[128,1536]{1,0:T(8,128)(2,1)S(1)} %pad_maximum_fusion.3), channel_id=1, source_target_pairs={{0,8},{1,9},{2,10},{3,11},{4,12},{5,13},{6,14},{7,15},{8,0},{9,1},... | collective-permute-start | bytes 1179656 | tf_op jit(solution)/shard_map/ppermute | solution.py:578
  34.5 8.9 %collective-permute-start.8 = (bf16[3,128,512]{2,1,0:T(8,128)(2,1)S(1)}, bf16[3,128,512]{2,1,0:T(8,128)(2,1)S(1)}, u32[]{:S(2)}, u32[]{:S(2)}) collective-permute-start(bf16[3,128,512]{2,1,0:T(8,128)(2,1)S(1)} %get-tuple-element.123), channel_id=1, source_target_pairs={{0,4},{1,5},{2,6},{3,7},{4,0},{5,1},{6,2},{7,3},{8,12},{9,13},{10,... | collective-permute-start | bytes 1179656 | tf_op jit(solution)/shard_map/ppermute | solution.py:578
  44.2 11.1 %collective-permute-start.13 = (bf16[3,128,512]{2,1,0:T(8,128)(2,1)S(1)}, bf16[3,128,512]{2,1,0:T(8,128)(2,1)S(1)}, u32[]{:S(2)}, u32[]{:S(2)}) collective-permute-start(bf16[3,128,512]{2,1,0:T(8,128)(2,1)S(1)} %get-tuple-element.134), channel_id=1, source_target_pairs={{0,4},{1,5},{2,6},{3,7},{4,0},{5,1},{6,2},{7,3},{8,12},{9,13},{10,... | collective-permute-start | bytes 1179656 | tf_op jit(solution)/shard_map/ppermute | solution.py:578
  55.5 20.2 %collective-permute-start.15 = (bf16[512,512]{1,0:T(8,128)(2,1)S(1)}, bf16[512,512]{1,0:T(8,128)(2,1)S(1)}, u32[]{:S(2)}, u32[]{:S(2)}) collective-permute-start(bf16[512,512]{1,0:T(8,128)(2,1)S(1)} %get-tuple-element.126.refs_2_.refs_4_.refs_1_), channel_id=1, source_target_pairs={{0,1},{1,0},{2,3},{3,2},{4,5},{5,4},{6,7},{7,6},{8,9},{9,8},{10,11... | collective-permute-start | bytes 1572872 | tf_op jit(solution)/shard_map/ppermute | solution.py:578
  74.1 14.3 %collective-permute-start.20 = (bf16[16,16,1536]{2,1,0:T(8,128)(2,1)S(1)}, bf16[16,16,1536]{2,1,0:T(8,128)(2,1)S(1)}, u32[]{:S(2)}, u32[]{:S(2)}) collective-permute-start(bf16[16,16,1536]{2,1,0:T(8,128)(2,1)S(1)} %get-tuple-element.163), channel_id=1, source_target_pairs={{0,2},{1,3},{2,0},{3,1},{4,6},{5,7},{6,4},{7,5},{8,10},{9,11},{10,... | collective-permute-start | bytes 2359304 | tf_op jit(solution)/shard_map/ppermute | solution.py:578
  74.4 14.0 %collective-permute-start.19 = (bf16[512,512]{1,0:T(8,128)(2,1)S(1)}, bf16[512,512]{1,0:T(8,128)(2,1)S(1)}, u32[]{:S(2)}, u32[]{:S(2)}) collective-permute-start(bf16[512,512]{1,0:T(8,128)(2,1)S(1)} %get-tuple-element.159.refs_2_), channel_id=1, source_target_pairs={{0,1},{1,0},{2,3},{3,2},{4,5},{5,4},{6,7},{7,6},{8,9},{9,8},{10,11... | collective-permute-start | bytes 1572872 | tf_op jit(solution)/shard_map/ppermute | solution.py:578
  92.6 20.0 %collective-permute-start.18 = (bf16[8,32,1536]{2,1,0:T(8,128)(2,1)S(1)}, bf16[8,32,1536]{2,1,0:T(8,128)(2,1)S(1)}, u32[]{:S(2)}, u32[]{:S(2)}) collective-permute-start(bf16[8,32,1536]{2,1,0:T(8,128)(2,1)S(1)} %get-tuple-element.263.refs_14_), channel_id=1, source_target_pairs={{0,4},{1,5},{2,6},{3,7},{4,0},{5,1},{6,2},{7,3},{8,12},{9,13},{10,... | collective-permute-start | bytes 2359304 | tf_op jit(solution)/shard_map/ppermute | solution.py:578
  93.9 20.1 %collective-permute-start.17 = (bf16[17,16,1536]{2,1,0:T(8,128)(2,1)S(1)}, bf16[17,16,1536]{2,1,0:T(8,128)(2,1)S(1)}, u32[]{:S(2)}, u32[]{:S(2)}) collective-permute-start(bf16[17,16,1536]{2,1,0:T(8,128)(2,1)S(1)} %get-tuple-element.158), channel_id=1, source_target_pairs={{0,2},{1,3},{2,0},{3,1},{4,6},{5,7},{6,4},{7,5},{8,10},{9,11},{10,... | collective-permute-start | bytes 2506760 | tf_op jit(solution)/shard_map/ppermute | solution.py:578
  94.1 21.1 %collective-permute-start.25 = (bf16[8,16,1536]{2,1,0:T(8,128)(2,1)S(1)}, bf16[8,16,1536]{2,1,0:T(8,128)(2,1)S(1)}, u32[]{:S(2)}, u32[]{:S(2)}) collective-permute-start(bf16[8,16,1536]{2,1,0:T(8,128)(2,1)S(1)} %get-tuple-element.267.refs_9_), channel_id=1, source_target_pairs={{0,1},{1,0},{2,3},{3,2},{4,5},{5,4},{6,7},{7,6},{8,9},{9,8},{10,11... | collective-permute-start | bytes 1179656 | tf_op jit(solution)/shard_map/ppermute | solution.py:578
  95.9 20.8 %collective-permute-start.24 = (bf16[4,32,1536]{2,1,0:T(8,128)(2,1)S(1)}, bf16[4,32,1536]{2,1,0:T(8,128)(2,1)S(1)}, u32[]{:S(2)}, u32[]{:S(2)}) collective-permute-start(bf16[4,32,1536]{2,1,0:T(8,128)(2,1)S(1)} %get-tuple-element.269), channel_id=1, source_target_pairs={{0,8},{1,9},{2,10},{3,11},{4,12},{5,13},{6,14},{7,15},{8,0},{9,1},... | collective-permute-start | bytes 1179656 | tf_op jit(solution)/shard_map/ppermute | solution.py:578
  112.8 12.1 %collective-permute-start.23 = (bf16[4,32,1536]{2,1,0:T(8,128)(2,1)S(1)}, bf16[4,32,1536]{2,1,0:T(8,128)(2,1)S(1)}, u32[]{:S(2)}, u32[]{:S(2)}) collective-permute-start(bf16[4,32,1536]{2,1,0:T(8,128)(2,1)S(1)} %get-tuple-element.271), channel_id=1, source_target_pairs={{0,1},{1,0},{2,3},{3,2},{4,5},{5,4},{6,7},{7,6},{8,9},{9,8},{10,11... | collective-permute-start | bytes 1179656 | tf_op jit(solution)/shard_map/ppermute | solution.py:578
  114.4 18.6 %collective-permute-start.22 = (bf16[9,16,1536]{2,1,0:T(8,128)(2,1)S(1)}, bf16[9,16,1536]{2,1,0:T(8,128)(2,1)S(1)}, u32[]{:S(2)}, u32[]{:S(2)}) collective-permute-start(bf16[9,16,1536]{2,1,0:T(8,128)(2,1)S(1)} %maximum_maximum_fusion), channel_id=1, source_target_pairs={{0,1},{1,0},{2,3},{3,2},{4,5},{5,4},{6,7},{7,6},{8,9},{9,8},{10,11... | collective-permute-start | bytes 1327112 | tf_op jit(solution)/shard_map/ppermute | solution.py:578
  115.3 19.2 %collective-permute-start.29 = (bf16[4,16,1536]{2,1,0:T(8,128)(2,1)S(1)}, bf16[4,16,1536]{2,1,0:T(8,128)(2,1)S(1)}, u32[]{:S(2)}, u32[]{:S(2)}) collective-permute-start(bf16[4,16,1536]{2,1,0:T(8,128)(2,1)S(1)} %get-tuple-element.275), channel_id=1, source_target_pairs={{0,4},{1,5},{2,6},{3,7},{4,0},{5,1},{6,2},{7,3},{8,12},{9,13},{10,... | collective-permute-start | bytes 589832 | tf_op jit(solution)/shard_map/ppermute | solution.py:578
  116.8 19.4 %collective-permute-start.28 = (bf16[2,32,1536]{2,1,0:T(8,128)(2,1)S(1)}, bf16[2,32,1536]{2,1,0:T(8,128)(2,1)S(1)}, u32[]{:S(2)}, u32[]{:S(2)}) collective-permute-start(bf16[2,32,1536]{2,1,0:T(8,128)(2,1)S(1)} %get-tuple-element.277), channel_id=1, source_target_pairs={{0,16},{1,17},{2,18},{3,19},{4,20},{5,21},{6,22},{7,23},{8,24},{9,... | collective-permute-start | bytes 589832 | tf_op jit(solution)/shard_map/ppermute | solution.py:578
  124.9 11.9 %collective-permute-start.27 = (bf16[2,32,1536]{2,1,0:T(8,128)(2,1)S(1)}, bf16[2,32,1536]{2,1,0:T(8,128)(2,1)S(1)}, u32[]{:S(2)}, u32[]{:S(2)}) collective-permute-start(bf16[2,32,1536]{2,1,0:T(8,128)(2,1)S(1)} %get-tuple-element.279), channel_id=1, source_target_pairs={{0,8},{1,9},{2,10},{3,11},{4,12},{5,13},{6,14},{7,15},{8,0},{9,1},... | collective-permute-start | bytes 589832 | tf_op jit(solution)/shard_map/ppermute | solution.py:578
  136.9 9.9 %collective-permute-start.31 = (bf16[1,32,1536]{2,1,0:T(8,128)(2,1)S(1)}, bf16[1,32,1536]{2,1,0:T(8,128)(2,1)S(1)}, u32[]{:S(2)}, u32[]{:S(2)}) collective-permute-start(bf16[1,32,1536]{2,1,0:T(8,128)(2,1)S(1)} %add_convert_fusion.25), channel_id=1, source_target_pairs={{0,16},{1,17},{2,18},{3,19},{4,20},{5,21},{6,22},{7,23},{8,24},{9,... | collective-permute-start | bytes 294920 | tf_op jit(solution)/shard_map/ppermute | solution.py:578
  146.8 10.0 %collective-permute-start.35 = (bf16[1,32,1536]{2,1,0:T(8,128)(2,1)S(1)}, bf16[1,32,1536]{2,1,0:T(8,128)(2,1)S(1)}, u32[]{:S(2)}, u32[]{:S(2)}) collective-permute-start(bf16[1,32,1536]{2,1,0:T(8,128)(2,1)S(1)} %get-tuple-element.249), channel_id=1, source_target_pairs={{0,16},{1,17},{2,18},{3,19},{4,20},{5,21},{6,22},{7,23},{8,24},{9,... | collective-permute-start | bytes 294920 | tf_op jit(solution)/shard_map/ppermute | solution.py:578
  147.3 13.8 %collective-permute-start.34 = (bf16[2,16,1536]{2,1,0:T(8,128)(2,1)S(1)}, bf16[2,16,1536]{2,1,0:T(8,128)(2,1)S(1)}, u32[]{:S(2)}, u32[]{:S(2)}) collective-permute-start(bf16[2,16,1536]{2,1,0:T(8,128)(2,1)S(1)} %maximum_maximum_fusion.3), channel_id=1, source_target_pairs={{0,16},{1,17},{2,18},{3,19},{4,20},{5,21},{6,22},{7,23},{8,24},{9,... | collective-permute-start | bytes 294920 | tf_op jit(solution)/shard_map/ppermute | solution.py:578
  150.4 13.9 %collective-permute-start.38 = (bf16[2,32,1536]{2,1,0:T(8,128)(2,1)S(1)}, bf16[2,32,1536]{2,1,0:T(8,128)(2,1)S(1)}, u32[]{:S(2)}, u32[]{:S(2)}) collective-permute-start(bf16[2,32,1536]{2,1,0:T(8,128)(2,1)S(1)} %pad_maximum_fusion.10), channel_id=1, source_target_pairs={{0,16},{1,17},{2,18},{3,19},{4,20},{5,21},{6,22},{7,23},{8,24},{9,... | collective-permute-start | bytes 589832 | tf_op jit(solution)/shard_map/ppermute | solution.py:578
  156.9 9.5 %collective-permute-start.40 = (bf16[2,32,1536]{2,1,0:T(8,128)(2,1)S(1)}, bf16[2,32,1536]{2,1,0:T(8,128)(2,1)S(1)}, u32[]{:S(2)}, u32[]{:S(2)}) collective-permute-start(bf16[2,32,1536]{2,1,0:T(8,128)(2,1)S(1)} %pad_maximum_fusion.11), channel_id=1, source_target_pairs={{0,8},{1,9},{2,10},{3,11},{4,12},{5,13},{6,14},{7,15},{8,0},{9,1},... | collective-permute-start | bytes 589832 | tf_op jit(solution)/shard_map/ppermute | solution.py:578
  164.3 10.3 %collective-permute-start.39 = (bf16[4,32,1536]{2,1,0:T(8,128)(2,1)S(1)}, bf16[4,32,1536]{2,1,0:T(8,128)(2,1)S(1)}, u32[]{:S(2)}, u32[]{:S(2)}) collective-permute-start(bf16[4,32,1536]{2,1,0:T(8,128)(2,1)S(1)} %pad_maximum_fusion.5), channel_id=1, source_target_pairs={{0,8},{1,9},{2,10},{3,11},{4,12},{5,13},{6,14},{7,15},{8,0},{9,1},... | collective-permute-start | bytes 1179656 | tf_op jit(solution)/shard_map/ppermute | solution.py:578
  (40 other events, 197.6 us)

commit v7 on v6

--- a/solution.py
+++ b/solution.py
@@ -409,12 +409,16 @@
     for half in range(2):
         r.ff_grad[half, :, : 2 * width] = dot_tn(r.ff_in[...], r.grad_gate_up[half])
         r.ff_grad[half, :, 2 * width :] = dot_tn(r.hidden[half], r.grad[...])
-    count = len(ff_masks)
-    grain = r.ff_keep.shape[1]
-    for idx, mask in enumerate(ff_masks):
-        target = r.ff_keep if idx < count // 2 else r.ff_send
-        rows = pl.ds(pl.multiple_of((r.place[3] ^ (mask // 2)) * grain, grain), grain)
-        target[idx % (count // 2)] = r.ff_grad[mask % 2, rows, :].astype(bf16)
+    half_count = len(ff_masks[0]) // 2
+    grain, columns = r.ff_keep.shape[1:]
+    for side, side_masks in enumerate(ff_masks):
+        lanes = slice(side * columns, (side + 1) * columns)
+        for idx, mask in enumerate(side_masks):
+            target = r.ff_keep if idx < half_count else r.ff_send
+            rows = pl.ds(pl.multiple_of((r.place[3] ^ (mask // 2)) * grain, grain), grain)
+            target[side * half_count + idx % half_count] = r.ff_grad[mask % 2, rows, lanes].astype(
+                bf16
+            )
     put_row(r.small, 1, attention_backward(r, sizes, 1, True, piece_masks, heads))
     r.drain("outputs")
 
@@ -510,27 +514,27 @@
 
 def small_body(r):
     width = r.embed.shape[1]
-    heads = r.table.shape[1]
+    heads = r.table.shape[0]
     outs = ((r.gain_attn, 0), (r.gain_attn, 1), (r.gain_ff, 0), (r.gain_ff, 1), (r.embed, 0))
     for which, (out, row) in enumerate(outs):
         first = r.packed.shape[0] - 2 + which // 3
         at = which % 3 * width
         out[row : row + 1, :] = r.packed[first : first + 1, at : at + width]
-    r.table[...] = jnp.transpose(r.packed[:, :128])[: r.table.shape[0], :heads]
+    r.table[...] = r.packed[:heads, : r.table.shape[1]]
     r.write("gain_attn", "gain_ff", "embed", "table")
     r.drain("gain_attn", "gain_ff", "embed", "table")
 
 
 def cut_body(r):
-    rows = r.quarters.shape[2]
+    rows = r.quarter_0.shape[1]
     at = pl.ds(pl.multiple_of(r.place[1] * rows, rows), rows)
-    copies = [
-        pltpu.make_async_copy(w.at[layer_idx, at], r.quarters.at[layer_idx, k], r.cut_sem)
-        for layer_idx in range(2)
+    outs = (r.quarter_0, r.quarter_1)
+    start_all(
+        pltpu.make_async_copy(w.at[layer_idx, at], out.at[k], r.cut_sem)
+        for layer_idx, out in enumerate(outs)
         for k, w in enumerate((r.w_gate, r.w_up, r.w_down))
-    ]
-    start_all(copies)
-    wait_all(r.cut_sem, r.quarters)
+    )
+    wait_all(r.cut_sem, *outs)
 
 
 def order_masks(hops):
@@ -598,13 +602,20 @@
 
     quarter = width // 4
     packed = jnp.concatenate([w_query, w_key, w_value, jnp.swapaxes(w_output, 1, 2)], axis=2)
+    in_hbm = {
+        name: pltpu.with_memory_space_constraint(w, pltpu.HBM)
+        for name, w in (("w_gate", w_gate), ("w_up", w_up), ("w_down", w_down))
+    }
     ff_blocks = run(
         cut_body,
         "cut_quarters",
-        dict(place=place, w_gate=w_gate, w_up=w_up, w_down=w_down),
-        dict(quarters=Kept((2, 3, quarter, width), bf16)),
+        dict(place=place, **in_hbm),
+        dict(
+            quarter_0=Kept((3, quarter, width), bf16),
+            quarter_1=Kept((3, quarter, width), bf16),
+        ),
         dict(cut_sem=pltpu.SemaphoreType.DMA),
-    ).quarters
+    )
     own_rows = packed.shape[1]
     direct = own_rows % 16 == 0
     far = bits[2:]
@@ -644,7 +655,9 @@
         block_0, block_1 = packed[0], packed[1]
         got_1 = swap(block_1, hops_1[0])
         got_0 = swap(block_0, hops_0[0])
-        ff_quarter = swap(tie(ff_blocks, got_0), 1)
+        ff_0 = swap(tie(ff_blocks.quarter_0, got_0), 1)
+        got_ff_0 = swap(ff_0, 4)
+        ff_1 = swap(tie(ff_blocks.quarter_1, ff_0), 1)
         block_0 = join(block_0, got_0)
         block_1 = join(block_1, tie(got_1, block_0))
         for hop_0, hop_1 in zip(hops_0[1:-2], hops_1[1:-2]):
@@ -655,12 +668,10 @@
             block_1 = join(block_1, tie(got_1, block_0))
         got_0 = swap(block_0, hops_0[-2])
         got_1 = swap(block_1, hops_1[-2])
-        ff_0 = tie(ff_quarter[0], block_1)
-        got_ff_0 = swap(ff_0, 4)
         block_0 = join(block_0, tie(got_0, start.a, got_ff_0))
         block_1 = join(block_1, tie(got_1, block_0))
         ff_0 = join(ff_0, tie(got_ff_0, block_1))
-        got_ff_1 = swap(tie(ff_quarter[1], ff_0), 4)
+        got_ff_1 = swap(tie(ff_1, ff_0), 4)
         far_0 = swap(block_0, 2)
         attn_pieces = [
             (block_0, far_0, order_masks(hops_0[::-1])),
@@ -668,8 +679,8 @@
         ]
         after_first = (attn_pieces[1][1],)
     else:
-        ff_quarter = swap(ff_blocks, 1)
-        ff_0 = join(ff_quarter[0], swap(ff_quarter[0], 4))
+        ff_0, ff_1 = swap(ff_blocks.quarter_0, 1), swap(ff_blocks.quarter_1, 1)
+        ff_0 = join(ff_0, swap(ff_0, 4))
         start, wide_buckets, marks = prepare(packed)
         whole = lax.all_gather(packed[0], axes, axis=0, tiled=True)
         attn_pieces = [(whole, whole, [0])]
@@ -741,9 +752,9 @@
         micros=0.1,
     )
     if direct:
-        ff_1 = join(ff_quarter[1], tie(got_ff_1, first_ff.a_next))
+        ff_1 = join(ff_1, tie(got_ff_1, first_ff.a_next))
     else:
-        ff_1 = join(ff_quarter[1], swap(ff_quarter[1], 4))
+        ff_1 = join(ff_1, swap(ff_1, 4))
     ff_pieces.append((ff_1, swap(ff_1, 2)))
     second = attention(1, first_ff.x_next, first_ff.a_next, micros=0.1)
 
@@ -752,12 +763,12 @@
     attn_split = [[hop for hop in hops if hop >= attn_low] for hops in attn_hops]
     attn_whole = [hop for hop in bits if hop < attn_low]
     attn_masks = [[mask // attn_low for mask in order_masks(hops)] for hops in attn_split]
-    ff_hops = ([2] + bits[3:] + bits[2:3], [2] + bits[2:3] + [1] + bits[3:])
+    ff_hops = (bits[1:], [2, 4, 1] + bits[3:], [2, 1, 4] + bits[3:])
     ff_split = [[hop for hop in hops if hop // 2 < ff_count] for hops in ff_hops]
     ff_whole = [hop for hop in bits[1:] if hop // 2 >= ff_count]
-    ff_share = [[hop for hop in hops if hop > 1] for hops in ff_split]
+    ff_share = ff_split[0][::-1]
     ff_masks = [order_masks(hops) for hops in ff_split]
-    place_masks = [[mask // 2 for mask in order_masks(hops)] for hops in ff_share]
+    place_masks = [mask // 2 for mask in ff_masks[0]]
     attn_half = (attn_count // 2, attn_grain, 4 * inner)
     ff_half = (ff_count // 2, ff_grain, 3 * width)
     small_shape = (heads + 2, 3 * width)
@@ -807,12 +818,13 @@
 
     def sharing(piece, hops, out):
         for step, hop in enumerate(hops):
+            if step + 1 == len(hops):
+                out["near"] = piece
             got = yield swap(piece, hop)
             if step + 1 < len(hops):
                 out["token"] = piece = join(piece, got)
             else:
-                out["token"] = got
-        out["near"], out["far"] = piece, got
+                out["token"] = out["far"] = got
 
     def rounded(values):
         return lax.reduce_precision(values, exponent_bits=8, mantissa_bits=7)
@@ -852,10 +864,31 @@
         out["done"] = piece.astype(f32)
         out["small"] = small
 
-    def ff_chain(part, layer_idx, out):
-        yield from halving(part.ff_keep, part.ff_send, ff_split[layer_idx], out)
+    def first_ff_chain(part, out):
+        yield from halving(part.ff_keep, part.ff_send, ff_split[0], out)
         yield from summing(out["piece"], ff_whole, out)
-        yield from sharing(out["piece"], ff_share[layer_idx][::-1], out)
+        yield from sharing(out["piece"], ff_share, out)
+
+    def second_ff_chain(part, out):
+        got = yield swap(part.ff_send, 2)
+        count = ff_count
+        keeps, sends = [], []
+        for side in range(2):
+            at, half = side * count, count // 2
+            sends.append(add(part.ff_keep[at + half : at + count], got[at + half : at + count]))
+            keeps.append(add(part.ff_keep[at : at + half], got[at : at + half]))
+        out["token"] = tuple(sends)
+        for hops in ((4, 1), (1, 4)):
+            got = yield tuple(swap(send, hop) for send, hop in zip(sends, hops))
+            count //= 2
+            half = count // 2
+            sends = [add(keep[half:], one[half:]) for keep, one in zip(keeps, got)]
+            keeps = [add(keep[:half], one[:half]) for keep, one in zip(keeps, got)]
+            out["token"] = tuple(sends)
+        keep, send = (jnp.concatenate(sides, axis=2) for sides in (keeps, sends))
+        yield from halving(keep, send, ff_split[1][3:], out)
+        yield from summing(out["piece"], ff_whole, out)
+        yield from sharing(out["piece"], ff_share, out)
 
     class Chain:
         def __init__(self, steps, *args):
@@ -865,7 +898,11 @@
 
         def step(self, token, *others):
             if self.arriving is not None:
-                arrived = tie(self.arriving, token, *others)
+                tokens = (*(token if isinstance(token, tuple) else (token,)), *others)
+                many = isinstance(self.arriving, tuple)
+                arrived = self.arriving if many else (self.arriving,)
+                arrived = lax.optimization_barrier((*arrived, *tokens))[: len(arrived)]
+                arrived = arrived if many else arrived[0]
                 self.arriving = None
                 try:
                     self.arriving = self.steps.send(arrived)
@@ -879,7 +916,7 @@
             last_backward_body,
             sizes=sizes,
             piece_masks=attn_masks[1],
-            ff_masks=ff_masks[1],
+            ff_masks=ff_masks[1:],
             heads=heads,
         ),
         "layer_1_backward",
@@ -893,8 +930,8 @@
             **attn_back_ins(second, first_ff.x_next, first_ff.a_next),
         ),
         dict(
-            ff_keep=Kept((ff_count, ff_grain, 3 * width), bf16),
-            ff_send=Kept((ff_count, ff_grain, 3 * width), bf16),
+            ff_keep=Kept((2 * ff_count, ff_grain, 3 * width // 2), bf16),
+            ff_send=Kept((2 * ff_count, ff_grain, 3 * width // 2), bf16),
             small=Kept(small_shape, f32),
             **attn_back_outs,
             outputs=(matrix, bf16),
@@ -939,7 +976,7 @@
         after=(peer_in_0,),
         micros=10,
     )
-    ff_1 = Chain(ff_chain, back_1, 1)
+    ff_1 = Chain(second_ff_chain, back_1)
     token = ff_1.step(back_0.branch)
     back_attn_0 = run(
         functools.partial(
@@ -967,13 +1004,13 @@
             table_rows=pltpu.VMEM((bias_table.shape[0], heads * slots), f32),
             **attn_back_scratch,
         ),
-        after=(token,),
+        after=token,
         micros=7,
     )
     attn_0 = Chain(attn_chain, back_attn_0, 0)
     token = attn_1.step(back_attn_0.attn_send, peer_grad_0)
     part_0 = run(
-        functools.partial(weight_body, piece_masks=place_masks[0]),
+        functools.partial(weight_body, piece_masks=place_masks),
         "layer_0_weight_grads",
         dict(
             place=place,
@@ -995,14 +1032,24 @@
         after=(token,),
         micros=4,
     )
-    ff_0 = Chain(ff_chain, part_0, 0)
+    ff_0 = Chain(first_ff_chain, part_0)
     token = part_0.ff_send
     shape = (2, width, width)
-    near_masks = place_masks[0][: ff_count // 2]
-    far_masks = place_masks[0][ff_count // 2 :]
-    done_1 = sums = attn_grads = None
-    while True:
-        for chain in (ff_0, ff_1, attn_0, attn_1):
+    near_masks = place_masks[: ff_count // 2]
+    far_masks = place_masks[ff_count // 2 :]
+    done = ()
+    ended = False
+    sums = attn_grads = None
+    while ff_0.arriving is not None:
+        token = ff_1.step(token)
+        if not done and "near" in ff_1.out:
+            done = finish(tie(ff_1.out["near"], token), near_masks, 1, place, shape)
+            token = done[0]
+        elif not ended and ff_1.arriving is None:
+            done = finish(tie(ff_1.out["far"], token), far_masks, 1, place, shape, done)
+            token = done[0]
+            ended = True
+        for chain in (ff_0, attn_0, attn_1):
             token = chain.step(token)
         if sums is None and attn_0.arriving is None:
             sums = run(
@@ -1013,33 +1060,28 @@
                     gain_attn=((2, width), f32),
                     gain_ff=((2, width), f32),
                     embed=((1, width), f32),
-                    table=(bias_table.shape, f32),
+                    table=(bias_table.shape[::-1], f32),
                 ),
                 {},
             )
             token = sums.embed
         if attn_grads is None and attn_0.arriving is None and attn_1.arriving is None:
-            attn_grads = jnp.stack([attn_0.out["done"], tie(attn_1.out["done"], token)])
-            token = attn_grads
-        if done_1 is None and ff_1.arriving is None:
-            pieces = tie(join(ff_1.out["near"], ff_1.out["far"]), token)
-            done_1 = finish(pieces, place_masks[1], 1, place, shape)
-            token = done_1[0]
-        if ff_0.arriving is None:
-            break
-    near_0 = finish(ff_0.out["near"], near_masks, 0, place, shape, done_1)
-    done = finish(ff_0.out["far"], far_masks, 0, place, shape, near_0)
+            both = jnp.stack([attn_0.out["done"], tie(attn_1.out["done"], token)])
+            attn_grads = [both[:, :, k * inner : (k + 1) * inner] for k in range(4)]
+            attn_grads[3] = jnp.swapaxes(attn_grads[3], 1, 2)
+            token = tuple(attn_grads)
+    if not ended:
+        done = finish(ff_1.out["far"], far_masks, 1, place, shape, done)
+    for pieces, masks in ((ff_0.out["near"], near_masks), (ff_0.out["far"], far_masks)):
+        done = finish(pieces, masks, 0, place, shape, done)
     return (
         back_1.outputs.reshape(inputs.shape),
         back_attn_0.grad_next.reshape(inputs.shape),
-        attn_grads[:, :, :inner],
-        attn_grads[:, :, inner : 2 * inner],
-        attn_grads[:, :, 2 * inner : 3 * inner],
-        jnp.swapaxes(attn_grads[:, :, 3 * inner :], 1, 2),
+        *attn_grads,
         *done,
         sums.gain_attn,
         sums.gain_ff,
-        sums.table,
+        sums.table.T,
         sums.embed[0],
     )
 

time: 188 us -> 179 us (0.952)
  local copies, waits for them, and re-layouts: 10.6 us -> 3.91 us
  starting transfers between devices: 46.6 us -> 40.6 us
  other arithmetic: 7.28 us -> 9.34 us
    ppermute x44 -> x47, starting transfers between devices: 46.6 us -> 40.6 us  [swap(): return lax.ppermute(array, axes, [(n, n ^ mask) for n in range(devices)])]
    unnamed x52 -> x65, local copies, waits for them, and re-layouts: 7.44 us -> 3.04 us
    concatenate x25 -> x24, other arithmetic: 2.18 us -> 5.53 us  [join(): return jnp.concatenate([left, right], axis=0)]
    ppermute x44 -> x47, waiting for transfers between devices: 71 us -> 69.3 us  [swap(): return lax.ppermute(array, axes, [(n, n ^ mask) for n in range(devices)])]
    pallas_call x3 -> x4, Pallas kernels: 5.52 us -> 6.68 us  [finish(): pl.pallas_call(kernel, name='layer_%d_ff_grads' % layer_idx, in_specs=[pl...]
  transfers between devices with their start and end apart: 44 -> 47, of which waited for: 18 -> 23; matrix products, arithmetic and copies ran while one was open for 5% -> 7% of each run, Pallas kernels for 22% -> 27%
where the time goes in v7:
time: 179 us; the launch traced here: 176 us
  waiting for transfers between devices  69.3 us (39%)
  Pallas kernels  51.2 us (29%)
  starting transfers between devices  40.6 us (23%)
  other arithmetic  9.34 us (5%)
  local copies, waits for them, and re-layouts  3.91 us (2%)
  between operations  1.79 us (1%)
    ppermute x47, waiting for transfers between devices, swap(): return lax.ppermute(array, axes, [(n, n ^ mask) for n in range(devices)])  69.3 us
    pallas_call x10, Pallas kernels, run(): pl.pallas_call(kernel, name=name, in_specs=[pl.BlockSpec(memory_space=in_...  44.6 us
    ppermute x47, starting transfers between devices, swap(): return lax.ppermute(array, axes, [(n, n ^ mask) for n in range(devices)])  40.6 us
    pallas_call x4, Pallas kernels, finish(): pl.pallas_call(kernel, name='layer_%d_ff_grads' % layer_idx, in_specs=[pl...  6.68 us
    concatenate x24, other arithmetic, join(): return jnp.concatenate([left, right], axis=0)  5.53 us
  transfers between devices with their start and end apart: 47, of which 23 were waited for; matrix products, arithmetic and copies ran while one was open for 7% of the time, Pallas kernels for 27%

profile of v7, /device:TPU:0, one launch (start us, length us, event | category | flops | bytes accessed | tf_op | source)
XLA Modules:
  0.0 176.2 jit_solution(2959581632917972001)
XLA Ops:
  1.5 3.0 %collective-permute-start.1 = (bf16[16,1536]{1,0:T(8,128)(2,1)S(1)}, bf16[16,1536]{1,0:T(8,128)(2,1)S(1)}, u32[]{:S(2)}, u32[]{:S(2)}) collective-permute-start(bf16[16,1536]{1,0:T(8,128)(2,1)S(1)} %get-tuple-element.269), channel_id=1, source_target_pairs={{0,1},{1,0},{2,3},{3,2},{4,5},{5,4},{6,7},{7,6},{8,9},{9,8},{10,11... | collective-permute-start | bytes 147464 | tf_op jit(solution)/shard_map/ppermute | solution.py:582
  4.5 2.6 %collective-permute-start = (bf16[16,1536]{1,0:T(8,128)(2,1)S(1)}, bf16[16,1536]{1,0:T(8,128)(2,1)S(1)}, u32[]{:S(2)}, u32[]{:S(2)}) collective-permute-start(bf16[16,1536]{1,0:T(8,128)(2,1)S(1)} %get-tuple-element.270), channel_id=1, source_target_pairs={{0,16},{1,17},{2,18},{3,19},{4,20},{5,21},{6,22},{7,23},{8,24},{9,... | collective-permute-start | bytes 147464 | tf_op jit(solution)/shard_map/ppermute | solution.py:582
  29.6 4.9 %collective-permute-done.4 = bf16[128,1536]{1,0:T(8,128)(2,1)S(1)} collective-permute-done((bf16[128,1536]{1,0:T(8,128)(2,1)S(1)}, bf16[128,1536]{1,0:T(8,128)(2,1)S(1)}, u32[]{:S(2)}, u32[]{:S(2)}) %collective-permute-start.4) | collective-permute-done | bytes 393248 | tf_op jit(solution)/shard_map/ppermute | solution.py:582
  37.3 10.3 %collective-permute-done.13 = bf16[3,128,512]{2,1,0:T(8,128)(2,1)S(1)} collective-permute-done((bf16[3,128,512]{2,1,0:T(8,128)(2,1)S(1)}, bf16[3,128,512]{2,1,0:T(8,128)(2,1)S(1)}, u32[]{:S(2)}, u32[]{:S(2)}) %collective-permute-start.13) | collective-permute-done | bytes 393248 | tf_op jit(solution)/shard_map/ppermute | solution.py:582
  48.1 5.0 %layer_0_attention.1 = (bf16[512,1536]{1,0:T(8,128)(2,1)S(1)}, bf16[512,1152]{1,0:T(8,128)(2,1)S(1)}, f32[512,384]{1,0:T(8,128)S(1)}, bf16[512,384]{1,0:T(8,128)...) custom-call(s32[4]{0:T(128)S(1)} %pad_add_fusion.1.refs_0_.place_ref, ...), custom_call_target="tpu_custom_call" | custom-call | flops 11500000256 | tf_op jit(solution)/shard_map/layer_0_attention/pallas_call | solution.py:98
  53.2 3.9 %layer_0_ff.1 = (bf16[2,512,1024]{2,1,0:T(8,128)(2,1)S(1)}, bf16[2,512,512]{2,1,0:T(8,128)(2,1)S(1)}, f32[512,512]{1,0:T(8,128)S(1)}, bf16[512,512]{1,0:T(8,128)(2,1)S(1)}) custom-call(s32[4]{0:T(128)S(1)} %pad_add_fusion.1.refs_0_.place_ref, f32[512,512]{1,0:T(8,128)S(1)} %get-tuple-element.130.refs_1_.refs_3_, ...), custom_call_target="tpu_custom_call" | custom-call | flops 115000000 | tf_op jit(solution)/shard_map/layer_0_ff/pallas_call | solution.py:98
  58.9 5.0 %layer_1_attention.1 = (bf16[512,1536]{1,0:T(8,128)(2,1)S(1)}, bf16[512,1152]{1,0:T(8,128)(2,1)S(1)}, f32[512,384]{1,0:T(8,128)S(1)}, bf16[512,384]{1,0:T(8,128)...) custom-call(s32[4]{0:T(128)S(1)} %pad_add_fusion.1.refs_0_.place_ref, ...), custom_call_target="tpu_custom_call" | custom-call | flops 115000000 | tf_op jit(solution)/shard_map/layer_1_attention/pallas_call | solution.py:98
  63.9 12.5 %layer_1_backward.1 = (bf16[32,32,768]{2,1,0:T(8,128)(2,1)S(1)}, bf16[32,32,768]{2,1,0:T(8,128)(2,1)S(1)}, f32[8,1536]{1,0:T(8,128)S(1)}, bf16[16,16,1536]{2,1,0...) custom-call(s32[4]{0:T(128)S(1)} %pad_add_fusion.1.refs_0_.place_ref, ...), custom_call_target="tpu_custom_call" | custom-call | flops 11500000256 | tf_op jit(solution)/shard_map/layer_1_backward/pallas_call | solution.py:98
  78.6 4.6 %layer_0_ff_backward.1 = (bf16[1,512,512]{2,1,0:T(8,128)(2,1)S(1)}, bf16[1,512,1024]{2,1,0:T(8,128)(2,1)S(1)}, f32[8,1536]{1,0:T(8,128)S(1)}, f32[512,512]{1,0:T(8,128)S(1)}, bf16[512,512]{1,0:T(8,128)(2,1)S(1)}) custom-call(f32[512,512]{1,0:T(8,128)S(1)} %get-tuple-element.151.refs_0_, f32[2,512]{1,0:T(2,128)S(1)} %copy-done.3, ...), custom_call_target="tpu_custom_call" | custom-call | flops 11500000256 | tf_op jit(solution)/shard_map/layer_0_ff_backward/pallas_call | solution.py:98
  85.4 6.3 %layer_0_attention_backward.1 = (bf16[16,16,1536]{2,1,0:T(8,128)(2,1)S(1)}, bf16[17,16,1536]{2,1,0:T(8,128)(2,1)S(1)}, f32[8,1536]{1,0:T(8,128)S(1)}, f32[512,512]{1,0:T(8,128)}) custom-call(s32[4]{0:T(128)S(1)} %pad_add_fusion.1.refs_0_.place_ref, f32[64,384]{1,0:T(8,128)S(1)} %get-tuple-element.150.refs_1_, s32[512,2]{1,0:T(8,128)S(1)} %copy.46.refs_1_.refs_2_, ...), custom_call_target="tpu_custom_call" | custom-call | flops 8049999872 | tf_op jit(solution)/shard_map/layer_0_attention_backward/pallas_call | solution.py:98
  92.0 3.8 %layer_0_weight_grads.1 = (bf16[8,32,1536]{2,1,0:T(8,128)(2,1)S(1)}, bf16[8,32,1536]{2,1,0:T(8,128)(2,1)S(1)}) custom-call(s32[4]{0:T(128)S(1)} %pad_add_fusion.1.refs_0_.place_ref, bf16[512,512]{1,0:T(8,128)(2,1)S(1)} %get-tuple-element.131.refs_2_.refs_4_.refs_1_, bf16[512,512]{1,0:T(8,128)(2,1)S(1)} %get-tuple-element.168.refs_2_, ...), custom_call_target="tpu_custom_call" | custom-call | flops 4600000000 | tf_op jit(solution)/shard_map/layer_0_weight_grads/pallas_call | solution.py:98
  104.6 3.8 %collective-permute-done.28 = bf16[8,16,1536]{2,1,0:T(8,128)(2,1)S(1)} collective-permute-done((bf16[8,16,1536]{2,1,0:T(8,128)(2,1)S(1)}, bf16[8,16,1536]{2,1,0:T(8,128)(2,1)S(1)}, u32[]{:S(2)}, u32[]{:S(2)}) %collective-permute-start.28) | collective-permute-done | bytes 393248 | tf_op jit(solution)/shard_map/ppermute | solution.py:582
  109.6 3.1 %collective-permute-done.26 = bf16[4,32,768]{2,1,0:T(8,128)(2,1)S(1)} collective-permute-done((bf16[4,32,768]{2,1,0:T(8,128)(2,1)S(1)}, bf16[4,32,768]{2,1,0:T(8,128)(2,1)S(1)}, u32[]{:S(2)}, u32[]{:S(2)}) %collective-permute-start.26) | collective-permute-done | bytes 196640 | tf_op jit(solution)/shard_map/ppermute | solution.py:582
  113.7 2.2 %collective-permute-done.25 = bf16[4,32,1536]{2,1,0:T(8,128)(2,1)S(1)} collective-permute-done((bf16[4,32,1536]{2,1,0:T(8,128)(2,1)S(1)}, bf16[4,32,1536]{2,1,0:T(8,128)(2,1)S(1)}, u32[]{:S(2)}, u32[]{:S(2)}) %collective-permute-start.25) | collective-permute-done | bytes 393248 | tf_op jit(solution)/shard_map/ppermute | solution.py:582
  116.5 5.0 %collective-permute-done.24 = bf16[9,16,1536]{2,1,0:T(8,128)(2,1)S(1)} collective-permute-done((bf16[9,16,1536]{2,1,0:T(8,128)(2,1)S(1)}, bf16[9,16,1536]{2,1,0:T(8,128)(2,1)S(1)}, u32[]{:S(2)}, u32[]{:S(2)}) %collective-permute-start.24) | collective-permute-done | bytes 442400 | tf_op jit(solution)/shard_map/ppermute | solution.py:582
  127.0 2.1 %collective-permute-done.29 = bf16[5,16,1536]{2,1,0:T(8,128)(2,1)S(1)} collective-permute-done((bf16[5,16,1536]{2,1,0:T(8,128)(2,1)S(1)}, bf16[5,16,1536]{2,1,0:T(8,128)(2,1)S(1)}, u32[]{:S(2)}, u32[]{:S(2)}) %collective-permute-start.29) | collective-permute-done | bytes 245792 | tf_op jit(solution)/shard_map/ppermute | solution.py:582
  132.1 2.1 %collective-permute-done.35 = bf16[1,32,1536]{2,1,0:T(8,128)(2,1)S(1)} collective-permute-done((bf16[1,32,1536]{2,1,0:T(8,128)(2,1)S(1)}, bf16[1,32,1536]{2,1,0:T(8,128)(2,1)S(1)}, u32[]{:S(2)}, u32[]{:S(2)}) %collective-permute-start.35) | collective-permute-done | bytes 98336 | tf_op jit(solution)/shard_map/ppermute | solution.py:582
  134.3 6.9 %collective-permute-done.34 = bf16[1,32,1536]{2,1,0:T(8,128)(2,1)S(1)} collective-permute-done((bf16[1,32,1536]{2,1,0:T(8,128)(2,1)S(1)}, bf16[1,32,1536]{2,1,0:T(8,128)(2,1)S(1)}, u32[]{:S(2)}, u32[]{:S(2)}) %collective-permute-start.34) | collective-permute-done | bytes 98336 | tf_op jit(solution)/shard_map/ppermute | solution.py:582
  141.4 3.0 %collective-permute-start.37 = (bf16[2,16,1536]{2,1,0:T(8,128)(2,1)S(1)}, bf16[2,16,1536]{2,1,0:T(8,128)(2,1)S(1)}, u32[]{:S(2)}, u32[]{:S(2)}) collective-permute-start(bf16[2,16,1536]{2,1,0:T(8,128)(2,1)S(1)} %maximum_maximum_fusion.3), channel_id=1, source_target_pairs={{0,16},{1,17},{2,18},{3,19},{4,20},{5,21},{6,22},{7,23},{8,24},{9,... | collective-permute-start | bytes 294920 | tf_op jit(solution)/shard_map/ppermute | solution.py:582
  144.5 3.1 %collective-permute-done.38 = bf16[1,32,1536]{2,1,0:T(8,128)(2,1)S(1)} collective-permute-done((bf16[1,32,1536]{2,1,0:T(8,128)(2,1)S(1)}, bf16[1,32,1536]{2,1,0:T(8,128)(2,1)S(1)}, u32[]{:S(2)}, u32[]{:S(2)}) %collective-permute-start.38) | collective-permute-done | bytes 98336 | tf_op jit(solution)/shard_map/ppermute | solution.py:582
  150.6 2.4 %collective-permute-done.42 = bf16[2,32,1536]{2,1,0:T(8,128)(2,1)S(1)} collective-permute-done((bf16[2,32,1536]{2,1,0:T(8,128)(2,1)S(1)}, bf16[2,32,1536]{2,1,0:T(8,128)(2,1)S(1)}, u32[]{:S(2)}, u32[]{:S(2)}) %collective-permute-start.42) | collective-permute-done | bytes 196640 | tf_op jit(solution)/shard_map/ppermute | solution.py:582
  154.0 2.0 %collective-permute-done.41 = bf16[2,32,1536]{2,1,0:T(8,128)(2,1)S(1)} collective-permute-done((bf16[2,32,1536]{2,1,0:T(8,128)(2,1)S(1)}, bf16[2,32,1536]{2,1,0:T(8,128)(2,1)S(1)}, u32[]{:S(2)}, u32[]{:S(2)}) %collective-permute-start.41) | collective-permute-done | bytes 196640 | tf_op jit(solution)/shard_map/ppermute | solution.py:582
  156.9 8.2 %collective-permute-done.44 = bf16[4,32,1536]{2,1,0:T(8,128)(2,1)S(1)} collective-permute-done((bf16[4,32,1536]{2,1,0:T(8,128)(2,1)S(1)}, bf16[4,32,1536]{2,1,0:T(8,128)(2,1)S(1)}, u32[]{:S(2)}, u32[]{:S(2)}) %collective-permute-start.44) | collective-permute-done | bytes 393248 | tf_op jit(solution)/shard_map/ppermute | solution.py:582
  166.9 3.3 %collective-permute-done.43 = bf16[4,32,1536]{2,1,0:T(8,128)(2,1)S(1)} collective-permute-done((bf16[4,32,1536]{2,1,0:T(8,128)(2,1)S(1)}, bf16[4,32,1536]{2,1,0:T(8,128)(2,1)S(1)}, u32[]{:S(2)}, u32[]{:S(2)}) %collective-permute-start.43) | collective-permute-done | bytes 393248 | tf_op jit(solution)/shard_map/ppermute | solution.py:582
  (218 shorter events, 65.3 us)
Async XLA Ops:
  13.3 14.8 %collective-permute-start.5 = (bf16[3,128,512]{2,1,0:T(8,128)(2,1)S(1)}, bf16[3,128,512]{2,1,0:T(8,128)(2,1)S(1)}, u32[]{:S(2)}, u32[]{:S(2)}) collective-permute-start(bf16[3,128,512]{2,1,0:T(8,128)(2,1)S(1)} %get-tuple-element.128), channel_id=1, source_target_pairs={{0,1},{1,0},{2,3},{3,2},{4,5},{5,4},{6,7},{7,6},{8,9},{9,8},{10,11... | collective-permute-start | bytes 1179656 | tf_op jit(solution)/shard_map/ppermute | solution.py:582
  35.9 12.0 %collective-permute-start.7 = (bf16[256,1536]{1,0:T(8,128)(2,1)S(1)}, bf16[256,1536]{1,0:T(8,128)(2,1)S(1)}, u32[]{:S(2)}, u32[]{:S(2)}) collective-permute-start(bf16[256,1536]{1,0:T(8,128)(2,1)S(1)} %constant_dynamic-update-slice_fusion.refs_6_), channel_id=1, source_target_pairs={{0,2},{1,3},{2,0},{3,1},{4,6},{5,7},{6,4},{7,5},{8,10},{9,11},{10,... | collective-permute-start | bytes 2359304 | tf_op jit(solution)/shard_map/ppermute | solution.py:582
  36.0 11.6 %collective-permute-start.13 = (bf16[3,128,512]{2,1,0:T(8,128)(2,1)S(1)}, bf16[3,128,512]{2,1,0:T(8,128)(2,1)S(1)}, u32[]{:S(2)}, u32[]{:S(2)}) collective-permute-start(bf16[3,128,512]{2,1,0:T(8,128)(2,1)S(1)} %get-tuple-element.142), channel_id=1, source_target_pairs={{0,1},{1,0},{2,3},{3,2},{4,5},{5,4},{6,7},{7,6},{8,9},{9,8},{10,11... | collective-permute-start | bytes 1179656 | tf_op jit(solution)/shard_map/ppermute | solution.py:582
  37.2 15.9 %collective-permute-start.11 = (bf16[6,128,512]{2,1,0:T(8,128)(2,1)S(1)}, bf16[6,128,512]{2,1,0:T(8,128)(2,1)S(1)}, u32[]{:S(2)}, u32[]{:S(2)}) collective-permute-start(bf16[6,128,512]{2,1,0:T(8,128)(2,1)S(1)} %constant_dynamic-update-slice_fusion.10.refs_7_), channel_id=1, source_target_pairs={{0,2},{1,3},{2,0},{3,1},{4,6},{5,7},{6,4},{7,5},{8,10},{9,11},{10,... | collective-permute-start | bytes 2359304 | tf_op jit(solution)/shard_map/ppermute | solution.py:582
  47.6 10.7 %collective-permute-start.14 = (bf16[3,128,512]{2,1,0:T(8,128)(2,1)S(1)}, bf16[3,128,512]{2,1,0:T(8,128)(2,1)S(1)}, u32[]{:S(2)}, u32[]{:S(2)}) collective-permute-start(bf16[3,128,512]{2,1,0:T(8,128)(2,1)S(1)} %collective-permute-done.13), channel_id=1, source_target_pairs={{0,4},{1,5},{2,6},{3,7},{4,0},{5,1},{6,2},{7,3},{8,12},{9,13},{10,... | collective-permute-start | bytes 1179656 | tf_op jit(solution)/shard_map/ppermute | solution.py:582
  58.5 20.2 %collective-permute-start.16 = (bf16[512,512]{1,0:T(8,128)(2,1)S(1)}, bf16[512,512]{1,0:T(8,128)(2,1)S(1)}, u32[]{:S(2)}, u32[]{:S(2)}) collective-permute-start(bf16[512,512]{1,0:T(8,128)(2,1)S(1)} %get-tuple-element.131.refs_2_.refs_4_.refs_1_), channel_id=1, source_target_pairs={{0,1},{1,0},{2,3},{3,2},{4,5},{5,4},{6,7},{7,6},{8,9},{9,8},{10,11... | collective-permute-start | bytes 1572872 | tf_op jit(solution)/shard_map/ppermute | solution.py:582
  76.6 15.2 %collective-permute-start.20 = (bf16[16,16,1536]{2,1,0:T(8,128)(2,1)S(1)}, bf16[16,16,1536]{2,1,0:T(8,128)(2,1)S(1)}, u32[]{:S(2)}, u32[]{:S(2)}) collective-permute-start(bf16[16,16,1536]{2,1,0:T(8,128)(2,1)S(1)} %get-tuple-element.172), channel_id=1, source_target_pairs={{0,2},{1,3},{2,0},{3,1},{4,6},{5,7},{6,4},{7,5},{8,10},{9,11},{10,... | collective-permute-start | bytes 2359304 | tf_op jit(solution)/shard_map/ppermute | solution.py:582
  77.0 14.8 %collective-permute-start.19 = (bf16[512,512]{1,0:T(8,128)(2,1)S(1)}, bf16[512,512]{1,0:T(8,128)(2,1)S(1)}, u32[]{:S(2)}, u32[]{:S(2)}) collective-permute-start(bf16[512,512]{1,0:T(8,128)(2,1)S(1)} %get-tuple-element.168.refs_2_), channel_id=1, source_target_pairs={{0,1},{1,0},{2,3},{3,2},{4,5},{5,4},{6,7},{7,6},{8,9},{9,8},{10,11... | collective-permute-start | bytes 1572872 | tf_op jit(solution)/shard_map/ppermute | solution.py:582
  83.9 14.2 %collective-permute-start.22 = (bf16[8,32,768]{2,1,0:T(8,128)(2,1)S(1)}, bf16[8,32,768]{2,1,0:T(8,128)(2,1)S(1)}, u32[]{:S(2)}, u32[]{:S(2)}) collective-permute-start(bf16[8,32,768]{2,1,0:T(8,128)(2,1)S(1)} %get-tuple-element.238.refs_14_), channel_id=1, source_target_pairs={{0,4},{1,5},{2,6},{3,7},{4,0},{5,1},{6,2},{7,3},{8,12},{9,13},{10,... | collective-permute-start | bytes 1179656 | tf_op jit(solution)/shard_map/ppermute | solution.py:582
  84.9 14.6 %collective-permute-start.23 = (bf16[8,32,768]{2,1,0:T(8,128)(2,1)S(1)}, bf16[8,32,768]{2,1,0:T(8,128)(2,1)S(1)}, u32[]{:S(2)}, u32[]{:S(2)}) collective-permute-start(bf16[8,32,768]{2,1,0:T(8,128)(2,1)S(1)} %get-tuple-element.237.refs_15_), channel_id=1, source_target_pairs={{0,1},{1,0},{2,3},{3,2},{4,5},{5,4},{6,7},{7,6},{8,9},{9,8},{10,11... | collective-permute-start | bytes 1179656 | tf_op jit(solution)/shard_map/ppermute | solution.py:582
  96.5 12.0 %collective-permute-start.28 = (bf16[8,16,1536]{2,1,0:T(8,128)(2,1)S(1)}, bf16[8,16,1536]{2,1,0:T(8,128)(2,1)S(1)}, u32[]{:S(2)}, u32[]{:S(2)}) collective-permute-start(bf16[8,16,1536]{2,1,0:T(8,128)(2,1)S(1)} %get-tuple-element.242.refs_9_), channel_id=1, source_target_pairs={{0,1},{1,0},{2,3},{3,2},{4,5},{5,4},{6,7},{7,6},{8,9},{9,8},{10,11... | collective-permute-start | bytes 1179656 | tf_op jit(solution)/shard_map/ppermute | solution.py:582
  99.6 9.9 %collective-permute-start.27 = (bf16[4,32,768]{2,1,0:T(8,128)(2,1)S(1)}, bf16[4,32,768]{2,1,0:T(8,128)(2,1)S(1)}, u32[]{:S(2)}, u32[]{:S(2)}) collective-permute-start(bf16[4,32,768]{2,1,0:T(8,128)(2,1)S(1)} %get-tuple-element.252), channel_id=1, source_target_pairs={{0,4},{1,5},{2,6},{3,7},{4,0},{5,1},{6,2},{7,3},{8,12},{9,13},{10,... | collective-permute-start | bytes 589832 | tf_op jit(solution)/shard_map/ppermute | solution.py:582
  100.6 12.1 %collective-permute-start.26 = (bf16[4,32,768]{2,1,0:T(8,128)(2,1)S(1)}, bf16[4,32,768]{2,1,0:T(8,128)(2,1)S(1)}, u32[]{:S(2)}, u32[]{:S(2)}) collective-permute-start(bf16[4,32,768]{2,1,0:T(8,128)(2,1)S(1)} %get-tuple-element.254), channel_id=1, source_target_pairs={{0,1},{1,0},{2,3},{3,2},{4,5},{5,4},{6,7},{7,6},{8,9},{9,8},{10,11... | collective-permute-start | bytes 589832 | tf_op jit(solution)/shard_map/ppermute | solution.py:582
  102.6 13.4 %collective-permute-start.25 = (bf16[4,32,1536]{2,1,0:T(8,128)(2,1)S(1)}, bf16[4,32,1536]{2,1,0:T(8,128)(2,1)S(1)}, u32[]{:S(2)}, u32[]{:S(2)}) collective-permute-start(bf16[4,32,1536]{2,1,0:T(8,128)(2,1)S(1)} %get-tuple-element.244), channel_id=1, source_target_pairs={{0,4},{1,5},{2,6},{3,7},{4,0},{5,1},{6,2},{7,3},{8,12},{9,13},{10,... | collective-permute-start | bytes 1179656 | tf_op jit(solution)/shard_map/ppermute | solution.py:582
  104.3 17.2 %collective-permute-start.24 = (bf16[9,16,1536]{2,1,0:T(8,128)(2,1)S(1)}, bf16[9,16,1536]{2,1,0:T(8,128)(2,1)S(1)}, u32[]{:S(2)}, u32[]{:S(2)}) collective-permute-start(bf16[9,16,1536]{2,1,0:T(8,128)(2,1)S(1)} %maximum_maximum_fusion), channel_id=1, source_target_pairs={{0,1},{1,0},{2,3},{3,2},{4,5},{5,4},{6,7},{7,6},{8,9},{9,8},{10,11... | collective-permute-start | bytes 1327112 | tf_op jit(solution)/shard_map/ppermute | solution.py:582
  108.5 14.1 %collective-permute-start.32 = (bf16[4,16,1536]{2,1,0:T(8,128)(2,1)S(1)}, bf16[4,16,1536]{2,1,0:T(8,128)(2,1)S(1)}, u32[]{:S(2)}, u32[]{:S(2)}) collective-permute-start(bf16[4,16,1536]{2,1,0:T(8,128)(2,1)S(1)} %get-tuple-element.248), channel_id=1, source_target_pairs={{0,4},{1,5},{2,6},{3,7},{4,0},{5,1},{6,2},{7,3},{8,12},{9,13},{10,... | collective-permute-start | bytes 589832 | tf_op jit(solution)/shard_map/ppermute | solution.py:582
  112.8 11.1 %collective-permute-start.31 = (bf16[2,32,1536]{2,1,0:T(8,128)(2,1)S(1)}, bf16[2,32,1536]{2,1,0:T(8,128)(2,1)S(1)}, u32[]{:S(2)}, u32[]{:S(2)}) collective-permute-start(bf16[2,32,1536]{2,1,0:T(8,128)(2,1)S(1)} %pad_maximum_fusion.8), channel_id=1, source_target_pairs={{0,8},{1,9},{2,10},{3,11},{4,12},{5,13},{6,14},{7,15},{8,0},{9,1},... | collective-permute-start | bytes 589832 | tf_op jit(solution)/shard_map/ppermute | solution.py:582
  123.9 10.2 %collective-permute-start.35 = (bf16[1,32,1536]{2,1,0:T(8,128)(2,1)S(1)}, bf16[1,32,1536]{2,1,0:T(8,128)(2,1)S(1)}, u32[]{:S(2)}, u32[]{:S(2)}) collective-permute-start(bf16[1,32,1536]{2,1,0:T(8,128)(2,1)S(1)} %add_convert_fusion.28), channel_id=1, source_target_pairs={{0,16},{1,17},{2,18},{3,19},{4,20},{5,21},{6,22},{7,23},{8,24},{9,... | collective-permute-start | bytes 294920 | tf_op jit(solution)/shard_map/ppermute | solution.py:582
  125.9 15.3 %collective-permute-start.34 = (bf16[1,32,1536]{2,1,0:T(8,128)(2,1)S(1)}, bf16[1,32,1536]{2,1,0:T(8,128)(2,1)S(1)}, u32[]{:S(2)}, u32[]{:S(2)}) collective-permute-start(bf16[1,32,1536]{2,1,0:T(8,128)(2,1)S(1)} %add_convert_fusion.27), channel_id=1, source_target_pairs={{0,16},{1,17},{2,18},{3,19},{4,20},{5,21},{6,22},{7,23},{8,24},{9,... | collective-permute-start | bytes 294920 | tf_op jit(solution)/shard_map/ppermute | solution.py:582
  129.2 12.1 %collective-permute-start.33 = (bf16[3,16,1536]{2,1,0:T(8,128)(2,1)S(1)}, bf16[3,16,1536]{2,1,0:T(8,128)(2,1)S(1)}, u32[]{:S(2)}, u32[]{:S(2)}) collective-permute-start(bf16[3,16,1536]{2,1,0:T(8,128)(2,1)S(1)} %maximum_maximum_fusion.2), channel_id=1, source_target_pairs={{0,8},{1,9},{2,10},{3,11},{4,12},{5,13},{6,14},{7,15},{8,0},{9,1},... | collective-permute-start | bytes 442376 | tf_op jit(solution)/shard_map/ppermute | solution.py:582
  130.1 14.3 %collective-permute-start.40 = (bf16[1,16,1536]{2,1,0:T(8,128)(2,1)S(1)}, bf16[1,16,1536]{2,1,0:T(8,128)(2,1)S(1)}, u32[]{:S(2)}, u32[]{:S(2)}) collective-permute-start(bf16[1,16,1536]{2,1,0:T(8,128)(2,1)S(1)} %add_convert_fusion.39), channel_id=1, source_target_pairs={{0,16},{1,17},{2,18},{3,19},{4,20},{5,21},{6,22},{7,23},{8,24},{9,... | collective-permute-start | bytes 147464 | tf_op jit(solution)/shard_map/ppermute | solution.py:582
  134.2 10.2 %collective-permute-start.39 = (bf16[1,32,1536]{2,1,0:T(8,128)(2,1)S(1)}, bf16[1,32,1536]{2,1,0:T(8,128)(2,1)S(1)}, u32[]{:S(2)}, u32[]{:S(2)}) collective-permute-start(bf16[1,32,1536]{2,1,0:T(8,128)(2,1)S(1)} %add_convert_fusion.21), channel_id=1, source_target_pairs={{0,16},{1,17},{2,18},{3,19},{4,20},{5,21},{6,22},{7,23},{8,24},{9,... | collective-permute-start | bytes 294920 | tf_op jit(solution)/shard_map/ppermute | solution.py:582
  153.0 12.1 %collective-permute-start.44 = (bf16[4,32,1536]{2,1,0:T(8,128)(2,1)S(1)}, bf16[4,32,1536]{2,1,0:T(8,128)(2,1)S(1)}, u32[]{:S(2)}, u32[]{:S(2)}) collective-permute-start(bf16[4,32,1536]{2,1,0:T(8,128)(2,1)S(1)} %pad_maximum_fusion.4), channel_id=1, source_target_pairs={{0,4},{1,5},{2,6},{3,7},{4,0},{5,1},{6,2},{7,3},{8,12},{9,13},{10,... | collective-permute-start | bytes 1179656 | tf_op jit(solution)/shard_map/ppermute | solution.py:582
  156.0 14.2 %collective-permute-start.43 = (bf16[4,32,1536]{2,1,0:T(8,128)(2,1)S(1)}, bf16[4,32,1536]{2,1,0:T(8,128)(2,1)S(1)}, u32[]{:S(2)}, u32[]{:S(2)}) collective-permute-start(bf16[4,32,1536]{2,1,0:T(8,128)(2,1)S(1)} %pad_maximum_fusion.5), channel_id=1, source_target_pairs={{0,4},{1,5},{2,6},{3,7},{4,0},{5,1},{6,2},{7,3},{8,12},{9,13},{10,... | collective-permute-start | bytes 1179656 | tf_op jit(solution)/shard_map/ppermute | solution.py:582
  (51 other events, 355.1 us)

commit v8 on v7

--- a/solution.py
+++ b/solution.py
@@ -13,7 +13,7 @@
 bf16 = jnp.bfloat16
 f32 = jnp.float32
 axes = ("dp", "tensor")
-vmem_bytes = 32 * 1024 * 1024
+mebibyte = 1024 * 1024
 raw_names = ("attn_near", "attn_far", "ff_near", "ff_far", "w_gate", "w_up", "w_down")
 
 
@@ -55,7 +55,7 @@
     return pl.CostEstimate(flops=int(micros * 1.15e9), bytes_accessed=0, transcendentals=0)
 
 
-def run(body, name, ins, outs, scratch, after=(), micros=1):
+def run(body, name, ins, outs, scratch, after=(), micros=1, vmem=8):
     in_names, out_names, scratch_names = list(ins), list(outs), list(scratch)
     direct = {n for n in in_names if n == "place" or n in raw_names or isinstance(ins[n], Kept)}
     staged = [n for n in in_names if n not in direct]
@@ -115,7 +115,7 @@
             pltpu.SemaphoreType.DMA((max(1, len(staged)),)),
             pltpu.SemaphoreType.DMA((max(1, len(copied)),)),
         ],
-        compiler_params=pltpu.CompilerParams(vmem_limit_bytes=vmem_bytes),
+        compiler_params=pltpu.CompilerParams(vmem_limit_bytes=vmem * mebibyte),
         cost_estimate=cost(micros),
     )(
         *[
@@ -143,35 +143,26 @@
     return [slice(start, start + size) for start in range(0, extent, size)]
 
 
-def attention_copies(r, masks, rows):
-    copies = []
+def lay_out_attention(r, masks, rows):
     for idx, mask in enumerate(masks):
         half, at = divmod(idx, max(1, len(masks) // 2))
-        source = (r.attn_near if half == 0 else r.attn_far).at[pl.ds(at * rows, rows)]
-        place = (r.place[0] ^ mask) * rows if len(masks) > 1 else 0
-        target = r.attn_w.at[pl.ds(pl.multiple_of(place, rows), rows)]
-        copies.append(pltpu.make_async_copy(source, target, r.attn_sem))
-    return copies
-
-
-def ff_copies(r, layer_idx):
+        source = r.attn_near if half == 0 else r.attn_far
+        place = pl.multiple_of((r.place[0] ^ mask) * rows, rows) if len(masks) > 1 else 0
+        r.attn_w[pl.ds(place, rows), :] = source[at * rows : (at + 1) * rows, :]
+
+
+def lay_out_ff(r, layer_idx):
     width = r.ff_down.shape[-1]
-    copies = []
     for k, own in enumerate((r.w_gate, r.w_up)):
-        target = r.ff_gate_up.at[0, :, pl.ds(k * width, width)]
-        copies.append(pltpu.make_async_copy(own.at[layer_idx], target, r.ff_sem))
-    copies.append(pltpu.make_async_copy(r.w_down.at[layer_idx], r.ff_down.at[0], r.ff_sem))
+        r.ff_gate_up[0, :, k * width : (k + 1) * width] = own[layer_idx]
+    r.ff_down[0] = r.w_down[layer_idx]
     part = r.ff_near.shape[1]
     for source, base in ((r.ff_near, 0), (r.ff_far, 1)):
         for m in range(2):
             rows = pl.ds(pl.multiple_of((r.place[1] ^ (2 * m + base)) * part, part), part)
             for k in range(2):
-                target = r.ff_gate_up.at[1, rows, pl.ds(k * width, width)]
-                copies.append(pltpu.make_async_copy(source.at[3 * m + k], target, r.ff_sem))
-            copies.append(
-                pltpu.make_async_copy(source.at[3 * m + 2], r.ff_down.at[1, rows], r.ff_sem)
-            )
-    return copies
+                r.ff_gate_up[1, rows, k * width : (k + 1) * width] = source[3 * m + k]
+            r.ff_down[1, rows, :] = source[3 * m + 2]
 
 
 def start_all(copies):
@@ -251,18 +242,16 @@
 
 
 def attention_body(r, sizes, masks, grain, layer_idx):
-    start_all(attention_copies(r, masks, grain))
     r.fetch("gain_ff")
+    lay_out_attention(r, masks, grain)
     r.need("gain_ff")
-    wait_all(r.attn_sem, r.attn_w)
     attention_forward(r, r.x, r.a, sizes, layer_idx)
 
 
 def ff_body(r):
-    start_all(ff_copies(r, 0))
     r.fetch("gain_attn")
+    lay_out_ff(r, 0)
     r.need("gain_attn")
-    wait_all(r.ff_sem, r.ff_gate_up, r.ff_down)
     width = r.middle.shape[1]
     for part in chunks(r.middle.shape[0], 256):
         x_next = r.middle[part, :]
@@ -274,14 +263,12 @@
         r.a_next[part, :] = (x_next * inverse_rms(x_next) * r.gain_attn[1:2, :]).astype(bf16)
 
 
-def ff_backward(r, layer_idx, last):
+def ff_backward(r, layer_idx, last, masks):
     rows, width = r.middle.shape
     r.fetch("grad", "gain_ff")
     if last:
-        start_all(ff_copies(r, layer_idx))
+        lay_out_ff(r, layer_idx)
     r.need("grad", "gain_ff")
-    if last:
-        wait_all(r.ff_sem, r.ff_gate_up, r.ff_down)
     gain_ff = r.gain_ff[layer_idx : layer_idx + 1, :]
     gain_total = jnp.zeros((1, width), f32)
     for part in chunks(rows, 256):
@@ -297,14 +284,10 @@
             gate_act, up_act = both[:, :width], both[:, width:]
             mixed, slope = gelu_terms(gate_act)
             hidden = (mixed * up_act).astype(bf16)
-            if last or half == 0:
-                r.hidden[half, part, :] = hidden
-                held = r.grad_gate_up.at[half, part]
-            else:
-                held = r.pulled
-            held[:, :width] = (grad_hidden * up_act * slope).astype(bf16)
-            held[:, width:] = (grad_hidden * mixed).astype(bf16)
-            pulled = held[...]
+            r.hidden[half, part, :] = hidden
+            r.grad_gate_up[half, part, :width] = (grad_hidden * up_act * slope).astype(bf16)
+            r.grad_gate_up[half, part, width:] = (grad_hidden * mixed).astype(bf16)
+            pulled = r.grad_gate_up[half, part, :]
             if last:
                 total = total + dot_nn(hidden, r.ff_down[half])
             term = dot_nt(pulled, r.ff_gate_up[half])
@@ -316,8 +299,24 @@
         grad_mid = grad + grad_mid
         r.grad_mid[part, :] = grad_mid
         r.branch[part, :] = grad_mid.astype(bf16)
+        r.grad_low[part, :] = rounded
     if last:
         r.write("outputs")
+    for half in range(2):
+        r.ff_grad[half, :, : 2 * width] = dot_tn(r.ff_in[...], r.grad_gate_up[half])
+        r.ff_grad[half, :, 2 * width :] = dot_tn(r.hidden[half], r.grad_low[...])
+    half_count = len(masks[0]) // 2
+    grain, columns = r.ff_keep.shape[1:]
+    for side, side_masks in enumerate(masks):
+        lanes = slice(side * columns, (side + 1) * columns)
+        for idx, mask in enumerate(side_masks):
+            target = r.ff_keep if idx < half_count else r.ff_send
+            piece = pl.ds(pl.multiple_of((r.place[3] ^ (mask // 2)) * grain, grain), grain)
+            target[side * half_count + idx % half_count] = r.ff_grad[mask % 2, piece, lanes].astype(
+                bf16
+            )
+    if last:
+        r.drain("outputs")
     return gain_total
 
 
@@ -375,7 +374,6 @@
         grad_in = r.grad_mid[part, :] + grad_in
         if last:
             r.grad_next[part, :] = grad_in
-            r.grad_next_low[part, :] = grad_in.astype(bf16)
         else:
             seen = r.marks[part, 0:1] == 1
             r.grad_next[part, :] = jnp.where(seen, grad_in, 0.0)
@@ -402,30 +400,19 @@
     return high, (values - high).astype(bf16).astype(f32)
 
 
-def last_backward_body(r, sizes, piece_masks, ff_masks, heads):
+def last_ff_body(r, masks):
     r.small[...] = jnp.zeros(r.small.shape, f32)
-    put_row(r.small, 3, ff_backward(r, 1, True))
-    width = r.middle.shape[1]
-    for half in range(2):
-        r.ff_grad[half, :, : 2 * width] = dot_tn(r.ff_in[...], r.grad_gate_up[half])
-        r.ff_grad[half, :, 2 * width :] = dot_tn(r.hidden[half], r.grad[...])
-    half_count = len(ff_masks[0]) // 2
-    grain, columns = r.ff_keep.shape[1:]
-    for side, side_masks in enumerate(ff_masks):
-        lanes = slice(side * columns, (side + 1) * columns)
-        for idx, mask in enumerate(side_masks):
-            target = r.ff_keep if idx < half_count else r.ff_send
-            rows = pl.ds(pl.multiple_of((r.place[3] ^ (mask // 2)) * grain, grain), grain)
-            target[side * half_count + idx % half_count] = r.ff_grad[mask % 2, rows, lanes].astype(
-                bf16
-            )
+    put_row(r.small, 3, ff_backward(r, 1, True, masks))
+
+
+def last_attention_body(r, sizes, piece_masks, heads):
+    r.small[...] = r.small_before[...]
     put_row(r.small, 1, attention_backward(r, sizes, 1, True, piece_masks, heads))
-    r.drain("outputs")
-
-
-def ff_backward_body(r):
+
+
+def ff_backward_body(r, masks):
     r.small[...] = r.small_before[...]
-    put_row(r.small, 2, ff_backward(r, 0, False))
+    put_row(r.small, 2, ff_backward(r, 0, False, masks))
 
 
 def attention_backward_body(r, sizes, piece_masks, heads):
@@ -450,32 +437,6 @@
         target = keep if idx < count // 2 else send
         source = pl.ds(pl.multiple_of((place ^ mask) * grain, grain), grain)
         target[idx % (count // 2)] = whole[source, :].astype(bf16)
-
-
-def weight_body(r, piece_masks):
-    width = r.ff_in.shape[1]
-    rows = r.ff_in.shape[0]
-    r.fetch("peer_in", "peer_grad")
-    r.fetch("ff_in", "grad_gate_up", "hidden", "grad")
-    r.need("peer_in", "peer_grad")
-    for part in chunks(rows, 256):
-        both = dot_nn(r.peer_in[part, :], r.ff_gate_up[0])
-        grad_hidden = dot_nt(r.peer_grad[part, :], r.ff_down[0])
-        gate_act, up_act = both[:, :width], both[:, width:]
-        mixed, slope = gelu_terms(gate_act)
-        r.peer_gate_up[part, :width] = (grad_hidden * up_act * slope).astype(bf16)
-        r.peer_gate_up[part, width:] = (grad_hidden * mixed).astype(bf16)
-        r.peer_hidden[part, :] = (mixed * up_act).astype(bf16)
-    r.need("ff_in", "grad_gate_up", "hidden", "grad")
-    r.ff_grad[:, : 2 * width] = dot_tn(r.ff_in[...], r.grad_gate_up[0]) + dot_tn(
-        r.peer_in[...], r.peer_gate_up[...]
-    )
-    r.ff_grad[:, 2 * width :] = dot_tn(r.hidden[0], r.grad[...]) + dot_tn(
-        r.peer_hidden[...], r.peer_grad[...]
-    )
-    scatter_pieces(r.ff_grad, r.ff_keep, r.ff_send, piece_masks, r.place[3])
-    r.write("ff_send", "ff_keep")
-    r.drain("ff_send", "ff_keep")
 
 
 def finish(pieces, masks, layer_idx, place, shape, before=()):
@@ -507,7 +468,7 @@
             pltpu.VMEM((3, len(masks), grain, width), f32),
             pltpu.SemaphoreType.DMA,
         ],
-        compiler_params=pltpu.CompilerParams(vmem_limit_bytes=vmem_bytes),
+        compiler_params=pltpu.CompilerParams(vmem_limit_bytes=6 * mebibyte),
         cost_estimate=cost(3),
     )(place, pltpu.with_memory_space_constraint(pieces, pltpu.VMEM), *before)
 
@@ -668,7 +629,7 @@
             block_1 = join(block_1, tie(got_1, block_0))
         got_0 = swap(block_0, hops_0[-2])
         got_1 = swap(block_1, hops_1[-2])
-        block_0 = join(block_0, tie(got_0, start.a, got_ff_0))
+        block_0 = join(block_0, tie(got_0, start.a, got_ff_0, ff_1))
         block_1 = join(block_1, tie(got_1, block_0))
         ff_0 = join(ff_0, tie(got_ff_0, block_1))
         got_ff_1 = swap(tie(ff_1, ff_0), 4)
@@ -695,10 +656,9 @@
 
     def ff_ins(layer_idx):
         near, far = ff_pieces[layer_idx]
-        return dict(w_gate=w_gate, w_up=w_up, w_down=w_down, ff_near=Kept(near), ff_far=Kept(far))
-
-    attn_scratch = dict(attn_sem=pltpu.SemaphoreType.DMA)
-    ff_scratch = dict(ff_sem=pltpu.SemaphoreType.DMA)
+        own = keep_all(dict(w_gate=w_gate, w_up=w_up, w_down=w_down))
+        return dict(**own, ff_near=Kept(near), ff_far=Kept(far))
+
     ff_outs = dict(
         ff_gate_up=Kept((2, width, 2 * width), bf16), ff_down=Kept((2, width, width), bf16)
     )
@@ -729,13 +689,12 @@
                 **pieces,
             ),
             attn_outs,
-            attn_scratch,
+            {},
             after=after,
             micros=micros,
         )
 
     first = attention(0, start.x, start.a, micros=10)
-    peer_in_0 = swap(first.ff_in, 1)
     first_ff = run(
         ff_body,
         "layer_0_ff",
@@ -747,7 +706,7 @@
             **ff_ins(0),
         ),
         dict(**ff_outs, x_next=Kept(matrix, f32), a_next=Kept(matrix, bf16)),
-        ff_scratch,
+        {},
         after=after_first,
         micros=0.1,
     )
@@ -759,18 +718,17 @@
     second = attention(1, first_ff.x_next, first_ff.a_next, micros=0.1)
 
     attn_low = devices // attn_count
-    attn_hops = ([2, 1] + bits[2:], [2, 1] + bits[2:])
+    attn_hops = ([2, 1] + bits[2:], [2] + bits[3:] + bits[2:3] + [1])
     attn_split = [[hop for hop in hops if hop >= attn_low] for hops in attn_hops]
     attn_whole = [hop for hop in bits if hop < attn_low]
     attn_masks = [[mask // attn_low for mask in order_masks(hops)] for hops in attn_split]
-    ff_hops = (bits[1:], [2, 4, 1] + bits[3:], [2, 1, 4] + bits[3:])
+    ff_hops = ([2, 4, 1] + bits[3:], [2, 1, 4] + bits[3:])
     ff_split = [[hop for hop in hops if hop // 2 < ff_count] for hops in ff_hops]
     ff_whole = [hop for hop in bits[1:] if hop // 2 >= ff_count]
-    ff_share = ff_split[0][::-1]
+    ff_share = [hop for hop in bits[:0:-1] if hop // 2 < ff_count]
     ff_masks = [order_masks(hops) for hops in ff_split]
-    place_masks = [mask // 2 for mask in ff_masks[0]]
+    place_masks = [mask // 2 for mask in order_masks(ff_share[::-1])]
     attn_half = (attn_count // 2, attn_grain, 4 * inner)
-    ff_half = (ff_count // 2, ff_grain, 3 * width)
     small_shape = (heads + 2, 3 * width)
 
     attn_back_outs = dict(attn_keep=Kept(attn_half, bf16), attn_send=Kept(attn_half, bf16))
@@ -780,8 +738,19 @@
         grad_scores=pltpu.VMEM((rows, heads * slots), bf16),
         attn_grad=pltpu.VMEM((width, 4 * inner), f32),
     )
-    mid_scratch = dict(grad_mid=pltpu.VMEM(matrix, f32), branch=pltpu.VMEM(matrix, bf16))
-    pulled_scratch = dict(pulled=pltpu.VMEM((256, 2 * width), bf16))
+    ff_back_outs = dict(
+        ff_keep=Kept((2 * ff_count, ff_grain, 3 * width // 2), bf16),
+        ff_send=Kept((2 * ff_count, ff_grain, 3 * width // 2), bf16),
+        small=Kept(small_shape, f32),
+        grad_mid=Kept(matrix, f32),
+        branch=Kept(matrix, bf16),
+    )
+    ff_back_scratch = dict(
+        hidden=pltpu.VMEM((2, rows, width), bf16),
+        grad_gate_up=pltpu.VMEM((2, rows, 2 * width), bf16),
+        ff_grad=pltpu.VMEM((2, width, 3 * width), f32),
+        grad_low=pltpu.VMEM(matrix, bf16),
+    )
     bias_shape = (slots, heads * slots)
 
     def attn_back_ins(kept, x, a):
@@ -864,12 +833,7 @@
         out["done"] = piece.astype(f32)
         out["small"] = small
 
-    def first_ff_chain(part, out):
-        yield from halving(part.ff_keep, part.ff_send, ff_split[0], out)
-        yield from summing(out["piece"], ff_whole, out)
-        yield from sharing(out["piece"], ff_share, out)
-
-    def second_ff_chain(part, out):
+    def ff_chain(part, out):
         got = yield swap(part.ff_send, 2)
         count = ff_count
         keeps, sends = [], []
@@ -878,15 +842,14 @@
             sends.append(add(part.ff_keep[at + half : at + count], got[at + half : at + count]))
             keeps.append(add(part.ff_keep[at : at + half], got[at : at + half]))
         out["token"] = tuple(sends)
-        for hops in ((4, 1), (1, 4)):
+        for hops in zip(ff_split[0][1:3], ff_split[1][1:3]):
             got = yield tuple(swap(send, hop) for send, hop in zip(sends, hops))
-            count //= 2
-            half = count // 2
+            half = keeps[0].shape[0] // 2
             sends = [add(keep[half:], one[half:]) for keep, one in zip(keeps, got)]
             keeps = [add(keep[:half], one[:half]) for keep, one in zip(keeps, got)]
             out["token"] = tuple(sends)
         keep, send = (jnp.concatenate(sides, axis=2) for sides in (keeps, sends))
-        yield from halving(keep, send, ff_split[1][3:], out)
+        yield from halving(keep, send, ff_split[0][3:], out)
         yield from summing(out["piece"], ff_whole, out)
         yield from sharing(out["piece"], ff_share, out)
 
@@ -911,15 +874,9 @@
                 return self.out["token"]
             return token
 
-    back_1 = run(
-        functools.partial(
-            last_backward_body,
-            sizes=sizes,
-            piece_masks=attn_masks[1],
-            ff_masks=ff_masks[1:],
-            heads=heads,
-        ),
-        "layer_1_backward",
+    back_ff_1 = run(
+        functools.partial(last_ff_body, masks=ff_masks),
+        "layer_1_ff",
         dict(
             place=place,
             grad=cotangent,
@@ -927,36 +884,47 @@
             middle=Kept(second.middle),
             ff_in=Kept(second.ff_in),
             **ff_ins(1),
-            **attn_back_ins(second, first_ff.x_next, first_ff.a_next),
-        ),
-        dict(
-            ff_keep=Kept((2 * ff_count, ff_grain, 3 * width // 2), bf16),
-            ff_send=Kept((2 * ff_count, ff_grain, 3 * width // 2), bf16),
-            small=Kept(small_shape, f32),
-            **attn_back_outs,
-            outputs=(matrix, bf16),
-            grad_next=Kept(matrix, f32),
-            grad_next_low=Kept(matrix, bf16),
-            bias_acc=Kept(bias_shape, f32),
-        ),
+        ),
+        dict(**ff_back_outs, outputs=(matrix, bf16)),
         dict(
             ff_gate_up=pltpu.VMEM((2, width, 2 * width), bf16),
             ff_down=pltpu.VMEM((2, width, width), bf16),
-            hidden=pltpu.VMEM((2, rows, width), bf16),
-            grad_gate_up=pltpu.VMEM((2, rows, 2 * width), bf16),
-            ff_grad=pltpu.VMEM((2, width, 3 * width), f32),
-            **mid_scratch,
-            **attn_back_scratch,
-            **ff_scratch,
-        ),
-        micros=10,
-    )
-    peer_grad_0 = swap(back_1.grad_next_low, 1)
+            **ff_back_scratch,
+        ),
+        micros=8,
+        vmem=24,
+    )
+    ff_1 = Chain(ff_chain, back_ff_1)
+    back_1 = run(
+        functools.partial(
+            last_attention_body, sizes=sizes, piece_masks=attn_masks[1], heads=heads
+        ),
+        "layer_1_attention_backward",
+        dict(
+            place=place,
+            small_before=Kept(back_ff_1.small),
+            grad_mid=Kept(back_ff_1.grad_mid),
+            branch=Kept(back_ff_1.branch),
+            **attn_back_ins(second, first_ff.x_next, first_ff.a_next),
+        ),
+        dict(
+            **attn_back_outs,
+            small=Kept(small_shape, f32),
+            grad_next=Kept(matrix, f32),
+            bias_acc=Kept(bias_shape, f32),
+        ),
+        attn_back_scratch,
+        micros=6,
+        vmem=14,
+    )
     attn_1 = Chain(attn_chain, back_1, 1)
+    token = ff_1.step(back_1.attn_send)
+    token = (attn_1.step(token),)
     back_0 = run(
-        ff_backward_body,
+        functools.partial(ff_backward_body, masks=ff_masks),
         "layer_0_ff_backward",
         dict(
+            place=place,
             grad=Kept(back_1.grad_next),
             gain_ff=gain_ff,
             small_before=Kept(back_1.small),
@@ -965,19 +933,16 @@
             ff_gate_up=Kept(first_ff.ff_gate_up),
             ff_down=Kept(first_ff.ff_down),
         ),
-        dict(
-            hidden=Kept((1, rows, width), bf16),
-            grad_gate_up=Kept((1, rows, 2 * width), bf16),
-            small=Kept(small_shape, f32),
-            grad_mid=Kept(matrix, f32),
-            branch=Kept(matrix, bf16),
-        ),
-        pulled_scratch,
-        after=(peer_in_0,),
-        micros=10,
-    )
-    ff_1 = Chain(second_ff_chain, back_1)
+        ff_back_outs,
+        ff_back_scratch,
+        after=token,
+        micros=8,
+        vmem=20,
+    )
     token = ff_1.step(back_0.branch)
+    back_0.ff_send = tie(back_0.ff_send, *token)
+    ff_0 = Chain(ff_chain, back_0)
+    token = ff_0.step(token)
     back_attn_0 = run(
         functools.partial(
             attention_backward_body, sizes=sizes, piece_masks=attn_masks[0], heads=heads
@@ -1006,39 +971,16 @@
         ),
         after=token,
         micros=7,
+        vmem=14,
     )
     attn_0 = Chain(attn_chain, back_attn_0, 0)
-    token = attn_1.step(back_attn_0.attn_send, peer_grad_0)
-    part_0 = run(
-        functools.partial(weight_body, piece_masks=place_masks),
-        "layer_0_weight_grads",
-        dict(
-            place=place,
-            ff_in=Kept(first.ff_in),
-            grad=Kept(back_1.grad_next_low),
-            hidden=Kept(back_0.hidden),
-            grad_gate_up=Kept(back_0.grad_gate_up),
-            peer_in=Kept(peer_in_0),
-            peer_grad=Kept(peer_grad_0),
-            ff_gate_up=Kept(first_ff.ff_gate_up),
-            ff_down=Kept(first_ff.ff_down),
-        ),
-        dict(ff_keep=Kept(ff_half, bf16), ff_send=Kept(ff_half, bf16)),
-        dict(
-            peer_gate_up=pltpu.VMEM((rows, 2 * width), bf16),
-            peer_hidden=pltpu.VMEM(matrix, bf16),
-            ff_grad=pltpu.VMEM((width, 3 * width), f32),
-        ),
-        after=(token,),
-        micros=4,
-    )
-    ff_0 = Chain(first_ff_chain, part_0)
-    token = part_0.ff_send
+    token = back_attn_0.attn_send
     shape = (2, width, width)
     near_masks = place_masks[: ff_count // 2]
     far_masks = place_masks[ff_count // 2 :]
     done = ()
     ended = False
+    turn = 0
     sums = attn_grads = None
     while ff_0.arriving is not None:
         token = ff_1.step(token)
@@ -1049,8 +991,11 @@
             done = finish(tie(ff_1.out["far"], token), far_masks, 1, place, shape, done)
             token = done[0]
             ended = True
-        for chain in (ff_0, attn_0, attn_1):
-            token = chain.step(token)
+        turn += 1
+        token = ff_0.step(token)
+        if turn != 2:
+            token = attn_0.step(token)
+        token = attn_1.step(token)
         if sums is None and attn_0.arriving is None:
             sums = run(
                 small_body,
@@ -1075,7 +1020,7 @@
     for pieces, masks in ((ff_0.out["near"], near_masks), (ff_0.out["far"], far_masks)):
         done = finish(pieces, masks, 0, place, shape, done)
     return (
-        back_1.outputs.reshape(inputs.shape),
+        back_ff_1.outputs.reshape(inputs.shape),
         back_attn_0.grad_next.reshape(inputs.shape),
         *attn_grads,
         *done,

time: 179 us -> 167 us (0.933); the launches traced: 176 us -> 166 us
  Pallas kernels: 51.2 us -> 44.1 us
  waiting for transfers between devices: 69.3 us -> 64.5 us
  starting transfers between devices: 40.6 us -> 43.4 us
  other arithmetic: 9.34 us -> 6.91 us
    pallas_call x10, Pallas kernels: 44.6 us -> 37.4 us  [run(): pl.pallas_call(kernel, name=name, in_specs=[pl.BlockSpec(memory_space=in_...]
    ppermute x47 -> x48, waiting for transfers between devices: 69.3 us -> 64.5 us  [swap(): return lax.ppermute(array, axes, [(n, n ^ mask) for n in range(devices)])]
    concatenate x24, other arithmetic: 5.53 us -> 1.83 us  [join(): return jnp.concatenate([left, right], axis=0)]
    ppermute x47 -> x48, starting transfers between devices: 40.6 us -> 43.4 us  [swap(): return lax.ppermute(array, axes, [(n, n ^ mask) for n in range(devices)])]
  transfers between devices with their start and end apart: 47 -> 48, of which waited for: 23 -> 21; matrix products, arithmetic and copies ran while one was open for 7% -> 6% of each run, Pallas kernels for 27% -> 21%
where the time goes in v8:
time: 167 us; the launch traced here: 166 us
  waiting for transfers between devices  64.5 us (39%)
  Pallas kernels  44.1 us (26%)
  starting transfers between devices  43.4 us (26%)
  other arithmetic  6.91 us (4%)
  local copies, waits for them, and re-layouts  5.63 us (3%)
  between operations  1.69 us (1%)
    ppermute x48, waiting for transfers between devices, swap(): return lax.ppermute(array, axes, [(n, n ^ mask) for n in range(devices)])  64.5 us
    ppermute x48, starting transfers between devices, swap(): return lax.ppermute(array, axes, [(n, n ^ mask) for n in range(devices)])  43.4 us
    pallas_call x10, Pallas kernels, run(): pl.pallas_call(kernel, name=name, in_specs=[pl.BlockSpec(memory_space=in_...  37.4 us
    pallas_call x4, Pallas kernels, finish(): pl.pallas_call(kernel, name='layer_%d_ff_grads' % layer_idx, in_specs=[pl...  6.67 us
  transfers between devices with their start and end apart: 48, of which 21 were waited for; matrix products, arithmetic and copies ran while one was open for 6% of the time, Pallas kernels for 21%

profile of v8, /device:TPU:0, one launch (start us, length us, event | category | flops | bytes accessed | tf_op | source)
XLA Modules:
  0.0 166.2 jit_solution(17767423808907485015)
XLA Ops:
  1.5 3.0 %collective-permute-start.1 = (bf16[16,1536]{1,0:T(8,128)(2,1)S(1)}, bf16[16,1536]{1,0:T(8,128)(2,1)S(1)}, u32[]{:S(2)}, u32[]{:S(2)}) collective-permute-start(bf16[16,1536]{1,0:T(8,128)(2,1)S(1)} %get-tuple-element.285), channel_id=1, source_target_pairs={{0,1},{1,0},{2,3},{3,2},{4,5},{5,4},{6,7},{7,6},{8,9},{9,8},{10,11... | collective-permute-start | bytes 147464 | tf_op jit(solution)/shard_map/ppermute | solution.py:543
  4.5 2.6 %collective-permute-start = (bf16[16,1536]{1,0:T(8,128)(2,1)S(1)}, bf16[16,1536]{1,0:T(8,128)(2,1)S(1)}, u32[]{:S(2)}, u32[]{:S(2)}) collective-permute-start(bf16[16,1536]{1,0:T(8,128)(2,1)S(1)} %get-tuple-element.286), channel_id=1, source_target_pairs={{0,16},{1,17},{2,18},{3,19},{4,20},{5,21},{6,22},{7,23},{8,24},{9,... | collective-permute-start | bytes 147464 | tf_op jit(solution)/shard_map/ppermute | solution.py:543
  23.5 3.5 %collective-permute-done.3 = bf16[64,1536]{1,0:T(8,128)(2,1)S(1)} collective-permute-done((bf16[64,1536]{1,0:T(8,128)(2,1)S(1)}, bf16[64,1536]{1,0:T(8,128)(2,1)S(1)}, u32[]{:S(2)}, u32[]{:S(2)}) %collective-permute-start.3) | collective-permute-done | bytes 196640 | tf_op jit(solution)/shard_map/ppermute | solution.py:543
  29.2 2.2 %collective-permute-start.6 = (bf16[3,128,512]{2,1,0:T(8,128)(2,1)S(1)}, bf16[3,128,512]{2,1,0:T(8,128)(2,1)S(1)}, u32[]{:S(2)}, u32[]{:S(2)}) collective-permute-start(bf16[3,128,512]{2,1,0:T(8,128)(2,1)S(1)} %collective-permute-done.5), channel_id=1, source_target_pairs={{0,4},{1,5},{2,6},{3,7},{4,0},{5,1},{6,2},{7,3},{8,12},{9,13},{10,... | collective-permute-start | bytes 1179656 | tf_op jit(solution)/shard_map/ppermute | solution.py:543
  33.2 2.8 %collective-permute-done.4 = bf16[128,1536]{1,0:T(8,128)(2,1)S(1)} collective-permute-done((bf16[128,1536]{1,0:T(8,128)(2,1)S(1)}, bf16[128,1536]{1,0:T(8,128)(2,1)S(1)}, u32[]{:S(2)}, u32[]{:S(2)}) %collective-permute-start.4) | collective-permute-done | bytes 393248 | tf_op jit(solution)/shard_map/ppermute | solution.py:543
  36.0 4.6 %collective-permute-done.7 = bf16[3,128,512]{2,1,0:T(8,128)(2,1)S(1)} collective-permute-done((bf16[3,128,512]{2,1,0:T(8,128)(2,1)S(1)}, bf16[3,128,512]{2,1,0:T(8,128)(2,1)S(1)}, u32[]{:S(2)}, u32[]{:S(2)}) %collective-permute-start.7) | collective-permute-done | bytes 393248 | tf_op jit(solution)/shard_map/ppermute | solution.py:543
  40.8 4.0 %collective-permute-done.11 = bf16[128,1536]{1,0:T(8,128)(2,1)S(1)} collective-permute-done((bf16[128,1536]{1,0:T(8,128)(2,1)S(1)}, bf16[128,1536]{1,0:T(8,128)(2,1)S(1)}, u32[]{:S(2)}, u32[]{:S(2)}) %collective-permute-start.11) | collective-permute-done | bytes 393248 | tf_op jit(solution)/shard_map/ppermute | solution.py:543
  45.8 2.8 %layer_0_attention.1 = (bf16[512,1536]{1,0:T(8,128)(2,1)S(1)}, bf16[512,1152]{1,0:T(8,128)(2,1)S(1)}, f32[512,384]{1,0:T(8,128)S(1)}, bf16[512,384]{1,0:T(8,128)...) custom-call(s32[4]{0:T(128)S(1)} %pad_add_fusion.1.refs_0_.place_ref, ...), custom_call_target="tpu_custom_call" | custom-call | flops 11500000256 | tf_op jit(solution)/shard_map/layer_0_attention/pallas_call | solution.py:98
  48.7 3.1 %layer_0_ff.1 = (bf16[2,512,1024]{2,1,0:T(8,128)(2,1)S(1)}, bf16[2,512,512]{2,1,0:T(8,128)(2,1)S(1)}, f32[512,512]{1,0:T(8,128)S(1)}, bf16[512,512]{1,0:T(8,128)(2,1)S(1)}) custom-call(s32[4]{0:T(128)S(1)} %pad_add_fusion.1.refs_0_.place_ref, f32[512,512]{1,0:T(8,128)S(1)} %get-tuple-element.136.refs_1_.refs_4_, ...), custom_call_target="tpu_custom_call" | custom-call | flops 115000000 | tf_op jit(solution)/shard_map/layer_0_ff/pallas_call | solution.py:98
  51.8 4.7 %collective-permute-done.14 = bf16[3,128,512]{2,1,0:T(8,128)(2,1)S(1)} collective-permute-done((bf16[3,128,512]{2,1,0:T(8,128)(2,1)S(1)}, bf16[3,128,512]{2,1,0:T(8,128)(2,1)S(1)}, u32[]{:S(2)}, u32[]{:S(2)}) %collective-permute-start.14) | collective-permute-done | bytes 393248 | tf_op jit(solution)/shard_map/ppermute | solution.py:543
  56.6 2.8 %layer_1_attention.1 = (bf16[512,1536]{1,0:T(8,128)(2,1)S(1)}, bf16[512,1152]{1,0:T(8,128)(2,1)S(1)}, f32[512,384]{1,0:T(8,128)S(1)}, bf16[512,384]{1,0:T(8,128)...) custom-call(s32[4]{0:T(128)S(1)} %pad_add_fusion.1.refs_0_.place_ref, ...), custom_call_target="tpu_custom_call" | custom-call | flops 115000000 | tf_op jit(solution)/shard_map/layer_1_attention/pallas_call | solution.py:98
  59.4 7.4 %layer_1_ff.1 = (bf16[32,32,768]{2,1,0:T(8,128)(2,1)S(1)}, bf16[32,32,768]{2,1,0:T(8,128)(2,1)S(1)}, f32[8,1536]{1,0:T(8,128)S(1)}, f32[512,512]{1,0:T(8,128)S(1...) custom-call(s32[4]{0:T(128)S(1)} %pad_add_fusion.1.refs_0_.place_ref, bf16[512,512]{1,0:T(8,128)(2,1)S(1)} %bitcast.67, ...), custom_call_target="tpu_custom_call" | custom-call | flops 9200000000 | tf_op jit(solution)/shard_map/layer_1_ff/pallas_call | solution.py:98
  67.4 4.5 %layer_1_attention_backward.1 = (bf16[16,16,1536]{2,1,0:T(8,128)(2,1)S(1)}, bf16[16,16,1536]{2,1,0:T(8,128)(2,1)S(1)}, f32[8,1536]{1,0:T(8,128)S(1)}, f32[512,512]{1,0:T(8,128)S(1)}, f32[64,384]{1,0:T(8,128)S(1)}) custom-call(s32[4]{0:T(128)S(1)} %pad_add_fusion.1.refs_0_.place_ref, f32[8,1536]{1,0:T(8,128)S(1)} %get-tuple-element.150.refs_1_, ...), custom_call_target="tpu_custom_call" | custom-call | flops 6899999744 | tf_op jit(solution)/shard_map/layer_1_attention_backward/pallas_call | solution.py:98
  74.5 7.0 %layer_0_ff_backward.1 = (bf16[32,32,768]{2,1,0:T(8,128)(2,1)S(1)}, bf16[32,32,768]{2,1,0:T(8,128)(2,1)S(1)}, f32[8,1536]{1,0:T(8,128)S(1)}, f32[512,512]{1,0:T(8,128)S(1)}, bf16[512,512]{1,0:T(8,128)(2,1)S(1)}) custom-call(s32[4]{0:T(128)S(1)} %pad_add_fusion.1.refs_0_.place_ref, f32[512,512]{1,0:T(8,128)S(1)} %get-tuple-element.158.refs_1_, ...), custom_call_target="tpu_custom_call" | custom-call | flops 9200000000 | tf_op jit(solution)/shard_map/layer_0_ff_backward/pallas_call | solution.py:98
  81.5 2.6 %collective-permute-done.19 = bf16[8,32,768]{2,1,0:T(8,128)(2,1)S(1)} collective-permute-done((bf16[8,32,768]{2,1,0:T(8,128)(2,1)S(1)}, bf16[8,32,768]{2,1,0:T(8,128)(2,1)S(1)}, u32[]{:S(2)}, u32[]{:S(2)}) %collective-permute-start.19) | collective-permute-done | bytes 393248 | tf_op jit(solution)/shard_map/ppermute | solution.py:543
  91.0 6.4 %layer_0_attention_backward.1 = (bf16[16,16,1536]{2,1,0:T(8,128)(2,1)S(1)}, bf16[17,16,1536]{2,1,0:T(8,128)(2,1)S(1)}, f32[8,1536]{1,0:T(8,128)S(1)}, f32[512,512]{1,0:T(8,128)}) custom-call(s32[4]{0:T(128)S(1)} %pad_add_fusion.1.refs_0_.place_ref, f32[64,384]{1,0:T(8,128)S(1)} %get-tuple-element.157.refs_1_, s32[512,2]{1,0:T(8,128)S(1)} %copy.46.refs_1_.refs_2_, ...), custom_call_target="tpu_custom_call" | custom-call | flops 8049999872 | tf_op jit(solution)/shard_map/layer_0_attention_backward/pallas_call | solution.py:98
  99.0 3.2 %collective-permute-done.23 = bf16[8,32,768]{2,1,0:T(8,128)(2,1)S(1)} collective-permute-done((bf16[8,32,768]{2,1,0:T(8,128)(2,1)S(1)}, bf16[8,32,768]{2,1,0:T(8,128)(2,1)S(1)}, u32[]{:S(2)}, u32[]{:S(2)}) %collective-permute-start.23) | collective-permute-done | bytes 393248 | tf_op jit(solution)/shard_map/ppermute | solution.py:543
  106.3 2.3 %collective-permute-start.33 = (bf16[4,16,1536]{2,1,0:T(8,128)(2,1)S(1)}, bf16[4,16,1536]{2,1,0:T(8,128)(2,1)S(1)}, u32[]{:S(2)}, u32[]{:S(2)}) collective-permute-start(bf16[4,16,1536]{2,1,0:T(8,128)(2,1)S(1)} %get-tuple-element.258), channel_id=1, source_target_pairs={{0,16},{1,17},{2,18},{3,19},{4,20},{5,21},{6,22},{7,23},{8,24},{9,... | collective-permute-start | bytes 589832 | tf_op jit(solution)/shard_map/ppermute | solution.py:543
  109.4 2.2 %collective-permute-done.27 = bf16[4,32,768]{2,1,0:T(8,128)(2,1)S(1)} collective-permute-done((bf16[4,32,768]{2,1,0:T(8,128)(2,1)S(1)}, bf16[4,32,768]{2,1,0:T(8,128)(2,1)S(1)}, u32[]{:S(2)}, u32[]{:S(2)}) %collective-permute-start.27) | collective-permute-done | bytes 196640 | tf_op jit(solution)/shard_map/ppermute | solution.py:543
  112.6 6.7 %collective-permute-done.33 = bf16[4,16,1536]{2,1,0:T(8,128)(2,1)S(1)} collective-permute-done((bf16[4,16,1536]{2,1,0:T(8,128)(2,1)S(1)}, bf16[4,16,1536]{2,1,0:T(8,128)(2,1)S(1)}, u32[]{:S(2)}, u32[]{:S(2)}) %collective-permute-start.33) | collective-permute-done | bytes 196640 | tf_op jit(solution)/shard_map/ppermute | solution.py:543
  126.2 4.3 %collective-permute-done.36 = bf16[1,32,1536]{2,1,0:T(8,128)(2,1)S(1)} collective-permute-done((bf16[1,32,1536]{2,1,0:T(8,128)(2,1)S(1)}, bf16[1,32,1536]{2,1,0:T(8,128)(2,1)S(1)}, u32[]{:S(2)}, u32[]{:S(2)}) %collective-permute-start.36) | collective-permute-done | bytes 98336 | tf_op jit(solution)/shard_map/ppermute | solution.py:543
  134.5 6.0 %collective-permute-done.40 = bf16[2,32,1536]{2,1,0:T(8,128)(2,1)S(1)} collective-permute-done((bf16[2,32,1536]{2,1,0:T(8,128)(2,1)S(1)}, bf16[2,32,1536]{2,1,0:T(8,128)(2,1)S(1)}, u32[]{:S(2)}, u32[]{:S(2)}) %collective-permute-start.40) | collective-permute-done | bytes 196640 | tf_op jit(solution)/shard_map/ppermute | solution.py:543
  143.8 4.7 %collective-permute-done.44 = bf16[4,32,1536]{2,1,0:T(8,128)(2,1)S(1)} collective-permute-done((bf16[4,32,1536]{2,1,0:T(8,128)(2,1)S(1)}, bf16[4,32,1536]{2,1,0:T(8,128)(2,1)S(1)}, u32[]{:S(2)}, u32[]{:S(2)}) %collective-permute-start.44) | collective-permute-done | bytes 393248 | tf_op jit(solution)/shard_map/ppermute | solution.py:543
  153.5 8.3 %collective-permute-done.45 = bf16[4,32,1536]{2,1,0:T(8,128)(2,1)S(1)} collective-permute-done((bf16[4,32,1536]{2,1,0:T(8,128)(2,1)S(1)}, bf16[4,32,1536]{2,1,0:T(8,128)(2,1)S(1)}, u32[]{:S(2)}, u32[]{:S(2)}) %collective-permute-start.45) | collective-permute-done | bytes 393248 | tf_op jit(solution)/shard_map/ppermute | solution.py:543
  (204 shorter events, 62.8 us)
Async XLA Ops:
  10.3 11.0 %collective-permute-start.2 = (bf16[32,1536]{1,0:T(8,128)(2,1)}, bf16[32,1536]{1,0:T(8,128)(2,1)S(1)}, u32[]{:S(2)}, u32[]{:S(2)}) collective-permute-start(bf16[32,1536]{1,0:T(8,128)(2,1)} %pad_maximum_fusion.15), channel_id=1, source_target_pairs={{0,16},{1,17},{2,18},{3,19},{4,20},{5,21},{6,22},{7,23},{8,24},{9,... | collective-permute-start | bytes 294920 | tf_op jit(solution)/shard_map/ppermute | solution.py:543
  12.2 9.6 %collective-permute-start.9 = (bf16[32,1536]{1,0:T(8,128)(2,1)}, bf16[32,1536]{1,0:T(8,128)(2,1)S(1)}, u32[]{:S(2)}, u32[]{:S(2)}) collective-permute-start(bf16[32,1536]{1,0:T(8,128)(2,1)} %pad_maximum_fusion.16), channel_id=1, source_target_pairs={{0,4},{1,5},{2,6},{3,7},{4,0},{5,1},{6,2},{7,3},{8,12},{9,13},{10,... | collective-permute-start | bytes 294920 | tf_op jit(solution)/shard_map/ppermute | solution.py:543
  17.8 10.9 %collective-permute-start.5 = (bf16[3,128,512]{2,1,0:T(8,128)(2,1)S(1)}, bf16[3,128,512]{2,1,0:T(8,128)(2,1)S(1)}, u32[]{:S(2)}, u32[]{:S(2)}) collective-permute-start(bf16[3,128,512]{2,1,0:T(8,128)(2,1)S(1)} %get-tuple-element.132), channel_id=1, source_target_pairs={{0,1},{1,0},{2,3},{3,2},{4,5},{5,4},{6,7},{7,6},{8,9},{9,8},{10,11... | collective-permute-start | bytes 1179656 | tf_op jit(solution)/shard_map/ppermute | solution.py:543
  28.7 11.9 %collective-permute-start.7 = (bf16[3,128,512]{2,1,0:T(8,128)(2,1)S(1)}, bf16[3,128,512]{2,1,0:T(8,128)(2,1)S(1)}, u32[]{:S(2)}, u32[]{:S(2)}) collective-permute-start(bf16[3,128,512]{2,1,0:T(8,128)(2,1)S(1)} %get-tuple-element.134), channel_id=1, source_target_pairs={{0,1},{1,0},{2,3},{3,2},{4,5},{5,4},{6,7},{7,6},{8,9},{9,8},{10,11... | collective-permute-start | bytes 1179656 | tf_op jit(solution)/shard_map/ppermute | solution.py:543
  29.2 11.4 %collective-permute-start.6 = (bf16[3,128,512]{2,1,0:T(8,128)(2,1)S(1)}, bf16[3,128,512]{2,1,0:T(8,128)(2,1)S(1)}, u32[]{:S(2)}, u32[]{:S(2)}) collective-permute-start(bf16[3,128,512]{2,1,0:T(8,128)(2,1)S(1)} %collective-permute-done.5), channel_id=1, source_target_pairs={{0,4},{1,5},{2,6},{3,7},{4,0},{5,1},{6,2},{7,3},{8,12},{9,13},{10,... | collective-permute-start | bytes 1179656 | tf_op jit(solution)/shard_map/ppermute | solution.py:543
  31.4 13.4 %collective-permute-start.11 = (bf16[128,1536]{1,0:T(8,128)(2,1)S(1)}, bf16[128,1536]{1,0:T(8,128)(2,1)S(1)}, u32[]{:S(2)}, u32[]{:S(2)}) collective-permute-start(bf16[128,1536]{1,0:T(8,128)(2,1)S(1)} %pad_maximum_fusion.3), channel_id=1, source_target_pairs={{0,1},{1,0},{2,3},{3,2},{4,5},{5,4},{6,7},{7,6},{8,9},{9,8},{10,11... | collective-permute-start | bytes 1179656 | tf_op jit(solution)/shard_map/ppermute | solution.py:543
  45.0 11.5 %collective-permute-start.14 = (bf16[3,128,512]{2,1,0:T(8,128)(2,1)S(1)}, bf16[3,128,512]{2,1,0:T(8,128)(2,1)S(1)}, u32[]{:S(2)}, u32[]{:S(2)}) collective-permute-start(bf16[3,128,512]{2,1,0:T(8,128)(2,1)S(1)} %collective-permute-done.7), channel_id=1, source_target_pairs={{0,4},{1,5},{2,6},{3,7},{4,0},{5,1},{6,2},{7,3},{8,12},{9,13},{10,... | collective-permute-start | bytes 1179656 | tf_op jit(solution)/shard_map/ppermute | solution.py:543
  72.6 11.6 %collective-permute-start.19 = (bf16[8,32,768]{2,1,0:T(8,128)(2,1)S(1)}, bf16[8,32,768]{2,1,0:T(8,128)(2,1)S(1)}, u32[]{:S(2)}, u32[]{:S(2)}) collective-permute-start(bf16[8,32,768]{2,1,0:T(8,128)(2,1)S(1)} %get-tuple-element.249), channel_id=1, source_target_pairs={{0,1},{1,0},{2,3},{3,2},{4,5},{5,4},{6,7},{7,6},{8,9},{9,8},{10,11... | collective-permute-start | bytes 1179656 | tf_op jit(solution)/shard_map/ppermute | solution.py:543
  73.5 11.2 %collective-permute-start.18 = (bf16[8,32,768]{2,1,0:T(8,128)(2,1)S(1)}, bf16[8,32,768]{2,1,0:T(8,128)(2,1)S(1)}, u32[]{:S(2)}, u32[]{:S(2)}) collective-permute-start(bf16[8,32,768]{2,1,0:T(8,128)(2,1)S(1)} %get-tuple-element.250), channel_id=1, source_target_pairs={{0,4},{1,5},{2,6},{3,7},{4,0},{5,1},{6,2},{7,3},{8,12},{9,13},{10,... | collective-permute-start | bytes 1179656 | tf_op jit(solution)/shard_map/ppermute | solution.py:543
  84.9 21.2 %collective-permute-start.30 = (bf16[8,16,1536]{2,1,0:T(8,128)(2,1)S(1)}, bf16[8,16,1536]{2,1,0:T(8,128)(2,1)S(1)}, u32[]{:S(2)}, u32[]{:S(2)}) collective-permute-start(bf16[8,16,1536]{2,1,0:T(8,128)(2,1)S(1)} %get-tuple-element.254.refs_8_), channel_id=1, source_target_pairs={{0,8},{1,9},{2,10},{3,11},{4,12},{5,13},{6,14},{7,15},{8,0},{9,1},... | collective-permute-start | bytes 1179656 | tf_op jit(solution)/shard_map/ppermute | solution.py:543
  86.3 11.1 %collective-permute-start.25 = (bf16[4,32,768]{2,1,0:T(8,128)(2,1)S(1)}, bf16[4,32,768]{2,1,0:T(8,128)(2,1)S(1)}, u32[]{:S(2)}, u32[]{:S(2)}) collective-permute-start(bf16[4,32,768]{2,1,0:T(8,128)(2,1)S(1)} %get-tuple-element.264), channel_id=1, source_target_pairs={{0,4},{1,5},{2,6},{3,7},{4,0},{5,1},{6,2},{7,3},{8,12},{9,13},{10,... | collective-permute-start | bytes 589832 | tf_op jit(solution)/shard_map/ppermute | solution.py:543
  87.0 10.5 %collective-permute-start.24 = (bf16[4,32,768]{2,1,0:T(8,128)(2,1)S(1)}, bf16[4,32,768]{2,1,0:T(8,128)(2,1)S(1)}, u32[]{:S(2)}, u32[]{:S(2)}) collective-permute-start(bf16[4,32,768]{2,1,0:T(8,128)(2,1)S(1)} %get-tuple-element.266), channel_id=1, source_target_pairs={{0,1},{1,0},{2,3},{3,2},{4,5},{5,4},{6,7},{7,6},{8,9},{9,8},{10,11... | collective-permute-start | bytes 589832 | tf_op jit(solution)/shard_map/ppermute | solution.py:543
  88.9 13.2 %collective-permute-start.23 = (bf16[8,32,768]{2,1,0:T(8,128)(2,1)S(1)}, bf16[8,32,768]{2,1,0:T(8,128)(2,1)S(1)}, u32[]{:S(2)}, u32[]{:S(2)}) collective-permute-start(bf16[8,32,768]{2,1,0:T(8,128)(2,1)S(1)} %get-tuple-element.245.refs_15_), channel_id=1, source_target_pairs={{0,1},{1,0},{2,3},{3,2},{4,5},{5,4},{6,7},{7,6},{8,9},{9,8},{10,11... | collective-permute-start | bytes 1179656 | tf_op jit(solution)/shard_map/ppermute | solution.py:543
  90.2 11.9 %collective-permute-start.22 = (bf16[8,32,768]{2,1,0:T(8,128)(2,1)S(1)}, bf16[8,32,768]{2,1,0:T(8,128)(2,1)S(1)}, u32[]{:S(2)}, u32[]{:S(2)}) collective-permute-start(bf16[8,32,768]{2,1,0:T(8,128)(2,1)S(1)} %get-tuple-element.246.refs_14_), channel_id=1, source_target_pairs={{0,4},{1,5},{2,6},{3,7},{4,0},{5,1},{6,2},{7,3},{8,12},{9,13},{10,... | collective-permute-start | bytes 1179656 | tf_op jit(solution)/shard_map/ppermute | solution.py:543
  97.6 11.0 %collective-permute-start.29 = (bf16[2,32,1536]{2,1,0:T(8,128)(2,1)S(1)}, bf16[2,32,1536]{2,1,0:T(8,128)(2,1)S(1)}, u32[]{:S(2)}, u32[]{:S(2)}) collective-permute-start(bf16[2,32,1536]{2,1,0:T(8,128)(2,1)S(1)} %pad_maximum_fusion.8), channel_id=1, source_target_pairs={{0,8},{1,9},{2,10},{3,11},{4,12},{5,13},{6,14},{7,15},{8,0},{9,1},... | collective-permute-start | bytes 589832 | tf_op jit(solution)/shard_map/ppermute | solution.py:543
  105.0 19.0 %collective-permute-start.26 = (bf16[9,16,1536]{2,1,0:T(8,128)(2,1)S(1)}, bf16[9,16,1536]{2,1,0:T(8,128)(2,1)S(1)}, u32[]{:S(2)}, u32[]{:S(2)}) collective-permute-start(bf16[9,16,1536]{2,1,0:T(8,128)(2,1)S(1)} %maximum_maximum_fusion), channel_id=1, source_target_pairs={{0,1},{1,0},{2,3},{3,2},{4,5},{5,4},{6,7},{7,6},{8,9},{9,8},{10,11... | collective-permute-start | bytes 1327112 | tf_op jit(solution)/shard_map/ppermute | solution.py:543
  106.3 12.9 %collective-permute-start.33 = (bf16[4,16,1536]{2,1,0:T(8,128)(2,1)S(1)}, bf16[4,16,1536]{2,1,0:T(8,128)(2,1)S(1)}, u32[]{:S(2)}, u32[]{:S(2)}) collective-permute-start(bf16[4,16,1536]{2,1,0:T(8,128)(2,1)S(1)} %get-tuple-element.258), channel_id=1, source_target_pairs={{0,16},{1,17},{2,18},{3,19},{4,20},{5,21},{6,22},{7,23},{8,24},{9,... | collective-permute-start | bytes 589832 | tf_op jit(solution)/shard_map/ppermute | solution.py:543
  108.7 12.1 %collective-permute-start.32 = (bf16[1,32,1536]{2,1,0:T(8,128)(2,1)S(1)}, bf16[1,32,1536]{2,1,0:T(8,128)(2,1)S(1)}, u32[]{:S(2)}, u32[]{:S(2)}) collective-permute-start(bf16[1,32,1536]{2,1,0:T(8,128)(2,1)S(1)} %add_convert_fusion.37), channel_id=1, source_target_pairs={{0,16},{1,17},{2,18},{3,19},{4,20},{5,21},{6,22},{7,23},{8,24},{9,... | collective-permute-start | bytes 294920 | tf_op jit(solution)/shard_map/ppermute | solution.py:543
  111.7 10.1 %collective-permute-start.31 = (bf16[2,32,1536]{2,1,0:T(8,128)(2,1)S(1)}, bf16[2,32,1536]{2,1,0:T(8,128)(2,1)S(1)}, u32[]{:S(2)}, u32[]{:S(2)}) collective-permute-start(bf16[2,32,1536]{2,1,0:T(8,128)(2,1)S(1)} %pad_maximum_fusion.9), channel_id=1, source_target_pairs={{0,8},{1,9},{2,10},{3,11},{4,12},{5,13},{6,14},{7,15},{8,0},{9,1},... | collective-permute-start | bytes 589832 | tf_op jit(solution)/shard_map/ppermute | solution.py:543
  120.8 9.7 %collective-permute-start.36 = (bf16[1,32,1536]{2,1,0:T(8,128)(2,1)S(1)}, bf16[1,32,1536]{2,1,0:T(8,128)(2,1)S(1)}, u32[]{:S(2)}, u32[]{:S(2)}) collective-permute-start(bf16[1,32,1536]{2,1,0:T(8,128)(2,1)S(1)} %add_convert_fusion.30), channel_id=1, source_target_pairs={{0,16},{1,17},{2,18},{3,19},{4,20},{5,21},{6,22},{7,23},{8,24},{9,... | collective-permute-start | bytes 294920 | tf_op jit(solution)/shard_map/ppermute | solution.py:543
  121.8 10.4 %collective-permute-start.35 = (bf16[1,32,1536]{2,1,0:T(8,128)(2,1)S(1)}, bf16[1,32,1536]{2,1,0:T(8,128)(2,1)S(1)}, u32[]{:S(2)}, u32[]{:S(2)}) collective-permute-start(bf16[1,32,1536]{2,1,0:T(8,128)(2,1)S(1)} %add_convert_fusion.29), channel_id=1, source_target_pairs={{0,16},{1,17},{2,18},{3,19},{4,20},{5,21},{6,22},{7,23},{8,24},{9,... | collective-permute-start | bytes 294920 | tf_op jit(solution)/shard_map/ppermute | solution.py:543
  130.5 10.0 %collective-permute-start.40 = (bf16[2,32,1536]{2,1,0:T(8,128)(2,1)S(1)}, bf16[2,32,1536]{2,1,0:T(8,128)(2,1)S(1)}, u32[]{:S(2)}, u32[]{:S(2)}) collective-permute-start(bf16[2,32,1536]{2,1,0:T(8,128)(2,1)S(1)} %pad_maximum_fusion.10), channel_id=1, source_target_pairs={{0,8},{1,9},{2,10},{3,11},{4,12},{5,13},{6,14},{7,15},{8,0},{9,1},... | collective-permute-start | bytes 589832 | tf_op jit(solution)/shard_map/ppermute | solution.py:543
  132.6 9.9 %collective-permute-start.38 = (bf16[3,16,1536]{2,1,0:T(8,128)(2,1)S(1)}, bf16[3,16,1536]{2,1,0:T(8,128)(2,1)S(1)}, u32[]{:S(2)}, u32[]{:S(2)}) collective-permute-start(bf16[3,16,1536]{2,1,0:T(8,128)(2,1)S(1)} %maximum_maximum_fusion.2), channel_id=1, source_target_pairs={{0,8},{1,9},{2,10},{3,11},{4,12},{5,13},{6,14},{7,15},{8,0},{9,1},... | collective-permute-start | bytes 442376 | tf_op jit(solution)/shard_map/ppermute | solution.py:543
  150.3 11.6 %collective-permute-start.45 = (bf16[4,32,1536]{2,1,0:T(8,128)(2,1)S(1)}, bf16[4,32,1536]{2,1,0:T(8,128)(2,1)S(1)}, u32[]{:S(2)}, u32[]{:S(2)}) collective-permute-start(bf16[4,32,1536]{2,1,0:T(8,128)(2,1)S(1)} %pad_maximum_fusion.5), channel_id=1, source_target_pairs={{0,4},{1,5},{2,6},{3,7},{4,0},{5,1},{6,2},{7,3},{8,12},{9,13},{10,... | collective-permute-start | bytes 1179656 | tf_op jit(solution)/shard_map/ppermute | solution.py:543
  (42 other events, 238.2 us)

commit v9 on v8

--- a/solution.py
+++ b/solution.py
@@ -14,7 +14,8 @@
 f32 = jnp.float32
 axes = ("dp", "tensor")
 mebibyte = 1024 * 1024
-raw_names = ("attn_near", "attn_far", "ff_near", "ff_far", "w_gate", "w_up", "w_down")
+raw_names = ("w_query", "w_key", "w_value", "w_out", "w_gate", "w_up", "w_down")
+scalar_names = ("place", "table")
 
 
 def dot_nn(left, right):
@@ -57,7 +58,7 @@
 
 def run(body, name, ins, outs, scratch, after=(), micros=1, vmem=8):
     in_names, out_names, scratch_names = list(ins), list(outs), list(scratch)
-    direct = {n for n in in_names if n == "place" or n in raw_names or isinstance(ins[n], Kept)}
+    direct = {n for n in in_names if n in scalar_names + raw_names or isinstance(ins[n], Kept)}
     staged = [n for n in in_names if n not in direct]
     copied = [n for n in out_names if not isinstance(outs[n], Kept)]
     in_sems = {n: i for i, n in enumerate(staged)}
@@ -91,7 +92,7 @@
         body(r)
 
     def in_space(n):
-        if n == "place":
+        if n in scalar_names:
             return pltpu.SMEM
         return pltpu.VMEM if isinstance(ins[n], Kept) else pl.ANY
 
@@ -226,19 +227,32 @@
 
 
 def prepare_body(r):
-    r.fetch("inputs", "marks", "embed", "gain_attn", "buckets", "table")
-    r.need("inputs", "marks", "embed", "gain_attn", "buckets", "table")
-    x = jnp.where(r.marks[:, 0:1] == 1, r.inputs[...].astype(f32), r.embed[...])
-    r.x[...] = x
-    r.a[...] = (x * inverse_rms(x) * r.gain_attn[0:1, :]).astype(bf16)
-    buckets = r.buckets[...]
-    bias = jnp.zeros(buckets.shape, f32)
-    for idx in range(r.table.shape[0]):
-        bias = jnp.where(buckets == idx, r.table[idx : idx + 1, :], bias)
-    r.bias[...] = bias
-    r.mask[...] = jnp.broadcast_to(r.marks[:, 1:2], r.mask.shape)
-    r.write("x", "a", "bias", "mask")
-    r.drain("x", "a", "bias", "mask")
+    names = ("inputs", "valid", "keep", "embed", "gain_attn", "buckets")
+    r.fetch(*names)
+    r.need(*names)
+    series, slots = r.valid.shape
+    gain = r.gain_attn[0:1, :]
+    valid = jnp.transpose(r.valid[...].astype(f32))
+    keep = jnp.transpose(r.keep[...].astype(f32))
+    for s in range(series):
+        here = slice(s * slots, (s + 1) * slots)
+        seen = valid[:, s : s + 1]
+        x = jnp.where(seen == 1.0, r.inputs[here, :].astype(f32), r.embed[...])
+        r.x[here, :] = x
+        r.a[here, :] = (x * inverse_rms(x) * gain).astype(bf16)
+        r.seen[here, :] = jnp.broadcast_to(seen, (slots, 128)).astype(jnp.int32)
+        r.mask[here, :] = jnp.broadcast_to(keep[:, s : s + 1], (slots, 128)).astype(jnp.int32)
+    turned = jnp.transpose(r.buckets[...].astype(f32)).astype(jnp.int32)
+    wide = jnp.concatenate([turned, turned], axis=1)
+    r.wide[...] = wide
+    is_low = lane_low(slots)
+    bucket_count, heads = r.table.shape
+    for pair in range(heads // 2):
+        bias = jnp.zeros((slots, 128), f32)
+        for idx in range(bucket_count):
+            entry = jnp.where(is_low, r.table[idx, 2 * pair], r.table[idx, 2 * pair + 1])
+            bias = jnp.where(wide == idx, entry, bias)
+        r.bias[:, pair * 128 : (pair + 1) * 128] = bias
 
 
 def attention_body(r, sizes, masks, grain, layer_idx):
@@ -325,8 +339,6 @@
     rows = series * slots
     width = r.x.shape[1]
     r.fetch("gain_attn")
-    if not last:
-        r.fetch("marks", "buckets")
     for part in chunks(rows, 256):
         r.grad_heads[part, :] = dot_nn(r.branch[part, :], r.attn_w[:, 3 * inner :]).astype(bf16)
     is_low = lane_low(slots)
@@ -362,8 +374,6 @@
     r.attn_grad[:, 3 * inner :] = dot_tn(r.branch[...], r.heads[...])
     scatter_pieces(r.attn_grad, r.attn_keep, r.attn_send, piece_masks, r.place[2])
     r.need("gain_attn")
-    if not last:
-        r.need("marks", "buckets")
     gain_attn = r.gain_attn[layer_idx : layer_idx + 1, :]
     gain_total = jnp.zeros((1, width), f32)
     embed_total = jnp.zeros((1, width), f32)
@@ -375,7 +385,7 @@
         if last:
             r.grad_next[part, :] = grad_in
         else:
-            seen = r.marks[part, 0:1] == 1
+            seen = r.seen[part, 0:1] == 1
             r.grad_next[part, :] = jnp.where(seen, grad_in, 0.0)
             embed_total += jnp.sum(jnp.where(seen, 0.0, grad_in), axis=0, keepdims=True)
     r.write("grad_next")
@@ -383,8 +393,10 @@
         put_row(r.small, 4, embed_total)
         head_size = inner // heads
         for idx in range(r.table_rows.shape[0]):
-            chosen = jnp.where(r.buckets[...] == idx, r.bias_acc[...], 0.0)
-            r.table_rows[idx : idx + 1, :] = jnp.sum(chosen, axis=0, keepdims=True)
+            for start in range(0, inner, 128):
+                at = slice(start, start + 128)
+                chosen = jnp.where(r.wide[...] == idx, r.bias_acc[:, at], 0.0)
+                r.table_rows[idx : idx + 1, at] = jnp.sum(chosen, axis=0, keepdims=True)
         lane = lax.broadcasted_iota(jnp.int32, (r.table_rows.shape[0], 128), 1)
         table = jnp.zeros(lane.shape, f32)
         for head in range(heads):
@@ -486,16 +498,23 @@
     r.drain("gain_attn", "gain_ff", "embed", "table")
 
 
-def cut_body(r):
+def pack_body(r, packs):
     rows = r.quarter_0.shape[1]
     at = pl.ds(pl.multiple_of(r.place[1] * rows, rows), rows)
-    outs = (r.quarter_0, r.quarter_1)
-    start_all(
-        pltpu.make_async_copy(w.at[layer_idx, at], out.at[k], r.cut_sem)
-        for layer_idx, out in enumerate(outs)
-        for k, w in enumerate((r.w_gate, r.w_up, r.w_down))
-    )
-    wait_all(r.cut_sem, *outs)
+    copies = []
+    outs = [r.quarter_0, r.quarter_1]
+    for layer_idx in range(2):
+        for k, w in enumerate((r.w_gate, r.w_up, r.w_down)):
+            copies.append((w.at[layer_idx, at], outs[layer_idx].at[k]))
+    if packs:
+        outs += [r.block_0, r.block_1]
+        inner = r.w_query.shape[2]
+        for layer_idx in range(2):
+            for k, w in enumerate((r.w_query, r.w_key, r.w_value, r.w_out)):
+                lanes = pl.ds(k * inner, inner)
+                copies.append((w.at[layer_idx], outs[2 + layer_idx].at[:, lanes]))
+    start_all([pltpu.make_async_copy(*ends, r.pack_sem) for ends in copies])
+    wait_all(r.pack_sem, *outs)
 
 
 def order_masks(hops):
@@ -562,92 +581,89 @@
     ).astype(jnp.int32)
 
     quarter = width // 4
-    packed = jnp.concatenate([w_query, w_key, w_value, jnp.swapaxes(w_output, 1, 2)], axis=2)
-    in_hbm = {
-        name: pltpu.with_memory_space_constraint(w, pltpu.HBM)
-        for name, w in (("w_gate", w_gate), ("w_up", w_up), ("w_down", w_down))
-    }
-    ff_blocks = run(
-        cut_body,
-        "cut_quarters",
-        dict(place=place, **in_hbm),
+    own_rows = w_query.shape[1]
+    direct = own_rows % 16 == 0
+    w_out = jnp.swapaxes(w_output, 1, 2)
+    sources = dict(w_gate=w_gate, w_up=w_up, w_down=w_down)
+    block_outs = {}
+    if direct:
+        sources |= dict(w_query=w_query, w_key=w_key, w_value=w_value, w_out=w_out)
+        block_outs = {"block_%d" % k: Kept((own_rows, 4 * inner), bf16) for k in range(2)}
+    packed = run(
+        functools.partial(pack_body, packs=direct),
+        "pack",
+        dict(
+            place=place,
+            **{n: pltpu.with_memory_space_constraint(w, pltpu.HBM) for n, w in sources.items()},
+        ),
         dict(
             quarter_0=Kept((3, quarter, width), bf16),
             quarter_1=Kept((3, quarter, width), bf16),
-        ),
-        dict(cut_sem=pltpu.SemaphoreType.DMA),
-    )
-    own_rows = packed.shape[1]
-    direct = own_rows % 16 == 0
+            **block_outs,
+        ),
+        dict(pack_sem=pltpu.SemaphoreType.DMA),
+        vmem=4,
+    )
     far = bits[2:]
 
     def prepare(token):
-        table, marked, kept, near = (
-            tie(array, token) for array in (bias_table, patch_valid, attention_mask, buckets)
-        )
-        wide_buckets = jnp.tile(near.T, (1, heads))
-        wide_table = jnp.repeat(table, slots, axis=1)
-        marks = jnp.stack([marked.reshape(rows), kept.reshape(rows)], axis=1)
-        result = run(
+        return run(
             prepare_body,
             "prepare",
             dict(
-                inputs=inputs.reshape(matrix),
-                marks=marks,
+                inputs=tie(inputs, token).reshape(matrix),
+                valid=patch_valid,
+                keep=attention_mask,
                 embed=mask_embed[None, :],
                 gain_attn=gain_attn,
-                buckets=wide_buckets,
-                table=wide_table,
+                buckets=buckets,
+                table=bias_table,
             ),
             dict(
                 x=Kept(matrix, f32),
                 a=Kept(matrix, bf16),
                 bias=Kept((slots, heads * slots), f32),
                 mask=Kept((rows, 128), jnp.int32),
+                seen=Kept((rows, 128), jnp.int32),
+                wide=Kept((slots, 128), jnp.int32),
             ),
             {},
             micros=3,
         )
-        return result, wide_buckets, marks
 
     if direct:
         hops_0 = [1] + far[2:] + far[:2] + [2]
-        hops_1 = far[2:] + far[:2] + [1, 2]
-        block_0, block_1 = packed[0], packed[1]
+        hops_1 = far[2:] + far[1:2] + [1] + far[:1] + [2]
+        block_0, block_1 = packed.block_0, packed.block_1
         got_1 = swap(block_1, hops_1[0])
         got_0 = swap(block_0, hops_0[0])
-        ff_0 = swap(tie(ff_blocks.quarter_0, got_0), 1)
+        ff_0 = swap(tie(packed.quarter_0, got_0), 1)
+        ff_1 = swap(tie(packed.quarter_1, ff_0), 1)
         got_ff_0 = swap(ff_0, 4)
-        ff_1 = swap(tie(ff_blocks.quarter_1, ff_0), 1)
         block_0 = join(block_0, got_0)
         block_1 = join(block_1, tie(got_1, block_0))
         for hop_0, hop_1 in zip(hops_0[1:-2], hops_1[1:-2]):
             got_1, got_0 = swap(block_1, hop_1), swap(block_0, hop_0)
-            if hop_1 == hops_1[1]:
-                start, wide_buckets, marks = prepare(block_1)
+            if hop_0 == hops_0[1]:
+                start = prepare(block_1)
+                got_0 = tie(got_0, ff_0)
             block_0 = join(block_0, got_0)
             block_1 = join(block_1, tie(got_1, block_0))
         got_0 = swap(block_0, hops_0[-2])
         got_1 = swap(block_1, hops_1[-2])
         block_0 = join(block_0, tie(got_0, start.a, got_ff_0, ff_1))
-        block_1 = join(block_1, tie(got_1, block_0))
-        ff_0 = join(ff_0, tie(got_ff_0, block_1))
+        ff_0 = join(ff_0, tie(got_ff_0, block_0))
         got_ff_1 = swap(tie(ff_1, ff_0), 4)
-        far_0 = swap(block_0, 2)
-        attn_pieces = [
-            (block_0, far_0, order_masks(hops_0[::-1])),
-            (block_1, swap(tie(block_1, far_0), 2), order_masks(hops_1[::-1])),
-        ]
-        after_first = (attn_pieces[1][1],)
+        attn_pieces = [(block_0, swap(block_0, 2), order_masks(hops_0[::-1]))]
     else:
-        ff_0, ff_1 = swap(ff_blocks.quarter_0, 1), swap(ff_blocks.quarter_1, 1)
+        ff_0, ff_1 = swap(packed.quarter_0, 1), swap(packed.quarter_1, 1)
         ff_0 = join(ff_0, swap(ff_0, 4))
-        start, wide_buckets, marks = prepare(packed)
-        whole = lax.all_gather(packed[0], axes, axis=0, tiled=True)
-        attn_pieces = [(whole, whole, [0])]
-        whole = lax.all_gather(packed[1], axes, axis=0, tiled=True)
-        attn_pieces.append((whole, whole, [0]))
-        after_first = ()
+        start = prepare(ff_0)
+        attn_pieces = []
+        rows_of = jnp.concatenate([w_query, w_key, w_value, w_out], axis=2)
+        for layer_idx in range(2):
+            whole = lax.all_gather(rows_of[layer_idx], axes, axis=0, tiled=True)
+            attn_pieces.append((whole, whole, [0]))
     ff_pieces = [(ff_0, swap(ff_0, 2))]
 
     def attn_ins(layer_idx):
@@ -695,6 +711,13 @@
         )
 
     first = attention(0, start.x, start.a, micros=10)
+    if direct:
+        block_1 = join(block_1, tie(got_1, first.ff_in))
+        attn_pieces.append((block_1, swap(block_1, 2), order_masks(hops_1[::-1])))
+        ff_1 = join(ff_1, tie(got_ff_1, block_1))
+    else:
+        ff_1 = join(ff_1, swap(ff_1, 4))
+    ff_pieces.append((ff_1, swap(ff_1, 2)))
     first_ff = run(
         ff_body,
         "layer_0_ff",
@@ -707,14 +730,9 @@
         ),
         dict(**ff_outs, x_next=Kept(matrix, f32), a_next=Kept(matrix, bf16)),
         {},
-        after=after_first,
-        micros=0.1,
-    )
-    if direct:
-        ff_1 = join(ff_1, tie(got_ff_1, first_ff.a_next))
-    else:
-        ff_1 = join(ff_1, swap(ff_1, 4))
-    ff_pieces.append((ff_1, swap(ff_1, 2)))
+        after=(block_1, ff_1) if direct else (),
+        micros=3,
+    )
     second = attention(1, first_ff.x_next, first_ff.a_next, micros=0.1)
 
     attn_low = devices // attn_count
@@ -951,8 +969,8 @@
         dict(
             place=place,
             bias_before=Kept(back_1.bias_acc),
-            marks=marks,
-            buckets=wide_buckets,
+            seen=Kept(start.seen),
+            wide=Kept(start.wide),
             small_before=Kept(back_0.small),
             grad_mid=Kept(back_0.grad_mid),
             branch=Kept(back_0.branch),
@@ -983,19 +1001,19 @@
     turn = 0
     sums = attn_grads = None
     while ff_0.arriving is not None:
+        turn += 1
         token = ff_1.step(token)
+        if done and not ended:
+            done = finish(tie(ff_1.out["far"], token), far_masks, 1, place, shape, done)
+            token = done[0]
+            ended = True
+        token = ff_0.step(token)
         if not done and "near" in ff_1.out:
             done = finish(tie(ff_1.out["near"], token), near_masks, 1, place, shape)
             token = done[0]
-        elif not ended and ff_1.arriving is None:
-            done = finish(tie(ff_1.out["far"], token), far_masks, 1, place, shape, done)
-            token = done[0]
-            ended = True
-        turn += 1
-        token = ff_0.step(token)
         if turn != 2:
             token = attn_0.step(token)
-        token = attn_1.step(token)
+            token = attn_1.step(token)
         if sums is None and attn_0.arriving is None:
             sums = run(
                 small_body,

time: 167 us -> 163 us (0.976)
  starting transfers between devices: 43.4 us -> 48 us
  local copies, waits for them, and re-layouts: 5.63 us -> 2.3 us
  waiting for transfers between devices: 64.5 us -> 61.6 us
  other arithmetic: 6.91 us -> 4.06 us
    ppermute x48, starting transfers between devices: 43.4 us -> 48 us  [swap(): return lax.ppermute(array, axes, [(n, n ^ mask) for n in range(devices)])]
    ppermute x48, waiting for transfers between devices: 64.5 us -> 61.6 us  [swap(): return lax.ppermute(array, axes, [(n, n ^ mask) for n in range(devices)])]
    another operation x5 -> x0, local copies, waits for them, and re-layouts: 2.33 us -> none  [the longest x3 1.45 us: prepare(): marks = jnp.stack([marked.reshape(rows), kept.reshape(rows)], axis=1)]
  transfers between devices with their start and end apart: 48 -> 48, of which waited for: 21 -> 20; matrix products, arithmetic and copies ran while one was open for 6% -> 4% of each run, Pallas kernels for 21% -> 21%
where the time goes in v9:
time: 163 us
  waiting for transfers between devices  61.6 us (38%)
  starting transfers between devices  48 us (29%)
  Pallas kernels  44.9 us (28%)
  other arithmetic  4.06 us (2%)
  local copies, waits for them, and re-layouts  2.3 us (1%)
    ppermute x48, waiting for transfers between devices, swap(): return lax.ppermute(array, axes, [(n, n ^ mask) for n in range(devices)])  61.6 us
    ppermute x48, starting transfers between devices, swap(): return lax.ppermute(array, axes, [(n, n ^ mask) for n in range(devices)])  48 us
    pallas_call x10, Pallas kernels, run(): pl.pallas_call(kernel, name=name, in_specs=[pl.BlockSpec(memory_space=in_...  38.3 us
    pallas_call x4, Pallas kernels, finish(): pl.pallas_call(kernel, name='layer_%d_ff_grads' % layer_idx, in_specs=[pl...  6.67 us
  transfers between devices with their start and end apart: 48, of which 20 were waited for; matrix products, arithmetic and copies ran while one was open for 4% of the time, Pallas kernels for 21%

profile of v9, /device:TPU:0, one launch (start us, length us, event | category | flops | bytes accessed | tf_op | source)
XLA Modules:
  0.0 162.5 jit_solution(4047197503616745535)
XLA Ops:
  2.6 3.0 %collective-permute-start.1 = (bf16[16,1536]{1,0:T(8,128)(2,1)S(1)}, bf16[16,1536]{1,0:T(8,128)(2,1)S(1)}, u32[]{:S(2)}, u32[]{:S(2)}) collective-permute-start(bf16[16,1536]{1,0:T(8,128)(2,1)S(1)} %get-tuple-element.124), channel_id=1, source_target_pairs={{0,1},{1,0},{2,3},{3,2},{4,5},{5,4},{6,7},{7,6},{8,9},{9,8},{10,11... | collective-permute-start | bytes 147464 | tf_op jit(solution)/shard_map/ppermute | solution.py:562
  5.6 2.6 %collective-permute-start = (bf16[16,1536]{1,0:T(8,128)(2,1)S(1)}, bf16[16,1536]{1,0:T(8,128)(2,1)S(1)}, u32[]{:S(2)}, u32[]{:S(2)}) collective-permute-start(bf16[16,1536]{1,0:T(8,128)(2,1)S(1)} %get-tuple-element.123), channel_id=1, source_target_pairs={{0,16},{1,17},{2,18},{3,19},{4,20},{5,21},{6,22},{7,23},{8,24},{9,... | collective-permute-start | bytes 147464 | tf_op jit(solution)/shard_map/ppermute | solution.py:562
  10.3 2.6 %collective-permute-start.2 = (bf16[32,1536]{1,0:T(8,128)(2,1)S(1)}, bf16[32,1536]{1,0:T(8,128)(2,1)S(1)}, u32[]{:S(2)}, u32[]{:S(2)}) collective-permute-start(bf16[32,1536]{1,0:T(8,128)(2,1)S(1)} %get-tuple-element.297), channel_id=1, source_target_pairs={{0,16},{1,17},{2,18},{3,19},{4,20},{5,21},{6,22},{7,23},{8,24},{9,... | collective-permute-start | bytes 294920 | tf_op jit(solution)/shard_map/ppermute | solution.py:562
  15.8 3.4 %collective-permute-done.3 = bf16[3,128,512]{2,1,0:T(8,128)(2,1)S(1)} collective-permute-done((bf16[3,128,512]{2,1,0:T(8,128)(2,1)S(1)}, bf16[3,128,512]{2,1,0:T(8,128)(2,1)S(1)}, u32[]{:S(2)}, u32[]{:S(2)}) %collective-permute-start.3) | collective-permute-done | bytes 393248 | tf_op jit(solution)/shard_map/ppermute | solution.py:562
  21.4 2.1 %prepare.1 = (f32[512,512]{1,0:T(8,128)S(1)}, bf16[512,512]{1,0:T(8,128)(2,1)S(1)}, f32[64,384]{1,0:T(8,128)S(1)}, s32[512,128]{1,0:T(8,128)S(1)}, s32[512,128]{1,0:T(8,128)S(1)}, /*index=5*/s32[64,128]{1,0:T(8,128)S(1)}) custom-call(bf16[512,512]{1,0:T(8,128)(2,1)S(1)} %bitcast.57, s32[8,64]{1,0:T(8,128)S(1)} %copy-done.7, s32[8,64]{1,0:T(8,128)S(1)} %copy-done.8, ...), custom_call_target="tpu_custom_call" | custom-call | flops 3449999872 | tf_op jit(solution)/shard_map/prepare/pallas_call | solution.py:99
  28.5 6.4 %collective-permute-done.7 = bf16[3,128,512]{2,1,0:T(8,128)(2,1)S(1)} collective-permute-done((bf16[3,128,512]{2,1,0:T(8,128)(2,1)S(1)}, bf16[3,128,512]{2,1,0:T(8,128)(2,1)S(1)}, u32[]{:S(2)}, u32[]{:S(2)}) %collective-permute-start.7) | collective-permute-done | bytes 393248 | tf_op jit(solution)/shard_map/ppermute | solution.py:562
  39.3 2.8 %layer_0_attention.1 = (bf16[512,1536]{1,0:T(8,128)(2,1)S(1)}, bf16[512,1152]{1,0:T(8,128)(2,1)S(1)}, f32[512,384]{1,0:T(8,128)S(1)}, bf16[512,384]{1,0:T(8,128)...) custom-call(s32[4]{0:T(128)S(1)} %pad_add_fusion.refs_0_.place_ref, ...), custom_call_target="tpu_custom_call" | custom-call | flops 11500000256 | tf_op jit(solution)/shard_map/layer_0_attention/pallas_call | solution.py:99
  42.1 7.0 %collective-permute-done.12 = bf16[128,1536]{1,0:T(8,128)(2,1)S(1)} collective-permute-done((bf16[128,1536]{1,0:T(8,128)(2,1)S(1)}, bf16[128,1536]{1,0:T(8,128)(2,1)S(1)}, u32[]{:S(2)}, u32[]{:S(2)}) %collective-permute-start.12) | collective-permute-done | bytes 393248 | tf_op jit(solution)/shard_map/ppermute | solution.py:562
  49.2 6.3 %collective-permute-done.13 = bf16[3,128,512]{2,1,0:T(8,128)(2,1)S(1)} collective-permute-done((bf16[3,128,512]{2,1,0:T(8,128)(2,1)S(1)}, bf16[3,128,512]{2,1,0:T(8,128)(2,1)S(1)}, u32[]{:S(2)}, u32[]{:S(2)}) %collective-permute-start.13) | collective-permute-done | bytes 393248 | tf_op jit(solution)/shard_map/ppermute | solution.py:562
  55.6 3.1 %layer_0_ff.1 = (bf16[2,512,1024]{2,1,0:T(8,128)(2,1)S(1)}, bf16[2,512,512]{2,1,0:T(8,128)(2,1)S(1)}, f32[512,512]{1,0:T(8,128)S(1)}, bf16[512,512]{1,0:T(8,128)(2,1)S(1)}) custom-call(s32[4]{0:T(128)S(1)} %pad_add_fusion.refs_0_.place_ref, f32[512,512]{1,0:T(8,128)S(1)} %get-tuple-element.137.refs_1_.refs_4_, ...), custom_call_target="tpu_custom_call" | custom-call | flops 3449999872 | tf_op jit(solution)/shard_map/layer_0_ff/pallas_call | solution.py:99
  58.8 2.8 %layer_1_attention.1 = (bf16[512,1536]{1,0:T(8,128)(2,1)S(1)}, bf16[512,1152]{1,0:T(8,128)(2,1)S(1)}, f32[512,384]{1,0:T(8,128)S(1)}, bf16[512,384]{1,0:T(8,128)...) custom-call(s32[4]{0:T(128)S(1)} %pad_add_fusion.refs_0_.place_ref, ...), custom_call_target="tpu_custom_call" | custom-call | flops 115000000 | tf_op jit(solution)/shard_map/layer_1_attention/pallas_call | solution.py:99
  61.6 7.4 %layer_1_ff.1 = (bf16[32,32,768]{2,1,0:T(8,128)(2,1)S(1)}, bf16[32,32,768]{2,1,0:T(8,128)(2,1)S(1)}, f32[8,1536]{1,0:T(8,128)S(1)}, f32[512,512]{1,0:T(8,128)S(1...) custom-call(s32[4]{0:T(128)S(1)} %pad_add_fusion.refs_0_.place_ref, bf16[512,512]{1,0:T(8,128)(2,1)S(1)} %bitcast.58, ...), custom_call_target="tpu_custom_call" | custom-call | flops 9200000000 | tf_op jit(solution)/shard_map/layer_1_ff/pallas_call | solution.py:99
  69.5 4.5 %layer_1_attention_backward.1 = (bf16[16,16,1536]{2,1,0:T(8,128)(2,1)S(1)}, bf16[16,16,1536]{2,1,0:T(8,128)(2,1)S(1)}, f32[8,1536]{1,0:T(8,128)S(1)}, f32[512,512]{1,0:T(8,128)S(1)}, f32[64,384]{1,0:T(8,128)S(1)}) custom-call(s32[4]{0:T(128)S(1)} %pad_add_fusion.refs_0_.place_ref, f32[8,1536]{1,0:T(8,128)S(1)} %get-tuple-element.150.refs_1_, ...), custom_call_target="tpu_custom_call" | custom-call | flops 6899999744 | tf_op jit(solution)/shard_map/layer_1_attention_backward/pallas_call | solution.py:99
  76.8 7.0 %layer_0_ff_backward.1 = (bf16[32,32,768]{2,1,0:T(8,128)(2,1)S(1)}, bf16[32,32,768]{2,1,0:T(8,128)(2,1)S(1)}, f32[8,1536]{1,0:T(8,128)S(1)}, f32[512,512]{1,0:T(8,128)S(1)}, bf16[512,512]{1,0:T(8,128)(2,1)S(1)}) custom-call(s32[4]{0:T(128)S(1)} %pad_add_fusion.refs_0_.place_ref, f32[512,512]{1,0:T(8,128)S(1)} %get-tuple-element.160.refs_1_, ...), custom_call_target="tpu_custom_call" | custom-call | flops 9200000000 | tf_op jit(solution)/shard_map/layer_0_ff_backward/pallas_call | solution.py:99
  83.9 2.4 %collective-permute-done.19 = bf16[8,32,768]{2,1,0:T(8,128)(2,1)S(1)} collective-permute-done((bf16[8,32,768]{2,1,0:T(8,128)(2,1)S(1)}, bf16[8,32,768]{2,1,0:T(8,128)(2,1)S(1)}, u32[]{:S(2)}, u32[]{:S(2)}) %collective-permute-start.19) | collective-permute-done | bytes 393248 | tf_op jit(solution)/shard_map/ppermute | solution.py:562
  94.1 6.2 %layer_0_attention_backward.1 = (bf16[16,16,1536]{2,1,0:T(8,128)(2,1)S(1)}, bf16[17,16,1536]{2,1,0:T(8,128)(2,1)S(1)}, f32[8,1536]{1,0:T(8,128)S(1)}, f32[512,512]{1,0:T(8,128)}) custom-call(s32[4]{0:T(128)S(1)} %pad_add_fusion.refs_0_.place_ref, f32[64,384]{1,0:T(8,128)S(1)} %get-tuple-element.157.refs_1_, s32[512,128]{1,0:T(8,128)S(1)} %get-tuple-element.158.refs_2_, ...), custom_call_target="tpu_custom_call" | custom-call | flops 8049999872 | tf_op jit(solution)/shard_map/layer_0_attention_backward/pallas_call | solution.py:99
  102.1 3.0 %collective-permute-done.23 = bf16[8,32,768]{2,1,0:T(8,128)(2,1)S(1)} collective-permute-done((bf16[8,32,768]{2,1,0:T(8,128)(2,1)S(1)}, bf16[8,32,768]{2,1,0:T(8,128)(2,1)S(1)}, u32[]{:S(2)}, u32[]{:S(2)}) %collective-permute-start.23) | collective-permute-done | bytes 393248 | tf_op jit(solution)/shard_map/ppermute | solution.py:562
  108.3 2.4 %collective-permute-start.36 = (bf16[4,16,1536]{2,1,0:T(8,128)(2,1)S(1)}, bf16[4,16,1536]{2,1,0:T(8,128)(2,1)S(1)}, u32[]{:S(2)}, u32[]{:S(2)}) collective-permute-start(bf16[4,16,1536]{2,1,0:T(8,128)(2,1)S(1)} %get-tuple-element.260), channel_id=1, source_target_pairs={{0,16},{1,17},{2,18},{3,19},{4,20},{5,21},{6,22},{7,23},{8,24},{9,... | collective-permute-start | bytes 589832 | tf_op jit(solution)/shard_map/ppermute | solution.py:562
  111.4 2.2 %collective-permute-done.27 = bf16[4,32,768]{2,1,0:T(8,128)(2,1)S(1)} collective-permute-done((bf16[4,32,768]{2,1,0:T(8,128)(2,1)S(1)}, bf16[4,32,768]{2,1,0:T(8,128)(2,1)S(1)}, u32[]{:S(2)}, u32[]{:S(2)}) %collective-permute-start.27) | collective-permute-done | bytes 196640 | tf_op jit(solution)/shard_map/ppermute | solution.py:562
  114.9 8.2 %collective-permute-done.32 = bf16[1,32,1536]{2,1,0:T(8,128)(2,1)S(1)} collective-permute-done((bf16[1,32,1536]{2,1,0:T(8,128)(2,1)S(1)}, bf16[1,32,1536]{2,1,0:T(8,128)(2,1)S(1)}, u32[]{:S(2)}, u32[]{:S(2)}) %collective-permute-start.32) | collective-permute-done | bytes 98336 | tf_op jit(solution)/shard_map/ppermute | solution.py:562
  124.1 2.2 %collective-permute-start.34 = (bf16[1,32,1536]{2,1,0:T(8,128)(2,1)S(1)}, bf16[1,32,1536]{2,1,0:T(8,128)(2,1)S(1)}, u32[]{:S(2)}, u32[]{:S(2)}) collective-permute-start(bf16[1,32,1536]{2,1,0:T(8,128)(2,1)S(1)} %add_convert_fusion.30), channel_id=1, source_target_pairs={{0,16},{1,17},{2,18},{3,19},{4,20},{5,21},{6,22},{7,23},{8,24},{9,... | collective-permute-start | bytes 294920 | tf_op jit(solution)/shard_map/ppermute | solution.py:562
  128.7 3.9 %collective-permute-done.35 = bf16[1,32,1536]{2,1,0:T(8,128)(2,1)S(1)} collective-permute-done((bf16[1,32,1536]{2,1,0:T(8,128)(2,1)S(1)}, bf16[1,32,1536]{2,1,0:T(8,128)(2,1)S(1)}, u32[]{:S(2)}, u32[]{:S(2)}) %collective-permute-start.35) | collective-permute-done | bytes 98336 | tf_op jit(solution)/shard_map/ppermute | solution.py:562
  138.2 3.3 %collective-permute-done.39 = bf16[2,32,1536]{2,1,0:T(8,128)(2,1)S(1)} collective-permute-done((bf16[2,32,1536]{2,1,0:T(8,128)(2,1)S(1)}, bf16[2,32,1536]{2,1,0:T(8,128)(2,1)S(1)}, u32[]{:S(2)}, u32[]{:S(2)}) %collective-permute-start.39) | collective-permute-done | bytes 196640 | tf_op jit(solution)/shard_map/ppermute | solution.py:562
  146.5 3.8 %collective-permute-done.42 = bf16[4,32,1536]{2,1,0:T(8,128)(2,1)S(1)} collective-permute-done((bf16[4,32,1536]{2,1,0:T(8,128)(2,1)S(1)}, bf16[4,32,1536]{2,1,0:T(8,128)(2,1)S(1)}, u32[]{:S(2)}, u32[]{:S(2)}) %collective-permute-start.42) | collective-permute-done | bytes 393248 | tf_op jit(solution)/shard_map/ppermute | solution.py:562
  (180 shorter events, 62.4 us)
Async XLA Ops:
  8.9 10.3 %collective-permute-start.3 = (bf16[3,128,512]{2,1,0:T(8,128)(2,1)S(1)}, bf16[3,128,512]{2,1,0:T(8,128)(2,1)S(1)}, u32[]{:S(2)}, u32[]{:S(2)}) collective-permute-start(bf16[3,128,512]{2,1,0:T(8,128)(2,1)S(1)} %get-tuple-element.132), channel_id=1, source_target_pairs={{0,1},{1,0},{2,3},{3,2},{4,5},{5,4},{6,7},{7,6},{8,9},{9,8},{10,11... | collective-permute-start | bytes 1179656 | tf_op jit(solution)/shard_map/ppermute | solution.py:562
  12.9 11.3 %collective-permute-start.10 = (bf16[32,1536]{1,0:T(8,128)(2,1)S(1)}, bf16[32,1536]{1,0:T(8,128)(2,1)S(1)}, u32[]{:S(2)}, u32[]{:S(2)}) collective-permute-start(bf16[32,1536]{1,0:T(8,128)(2,1)S(1)} %get-tuple-element.291), channel_id=1, source_target_pairs={{0,8},{1,9},{2,10},{3,11},{4,12},{5,13},{6,14},{7,15},{8,0},{9,1},... | collective-permute-start | bytes 294920 | tf_op jit(solution)/shard_map/ppermute | solution.py:562
  23.5 11.3 %collective-permute-start.7 = (bf16[3,128,512]{2,1,0:T(8,128)(2,1)S(1)}, bf16[3,128,512]{2,1,0:T(8,128)(2,1)S(1)}, u32[]{:S(2)}, u32[]{:S(2)}) collective-permute-start(bf16[3,128,512]{2,1,0:T(8,128)(2,1)S(1)} %get-tuple-element.135), channel_id=1, source_target_pairs={{0,1},{1,0},{2,3},{3,2},{4,5},{5,4},{6,7},{7,6},{8,9},{9,8},{10,11... | collective-permute-start | bytes 1179656 | tf_op jit(solution)/shard_map/ppermute | solution.py:562
  24.2 10.7 %collective-permute-start.6 = (bf16[3,128,512]{2,1,0:T(8,128)(2,1)S(1)}, bf16[3,128,512]{2,1,0:T(8,128)(2,1)S(1)}, u32[]{:S(2)}, u32[]{:S(2)}) collective-permute-start(bf16[3,128,512]{2,1,0:T(8,128)(2,1)S(1)} %collective-permute-done.3), channel_id=1, source_target_pairs={{0,4},{1,5},{2,6},{3,7},{4,0},{5,1},{6,2},{7,3},{8,12},{9,13},{10,... | collective-permute-start | bytes 1179656 | tf_op jit(solution)/shard_map/ppermute | solution.py:562
  36.9 12.1 %collective-permute-start.12 = (bf16[128,1536]{1,0:T(8,128)(2,1)S(1)}, bf16[128,1536]{1,0:T(8,128)(2,1)S(1)}, u32[]{:S(2)}, u32[]{:S(2)}) collective-permute-start(bf16[128,1536]{1,0:T(8,128)(2,1)S(1)} %pad_maximum_fusion.2), channel_id=1, source_target_pairs={{0,4},{1,5},{2,6},{3,7},{4,0},{5,1},{6,2},{7,3},{8,12},{9,13},{10,... | collective-permute-start | bytes 1179656 | tf_op jit(solution)/shard_map/ppermute | solution.py:562
  37.6 18.0 %collective-permute-start.9 = (bf16[6,128,512]{2,1,0:T(8,128)(2,1)S(1)}, bf16[6,128,512]{2,1,0:T(8,128)(2,1)S(1)}, u32[]{:S(2)}, u32[]{:S(2)}) collective-permute-start(bf16[6,128,512]{2,1,0:T(8,128)(2,1)S(1)} %constant_dynamic-update-slice_fusion.16.refs_7_), channel_id=1, source_target_pairs={{0,2},{1,3},{2,0},{3,1},{4,6},{5,7},{6,4},{7,5},{8,10},{9,11},{10,... | collective-permute-start | bytes 2359304 | tf_op jit(solution)/shard_map/ppermute | solution.py:562
  37.7 17.8 %collective-permute-start.13 = (bf16[3,128,512]{2,1,0:T(8,128)(2,1)S(1)}, bf16[3,128,512]{2,1,0:T(8,128)(2,1)S(1)}, u32[]{:S(2)}, u32[]{:S(2)}) collective-permute-start(bf16[3,128,512]{2,1,0:T(8,128)(2,1)S(1)} %collective-permute-done.7), channel_id=1, source_target_pairs={{0,4},{1,5},{2,6},{3,7},{4,0},{5,1},{6,2},{7,3},{8,12},{9,13},{10,... | collective-permute-start | bytes 1179656 | tf_op jit(solution)/shard_map/ppermute | solution.py:562
  49.1 9.6 %collective-permute-start.14 = (bf16[256,1536]{1,0:T(8,128)(2,1)S(1)}, bf16[256,1536]{1,0:T(8,128)(2,1)S(1)}, u32[]{:S(2)}, u32[]{:S(2)}) collective-permute-start(bf16[256,1536]{1,0:T(8,128)(2,1)S(1)} %constant_dynamic-update-slice_fusion.18.refs_9_.refs_6_), channel_id=1, source_target_pairs={{0,2},{1,3},{2,0},{3,1},{4,6},{5,7},{6,4},{7,5},{8,10},{9,11},{10,... | collective-permute-start | bytes 2359304 | tf_op jit(solution)/shard_map/ppermute | solution.py:562
  74.7 11.6 %collective-permute-start.19 = (bf16[8,32,768]{2,1,0:T(8,128)(2,1)S(1)}, bf16[8,32,768]{2,1,0:T(8,128)(2,1)S(1)}, u32[]{:S(2)}, u32[]{:S(2)}) collective-permute-start(bf16[8,32,768]{2,1,0:T(8,128)(2,1)S(1)} %get-tuple-element.251), channel_id=1, source_target_pairs={{0,1},{1,0},{2,3},{3,2},{4,5},{5,4},{6,7},{7,6},{8,9},{9,8},{10,11... | collective-permute-start | bytes 1179656 | tf_op jit(solution)/shard_map/ppermute | solution.py:562
  74.8 11.6 %collective-permute-start.18 = (bf16[8,32,768]{2,1,0:T(8,128)(2,1)S(1)}, bf16[8,32,768]{2,1,0:T(8,128)(2,1)S(1)}, u32[]{:S(2)}, u32[]{:S(2)}) collective-permute-start(bf16[8,32,768]{2,1,0:T(8,128)(2,1)S(1)} %get-tuple-element.252), channel_id=1, source_target_pairs={{0,4},{1,5},{2,6},{3,7},{4,0},{5,1},{6,2},{7,3},{8,12},{9,13},{10,... | collective-permute-start | bytes 1179656 | tf_op jit(solution)/shard_map/ppermute | solution.py:562
  86.6 21.6 %collective-permute-start.30 = (bf16[8,16,1536]{2,1,0:T(8,128)(2,1)S(1)}, bf16[8,16,1536]{2,1,0:T(8,128)(2,1)S(1)}, u32[]{:S(2)}, u32[]{:S(2)}) collective-permute-start(bf16[8,16,1536]{2,1,0:T(8,128)(2,1)S(1)} %get-tuple-element.256.refs_8_), channel_id=1, source_target_pairs={{0,8},{1,9},{2,10},{3,11},{4,12},{5,13},{6,14},{7,15},{8,0},{9,1},... | collective-permute-start | bytes 1179656 | tf_op jit(solution)/shard_map/ppermute | solution.py:562
  88.2 12.0 %collective-permute-start.25 = (bf16[4,32,768]{2,1,0:T(8,128)(2,1)S(1)}, bf16[4,32,768]{2,1,0:T(8,128)(2,1)S(1)}, u32[]{:S(2)}, u32[]{:S(2)}) collective-permute-start(bf16[4,32,768]{2,1,0:T(8,128)(2,1)S(1)} %get-tuple-element.266), channel_id=1, source_target_pairs={{0,4},{1,5},{2,6},{3,7},{4,0},{5,1},{6,2},{7,3},{8,12},{9,13},{10,... | collective-permute-start | bytes 589832 | tf_op jit(solution)/shard_map/ppermute | solution.py:562
  90.0 10.3 %collective-permute-start.24 = (bf16[4,32,768]{2,1,0:T(8,128)(2,1)S(1)}, bf16[4,32,768]{2,1,0:T(8,128)(2,1)S(1)}, u32[]{:S(2)}, u32[]{:S(2)}) collective-permute-start(bf16[4,32,768]{2,1,0:T(8,128)(2,1)S(1)} %get-tuple-element.268), channel_id=1, source_target_pairs={{0,1},{1,0},{2,3},{3,2},{4,5},{5,4},{6,7},{7,6},{8,9},{9,8},{10,11... | collective-permute-start | bytes 589832 | tf_op jit(solution)/shard_map/ppermute | solution.py:562
  92.2 12.9 %collective-permute-start.23 = (bf16[8,32,768]{2,1,0:T(8,128)(2,1)S(1)}, bf16[8,32,768]{2,1,0:T(8,128)(2,1)S(1)}, u32[]{:S(2)}, u32[]{:S(2)}) collective-permute-start(bf16[8,32,768]{2,1,0:T(8,128)(2,1)S(1)} %get-tuple-element.247.refs_15_), channel_id=1, source_target_pairs={{0,1},{1,0},{2,3},{3,2},{4,5},{5,4},{6,7},{7,6},{8,9},{9,8},{10,11... | collective-permute-start | bytes 1179656 | tf_op jit(solution)/shard_map/ppermute | solution.py:562
  92.7 12.4 %collective-permute-start.22 = (bf16[8,32,768]{2,1,0:T(8,128)(2,1)S(1)}, bf16[8,32,768]{2,1,0:T(8,128)(2,1)S(1)}, u32[]{:S(2)}, u32[]{:S(2)}) collective-permute-start(bf16[8,32,768]{2,1,0:T(8,128)(2,1)S(1)} %get-tuple-element.248.refs_14_), channel_id=1, source_target_pairs={{0,4},{1,5},{2,6},{3,7},{4,0},{5,1},{6,2},{7,3},{8,12},{9,13},{10,... | collective-permute-start | bytes 1179656 | tf_op jit(solution)/shard_map/ppermute | solution.py:562
  100.5 10.2 %collective-permute-start.29 = (bf16[2,32,1536]{2,1,0:T(8,128)(2,1)S(1)}, bf16[2,32,1536]{2,1,0:T(8,128)(2,1)S(1)}, u32[]{:S(2)}, u32[]{:S(2)}) collective-permute-start(bf16[2,32,1536]{2,1,0:T(8,128)(2,1)S(1)} %pad_maximum_fusion.6), channel_id=1, source_target_pairs={{0,8},{1,9},{2,10},{3,11},{4,12},{5,13},{6,14},{7,15},{8,0},{9,1},... | collective-permute-start | bytes 589832 | tf_op jit(solution)/shard_map/ppermute | solution.py:562
  107.7 18.5 %collective-permute-start.26 = (bf16[9,16,1536]{2,1,0:T(8,128)(2,1)S(1)}, bf16[9,16,1536]{2,1,0:T(8,128)(2,1)S(1)}, u32[]{:S(2)}, u32[]{:S(2)}) collective-permute-start(bf16[9,16,1536]{2,1,0:T(8,128)(2,1)S(1)} %maximum_maximum_fusion), channel_id=1, source_target_pairs={{0,1},{1,0},{2,3},{3,2},{4,5},{5,4},{6,7},{7,6},{8,9},{9,8},{10,11... | collective-permute-start | bytes 1327112 | tf_op jit(solution)/shard_map/ppermute | solution.py:562
  108.3 19.5 %collective-permute-start.36 = (bf16[4,16,1536]{2,1,0:T(8,128)(2,1)S(1)}, bf16[4,16,1536]{2,1,0:T(8,128)(2,1)S(1)}, u32[]{:S(2)}, u32[]{:S(2)}) collective-permute-start(bf16[4,16,1536]{2,1,0:T(8,128)(2,1)S(1)} %get-tuple-element.260), channel_id=1, source_target_pairs={{0,16},{1,17},{2,18},{3,19},{4,20},{5,21},{6,22},{7,23},{8,24},{9,... | collective-permute-start | bytes 589832 | tf_op jit(solution)/shard_map/ppermute | solution.py:562
  110.7 12.4 %collective-permute-start.32 = (bf16[1,32,1536]{2,1,0:T(8,128)(2,1)S(1)}, bf16[1,32,1536]{2,1,0:T(8,128)(2,1)S(1)}, u32[]{:S(2)}, u32[]{:S(2)}) collective-permute-start(bf16[1,32,1536]{2,1,0:T(8,128)(2,1)S(1)} %add_convert_fusion.37), channel_id=1, source_target_pairs={{0,16},{1,17},{2,18},{3,19},{4,20},{5,21},{6,22},{7,23},{8,24},{9,... | collective-permute-start | bytes 294920 | tf_op jit(solution)/shard_map/ppermute | solution.py:562
  113.7 10.4 %collective-permute-start.31 = (bf16[2,32,1536]{2,1,0:T(8,128)(2,1)S(1)}, bf16[2,32,1536]{2,1,0:T(8,128)(2,1)S(1)}, u32[]{:S(2)}, u32[]{:S(2)}) collective-permute-start(bf16[2,32,1536]{2,1,0:T(8,128)(2,1)S(1)} %pad_maximum_fusion.7), channel_id=1, source_target_pairs={{0,8},{1,9},{2,10},{3,11},{4,12},{5,13},{6,14},{7,15},{8,0},{9,1},... | collective-permute-start | bytes 589832 | tf_op jit(solution)/shard_map/ppermute | solution.py:562
  123.2 9.3 %collective-permute-start.35 = (bf16[1,32,1536]{2,1,0:T(8,128)(2,1)S(1)}, bf16[1,32,1536]{2,1,0:T(8,128)(2,1)S(1)}, u32[]{:S(2)}, u32[]{:S(2)}) collective-permute-start(bf16[1,32,1536]{2,1,0:T(8,128)(2,1)S(1)} %add_convert_fusion.31), channel_id=1, source_target_pairs={{0,16},{1,17},{2,18},{3,19},{4,20},{5,21},{6,22},{7,23},{8,24},{9,... | collective-permute-start | bytes 294920 | tf_op jit(solution)/shard_map/ppermute | solution.py:562
  124.1 10.0 %collective-permute-start.34 = (bf16[1,32,1536]{2,1,0:T(8,128)(2,1)S(1)}, bf16[1,32,1536]{2,1,0:T(8,128)(2,1)S(1)}, u32[]{:S(2)}, u32[]{:S(2)}) collective-permute-start(bf16[1,32,1536]{2,1,0:T(8,128)(2,1)S(1)} %add_convert_fusion.30), channel_id=1, source_target_pairs={{0,16},{1,17},{2,18},{3,19},{4,20},{5,21},{6,22},{7,23},{8,24},{9,... | collective-permute-start | bytes 294920 | tf_op jit(solution)/shard_map/ppermute | solution.py:562
  135.2 9.5 %collective-permute-start.37 = (bf16[3,16,1536]{2,1,0:T(8,128)(2,1)S(1)}, bf16[3,16,1536]{2,1,0:T(8,128)(2,1)S(1)}, u32[]{:S(2)}, u32[]{:S(2)}) collective-permute-start(bf16[3,16,1536]{2,1,0:T(8,128)(2,1)S(1)} %maximum_maximum_fusion.2), channel_id=1, source_target_pairs={{0,8},{1,9},{2,10},{3,11},{4,12},{5,13},{6,14},{7,15},{8,0},{9,1},... | collective-permute-start | bytes 442376 | tf_op jit(solution)/shard_map/ppermute | solution.py:562
  137.1 9.3 %collective-permute-start.43 = (bf16[1,16,1536]{2,1,0:T(8,128)(2,1)S(1)}, bf16[1,16,1536]{2,1,0:T(8,128)(2,1)S(1)}, u32[]{:S(2)}, u32[]{:S(2)}) collective-permute-start(bf16[1,16,1536]{2,1,0:T(8,128)(2,1)S(1)} %add_convert_fusion.47), channel_id=1, source_target_pairs={{0,1},{1,0},{2,3},{3,2},{4,5},{5,4},{6,7},{7,6},{8,9},{9,8},{10,11... | collective-permute-start | bytes 147464 | tf_op jit(solution)/shard_map/ppermute | solution.py:562
  (37 other events, 351.1 us)

commit v10 on v9

--- a/solution.py
+++ b/solution.py
@@ -633,7 +633,7 @@
 
     if direct:
         hops_0 = [1] + far[2:] + far[:2] + [2]
-        hops_1 = far[2:] + far[1:2] + [1] + far[:1] + [2]
+        hops_1 = far[2:] + far[:2] + [1, 2]
         block_0, block_1 = packed.block_0, packed.block_1
         got_1 = swap(block_1, hops_1[0])
         got_0 = swap(block_0, hops_0[0])
@@ -649,6 +649,7 @@
                 got_0 = tie(got_0, ff_0)
             block_0 = join(block_0, got_0)
             block_1 = join(block_1, tie(got_1, block_0))
+        block_0 = tie(block_0, block_1)
         got_0 = swap(block_0, hops_0[-2])
         got_1 = swap(block_1, hops_1[-2])
         block_0 = join(block_0, tie(got_0, start.a, got_ff_0, ff_1))
@@ -714,10 +715,6 @@
     if direct:
         block_1 = join(block_1, tie(got_1, first.ff_in))
         attn_pieces.append((block_1, swap(block_1, 2), order_masks(hops_1[::-1])))
-        ff_1 = join(ff_1, tie(got_ff_1, block_1))
-    else:
-        ff_1 = join(ff_1, swap(ff_1, 4))
-    ff_pieces.append((ff_1, swap(ff_1, 2)))
     first_ff = run(
         ff_body,
         "layer_0_ff",
@@ -730,13 +727,18 @@
         ),
         dict(**ff_outs, x_next=Kept(matrix, f32), a_next=Kept(matrix, bf16)),
         {},
-        after=(block_1, ff_1) if direct else (),
+        after=(block_1,) if direct else (),
         micros=3,
     )
+    if direct:
+        ff_1 = join(ff_1, tie(got_ff_1, first_ff.x_next))
+    else:
+        ff_1 = join(ff_1, swap(ff_1, 4))
+    ff_pieces.append((ff_1, swap(ff_1, 2)))
     second = attention(1, first_ff.x_next, first_ff.a_next, micros=0.1)
 
     attn_low = devices // attn_count
-    attn_hops = ([2, 1] + bits[2:], [2] + bits[3:] + bits[2:3] + [1])
+    attn_hops = ([2, 1] + bits[2:], [2] + bits[3:4] + bits[2:3] + bits[4:] + [1])
     attn_split = [[hop for hop in hops if hop >= attn_low] for hops in attn_hops]
     attn_whole = [hop for hop in bits if hop < attn_low]
     attn_masks = [[mask // attn_low for mask in order_masks(hops)] for hops in attn_split]
@@ -844,6 +846,8 @@
             if small is not None and step + 1 < len(hops):
                 send, small = with_small(send, small)
             out["token"] = send
+            if layer_idx == 1 and step == 0:
+                send = tie(send, *(yield None))
         piece = keep[0]
         if own_rows < attn_grain:
             first_row = lax.rem(device_at, attn_low) * own_rows
@@ -877,6 +881,9 @@
             self.steps = steps(*args, self.out)
             self.arriving = next(self.steps)
 
+        def resume(self, *tokens):
+            self.arriving = self.steps.send(tokens)
+
         def step(self, token, *others):
             if self.arriving is not None:
                 tokens = (*(token if isinstance(token, tuple) else (token,)), *others)
@@ -992,6 +999,7 @@
         vmem=14,
     )
     attn_0 = Chain(attn_chain, back_attn_0, 0)
+    attn_1.resume(back_attn_0.attn_send)
     token = back_attn_0.attn_send
     shape = (2, width, width)
     near_masks = place_masks[: ff_count // 2]

time: 163 us -> 159 us (0.975)
  waiting for transfers between devices: 61.6 us -> 49.6 us
  starting transfers between devices: 48 us -> 56.6 us
  local copies, waits for them, and re-layouts: 2.3 us -> 0.45 us
    ppermute x48, waiting for transfers between devices: 61.6 us -> 49.6 us  [swap(): return lax.ppermute(array, axes, [(n, n ^ mask) for n in range(devices)])]
    ppermute x48, starting transfers between devices: 48 us -> 56.6 us  [swap(): return lax.ppermute(array, axes, [(n, n ^ mask) for n in range(devices)])]
    unnamed x35 -> x33, local copies, waits for them, and re-layouts: 2.17 us -> 0.31 us
  transfers between devices with their start and end apart: 48 -> 48, of which waited for: 20 -> 20; matrix products, arithmetic and copies ran while one was open for 4% -> 3% of each run, Pallas kernels for 21% -> 22%
where the time goes in v10:
time: 159 us; the launch traced here: 157 us
  starting transfers between devices  56.6 us (36%)
  waiting for transfers between devices  49.6 us (31%)
  Pallas kernels  45.1 us (28%)
  other arithmetic  4.07 us (3%)
  between operations  1.6 us (1%)
    ppermute x48, starting transfers between devices, swap(): return lax.ppermute(array, axes, [(n, n ^ mask) for n in range(devices)])  56.6 us
    ppermute x48, waiting for transfers between devices, swap(): return lax.ppermute(array, axes, [(n, n ^ mask) for n in range(devices)])  49.6 us
    pallas_call x10, Pallas kernels, run(): pl.pallas_call(kernel, name=name, in_specs=[pl.BlockSpec(memory_space=in_...  38.4 us
    pallas_call x4, Pallas kernels, finish(): pl.pallas_call(kernel, name='layer_%d_ff_grads' % layer_idx, in_specs=[pl...  6.67 us
  transfers between devices with their start and end apart: 48, of which 20 were waited for; matrix products, arithmetic and copies ran while one was open for 3% of the time, Pallas kernels for 22%

profile of v10, /device:TPU:0, one launch (start us, length us, event | category | flops | bytes accessed | tf_op | source)
XLA Modules:
  0.0 157.4 jit_solution(15157049381789761965)
XLA Ops:
  2.6 3.0 %collective-permute-start.1 = (bf16[16,1536]{1,0:T(8,128)(2,1)S(1)}, bf16[16,1536]{1,0:T(8,128)(2,1)S(1)}, u32[]{:S(2)}, u32[]{:S(2)}) collective-permute-start(bf16[16,1536]{1,0:T(8,128)(2,1)S(1)} %get-tuple-element.126), channel_id=1, source_target_pairs={{0,1},{1,0},{2,3},{3,2},{4,5},{5,4},{6,7},{7,6},{8,9},{9,8},{10,11... | collective-permute-start | bytes 147464 | tf_op jit(solution)/shard_map/ppermute | solution.py:562
  5.6 2.6 %collective-permute-start = (bf16[16,1536]{1,0:T(8,128)(2,1)S(1)}, bf16[16,1536]{1,0:T(8,128)(2,1)S(1)}, u32[]{:S(2)}, u32[]{:S(2)}) collective-permute-start(bf16[16,1536]{1,0:T(8,128)(2,1)S(1)} %get-tuple-element.125), channel_id=1, source_target_pairs={{0,16},{1,17},{2,18},{3,19},{4,20},{5,21},{6,22},{7,23},{8,24},{9,... | collective-permute-start | bytes 147464 | tf_op jit(solution)/shard_map/ppermute | solution.py:562
  9.7 2.7 %collective-permute-start.2 = (bf16[32,1536]{1,0:T(8,128)(2,1)S(1)}, bf16[32,1536]{1,0:T(8,128)(2,1)S(1)}, u32[]{:S(2)}, u32[]{:S(2)}) collective-permute-start(bf16[32,1536]{1,0:T(8,128)(2,1)S(1)} %get-tuple-element.303), channel_id=1, source_target_pairs={{0,16},{1,17},{2,18},{3,19},{4,20},{5,21},{6,22},{7,23},{8,24},{9,... | collective-permute-start | bytes 294920 | tf_op jit(solution)/shard_map/ppermute | solution.py:562
  13.9 4.6 %collective-permute-done.3 = bf16[3,128,512]{2,1,0:T(8,128)(2,1)S(1)} collective-permute-done((bf16[3,128,512]{2,1,0:T(8,128)(2,1)S(1)}, bf16[3,128,512]{2,1,0:T(8,128)(2,1)S(1)}, u32[]{:S(2)}, u32[]{:S(2)}) %collective-permute-start.3) | collective-permute-done | bytes 393248 | tf_op jit(solution)/shard_map/ppermute | solution.py:562
  23.2 4.0 %collective-permute-done.4 = bf16[64,1536]{1,0:T(8,128)(2,1)S(1)} collective-permute-done((bf16[64,1536]{1,0:T(8,128)(2,1)S(1)}, bf16[64,1536]{1,0:T(8,128)(2,1)S(1)}, u32[]{:S(2)}, u32[]{:S(2)}) %collective-permute-start.4) | collective-permute-done | bytes 196640 | tf_op jit(solution)/shard_map/ppermute | solution.py:562
  32.8 2.7 %collective-permute-done.7 = bf16[128,1536]{1,0:T(8,128)(2,1)S(1)} collective-permute-done((bf16[128,1536]{1,0:T(8,128)(2,1)S(1)}, bf16[128,1536]{1,0:T(8,128)(2,1)S(1)}, u32[]{:S(2)}, u32[]{:S(2)}) %collective-permute-start.7) | collective-permute-done | bytes 393248 | tf_op jit(solution)/shard_map/ppermute | solution.py:562
  38.6 2.8 %layer_0_attention.1 = (bf16[512,1536]{1,0:T(8,128)(2,1)S(1)}, bf16[512,1152]{1,0:T(8,128)(2,1)S(1)}, f32[512,384]{1,0:T(8,128)S(1)}, bf16[512,384]{1,0:T(8,128)...) custom-call(s32[4]{0:T(128)S(1)} %pad_add_fusion.refs_0_.place_ref, ...), custom_call_target="tpu_custom_call" | custom-call | flops 11500000256 | tf_op jit(solution)/shard_map/layer_0_attention/pallas_call | solution.py:99
  41.3 5.9 %collective-permute-done.12 = bf16[128,1536]{1,0:T(8,128)(2,1)S(1)} collective-permute-done((bf16[128,1536]{1,0:T(8,128)(2,1)S(1)}, bf16[128,1536]{1,0:T(8,128)(2,1)S(1)}, u32[]{:S(2)}, u32[]{:S(2)}) %collective-permute-start.12) | collective-permute-done | bytes 393248 | tf_op jit(solution)/shard_map/ppermute | solution.py:562
  47.3 3.2 %layer_0_ff.1 = (bf16[2,512,1024]{2,1,0:T(8,128)(2,1)S(1)}, bf16[2,512,512]{2,1,0:T(8,128)(2,1)S(1)}, f32[512,512]{1,0:T(8,128)S(1)}, bf16[512,512]{1,0:T(8,128)(2,1)S(1)}) custom-call(s32[4]{0:T(128)S(1)} %pad_add_fusion.refs_0_.place_ref, f32[512,512]{1,0:T(8,128)S(1)} %get-tuple-element.142.refs_1_.refs_4_, ...), custom_call_target="tpu_custom_call" | custom-call | flops 3449999872 | tf_op jit(solution)/shard_map/layer_0_ff/pallas_call | solution.py:99
  51.1 2.8 %layer_1_attention.1 = (bf16[512,1536]{1,0:T(8,128)(2,1)S(1)}, bf16[512,1152]{1,0:T(8,128)(2,1)S(1)}, f32[512,384]{1,0:T(8,128)S(1)}, bf16[512,384]{1,0:T(8,128)...) custom-call(s32[4]{0:T(128)S(1)} %pad_add_fusion.refs_0_.place_ref, ...), custom_call_target="tpu_custom_call" | custom-call | flops 115000000 | tf_op jit(solution)/shard_map/layer_1_attention/pallas_call | solution.py:99
  53.9 7.3 %layer_1_ff.1 = (bf16[32,32,768]{2,1,0:T(8,128)(2,1)S(1)}, bf16[32,32,768]{2,1,0:T(8,128)(2,1)S(1)}, f32[8,1536]{1,0:T(8,128)S(1)}, f32[512,512]{1,0:T(8,128)S(1...) custom-call(s32[4]{0:T(128)S(1)} %pad_add_fusion.refs_0_.place_ref, bf16[512,512]{1,0:T(8,128)(2,1)S(1)} %bitcast.58, ...), custom_call_target="tpu_custom_call" | custom-call | flops 9200000000 | tf_op jit(solution)/shard_map/layer_1_ff/pallas_call | solution.py:99
  61.4 4.6 %layer_1_attention_backward.1 = (bf16[16,16,1536]{2,1,0:T(8,128)(2,1)S(1)}, bf16[16,16,1536]{2,1,0:T(8,128)(2,1)S(1)}, f32[8,1536]{1,0:T(8,128)S(1)}, f32[512,512]{1,0:T(8,128)S(1)}, f32[64,384]{1,0:T(8,128)S(1)}) custom-call(s32[4]{0:T(128)S(1)} %pad_add_fusion.refs_0_.place_ref, f32[8,1536]{1,0:T(8,128)S(1)} %get-tuple-element.153.refs_1_, ...), custom_call_target="tpu_custom_call" | custom-call | flops 6899999744 | tf_op jit(solution)/shard_map/layer_1_attention_backward/pallas_call | solution.py:99
  69.9 7.1 %layer_0_ff_backward.1 = (bf16[32,32,768]{2,1,0:T(8,128)(2,1)S(1)}, bf16[32,32,768]{2,1,0:T(8,128)(2,1)S(1)}, f32[8,1536]{1,0:T(8,128)S(1)}, f32[512,512]{1,0:T(8,128)S(1)}, bf16[512,512]{1,0:T(8,128)(2,1)S(1)}) custom-call(s32[4]{0:T(128)S(1)} %pad_add_fusion.refs_0_.place_ref, f32[512,512]{1,0:T(8,128)S(1)} %get-tuple-element.163.refs_1_, ...), custom_call_target="tpu_custom_call" | custom-call | flops 9200000000 | tf_op jit(solution)/shard_map/layer_0_ff_backward/pallas_call | solution.py:99
  85.5 6.1 %layer_0_attention_backward.1 = (bf16[16,16,1536]{2,1,0:T(8,128)(2,1)S(1)}, bf16[17,16,1536]{2,1,0:T(8,128)(2,1)S(1)}, f32[8,1536]{1,0:T(8,128)S(1)}, f32[512,512]{1,0:T(8,128)}) custom-call(s32[4]{0:T(128)S(1)} %pad_add_fusion.refs_0_.place_ref, f32[64,384]{1,0:T(8,128)S(1)} %get-tuple-element.160.refs_1_, s32[512,128]{1,0:T(8,128)S(1)} %get-tuple-element.161.refs_2_, ...), custom_call_target="tpu_custom_call" | custom-call | flops 8049999872 | tf_op jit(solution)/shard_map/layer_0_attention_backward/pallas_call | solution.py:99
  99.4 8.3 %collective-permute-done.30 = bf16[8,16,1536]{2,1,0:T(8,128)(2,1)S(1)} collective-permute-done((bf16[8,16,1536]{2,1,0:T(8,128)(2,1)S(1)}, bf16[8,16,1536]{2,1,0:T(8,128)(2,1)S(1)}, u32[]{:S(2)}, u32[]{:S(2)}) %collective-permute-start.30) | collective-permute-done | bytes 393248 | tf_op jit(solution)/shard_map/ppermute | solution.py:562
  108.6 2.7 %collective-permute-start.32 = (bf16[1,32,1536]{2,1,0:T(8,128)(2,1)S(1)}, bf16[1,32,1536]{2,1,0:T(8,128)(2,1)S(1)}, u32[]{:S(2)}, u32[]{:S(2)}) collective-permute-start(bf16[1,32,1536]{2,1,0:T(8,128)(2,1)S(1)} %add_convert_fusion.37), channel_id=1, source_target_pairs={{0,16},{1,17},{2,18},{3,19},{4,20},{5,21},{6,22},{7,23},{8,24},{9,... | collective-permute-start | bytes 294920 | tf_op jit(solution)/shard_map/ppermute | solution.py:562
  113.2 2.2 %collective-permute-done.32 = bf16[1,32,1536]{2,1,0:T(8,128)(2,1)S(1)} collective-permute-done((bf16[1,32,1536]{2,1,0:T(8,128)(2,1)S(1)}, bf16[1,32,1536]{2,1,0:T(8,128)(2,1)S(1)}, u32[]{:S(2)}, u32[]{:S(2)}) %collective-permute-start.32) | collective-permute-done | bytes 98336 | tf_op jit(solution)/shard_map/ppermute | solution.py:562
  115.4 2.6 %collective-permute-start.35 = (bf16[1,32,1536]{2,1,0:T(8,128)(2,1)S(1)}, bf16[1,32,1536]{2,1,0:T(8,128)(2,1)S(1)}, u32[]{:S(2)}, u32[]{:S(2)}) collective-permute-start(bf16[1,32,1536]{2,1,0:T(8,128)(2,1)S(1)} %add_convert_fusion.31), channel_id=1, source_target_pairs={{0,16},{1,17},{2,18},{3,19},{4,20},{5,21},{6,22},{7,23},{8,24},{9,... | collective-permute-start | bytes 294920 | tf_op jit(solution)/shard_map/ppermute | solution.py:562
  121.2 3.0 %collective-permute-start.40 = (bf16[2,16,1536]{2,1,0:T(8,128)(2,1)S(1)}, bf16[2,16,1536]{2,1,0:T(8,128)(2,1)S(1)}, u32[]{:S(2)}, u32[]{:S(2)}) collective-permute-start(bf16[2,16,1536]{2,1,0:T(8,128)(2,1)S(1)} %get-tuple-element.276), channel_id=1, source_target_pairs={{0,16},{1,17},{2,18},{3,19},{4,20},{5,21},{6,22},{7,23},{8,24},{9,... | collective-permute-start | bytes 294920 | tf_op jit(solution)/shard_map/ppermute | solution.py:562
  124.2 2.6 %collective-permute-done.35 = bf16[1,32,1536]{2,1,0:T(8,128)(2,1)S(1)} collective-permute-done((bf16[1,32,1536]{2,1,0:T(8,128)(2,1)S(1)}, bf16[1,32,1536]{2,1,0:T(8,128)(2,1)S(1)}, u32[]{:S(2)}, u32[]{:S(2)}) %collective-permute-start.35) | collective-permute-done | bytes 98336 | tf_op jit(solution)/shard_map/ppermute | solution.py:562
  127.1 2.8 %collective-permute-done.34 = bf16[1,32,1536]{2,1,0:T(8,128)(2,1)S(1)} collective-permute-done((bf16[1,32,1536]{2,1,0:T(8,128)(2,1)S(1)}, bf16[1,32,1536]{2,1,0:T(8,128)(2,1)S(1)}, u32[]{:S(2)}, u32[]{:S(2)}) %collective-permute-start.34) | collective-permute-done | bytes 98336 | tf_op jit(solution)/shard_map/ppermute | solution.py:562
  131.1 2.9 %collective-permute-start.37 = (bf16[3,16,1536]{2,1,0:T(8,128)(2,1)S(1)}, bf16[3,16,1536]{2,1,0:T(8,128)(2,1)S(1)}, u32[]{:S(2)}, u32[]{:S(2)}) collective-permute-start(bf16[3,16,1536]{2,1,0:T(8,128)(2,1)S(1)} %maximum_maximum_fusion.2), channel_id=1, source_target_pairs={{0,8},{1,9},{2,10},{3,11},{4,12},{5,13},{6,14},{7,15},{8,0},{9,1},... | collective-permute-start | bytes 442376 | tf_op jit(solution)/shard_map/ppermute | solution.py:562
  139.9 3.2 %collective-permute-start.41 = (bf16[2,16,1536]{2,1,0:T(8,128)(2,1)S(1)}, bf16[2,16,1536]{2,1,0:T(8,128)(2,1)S(1)}, u32[]{:S(2)}, u32[]{:S(2)}) collective-permute-start(bf16[2,16,1536]{2,1,0:T(8,128)(2,1)S(1)} %maximum_maximum_fusion.3), channel_id=1, source_target_pairs={{0,16},{1,17},{2,18},{3,19},{4,20},{5,21},{6,22},{7,23},{8,24},{9,... | collective-permute-start | bytes 294920 | tf_op jit(solution)/shard_map/ppermute | solution.py:562
  150.9 2.2 %collective-permute-done.45 = bf16[4,32,1536]{2,1,0:T(8,128)(2,1)S(1)} collective-permute-done((bf16[4,32,1536]{2,1,0:T(8,128)(2,1)S(1)}, bf16[4,32,1536]{2,1,0:T(8,128)(2,1)S(1)}, u32[]{:S(2)}, u32[]{:S(2)}) %collective-permute-start.45) | collective-permute-done | bytes 393248 | tf_op jit(solution)/shard_map/ppermute | solution.py:562
  (178 shorter events, 63.9 us)
Async XLA Ops:
  8.3 10.3 %collective-permute-start.3 = (bf16[3,128,512]{2,1,0:T(8,128)(2,1)S(1)}, bf16[3,128,512]{2,1,0:T(8,128)(2,1)S(1)}, u32[]{:S(2)}, u32[]{:S(2)}) collective-permute-start(bf16[3,128,512]{2,1,0:T(8,128)(2,1)S(1)} %get-tuple-element.134), channel_id=1, source_target_pairs={{0,1},{1,0},{2,3},{3,2},{4,5},{5,4},{6,7},{7,6},{8,9},{9,8},{10,11... | collective-permute-start | bytes 1179656 | tf_op jit(solution)/shard_map/ppermute | solution.py:562
  9.7 9.7 %collective-permute-start.2 = (bf16[32,1536]{1,0:T(8,128)(2,1)S(1)}, bf16[32,1536]{1,0:T(8,128)(2,1)S(1)}, u32[]{:S(2)}, u32[]{:S(2)}) collective-permute-start(bf16[32,1536]{1,0:T(8,128)(2,1)S(1)} %get-tuple-element.303), channel_id=1, source_target_pairs={{0,16},{1,17},{2,18},{3,19},{4,20},{5,21},{6,22},{7,23},{8,24},{9,... | collective-permute-start | bytes 294920 | tf_op jit(solution)/shard_map/ppermute | solution.py:562
  18.6 12.9 %collective-permute-start.9 = (bf16[3,128,512]{2,1,0:T(8,128)(2,1)S(1)}, bf16[3,128,512]{2,1,0:T(8,128)(2,1)S(1)}, u32[]{:S(2)}, u32[]{:S(2)}) collective-permute-start(bf16[3,128,512]{2,1,0:T(8,128)(2,1)S(1)} %get-tuple-element.140), channel_id=1, source_target_pairs={{0,1},{1,0},{2,3},{3,2},{4,5},{5,4},{6,7},{7,6},{8,9},{9,8},{10,11... | collective-permute-start | bytes 1179656 | tf_op jit(solution)/shard_map/ppermute | solution.py:562
  22.7 10.1 %collective-permute-start.8 = (bf16[3,128,512]{2,1,0:T(8,128)(2,1)S(1)}, bf16[3,128,512]{2,1,0:T(8,128)(2,1)S(1)}, u32[]{:S(2)}, u32[]{:S(2)}) collective-permute-start(bf16[3,128,512]{2,1,0:T(8,128)(2,1)S(1)} %collective-permute-done.3), channel_id=1, source_target_pairs={{0,4},{1,5},{2,6},{3,7},{4,0},{5,1},{6,2},{7,3},{8,12},{9,13},{10,... | collective-permute-start | bytes 1179656 | tf_op jit(solution)/shard_map/ppermute | solution.py:562
  35.6 11.6 %collective-permute-start.12 = (bf16[128,1536]{1,0:T(8,128)(2,1)S(1)}, bf16[128,1536]{1,0:T(8,128)(2,1)S(1)}, u32[]{:S(2)}, u32[]{:S(2)}) collective-permute-start(bf16[128,1536]{1,0:T(8,128)(2,1)S(1)} %get-tuple-element.290), channel_id=1, source_target_pairs={{0,1},{1,0},{2,3},{3,2},{4,5},{5,4},{6,7},{7,6},{8,9},{9,8},{10,11... | collective-permute-start | bytes 1179656 | tf_op jit(solution)/shard_map/ppermute | solution.py:562
  36.7 10.6 %collective-permute-start.11 = (bf16[6,128,512]{2,1,0:T(8,128)(2,1)S(1)}, bf16[6,128,512]{2,1,0:T(8,128)(2,1)S(1)}, u32[]{:S(2)}, u32[]{:S(2)}) collective-permute-start(bf16[6,128,512]{2,1,0:T(8,128)(2,1)S(1)} %constant_dynamic-update-slice_fusion.17.refs_7_), channel_id=1, source_target_pairs={{0,2},{1,3},{2,0},{3,1},{4,6},{5,7},{6,4},{7,5},{8,10},{9,11},{10,... | collective-permute-start | bytes 2359304 | tf_op jit(solution)/shard_map/ppermute | solution.py:562
  37.0 13.6 %collective-permute-start.14 = (bf16[3,128,512]{2,1,0:T(8,128)(2,1)S(1)}, bf16[3,128,512]{2,1,0:T(8,128)(2,1)S(1)}, u32[]{:S(2)}, u32[]{:S(2)}) collective-permute-start(bf16[3,128,512]{2,1,0:T(8,128)(2,1)S(1)} %collective-permute-done.9), channel_id=1, source_target_pairs={{0,4},{1,5},{2,6},{3,7},{4,0},{5,1},{6,2},{7,3},{8,12},{9,13},{10,... | collective-permute-start | bytes 1179656 | tf_op jit(solution)/shard_map/ppermute | solution.py:562
  67.0 11.1 %collective-permute-start.19 = (bf16[8,32,768]{2,1,0:T(8,128)(2,1)S(1)}, bf16[8,32,768]{2,1,0:T(8,128)(2,1)S(1)}, u32[]{:S(2)}, u32[]{:S(2)}) collective-permute-start(bf16[8,32,768]{2,1,0:T(8,128)(2,1)S(1)} %get-tuple-element.255), channel_id=1, source_target_pairs={{0,1},{1,0},{2,3},{3,2},{4,5},{5,4},{6,7},{7,6},{8,9},{9,8},{10,11... | collective-permute-start | bytes 1179656 | tf_op jit(solution)/shard_map/ppermute | solution.py:562
  68.1 10.8 %collective-permute-start.18 = (bf16[8,32,768]{2,1,0:T(8,128)(2,1)S(1)}, bf16[8,32,768]{2,1,0:T(8,128)(2,1)S(1)}, u32[]{:S(2)}, u32[]{:S(2)}) collective-permute-start(bf16[8,32,768]{2,1,0:T(8,128)(2,1)S(1)} %get-tuple-element.256), channel_id=1, source_target_pairs={{0,4},{1,5},{2,6},{3,7},{4,0},{5,1},{6,2},{7,3},{8,12},{9,13},{10,... | collective-permute-start | bytes 1179656 | tf_op jit(solution)/shard_map/ppermute | solution.py:562
  79.1 12.6 %collective-permute-start.25 = (bf16[4,32,768]{2,1,0:T(8,128)(2,1)S(1)}, bf16[4,32,768]{2,1,0:T(8,128)(2,1)S(1)}, u32[]{:S(2)}, u32[]{:S(2)}) collective-permute-start(bf16[4,32,768]{2,1,0:T(8,128)(2,1)S(1)} %get-tuple-element.270), channel_id=1, source_target_pairs={{0,4},{1,5},{2,6},{3,7},{4,0},{5,1},{6,2},{7,3},{8,12},{9,13},{10,... | collective-permute-start | bytes 589832 | tf_op jit(solution)/shard_map/ppermute | solution.py:562
  80.8 11.0 %collective-permute-start.24 = (bf16[4,32,768]{2,1,0:T(8,128)(2,1)S(1)}, bf16[4,32,768]{2,1,0:T(8,128)(2,1)S(1)}, u32[]{:S(2)}, u32[]{:S(2)}) collective-permute-start(bf16[4,32,768]{2,1,0:T(8,128)(2,1)S(1)} %get-tuple-element.272), channel_id=1, source_target_pairs={{0,1},{1,0},{2,3},{3,2},{4,5},{5,4},{6,7},{7,6},{8,9},{9,8},{10,11... | collective-permute-start | bytes 589832 | tf_op jit(solution)/shard_map/ppermute | solution.py:562
  83.1 13.1 %collective-permute-start.23 = (bf16[8,32,768]{2,1,0:T(8,128)(2,1)S(1)}, bf16[8,32,768]{2,1,0:T(8,128)(2,1)S(1)}, u32[]{:S(2)}, u32[]{:S(2)}) collective-permute-start(bf16[8,32,768]{2,1,0:T(8,128)(2,1)S(1)} %get-tuple-element.251.refs_15_), channel_id=1, source_target_pairs={{0,1},{1,0},{2,3},{3,2},{4,5},{5,4},{6,7},{7,6},{8,9},{9,8},{10,11... | collective-permute-start | bytes 1179656 | tf_op jit(solution)/shard_map/ppermute | solution.py:562
  84.2 11.9 %collective-permute-start.22 = (bf16[8,32,768]{2,1,0:T(8,128)(2,1)S(1)}, bf16[8,32,768]{2,1,0:T(8,128)(2,1)S(1)}, u32[]{:S(2)}, u32[]{:S(2)}) collective-permute-start(bf16[8,32,768]{2,1,0:T(8,128)(2,1)S(1)} %get-tuple-element.252.refs_14_), channel_id=1, source_target_pairs={{0,4},{1,5},{2,6},{3,7},{4,0},{5,1},{6,2},{7,3},{8,12},{9,13},{10,... | collective-permute-start | bytes 1179656 | tf_op jit(solution)/shard_map/ppermute | solution.py:562
  91.9 16.7 %collective-permute-start.29 = (bf16[2,32,1536]{2,1,0:T(8,128)(2,1)S(1)}, bf16[2,32,1536]{2,1,0:T(8,128)(2,1)S(1)}, u32[]{:S(2)}, u32[]{:S(2)}) collective-permute-start(bf16[2,32,1536]{2,1,0:T(8,128)(2,1)S(1)} %pad_maximum_fusion.5), channel_id=1, source_target_pairs={{0,8},{1,9},{2,10},{3,11},{4,12},{5,13},{6,14},{7,15},{8,0},{9,1},... | collective-permute-start | bytes 589832 | tf_op jit(solution)/shard_map/ppermute | solution.py:562
  93.6 14.1 %collective-permute-start.30 = (bf16[8,16,1536]{2,1,0:T(8,128)(2,1)S(1)}, bf16[8,16,1536]{2,1,0:T(8,128)(2,1)S(1)}, u32[]{:S(2)}, u32[]{:S(2)}) collective-permute-start(bf16[8,16,1536]{2,1,0:T(8,128)(2,1)S(1)} %get-tuple-element.195.refs_8_), channel_id=1, source_target_pairs={{0,8},{1,9},{2,10},{3,11},{4,12},{5,13},{6,14},{7,15},{8,0},{9,1},... | collective-permute-start | bytes 1179656 | tf_op jit(solution)/shard_map/ppermute | solution.py:562
  96.3 15.1 %collective-permute-start.28 = (bf16[4,32,768]{2,1,0:T(8,128)(2,1)S(1)}, bf16[4,32,768]{2,1,0:T(8,128)(2,1)S(1)}, u32[]{:S(2)}, u32[]{:S(2)}) collective-permute-start(bf16[4,32,768]{2,1,0:T(8,128)(2,1)S(1)} %get-tuple-element.266), channel_id=1, source_target_pairs={{0,4},{1,5},{2,6},{3,7},{4,0},{5,1},{6,2},{7,3},{8,12},{9,13},{10,... | collective-permute-start | bytes 589832 | tf_op jit(solution)/shard_map/ppermute | solution.py:562
  96.9 14.5 %collective-permute-start.27 = (bf16[4,32,768]{2,1,0:T(8,128)(2,1)S(1)}, bf16[4,32,768]{2,1,0:T(8,128)(2,1)S(1)}, u32[]{:S(2)}, u32[]{:S(2)}) collective-permute-start(bf16[4,32,768]{2,1,0:T(8,128)(2,1)S(1)} %get-tuple-element.268), channel_id=1, source_target_pairs={{0,1},{1,0},{2,3},{3,2},{4,5},{5,4},{6,7},{7,6},{8,9},{9,8},{10,11... | collective-permute-start | bytes 589832 | tf_op jit(solution)/shard_map/ppermute | solution.py:562
  98.4 21.3 %collective-permute-start.26 = (bf16[9,16,1536]{2,1,0:T(8,128)(2,1)S(1)}, bf16[9,16,1536]{2,1,0:T(8,128)(2,1)S(1)}, u32[]{:S(2)}, u32[]{:S(2)}) collective-permute-start(bf16[9,16,1536]{2,1,0:T(8,128)(2,1)S(1)} %maximum_maximum_fusion), channel_id=1, source_target_pairs={{0,1},{1,0},{2,3},{3,2},{4,5},{5,4},{6,7},{7,6},{8,9},{9,8},{10,11... | collective-permute-start | bytes 1327112 | tf_op jit(solution)/shard_map/ppermute | solution.py:562
  107.8 13.4 %collective-permute-start.36 = (bf16[4,16,1536]{2,1,0:T(8,128)(2,1)S(1)}, bf16[4,16,1536]{2,1,0:T(8,128)(2,1)S(1)}, u32[]{:S(2)}, u32[]{:S(2)}) collective-permute-start(bf16[4,16,1536]{2,1,0:T(8,128)(2,1)S(1)} %get-tuple-element.264), channel_id=1, source_target_pairs={{0,4},{1,5},{2,6},{3,7},{4,0},{5,1},{6,2},{7,3},{8,12},{9,13},{10,... | collective-permute-start | bytes 589832 | tf_op jit(solution)/shard_map/ppermute | solution.py:562
  115.4 11.4 %collective-permute-start.35 = (bf16[1,32,1536]{2,1,0:T(8,128)(2,1)S(1)}, bf16[1,32,1536]{2,1,0:T(8,128)(2,1)S(1)}, u32[]{:S(2)}, u32[]{:S(2)}) collective-permute-start(bf16[1,32,1536]{2,1,0:T(8,128)(2,1)S(1)} %add_convert_fusion.31), channel_id=1, source_target_pairs={{0,16},{1,17},{2,18},{3,19},{4,20},{5,21},{6,22},{7,23},{8,24},{9,... | collective-permute-start | bytes 294920 | tf_op jit(solution)/shard_map/ppermute | solution.py:562
  119.7 10.2 %collective-permute-start.34 = (bf16[1,32,1536]{2,1,0:T(8,128)(2,1)S(1)}, bf16[1,32,1536]{2,1,0:T(8,128)(2,1)S(1)}, u32[]{:S(2)}, u32[]{:S(2)}) collective-permute-start(bf16[1,32,1536]{2,1,0:T(8,128)(2,1)S(1)} %add_convert_fusion.30), channel_id=1, source_target_pairs={{0,16},{1,17},{2,18},{3,19},{4,20},{5,21},{6,22},{7,23},{8,24},{9,... | collective-permute-start | bytes 294920 | tf_op jit(solution)/shard_map/ppermute | solution.py:562
  119.9 11.0 %collective-permute-start.33 = (bf16[5,16,1536]{2,1,0:T(8,128)(2,1)S(1)}, bf16[5,16,1536]{2,1,0:T(8,128)(2,1)S(1)}, u32[]{:S(2)}, u32[]{:S(2)}) collective-permute-start(bf16[5,16,1536]{2,1,0:T(8,128)(2,1)S(1)} %maximum_maximum_fusion.1), channel_id=1, source_target_pairs={{0,4},{1,5},{2,6},{3,7},{4,0},{5,1},{6,2},{7,3},{8,12},{9,13},{10,... | collective-permute-start | bytes 737288 | tf_op jit(solution)/shard_map/ppermute | solution.py:562
  121.2 12.8 %collective-permute-start.40 = (bf16[2,16,1536]{2,1,0:T(8,128)(2,1)S(1)}, bf16[2,16,1536]{2,1,0:T(8,128)(2,1)S(1)}, u32[]{:S(2)}, u32[]{:S(2)}) collective-permute-start(bf16[2,16,1536]{2,1,0:T(8,128)(2,1)S(1)} %get-tuple-element.276), channel_id=1, source_target_pairs={{0,16},{1,17},{2,18},{3,19},{4,20},{5,21},{6,22},{7,23},{8,24},{9,... | collective-permute-start | bytes 294920 | tf_op jit(solution)/shard_map/ppermute | solution.py:562
  126.8 9.8 %collective-permute-start.39 = (bf16[2,32,1536]{2,1,0:T(8,128)(2,1)S(1)}, bf16[2,32,1536]{2,1,0:T(8,128)(2,1)S(1)}, u32[]{:S(2)}, u32[]{:S(2)}) collective-permute-start(bf16[2,32,1536]{2,1,0:T(8,128)(2,1)S(1)} %pad_maximum_fusion.7), channel_id=1, source_target_pairs={{0,8},{1,9},{2,10},{3,11},{4,12},{5,13},{6,14},{7,15},{8,0},{9,1},... | collective-permute-start | bytes 589832 | tf_op jit(solution)/shard_map/ppermute | solution.py:562
  (36 other events, 350.2 us)

commit v11 on v10

--- a/solution.py
+++ b/solution.py
@@ -652,7 +652,7 @@
         block_0 = tie(block_0, block_1)
         got_0 = swap(block_0, hops_0[-2])
         got_1 = swap(block_1, hops_1[-2])
-        block_0 = join(block_0, tie(got_0, start.a, got_ff_0, ff_1))
+        block_0 = join(block_0, tie(got_0, start.a, got_ff_0, ff_1, got_1))
         ff_0 = join(ff_0, tie(got_ff_0, block_0))
         got_ff_1 = swap(tie(ff_1, ff_0), 4)
         attn_pieces = [(block_0, swap(block_0, 2), order_masks(hops_0[::-1]))]
@@ -1021,6 +1021,7 @@
             token = done[0]
         if turn != 2:
             token = attn_0.step(token)
+        if turn > 2:
             token = attn_1.step(token)
         if sums is None and attn_0.arriving is None:
             sums = run(

time: 159 us -> 153 us (0.962)
  waiting for transfers between devices: 49.6 us -> 46.2 us
    ppermute x48, waiting for transfers between devices: 49.6 us -> 46.2 us  [swap(): return lax.ppermute(array, axes, [(n, n ^ mask) for n in range(devices)])]
  transfers between devices with their start and end apart: 48 -> 48, of which waited for: 20 -> 22; matrix products, arithmetic and copies ran while one was open for 3% -> 3% of each run, Pallas kernels for 22% -> 22%
where the time goes in v11:
time: 153 us
  starting transfers between devices  55.6 us (36%)
  waiting for transfers between devices  46.2 us (30%)
  Pallas kernels  45.1 us (29%)
  other arithmetic  4.08 us (3%)
  between operations  1.6 us (1%)
    ppermute x48, starting transfers between devices, swap(): return lax.ppermute(array, axes, [(n, n ^ mask) for n in range(devices)])  55.6 us
    ppermute x48, waiting for transfers between devices, swap(): return lax.ppermute(array, axes, [(n, n ^ mask) for n in range(devices)])  46.2 us
    pallas_call x10, Pallas kernels, run(): pl.pallas_call(kernel, name=name, in_specs=[pl.BlockSpec(memory_space=in_...  38.4 us
    pallas_call x4, Pallas kernels, finish(): pl.pallas_call(kernel, name='layer_%d_ff_grads' % layer_idx, in_specs=[pl...  6.67 us
  transfers between devices with their start and end apart: 48, of which 22 were waited for; matrix products, arithmetic and copies ran while one was open for 3% of the time, Pallas kernels for 22%

profile of v11, /device:TPU:0, one launch (start us, length us, event | category | flops | bytes accessed | tf_op | source)
XLA Modules:
  0.0 153.0 jit_solution(8110699774494423643)
XLA Ops:
  2.6 3.0 %collective-permute-start.1 = (bf16[16,1536]{1,0:T(8,128)(2,1)S(1)}, bf16[16,1536]{1,0:T(8,128)(2,1)S(1)}, u32[]{:S(2)}, u32[]{:S(2)}) collective-permute-start(bf16[16,1536]{1,0:T(8,128)(2,1)S(1)} %get-tuple-element.126), channel_id=1, source_target_pairs={{0,1},{1,0},{2,3},{3,2},{4,5},{5,4},{6,7},{7,6},{8,9},{9,8},{10,11... | collective-permute-start | bytes 147464 | tf_op jit(solution)/shard_map/ppermute | solution.py:562
  5.6 2.6 %collective-permute-start = (bf16[16,1536]{1,0:T(8,128)(2,1)S(1)}, bf16[16,1536]{1,0:T(8,128)(2,1)S(1)}, u32[]{:S(2)}, u32[]{:S(2)}) collective-permute-start(bf16[16,1536]{1,0:T(8,128)(2,1)S(1)} %get-tuple-element.125), channel_id=1, source_target_pairs={{0,16},{1,17},{2,18},{3,19},{4,20},{5,21},{6,22},{7,23},{8,24},{9,... | collective-permute-start | bytes 147464 | tf_op jit(solution)/shard_map/ppermute | solution.py:562
  9.7 2.7 %collective-permute-start.2 = (bf16[32,1536]{1,0:T(8,128)(2,1)S(1)}, bf16[32,1536]{1,0:T(8,128)(2,1)S(1)}, u32[]{:S(2)}, u32[]{:S(2)}) collective-permute-start(bf16[32,1536]{1,0:T(8,128)(2,1)S(1)} %get-tuple-element.303), channel_id=1, source_target_pairs={{0,16},{1,17},{2,18},{3,19},{4,20},{5,21},{6,22},{7,23},{8,24},{9,... | collective-permute-start | bytes 294920 | tf_op jit(solution)/shard_map/ppermute | solution.py:562
  13.9 4.6 %collective-permute-done.3 = bf16[3,128,512]{2,1,0:T(8,128)(2,1)S(1)} collective-permute-done((bf16[3,128,512]{2,1,0:T(8,128)(2,1)S(1)}, bf16[3,128,512]{2,1,0:T(8,128)(2,1)S(1)}, u32[]{:S(2)}, u32[]{:S(2)}) %collective-permute-start.3) | collective-permute-done | bytes 393248 | tf_op jit(solution)/shard_map/ppermute | solution.py:562
  23.2 4.0 %collective-permute-done.4 = bf16[64,1536]{1,0:T(8,128)(2,1)S(1)} collective-permute-done((bf16[64,1536]{1,0:T(8,128)(2,1)S(1)}, bf16[64,1536]{1,0:T(8,128)(2,1)S(1)}, u32[]{:S(2)}, u32[]{:S(2)}) %collective-permute-start.4) | collective-permute-done | bytes 196640 | tf_op jit(solution)/shard_map/ppermute | solution.py:562
  32.8 3.6 %collective-permute-done.7 = bf16[128,1536]{1,0:T(8,128)(2,1)S(1)} collective-permute-done((bf16[128,1536]{1,0:T(8,128)(2,1)S(1)}, bf16[128,1536]{1,0:T(8,128)(2,1)S(1)}, u32[]{:S(2)}, u32[]{:S(2)}) %collective-permute-start.7) | collective-permute-done | bytes 393248 | tf_op jit(solution)/shard_map/ppermute | solution.py:562
  38.8 2.8 %layer_0_attention.1 = (bf16[512,1536]{1,0:T(8,128)(2,1)S(1)}, bf16[512,1152]{1,0:T(8,128)(2,1)S(1)}, f32[512,384]{1,0:T(8,128)S(1)}, bf16[512,384]{1,0:T(8,128)...) custom-call(s32[4]{0:T(128)S(1)} %pad_add_fusion.refs_0_.place_ref, ...), custom_call_target="tpu_custom_call" | custom-call | flops 11500000256 | tf_op jit(solution)/shard_map/layer_0_attention/pallas_call | solution.py:99
  41.8 3.2 %layer_0_ff.1 = (bf16[2,512,1024]{2,1,0:T(8,128)(2,1)S(1)}, bf16[2,512,512]{2,1,0:T(8,128)(2,1)S(1)}, f32[512,512]{1,0:T(8,128)S(1)}, bf16[512,512]{1,0:T(8,128)(2,1)S(1)}) custom-call(s32[4]{0:T(128)S(1)} %pad_add_fusion.refs_0_.place_ref, f32[512,512]{1,0:T(8,128)S(1)} %get-tuple-element.142.refs_1_.refs_4_, ...), custom_call_target="tpu_custom_call" | custom-call | flops 3449999872 | tf_op jit(solution)/shard_map/layer_0_ff/pallas_call | solution.py:99
  45.0 3.3 %collective-permute-done.14 = bf16[3,128,512]{2,1,0:T(8,128)(2,1)S(1)} collective-permute-done((bf16[3,128,512]{2,1,0:T(8,128)(2,1)S(1)}, bf16[3,128,512]{2,1,0:T(8,128)(2,1)S(1)}, u32[]{:S(2)}, u32[]{:S(2)}) %collective-permute-start.14) | collective-permute-done | bytes 393248 | tf_op jit(solution)/shard_map/ppermute | solution.py:562
  48.4 2.8 %layer_1_attention.1 = (bf16[512,1536]{1,0:T(8,128)(2,1)S(1)}, bf16[512,1152]{1,0:T(8,128)(2,1)S(1)}, f32[512,384]{1,0:T(8,128)S(1)}, bf16[512,384]{1,0:T(8,128)...) custom-call(s32[4]{0:T(128)S(1)} %pad_add_fusion.refs_0_.place_ref, ...), custom_call_target="tpu_custom_call" | custom-call | flops 115000000 | tf_op jit(solution)/shard_map/layer_1_attention/pallas_call | solution.py:99
  51.2 7.3 %layer_1_ff.1 = (bf16[32,32,768]{2,1,0:T(8,128)(2,1)S(1)}, bf16[32,32,768]{2,1,0:T(8,128)(2,1)S(1)}, f32[8,1536]{1,0:T(8,128)S(1)}, f32[512,512]{1,0:T(8,128)S(1...) custom-call(s32[4]{0:T(128)S(1)} %pad_add_fusion.refs_0_.place_ref, bf16[512,512]{1,0:T(8,128)(2,1)S(1)} %bitcast.58, ...), custom_call_target="tpu_custom_call" | custom-call | flops 9200000000 | tf_op jit(solution)/shard_map/layer_1_ff/pallas_call | solution.py:99
  59.1 4.6 %layer_1_attention_backward.1 = (bf16[16,16,1536]{2,1,0:T(8,128)(2,1)S(1)}, bf16[16,16,1536]{2,1,0:T(8,128)(2,1)S(1)}, f32[8,1536]{1,0:T(8,128)S(1)}, f32[512,512]{1,0:T(8,128)S(1)}, f32[64,384]{1,0:T(8,128)S(1)}) custom-call(s32[4]{0:T(128)S(1)} %pad_add_fusion.refs_0_.place_ref, f32[8,1536]{1,0:T(8,128)S(1)} %get-tuple-element.153.refs_1_, ...), custom_call_target="tpu_custom_call" | custom-call | flops 6899999744 | tf_op jit(solution)/shard_map/layer_1_attention_backward/pallas_call | solution.py:99
  67.0 7.1 %layer_0_ff_backward.1 = (bf16[32,32,768]{2,1,0:T(8,128)(2,1)S(1)}, bf16[32,32,768]{2,1,0:T(8,128)(2,1)S(1)}, f32[8,1536]{1,0:T(8,128)S(1)}, f32[512,512]{1,0:T(8,128)S(1)}, bf16[512,512]{1,0:T(8,128)(2,1)S(1)}) custom-call(s32[4]{0:T(128)S(1)} %pad_add_fusion.refs_0_.place_ref, f32[512,512]{1,0:T(8,128)S(1)} %get-tuple-element.163.refs_1_, ...), custom_call_target="tpu_custom_call" | custom-call | flops 9200000000 | tf_op jit(solution)/shard_map/layer_0_ff_backward/pallas_call | solution.py:99
  83.6 6.1 %layer_0_attention_backward.1 = (bf16[16,16,1536]{2,1,0:T(8,128)(2,1)S(1)}, bf16[17,16,1536]{2,1,0:T(8,128)(2,1)S(1)}, f32[8,1536]{1,0:T(8,128)S(1)}, f32[512,512]{1,0:T(8,128)}) custom-call(s32[4]{0:T(128)S(1)} %pad_add_fusion.refs_0_.place_ref, f32[64,384]{1,0:T(8,128)S(1)} %get-tuple-element.160.refs_1_, s32[512,128]{1,0:T(8,128)S(1)} %get-tuple-element.161.refs_2_, ...), custom_call_target="tpu_custom_call" | custom-call | flops 8049999872 | tf_op jit(solution)/shard_map/layer_0_attention_backward/pallas_call | solution.py:99
  100.1 2.6 %collective-permute-done.27 = bf16[4,32,768]{2,1,0:T(8,128)(2,1)S(1)} collective-permute-done((bf16[4,32,768]{2,1,0:T(8,128)(2,1)S(1)}, bf16[4,32,768]{2,1,0:T(8,128)(2,1)S(1)}, u32[]{:S(2)}, u32[]{:S(2)}) %collective-permute-start.27) | collective-permute-done | bytes 196640 | tf_op jit(solution)/shard_map/ppermute | solution.py:562
  104.4 2.9 %collective-permute-done.31 = bf16[1,32,1536]{2,1,0:T(8,128)(2,1)S(1)} collective-permute-done((bf16[1,32,1536]{2,1,0:T(8,128)(2,1)S(1)}, bf16[1,32,1536]{2,1,0:T(8,128)(2,1)S(1)}, u32[]{:S(2)}, u32[]{:S(2)}) %collective-permute-start.31) | collective-permute-done | bytes 98336 | tf_op jit(solution)/shard_map/ppermute | solution.py:562
  107.4 3.4 %collective-permute-start.34 = (bf16[1,32,1536]{2,1,0:T(8,128)(2,1)S(1)}, bf16[1,32,1536]{2,1,0:T(8,128)(2,1)S(1)}, u32[]{:S(2)}, u32[]{:S(2)}) collective-permute-start(bf16[1,32,1536]{2,1,0:T(8,128)(2,1)S(1)} %add_convert_fusion.31), channel_id=1, source_target_pairs={{0,16},{1,17},{2,18},{3,19},{4,20},{5,21},{6,22},{7,23},{8,24},{9,... | collective-permute-start | bytes 294920 | tf_op jit(solution)/shard_map/ppermute | solution.py:562
  110.8 3.3 %collective-permute-done.30 = bf16[2,32,1536]{2,1,0:T(8,128)(2,1)S(1)} collective-permute-done((bf16[2,32,1536]{2,1,0:T(8,128)(2,1)S(1)}, bf16[2,32,1536]{2,1,0:T(8,128)(2,1)S(1)}, u32[]{:S(2)}, u32[]{:S(2)}) %collective-permute-start.30) | collective-permute-done | bytes 196640 | tf_op jit(solution)/shard_map/ppermute | solution.py:562
  117.7 2.5 %collective-permute-start.38 = (bf16[2,32,1536]{2,1,0:T(8,128)(2,1)S(1)}, bf16[2,32,1536]{2,1,0:T(8,128)(2,1)S(1)}, u32[]{:S(2)}, u32[]{:S(2)}) collective-permute-start(bf16[2,32,1536]{2,1,0:T(8,128)(2,1)S(1)} %pad_maximum_fusion.7), channel_id=1, source_target_pairs={{0,8},{1,9},{2,10},{3,11},{4,12},{5,13},{6,14},{7,15},{8,0},{9,1},... | collective-permute-start | bytes 589832 | tf_op jit(solution)/shard_map/ppermute | solution.py:562
  121.7 2.7 %collective-permute-done.32 = bf16[5,16,1536]{2,1,0:T(8,128)(2,1)S(1)} collective-permute-done((bf16[5,16,1536]{2,1,0:T(8,128)(2,1)S(1)}, bf16[5,16,1536]{2,1,0:T(8,128)(2,1)S(1)}, u32[]{:S(2)}, u32[]{:S(2)}) %collective-permute-start.32) | collective-permute-done | bytes 245792 | tf_op jit(solution)/shard_map/ppermute | solution.py:562
  124.5 2.5 %collective-permute-start.36 = (bf16[3,16,1536]{2,1,0:T(8,128)(2,1)S(1)}, bf16[3,16,1536]{2,1,0:T(8,128)(2,1)S(1)}, u32[]{:S(2)}, u32[]{:S(2)}) collective-permute-start(bf16[3,16,1536]{2,1,0:T(8,128)(2,1)S(1)} %maximum_maximum_fusion.2), channel_id=1, source_target_pairs={{0,8},{1,9},{2,10},{3,11},{4,12},{5,13},{6,14},{7,15},{8,0},{9,1},... | collective-permute-start | bytes 442376 | tf_op jit(solution)/shard_map/ppermute | solution.py:562
  130.6 3.3 %collective-permute-done.36 = bf16[3,16,1536]{2,1,0:T(8,128)(2,1)S(1)} collective-permute-done((bf16[3,16,1536]{2,1,0:T(8,128)(2,1)S(1)}, bf16[3,16,1536]{2,1,0:T(8,128)(2,1)S(1)}, u32[]{:S(2)}, u32[]{:S(2)}) %collective-permute-start.36) | collective-permute-done | bytes 147488 | tf_op jit(solution)/shard_map/ppermute | solution.py:562
  135.0 2.9 %collective-permute-done.41 = bf16[4,32,1536]{2,1,0:T(8,128)(2,1)S(1)} collective-permute-done((bf16[4,32,1536]{2,1,0:T(8,128)(2,1)S(1)}, bf16[4,32,1536]{2,1,0:T(8,128)(2,1)S(1)}, u32[]{:S(2)}, u32[]{:S(2)}) %collective-permute-start.41) | collective-permute-done | bytes 393248 | tf_op jit(solution)/shard_map/ppermute | solution.py:562
  143.7 5.0 %collective-permute-done.45 = bf16[4,32,1536]{2,1,0:T(8,128)(2,1)S(1)} collective-permute-done((bf16[4,32,1536]{2,1,0:T(8,128)(2,1)S(1)}, bf16[4,32,1536]{2,1,0:T(8,128)(2,1)S(1)}, u32[]{:S(2)}, u32[]{:S(2)}) %collective-permute-start.45) | collective-permute-done | bytes 393248 | tf_op jit(solution)/shard_map/ppermute | solution.py:562
  (178 shorter events, 62.4 us)
Async XLA Ops:
  8.3 10.3 %collective-permute-start.3 = (bf16[3,128,512]{2,1,0:T(8,128)(2,1)S(1)}, bf16[3,128,512]{2,1,0:T(8,128)(2,1)S(1)}, u32[]{:S(2)}, u32[]{:S(2)}) collective-permute-start(bf16[3,128,512]{2,1,0:T(8,128)(2,1)S(1)} %get-tuple-element.134), channel_id=1, source_target_pairs={{0,1},{1,0},{2,3},{3,2},{4,5},{5,4},{6,7},{7,6},{8,9},{9,8},{10,11... | collective-permute-start | bytes 1179656 | tf_op jit(solution)/shard_map/ppermute | solution.py:562
  9.7 9.7 %collective-permute-start.2 = (bf16[32,1536]{1,0:T(8,128)(2,1)S(1)}, bf16[32,1536]{1,0:T(8,128)(2,1)S(1)}, u32[]{:S(2)}, u32[]{:S(2)}) collective-permute-start(bf16[32,1536]{1,0:T(8,128)(2,1)S(1)} %get-tuple-element.303), channel_id=1, source_target_pairs={{0,16},{1,17},{2,18},{3,19},{4,20},{5,21},{6,22},{7,23},{8,24},{9,... | collective-permute-start | bytes 294920 | tf_op jit(solution)/shard_map/ppermute | solution.py:562
  18.6 13.9 %collective-permute-start.9 = (bf16[3,128,512]{2,1,0:T(8,128)(2,1)S(1)}, bf16[3,128,512]{2,1,0:T(8,128)(2,1)S(1)}, u32[]{:S(2)}, u32[]{:S(2)}) collective-permute-start(bf16[3,128,512]{2,1,0:T(8,128)(2,1)S(1)} %get-tuple-element.140), channel_id=1, source_target_pairs={{0,1},{1,0},{2,3},{3,2},{4,5},{5,4},{6,7},{7,6},{8,9},{9,8},{10,11... | collective-permute-start | bytes 1179656 | tf_op jit(solution)/shard_map/ppermute | solution.py:562
  22.7 10.1 %collective-permute-start.8 = (bf16[3,128,512]{2,1,0:T(8,128)(2,1)S(1)}, bf16[3,128,512]{2,1,0:T(8,128)(2,1)S(1)}, u32[]{:S(2)}, u32[]{:S(2)}) collective-permute-start(bf16[3,128,512]{2,1,0:T(8,128)(2,1)S(1)} %collective-permute-done.3), channel_id=1, source_target_pairs={{0,4},{1,5},{2,6},{3,7},{4,0},{5,1},{6,2},{7,3},{8,12},{9,13},{10,... | collective-permute-start | bytes 1179656 | tf_op jit(solution)/shard_map/ppermute | solution.py:562
  27.3 9.1 %collective-permute-start.10 = (bf16[128,1536]{1,0:T(8,128)(2,1)S(1)}, bf16[128,1536]{1,0:T(8,128)(2,1)S(1)}, u32[]{:S(2)}, u32[]{:S(2)}) collective-permute-start(bf16[128,1536]{1,0:T(8,128)(2,1)S(1)} %get-tuple-element.290), channel_id=1, source_target_pairs={{0,1},{1,0},{2,3},{3,2},{4,5},{5,4},{6,7},{7,6},{8,9},{9,8},{10,11... | collective-permute-start | bytes 1179656 | tf_op jit(solution)/shard_map/ppermute | solution.py:562
  37.2 11.1 %collective-permute-start.14 = (bf16[3,128,512]{2,1,0:T(8,128)(2,1)S(1)}, bf16[3,128,512]{2,1,0:T(8,128)(2,1)S(1)}, u32[]{:S(2)}, u32[]{:S(2)}) collective-permute-start(bf16[3,128,512]{2,1,0:T(8,128)(2,1)S(1)} %collective-permute-done.9), channel_id=1, source_target_pairs={{0,4},{1,5},{2,6},{3,7},{4,0},{5,1},{6,2},{7,3},{8,12},{9,13},{10,... | collective-permute-start | bytes 1179656 | tf_op jit(solution)/shard_map/ppermute | solution.py:562
  64.3 11.6 %collective-permute-start.19 = (bf16[8,32,768]{2,1,0:T(8,128)(2,1)S(1)}, bf16[8,32,768]{2,1,0:T(8,128)(2,1)S(1)}, u32[]{:S(2)}, u32[]{:S(2)}) collective-permute-start(bf16[8,32,768]{2,1,0:T(8,128)(2,1)S(1)} %get-tuple-element.255), channel_id=1, source_target_pairs={{0,1},{1,0},{2,3},{3,2},{4,5},{5,4},{6,7},{7,6},{8,9},{9,8},{10,11... | collective-permute-start | bytes 1179656 | tf_op jit(solution)/shard_map/ppermute | solution.py:562
  65.1 11.2 %collective-permute-start.18 = (bf16[8,32,768]{2,1,0:T(8,128)(2,1)S(1)}, bf16[8,32,768]{2,1,0:T(8,128)(2,1)S(1)}, u32[]{:S(2)}, u32[]{:S(2)}) collective-permute-start(bf16[8,32,768]{2,1,0:T(8,128)(2,1)S(1)} %get-tuple-element.256), channel_id=1, source_target_pairs={{0,4},{1,5},{2,6},{3,7},{4,0},{5,1},{6,2},{7,3},{8,12},{9,13},{10,... | collective-permute-start | bytes 1179656 | tf_op jit(solution)/shard_map/ppermute | solution.py:562
  76.7 13.1 %collective-permute-start.25 = (bf16[4,32,768]{2,1,0:T(8,128)(2,1)S(1)}, bf16[4,32,768]{2,1,0:T(8,128)(2,1)S(1)}, u32[]{:S(2)}, u32[]{:S(2)}) collective-permute-start(bf16[4,32,768]{2,1,0:T(8,128)(2,1)S(1)} %get-tuple-element.270), channel_id=1, source_target_pairs={{0,4},{1,5},{2,6},{3,7},{4,0},{5,1},{6,2},{7,3},{8,12},{9,13},{10,... | collective-permute-start | bytes 589832 | tf_op jit(solution)/shard_map/ppermute | solution.py:562
  78.3 11.5 %collective-permute-start.24 = (bf16[4,32,768]{2,1,0:T(8,128)(2,1)S(1)}, bf16[4,32,768]{2,1,0:T(8,128)(2,1)S(1)}, u32[]{:S(2)}, u32[]{:S(2)}) collective-permute-start(bf16[4,32,768]{2,1,0:T(8,128)(2,1)S(1)} %get-tuple-element.272), channel_id=1, source_target_pairs={{0,1},{1,0},{2,3},{3,2},{4,5},{5,4},{6,7},{7,6},{8,9},{9,8},{10,11... | collective-permute-start | bytes 589832 | tf_op jit(solution)/shard_map/ppermute | solution.py:562
  80.6 13.1 %collective-permute-start.23 = (bf16[8,32,768]{2,1,0:T(8,128)(2,1)S(1)}, bf16[8,32,768]{2,1,0:T(8,128)(2,1)S(1)}, u32[]{:S(2)}, u32[]{:S(2)}) collective-permute-start(bf16[8,32,768]{2,1,0:T(8,128)(2,1)S(1)} %get-tuple-element.251.refs_15_), channel_id=1, source_target_pairs={{0,1},{1,0},{2,3},{3,2},{4,5},{5,4},{6,7},{7,6},{8,9},{9,8},{10,11... | collective-permute-start | bytes 1179656 | tf_op jit(solution)/shard_map/ppermute | solution.py:562
  82.0 11.8 %collective-permute-start.22 = (bf16[8,32,768]{2,1,0:T(8,128)(2,1)S(1)}, bf16[8,32,768]{2,1,0:T(8,128)(2,1)S(1)}, u32[]{:S(2)}, u32[]{:S(2)}) collective-permute-start(bf16[8,32,768]{2,1,0:T(8,128)(2,1)S(1)} %get-tuple-element.252.refs_14_), channel_id=1, source_target_pairs={{0,4},{1,5},{2,6},{3,7},{4,0},{5,1},{6,2},{7,3},{8,12},{9,13},{10,... | collective-permute-start | bytes 1179656 | tf_op jit(solution)/shard_map/ppermute | solution.py:562
  91.6 24.4 %collective-permute-start.35 = (bf16[8,16,1536]{2,1,0:T(8,128)(2,1)S(1)}, bf16[8,16,1536]{2,1,0:T(8,128)(2,1)S(1)}, u32[]{:S(2)}, u32[]{:S(2)}) collective-permute-start(bf16[8,16,1536]{2,1,0:T(8,128)(2,1)S(1)} %get-tuple-element.201.refs_8_), channel_id=1, source_target_pairs={{0,8},{1,9},{2,10},{3,11},{4,12},{5,13},{6,14},{7,15},{8,0},{9,1},... | collective-permute-start | bytes 1179656 | tf_op jit(solution)/shard_map/ppermute | solution.py:562
  96.1 19.1 %collective-permute-start.26 = (bf16[9,16,1536]{2,1,0:T(8,128)(2,1)S(1)}, bf16[9,16,1536]{2,1,0:T(8,128)(2,1)S(1)}, u32[]{:S(2)}, u32[]{:S(2)}) collective-permute-start(bf16[9,16,1536]{2,1,0:T(8,128)(2,1)S(1)} %maximum_maximum_fusion), channel_id=1, source_target_pairs={{0,1},{1,0},{2,3},{3,2},{4,5},{5,4},{6,7},{7,6},{8,9},{9,8},{10,11... | collective-permute-start | bytes 1327112 | tf_op jit(solution)/shard_map/ppermute | solution.py:562
  97.7 9.6 %collective-permute-start.31 = (bf16[1,32,1536]{2,1,0:T(8,128)(2,1)S(1)}, bf16[1,32,1536]{2,1,0:T(8,128)(2,1)S(1)}, u32[]{:S(2)}, u32[]{:S(2)}) collective-permute-start(bf16[1,32,1536]{2,1,0:T(8,128)(2,1)S(1)} %add_convert_fusion.37), channel_id=1, source_target_pairs={{0,16},{1,17},{2,18},{3,19},{4,20},{5,21},{6,22},{7,23},{8,24},{9,... | collective-permute-start | bytes 294920 | tf_op jit(solution)/shard_map/ppermute | solution.py:562
  102.8 11.4 %collective-permute-start.30 = (bf16[2,32,1536]{2,1,0:T(8,128)(2,1)S(1)}, bf16[2,32,1536]{2,1,0:T(8,128)(2,1)S(1)}, u32[]{:S(2)}, u32[]{:S(2)}) collective-permute-start(bf16[2,32,1536]{2,1,0:T(8,128)(2,1)S(1)} %pad_maximum_fusion.6), channel_id=1, source_target_pairs={{0,8},{1,9},{2,10},{3,11},{4,12},{5,13},{6,14},{7,15},{8,0},{9,1},... | collective-permute-start | bytes 589832 | tf_op jit(solution)/shard_map/ppermute | solution.py:562
  107.4 10.3 %collective-permute-start.34 = (bf16[1,32,1536]{2,1,0:T(8,128)(2,1)S(1)}, bf16[1,32,1536]{2,1,0:T(8,128)(2,1)S(1)}, u32[]{:S(2)}, u32[]{:S(2)}) collective-permute-start(bf16[1,32,1536]{2,1,0:T(8,128)(2,1)S(1)} %add_convert_fusion.31), channel_id=1, source_target_pairs={{0,16},{1,17},{2,18},{3,19},{4,20},{5,21},{6,22},{7,23},{8,24},{9,... | collective-permute-start | bytes 294920 | tf_op jit(solution)/shard_map/ppermute | solution.py:562
  115.4 9.0 %collective-permute-start.32 = (bf16[5,16,1536]{2,1,0:T(8,128)(2,1)S(1)}, bf16[5,16,1536]{2,1,0:T(8,128)(2,1)S(1)}, u32[]{:S(2)}, u32[]{:S(2)}) collective-permute-start(bf16[5,16,1536]{2,1,0:T(8,128)(2,1)S(1)} %maximum_maximum_fusion.1), channel_id=1, source_target_pairs={{0,4},{1,5},{2,6},{3,7},{4,0},{5,1},{6,2},{7,3},{8,12},{9,13},{10,... | collective-permute-start | bytes 737288 | tf_op jit(solution)/shard_map/ppermute | solution.py:562
  116.1 10.9 %collective-permute-start.39 = (bf16[4,16,1536]{2,1,0:T(8,128)(2,1)S(1)}, bf16[4,16,1536]{2,1,0:T(8,128)(2,1)S(1)}, u32[]{:S(2)}, u32[]{:S(2)}) collective-permute-start(bf16[4,16,1536]{2,1,0:T(8,128)(2,1)S(1)} %get-tuple-element.264), channel_id=1, source_target_pairs={{0,4},{1,5},{2,6},{3,7},{4,0},{5,1},{6,2},{7,3},{8,12},{9,13},{10,... | collective-permute-start | bytes 589832 | tf_op jit(solution)/shard_map/ppermute | solution.py:562
  117.7 11.1 %collective-permute-start.38 = (bf16[2,32,1536]{2,1,0:T(8,128)(2,1)S(1)}, bf16[2,32,1536]{2,1,0:T(8,128)(2,1)S(1)}, u32[]{:S(2)}, u32[]{:S(2)}) collective-permute-start(bf16[2,32,1536]{2,1,0:T(8,128)(2,1)S(1)} %pad_maximum_fusion.7), channel_id=1, source_target_pairs={{0,8},{1,9},{2,10},{3,11},{4,12},{5,13},{6,14},{7,15},{8,0},{9,1},... | collective-permute-start | bytes 589832 | tf_op jit(solution)/shard_map/ppermute | solution.py:562
  124.5 9.4 %collective-permute-start.36 = (bf16[3,16,1536]{2,1,0:T(8,128)(2,1)S(1)}, bf16[3,16,1536]{2,1,0:T(8,128)(2,1)S(1)}, u32[]{:S(2)}, u32[]{:S(2)}) collective-permute-start(bf16[3,16,1536]{2,1,0:T(8,128)(2,1)S(1)} %maximum_maximum_fusion.2), channel_id=1, source_target_pairs={{0,8},{1,9},{2,10},{3,11},{4,12},{5,13},{6,14},{7,15},{8,0},{9,1},... | collective-permute-start | bytes 442376 | tf_op jit(solution)/shard_map/ppermute | solution.py:562
  128.9 9.1 %collective-permute-start.41 = (bf16[4,32,1536]{2,1,0:T(8,128)(2,1)S(1)}, bf16[4,32,1536]{2,1,0:T(8,128)(2,1)S(1)}, u32[]{:S(2)}, u32[]{:S(2)}) collective-permute-start(bf16[4,32,1536]{2,1,0:T(8,128)(2,1)S(1)} %pad_maximum_fusion.2), channel_id=1, source_target_pairs={{0,4},{1,5},{2,6},{3,7},{4,0},{5,1},{6,2},{7,3},{8,12},{9,13},{10,... | collective-permute-start | bytes 1179656 | tf_op jit(solution)/shard_map/ppermute | solution.py:562
  129.3 9.0 %collective-permute-start.43 = (bf16[2,32,1536]{2,1,0:T(8,128)(2,1)S(1)}, bf16[2,32,1536]{2,1,0:T(8,128)(2,1)S(1)}, u32[]{:S(2)}, u32[]{:S(2)}) collective-permute-start(bf16[2,32,1536]{2,1,0:T(8,128)(2,1)S(1)} %pad_maximum_fusion.8), channel_id=1, source_target_pairs={{0,8},{1,9},{2,10},{3,11},{4,12},{5,13},{6,14},{7,15},{8,0},{9,1},... | collective-permute-start | bytes 589832 | tf_op jit(solution)/shard_map/ppermute | solution.py:562
  138.3 10.3 %collective-permute-start.45 = (bf16[4,32,1536]{2,1,0:T(8,128)(2,1)S(1)}, bf16[4,32,1536]{2,1,0:T(8,128)(2,1)S(1)}, u32[]{:S(2)}, u32[]{:S(2)}) collective-permute-start(bf16[4,32,1536]{2,1,0:T(8,128)(2,1)S(1)} %pad_maximum_fusion.3), channel_id=1, source_target_pairs={{0,4},{1,5},{2,6},{3,7},{4,0},{5,1},{6,2},{7,3},{8,12},{9,13},{10,... | collective-permute-start | bytes 1179656 | tf_op jit(solution)/shard_map/ppermute | solution.py:562
  (36 other events, 328.7 us)

commit v12 on v11

--- a/solution.py
+++ b/solution.py
@@ -451,38 +451,47 @@
         target[idx % (count // 2)] = whole[source, :].astype(bf16)
 
 
-def finish(pieces, masks, layer_idx, place, shape, before=()):
-    grain, width = pieces.shape[1], shape[-1]
+def finish(parts, layer_idx, place, shape, before=()):
+    width = shape[-1]
+    grain, columns = parts[0][0].shape[1:]
     count = len(before)
 
-    def kernel(place_ref, source, *refs):
-        outs = refs[count : count + 3]
-        stage, out_sem = refs[count + 3 :]
-        for idx, mask in enumerate(masks):
-            rows = pl.ds(pl.multiple_of((place_ref[3] ^ mask) * grain, grain), grain)
-            for k, out in enumerate(outs):
-                stage[k, idx] = source[idx, :, k * width : (k + 1) * width].astype(f32)
-                pltpu.make_async_copy(stage.at[k, idx], out.at[layer_idx, rows], out_sem).start()
-        pltpu.make_async_copy(stage, stage, out_sem).wait()
-
+    def kernel(place_ref, *refs):
+        sources = refs[: len(parts)]
+        refs = refs[len(parts) + count :]
+        outs, stages, out_sem = refs[:3], refs[3:-1], refs[-1]
+        for source, stage, (_, masks, side) in zip(sources, stages, parts):
+            for idx, mask in enumerate(masks):
+                stage[idx] = source[idx].astype(f32)
+                at = idx // (len(masks) // 2) if side is None else side
+                rows = pl.ds(pl.multiple_of((place_ref[3] ^ (mask // 2)) * grain, grain), grain)
+                for k, out in enumerate(outs):
+                    low = max(at * columns, k * width)
+                    size = min((at + 1) * columns, (k + 1) * width) - low
+                    if size > 0:
+                        pltpu.make_async_copy(
+                            stage.at[idx, :, pl.ds(low - at * columns, size)],
+                            out.at[layer_idx, rows, pl.ds(low - k * width, size)],
+                            out_sem,
+                        ).start()
+        for stage in stages:
+            pltpu.make_async_copy(stage, stage, out_sem).wait()
+
+    arrays = [pltpu.with_memory_space_constraint(array, pltpu.VMEM) for array, _, _ in parts]
     return pl.pallas_call(
         kernel,
         name="layer_%d_ff_grads" % layer_idx,
-        in_specs=[
-            pl.BlockSpec(memory_space=pltpu.SMEM),
-            pl.BlockSpec(memory_space=pltpu.VMEM),
-        ]
+        in_specs=[pl.BlockSpec(memory_space=pltpu.SMEM)]
+        + [pl.BlockSpec(memory_space=pltpu.VMEM)] * len(parts)
         + [pl.BlockSpec(memory_space=pl.ANY)] * count,
         out_specs=[pl.BlockSpec(memory_space=pl.ANY)] * 3,
         out_shape=[jax.ShapeDtypeStruct(shape, f32)] * 3,
-        input_output_aliases={2 + k: k for k in range(count)},
-        scratch_shapes=[
-            pltpu.VMEM((3, len(masks), grain, width), f32),
-            pltpu.SemaphoreType.DMA,
-        ],
+        input_output_aliases={1 + len(parts) + k: k for k in range(count)},
+        scratch_shapes=[pltpu.VMEM(array.shape, f32) for array, _, _ in parts]
+        + [pltpu.SemaphoreType.DMA],
         compiler_params=pltpu.CompilerParams(vmem_limit_bytes=6 * mebibyte),
-        cost_estimate=cost(3),
-    )(place, pltpu.with_memory_space_constraint(pieces, pltpu.VMEM), *before)
+        cost_estimate=cost(2),
+    )(place, *arrays, *before)
 
 
 def small_body(r):
@@ -747,7 +756,6 @@
     ff_whole = [hop for hop in bits[1:] if hop // 2 >= ff_count]
     ff_share = [hop for hop in bits[:0:-1] if hop // 2 < ff_count]
     ff_masks = [order_masks(hops) for hops in ff_split]
-    place_masks = [mask // 2 for mask in order_masks(ff_share[::-1])]
     attn_half = (attn_count // 2, attn_grain, 4 * inner)
     small_shape = (heads + 2, 3 * width)
 
@@ -805,15 +813,33 @@
             out["token"] = piece = add(piece, got)
         out["piece"] = piece
 
-    def sharing(piece, hops, out):
-        for step, hop in enumerate(hops):
-            if step + 1 == len(hops):
-                out["near"] = piece
-            got = yield swap(piece, hop)
-            if step + 1 < len(hops):
-                out["token"] = piece = join(piece, got)
-            else:
-                out["token"] = out["far"] = got
+    def apart(both, masks):
+        return [(both, masks[0] + masks[1], None)]
+
+    def sharing(piece, out):
+        columns = piece.shape[2] // 2
+        halves = [piece[:, :, :columns], piece[:, :, columns:]]
+        masks = [[0], [0]]
+        others = ff_share[:-1]
+        orders = (others, others[-1:] + others[:-1])
+        for step, hops in enumerate(zip(*orders)):
+            sent = tuple(swap(half, hop) for half, hop in zip(halves, hops))
+            new_masks = [[m ^ hop for m in side] for side, hop in zip(masks, hops)]
+            if step + 1 < len(others):
+                got = yield sent
+                halves = [join(half, one) for half, one in zip(halves, got)]
+                masks = [side + new for side, new in zip(masks, new_masks)]
+                out["token"] = tuple(halves)
+        got = yield swap(join(*halves), 2)
+        crossed = [[m ^ 2 for m in side] for side in masks]
+        out["early"] = [*zip(halves, masks, (0, 1)), *apart(got, crossed)]
+        out["token"] = got
+        got = yield sent
+        out["near"] = [*zip(got, new_masks, (0, 1))]
+        out["token"] = got
+        got = yield swap(join(*got), 2)
+        out["far"] = apart(got, [[m ^ 2 for m in side] for side in new_masks])
+        out["token"] = got
 
     def rounded(values):
         return lax.reduce_precision(values, exponent_bits=8, mantissa_bits=7)
@@ -873,7 +899,7 @@
         keep, send = (jnp.concatenate(sides, axis=2) for sides in (keeps, sends))
         yield from halving(keep, send, ff_split[0][3:], out)
         yield from summing(out["piece"], ff_whole, out)
-        yield from sharing(out["piece"], ff_share, out)
+        yield from sharing(out["piece"], out)
 
     class Chain:
         def __init__(self, steps, *args):
@@ -1002,23 +1028,40 @@
     attn_1.resume(back_attn_0.attn_send)
     token = back_attn_0.attn_send
     shape = (2, width, width)
-    near_masks = place_masks[: ff_count // 2]
-    far_masks = place_masks[ff_count // 2 :]
     done = ()
-    ended = False
+    written = set()
+
+    def write(chain, layer_idx, key, token):
+        nonlocal done
+        if key not in chain.out or (layer_idx, key) in written:
+            return token
+        written.add((layer_idx, key))
+        parts = chain.out[key]
+        tokens = token if isinstance(token, tuple) else (token,)
+        arrays = lax.optimization_barrier((*(part[0] for part in parts), *tokens))
+        parts = [(array, *part[1:]) for array, part in zip(arrays, parts)]
+        done = finish(parts, layer_idx, place, shape, done)
+        return done[0]
+
     turn = 0
     sums = attn_grads = None
     while ff_0.arriving is not None:
         turn += 1
-        token = ff_1.step(token)
-        if done and not ended:
-            done = finish(tie(ff_1.out["far"], token), far_masks, 1, place, shape, done)
-            token = done[0]
-            ended = True
+        last_of_1 = "near" in ff_1.out
+        if not last_of_1:
+            token = ff_1.step(token)
+        for chain, layer_idx, key in ((ff_1, 1, "near"), (ff_0, 0, "near")):
+            token = write(chain, layer_idx, key, token)
         token = ff_0.step(token)
-        if not done and "near" in ff_1.out:
-            done = finish(tie(ff_1.out["near"], token), near_masks, 1, place, shape)
-            token = done[0]
+        if last_of_1:
+            token = ff_1.step(token)
+        for chain, layer_idx, key in (
+            (ff_1, 1, "early"),
+            (ff_0, 0, "early"),
+            (ff_1, 1, "far"),
+            (ff_0, 0, "far"),
+        ):
+            token = write(chain, layer_idx, key, token)
         if turn != 2:
             token = attn_0.step(token)
         if turn > 2:
@@ -1042,10 +1085,6 @@
             attn_grads = [both[:, :, k * inner : (k + 1) * inner] for k in range(4)]
             attn_grads[3] = jnp.swapaxes(attn_grads[3], 1, 2)
             token = tuple(attn_grads)
-    if not ended:
-        done = finish(ff_1.out["far"], far_masks, 1, place, shape, done)
-    for pieces, masks in ((ff_0.out["near"], near_masks), (ff_0.out["far"], far_masks)):
-        done = finish(pieces, masks, 0, place, shape, done)
     return (
         back_ff_1.outputs.reshape(inputs.shape),
         back_attn_0.grad_next.reshape(inputs.shape),

time: 153 us -> 159 us (1.039)
  starting transfers between devices: 55.6 us -> 61.6 us
  waiting for transfers between devices: 46.2 us -> 43.2 us
  Pallas kernels: 45.1 us -> 47.4 us
    ppermute x48 -> x56, starting transfers between devices: 55.6 us -> 61.6 us  [swap(): return lax.ppermute(array, axes, [(n, n ^ mask) for n in range(devices)])]
    ppermute x48 -> x56, waiting for transfers between devices: 46.2 us -> 43.2 us  [swap(): return lax.ppermute(array, axes, [(n, n ^ mask) for n in range(devices)])]
    pallas_call x4 -> x6, Pallas kernels: 6.67 us -> 9.02 us  [finish(): pl.pallas_call(kernel, name='layer_%d_ff_grads' % layer_idx, in_specs=[pl...]
  transfers between devices with their start and end apart: 48 -> 56, of which waited for: 22 -> 21; matrix products, arithmetic and copies ran while one was open for 3% -> 3% of each run, Pallas kernels for 22% -> 23%
where the time goes in v12:
time: 159 us
  starting transfers between devices  61.6 us (39%)
  Pallas kernels  47.4 us (30%)
  waiting for transfers between devices  43.2 us (27%)
  other arithmetic  4.01 us (3%)
  between operations  1.78 us (1%)
    ppermute x56, starting transfers between devices, swap(): return lax.ppermute(array, axes, [(n, n ^ mask) for n in range(devices)])  61.6 us
    ppermute x56, waiting for transfers between devices, swap(): return lax.ppermute(array, axes, [(n, n ^ mask) for n in range(devices)])  43.2 us
    pallas_call x10, Pallas kernels, run(): pl.pallas_call(kernel, name=name, in_specs=[pl.BlockSpec(memory_space=in_...  38.4 us
    pallas_call x6, Pallas kernels, finish(): pl.pallas_call(kernel, name='layer_%d_ff_grads' % layer_idx, in_specs=[pl...  9.02 us
  transfers between devices with their start and end apart: 56, of which 21 were waited for; matrix products, arithmetic and copies ran while one was open for 3% of the time, Pallas kernels for 23%

profile of v12, /device:TPU:0, one launch (start us, length us, event | category | flops | bytes accessed | tf_op | source)
XLA Modules:
  0.0 158.6 jit_solution(12266389611570403157)
XLA Ops:
  2.6 3.0 %collective-permute-start.1 = (bf16[16,1536]{1,0:T(8,128)(2,1)S(1)}, bf16[16,1536]{1,0:T(8,128)(2,1)S(1)}, u32[]{:S(2)}, u32[]{:S(2)}) collective-permute-start(bf16[16,1536]{1,0:T(8,128)(2,1)S(1)} %get-tuple-element.149), channel_id=1, source_target_pairs={{0,1},{1,0},{2,3},{3,2},{4,5},{5,4},{6,7},{7,6},{8,9},{9,8},{10,11... | collective-permute-start | bytes 147464 | tf_op jit(solution)/shard_map/ppermute | solution.py:571
  5.6 2.6 %collective-permute-start = (bf16[16,1536]{1,0:T(8,128)(2,1)S(1)}, bf16[16,1536]{1,0:T(8,128)(2,1)S(1)}, u32[]{:S(2)}, u32[]{:S(2)}) collective-permute-start(bf16[16,1536]{1,0:T(8,128)(2,1)S(1)} %get-tuple-element.148), channel_id=1, source_target_pairs={{0,16},{1,17},{2,18},{3,19},{4,20},{5,21},{6,22},{7,23},{8,24},{9,... | collective-permute-start | bytes 147464 | tf_op jit(solution)/shard_map/ppermute | solution.py:571
  9.7 2.7 %collective-permute-start.2 = (bf16[32,1536]{1,0:T(8,128)(2,1)S(1)}, bf16[32,1536]{1,0:T(8,128)(2,1)S(1)}, u32[]{:S(2)}, u32[]{:S(2)}) collective-permute-start(bf16[32,1536]{1,0:T(8,128)(2,1)S(1)} %get-tuple-element.355), channel_id=1, source_target_pairs={{0,16},{1,17},{2,18},{3,19},{4,20},{5,21},{6,22},{7,23},{8,24},{9,... | collective-permute-start | bytes 294920 | tf_op jit(solution)/shard_map/ppermute | solution.py:571
  13.9 4.6 %collective-permute-done.3 = bf16[3,128,512]{2,1,0:T(8,128)(2,1)S(1)} collective-permute-done((bf16[3,128,512]{2,1,0:T(8,128)(2,1)S(1)}, bf16[3,128,512]{2,1,0:T(8,128)(2,1)S(1)}, u32[]{:S(2)}, u32[]{:S(2)}) %collective-permute-start.3) | collective-permute-done | bytes 393248 | tf_op jit(solution)/shard_map/ppermute | solution.py:571
  23.2 4.0 %collective-permute-done.4 = bf16[64,1536]{1,0:T(8,128)(2,1)S(1)} collective-permute-done((bf16[64,1536]{1,0:T(8,128)(2,1)S(1)}, bf16[64,1536]{1,0:T(8,128)(2,1)S(1)}, u32[]{:S(2)}, u32[]{:S(2)}) %collective-permute-start.4) | collective-permute-done | bytes 196640 | tf_op jit(solution)/shard_map/ppermute | solution.py:571
  30.3 2.1 %prepare.1 = (f32[512,512]{1,0:T(8,128)S(1)}, bf16[512,512]{1,0:T(8,128)(2,1)S(1)}, f32[64,384]{1,0:T(8,128)S(1)}, s32[512,128]{1,0:T(8,128)S(1)}, s32[512,128]{1,0:T(8,128)S(1)}, /*index=5*/s32[64,128]{1,0:T(8,128)S(1)}) custom-call(bf16[512,512]{1,0:T(8,128)(2,1)S(1)} %bitcast.57, s32[8,64]{1,0:T(8,128)S(1)} %copy-done.7, s32[8,64]{1,0:T(8,128)S(1)} %copy-done.8, ...), custom_call_target="tpu_custom_call" | custom-call | flops 3449999872 | tf_op jit(solution)/shard_map/prepare/pallas_call | solution.py:99
  32.8 3.6 %collective-permute-done.7 = bf16[128,1536]{1,0:T(8,128)(2,1)S(1)} collective-permute-done((bf16[128,1536]{1,0:T(8,128)(2,1)S(1)}, bf16[128,1536]{1,0:T(8,128)(2,1)S(1)}, u32[]{:S(2)}, u32[]{:S(2)}) %collective-permute-start.7) | collective-permute-done | bytes 393248 | tf_op jit(solution)/shard_map/ppermute | solution.py:571
  38.8 2.8 %layer_0_attention.1 = (bf16[512,1536]{1,0:T(8,128)(2,1)S(1)}, bf16[512,1152]{1,0:T(8,128)(2,1)S(1)}, f32[512,384]{1,0:T(8,128)S(1)}, bf16[512,384]{1,0:T(8,128)...) custom-call(s32[4]{0:T(128)S(1)} %pad_add_fusion.refs_0_.place_ref, ...), custom_call_target="tpu_custom_call" | custom-call | flops 11500000256 | tf_op jit(solution)/shard_map/layer_0_attention/pallas_call | solution.py:99
  41.8 3.2 %layer_0_ff.1 = (bf16[2,512,1024]{2,1,0:T(8,128)(2,1)S(1)}, bf16[2,512,512]{2,1,0:T(8,128)(2,1)S(1)}, f32[512,512]{1,0:T(8,128)S(1)}, bf16[512,512]{1,0:T(8,128)(2,1)S(1)}) custom-call(s32[4]{0:T(128)S(1)} %pad_add_fusion.refs_0_.place_ref, f32[512,512]{1,0:T(8,128)S(1)} %get-tuple-element.165.refs_1_.refs_4_, ...), custom_call_target="tpu_custom_call" | custom-call | flops 3449999872 | tf_op jit(solution)/shard_map/layer_0_ff/pallas_call | solution.py:99
  45.0 3.2 %collective-permute-done.14 = bf16[3,128,512]{2,1,0:T(8,128)(2,1)S(1)} collective-permute-done((bf16[3,128,512]{2,1,0:T(8,128)(2,1)S(1)}, bf16[3,128,512]{2,1,0:T(8,128)(2,1)S(1)}, u32[]{:S(2)}, u32[]{:S(2)}) %collective-permute-start.14) | collective-permute-done | bytes 393248 | tf_op jit(solution)/shard_map/ppermute | solution.py:571
  48.4 2.8 %layer_1_attention.1 = (bf16[512,1536]{1,0:T(8,128)(2,1)S(1)}, bf16[512,1152]{1,0:T(8,128)(2,1)S(1)}, f32[512,384]{1,0:T(8,128)S(1)}, bf16[512,384]{1,0:T(8,128)...) custom-call(s32[4]{0:T(128)S(1)} %pad_add_fusion.refs_0_.place_ref, ...), custom_call_target="tpu_custom_call" | custom-call | flops 115000000 | tf_op jit(solution)/shard_map/layer_1_attention/pallas_call | solution.py:99
  51.2 7.3 %layer_1_ff.1 = (bf16[32,32,768]{2,1,0:T(8,128)(2,1)S(1)}, bf16[32,32,768]{2,1,0:T(8,128)(2,1)S(1)}, f32[8,1536]{1,0:T(8,128)S(1)}, f32[512,512]{1,0:T(8,128)S(1...) custom-call(s32[4]{0:T(128)S(1)} %pad_add_fusion.refs_0_.place_ref, bf16[512,512]{1,0:T(8,128)(2,1)S(1)} %bitcast.58, ...), custom_call_target="tpu_custom_call" | custom-call | flops 9200000000 | tf_op jit(solution)/shard_map/layer_1_ff/pallas_call | solution.py:99
  59.1 4.6 %layer_1_attention_backward.1 = (bf16[16,16,1536]{2,1,0:T(8,128)(2,1)S(1)}, bf16[16,16,1536]{2,1,0:T(8,128)(2,1)S(1)}, f32[8,1536]{1,0:T(8,128)S(1)}, f32[512,512]{1,0:T(8,128)S(1)}, f32[64,384]{1,0:T(8,128)S(1)}) custom-call(s32[4]{0:T(128)S(1)} %pad_add_fusion.refs_0_.place_ref, f32[8,1536]{1,0:T(8,128)S(1)} %get-tuple-element.176.refs_1_, ...), custom_call_target="tpu_custom_call" | custom-call | flops 6899999744 | tf_op jit(solution)/shard_map/layer_1_attention_backward/pallas_call | solution.py:99
  67.0 7.1 %layer_0_ff_backward.1 = (bf16[32,32,768]{2,1,0:T(8,128)(2,1)S(1)}, bf16[32,32,768]{2,1,0:T(8,128)(2,1)S(1)}, f32[8,1536]{1,0:T(8,128)S(1)}, f32[512,512]{1,0:T(8,128)S(1)}, bf16[512,512]{1,0:T(8,128)(2,1)S(1)}) custom-call(s32[4]{0:T(128)S(1)} %pad_add_fusion.refs_0_.place_ref, f32[512,512]{1,0:T(8,128)S(1)} %get-tuple-element.186.refs_1_, ...), custom_call_target="tpu_custom_call" | custom-call | flops 9200000000 | tf_op jit(solution)/shard_map/layer_0_ff_backward/pallas_call | solution.py:99
  83.6 6.1 %layer_0_attention_backward.1 = (bf16[16,16,1536]{2,1,0:T(8,128)(2,1)S(1)}, bf16[17,16,1536]{2,1,0:T(8,128)(2,1)S(1)}, f32[8,1536]{1,0:T(8,128)S(1)}, f32[512,512]{1,0:T(8,128)}) custom-call(s32[4]{0:T(128)S(1)} %pad_add_fusion.refs_0_.place_ref, f32[64,384]{1,0:T(8,128)S(1)} %get-tuple-element.183.refs_1_, s32[512,128]{1,0:T(8,128)S(1)} %get-tuple-element.184.refs_2_, ...), custom_call_target="tpu_custom_call" | custom-call | flops 8049999872 | tf_op jit(solution)/shard_map/layer_0_attention_backward/pallas_call | solution.py:99
  100.1 2.6 %collective-permute-done.27 = bf16[4,32,768]{2,1,0:T(8,128)(2,1)S(1)} collective-permute-done((bf16[4,32,768]{2,1,0:T(8,128)(2,1)S(1)}, bf16[4,32,768]{2,1,0:T(8,128)(2,1)S(1)}, u32[]{:S(2)}, u32[]{:S(2)}) %collective-permute-start.27) | collective-permute-done | bytes 196640 | tf_op jit(solution)/shard_map/ppermute | solution.py:571
  104.4 2.9 %collective-permute-done.31 = bf16[1,32,1536]{2,1,0:T(8,128)(2,1)S(1)} collective-permute-done((bf16[1,32,1536]{2,1,0:T(8,128)(2,1)S(1)}, bf16[1,32,1536]{2,1,0:T(8,128)(2,1)S(1)}, u32[]{:S(2)}, u32[]{:S(2)}) %collective-permute-start.31) | collective-permute-done | bytes 98336 | tf_op jit(solution)/shard_map/ppermute | solution.py:571
  108.0 3.4 %collective-permute-start.34 = (bf16[1,32,768]{2,1,0:T(8,128)(2,1)S(1)}, bf16[1,32,768]{2,1,0:T(8,128)(2,1)S(1)}, u32[]{:S(2)}, u32[]{:S(2)}) collective-permute-start(bf16[1,32,768]{2,1,0:T(8,128)(2,1)S(1)} %get-tuple-element.342), channel_id=1, source_target_pairs={{0,16},{1,17},{2,18},{3,19},{4,20},{5,21},{6,22},{7,23},{8,24},{9,... | collective-permute-start | bytes 147464 | tf_op jit(solution)/shard_map/ppermute | solution.py:571
  114.8 2.1 %collective-permute-start.42 = (bf16[4,16,1536]{2,1,0:T(8,128)(2,1)S(1)}, bf16[4,16,1536]{2,1,0:T(8,128)(2,1)S(1)}, u32[]{:S(2)}, u32[]{:S(2)}) collective-permute-start(bf16[4,16,1536]{2,1,0:T(8,128)(2,1)S(1)} %get-tuple-element.310), channel_id=1, source_target_pairs={{0,4},{1,5},{2,6},{3,7},{4,0},{5,1},{6,2},{7,3},{8,12},{9,13},{10,... | collective-permute-start | bytes 589832 | tf_op jit(solution)/shard_map/ppermute | solution.py:571
  121.4 2.2 %collective-permute-done.32 = bf16[5,16,1536]{2,1,0:T(8,128)(2,1)S(1)} collective-permute-done((bf16[5,16,1536]{2,1,0:T(8,128)(2,1)S(1)}, bf16[5,16,1536]{2,1,0:T(8,128)(2,1)S(1)}, u32[]{:S(2)}, u32[]{:S(2)}) %collective-permute-start.32) | collective-permute-done | bytes 245792 | tf_op jit(solution)/shard_map/ppermute | solution.py:571
  126.3 2.6 %collective-permute-start.37 = (bf16[3,16,1536]{2,1,0:T(8,128)(2,1)S(1)}, bf16[3,16,1536]{2,1,0:T(8,128)(2,1)S(1)}, u32[]{:S(2)}, u32[]{:S(2)}) collective-permute-start(bf16[3,16,1536]{2,1,0:T(8,128)(2,1)S(1)} %maximum_maximum_fusion.2), channel_id=1, source_target_pairs={{0,8},{1,9},{2,10},{3,11},{4,12},{5,13},{6,14},{7,15},{8,0},{9,1},... | collective-permute-start | bytes 442376 | tf_op jit(solution)/shard_map/ppermute | solution.py:571
  130.5 2.1 %collective-permute-start.47 = (bf16[2,32,768]{2,1,0:T(8,128)(2,1)S(1)}, bf16[2,32,768]{2,1,0:T(8,128)(2,1)S(1)}, u32[]{:S(2)}, u32[]{:S(2)}) collective-permute-start(bf16[2,32,768]{2,1,0:T(8,128)(2,1)S(1)} %pad_maximum_fusion.14), channel_id=1, source_target_pairs={{0,16},{1,17},{2,18},{3,19},{4,20},{5,21},{6,22},{7,23},{8,24},{9,... | collective-permute-start | bytes 294920 | tf_op jit(solution)/shard_map/ppermute | solution.py:571
  132.6 5.2 %collective-permute-done.37 = bf16[3,16,1536]{2,1,0:T(8,128)(2,1)S(1)} collective-permute-done((bf16[3,16,1536]{2,1,0:T(8,128)(2,1)S(1)}, bf16[3,16,1536]{2,1,0:T(8,128)(2,1)S(1)}, u32[]{:S(2)}, u32[]{:S(2)}) %collective-permute-start.37) | collective-permute-done | bytes 147488 | tf_op jit(solution)/shard_map/ppermute | solution.py:571
  145.0 3.3 %collective-permute-done.43 = bf16[2,16,1536]{2,1,0:T(8,128)(2,1)S(1)} collective-permute-done((bf16[2,16,1536]{2,1,0:T(8,128)(2,1)S(1)}, bf16[2,16,1536]{2,1,0:T(8,128)(2,1)S(1)}, u32[]{:S(2)}, u32[]{:S(2)}) %collective-permute-start.43) | collective-permute-done | bytes 98336 | tf_op jit(solution)/shard_map/ppermute | solution.py:571
  (212 shorter events, 70.5 us)
Async XLA Ops:
  8.3 10.3 %collective-permute-start.3 = (bf16[3,128,512]{2,1,0:T(8,128)(2,1)S(1)}, bf16[3,128,512]{2,1,0:T(8,128)(2,1)S(1)}, u32[]{:S(2)}, u32[]{:S(2)}) collective-permute-start(bf16[3,128,512]{2,1,0:T(8,128)(2,1)S(1)} %get-tuple-element.157), channel_id=1, source_target_pairs={{0,1},{1,0},{2,3},{3,2},{4,5},{5,4},{6,7},{7,6},{8,9},{9,8},{10,11... | collective-permute-start | bytes 1179656 | tf_op jit(solution)/shard_map/ppermute | solution.py:571
  9.7 9.7 %collective-permute-start.2 = (bf16[32,1536]{1,0:T(8,128)(2,1)S(1)}, bf16[32,1536]{1,0:T(8,128)(2,1)S(1)}, u32[]{:S(2)}, u32[]{:S(2)}) collective-permute-start(bf16[32,1536]{1,0:T(8,128)(2,1)S(1)} %get-tuple-element.355), channel_id=1, source_target_pairs={{0,16},{1,17},{2,18},{3,19},{4,20},{5,21},{6,22},{7,23},{8,24},{9,... | collective-permute-start | bytes 294920 | tf_op jit(solution)/shard_map/ppermute | solution.py:571
  18.6 13.9 %collective-permute-start.9 = (bf16[3,128,512]{2,1,0:T(8,128)(2,1)S(1)}, bf16[3,128,512]{2,1,0:T(8,128)(2,1)S(1)}, u32[]{:S(2)}, u32[]{:S(2)}) collective-permute-start(bf16[3,128,512]{2,1,0:T(8,128)(2,1)S(1)} %get-tuple-element.163), channel_id=1, source_target_pairs={{0,1},{1,0},{2,3},{3,2},{4,5},{5,4},{6,7},{7,6},{8,9},{9,8},{10,11... | collective-permute-start | bytes 1179656 | tf_op jit(solution)/shard_map/ppermute | solution.py:571
  22.7 10.1 %collective-permute-start.8 = (bf16[3,128,512]{2,1,0:T(8,128)(2,1)S(1)}, bf16[3,128,512]{2,1,0:T(8,128)(2,1)S(1)}, u32[]{:S(2)}, u32[]{:S(2)}) collective-permute-start(bf16[3,128,512]{2,1,0:T(8,128)(2,1)S(1)} %collective-permute-done.3), channel_id=1, source_target_pairs={{0,4},{1,5},{2,6},{3,7},{4,0},{5,1},{6,2},{7,3},{8,12},{9,13},{10,... | collective-permute-start | bytes 1179656 | tf_op jit(solution)/shard_map/ppermute | solution.py:571
  37.2 11.1 %collective-permute-start.14 = (bf16[3,128,512]{2,1,0:T(8,128)(2,1)S(1)}, bf16[3,128,512]{2,1,0:T(8,128)(2,1)S(1)}, u32[]{:S(2)}, u32[]{:S(2)}) collective-permute-start(bf16[3,128,512]{2,1,0:T(8,128)(2,1)S(1)} %collective-permute-done.9), channel_id=1, source_target_pairs={{0,4},{1,5},{2,6},{3,7},{4,0},{5,1},{6,2},{7,3},{8,12},{9,13},{10,... | collective-permute-start | bytes 1179656 | tf_op jit(solution)/shard_map/ppermute | solution.py:571
  64.3 11.6 %collective-permute-start.19 = (bf16[8,32,768]{2,1,0:T(8,128)(2,1)S(1)}, bf16[8,32,768]{2,1,0:T(8,128)(2,1)S(1)}, u32[]{:S(2)}, u32[]{:S(2)}) collective-permute-start(bf16[8,32,768]{2,1,0:T(8,128)(2,1)S(1)} %get-tuple-element.301), channel_id=1, source_target_pairs={{0,1},{1,0},{2,3},{3,2},{4,5},{5,4},{6,7},{7,6},{8,9},{9,8},{10,11... | collective-permute-start | bytes 1179656 | tf_op jit(solution)/shard_map/ppermute | solution.py:571
  65.1 11.2 %collective-permute-start.18 = (bf16[8,32,768]{2,1,0:T(8,128)(2,1)S(1)}, bf16[8,32,768]{2,1,0:T(8,128)(2,1)S(1)}, u32[]{:S(2)}, u32[]{:S(2)}) collective-permute-start(bf16[8,32,768]{2,1,0:T(8,128)(2,1)S(1)} %get-tuple-element.302), channel_id=1, source_target_pairs={{0,4},{1,5},{2,6},{3,7},{4,0},{5,1},{6,2},{7,3},{8,12},{9,13},{10,... | collective-permute-start | bytes 1179656 | tf_op jit(solution)/shard_map/ppermute | solution.py:571
  76.7 13.1 %collective-permute-start.25 = (bf16[4,32,768]{2,1,0:T(8,128)(2,1)S(1)}, bf16[4,32,768]{2,1,0:T(8,128)(2,1)S(1)}, u32[]{:S(2)}, u32[]{:S(2)}) collective-permute-start(bf16[4,32,768]{2,1,0:T(8,128)(2,1)S(1)} %get-tuple-element.316), channel_id=1, source_target_pairs={{0,4},{1,5},{2,6},{3,7},{4,0},{5,1},{6,2},{7,3},{8,12},{9,13},{10,... | collective-permute-start | bytes 589832 | tf_op jit(solution)/shard_map/ppermute | solution.py:571
  78.3 11.5 %collective-permute-start.24 = (bf16[4,32,768]{2,1,0:T(8,128)(2,1)S(1)}, bf16[4,32,768]{2,1,0:T(8,128)(2,1)S(1)}, u32[]{:S(2)}, u32[]{:S(2)}) collective-permute-start(bf16[4,32,768]{2,1,0:T(8,128)(2,1)S(1)} %get-tuple-element.318), channel_id=1, source_target_pairs={{0,1},{1,0},{2,3},{3,2},{4,5},{5,4},{6,7},{7,6},{8,9},{9,8},{10,11... | collective-permute-start | bytes 589832 | tf_op jit(solution)/shard_map/ppermute | solution.py:571
  80.6 13.1 %collective-permute-start.23 = (bf16[8,32,768]{2,1,0:T(8,128)(2,1)S(1)}, bf16[8,32,768]{2,1,0:T(8,128)(2,1)S(1)}, u32[]{:S(2)}, u32[]{:S(2)}) collective-permute-start(bf16[8,32,768]{2,1,0:T(8,128)(2,1)S(1)} %get-tuple-element.297.refs_15_), channel_id=1, source_target_pairs={{0,1},{1,0},{2,3},{3,2},{4,5},{5,4},{6,7},{7,6},{8,9},{9,8},{10,11... | collective-permute-start | bytes 1179656 | tf_op jit(solution)/shard_map/ppermute | solution.py:571
  82.0 11.8 %collective-permute-start.22 = (bf16[8,32,768]{2,1,0:T(8,128)(2,1)S(1)}, bf16[8,32,768]{2,1,0:T(8,128)(2,1)S(1)}, u32[]{:S(2)}, u32[]{:S(2)}) collective-permute-start(bf16[8,32,768]{2,1,0:T(8,128)(2,1)S(1)} %get-tuple-element.298.refs_14_), channel_id=1, source_target_pairs={{0,4},{1,5},{2,6},{3,7},{4,0},{5,1},{6,2},{7,3},{8,12},{9,13},{10,... | collective-permute-start | bytes 1179656 | tf_op jit(solution)/shard_map/ppermute | solution.py:571
  91.6 23.1 %collective-permute-start.36 = (bf16[8,16,1536]{2,1,0:T(8,128)(2,1)S(1)}, bf16[8,16,1536]{2,1,0:T(8,128)(2,1)S(1)}, u32[]{:S(2)}, u32[]{:S(2)}) collective-permute-start(bf16[8,16,1536]{2,1,0:T(8,128)(2,1)S(1)} %get-tuple-element.224.refs_8_), channel_id=1, source_target_pairs={{0,8},{1,9},{2,10},{3,11},{4,12},{5,13},{6,14},{7,15},{8,0},{9,1},... | collective-permute-start | bytes 1179656 | tf_op jit(solution)/shard_map/ppermute | solution.py:571
  96.1 18.3 %collective-permute-start.26 = (bf16[9,16,1536]{2,1,0:T(8,128)(2,1)S(1)}, bf16[9,16,1536]{2,1,0:T(8,128)(2,1)S(1)}, u32[]{:S(2)}, u32[]{:S(2)}) collective-permute-start(bf16[9,16,1536]{2,1,0:T(8,128)(2,1)S(1)} %maximum_maximum_fusion), channel_id=1, source_target_pairs={{0,1},{1,0},{2,3},{3,2},{4,5},{5,4},{6,7},{7,6},{8,9},{9,8},{10,11... | collective-permute-start | bytes 1327112 | tf_op jit(solution)/shard_map/ppermute | solution.py:571
  97.7 9.6 %collective-permute-start.31 = (bf16[1,32,1536]{2,1,0:T(8,128)(2,1)S(1)}, bf16[1,32,1536]{2,1,0:T(8,128)(2,1)S(1)}, u32[]{:S(2)}, u32[]{:S(2)}) collective-permute-start(bf16[1,32,1536]{2,1,0:T(8,128)(2,1)S(1)} %add_convert_fusion.37), channel_id=1, source_target_pairs={{0,16},{1,17},{2,18},{3,19},{4,20},{5,21},{6,22},{7,23},{8,24},{9,... | collective-permute-start | bytes 294920 | tf_op jit(solution)/shard_map/ppermute | solution.py:571
  102.8 9.8 %collective-permute-start.30 = (bf16[2,32,1536]{2,1,0:T(8,128)(2,1)S(1)}, bf16[2,32,1536]{2,1,0:T(8,128)(2,1)S(1)}, u32[]{:S(2)}, u32[]{:S(2)}) collective-permute-start(bf16[2,32,1536]{2,1,0:T(8,128)(2,1)S(1)} %pad_maximum_fusion.4), channel_id=1, source_target_pairs={{0,8},{1,9},{2,10},{3,11},{4,12},{5,13},{6,14},{7,15},{8,0},{9,1},... | collective-permute-start | bytes 589832 | tf_op jit(solution)/shard_map/ppermute | solution.py:571
  107.4 9.5 %collective-permute-start.35 = (bf16[1,32,768]{2,1,0:T(8,128)(2,1)S(1)}, bf16[1,32,768]{2,1,0:T(8,128)(2,1)S(1)}, u32[]{:S(2)}, u32[]{:S(2)}) collective-permute-start(bf16[1,32,768]{2,1,0:T(8,128)(2,1)S(1)} %get-tuple-element.341), channel_id=1, source_target_pairs={{0,4},{1,5},{2,6},{3,7},{4,0},{5,1},{6,2},{7,3},{8,12},{9,13},{10,... | collective-permute-start | bytes 147464 | tf_op jit(solution)/shard_map/ppermute | solution.py:571
  114.8 11.5 %collective-permute-start.42 = (bf16[4,16,1536]{2,1,0:T(8,128)(2,1)S(1)}, bf16[4,16,1536]{2,1,0:T(8,128)(2,1)S(1)}, u32[]{:S(2)}, u32[]{:S(2)}) collective-permute-start(bf16[4,16,1536]{2,1,0:T(8,128)(2,1)S(1)} %get-tuple-element.310), channel_id=1, source_target_pairs={{0,4},{1,5},{2,6},{3,7},{4,0},{5,1},{6,2},{7,3},{8,12},{9,13},{10,... | collective-permute-start | bytes 589832 | tf_op jit(solution)/shard_map/ppermute | solution.py:571
  116.9 12.1 %collective-permute-start.41 = (bf16[2,32,768]{2,1,0:T(8,128)(2,1)S(1)}, bf16[2,32,768]{2,1,0:T(8,128)(2,1)S(1)}, u32[]{:S(2)}, u32[]{:S(2)}) collective-permute-start(bf16[2,32,768]{2,1,0:T(8,128)(2,1)S(1)} %pad_maximum_fusion.12), channel_id=1, source_target_pairs={{0,16},{1,17},{2,18},{3,19},{4,20},{5,21},{6,22},{7,23},{8,24},{9,... | collective-permute-start | bytes 294920 | tf_op jit(solution)/shard_map/ppermute | solution.py:571
  118.1 11.2 %collective-permute-start.40 = (bf16[2,32,768]{2,1,0:T(8,128)(2,1)S(1)}, bf16[2,32,768]{2,1,0:T(8,128)(2,1)S(1)}, u32[]{:S(2)}, u32[]{:S(2)}) collective-permute-start(bf16[2,32,768]{2,1,0:T(8,128)(2,1)S(1)} %pad_maximum_fusion.11), channel_id=1, source_target_pairs={{0,8},{1,9},{2,10},{3,11},{4,12},{5,13},{6,14},{7,15},{8,0},{9,1},... | collective-permute-start | bytes 294920 | tf_op jit(solution)/shard_map/ppermute | solution.py:571
  126.3 11.6 %collective-permute-start.37 = (bf16[3,16,1536]{2,1,0:T(8,128)(2,1)S(1)}, bf16[3,16,1536]{2,1,0:T(8,128)(2,1)S(1)}, u32[]{:S(2)}, u32[]{:S(2)}) collective-permute-start(bf16[3,16,1536]{2,1,0:T(8,128)(2,1)S(1)} %maximum_maximum_fusion.2), channel_id=1, source_target_pairs={{0,8},{1,9},{2,10},{3,11},{4,12},{5,13},{6,14},{7,15},{8,0},{9,1},... | collective-permute-start | bytes 442376 | tf_op jit(solution)/shard_map/ppermute | solution.py:571
  129.5 20.7 %collective-permute-start.53 = (bf16[4,32,768]{2,1,0:T(8,128)(2,1)S(1)}, bf16[4,32,768]{2,1,0:T(8,128)(2,1)S(1)}, u32[]{:S(2)}, u32[]{:S(2)}) collective-permute-start(bf16[4,32,768]{2,1,0:T(8,128)(2,1)S(1)} %pad_maximum_fusion.6.refs_1_), channel_id=1, source_target_pairs={{0,8},{1,9},{2,10},{3,11},{4,12},{5,13},{6,14},{7,15},{8,0},{9,1},... | collective-permute-start | bytes 589832 | tf_op jit(solution)/shard_map/ppermute | solution.py:571
  130.2 20.0 %collective-permute-start.52 = (bf16[4,32,768]{2,1,0:T(8,128)(2,1)S(1)}, bf16[4,32,768]{2,1,0:T(8,128)(2,1)S(1)}, u32[]{:S(2)}, u32[]{:S(2)}) collective-permute-start(bf16[4,32,768]{2,1,0:T(8,128)(2,1)S(1)} %pad_maximum_fusion.5.refs_0_), channel_id=1, source_target_pairs={{0,4},{1,5},{2,6},{3,7},{4,0},{5,1},{6,2},{7,3},{8,12},{9,13},{10,... | collective-permute-start | bytes 589832 | tf_op jit(solution)/shard_map/ppermute | solution.py:571
  130.5 10.5 %collective-permute-start.47 = (bf16[2,32,768]{2,1,0:T(8,128)(2,1)S(1)}, bf16[2,32,768]{2,1,0:T(8,128)(2,1)S(1)}, u32[]{:S(2)}, u32[]{:S(2)}) collective-permute-start(bf16[2,32,768]{2,1,0:T(8,128)(2,1)S(1)} %pad_maximum_fusion.14), channel_id=1, source_target_pairs={{0,16},{1,17},{2,18},{3,19},{4,20},{5,21},{6,22},{7,23},{8,24},{9,... | collective-permute-start | bytes 294920 | tf_op jit(solution)/shard_map/ppermute | solution.py:571
  143.1 10.8 %collective-permute-start.50 = (bf16[4,32,768]{2,1,0:T(8,128)(2,1)S(1)}, bf16[4,32,768]{2,1,0:T(8,128)(2,1)S(1)}, u32[]{:S(2)}, u32[]{:S(2)}) collective-permute-start(bf16[4,32,768]{2,1,0:T(8,128)(2,1)S(1)} %pad_maximum_fusion.8.refs_1_), channel_id=1, source_target_pairs={{0,8},{1,9},{2,10},{3,11},{4,12},{5,13},{6,14},{7,15},{8,0},{9,1},... | collective-permute-start | bytes 589832 | tf_op jit(solution)/shard_map/ppermute | solution.py:571
  (44 other events, 391.4 us)

commit v13 on v11

--- a/solution.py
+++ b/solution.py
@@ -568,7 +568,7 @@
 
     attn_grain = max(16, width // devices)
     attn_count = width // attn_grain
-    ff_grain = max(16, width // dp_size)
+    ff_grain = max(16, 2 * width // dp_size)
     ff_count = width // ff_grain
     quarter_at = lax.rem(dp_at, 4)
     place = jnp.stack(
@@ -1019,9 +1019,8 @@
         if not done and "near" in ff_1.out:
             done = finish(tie(ff_1.out["near"], token), near_masks, 1, place, shape)
             token = done[0]
-        if turn != 2:
-            token = attn_0.step(token)
-        if turn > 2:
+        token = attn_0.step(token)
+        if turn > 1:
             token = attn_1.step(token)
         if sums is None and attn_0.arriving is None:
             sums = run(

time: 153 us -> 147 us (0.961)
  waiting for transfers between devices: 46.2 us -> 37.2 us
  starting transfers between devices: 55.6 us -> 58.7 us
    ppermute x48 -> x46, waiting for transfers between devices: 46.2 us -> 37.2 us  [swap(): return lax.ppermute(array, axes, [(n, n ^ mask) for n in range(devices)])]
    ppermute x48 -> x46, starting transfers between devices: 55.6 us -> 58.7 us  [swap(): return lax.ppermute(array, axes, [(n, n ^ mask) for n in range(devices)])]
  transfers between devices with their start and end apart: 48 -> 46, of which waited for: 22 -> 20; matrix products, arithmetic and copies ran while one was open for 3% -> 3% of each run, Pallas kernels for 22% -> 23%
where the time goes in v13:
time: 147 us
  starting transfers between devices  58.7 us (40%)
  Pallas kernels  45.1 us (31%)
  waiting for transfers between devices  37.2 us (25%)
  other arithmetic  3.86 us (3%)
  between operations  1.6 us (1%)
    ppermute x46, starting transfers between devices, swap(): return lax.ppermute(array, axes, [(n, n ^ mask) for n in range(devices)])  58.7 us
    pallas_call x10, Pallas kernels, run(): pl.pallas_call(kernel, name=name, in_specs=[pl.BlockSpec(memory_space=in_...  38.4 us
    ppermute x46, waiting for transfers between devices, swap(): return lax.ppermute(array, axes, [(n, n ^ mask) for n in range(devices)])  37.2 us
    pallas_call x4, Pallas kernels, finish(): pl.pallas_call(kernel, name='layer_%d_ff_grads' % layer_idx, in_specs=[pl...  6.73 us
  transfers between devices with their start and end apart: 46, of which 20 were waited for; matrix products, arithmetic and copies ran while one was open for 3% of the time, Pallas kernels for 23%

profile of v13, /device:TPU:0, one launch (start us, length us, event | category | flops | bytes accessed | tf_op | source)
XLA Modules:
  0.0 147.0 jit_solution(3455948160139794048)
XLA Ops:
  2.6 3.0 %collective-permute-start.1 = (bf16[16,1536]{1,0:T(8,128)(2,1)S(1)}, bf16[16,1536]{1,0:T(8,128)(2,1)S(1)}, u32[]{:S(2)}, u32[]{:S(2)}) collective-permute-start(bf16[16,1536]{1,0:T(8,128)(2,1)S(1)} %get-tuple-element.124), channel_id=1, source_target_pairs={{0,1},{1,0},{2,3},{3,2},{4,5},{5,4},{6,7},{7,6},{8,9},{9,8},{10,11... | collective-permute-start | bytes 147464 | tf_op jit(solution)/shard_map/ppermute | solution.py:562
  5.6 2.6 %collective-permute-start = (bf16[16,1536]{1,0:T(8,128)(2,1)S(1)}, bf16[16,1536]{1,0:T(8,128)(2,1)S(1)}, u32[]{:S(2)}, u32[]{:S(2)}) collective-permute-start(bf16[16,1536]{1,0:T(8,128)(2,1)S(1)} %get-tuple-element.123), channel_id=1, source_target_pairs={{0,16},{1,17},{2,18},{3,19},{4,20},{5,21},{6,22},{7,23},{8,24},{9,... | collective-permute-start | bytes 147464 | tf_op jit(solution)/shard_map/ppermute | solution.py:562
  9.7 2.7 %collective-permute-start.2 = (bf16[32,1536]{1,0:T(8,128)(2,1)S(1)}, bf16[32,1536]{1,0:T(8,128)(2,1)S(1)}, u32[]{:S(2)}, u32[]{:S(2)}) collective-permute-start(bf16[32,1536]{1,0:T(8,128)(2,1)S(1)} %get-tuple-element.299), channel_id=1, source_target_pairs={{0,16},{1,17},{2,18},{3,19},{4,20},{5,21},{6,22},{7,23},{8,24},{9,... | collective-permute-start | bytes 294920 | tf_op jit(solution)/shard_map/ppermute | solution.py:562
  13.9 4.6 %collective-permute-done.3 = bf16[3,128,512]{2,1,0:T(8,128)(2,1)S(1)} collective-permute-done((bf16[3,128,512]{2,1,0:T(8,128)(2,1)S(1)}, bf16[3,128,512]{2,1,0:T(8,128)(2,1)S(1)}, u32[]{:S(2)}, u32[]{:S(2)}) %collective-permute-start.3) | collective-permute-done | bytes 393248 | tf_op jit(solution)/shard_map/ppermute | solution.py:562
  23.2 4.0 %collective-permute-done.4 = bf16[64,1536]{1,0:T(8,128)(2,1)S(1)} collective-permute-done((bf16[64,1536]{1,0:T(8,128)(2,1)S(1)}, bf16[64,1536]{1,0:T(8,128)(2,1)S(1)}, u32[]{:S(2)}, u32[]{:S(2)}) %collective-permute-start.4) | collective-permute-done | bytes 196640 | tf_op jit(solution)/shard_map/ppermute | solution.py:562
  30.3 2.1 %prepare.1 = (f32[512,512]{1,0:T(8,128)S(1)}, bf16[512,512]{1,0:T(8,128)(2,1)S(1)}, f32[64,384]{1,0:T(8,128)S(1)}, s32[512,128]{1,0:T(8,128)S(1)}, s32[512,128]{1,0:T(8,128)S(1)}, /*index=5*/s32[64,128]{1,0:T(8,128)S(1)}) custom-call(bf16[512,512]{1,0:T(8,128)(2,1)S(1)} %bitcast.57, s32[8,64]{1,0:T(8,128)S(1)} %copy-done.7, s32[8,64]{1,0:T(8,128)S(1)} %copy-done.8, ...), custom_call_target="tpu_custom_call" | custom-call | flops 3449999872 | tf_op jit(solution)/shard_map/prepare/pallas_call | solution.py:99
  32.8 3.6 %collective-permute-done.7 = bf16[128,1536]{1,0:T(8,128)(2,1)S(1)} collective-permute-done((bf16[128,1536]{1,0:T(8,128)(2,1)S(1)}, bf16[128,1536]{1,0:T(8,128)(2,1)S(1)}, u32[]{:S(2)}, u32[]{:S(2)}) %collective-permute-start.7) | collective-permute-done | bytes 393248 | tf_op jit(solution)/shard_map/ppermute | solution.py:562
  38.8 2.8 %layer_0_attention.1 = (bf16[512,1536]{1,0:T(8,128)(2,1)S(1)}, bf16[512,1152]{1,0:T(8,128)(2,1)S(1)}, f32[512,384]{1,0:T(8,128)S(1)}, bf16[512,384]{1,0:T(8,128)...) custom-call(s32[4]{0:T(128)S(1)} %pad_add_fusion.refs_0_.place_ref, ...), custom_call_target="tpu_custom_call" | custom-call | flops 11500000256 | tf_op jit(solution)/shard_map/layer_0_attention/pallas_call | solution.py:99
  41.8 3.2 %layer_0_ff.1 = (bf16[2,512,1024]{2,1,0:T(8,128)(2,1)S(1)}, bf16[2,512,512]{2,1,0:T(8,128)(2,1)S(1)}, f32[512,512]{1,0:T(8,128)S(1)}, bf16[512,512]{1,0:T(8,128)(2,1)S(1)}) custom-call(s32[4]{0:T(128)S(1)} %pad_add_fusion.refs_0_.place_ref, f32[512,512]{1,0:T(8,128)S(1)} %get-tuple-element.140.refs_1_.refs_4_, ...), custom_call_target="tpu_custom_call" | custom-call | flops 3449999872 | tf_op jit(solution)/shard_map/layer_0_ff/pallas_call | solution.py:99
  45.0 3.3 %collective-permute-done.14 = bf16[3,128,512]{2,1,0:T(8,128)(2,1)S(1)} collective-permute-done((bf16[3,128,512]{2,1,0:T(8,128)(2,1)S(1)}, bf16[3,128,512]{2,1,0:T(8,128)(2,1)S(1)}, u32[]{:S(2)}, u32[]{:S(2)}) %collective-permute-start.14) | collective-permute-done | bytes 393248 | tf_op jit(solution)/shard_map/ppermute | solution.py:562
  48.4 2.8 %layer_1_attention.1 = (bf16[512,1536]{1,0:T(8,128)(2,1)S(1)}, bf16[512,1152]{1,0:T(8,128)(2,1)S(1)}, f32[512,384]{1,0:T(8,128)S(1)}, bf16[512,384]{1,0:T(8,128)...) custom-call(s32[4]{0:T(128)S(1)} %pad_add_fusion.refs_0_.place_ref, ...), custom_call_target="tpu_custom_call" | custom-call | flops 115000000 | tf_op jit(solution)/shard_map/layer_1_attention/pallas_call | solution.py:99
  51.2 7.3 %layer_1_ff.1 = (bf16[16,64,768]{2,1,0:T(8,128)(2,1)S(1)}, bf16[16,64,768]{2,1,0:T(8,128)(2,1)S(1)}, f32[8,1536]{1,0:T(8,128)S(1)}, f32[512,512]{1,0:T(8,128)S(1...) custom-call(s32[4]{0:T(128)S(1)} %pad_add_fusion.refs_0_.place_ref, bf16[512,512]{1,0:T(8,128)(2,1)S(1)} %bitcast.58, ...), custom_call_target="tpu_custom_call" | custom-call | flops 9200000000 | tf_op jit(solution)/shard_map/layer_1_ff/pallas_call | solution.py:99
  59.1 4.6 %layer_1_attention_backward.1 = (bf16[16,16,1536]{2,1,0:T(8,128)(2,1)S(1)}, bf16[16,16,1536]{2,1,0:T(8,128)(2,1)S(1)}, f32[8,1536]{1,0:T(8,128)S(1)}, f32[512,512]{1,0:T(8,128)S(1)}, f32[64,384]{1,0:T(8,128)S(1)}) custom-call(s32[4]{0:T(128)S(1)} %pad_add_fusion.refs_0_.place_ref, f32[8,1536]{1,0:T(8,128)S(1)} %get-tuple-element.151.refs_1_, ...), custom_call_target="tpu_custom_call" | custom-call | flops 6899999744 | tf_op jit(solution)/shard_map/layer_1_attention_backward/pallas_call | solution.py:99
  66.9 7.1 %layer_0_ff_backward.1 = (bf16[16,64,768]{2,1,0:T(8,128)(2,1)S(1)}, bf16[16,64,768]{2,1,0:T(8,128)(2,1)S(1)}, f32[8,1536]{1,0:T(8,128)S(1)}, f32[512,512]{1,0:T(8,128)S(1)}, bf16[512,512]{1,0:T(8,128)(2,1)S(1)}) custom-call(s32[4]{0:T(128)S(1)} %pad_add_fusion.refs_0_.place_ref, f32[512,512]{1,0:T(8,128)S(1)} %get-tuple-element.161.refs_1_, ...), custom_call_target="tpu_custom_call" | custom-call | flops 9200000000 | tf_op jit(solution)/shard_map/layer_0_ff_backward/pallas_call | solution.py:99
  83.3 6.1 %layer_0_attention_backward.1 = (bf16[16,16,1536]{2,1,0:T(8,128)(2,1)S(1)}, bf16[17,16,1536]{2,1,0:T(8,128)(2,1)S(1)}, f32[8,1536]{1,0:T(8,128)S(1)}, f32[512,512]{1,0:T(8,128)}) custom-call(s32[4]{0:T(128)S(1)} %pad_add_fusion.refs_0_.place_ref, f32[64,384]{1,0:T(8,128)S(1)} %get-tuple-element.158.refs_1_, s32[512,128]{1,0:T(8,128)S(1)} %get-tuple-element.159.refs_2_, ...), custom_call_target="tpu_custom_call" | custom-call | flops 8049999872 | tf_op jit(solution)/shard_map/layer_0_attention_backward/pallas_call | solution.py:99
  97.5 2.2 %collective-permute-start.32 = (bf16[1,64,1536]{2,1,0:T(8,128)(2,1)S(1)}, bf16[1,64,1536]{2,1,0:T(8,128)(2,1)S(1)}, u32[]{:S(2)}, u32[]{:S(2)}) collective-permute-start(bf16[1,64,1536]{2,1,0:T(8,128)(2,1)S(1)} %add_convert_fusion.20), channel_id=1, source_target_pairs={{0,16},{1,17},{2,18},{3,19},{4,20},{5,21},{6,22},{7,23},{8,24},{9,... | collective-permute-start | bytes 589832 | tf_op jit(solution)/shard_map/ppermute | solution.py:562
  100.0 2.4 %collective-permute-done.27 = bf16[2,64,768]{2,1,0:T(8,128)(2,1)S(1)} collective-permute-done((bf16[2,64,768]{2,1,0:T(8,128)(2,1)S(1)}, bf16[2,64,768]{2,1,0:T(8,128)(2,1)S(1)}, u32[]{:S(2)}, u32[]{:S(2)}) %collective-permute-start.27) | collective-permute-done | bytes 196640 | tf_op jit(solution)/shard_map/ppermute | solution.py:562
  104.2 5.5 %collective-permute-done.26 = bf16[9,16,1536]{2,1,0:T(8,128)(2,1)S(1)} collective-permute-done((bf16[9,16,1536]{2,1,0:T(8,128)(2,1)S(1)}, bf16[9,16,1536]{2,1,0:T(8,128)(2,1)S(1)}, u32[]{:S(2)}, u32[]{:S(2)}) %collective-permute-start.26) | collective-permute-done | bytes 442400 | tf_op jit(solution)/shard_map/ppermute | solution.py:562
  114.4 2.4 %collective-permute-start.35 = (bf16[1,64,1536]{2,1,0:T(8,128)(2,1)S(1)}, bf16[1,64,1536]{2,1,0:T(8,128)(2,1)S(1)}, u32[]{:S(2)}, u32[]{:S(2)}) collective-permute-start(bf16[1,64,1536]{2,1,0:T(8,128)(2,1)S(1)} %add_convert_fusion.14), channel_id=1, source_target_pairs={{0,16},{1,17},{2,18},{3,19},{4,20},{5,21},{6,22},{7,23},{8,24},{9,... | collective-permute-start | bytes 589832 | tf_op jit(solution)/shard_map/ppermute | solution.py:562
  120.1 2.9 %collective-permute-start.40 = (bf16[2,16,1536]{2,1,0:T(8,128)(2,1)S(1)}, bf16[2,16,1536]{2,1,0:T(8,128)(2,1)S(1)}, u32[]{:S(2)}, u32[]{:S(2)}) collective-permute-start(bf16[2,16,1536]{2,1,0:T(8,128)(2,1)S(1)} %get-tuple-element.272), channel_id=1, source_target_pairs={{0,16},{1,17},{2,18},{3,19},{4,20},{5,21},{6,22},{7,23},{8,24},{9,... | collective-permute-start | bytes 294920 | tf_op jit(solution)/shard_map/ppermute | solution.py:562
  123.1 3.2 %collective-permute-start.39 = (bf16[2,64,1536]{2,1,0:T(8,128)(2,1)S(1)}, bf16[2,64,1536]{2,1,0:T(8,128)(2,1)S(1)}, u32[]{:S(2)}, u32[]{:S(2)}) collective-permute-start(bf16[2,64,1536]{2,1,0:T(8,128)(2,1)S(1)} %pad_maximum_fusion.2), channel_id=1, source_target_pairs={{0,4},{1,5},{2,6},{3,7},{4,0},{5,1},{6,2},{7,3},{8,12},{9,13},{10,... | collective-permute-start | bytes 1179656 | tf_op jit(solution)/shard_map/ppermute | solution.py:562
  128.2 3.1 %collective-permute-start.38 = (bf16[2,16,1536]{2,1,0:T(8,128)(2,1)S(1)}, bf16[2,16,1536]{2,1,0:T(8,128)(2,1)S(1)}, u32[]{:S(2)}, u32[]{:S(2)}) collective-permute-start(bf16[2,16,1536]{2,1,0:T(8,128)(2,1)S(1)} %maximum_maximum_fusion.3), channel_id=1, source_target_pairs={{0,16},{1,17},{2,18},{3,19},{4,20},{5,21},{6,22},{7,23},{8,24},{9,... | collective-permute-start | bytes 294920 | tf_op jit(solution)/shard_map/ppermute | solution.py:562
  131.3 2.2 %collective-permute-start.42 = (bf16[1,16,1536]{2,1,0:T(8,128)(2,1)S(1)}, bf16[1,16,1536]{2,1,0:T(8,128)(2,1)S(1)}, u32[]{:S(2)}, u32[]{:S(2)}) collective-permute-start(bf16[1,16,1536]{2,1,0:T(8,128)(2,1)S(1)} %add_convert_fusion.43), channel_id=1, source_target_pairs={{0,1},{1,0},{2,3},{3,2},{4,5},{5,4},{6,7},{7,6},{8,9},{9,8},{10,11... | collective-permute-start | bytes 147464 | tf_op jit(solution)/shard_map/ppermute | solution.py:562
  139.8 2.9 %collective-permute-done.43 = bf16[2,64,1536]{2,1,0:T(8,128)(2,1)S(1)} collective-permute-done((bf16[2,64,1536]{2,1,0:T(8,128)(2,1)S(1)}, bf16[2,64,1536]{2,1,0:T(8,128)(2,1)S(1)}, u32[]{:S(2)}, u32[]{:S(2)}) %collective-permute-start.43) | collective-permute-done | bytes 393248 | tf_op jit(solution)/shard_map/ppermute | solution.py:562
  (172 shorter events, 58.8 us)
Async XLA Ops:
  8.3 10.3 %collective-permute-start.3 = (bf16[3,128,512]{2,1,0:T(8,128)(2,1)S(1)}, bf16[3,128,512]{2,1,0:T(8,128)(2,1)S(1)}, u32[]{:S(2)}, u32[]{:S(2)}) collective-permute-start(bf16[3,128,512]{2,1,0:T(8,128)(2,1)S(1)} %get-tuple-element.132), channel_id=1, source_target_pairs={{0,1},{1,0},{2,3},{3,2},{4,5},{5,4},{6,7},{7,6},{8,9},{9,8},{10,11... | collective-permute-start | bytes 1179656 | tf_op jit(solution)/shard_map/ppermute | solution.py:562
  9.7 9.7 %collective-permute-start.2 = (bf16[32,1536]{1,0:T(8,128)(2,1)S(1)}, bf16[32,1536]{1,0:T(8,128)(2,1)S(1)}, u32[]{:S(2)}, u32[]{:S(2)}) collective-permute-start(bf16[32,1536]{1,0:T(8,128)(2,1)S(1)} %get-tuple-element.299), channel_id=1, source_target_pairs={{0,16},{1,17},{2,18},{3,19},{4,20},{5,21},{6,22},{7,23},{8,24},{9,... | collective-permute-start | bytes 294920 | tf_op jit(solution)/shard_map/ppermute | solution.py:562
  12.4 8.6 %collective-permute-start.5 = (bf16[32,1536]{1,0:T(8,128)(2,1)S(1)}, bf16[32,1536]{1,0:T(8,128)(2,1)S(1)}, u32[]{:S(2)}, u32[]{:S(2)}) collective-permute-start(bf16[32,1536]{1,0:T(8,128)(2,1)S(1)} %get-tuple-element.293), channel_id=1, source_target_pairs={{0,4},{1,5},{2,6},{3,7},{4,0},{5,1},{6,2},{7,3},{8,12},{9,13},{10,... | collective-permute-start | bytes 294920 | tf_op jit(solution)/shard_map/ppermute | solution.py:562
  18.6 13.9 %collective-permute-start.9 = (bf16[3,128,512]{2,1,0:T(8,128)(2,1)S(1)}, bf16[3,128,512]{2,1,0:T(8,128)(2,1)S(1)}, u32[]{:S(2)}, u32[]{:S(2)}) collective-permute-start(bf16[3,128,512]{2,1,0:T(8,128)(2,1)S(1)} %get-tuple-element.138), channel_id=1, source_target_pairs={{0,1},{1,0},{2,3},{3,2},{4,5},{5,4},{6,7},{7,6},{8,9},{9,8},{10,11... | collective-permute-start | bytes 1179656 | tf_op jit(solution)/shard_map/ppermute | solution.py:562
  22.7 10.1 %collective-permute-start.8 = (bf16[3,128,512]{2,1,0:T(8,128)(2,1)S(1)}, bf16[3,128,512]{2,1,0:T(8,128)(2,1)S(1)}, u32[]{:S(2)}, u32[]{:S(2)}) collective-permute-start(bf16[3,128,512]{2,1,0:T(8,128)(2,1)S(1)} %collective-permute-done.3), channel_id=1, source_target_pairs={{0,4},{1,5},{2,6},{3,7},{4,0},{5,1},{6,2},{7,3},{8,12},{9,13},{10,... | collective-permute-start | bytes 1179656 | tf_op jit(solution)/shard_map/ppermute | solution.py:562
  27.3 9.1 %collective-permute-start.10 = (bf16[128,1536]{1,0:T(8,128)(2,1)S(1)}, bf16[128,1536]{1,0:T(8,128)(2,1)S(1)}, u32[]{:S(2)}, u32[]{:S(2)}) collective-permute-start(bf16[128,1536]{1,0:T(8,128)(2,1)S(1)} %get-tuple-element.286), channel_id=1, source_target_pairs={{0,1},{1,0},{2,3},{3,2},{4,5},{5,4},{6,7},{7,6},{8,9},{9,8},{10,11... | collective-permute-start | bytes 1179656 | tf_op jit(solution)/shard_map/ppermute | solution.py:562
  37.2 11.1 %collective-permute-start.14 = (bf16[3,128,512]{2,1,0:T(8,128)(2,1)S(1)}, bf16[3,128,512]{2,1,0:T(8,128)(2,1)S(1)}, u32[]{:S(2)}, u32[]{:S(2)}) collective-permute-start(bf16[3,128,512]{2,1,0:T(8,128)(2,1)S(1)} %collective-permute-done.9), channel_id=1, source_target_pairs={{0,4},{1,5},{2,6},{3,7},{4,0},{5,1},{6,2},{7,3},{8,12},{9,13},{10,... | collective-permute-start | bytes 1179656 | tf_op jit(solution)/shard_map/ppermute | solution.py:562
  64.2 11.6 %collective-permute-start.19 = (bf16[4,64,768]{2,1,0:T(8,128)(2,1)S(1)}, bf16[4,64,768]{2,1,0:T(8,128)(2,1)S(1)}, u32[]{:S(2)}, u32[]{:S(2)}) collective-permute-start(bf16[4,64,768]{2,1,0:T(8,128)(2,1)S(1)} %get-tuple-element.251), channel_id=1, source_target_pairs={{0,1},{1,0},{2,3},{3,2},{4,5},{5,4},{6,7},{7,6},{8,9},{9,8},{10,11... | collective-permute-start | bytes 1179656 | tf_op jit(solution)/shard_map/ppermute | solution.py:562
  65.0 11.2 %collective-permute-start.18 = (bf16[4,64,768]{2,1,0:T(8,128)(2,1)S(1)}, bf16[4,64,768]{2,1,0:T(8,128)(2,1)S(1)}, u32[]{:S(2)}, u32[]{:S(2)}) collective-permute-start(bf16[4,64,768]{2,1,0:T(8,128)(2,1)S(1)} %get-tuple-element.252), channel_id=1, source_target_pairs={{0,4},{1,5},{2,6},{3,7},{4,0},{5,1},{6,2},{7,3},{8,12},{9,13},{10,... | collective-permute-start | bytes 1179656 | tf_op jit(solution)/shard_map/ppermute | solution.py:562
  76.5 13.0 %collective-permute-start.25 = (bf16[2,64,768]{2,1,0:T(8,128)(2,1)S(1)}, bf16[2,64,768]{2,1,0:T(8,128)(2,1)S(1)}, u32[]{:S(2)}, u32[]{:S(2)}) collective-permute-start(bf16[2,64,768]{2,1,0:T(8,128)(2,1)S(1)} %get-tuple-element.266), channel_id=1, source_target_pairs={{0,4},{1,5},{2,6},{3,7},{4,0},{5,1},{6,2},{7,3},{8,12},{9,13},{10,... | collective-permute-start | bytes 589832 | tf_op jit(solution)/shard_map/ppermute | solution.py:562
  78.2 11.3 %collective-permute-start.24 = (bf16[2,64,768]{2,1,0:T(8,128)(2,1)S(1)}, bf16[2,64,768]{2,1,0:T(8,128)(2,1)S(1)}, u32[]{:S(2)}, u32[]{:S(2)}) collective-permute-start(bf16[2,64,768]{2,1,0:T(8,128)(2,1)S(1)} %get-tuple-element.268), channel_id=1, source_target_pairs={{0,1},{1,0},{2,3},{3,2},{4,5},{5,4},{6,7},{7,6},{8,9},{9,8},{10,11... | collective-permute-start | bytes 589832 | tf_op jit(solution)/shard_map/ppermute | solution.py:562
  80.4 13.2 %collective-permute-start.23 = (bf16[4,64,768]{2,1,0:T(8,128)(2,1)S(1)}, bf16[4,64,768]{2,1,0:T(8,128)(2,1)S(1)}, u32[]{:S(2)}, u32[]{:S(2)}) collective-permute-start(bf16[4,64,768]{2,1,0:T(8,128)(2,1)S(1)} %get-tuple-element.247.refs_15_), channel_id=1, source_target_pairs={{0,1},{1,0},{2,3},{3,2},{4,5},{5,4},{6,7},{7,6},{8,9},{9,8},{10,11... | collective-permute-start | bytes 1179656 | tf_op jit(solution)/shard_map/ppermute | solution.py:562
  81.7 11.9 %collective-permute-start.22 = (bf16[4,64,768]{2,1,0:T(8,128)(2,1)S(1)}, bf16[4,64,768]{2,1,0:T(8,128)(2,1)S(1)}, u32[]{:S(2)}, u32[]{:S(2)}) collective-permute-start(bf16[4,64,768]{2,1,0:T(8,128)(2,1)S(1)} %get-tuple-element.248.refs_14_), channel_id=1, source_target_pairs={{0,4},{1,5},{2,6},{3,7},{4,0},{5,1},{6,2},{7,3},{8,12},{9,13},{10,... | collective-permute-start | bytes 1179656 | tf_op jit(solution)/shard_map/ppermute | solution.py:562
  91.4 20.2 %collective-permute-start.33 = (bf16[8,16,1536]{2,1,0:T(8,128)(2,1)S(1)}, bf16[8,16,1536]{2,1,0:T(8,128)(2,1)S(1)}, u32[]{:S(2)}, u32[]{:S(2)}) collective-permute-start(bf16[8,16,1536]{2,1,0:T(8,128)(2,1)S(1)} %get-tuple-element.197.refs_8_), channel_id=1, source_target_pairs={{0,8},{1,9},{2,10},{3,11},{4,12},{5,13},{6,14},{7,15},{8,0},{9,1},... | collective-permute-start | bytes 1179656 | tf_op jit(solution)/shard_map/ppermute | solution.py:562
  96.0 13.7 %collective-permute-start.26 = (bf16[9,16,1536]{2,1,0:T(8,128)(2,1)S(1)}, bf16[9,16,1536]{2,1,0:T(8,128)(2,1)S(1)}, u32[]{:S(2)}, u32[]{:S(2)}) collective-permute-start(bf16[9,16,1536]{2,1,0:T(8,128)(2,1)S(1)} %maximum_maximum_fusion), channel_id=1, source_target_pairs={{0,1},{1,0},{2,3},{3,2},{4,5},{5,4},{6,7},{7,6},{8,9},{9,8},{10,11... | collective-permute-start | bytes 1327112 | tf_op jit(solution)/shard_map/ppermute | solution.py:562
  97.5 14.6 %collective-permute-start.32 = (bf16[1,64,1536]{2,1,0:T(8,128)(2,1)S(1)}, bf16[1,64,1536]{2,1,0:T(8,128)(2,1)S(1)}, u32[]{:S(2)}, u32[]{:S(2)}) collective-permute-start(bf16[1,64,1536]{2,1,0:T(8,128)(2,1)S(1)} %add_convert_fusion.20), channel_id=1, source_target_pairs={{0,16},{1,17},{2,18},{3,19},{4,20},{5,21},{6,22},{7,23},{8,24},{9,... | collective-permute-start | bytes 589832 | tf_op jit(solution)/shard_map/ppermute | solution.py:562
  102.5 11.8 %collective-permute-start.31 = (bf16[1,64,1536]{2,1,0:T(8,128)(2,1)S(1)}, bf16[1,64,1536]{2,1,0:T(8,128)(2,1)S(1)}, u32[]{:S(2)}, u32[]{:S(2)}) collective-permute-start(bf16[1,64,1536]{2,1,0:T(8,128)(2,1)S(1)} %pad_maximum_fusion.6), channel_id=1, source_target_pairs={{0,8},{1,9},{2,10},{3,11},{4,12},{5,13},{6,14},{7,15},{8,0},{9,1},... | collective-permute-start | bytes 589832 | tf_op jit(solution)/shard_map/ppermute | solution.py:562
  111.7 8.4 %collective-permute-start.37 = (bf16[4,16,1536]{2,1,0:T(8,128)(2,1)S(1)}, bf16[4,16,1536]{2,1,0:T(8,128)(2,1)S(1)}, u32[]{:S(2)}, u32[]{:S(2)}) collective-permute-start(bf16[4,16,1536]{2,1,0:T(8,128)(2,1)S(1)} %get-tuple-element.260), channel_id=1, source_target_pairs={{0,4},{1,5},{2,6},{3,7},{4,0},{5,1},{6,2},{7,3},{8,12},{9,13},{10,... | collective-permute-start | bytes 589832 | tf_op jit(solution)/shard_map/ppermute | solution.py:562
  112.2 10.8 %collective-permute-start.36 = (bf16[1,64,1536]{2,1,0:T(8,128)(2,1)S(1)}, bf16[1,64,1536]{2,1,0:T(8,128)(2,1)S(1)}, u32[]{:S(2)}, u32[]{:S(2)}) collective-permute-start(bf16[1,64,1536]{2,1,0:T(8,128)(2,1)S(1)} %add_convert_fusion.15), channel_id=1, source_target_pairs={{0,8},{1,9},{2,10},{3,11},{4,12},{5,13},{6,14},{7,15},{8,0},{9,1},... | collective-permute-start | bytes 589832 | tf_op jit(solution)/shard_map/ppermute | solution.py:562
  114.4 13.5 %collective-permute-start.35 = (bf16[1,64,1536]{2,1,0:T(8,128)(2,1)S(1)}, bf16[1,64,1536]{2,1,0:T(8,128)(2,1)S(1)}, u32[]{:S(2)}, u32[]{:S(2)}) collective-permute-start(bf16[1,64,1536]{2,1,0:T(8,128)(2,1)S(1)} %add_convert_fusion.14), channel_id=1, source_target_pairs={{0,16},{1,17},{2,18},{3,19},{4,20},{5,21},{6,22},{7,23},{8,24},{9,... | collective-permute-start | bytes 589832 | tf_op jit(solution)/shard_map/ppermute | solution.py:562
  118.1 9.9 %collective-permute-start.34 = (bf16[3,16,1536]{2,1,0:T(8,128)(2,1)S(1)}, bf16[3,16,1536]{2,1,0:T(8,128)(2,1)S(1)}, u32[]{:S(2)}, u32[]{:S(2)}) collective-permute-start(bf16[3,16,1536]{2,1,0:T(8,128)(2,1)S(1)} %maximum_maximum_fusion.2), channel_id=1, source_target_pairs={{0,8},{1,9},{2,10},{3,11},{4,12},{5,13},{6,14},{7,15},{8,0},{9,1},... | collective-permute-start | bytes 442376 | tf_op jit(solution)/shard_map/ppermute | solution.py:562
  120.1 11.2 %collective-permute-start.40 = (bf16[2,16,1536]{2,1,0:T(8,128)(2,1)S(1)}, bf16[2,16,1536]{2,1,0:T(8,128)(2,1)S(1)}, u32[]{:S(2)}, u32[]{:S(2)}) collective-permute-start(bf16[2,16,1536]{2,1,0:T(8,128)(2,1)S(1)} %get-tuple-element.272), channel_id=1, source_target_pairs={{0,16},{1,17},{2,18},{3,19},{4,20},{5,21},{6,22},{7,23},{8,24},{9,... | collective-permute-start | bytes 294920 | tf_op jit(solution)/shard_map/ppermute | solution.py:562
  123.1 10.4 %collective-permute-start.39 = (bf16[2,64,1536]{2,1,0:T(8,128)(2,1)S(1)}, bf16[2,64,1536]{2,1,0:T(8,128)(2,1)S(1)}, u32[]{:S(2)}, u32[]{:S(2)}) collective-permute-start(bf16[2,64,1536]{2,1,0:T(8,128)(2,1)S(1)} %pad_maximum_fusion.2), channel_id=1, source_target_pairs={{0,4},{1,5},{2,6},{3,7},{4,0},{5,1},{6,2},{7,3},{8,12},{9,13},{10,... | collective-permute-start | bytes 1179656 | tf_op jit(solution)/shard_map/ppermute | solution.py:562
  128.2 8.5 %collective-permute-start.38 = (bf16[2,16,1536]{2,1,0:T(8,128)(2,1)S(1)}, bf16[2,16,1536]{2,1,0:T(8,128)(2,1)S(1)}, u32[]{:S(2)}, u32[]{:S(2)}) collective-permute-start(bf16[2,16,1536]{2,1,0:T(8,128)(2,1)S(1)} %maximum_maximum_fusion.3), channel_id=1, source_target_pairs={{0,16},{1,17},{2,18},{3,19},{4,20},{5,21},{6,22},{7,23},{8,24},{9,... | collective-permute-start | bytes 294920 | tf_op jit(solution)/shard_map/ppermute | solution.py:562
  (34 other events, 313.1 us)

commit v14 on v12

--- a/solution.py
+++ b/solution.py
@@ -453,31 +453,25 @@
 
 def finish(parts, layer_idx, place, shape, before=()):
     width = shape[-1]
-    grain, columns = parts[0][0].shape[1:]
+    grain = parts[0][0].shape[1]
     count = len(before)
 
     def kernel(place_ref, *refs):
         sources = refs[: len(parts)]
         refs = refs[len(parts) + count :]
         outs, stages, out_sem = refs[:3], refs[3:-1], refs[-1]
-        for source, stage, (_, masks, side) in zip(sources, stages, parts):
+        for source, stage, (_, masks) in zip(sources, stages, parts):
             for idx, mask in enumerate(masks):
-                stage[idx] = source[idx].astype(f32)
-                at = idx // (len(masks) // 2) if side is None else side
                 rows = pl.ds(pl.multiple_of((place_ref[3] ^ (mask // 2)) * grain, grain), grain)
                 for k, out in enumerate(outs):
-                    low = max(at * columns, k * width)
-                    size = min((at + 1) * columns, (k + 1) * width) - low
-                    if size > 0:
-                        pltpu.make_async_copy(
-                            stage.at[idx, :, pl.ds(low - at * columns, size)],
-                            out.at[layer_idx, rows, pl.ds(low - k * width, size)],
-                            out_sem,
-                        ).start()
+                    stage[k, idx] = source[idx, :, k * width : (k + 1) * width].astype(f32)
+                    pltpu.make_async_copy(
+                        stage.at[k, idx], out.at[layer_idx, rows], out_sem
+                    ).start()
         for stage in stages:
             pltpu.make_async_copy(stage, stage, out_sem).wait()
 
-    arrays = [pltpu.with_memory_space_constraint(array, pltpu.VMEM) for array, _, _ in parts]
+    arrays = [pltpu.with_memory_space_constraint(array, pltpu.VMEM) for array, _ in parts]
     return pl.pallas_call(
         kernel,
         name="layer_%d_ff_grads" % layer_idx,
@@ -487,7 +481,9 @@
         out_specs=[pl.BlockSpec(memory_space=pl.ANY)] * 3,
         out_shape=[jax.ShapeDtypeStruct(shape, f32)] * 3,
         input_output_aliases={1 + len(parts) + k: k for k in range(count)},
-        scratch_shapes=[pltpu.VMEM(array.shape, f32) for array, _, _ in parts]
+        scratch_shapes=[
+            pltpu.VMEM((3, array.shape[0], grain, width), f32) for array, _ in parts
+        ]
         + [pltpu.SemaphoreType.DMA],
         compiler_params=pltpu.CompilerParams(vmem_limit_bytes=6 * mebibyte),
         cost_estimate=cost(2),
@@ -577,7 +573,7 @@
 
     attn_grain = max(16, width // devices)
     attn_count = width // attn_grain
-    ff_grain = max(16, width // dp_size)
+    ff_grain = max(16, 2 * width // dp_size)
     ff_count = width // ff_grain
     quarter_at = lax.rem(dp_at, 4)
     place = jnp.stack(
@@ -813,32 +809,23 @@
             out["token"] = piece = add(piece, got)
         out["piece"] = piece
 
-    def apart(both, masks):
-        return [(both, masks[0] + masks[1], None)]
-
     def sharing(piece, out):
-        columns = piece.shape[2] // 2
-        halves = [piece[:, :, :columns], piece[:, :, columns:]]
-        masks = [[0], [0]]
-        others = ff_share[:-1]
-        orders = (others, others[-1:] + others[:-1])
-        for step, hops in enumerate(zip(*orders)):
-            sent = tuple(swap(half, hop) for half, hop in zip(halves, hops))
-            new_masks = [[m ^ hop for m in side] for side, hop in zip(masks, hops)]
-            if step + 1 < len(others):
-                got = yield sent
-                halves = [join(half, one) for half, one in zip(halves, got)]
-                masks = [side + new for side, new in zip(masks, new_masks)]
-                out["token"] = tuple(halves)
-        got = yield swap(join(*halves), 2)
-        crossed = [[m ^ 2 for m in side] for side in masks]
-        out["early"] = [*zip(halves, masks, (0, 1)), *apart(got, crossed)]
+        masks = [0]
+        for hop in ff_share[:-2]:
+            got = yield swap(piece, hop)
+            out["token"] = piece = join(piece, got)
+            masks = masks + [mask ^ hop for mask in masks]
+        last, cross = ff_share[-2:]
+        sent = swap(piece, last)
+        got = yield swap(piece, cross)
+        out["early"] = [(piece, masks), (got, [mask ^ cross for mask in masks])]
         out["token"] = got
+        masks = [mask ^ last for mask in masks]
         got = yield sent
-        out["near"] = [*zip(got, new_masks, (0, 1))]
+        out["near"] = [(got, masks)]
         out["token"] = got
-        got = yield swap(join(*got), 2)
-        out["far"] = apart(got, [[m ^ 2 for m in side] for side in new_masks])
+        got = yield swap(got, cross)
+        out["far"] = [(got, [mask ^ cross for mask in masks])]
         out["token"] = got
 
     def rounded(values):
@@ -1038,8 +1025,8 @@
         written.add((layer_idx, key))
         parts = chain.out[key]
         tokens = token if isinstance(token, tuple) else (token,)
-        arrays = lax.optimization_barrier((*(part[0] for part in parts), *tokens))
-        parts = [(array, *part[1:]) for array, part in zip(arrays, parts)]
+        arrays = lax.optimization_barrier((*(array for array, _ in parts), *tokens))
+        parts = [(array, masks) for array, (_, masks) in zip(arrays, parts)]
         done = finish(parts, layer_idx, place, shape, done)
         return done[0]
 
@@ -1047,21 +1034,14 @@
     sums = attn_grads = None
     while ff_0.arriving is not None:
         turn += 1
-        last_of_1 = "near" in ff_1.out
-        if not last_of_1:
-            token = ff_1.step(token)
-        for chain, layer_idx, key in ((ff_1, 1, "near"), (ff_0, 0, "near")):
-            token = write(chain, layer_idx, key, token)
-        token = ff_0.step(token)
-        if last_of_1:
-            token = ff_1.step(token)
-        for chain, layer_idx, key in (
-            (ff_1, 1, "early"),
-            (ff_0, 0, "early"),
-            (ff_1, 1, "far"),
-            (ff_0, 0, "far"),
-        ):
-            token = write(chain, layer_idx, key, token)
+        chains = (ff_0, ff_1) if turn == 3 or "near" in ff_1.out else (ff_1, ff_0)
+        for layer_idx, chain in ((1, ff_1), (0, ff_0)):
+            token = write(chain, layer_idx, "near", token)
+        for chain in chains:
+            token = chain.step(token)
+        for key in ("early", "far"):
+            for layer_idx, chain in ((1, ff_1), (0, ff_0)):
+                token = write(chain, layer_idx, key, token)
         if turn != 2:
             token = attn_0.step(token)
         if turn > 2:

time: 159 us -> 157 us (0.987)
  starting transfers between devices: 61.6 us -> 52.7 us
  waiting for transfers between devices: 43.2 us -> 51 us
    ppermute x56 -> x48, starting transfers between devices: 61.6 us -> 52.7 us  [swap(): return lax.ppermute(array, axes, [(n, n ^ mask) for n in range(devices)])]
    ppermute x56 -> x48, waiting for transfers between devices: 43.2 us -> 51 us  [swap(): return lax.ppermute(array, axes, [(n, n ^ mask) for n in range(devices)])]
  transfers between devices with their start and end apart: 56 -> 48, of which waited for: 21 -> 20; matrix products, arithmetic and copies ran while one was open for 3% -> 2% of each run, Pallas kernels for 23% -> 24%
where the time goes in v14:
time: 157 us
  starting transfers between devices  52.7 us (34%)
  waiting for transfers between devices  51 us (32%)
  Pallas kernels  47.5 us (30%)
  other arithmetic  3.7 us (2%)
  between operations  1.58 us (1%)
    ppermute x48, starting transfers between devices, swap(): return lax.ppermute(array, axes, [(n, n ^ mask) for n in range(devices)])  52.7 us
    ppermute x48, waiting for transfers between devices, swap(): return lax.ppermute(array, axes, [(n, n ^ mask) for n in range(devices)])  51 us
    pallas_call x10, Pallas kernels, run(): pl.pallas_call(kernel, name=name, in_specs=[pl.BlockSpec(memory_space=in_...  38.4 us
    pallas_call x6, Pallas kernels, finish(): pl.pallas_call(kernel, name='layer_%d_ff_grads' % layer_idx, in_specs=[pl...  9.08 us
  transfers between devices with their start and end apart: 48, of which 20 were waited for; matrix products, arithmetic and copies ran while one was open for 2% of the time, Pallas kernels for 24%

profile of v14, /device:TPU:0, one launch (start us, length us, event | category | flops | bytes accessed | tf_op | source)
XLA Modules:
  0.0 156.9 jit_solution(3480098474057798295)
XLA Ops:
  2.6 3.0 %collective-permute-start.1 = (bf16[16,1536]{1,0:T(8,128)(2,1)S(1)}, bf16[16,1536]{1,0:T(8,128)(2,1)S(1)}, u32[]{:S(2)}, u32[]{:S(2)}) collective-permute-start(bf16[16,1536]{1,0:T(8,128)(2,1)S(1)} %get-tuple-element.137), channel_id=1, source_target_pairs={{0,1},{1,0},{2,3},{3,2},{4,5},{5,4},{6,7},{7,6},{8,9},{9,8},{10,11... | collective-permute-start | bytes 147464 | tf_op jit(solution)/shard_map/ppermute | solution.py:567
  5.6 2.6 %collective-permute-start = (bf16[16,1536]{1,0:T(8,128)(2,1)S(1)}, bf16[16,1536]{1,0:T(8,128)(2,1)S(1)}, u32[]{:S(2)}, u32[]{:S(2)}) collective-permute-start(bf16[16,1536]{1,0:T(8,128)(2,1)S(1)} %get-tuple-element.136), channel_id=1, source_target_pairs={{0,16},{1,17},{2,18},{3,19},{4,20},{5,21},{6,22},{7,23},{8,24},{9,... | collective-permute-start | bytes 147464 | tf_op jit(solution)/shard_map/ppermute | solution.py:567
  9.7 2.7 %collective-permute-start.2 = (bf16[32,1536]{1,0:T(8,128)(2,1)S(1)}, bf16[32,1536]{1,0:T(8,128)(2,1)S(1)}, u32[]{:S(2)}, u32[]{:S(2)}) collective-permute-start(bf16[32,1536]{1,0:T(8,128)(2,1)S(1)} %get-tuple-element.325), channel_id=1, source_target_pairs={{0,16},{1,17},{2,18},{3,19},{4,20},{5,21},{6,22},{7,23},{8,24},{9,... | collective-permute-start | bytes 294920 | tf_op jit(solution)/shard_map/ppermute | solution.py:567
  13.9 4.6 %collective-permute-done.3 = bf16[3,128,512]{2,1,0:T(8,128)(2,1)S(1)} collective-permute-done((bf16[3,128,512]{2,1,0:T(8,128)(2,1)S(1)}, bf16[3,128,512]{2,1,0:T(8,128)(2,1)S(1)}, u32[]{:S(2)}, u32[]{:S(2)}) %collective-permute-start.3) | collective-permute-done | bytes 393248 | tf_op jit(solution)/shard_map/ppermute | solution.py:567
  23.2 4.0 %collective-permute-done.4 = bf16[64,1536]{1,0:T(8,128)(2,1)S(1)} collective-permute-done((bf16[64,1536]{1,0:T(8,128)(2,1)S(1)}, bf16[64,1536]{1,0:T(8,128)(2,1)S(1)}, u32[]{:S(2)}, u32[]{:S(2)}) %collective-permute-start.4) | collective-permute-done | bytes 196640 | tf_op jit(solution)/shard_map/ppermute | solution.py:567
  30.3 2.1 %prepare.1 = (f32[512,512]{1,0:T(8,128)S(1)}, bf16[512,512]{1,0:T(8,128)(2,1)S(1)}, f32[64,384]{1,0:T(8,128)S(1)}, s32[512,128]{1,0:T(8,128)S(1)}, s32[512,128]{1,0:T(8,128)S(1)}, /*index=5*/s32[64,128]{1,0:T(8,128)S(1)}) custom-call(bf16[512,512]{1,0:T(8,128)(2,1)S(1)} %bitcast.57, s32[8,64]{1,0:T(8,128)S(1)} %copy-done.7, s32[8,64]{1,0:T(8,128)S(1)} %copy-done.8, ...), custom_call_target="tpu_custom_call" | custom-call | flops 3449999872 | tf_op jit(solution)/shard_map/prepare/pallas_call | solution.py:99
  32.8 3.6 %collective-permute-done.7 = bf16[128,1536]{1,0:T(8,128)(2,1)S(1)} collective-permute-done((bf16[128,1536]{1,0:T(8,128)(2,1)S(1)}, bf16[128,1536]{1,0:T(8,128)(2,1)S(1)}, u32[]{:S(2)}, u32[]{:S(2)}) %collective-permute-start.7) | collective-permute-done | bytes 393248 | tf_op jit(solution)/shard_map/ppermute | solution.py:567
  38.8 2.8 %layer_0_attention.1 = (bf16[512,1536]{1,0:T(8,128)(2,1)S(1)}, bf16[512,1152]{1,0:T(8,128)(2,1)S(1)}, f32[512,384]{1,0:T(8,128)S(1)}, bf16[512,384]{1,0:T(8,128)...) custom-call(s32[4]{0:T(128)S(1)} %pad_add_fusion.refs_0_.place_ref, ...), custom_call_target="tpu_custom_call" | custom-call | flops 11500000256 | tf_op jit(solution)/shard_map/layer_0_attention/pallas_call | solution.py:99
  41.8 3.2 %layer_0_ff.1 = (bf16[2,512,1024]{2,1,0:T(8,128)(2,1)S(1)}, bf16[2,512,512]{2,1,0:T(8,128)(2,1)S(1)}, f32[512,512]{1,0:T(8,128)S(1)}, bf16[512,512]{1,0:T(8,128)(2,1)S(1)}) custom-call(s32[4]{0:T(128)S(1)} %pad_add_fusion.refs_0_.place_ref, f32[512,512]{1,0:T(8,128)S(1)} %get-tuple-element.153.refs_1_.refs_4_, ...), custom_call_target="tpu_custom_call" | custom-call | flops 3449999872 | tf_op jit(solution)/shard_map/layer_0_ff/pallas_call | solution.py:99
  45.0 3.3 %collective-permute-done.14 = bf16[3,128,512]{2,1,0:T(8,128)(2,1)S(1)} collective-permute-done((bf16[3,128,512]{2,1,0:T(8,128)(2,1)S(1)}, bf16[3,128,512]{2,1,0:T(8,128)(2,1)S(1)}, u32[]{:S(2)}, u32[]{:S(2)}) %collective-permute-start.14) | collective-permute-done | bytes 393248 | tf_op jit(solution)/shard_map/ppermute | solution.py:567
  48.4 2.8 %layer_1_attention.1 = (bf16[512,1536]{1,0:T(8,128)(2,1)S(1)}, bf16[512,1152]{1,0:T(8,128)(2,1)S(1)}, f32[512,384]{1,0:T(8,128)S(1)}, bf16[512,384]{1,0:T(8,128)...) custom-call(s32[4]{0:T(128)S(1)} %pad_add_fusion.refs_0_.place_ref, ...), custom_call_target="tpu_custom_call" | custom-call | flops 115000000 | tf_op jit(solution)/shard_map/layer_1_attention/pallas_call | solution.py:99
  51.2 7.3 %layer_1_ff.1 = (bf16[16,64,768]{2,1,0:T(8,128)(2,1)S(1)}, bf16[16,64,768]{2,1,0:T(8,128)(2,1)S(1)}, f32[8,1536]{1,0:T(8,128)S(1)}, f32[512,512]{1,0:T(8,128)S(1...) custom-call(s32[4]{0:T(128)S(1)} %pad_add_fusion.refs_0_.place_ref, bf16[512,512]{1,0:T(8,128)(2,1)S(1)} %bitcast.58, ...), custom_call_target="tpu_custom_call" | custom-call | flops 9200000000 | tf_op jit(solution)/shard_map/layer_1_ff/pallas_call | solution.py:99
  59.1 4.6 %layer_1_attention_backward.1 = (bf16[16,16,1536]{2,1,0:T(8,128)(2,1)S(1)}, bf16[16,16,1536]{2,1,0:T(8,128)(2,1)S(1)}, f32[8,1536]{1,0:T(8,128)S(1)}, f32[512,512]{1,0:T(8,128)S(1)}, f32[64,384]{1,0:T(8,128)S(1)}) custom-call(s32[4]{0:T(128)S(1)} %pad_add_fusion.refs_0_.place_ref, f32[8,1536]{1,0:T(8,128)S(1)} %get-tuple-element.164.refs_1_, ...), custom_call_target="tpu_custom_call" | custom-call | flops 6899999744 | tf_op jit(solution)/shard_map/layer_1_attention_backward/pallas_call | solution.py:99
  66.9 7.1 %layer_0_ff_backward.1 = (bf16[16,64,768]{2,1,0:T(8,128)(2,1)S(1)}, bf16[16,64,768]{2,1,0:T(8,128)(2,1)S(1)}, f32[8,1536]{1,0:T(8,128)S(1)}, f32[512,512]{1,0:T(8,128)S(1)}, bf16[512,512]{1,0:T(8,128)(2,1)S(1)}) custom-call(s32[4]{0:T(128)S(1)} %pad_add_fusion.refs_0_.place_ref, f32[512,512]{1,0:T(8,128)S(1)} %get-tuple-element.174.refs_1_, ...), custom_call_target="tpu_custom_call" | custom-call | flops 9200000000 | tf_op jit(solution)/shard_map/layer_0_ff_backward/pallas_call | solution.py:99
  83.3 6.1 %layer_0_attention_backward.1 = (bf16[16,16,1536]{2,1,0:T(8,128)(2,1)S(1)}, bf16[17,16,1536]{2,1,0:T(8,128)(2,1)S(1)}, f32[8,1536]{1,0:T(8,128)S(1)}, f32[512,512]{1,0:T(8,128)}) custom-call(s32[4]{0:T(128)S(1)} %pad_add_fusion.refs_0_.place_ref, f32[64,384]{1,0:T(8,128)S(1)} %get-tuple-element.171.refs_1_, s32[512,128]{1,0:T(8,128)S(1)} %get-tuple-element.172.refs_2_, ...), custom_call_target="tpu_custom_call" | custom-call | flops 8049999872 | tf_op jit(solution)/shard_map/layer_0_attention_backward/pallas_call | solution.py:99
  91.4 2.3 %collective-permute-done.23 = bf16[4,64,768]{2,1,0:T(8,128)(2,1)S(1)} collective-permute-done((bf16[4,64,768]{2,1,0:T(8,128)(2,1)S(1)}, bf16[4,64,768]{2,1,0:T(8,128)(2,1)S(1)}, u32[]{:S(2)}, u32[]{:S(2)}) %collective-permute-start.23) | collective-permute-done | bytes 393248 | tf_op jit(solution)/shard_map/ppermute | solution.py:567
  97.1 2.8 %collective-permute-done.30 = bf16[2,64,768]{2,1,0:T(8,128)(2,1)S(1)} collective-permute-done((bf16[2,64,768]{2,1,0:T(8,128)(2,1)S(1)}, bf16[2,64,768]{2,1,0:T(8,128)(2,1)S(1)}, u32[]{:S(2)}, u32[]{:S(2)}) %collective-permute-start.30) | collective-permute-done | bytes 196640 | tf_op jit(solution)/shard_map/ppermute | solution.py:567
  102.5 2.8 %collective-permute-start.28 = (bf16[1,64,1536]{2,1,0:T(8,128)(2,1)S(1)}, bf16[1,64,1536]{2,1,0:T(8,128)(2,1)S(1)}, u32[]{:S(2)}, u32[]{:S(2)}) collective-permute-start(bf16[1,64,1536]{2,1,0:T(8,128)(2,1)S(1)} %add_convert_fusion.21), channel_id=1, source_target_pairs={{0,16},{1,17},{2,18},{3,19},{4,20},{5,21},{6,22},{7,23},{8,24},{9,... | collective-permute-start | bytes 589832 | tf_op jit(solution)/shard_map/ppermute | solution.py:567
  105.8 8.5 %collective-permute-done.31 = bf16[1,64,1536]{2,1,0:T(8,128)(2,1)S(1)} collective-permute-done((bf16[1,64,1536]{2,1,0:T(8,128)(2,1)S(1)}, bf16[1,64,1536]{2,1,0:T(8,128)(2,1)S(1)}, u32[]{:S(2)}, u32[]{:S(2)}) %collective-permute-start.31) | collective-permute-done | bytes 196640 | tf_op jit(solution)/shard_map/ppermute | solution.py:567
  116.2 3.9 %collective-permute-done.28 = bf16[1,64,1536]{2,1,0:T(8,128)(2,1)S(1)} collective-permute-done((bf16[1,64,1536]{2,1,0:T(8,128)(2,1)S(1)}, bf16[1,64,1536]{2,1,0:T(8,128)(2,1)S(1)}, u32[]{:S(2)}, u32[]{:S(2)}) %collective-permute-start.28) | collective-permute-done | bytes 196640 | tf_op jit(solution)/shard_map/ppermute | solution.py:567
  120.2 3.7 %collective-permute-start.34 = (bf16[1,64,1536]{2,1,0:T(8,128)(2,1)S(1)}, bf16[1,64,1536]{2,1,0:T(8,128)(2,1)S(1)}, u32[]{:S(2)}, u32[]{:S(2)}) collective-permute-start(bf16[1,64,1536]{2,1,0:T(8,128)(2,1)S(1)} %add_convert_fusion.17), channel_id=1, source_target_pairs={{0,8},{1,9},{2,10},{3,11},{4,12},{5,13},{6,14},{7,15},{8,0},{9,1},... | collective-permute-start | bytes 589832 | tf_op jit(solution)/shard_map/ppermute | solution.py:567
  129.3 1.9 %collective-permute-start.39 = (bf16[1,64,1536]{2,1,0:T(8,128)(2,1)S(1)}, bf16[1,64,1536]{2,1,0:T(8,128)(2,1)S(1)}, u32[]{:S(2)}, u32[]{:S(2)}) collective-permute-start(bf16[1,64,1536]{2,1,0:T(8,128)(2,1)S(1)} %add_convert_fusion.13), channel_id=1, source_target_pairs={{0,8},{1,9},{2,10},{3,11},{4,12},{5,13},{6,14},{7,15},{8,0},{9,1},... | collective-permute-start | bytes 589832 | tf_op jit(solution)/shard_map/ppermute | solution.py:567
  135.3 2.9 %collective-permute-done.39 = bf16[1,64,1536]{2,1,0:T(8,128)(2,1)S(1)} collective-permute-done((bf16[1,64,1536]{2,1,0:T(8,128)(2,1)S(1)}, bf16[1,64,1536]{2,1,0:T(8,128)(2,1)S(1)}, u32[]{:S(2)}, u32[]{:S(2)}) %collective-permute-start.39) | collective-permute-done | bytes 196640 | tf_op jit(solution)/shard_map/ppermute | solution.py:567
  145.1 4.3 %collective-permute-done.40 = bf16[2,16,1536]{2,1,0:T(8,128)(2,1)S(1)} collective-permute-done((bf16[2,16,1536]{2,1,0:T(8,128)(2,1)S(1)}, bf16[2,16,1536]{2,1,0:T(8,128)(2,1)S(1)}, u32[]{:S(2)}, u32[]{:S(2)}) %collective-permute-start.40) | collective-permute-done | bytes 98336 | tf_op jit(solution)/shard_map/ppermute | solution.py:567
  (176 shorter events, 62.5 us)
Async XLA Ops:
  8.3 10.3 %collective-permute-start.3 = (bf16[3,128,512]{2,1,0:T(8,128)(2,1)S(1)}, bf16[3,128,512]{2,1,0:T(8,128)(2,1)S(1)}, u32[]{:S(2)}, u32[]{:S(2)}) collective-permute-start(bf16[3,128,512]{2,1,0:T(8,128)(2,1)S(1)} %get-tuple-element.145), channel_id=1, source_target_pairs={{0,1},{1,0},{2,3},{3,2},{4,5},{5,4},{6,7},{7,6},{8,9},{9,8},{10,11... | collective-permute-start | bytes 1179656 | tf_op jit(solution)/shard_map/ppermute | solution.py:567
  9.7 9.7 %collective-permute-start.2 = (bf16[32,1536]{1,0:T(8,128)(2,1)S(1)}, bf16[32,1536]{1,0:T(8,128)(2,1)S(1)}, u32[]{:S(2)}, u32[]{:S(2)}) collective-permute-start(bf16[32,1536]{1,0:T(8,128)(2,1)S(1)} %get-tuple-element.325), channel_id=1, source_target_pairs={{0,16},{1,17},{2,18},{3,19},{4,20},{5,21},{6,22},{7,23},{8,24},{9,... | collective-permute-start | bytes 294920 | tf_op jit(solution)/shard_map/ppermute | solution.py:567
  18.6 13.9 %collective-permute-start.9 = (bf16[3,128,512]{2,1,0:T(8,128)(2,1)S(1)}, bf16[3,128,512]{2,1,0:T(8,128)(2,1)S(1)}, u32[]{:S(2)}, u32[]{:S(2)}) collective-permute-start(bf16[3,128,512]{2,1,0:T(8,128)(2,1)S(1)} %get-tuple-element.151), channel_id=1, source_target_pairs={{0,1},{1,0},{2,3},{3,2},{4,5},{5,4},{6,7},{7,6},{8,9},{9,8},{10,11... | collective-permute-start | bytes 1179656 | tf_op jit(solution)/shard_map/ppermute | solution.py:567
  22.7 10.1 %collective-permute-start.8 = (bf16[3,128,512]{2,1,0:T(8,128)(2,1)S(1)}, bf16[3,128,512]{2,1,0:T(8,128)(2,1)S(1)}, u32[]{:S(2)}, u32[]{:S(2)}) collective-permute-start(bf16[3,128,512]{2,1,0:T(8,128)(2,1)S(1)} %collective-permute-done.3), channel_id=1, source_target_pairs={{0,4},{1,5},{2,6},{3,7},{4,0},{5,1},{6,2},{7,3},{8,12},{9,13},{10,... | collective-permute-start | bytes 1179656 | tf_op jit(solution)/shard_map/ppermute | solution.py:567
  27.3 9.1 %collective-permute-start.10 = (bf16[128,1536]{1,0:T(8,128)(2,1)S(1)}, bf16[128,1536]{1,0:T(8,128)(2,1)S(1)}, u32[]{:S(2)}, u32[]{:S(2)}) collective-permute-start(bf16[128,1536]{1,0:T(8,128)(2,1)S(1)} %get-tuple-element.312), channel_id=1, source_target_pairs={{0,1},{1,0},{2,3},{3,2},{4,5},{5,4},{6,7},{7,6},{8,9},{9,8},{10,11... | collective-permute-start | bytes 1179656 | tf_op jit(solution)/shard_map/ppermute | solution.py:567
  37.2 11.1 %collective-permute-start.14 = (bf16[3,128,512]{2,1,0:T(8,128)(2,1)S(1)}, bf16[3,128,512]{2,1,0:T(8,128)(2,1)S(1)}, u32[]{:S(2)}, u32[]{:S(2)}) collective-permute-start(bf16[3,128,512]{2,1,0:T(8,128)(2,1)S(1)} %collective-permute-done.9), channel_id=1, source_target_pairs={{0,4},{1,5},{2,6},{3,7},{4,0},{5,1},{6,2},{7,3},{8,12},{9,13},{10,... | collective-permute-start | bytes 1179656 | tf_op jit(solution)/shard_map/ppermute | solution.py:567
  64.2 11.6 %collective-permute-start.19 = (bf16[4,64,768]{2,1,0:T(8,128)(2,1)S(1)}, bf16[4,64,768]{2,1,0:T(8,128)(2,1)S(1)}, u32[]{:S(2)}, u32[]{:S(2)}) collective-permute-start(bf16[4,64,768]{2,1,0:T(8,128)(2,1)S(1)} %get-tuple-element.277), channel_id=1, source_target_pairs={{0,1},{1,0},{2,3},{3,2},{4,5},{5,4},{6,7},{7,6},{8,9},{9,8},{10,11... | collective-permute-start | bytes 1179656 | tf_op jit(solution)/shard_map/ppermute | solution.py:567
  65.0 11.2 %collective-permute-start.18 = (bf16[4,64,768]{2,1,0:T(8,128)(2,1)S(1)}, bf16[4,64,768]{2,1,0:T(8,128)(2,1)S(1)}, u32[]{:S(2)}, u32[]{:S(2)}) collective-permute-start(bf16[4,64,768]{2,1,0:T(8,128)(2,1)S(1)} %get-tuple-element.278), channel_id=1, source_target_pairs={{0,4},{1,5},{2,6},{3,7},{4,0},{5,1},{6,2},{7,3},{8,12},{9,13},{10,... | collective-permute-start | bytes 1179656 | tf_op jit(solution)/shard_map/ppermute | solution.py:567
  76.5 13.0 %collective-permute-start.25 = (bf16[2,64,768]{2,1,0:T(8,128)(2,1)S(1)}, bf16[2,64,768]{2,1,0:T(8,128)(2,1)S(1)}, u32[]{:S(2)}, u32[]{:S(2)}) collective-permute-start(bf16[2,64,768]{2,1,0:T(8,128)(2,1)S(1)} %get-tuple-element.292), channel_id=1, source_target_pairs={{0,4},{1,5},{2,6},{3,7},{4,0},{5,1},{6,2},{7,3},{8,12},{9,13},{10,... | collective-permute-start | bytes 589832 | tf_op jit(solution)/shard_map/ppermute | solution.py:567
  78.2 11.3 %collective-permute-start.24 = (bf16[2,64,768]{2,1,0:T(8,128)(2,1)S(1)}, bf16[2,64,768]{2,1,0:T(8,128)(2,1)S(1)}, u32[]{:S(2)}, u32[]{:S(2)}) collective-permute-start(bf16[2,64,768]{2,1,0:T(8,128)(2,1)S(1)} %get-tuple-element.294), channel_id=1, source_target_pairs={{0,1},{1,0},{2,3},{3,2},{4,5},{5,4},{6,7},{7,6},{8,9},{9,8},{10,11... | collective-permute-start | bytes 589832 | tf_op jit(solution)/shard_map/ppermute | solution.py:567
  80.4 13.2 %collective-permute-start.23 = (bf16[4,64,768]{2,1,0:T(8,128)(2,1)S(1)}, bf16[4,64,768]{2,1,0:T(8,128)(2,1)S(1)}, u32[]{:S(2)}, u32[]{:S(2)}) collective-permute-start(bf16[4,64,768]{2,1,0:T(8,128)(2,1)S(1)} %get-tuple-element.273.refs_15_), channel_id=1, source_target_pairs={{0,1},{1,0},{2,3},{3,2},{4,5},{5,4},{6,7},{7,6},{8,9},{9,8},{10,11... | collective-permute-start | bytes 1179656 | tf_op jit(solution)/shard_map/ppermute | solution.py:567
  81.7 11.9 %collective-permute-start.22 = (bf16[4,64,768]{2,1,0:T(8,128)(2,1)S(1)}, bf16[4,64,768]{2,1,0:T(8,128)(2,1)S(1)}, u32[]{:S(2)}, u32[]{:S(2)}) collective-permute-start(bf16[4,64,768]{2,1,0:T(8,128)(2,1)S(1)} %get-tuple-element.274.refs_14_), channel_id=1, source_target_pairs={{0,4},{1,5},{2,6},{3,7},{4,0},{5,1},{6,2},{7,3},{8,12},{9,13},{10,... | collective-permute-start | bytes 1179656 | tf_op jit(solution)/shard_map/ppermute | solution.py:567
  100.4 14.0 %collective-permute-start.31 = (bf16[1,64,1536]{2,1,0:T(8,128)(2,1)S(1)}, bf16[1,64,1536]{2,1,0:T(8,128)(2,1)S(1)}, u32[]{:S(2)}, u32[]{:S(2)}) collective-permute-start(bf16[1,64,1536]{2,1,0:T(8,128)(2,1)S(1)} %pad_maximum_fusion.4), channel_id=1, source_target_pairs={{0,8},{1,9},{2,10},{3,11},{4,12},{5,13},{6,14},{7,15},{8,0},{9,1},... | collective-permute-start | bytes 589832 | tf_op jit(solution)/shard_map/ppermute | solution.py:567
  102.1 23.4 %collective-permute-start.35 = (bf16[8,16,1536]{2,1,0:T(8,128)(2,1)S(1)}, bf16[8,16,1536]{2,1,0:T(8,128)(2,1)S(1)}, u32[]{:S(2)}, u32[]{:S(2)}) collective-permute-start(bf16[8,16,1536]{2,1,0:T(8,128)(2,1)S(1)} %get-tuple-element.212.refs_8_), channel_id=1, source_target_pairs={{0,8},{1,9},{2,10},{3,11},{4,12},{5,13},{6,14},{7,15},{8,0},{9,1},... | collective-permute-start | bytes 1179656 | tf_op jit(solution)/shard_map/ppermute | solution.py:567
  102.5 17.6 %collective-permute-start.28 = (bf16[1,64,1536]{2,1,0:T(8,128)(2,1)S(1)}, bf16[1,64,1536]{2,1,0:T(8,128)(2,1)S(1)}, u32[]{:S(2)}, u32[]{:S(2)}) collective-permute-start(bf16[1,64,1536]{2,1,0:T(8,128)(2,1)S(1)} %add_convert_fusion.21), channel_id=1, source_target_pairs={{0,16},{1,17},{2,18},{3,19},{4,20},{5,21},{6,22},{7,23},{8,24},{9,... | collective-permute-start | bytes 589832 | tf_op jit(solution)/shard_map/ppermute | solution.py:567
  105.2 18.6 %collective-permute-start.26 = (bf16[9,16,1536]{2,1,0:T(8,128)(2,1)S(1)}, bf16[9,16,1536]{2,1,0:T(8,128)(2,1)S(1)}, u32[]{:S(2)}, u32[]{:S(2)}) collective-permute-start(bf16[9,16,1536]{2,1,0:T(8,128)(2,1)S(1)} %maximum_maximum_fusion), channel_id=1, source_target_pairs={{0,1},{1,0},{2,3},{3,2},{4,5},{5,4},{6,7},{7,6},{8,9},{9,8},{10,11... | collective-permute-start | bytes 1327112 | tf_op jit(solution)/shard_map/ppermute | solution.py:567
  114.4 14.8 %collective-permute-start.33 = (bf16[1,64,1536]{2,1,0:T(8,128)(2,1)S(1)}, bf16[1,64,1536]{2,1,0:T(8,128)(2,1)S(1)}, u32[]{:S(2)}, u32[]{:S(2)}) collective-permute-start(bf16[1,64,1536]{2,1,0:T(8,128)(2,1)S(1)} %add_convert_fusion.18), channel_id=1, source_target_pairs={{0,16},{1,17},{2,18},{3,19},{4,20},{5,21},{6,22},{7,23},{8,24},{9,... | collective-permute-start | bytes 589832 | tf_op jit(solution)/shard_map/ppermute | solution.py:567
  124.0 8.7 %collective-permute-start.32 = (bf16[5,16,1536]{2,1,0:T(8,128)(2,1)S(1)}, bf16[5,16,1536]{2,1,0:T(8,128)(2,1)S(1)}, u32[]{:S(2)}, u32[]{:S(2)}) collective-permute-start(bf16[5,16,1536]{2,1,0:T(8,128)(2,1)S(1)} %maximum_maximum_fusion.1), channel_id=1, source_target_pairs={{0,4},{1,5},{2,6},{3,7},{4,0},{5,1},{6,2},{7,3},{8,12},{9,13},{10,... | collective-permute-start | bytes 737288 | tf_op jit(solution)/shard_map/ppermute | solution.py:567
  125.6 9.2 %collective-permute-start.38 = (bf16[4,16,1536]{2,1,0:T(8,128)(2,1)S(1)}, bf16[4,16,1536]{2,1,0:T(8,128)(2,1)S(1)}, u32[]{:S(2)}, u32[]{:S(2)}) collective-permute-start(bf16[4,16,1536]{2,1,0:T(8,128)(2,1)S(1)} %get-tuple-element.286), channel_id=1, source_target_pairs={{0,4},{1,5},{2,6},{3,7},{4,0},{5,1},{6,2},{7,3},{8,12},{9,13},{10,... | collective-permute-start | bytes 589832 | tf_op jit(solution)/shard_map/ppermute | solution.py:567
  127.7 15.7 %collective-permute-start.42 = (bf16[2,64,1536]{2,1,0:T(8,128)(2,1)S(1)}, bf16[2,64,1536]{2,1,0:T(8,128)(2,1)S(1)}, u32[]{:S(2)}, u32[]{:S(2)}) collective-permute-start(bf16[2,64,1536]{2,1,0:T(8,128)(2,1)S(1)} %pad_maximum_fusion.refs_0_), channel_id=1, source_target_pairs={{0,4},{1,5},{2,6},{3,7},{4,0},{5,1},{6,2},{7,3},{8,12},{9,13},{10,... | collective-permute-start | bytes 1179656 | tf_op jit(solution)/shard_map/ppermute | solution.py:567
  129.3 8.9 %collective-permute-start.39 = (bf16[1,64,1536]{2,1,0:T(8,128)(2,1)S(1)}, bf16[1,64,1536]{2,1,0:T(8,128)(2,1)S(1)}, u32[]{:S(2)}, u32[]{:S(2)}) collective-permute-start(bf16[1,64,1536]{2,1,0:T(8,128)(2,1)S(1)} %add_convert_fusion.13), channel_id=1, source_target_pairs={{0,8},{1,9},{2,10},{3,11},{4,12},{5,13},{6,14},{7,15},{8,0},{9,1},... | collective-permute-start | bytes 589832 | tf_op jit(solution)/shard_map/ppermute | solution.py:567
  132.8 9.2 %collective-permute-start.36 = (bf16[3,16,1536]{2,1,0:T(8,128)(2,1)S(1)}, bf16[3,16,1536]{2,1,0:T(8,128)(2,1)S(1)}, u32[]{:S(2)}, u32[]{:S(2)}) collective-permute-start(bf16[3,16,1536]{2,1,0:T(8,128)(2,1)S(1)} %maximum_maximum_fusion.2), channel_id=1, source_target_pairs={{0,8},{1,9},{2,10},{3,11},{4,12},{5,13},{6,14},{7,15},{8,0},{9,1},... | collective-permute-start | bytes 442376 | tf_op jit(solution)/shard_map/ppermute | solution.py:567
  138.2 14.1 %collective-permute-start.45 = (bf16[2,64,1536]{2,1,0:T(8,128)(2,1)S(1)}, bf16[2,64,1536]{2,1,0:T(8,128)(2,1)S(1)}, u32[]{:S(2)}, u32[]{:S(2)}) collective-permute-start(bf16[2,64,1536]{2,1,0:T(8,128)(2,1)S(1)} %pad_maximum_fusion.1.refs_0_), channel_id=1, source_target_pairs={{0,4},{1,5},{2,6},{3,7},{4,0},{5,1},{6,2},{7,3},{8,12},{9,13},{10,... | collective-permute-start | bytes 1179656 | tf_op jit(solution)/shard_map/ppermute | solution.py:567
  143.4 9.0 %collective-permute-start.47 = (bf16[2,64,1536]{2,1,0:T(8,128)(2,1)S(1)}, bf16[2,64,1536]{2,1,0:T(8,128)(2,1)S(1)}, u32[]{:S(2)}, u32[]{:S(2)}) collective-permute-start(bf16[2,64,1536]{2,1,0:T(8,128)(2,1)S(1)} %collective-permute-done.42.refs_0_), channel_id=1, source_target_pairs={{0,2},{1,3},{2,0},{3,1},{4,6},{5,7},{6,4},{7,5},{8,10},{9,11},{10,... | collective-permute-start | bytes 1179656 | tf_op jit(solution)/shard_map/ppermute | solution.py:567
  (36 other events, 332.5 us)

commit v15 on v14

--- a/solution.py
+++ b/solution.py
@@ -1034,7 +1034,7 @@
     sums = attn_grads = None
     while ff_0.arriving is not None:
         turn += 1
-        chains = (ff_0, ff_1) if turn == 3 or "near" in ff_1.out else (ff_1, ff_0)
+        chains = (ff_0, ff_1) if "near" in ff_1.out else (ff_1, ff_0)
         for layer_idx, chain in ((1, ff_1), (0, ff_0)):
             token = write(chain, layer_idx, "near", token)
         for chain in chains:
@@ -1042,9 +1042,8 @@
         for key in ("early", "far"):
             for layer_idx, chain in ((1, ff_1), (0, ff_0)):
                 token = write(chain, layer_idx, key, token)
-        if turn != 2:
-            token = attn_0.step(token)
-        if turn > 2:
+        token = attn_0.step(token)
+        if turn > 1:
             token = attn_1.step(token)
         if sums is None and attn_0.arriving is None:
             sums = run(

time: 157 us -> 152 us (0.968)
  waiting for transfers between devices: 51 us -> 39.2 us
  starting transfers between devices: 52.7 us -> 59.5 us
    ppermute x48, waiting for transfers between devices: 51 us -> 39.2 us  [swap(): return lax.ppermute(array, axes, [(n, n ^ mask) for n in range(devices)])]
    ppermute x48, starting transfers between devices: 52.7 us -> 59.5 us  [swap(): return lax.ppermute(array, axes, [(n, n ^ mask) for n in range(devices)])]
  transfers between devices with their start and end apart: 48 -> 48, of which waited for: 20 -> 19; matrix products, arithmetic and copies ran while one was open for 2% -> 2% of each run, Pallas kernels for 24% -> 24%
where the time goes in v15:
time: 152 us
  starting transfers between devices  59.5 us (39%)
  Pallas kernels  47.5 us (31%)
  waiting for transfers between devices  39.2 us (26%)
  other arithmetic  3.71 us (2%)
  between operations  1.61 us (1%)
    ppermute x48, starting transfers between devices, swap(): return lax.ppermute(array, axes, [(n, n ^ mask) for n in range(devices)])  59.5 us
    ppermute x48, waiting for transfers between devices, swap(): return lax.ppermute(array, axes, [(n, n ^ mask) for n in range(devices)])  39.2 us
    pallas_call x10, Pallas kernels, run(): pl.pallas_call(kernel, name=name, in_specs=[pl.BlockSpec(memory_space=in_...  38.4 us
    pallas_call x6, Pallas kernels, finish(): pl.pallas_call(kernel, name='layer_%d_ff_grads' % layer_idx, in_specs=[pl...  9.08 us
  transfers between devices with their start and end apart: 48, of which 19 were waited for; matrix products, arithmetic and copies ran while one was open for 2% of the time, Pallas kernels for 24%

profile of v15, /device:TPU:0, one launch (start us, length us, event | category | flops | bytes accessed | tf_op | source)
XLA Modules:
  0.0 152.0 jit_solution(5567852288068655060)
XLA Ops:
  2.6 3.0 %collective-permute-start.1 = (bf16[16,1536]{1,0:T(8,128)(2,1)S(1)}, bf16[16,1536]{1,0:T(8,128)(2,1)S(1)}, u32[]{:S(2)}, u32[]{:S(2)}) collective-permute-start(bf16[16,1536]{1,0:T(8,128)(2,1)S(1)} %get-tuple-element.137), channel_id=1, source_target_pairs={{0,1},{1,0},{2,3},{3,2},{4,5},{5,4},{6,7},{7,6},{8,9},{9,8},{10,11... | collective-permute-start | bytes 147464 | tf_op jit(solution)/shard_map/ppermute | solution.py:567
  5.6 2.6 %collective-permute-start = (bf16[16,1536]{1,0:T(8,128)(2,1)S(1)}, bf16[16,1536]{1,0:T(8,128)(2,1)S(1)}, u32[]{:S(2)}, u32[]{:S(2)}) collective-permute-start(bf16[16,1536]{1,0:T(8,128)(2,1)S(1)} %get-tuple-element.136), channel_id=1, source_target_pairs={{0,16},{1,17},{2,18},{3,19},{4,20},{5,21},{6,22},{7,23},{8,24},{9,... | collective-permute-start | bytes 147464 | tf_op jit(solution)/shard_map/ppermute | solution.py:567
  9.7 2.7 %collective-permute-start.2 = (bf16[32,1536]{1,0:T(8,128)(2,1)S(1)}, bf16[32,1536]{1,0:T(8,128)(2,1)S(1)}, u32[]{:S(2)}, u32[]{:S(2)}) collective-permute-start(bf16[32,1536]{1,0:T(8,128)(2,1)S(1)} %get-tuple-element.325), channel_id=1, source_target_pairs={{0,16},{1,17},{2,18},{3,19},{4,20},{5,21},{6,22},{7,23},{8,24},{9,... | collective-permute-start | bytes 294920 | tf_op jit(solution)/shard_map/ppermute | solution.py:567
  13.9 4.6 %collective-permute-done.3 = bf16[3,128,512]{2,1,0:T(8,128)(2,1)S(1)} collective-permute-done((bf16[3,128,512]{2,1,0:T(8,128)(2,1)S(1)}, bf16[3,128,512]{2,1,0:T(8,128)(2,1)S(1)}, u32[]{:S(2)}, u32[]{:S(2)}) %collective-permute-start.3) | collective-permute-done | bytes 393248 | tf_op jit(solution)/shard_map/ppermute | solution.py:567
  23.2 4.0 %collective-permute-done.4 = bf16[64,1536]{1,0:T(8,128)(2,1)S(1)} collective-permute-done((bf16[64,1536]{1,0:T(8,128)(2,1)S(1)}, bf16[64,1536]{1,0:T(8,128)(2,1)S(1)}, u32[]{:S(2)}, u32[]{:S(2)}) %collective-permute-start.4) | collective-permute-done | bytes 196640 | tf_op jit(solution)/shard_map/ppermute | solution.py:567
  30.3 2.1 %prepare.1 = (f32[512,512]{1,0:T(8,128)S(1)}, bf16[512,512]{1,0:T(8,128)(2,1)S(1)}, f32[64,384]{1,0:T(8,128)S(1)}, s32[512,128]{1,0:T(8,128)S(1)}, s32[512,128]{1,0:T(8,128)S(1)}, /*index=5*/s32[64,128]{1,0:T(8,128)S(1)}) custom-call(bf16[512,512]{1,0:T(8,128)(2,1)S(1)} %bitcast.57, s32[8,64]{1,0:T(8,128)S(1)} %copy-done.7, s32[8,64]{1,0:T(8,128)S(1)} %copy-done.8, ...), custom_call_target="tpu_custom_call" | custom-call | flops 3449999872 | tf_op jit(solution)/shard_map/prepare/pallas_call | solution.py:99
  32.8 3.6 %collective-permute-done.7 = bf16[128,1536]{1,0:T(8,128)(2,1)S(1)} collective-permute-done((bf16[128,1536]{1,0:T(8,128)(2,1)S(1)}, bf16[128,1536]{1,0:T(8,128)(2,1)S(1)}, u32[]{:S(2)}, u32[]{:S(2)}) %collective-permute-start.7) | collective-permute-done | bytes 393248 | tf_op jit(solution)/shard_map/ppermute | solution.py:567
  38.8 2.8 %layer_0_attention.1 = (bf16[512,1536]{1,0:T(8,128)(2,1)S(1)}, bf16[512,1152]{1,0:T(8,128)(2,1)S(1)}, f32[512,384]{1,0:T(8,128)S(1)}, bf16[512,384]{1,0:T(8,128)...) custom-call(s32[4]{0:T(128)S(1)} %pad_add_fusion.refs_0_.place_ref, ...), custom_call_target="tpu_custom_call" | custom-call | flops 11500000256 | tf_op jit(solution)/shard_map/layer_0_attention/pallas_call | solution.py:99
  41.8 3.2 %layer_0_ff.1 = (bf16[2,512,1024]{2,1,0:T(8,128)(2,1)S(1)}, bf16[2,512,512]{2,1,0:T(8,128)(2,1)S(1)}, f32[512,512]{1,0:T(8,128)S(1)}, bf16[512,512]{1,0:T(8,128)(2,1)S(1)}) custom-call(s32[4]{0:T(128)S(1)} %pad_add_fusion.refs_0_.place_ref, f32[512,512]{1,0:T(8,128)S(1)} %get-tuple-element.153.refs_1_.refs_4_, ...), custom_call_target="tpu_custom_call" | custom-call | flops 3449999872 | tf_op jit(solution)/shard_map/layer_0_ff/pallas_call | solution.py:99
  45.0 3.3 %collective-permute-done.14 = bf16[3,128,512]{2,1,0:T(8,128)(2,1)S(1)} collective-permute-done((bf16[3,128,512]{2,1,0:T(8,128)(2,1)S(1)}, bf16[3,128,512]{2,1,0:T(8,128)(2,1)S(1)}, u32[]{:S(2)}, u32[]{:S(2)}) %collective-permute-start.14) | collective-permute-done | bytes 393248 | tf_op jit(solution)/shard_map/ppermute | solution.py:567
  48.4 2.8 %layer_1_attention.1 = (bf16[512,1536]{1,0:T(8,128)(2,1)S(1)}, bf16[512,1152]{1,0:T(8,128)(2,1)S(1)}, f32[512,384]{1,0:T(8,128)S(1)}, bf16[512,384]{1,0:T(8,128)...) custom-call(s32[4]{0:T(128)S(1)} %pad_add_fusion.refs_0_.place_ref, ...), custom_call_target="tpu_custom_call" | custom-call | flops 115000000 | tf_op jit(solution)/shard_map/layer_1_attention/pallas_call | solution.py:99
  51.2 7.3 %layer_1_ff.1 = (bf16[16,64,768]{2,1,0:T(8,128)(2,1)S(1)}, bf16[16,64,768]{2,1,0:T(8,128)(2,1)S(1)}, f32[8,1536]{1,0:T(8,128)S(1)}, f32[512,512]{1,0:T(8,128)S(1...) custom-call(s32[4]{0:T(128)S(1)} %pad_add_fusion.refs_0_.place_ref, bf16[512,512]{1,0:T(8,128)(2,1)S(1)} %bitcast.58, ...), custom_call_target="tpu_custom_call" | custom-call | flops 9200000000 | tf_op jit(solution)/shard_map/layer_1_ff/pallas_call | solution.py:99
  59.1 4.6 %layer_1_attention_backward.1 = (bf16[16,16,1536]{2,1,0:T(8,128)(2,1)S(1)}, bf16[16,16,1536]{2,1,0:T(8,128)(2,1)S(1)}, f32[8,1536]{1,0:T(8,128)S(1)}, f32[512,512]{1,0:T(8,128)S(1)}, f32[64,384]{1,0:T(8,128)S(1)}) custom-call(s32[4]{0:T(128)S(1)} %pad_add_fusion.refs_0_.place_ref, f32[8,1536]{1,0:T(8,128)S(1)} %get-tuple-element.164.refs_1_, ...), custom_call_target="tpu_custom_call" | custom-call | flops 6899999744 | tf_op jit(solution)/shard_map/layer_1_attention_backward/pallas_call | solution.py:99
  66.9 7.1 %layer_0_ff_backward.1 = (bf16[16,64,768]{2,1,0:T(8,128)(2,1)S(1)}, bf16[16,64,768]{2,1,0:T(8,128)(2,1)S(1)}, f32[8,1536]{1,0:T(8,128)S(1)}, f32[512,512]{1,0:T(8,128)S(1)}, bf16[512,512]{1,0:T(8,128)(2,1)S(1)}) custom-call(s32[4]{0:T(128)S(1)} %pad_add_fusion.refs_0_.place_ref, f32[512,512]{1,0:T(8,128)S(1)} %get-tuple-element.174.refs_1_, ...), custom_call_target="tpu_custom_call" | custom-call | flops 9200000000 | tf_op jit(solution)/shard_map/layer_0_ff_backward/pallas_call | solution.py:99
  83.3 6.1 %layer_0_attention_backward.1 = (bf16[16,16,1536]{2,1,0:T(8,128)(2,1)S(1)}, bf16[17,16,1536]{2,1,0:T(8,128)(2,1)S(1)}, f32[8,1536]{1,0:T(8,128)S(1)}, f32[512,512]{1,0:T(8,128)}) custom-call(s32[4]{0:T(128)S(1)} %pad_add_fusion.refs_0_.place_ref, f32[64,384]{1,0:T(8,128)S(1)} %get-tuple-element.171.refs_1_, s32[512,128]{1,0:T(8,128)S(1)} %get-tuple-element.172.refs_2_, ...), custom_call_target="tpu_custom_call" | custom-call | flops 8049999872 | tf_op jit(solution)/shard_map/layer_0_attention_backward/pallas_call | solution.py:99
  91.8 1.8 %collective-permute-done.23 = bf16[4,64,768]{2,1,0:T(8,128)(2,1)S(1)} collective-permute-done((bf16[4,64,768]{2,1,0:T(8,128)(2,1)S(1)}, bf16[4,64,768]{2,1,0:T(8,128)(2,1)S(1)}, u32[]{:S(2)}, u32[]{:S(2)}) %collective-permute-start.23) | collective-permute-done | bytes 393248 | tf_op jit(solution)/shard_map/ppermute | solution.py:567
  97.5 2.2 %collective-permute-start.32 = (bf16[1,64,1536]{2,1,0:T(8,128)(2,1)S(1)}, bf16[1,64,1536]{2,1,0:T(8,128)(2,1)S(1)}, u32[]{:S(2)}, u32[]{:S(2)}) collective-permute-start(bf16[1,64,1536]{2,1,0:T(8,128)(2,1)S(1)} %add_convert_fusion.20), channel_id=1, source_target_pairs={{0,16},{1,17},{2,18},{3,19},{4,20},{5,21},{6,22},{7,23},{8,24},{9,... | collective-permute-start | bytes 589832 | tf_op jit(solution)/shard_map/ppermute | solution.py:567
  100.0 2.5 %collective-permute-done.27 = bf16[2,64,768]{2,1,0:T(8,128)(2,1)S(1)} collective-permute-done((bf16[2,64,768]{2,1,0:T(8,128)(2,1)S(1)}, bf16[2,64,768]{2,1,0:T(8,128)(2,1)S(1)}, u32[]{:S(2)}, u32[]{:S(2)}) %collective-permute-start.27) | collective-permute-done | bytes 196640 | tf_op jit(solution)/shard_map/ppermute | solution.py:567
  104.2 5.5 %collective-permute-done.26 = bf16[9,16,1536]{2,1,0:T(8,128)(2,1)S(1)} collective-permute-done((bf16[9,16,1536]{2,1,0:T(8,128)(2,1)S(1)}, bf16[9,16,1536]{2,1,0:T(8,128)(2,1)S(1)}, u32[]{:S(2)}, u32[]{:S(2)}) %collective-permute-start.26) | collective-permute-done | bytes 442400 | tf_op jit(solution)/shard_map/ppermute | solution.py:567
  114.4 2.3 %collective-permute-start.35 = (bf16[1,64,1536]{2,1,0:T(8,128)(2,1)S(1)}, bf16[1,64,1536]{2,1,0:T(8,128)(2,1)S(1)}, u32[]{:S(2)}, u32[]{:S(2)}) collective-permute-start(bf16[1,64,1536]{2,1,0:T(8,128)(2,1)S(1)} %add_convert_fusion.14), channel_id=1, source_target_pairs={{0,16},{1,17},{2,18},{3,19},{4,20},{5,21},{6,22},{7,23},{8,24},{9,... | collective-permute-start | bytes 589832 | tf_op jit(solution)/shard_map/ppermute | solution.py:567
  120.1 2.9 %collective-permute-start.40 = (bf16[2,16,1536]{2,1,0:T(8,128)(2,1)S(1)}, bf16[2,16,1536]{2,1,0:T(8,128)(2,1)S(1)}, u32[]{:S(2)}, u32[]{:S(2)}) collective-permute-start(bf16[2,16,1536]{2,1,0:T(8,128)(2,1)S(1)} %get-tuple-element.298), channel_id=1, source_target_pairs={{0,16},{1,17},{2,18},{3,19},{4,20},{5,21},{6,22},{7,23},{8,24},{9,... | collective-permute-start | bytes 294920 | tf_op jit(solution)/shard_map/ppermute | solution.py:567
  123.1 3.0 %collective-permute-start.44 = (bf16[2,64,1536]{2,1,0:T(8,128)(2,1)S(1)}, bf16[2,64,1536]{2,1,0:T(8,128)(2,1)S(1)}, u32[]{:S(2)}, u32[]{:S(2)}) collective-permute-start(bf16[2,64,1536]{2,1,0:T(8,128)(2,1)S(1)} %pad_maximum_fusion.refs_0_), channel_id=1, source_target_pairs={{0,4},{1,5},{2,6},{3,7},{4,0},{5,1},{6,2},{7,3},{8,12},{9,13},{10,... | collective-permute-start | bytes 1179656 | tf_op jit(solution)/shard_map/ppermute | solution.py:567
  128.1 4.3 %collective-permute-start.38 = (bf16[2,16,1536]{2,1,0:T(8,128)(2,1)S(1)}, bf16[2,16,1536]{2,1,0:T(8,128)(2,1)S(1)}, u32[]{:S(2)}, u32[]{:S(2)}) collective-permute-start(bf16[2,16,1536]{2,1,0:T(8,128)(2,1)S(1)} %maximum_maximum_fusion.3), channel_id=1, source_target_pairs={{0,16},{1,17},{2,18},{3,19},{4,20},{5,21},{6,22},{7,23},{8,24},{9,... | collective-permute-start | bytes 294920 | tf_op jit(solution)/shard_map/ppermute | solution.py:567
  142.7 4.8 %collective-permute-done.43.refs_0_ = bf16[2,64,1536]{2,1,0:T(8,128)(2,1)S(1)} collective-permute-done((bf16[2,64,1536]{2,1,0:T(8,128)(2,1)S(1)}, bf16[2,64,1536]{2,1,0:T(8,128)(2,1)S(1)}, u32[]{:S(2)}, u32[]{:S(2)}) %collective-permute-start.43) | collective-permute-done | bytes 393248 | tf_op jit(solution)/shard_map/ppermute | solution.py:567
  (176 shorter events, 61.4 us)
Async XLA Ops:
  8.3 10.3 %collective-permute-start.3 = (bf16[3,128,512]{2,1,0:T(8,128)(2,1)S(1)}, bf16[3,128,512]{2,1,0:T(8,128)(2,1)S(1)}, u32[]{:S(2)}, u32[]{:S(2)}) collective-permute-start(bf16[3,128,512]{2,1,0:T(8,128)(2,1)S(1)} %get-tuple-element.145), channel_id=1, source_target_pairs={{0,1},{1,0},{2,3},{3,2},{4,5},{5,4},{6,7},{7,6},{8,9},{9,8},{10,11... | collective-permute-start | bytes 1179656 | tf_op jit(solution)/shard_map/ppermute | solution.py:567
  9.7 9.7 %collective-permute-start.2 = (bf16[32,1536]{1,0:T(8,128)(2,1)S(1)}, bf16[32,1536]{1,0:T(8,128)(2,1)S(1)}, u32[]{:S(2)}, u32[]{:S(2)}) collective-permute-start(bf16[32,1536]{1,0:T(8,128)(2,1)S(1)} %get-tuple-element.325), channel_id=1, source_target_pairs={{0,16},{1,17},{2,18},{3,19},{4,20},{5,21},{6,22},{7,23},{8,24},{9,... | collective-permute-start | bytes 294920 | tf_op jit(solution)/shard_map/ppermute | solution.py:567
  12.4 8.6 %collective-permute-start.5 = (bf16[32,1536]{1,0:T(8,128)(2,1)S(1)}, bf16[32,1536]{1,0:T(8,128)(2,1)S(1)}, u32[]{:S(2)}, u32[]{:S(2)}) collective-permute-start(bf16[32,1536]{1,0:T(8,128)(2,1)S(1)} %get-tuple-element.319), channel_id=1, source_target_pairs={{0,4},{1,5},{2,6},{3,7},{4,0},{5,1},{6,2},{7,3},{8,12},{9,13},{10,... | collective-permute-start | bytes 294920 | tf_op jit(solution)/shard_map/ppermute | solution.py:567
  18.6 13.9 %collective-permute-start.9 = (bf16[3,128,512]{2,1,0:T(8,128)(2,1)S(1)}, bf16[3,128,512]{2,1,0:T(8,128)(2,1)S(1)}, u32[]{:S(2)}, u32[]{:S(2)}) collective-permute-start(bf16[3,128,512]{2,1,0:T(8,128)(2,1)S(1)} %get-tuple-element.151), channel_id=1, source_target_pairs={{0,1},{1,0},{2,3},{3,2},{4,5},{5,4},{6,7},{7,6},{8,9},{9,8},{10,11... | collective-permute-start | bytes 1179656 | tf_op jit(solution)/shard_map/ppermute | solution.py:567
  22.7 10.1 %collective-permute-start.8 = (bf16[3,128,512]{2,1,0:T(8,128)(2,1)S(1)}, bf16[3,128,512]{2,1,0:T(8,128)(2,1)S(1)}, u32[]{:S(2)}, u32[]{:S(2)}) collective-permute-start(bf16[3,128,512]{2,1,0:T(8,128)(2,1)S(1)} %collective-permute-done.3), channel_id=1, source_target_pairs={{0,4},{1,5},{2,6},{3,7},{4,0},{5,1},{6,2},{7,3},{8,12},{9,13},{10,... | collective-permute-start | bytes 1179656 | tf_op jit(solution)/shard_map/ppermute | solution.py:567
  27.3 9.1 %collective-permute-start.10 = (bf16[128,1536]{1,0:T(8,128)(2,1)S(1)}, bf16[128,1536]{1,0:T(8,128)(2,1)S(1)}, u32[]{:S(2)}, u32[]{:S(2)}) collective-permute-start(bf16[128,1536]{1,0:T(8,128)(2,1)S(1)} %get-tuple-element.312), channel_id=1, source_target_pairs={{0,1},{1,0},{2,3},{3,2},{4,5},{5,4},{6,7},{7,6},{8,9},{9,8},{10,11... | collective-permute-start | bytes 1179656 | tf_op jit(solution)/shard_map/ppermute | solution.py:567
  37.2 11.1 %collective-permute-start.14 = (bf16[3,128,512]{2,1,0:T(8,128)(2,1)S(1)}, bf16[3,128,512]{2,1,0:T(8,128)(2,1)S(1)}, u32[]{:S(2)}, u32[]{:S(2)}) collective-permute-start(bf16[3,128,512]{2,1,0:T(8,128)(2,1)S(1)} %collective-permute-done.9), channel_id=1, source_target_pairs={{0,4},{1,5},{2,6},{3,7},{4,0},{5,1},{6,2},{7,3},{8,12},{9,13},{10,... | collective-permute-start | bytes 1179656 | tf_op jit(solution)/shard_map/ppermute | solution.py:567
  64.2 11.6 %collective-permute-start.19 = (bf16[4,64,768]{2,1,0:T(8,128)(2,1)S(1)}, bf16[4,64,768]{2,1,0:T(8,128)(2,1)S(1)}, u32[]{:S(2)}, u32[]{:S(2)}) collective-permute-start(bf16[4,64,768]{2,1,0:T(8,128)(2,1)S(1)} %get-tuple-element.277), channel_id=1, source_target_pairs={{0,1},{1,0},{2,3},{3,2},{4,5},{5,4},{6,7},{7,6},{8,9},{9,8},{10,11... | collective-permute-start | bytes 1179656 | tf_op jit(solution)/shard_map/ppermute | solution.py:567
  65.0 11.2 %collective-permute-start.18 = (bf16[4,64,768]{2,1,0:T(8,128)(2,1)S(1)}, bf16[4,64,768]{2,1,0:T(8,128)(2,1)S(1)}, u32[]{:S(2)}, u32[]{:S(2)}) collective-permute-start(bf16[4,64,768]{2,1,0:T(8,128)(2,1)S(1)} %get-tuple-element.278), channel_id=1, source_target_pairs={{0,4},{1,5},{2,6},{3,7},{4,0},{5,1},{6,2},{7,3},{8,12},{9,13},{10,... | collective-permute-start | bytes 1179656 | tf_op jit(solution)/shard_map/ppermute | solution.py:567
  76.5 13.0 %collective-permute-start.25 = (bf16[2,64,768]{2,1,0:T(8,128)(2,1)S(1)}, bf16[2,64,768]{2,1,0:T(8,128)(2,1)S(1)}, u32[]{:S(2)}, u32[]{:S(2)}) collective-permute-start(bf16[2,64,768]{2,1,0:T(8,128)(2,1)S(1)} %get-tuple-element.292), channel_id=1, source_target_pairs={{0,4},{1,5},{2,6},{3,7},{4,0},{5,1},{6,2},{7,3},{8,12},{9,13},{10,... | collective-permute-start | bytes 589832 | tf_op jit(solution)/shard_map/ppermute | solution.py:567
  78.2 11.3 %collective-permute-start.24 = (bf16[2,64,768]{2,1,0:T(8,128)(2,1)S(1)}, bf16[2,64,768]{2,1,0:T(8,128)(2,1)S(1)}, u32[]{:S(2)}, u32[]{:S(2)}) collective-permute-start(bf16[2,64,768]{2,1,0:T(8,128)(2,1)S(1)} %get-tuple-element.294), channel_id=1, source_target_pairs={{0,1},{1,0},{2,3},{3,2},{4,5},{5,4},{6,7},{7,6},{8,9},{9,8},{10,11... | collective-permute-start | bytes 589832 | tf_op jit(solution)/shard_map/ppermute | solution.py:567
  80.4 13.2 %collective-permute-start.23 = (bf16[4,64,768]{2,1,0:T(8,128)(2,1)S(1)}, bf16[4,64,768]{2,1,0:T(8,128)(2,1)S(1)}, u32[]{:S(2)}, u32[]{:S(2)}) collective-permute-start(bf16[4,64,768]{2,1,0:T(8,128)(2,1)S(1)} %get-tuple-element.273.refs_15_), channel_id=1, source_target_pairs={{0,1},{1,0},{2,3},{3,2},{4,5},{5,4},{6,7},{7,6},{8,9},{9,8},{10,11... | collective-permute-start | bytes 1179656 | tf_op jit(solution)/shard_map/ppermute | solution.py:567
  81.7 11.9 %collective-permute-start.22 = (bf16[4,64,768]{2,1,0:T(8,128)(2,1)S(1)}, bf16[4,64,768]{2,1,0:T(8,128)(2,1)S(1)}, u32[]{:S(2)}, u32[]{:S(2)}) collective-permute-start(bf16[4,64,768]{2,1,0:T(8,128)(2,1)S(1)} %get-tuple-element.274.refs_14_), channel_id=1, source_target_pairs={{0,4},{1,5},{2,6},{3,7},{4,0},{5,1},{6,2},{7,3},{8,12},{9,13},{10,... | collective-permute-start | bytes 1179656 | tf_op jit(solution)/shard_map/ppermute | solution.py:567
  91.4 20.2 %collective-permute-start.33 = (bf16[8,16,1536]{2,1,0:T(8,128)(2,1)S(1)}, bf16[8,16,1536]{2,1,0:T(8,128)(2,1)S(1)}, u32[]{:S(2)}, u32[]{:S(2)}) collective-permute-start(bf16[8,16,1536]{2,1,0:T(8,128)(2,1)S(1)} %get-tuple-element.210.refs_8_), channel_id=1, source_target_pairs={{0,8},{1,9},{2,10},{3,11},{4,12},{5,13},{6,14},{7,15},{8,0},{9,1},... | collective-permute-start | bytes 1179656 | tf_op jit(solution)/shard_map/ppermute | solution.py:567
  96.0 13.7 %collective-permute-start.26 = (bf16[9,16,1536]{2,1,0:T(8,128)(2,1)S(1)}, bf16[9,16,1536]{2,1,0:T(8,128)(2,1)S(1)}, u32[]{:S(2)}, u32[]{:S(2)}) collective-permute-start(bf16[9,16,1536]{2,1,0:T(8,128)(2,1)S(1)} %maximum_maximum_fusion), channel_id=1, source_target_pairs={{0,1},{1,0},{2,3},{3,2},{4,5},{5,4},{6,7},{7,6},{8,9},{9,8},{10,11... | collective-permute-start | bytes 1327112 | tf_op jit(solution)/shard_map/ppermute | solution.py:567
  97.5 14.6 %collective-permute-start.32 = (bf16[1,64,1536]{2,1,0:T(8,128)(2,1)S(1)}, bf16[1,64,1536]{2,1,0:T(8,128)(2,1)S(1)}, u32[]{:S(2)}, u32[]{:S(2)}) collective-permute-start(bf16[1,64,1536]{2,1,0:T(8,128)(2,1)S(1)} %add_convert_fusion.20), channel_id=1, source_target_pairs={{0,16},{1,17},{2,18},{3,19},{4,20},{5,21},{6,22},{7,23},{8,24},{9,... | collective-permute-start | bytes 589832 | tf_op jit(solution)/shard_map/ppermute | solution.py:567
  102.5 11.8 %collective-permute-start.31 = (bf16[1,64,1536]{2,1,0:T(8,128)(2,1)S(1)}, bf16[1,64,1536]{2,1,0:T(8,128)(2,1)S(1)}, u32[]{:S(2)}, u32[]{:S(2)}) collective-permute-start(bf16[1,64,1536]{2,1,0:T(8,128)(2,1)S(1)} %pad_maximum_fusion.4), channel_id=1, source_target_pairs={{0,8},{1,9},{2,10},{3,11},{4,12},{5,13},{6,14},{7,15},{8,0},{9,1},... | collective-permute-start | bytes 589832 | tf_op jit(solution)/shard_map/ppermute | solution.py:567
  112.2 10.8 %collective-permute-start.36 = (bf16[1,64,1536]{2,1,0:T(8,128)(2,1)S(1)}, bf16[1,64,1536]{2,1,0:T(8,128)(2,1)S(1)}, u32[]{:S(2)}, u32[]{:S(2)}) collective-permute-start(bf16[1,64,1536]{2,1,0:T(8,128)(2,1)S(1)} %add_convert_fusion.15), channel_id=1, source_target_pairs={{0,8},{1,9},{2,10},{3,11},{4,12},{5,13},{6,14},{7,15},{8,0},{9,1},... | collective-permute-start | bytes 589832 | tf_op jit(solution)/shard_map/ppermute | solution.py:567
  114.4 13.4 %collective-permute-start.35 = (bf16[1,64,1536]{2,1,0:T(8,128)(2,1)S(1)}, bf16[1,64,1536]{2,1,0:T(8,128)(2,1)S(1)}, u32[]{:S(2)}, u32[]{:S(2)}) collective-permute-start(bf16[1,64,1536]{2,1,0:T(8,128)(2,1)S(1)} %add_convert_fusion.14), channel_id=1, source_target_pairs={{0,16},{1,17},{2,18},{3,19},{4,20},{5,21},{6,22},{7,23},{8,24},{9,... | collective-permute-start | bytes 589832 | tf_op jit(solution)/shard_map/ppermute | solution.py:567
  118.1 9.8 %collective-permute-start.34 = (bf16[3,16,1536]{2,1,0:T(8,128)(2,1)S(1)}, bf16[3,16,1536]{2,1,0:T(8,128)(2,1)S(1)}, u32[]{:S(2)}, u32[]{:S(2)}) collective-permute-start(bf16[3,16,1536]{2,1,0:T(8,128)(2,1)S(1)} %maximum_maximum_fusion.2), channel_id=1, source_target_pairs={{0,8},{1,9},{2,10},{3,11},{4,12},{5,13},{6,14},{7,15},{8,0},{9,1},... | collective-permute-start | bytes 442376 | tf_op jit(solution)/shard_map/ppermute | solution.py:567
  120.1 12.2 %collective-permute-start.40 = (bf16[2,16,1536]{2,1,0:T(8,128)(2,1)S(1)}, bf16[2,16,1536]{2,1,0:T(8,128)(2,1)S(1)}, u32[]{:S(2)}, u32[]{:S(2)}) collective-permute-start(bf16[2,16,1536]{2,1,0:T(8,128)(2,1)S(1)} %get-tuple-element.298), channel_id=1, source_target_pairs={{0,16},{1,17},{2,18},{3,19},{4,20},{5,21},{6,22},{7,23},{8,24},{9,... | collective-permute-start | bytes 294920 | tf_op jit(solution)/shard_map/ppermute | solution.py:567
  123.1 16.0 %collective-permute-start.44 = (bf16[2,64,1536]{2,1,0:T(8,128)(2,1)S(1)}, bf16[2,64,1536]{2,1,0:T(8,128)(2,1)S(1)}, u32[]{:S(2)}, u32[]{:S(2)}) collective-permute-start(bf16[2,64,1536]{2,1,0:T(8,128)(2,1)S(1)} %pad_maximum_fusion.refs_0_), channel_id=1, source_target_pairs={{0,4},{1,5},{2,6},{3,7},{4,0},{5,1},{6,2},{7,3},{8,12},{9,13},{10,... | collective-permute-start | bytes 1179656 | tf_op jit(solution)/shard_map/ppermute | solution.py:567
  128.1 9.6 %collective-permute-start.38 = (bf16[2,16,1536]{2,1,0:T(8,128)(2,1)S(1)}, bf16[2,16,1536]{2,1,0:T(8,128)(2,1)S(1)}, u32[]{:S(2)}, u32[]{:S(2)}) collective-permute-start(bf16[2,16,1536]{2,1,0:T(8,128)(2,1)S(1)} %maximum_maximum_fusion.3), channel_id=1, source_target_pairs={{0,16},{1,17},{2,18},{3,19},{4,20},{5,21},{6,22},{7,23},{8,24},{9,... | collective-permute-start | bytes 294920 | tf_op jit(solution)/shard_map/ppermute | solution.py:567
  135.9 11.5 %collective-permute-start.43 = (bf16[2,64,1536]{2,1,0:T(8,128)(2,1)S(1)}, bf16[2,64,1536]{2,1,0:T(8,128)(2,1)S(1)}, u32[]{:S(2)}, u32[]{:S(2)}) collective-permute-start(bf16[2,64,1536]{2,1,0:T(8,128)(2,1)S(1)} %pad_maximum_fusion.1.refs_0_), channel_id=1, source_target_pairs={{0,4},{1,5},{2,6},{3,7},{4,0},{5,1},{6,2},{7,3},{8,12},{9,13},{10,... | collective-permute-start | bytes 1179656 | tf_op jit(solution)/shard_map/ppermute | solution.py:567
  (36 other events, 336.1 us)

commit v16 on v13

--- a/solution.py
+++ b/solution.py
@@ -1020,7 +1020,7 @@
             done = finish(tie(ff_1.out["near"], token), near_masks, 1, place, shape)
             token = done[0]
         token = attn_0.step(token)
-        if turn > 1:
+        if turn > 2:
             token = attn_1.step(token)
         if sums is None and attn_0.arriving is None:
             sums = run(

time: 147 us -> 147 us (level)
  starting transfers between devices: 58.7 us -> 53.5 us
  waiting for transfers between devices: 37.2 us -> 42.2 us
    ppermute x46, starting transfers between devices: 58.7 us -> 53.5 us  [swap(): return lax.ppermute(array, axes, [(n, n ^ mask) for n in range(devices)])]
    ppermute x46, waiting for transfers between devices: 37.2 us -> 42.2 us  [swap(): return lax.ppermute(array, axes, [(n, n ^ mask) for n in range(devices)])]
  transfers between devices with their start and end apart: 46 -> 46, of which waited for: 20 -> 19; matrix products, arithmetic and copies ran while one was open for 3% -> 3% of each run, Pallas kernels for 23% -> 23%
where the time goes in v16:
time: 147 us
  starting transfers between devices  53.5 us (36%)
  Pallas kernels  45.2 us (31%)
  waiting for transfers between devices  42.2 us (29%)
  other arithmetic  3.86 us (3%)
  between operations  1.6 us (1%)
    ppermute x46, starting transfers between devices, swap(): return lax.ppermute(array, axes, [(n, n ^ mask) for n in range(devices)])  53.5 us
    ppermute x46, waiting for transfers between devices, swap(): return lax.ppermute(array, axes, [(n, n ^ mask) for n in range(devices)])  42.2 us
    pallas_call x10, Pallas kernels, run(): pl.pallas_call(kernel, name=name, in_specs=[pl.BlockSpec(memory_space=in_...  38.4 us
    pallas_call x4, Pallas kernels, finish(): pl.pallas_call(kernel, name='layer_%d_ff_grads' % layer_idx, in_specs=[pl...  6.73 us
  transfers between devices with their start and end apart: 46, of which 19 were waited for; matrix products, arithmetic and copies ran while one was open for 3% of the time, Pallas kernels for 23%

profile of v16, /device:TPU:0, one launch (start us, length us, event | category | flops | bytes accessed | tf_op | source)
XLA Modules:
  0.0 146.7 jit_solution(646733695399706531)
XLA Ops:
  2.6 3.0 %collective-permute-start.1 = (bf16[16,1536]{1,0:T(8,128)(2,1)S(1)}, bf16[16,1536]{1,0:T(8,128)(2,1)S(1)}, u32[]{:S(2)}, u32[]{:S(2)}) collective-permute-start(bf16[16,1536]{1,0:T(8,128)(2,1)S(1)} %get-tuple-element.124), channel_id=1, source_target_pairs={{0,1},{1,0},{2,3},{3,2},{4,5},{5,4},{6,7},{7,6},{8,9},{9,8},{10,11... | collective-permute-start | bytes 147464 | tf_op jit(solution)/shard_map/ppermute | solution.py:562
  5.6 2.6 %collective-permute-start = (bf16[16,1536]{1,0:T(8,128)(2,1)S(1)}, bf16[16,1536]{1,0:T(8,128)(2,1)S(1)}, u32[]{:S(2)}, u32[]{:S(2)}) collective-permute-start(bf16[16,1536]{1,0:T(8,128)(2,1)S(1)} %get-tuple-element.123), channel_id=1, source_target_pairs={{0,16},{1,17},{2,18},{3,19},{4,20},{5,21},{6,22},{7,23},{8,24},{9,... | collective-permute-start | bytes 147464 | tf_op jit(solution)/shard_map/ppermute | solution.py:562
  9.7 2.7 %collective-permute-start.2 = (bf16[32,1536]{1,0:T(8,128)(2,1)S(1)}, bf16[32,1536]{1,0:T(8,128)(2,1)S(1)}, u32[]{:S(2)}, u32[]{:S(2)}) collective-permute-start(bf16[32,1536]{1,0:T(8,128)(2,1)S(1)} %get-tuple-element.299), channel_id=1, source_target_pairs={{0,16},{1,17},{2,18},{3,19},{4,20},{5,21},{6,22},{7,23},{8,24},{9,... | collective-permute-start | bytes 294920 | tf_op jit(solution)/shard_map/ppermute | solution.py:562
  13.9 4.6 %collective-permute-done.3 = bf16[3,128,512]{2,1,0:T(8,128)(2,1)S(1)} collective-permute-done((bf16[3,128,512]{2,1,0:T(8,128)(2,1)S(1)}, bf16[3,128,512]{2,1,0:T(8,128)(2,1)S(1)}, u32[]{:S(2)}, u32[]{:S(2)}) %collective-permute-start.3) | collective-permute-done | bytes 393248 | tf_op jit(solution)/shard_map/ppermute | solution.py:562
  23.2 4.0 %collective-permute-done.4 = bf16[64,1536]{1,0:T(8,128)(2,1)S(1)} collective-permute-done((bf16[64,1536]{1,0:T(8,128)(2,1)S(1)}, bf16[64,1536]{1,0:T(8,128)(2,1)S(1)}, u32[]{:S(2)}, u32[]{:S(2)}) %collective-permute-start.4) | collective-permute-done | bytes 196640 | tf_op jit(solution)/shard_map/ppermute | solution.py:562
  30.3 2.1 %prepare.1 = (f32[512,512]{1,0:T(8,128)S(1)}, bf16[512,512]{1,0:T(8,128)(2,1)S(1)}, f32[64,384]{1,0:T(8,128)S(1)}, s32[512,128]{1,0:T(8,128)S(1)}, s32[512,128]{1,0:T(8,128)S(1)}, /*index=5*/s32[64,128]{1,0:T(8,128)S(1)}) custom-call(bf16[512,512]{1,0:T(8,128)(2,1)S(1)} %bitcast.57, s32[8,64]{1,0:T(8,128)S(1)} %copy-done.7, s32[8,64]{1,0:T(8,128)S(1)} %copy-done.8, ...), custom_call_target="tpu_custom_call" | custom-call | flops 3449999872 | tf_op jit(solution)/shard_map/prepare/pallas_call | solution.py:99
  32.8 3.6 %collective-permute-done.7 = bf16[128,1536]{1,0:T(8,128)(2,1)S(1)} collective-permute-done((bf16[128,1536]{1,0:T(8,128)(2,1)S(1)}, bf16[128,1536]{1,0:T(8,128)(2,1)S(1)}, u32[]{:S(2)}, u32[]{:S(2)}) %collective-permute-start.7) | collective-permute-done | bytes 393248 | tf_op jit(solution)/shard_map/ppermute | solution.py:562
  38.8 2.8 %layer_0_attention.1 = (bf16[512,1536]{1,0:T(8,128)(2,1)S(1)}, bf16[512,1152]{1,0:T(8,128)(2,1)S(1)}, f32[512,384]{1,0:T(8,128)S(1)}, bf16[512,384]{1,0:T(8,128)...) custom-call(s32[4]{0:T(128)S(1)} %pad_add_fusion.refs_0_.place_ref, ...), custom_call_target="tpu_custom_call" | custom-call | flops 11500000256 | tf_op jit(solution)/shard_map/layer_0_attention/pallas_call | solution.py:99
  41.8 3.2 %layer_0_ff.1 = (bf16[2,512,1024]{2,1,0:T(8,128)(2,1)S(1)}, bf16[2,512,512]{2,1,0:T(8,128)(2,1)S(1)}, f32[512,512]{1,0:T(8,128)S(1)}, bf16[512,512]{1,0:T(8,128)(2,1)S(1)}) custom-call(s32[4]{0:T(128)S(1)} %pad_add_fusion.refs_0_.place_ref, f32[512,512]{1,0:T(8,128)S(1)} %get-tuple-element.140.refs_1_.refs_4_, ...), custom_call_target="tpu_custom_call" | custom-call | flops 3449999872 | tf_op jit(solution)/shard_map/layer_0_ff/pallas_call | solution.py:99
  45.0 3.3 %collective-permute-done.14 = bf16[3,128,512]{2,1,0:T(8,128)(2,1)S(1)} collective-permute-done((bf16[3,128,512]{2,1,0:T(8,128)(2,1)S(1)}, bf16[3,128,512]{2,1,0:T(8,128)(2,1)S(1)}, u32[]{:S(2)}, u32[]{:S(2)}) %collective-permute-start.14) | collective-permute-done | bytes 393248 | tf_op jit(solution)/shard_map/ppermute | solution.py:562
  48.4 2.8 %layer_1_attention.1 = (bf16[512,1536]{1,0:T(8,128)(2,1)S(1)}, bf16[512,1152]{1,0:T(8,128)(2,1)S(1)}, f32[512,384]{1,0:T(8,128)S(1)}, bf16[512,384]{1,0:T(8,128)...) custom-call(s32[4]{0:T(128)S(1)} %pad_add_fusion.refs_0_.place_ref, ...), custom_call_target="tpu_custom_call" | custom-call | flops 115000000 | tf_op jit(solution)/shard_map/layer_1_attention/pallas_call | solution.py:99
  51.2 7.3 %layer_1_ff.1 = (bf16[16,64,768]{2,1,0:T(8,128)(2,1)S(1)}, bf16[16,64,768]{2,1,0:T(8,128)(2,1)S(1)}, f32[8,1536]{1,0:T(8,128)S(1)}, f32[512,512]{1,0:T(8,128)S(1...) custom-call(s32[4]{0:T(128)S(1)} %pad_add_fusion.refs_0_.place_ref, bf16[512,512]{1,0:T(8,128)(2,1)S(1)} %bitcast.58, ...), custom_call_target="tpu_custom_call" | custom-call | flops 9200000000 | tf_op jit(solution)/shard_map/layer_1_ff/pallas_call | solution.py:99
  59.1 4.6 %layer_1_attention_backward.1 = (bf16[16,16,1536]{2,1,0:T(8,128)(2,1)S(1)}, bf16[16,16,1536]{2,1,0:T(8,128)(2,1)S(1)}, f32[8,1536]{1,0:T(8,128)S(1)}, f32[512,512]{1,0:T(8,128)S(1)}, f32[64,384]{1,0:T(8,128)S(1)}) custom-call(s32[4]{0:T(128)S(1)} %pad_add_fusion.refs_0_.place_ref, f32[8,1536]{1,0:T(8,128)S(1)} %get-tuple-element.151.refs_1_, ...), custom_call_target="tpu_custom_call" | custom-call | flops 6899999744 | tf_op jit(solution)/shard_map/layer_1_attention_backward/pallas_call | solution.py:99
  66.9 7.1 %layer_0_ff_backward.1 = (bf16[16,64,768]{2,1,0:T(8,128)(2,1)S(1)}, bf16[16,64,768]{2,1,0:T(8,128)(2,1)S(1)}, f32[8,1536]{1,0:T(8,128)S(1)}, f32[512,512]{1,0:T(8,128)S(1)}, bf16[512,512]{1,0:T(8,128)(2,1)S(1)}) custom-call(s32[4]{0:T(128)S(1)} %pad_add_fusion.refs_0_.place_ref, f32[512,512]{1,0:T(8,128)S(1)} %get-tuple-element.161.refs_1_, ...), custom_call_target="tpu_custom_call" | custom-call | flops 9200000000 | tf_op jit(solution)/shard_map/layer_0_ff_backward/pallas_call | solution.py:99
  83.3 6.1 %layer_0_attention_backward.1 = (bf16[16,16,1536]{2,1,0:T(8,128)(2,1)S(1)}, bf16[17,16,1536]{2,1,0:T(8,128)(2,1)S(1)}, f32[8,1536]{1,0:T(8,128)S(1)}, f32[512,512]{1,0:T(8,128)}) custom-call(s32[4]{0:T(128)S(1)} %pad_add_fusion.refs_0_.place_ref, f32[64,384]{1,0:T(8,128)S(1)} %get-tuple-element.158.refs_1_, s32[512,128]{1,0:T(8,128)S(1)} %get-tuple-element.159.refs_2_, ...), custom_call_target="tpu_custom_call" | custom-call | flops 8049999872 | tf_op jit(solution)/shard_map/layer_0_attention_backward/pallas_call | solution.py:99
  91.8 1.8 %collective-permute-done.23 = bf16[4,64,768]{2,1,0:T(8,128)(2,1)S(1)} collective-permute-done((bf16[4,64,768]{2,1,0:T(8,128)(2,1)S(1)}, bf16[4,64,768]{2,1,0:T(8,128)(2,1)S(1)}, u32[]{:S(2)}, u32[]{:S(2)}) %collective-permute-start.23) | collective-permute-done | bytes 393248 | tf_op jit(solution)/shard_map/ppermute | solution.py:562
  97.5 2.2 %collective-permute-start.32 = (bf16[1,64,1536]{2,1,0:T(8,128)(2,1)S(1)}, bf16[1,64,1536]{2,1,0:T(8,128)(2,1)S(1)}, u32[]{:S(2)}, u32[]{:S(2)}) collective-permute-start(bf16[1,64,1536]{2,1,0:T(8,128)(2,1)S(1)} %add_convert_fusion.20), channel_id=1, source_target_pairs={{0,16},{1,17},{2,18},{3,19},{4,20},{5,21},{6,22},{7,23},{8,24},{9,... | collective-permute-start | bytes 589832 | tf_op jit(solution)/shard_map/ppermute | solution.py:562
  100.0 2.4 %collective-permute-done.27 = bf16[2,64,768]{2,1,0:T(8,128)(2,1)S(1)} collective-permute-done((bf16[2,64,768]{2,1,0:T(8,128)(2,1)S(1)}, bf16[2,64,768]{2,1,0:T(8,128)(2,1)S(1)}, u32[]{:S(2)}, u32[]{:S(2)}) %collective-permute-start.27) | collective-permute-done | bytes 196640 | tf_op jit(solution)/shard_map/ppermute | solution.py:562
  104.2 5.5 %collective-permute-done.26 = bf16[9,16,1536]{2,1,0:T(8,128)(2,1)S(1)} collective-permute-done((bf16[9,16,1536]{2,1,0:T(8,128)(2,1)S(1)}, bf16[9,16,1536]{2,1,0:T(8,128)(2,1)S(1)}, u32[]{:S(2)}, u32[]{:S(2)}) %collective-permute-start.26) | collective-permute-done | bytes 442400 | tf_op jit(solution)/shard_map/ppermute | solution.py:562
  114.4 1.9 %collective-permute-start.34 = (bf16[1,64,1536]{2,1,0:T(8,128)(2,1)S(1)}, bf16[1,64,1536]{2,1,0:T(8,128)(2,1)S(1)}, u32[]{:S(2)}, u32[]{:S(2)}) collective-permute-start(bf16[1,64,1536]{2,1,0:T(8,128)(2,1)S(1)} %add_convert_fusion.15), channel_id=1, source_target_pairs={{0,16},{1,17},{2,18},{3,19},{4,20},{5,21},{6,22},{7,23},{8,24},{9,... | collective-permute-start | bytes 589832 | tf_op jit(solution)/shard_map/ppermute | solution.py:562
  121.7 4.0 %collective-permute-done.34 = bf16[1,64,1536]{2,1,0:T(8,128)(2,1)S(1)} collective-permute-done((bf16[1,64,1536]{2,1,0:T(8,128)(2,1)S(1)}, bf16[1,64,1536]{2,1,0:T(8,128)(2,1)S(1)}, u32[]{:S(2)}, u32[]{:S(2)}) %collective-permute-start.34) | collective-permute-done | bytes 196640 | tf_op jit(solution)/shard_map/ppermute | solution.py:562
  125.9 3.4 %collective-permute-start.37 = (bf16[2,16,1536]{2,1,0:T(8,128)(2,1)S(1)}, bf16[2,16,1536]{2,1,0:T(8,128)(2,1)S(1)}, u32[]{:S(2)}, u32[]{:S(2)}) collective-permute-start(bf16[2,16,1536]{2,1,0:T(8,128)(2,1)S(1)} %maximum_maximum_fusion.3), channel_id=1, source_target_pairs={{0,16},{1,17},{2,18},{3,19},{4,20},{5,21},{6,22},{7,23},{8,24},{9,... | collective-permute-start | bytes 294920 | tf_op jit(solution)/shard_map/ppermute | solution.py:562
  129.5 2.7 %collective-permute-done.38 = bf16[2,64,1536]{2,1,0:T(8,128)(2,1)S(1)} collective-permute-done((bf16[2,64,1536]{2,1,0:T(8,128)(2,1)S(1)}, bf16[2,64,1536]{2,1,0:T(8,128)(2,1)S(1)}, u32[]{:S(2)}, u32[]{:S(2)}) %collective-permute-start.38) | collective-permute-done | bytes 393248 | tf_op jit(solution)/shard_map/ppermute | solution.py:562
  136.2 2.1 %collective-permute-done.41 = bf16[2,16,1536]{2,1,0:T(8,128)(2,1)S(1)} collective-permute-done((bf16[2,16,1536]{2,1,0:T(8,128)(2,1)S(1)}, bf16[2,16,1536]{2,1,0:T(8,128)(2,1)S(1)}, u32[]{:S(2)}, u32[]{:S(2)}) %collective-permute-start.41) | collective-permute-done | bytes 98336 | tf_op jit(solution)/shard_map/ppermute | solution.py:562
  (172 shorter events, 59.2 us)
Async XLA Ops:
  8.3 10.3 %collective-permute-start.3 = (bf16[3,128,512]{2,1,0:T(8,128)(2,1)S(1)}, bf16[3,128,512]{2,1,0:T(8,128)(2,1)S(1)}, u32[]{:S(2)}, u32[]{:S(2)}) collective-permute-start(bf16[3,128,512]{2,1,0:T(8,128)(2,1)S(1)} %get-tuple-element.132), channel_id=1, source_target_pairs={{0,1},{1,0},{2,3},{3,2},{4,5},{5,4},{6,7},{7,6},{8,9},{9,8},{10,11... | collective-permute-start | bytes 1179656 | tf_op jit(solution)/shard_map/ppermute | solution.py:562
  9.7 9.7 %collective-permute-start.2 = (bf16[32,1536]{1,0:T(8,128)(2,1)S(1)}, bf16[32,1536]{1,0:T(8,128)(2,1)S(1)}, u32[]{:S(2)}, u32[]{:S(2)}) collective-permute-start(bf16[32,1536]{1,0:T(8,128)(2,1)S(1)} %get-tuple-element.299), channel_id=1, source_target_pairs={{0,16},{1,17},{2,18},{3,19},{4,20},{5,21},{6,22},{7,23},{8,24},{9,... | collective-permute-start | bytes 294920 | tf_op jit(solution)/shard_map/ppermute | solution.py:562
  12.4 8.6 %collective-permute-start.5 = (bf16[32,1536]{1,0:T(8,128)(2,1)S(1)}, bf16[32,1536]{1,0:T(8,128)(2,1)S(1)}, u32[]{:S(2)}, u32[]{:S(2)}) collective-permute-start(bf16[32,1536]{1,0:T(8,128)(2,1)S(1)} %get-tuple-element.293), channel_id=1, source_target_pairs={{0,4},{1,5},{2,6},{3,7},{4,0},{5,1},{6,2},{7,3},{8,12},{9,13},{10,... | collective-permute-start | bytes 294920 | tf_op jit(solution)/shard_map/ppermute | solution.py:562
  18.6 13.9 %collective-permute-start.9 = (bf16[3,128,512]{2,1,0:T(8,128)(2,1)S(1)}, bf16[3,128,512]{2,1,0:T(8,128)(2,1)S(1)}, u32[]{:S(2)}, u32[]{:S(2)}) collective-permute-start(bf16[3,128,512]{2,1,0:T(8,128)(2,1)S(1)} %get-tuple-element.138), channel_id=1, source_target_pairs={{0,1},{1,0},{2,3},{3,2},{4,5},{5,4},{6,7},{7,6},{8,9},{9,8},{10,11... | collective-permute-start | bytes 1179656 | tf_op jit(solution)/shard_map/ppermute | solution.py:562
  22.7 10.1 %collective-permute-start.8 = (bf16[3,128,512]{2,1,0:T(8,128)(2,1)S(1)}, bf16[3,128,512]{2,1,0:T(8,128)(2,1)S(1)}, u32[]{:S(2)}, u32[]{:S(2)}) collective-permute-start(bf16[3,128,512]{2,1,0:T(8,128)(2,1)S(1)} %collective-permute-done.3), channel_id=1, source_target_pairs={{0,4},{1,5},{2,6},{3,7},{4,0},{5,1},{6,2},{7,3},{8,12},{9,13},{10,... | collective-permute-start | bytes 1179656 | tf_op jit(solution)/shard_map/ppermute | solution.py:562
  27.3 9.1 %collective-permute-start.10 = (bf16[128,1536]{1,0:T(8,128)(2,1)S(1)}, bf16[128,1536]{1,0:T(8,128)(2,1)S(1)}, u32[]{:S(2)}, u32[]{:S(2)}) collective-permute-start(bf16[128,1536]{1,0:T(8,128)(2,1)S(1)} %get-tuple-element.286), channel_id=1, source_target_pairs={{0,1},{1,0},{2,3},{3,2},{4,5},{5,4},{6,7},{7,6},{8,9},{9,8},{10,11... | collective-permute-start | bytes 1179656 | tf_op jit(solution)/shard_map/ppermute | solution.py:562
  37.2 11.1 %collective-permute-start.14 = (bf16[3,128,512]{2,1,0:T(8,128)(2,1)S(1)}, bf16[3,128,512]{2,1,0:T(8,128)(2,1)S(1)}, u32[]{:S(2)}, u32[]{:S(2)}) collective-permute-start(bf16[3,128,512]{2,1,0:T(8,128)(2,1)S(1)} %collective-permute-done.9), channel_id=1, source_target_pairs={{0,4},{1,5},{2,6},{3,7},{4,0},{5,1},{6,2},{7,3},{8,12},{9,13},{10,... | collective-permute-start | bytes 1179656 | tf_op jit(solution)/shard_map/ppermute | solution.py:562
  64.2 11.6 %collective-permute-start.19 = (bf16[4,64,768]{2,1,0:T(8,128)(2,1)S(1)}, bf16[4,64,768]{2,1,0:T(8,128)(2,1)S(1)}, u32[]{:S(2)}, u32[]{:S(2)}) collective-permute-start(bf16[4,64,768]{2,1,0:T(8,128)(2,1)S(1)} %get-tuple-element.251), channel_id=1, source_target_pairs={{0,1},{1,0},{2,3},{3,2},{4,5},{5,4},{6,7},{7,6},{8,9},{9,8},{10,11... | collective-permute-start | bytes 1179656 | tf_op jit(solution)/shard_map/ppermute | solution.py:562
  65.0 11.2 %collective-permute-start.18 = (bf16[4,64,768]{2,1,0:T(8,128)(2,1)S(1)}, bf16[4,64,768]{2,1,0:T(8,128)(2,1)S(1)}, u32[]{:S(2)}, u32[]{:S(2)}) collective-permute-start(bf16[4,64,768]{2,1,0:T(8,128)(2,1)S(1)} %get-tuple-element.252), channel_id=1, source_target_pairs={{0,4},{1,5},{2,6},{3,7},{4,0},{5,1},{6,2},{7,3},{8,12},{9,13},{10,... | collective-permute-start | bytes 1179656 | tf_op jit(solution)/shard_map/ppermute | solution.py:562
  76.5 13.0 %collective-permute-start.25 = (bf16[2,64,768]{2,1,0:T(8,128)(2,1)S(1)}, bf16[2,64,768]{2,1,0:T(8,128)(2,1)S(1)}, u32[]{:S(2)}, u32[]{:S(2)}) collective-permute-start(bf16[2,64,768]{2,1,0:T(8,128)(2,1)S(1)} %get-tuple-element.266), channel_id=1, source_target_pairs={{0,4},{1,5},{2,6},{3,7},{4,0},{5,1},{6,2},{7,3},{8,12},{9,13},{10,... | collective-permute-start | bytes 589832 | tf_op jit(solution)/shard_map/ppermute | solution.py:562
  78.2 11.3 %collective-permute-start.24 = (bf16[2,64,768]{2,1,0:T(8,128)(2,1)S(1)}, bf16[2,64,768]{2,1,0:T(8,128)(2,1)S(1)}, u32[]{:S(2)}, u32[]{:S(2)}) collective-permute-start(bf16[2,64,768]{2,1,0:T(8,128)(2,1)S(1)} %get-tuple-element.268), channel_id=1, source_target_pairs={{0,1},{1,0},{2,3},{3,2},{4,5},{5,4},{6,7},{7,6},{8,9},{9,8},{10,11... | collective-permute-start | bytes 589832 | tf_op jit(solution)/shard_map/ppermute | solution.py:562
  80.4 13.2 %collective-permute-start.23 = (bf16[4,64,768]{2,1,0:T(8,128)(2,1)S(1)}, bf16[4,64,768]{2,1,0:T(8,128)(2,1)S(1)}, u32[]{:S(2)}, u32[]{:S(2)}) collective-permute-start(bf16[4,64,768]{2,1,0:T(8,128)(2,1)S(1)} %get-tuple-element.247.refs_15_), channel_id=1, source_target_pairs={{0,1},{1,0},{2,3},{3,2},{4,5},{5,4},{6,7},{7,6},{8,9},{9,8},{10,11... | collective-permute-start | bytes 1179656 | tf_op jit(solution)/shard_map/ppermute | solution.py:562
  81.7 11.9 %collective-permute-start.22 = (bf16[4,64,768]{2,1,0:T(8,128)(2,1)S(1)}, bf16[4,64,768]{2,1,0:T(8,128)(2,1)S(1)}, u32[]{:S(2)}, u32[]{:S(2)}) collective-permute-start(bf16[4,64,768]{2,1,0:T(8,128)(2,1)S(1)} %get-tuple-element.248.refs_14_), channel_id=1, source_target_pairs={{0,4},{1,5},{2,6},{3,7},{4,0},{5,1},{6,2},{7,3},{8,12},{9,13},{10,... | collective-permute-start | bytes 1179656 | tf_op jit(solution)/shard_map/ppermute | solution.py:562
  91.4 26.8 %collective-permute-start.36 = (bf16[8,16,1536]{2,1,0:T(8,128)(2,1)S(1)}, bf16[8,16,1536]{2,1,0:T(8,128)(2,1)S(1)}, u32[]{:S(2)}, u32[]{:S(2)}) collective-permute-start(bf16[8,16,1536]{2,1,0:T(8,128)(2,1)S(1)} %get-tuple-element.200.refs_8_), channel_id=1, source_target_pairs={{0,8},{1,9},{2,10},{3,11},{4,12},{5,13},{6,14},{7,15},{8,0},{9,1},... | collective-permute-start | bytes 1179656 | tf_op jit(solution)/shard_map/ppermute | solution.py:562
  96.0 13.7 %collective-permute-start.26 = (bf16[9,16,1536]{2,1,0:T(8,128)(2,1)S(1)}, bf16[9,16,1536]{2,1,0:T(8,128)(2,1)S(1)}, u32[]{:S(2)}, u32[]{:S(2)}) collective-permute-start(bf16[9,16,1536]{2,1,0:T(8,128)(2,1)S(1)} %maximum_maximum_fusion), channel_id=1, source_target_pairs={{0,1},{1,0},{2,3},{3,2},{4,5},{5,4},{6,7},{7,6},{8,9},{9,8},{10,11... | collective-permute-start | bytes 1327112 | tf_op jit(solution)/shard_map/ppermute | solution.py:562
  97.5 14.1 %collective-permute-start.32 = (bf16[1,64,1536]{2,1,0:T(8,128)(2,1)S(1)}, bf16[1,64,1536]{2,1,0:T(8,128)(2,1)S(1)}, u32[]{:S(2)}, u32[]{:S(2)}) collective-permute-start(bf16[1,64,1536]{2,1,0:T(8,128)(2,1)S(1)} %add_convert_fusion.20), channel_id=1, source_target_pairs={{0,16},{1,17},{2,18},{3,19},{4,20},{5,21},{6,22},{7,23},{8,24},{9,... | collective-permute-start | bytes 589832 | tf_op jit(solution)/shard_map/ppermute | solution.py:562
  102.5 11.8 %collective-permute-start.31 = (bf16[1,64,1536]{2,1,0:T(8,128)(2,1)S(1)}, bf16[1,64,1536]{2,1,0:T(8,128)(2,1)S(1)}, u32[]{:S(2)}, u32[]{:S(2)}) collective-permute-start(bf16[1,64,1536]{2,1,0:T(8,128)(2,1)S(1)} %pad_maximum_fusion.6), channel_id=1, source_target_pairs={{0,8},{1,9},{2,10},{3,11},{4,12},{5,13},{6,14},{7,15},{8,0},{9,1},... | collective-permute-start | bytes 589832 | tf_op jit(solution)/shard_map/ppermute | solution.py:562
  111.7 9.4 %collective-permute-start.35 = (bf16[1,64,1536]{2,1,0:T(8,128)(2,1)S(1)}, bf16[1,64,1536]{2,1,0:T(8,128)(2,1)S(1)}, u32[]{:S(2)}, u32[]{:S(2)}) collective-permute-start(bf16[1,64,1536]{2,1,0:T(8,128)(2,1)S(1)} %add_convert_fusion.16), channel_id=1, source_target_pairs={{0,8},{1,9},{2,10},{3,11},{4,12},{5,13},{6,14},{7,15},{8,0},{9,1},... | collective-permute-start | bytes 589832 | tf_op jit(solution)/shard_map/ppermute | solution.py:562
  114.4 11.3 %collective-permute-start.34 = (bf16[1,64,1536]{2,1,0:T(8,128)(2,1)S(1)}, bf16[1,64,1536]{2,1,0:T(8,128)(2,1)S(1)}, u32[]{:S(2)}, u32[]{:S(2)}) collective-permute-start(bf16[1,64,1536]{2,1,0:T(8,128)(2,1)S(1)} %add_convert_fusion.15), channel_id=1, source_target_pairs={{0,16},{1,17},{2,18},{3,19},{4,20},{5,21},{6,22},{7,23},{8,24},{9,... | collective-permute-start | bytes 589832 | tf_op jit(solution)/shard_map/ppermute | solution.py:562
  116.5 9.4 %collective-permute-start.33 = (bf16[3,16,1536]{2,1,0:T(8,128)(2,1)S(1)}, bf16[3,16,1536]{2,1,0:T(8,128)(2,1)S(1)}, u32[]{:S(2)}, u32[]{:S(2)}) collective-permute-start(bf16[3,16,1536]{2,1,0:T(8,128)(2,1)S(1)} %maximum_maximum_fusion.2), channel_id=1, source_target_pairs={{0,8},{1,9},{2,10},{3,11},{4,12},{5,13},{6,14},{7,15},{8,0},{9,1},... | collective-permute-start | bytes 442376 | tf_op jit(solution)/shard_map/ppermute | solution.py:562
  118.2 11.2 %collective-permute-start.39 = (bf16[4,16,1536]{2,1,0:T(8,128)(2,1)S(1)}, bf16[4,16,1536]{2,1,0:T(8,128)(2,1)S(1)}, u32[]{:S(2)}, u32[]{:S(2)}) collective-permute-start(bf16[4,16,1536]{2,1,0:T(8,128)(2,1)S(1)} %get-tuple-element.260), channel_id=1, source_target_pairs={{0,4},{1,5},{2,6},{3,7},{4,0},{5,1},{6,2},{7,3},{8,12},{9,13},{10,... | collective-permute-start | bytes 589832 | tf_op jit(solution)/shard_map/ppermute | solution.py:562
  121.1 11.1 %collective-permute-start.38 = (bf16[2,64,1536]{2,1,0:T(8,128)(2,1)S(1)}, bf16[2,64,1536]{2,1,0:T(8,128)(2,1)S(1)}, u32[]{:S(2)}, u32[]{:S(2)}) collective-permute-start(bf16[2,64,1536]{2,1,0:T(8,128)(2,1)S(1)} %pad_maximum_fusion.2), channel_id=1, source_target_pairs={{0,4},{1,5},{2,6},{3,7},{4,0},{5,1},{6,2},{7,3},{8,12},{9,13},{10,... | collective-permute-start | bytes 1179656 | tf_op jit(solution)/shard_map/ppermute | solution.py:562
  125.9 10.2 %collective-permute-start.37 = (bf16[2,16,1536]{2,1,0:T(8,128)(2,1)S(1)}, bf16[2,16,1536]{2,1,0:T(8,128)(2,1)S(1)}, u32[]{:S(2)}, u32[]{:S(2)}) collective-permute-start(bf16[2,16,1536]{2,1,0:T(8,128)(2,1)S(1)} %maximum_maximum_fusion.3), channel_id=1, source_target_pairs={{0,16},{1,17},{2,18},{3,19},{4,20},{5,21},{6,22},{7,23},{8,24},{9,... | collective-permute-start | bytes 294920 | tf_op jit(solution)/shard_map/ppermute | solution.py:562
  129.4 8.9 %collective-permute-start.41 = (bf16[2,16,1536]{2,1,0:T(8,128)(2,1)S(1)}, bf16[2,16,1536]{2,1,0:T(8,128)(2,1)S(1)}, u32[]{:S(2)}, u32[]{:S(2)}) collective-permute-start(bf16[2,16,1536]{2,1,0:T(8,128)(2,1)S(1)} %get-tuple-element.272), channel_id=1, source_target_pairs={{0,16},{1,17},{2,18},{3,19},{4,20},{5,21},{6,22},{7,23},{8,24},{9,... | collective-permute-start | bytes 294920 | tf_op jit(solution)/shard_map/ppermute | solution.py:562
  (34 other events, 315.0 us)

commit v17 on v11

--- a/solution.py
+++ b/solution.py
@@ -568,7 +568,7 @@
 
     attn_grain = max(16, width // devices)
     attn_count = width // attn_grain
-    ff_grain = max(16, width // dp_size)
+    ff_grain = max(16, 2 * width // dp_size)
     ff_count = width // ff_grain
     quarter_at = lax.rem(dp_at, 4)
     place = jnp.stack(
@@ -1015,6 +1015,8 @@
             done = finish(tie(ff_1.out["far"], token), far_masks, 1, place, shape, done)
             token = done[0]
             ended = True
+        if turn == 3:
+            token = attn_0.step(token)
         token = ff_0.step(token)
         if not done and "near" in ff_1.out:
             done = finish(tie(ff_1.out["near"], token), near_masks, 1, place, shape)

time: 153 us -> 147 us (0.961)
  starting transfers between devices: 55.6 us -> 52.2 us
  waiting for transfers between devices: 46.2 us -> 43.5 us
    ppermute x48 -> x46, starting transfers between devices: 55.6 us -> 52.2 us  [swap(): return lax.ppermute(array, axes, [(n, n ^ mask) for n in range(devices)])]
    ppermute x48 -> x46, waiting for transfers between devices: 46.2 us -> 43.5 us  [swap(): return lax.ppermute(array, axes, [(n, n ^ mask) for n in range(devices)])]
  transfers between devices with their start and end apart: 48 -> 46, of which waited for: 22 -> 21; matrix products, arithmetic and copies ran while one was open for 3% -> 3% of each run, Pallas kernels for 22% -> 23%
where the time goes in v17:
time: 147 us
  starting transfers between devices  52.2 us (36%)
  Pallas kernels  45.2 us (31%)
  waiting for transfers between devices  43.5 us (30%)
  other arithmetic  3.86 us (3%)
  between operations  1.6 us (1%)
    ppermute x46, starting transfers between devices, swap(): return lax.ppermute(array, axes, [(n, n ^ mask) for n in range(devices)])  52.2 us
    ppermute x46, waiting for transfers between devices, swap(): return lax.ppermute(array, axes, [(n, n ^ mask) for n in range(devices)])  43.5 us
    pallas_call x10, Pallas kernels, run(): pl.pallas_call(kernel, name=name, in_specs=[pl.BlockSpec(memory_space=in_...  38.4 us
    pallas_call x4, Pallas kernels, finish(): pl.pallas_call(kernel, name='layer_%d_ff_grads' % layer_idx, in_specs=[pl...  6.73 us
  transfers between devices with their start and end apart: 46, of which 21 were waited for; matrix products, arithmetic and copies ran while one was open for 3% of the time, Pallas kernels for 23%

profile of v17, /device:TPU:0, one launch (start us, length us, event | category | flops | bytes accessed | tf_op | source)
XLA Modules:
  0.0 146.8 jit_solution(18302638050381950821)
XLA Ops:
  2.6 3.0 %collective-permute-start.1 = (bf16[16,1536]{1,0:T(8,128)(2,1)S(1)}, bf16[16,1536]{1,0:T(8,128)(2,1)S(1)}, u32[]{:S(2)}, u32[]{:S(2)}) collective-permute-start(bf16[16,1536]{1,0:T(8,128)(2,1)S(1)} %get-tuple-element.124), channel_id=1, source_target_pairs={{0,1},{1,0},{2,3},{3,2},{4,5},{5,4},{6,7},{7,6},{8,9},{9,8},{10,11... | collective-permute-start | bytes 147464 | tf_op jit(solution)/shard_map/ppermute | solution.py:562
  5.6 2.6 %collective-permute-start = (bf16[16,1536]{1,0:T(8,128)(2,1)S(1)}, bf16[16,1536]{1,0:T(8,128)(2,1)S(1)}, u32[]{:S(2)}, u32[]{:S(2)}) collective-permute-start(bf16[16,1536]{1,0:T(8,128)(2,1)S(1)} %get-tuple-element.123), channel_id=1, source_target_pairs={{0,16},{1,17},{2,18},{3,19},{4,20},{5,21},{6,22},{7,23},{8,24},{9,... | collective-permute-start | bytes 147464 | tf_op jit(solution)/shard_map/ppermute | solution.py:562
  9.7 2.7 %collective-permute-start.2 = (bf16[32,1536]{1,0:T(8,128)(2,1)S(1)}, bf16[32,1536]{1,0:T(8,128)(2,1)S(1)}, u32[]{:S(2)}, u32[]{:S(2)}) collective-permute-start(bf16[32,1536]{1,0:T(8,128)(2,1)S(1)} %get-tuple-element.299), channel_id=1, source_target_pairs={{0,16},{1,17},{2,18},{3,19},{4,20},{5,21},{6,22},{7,23},{8,24},{9,... | collective-permute-start | bytes 294920 | tf_op jit(solution)/shard_map/ppermute | solution.py:562
  13.9 4.6 %collective-permute-done.3 = bf16[3,128,512]{2,1,0:T(8,128)(2,1)S(1)} collective-permute-done((bf16[3,128,512]{2,1,0:T(8,128)(2,1)S(1)}, bf16[3,128,512]{2,1,0:T(8,128)(2,1)S(1)}, u32[]{:S(2)}, u32[]{:S(2)}) %collective-permute-start.3) | collective-permute-done | bytes 393248 | tf_op jit(solution)/shard_map/ppermute | solution.py:562
  23.2 4.0 %collective-permute-done.4 = bf16[64,1536]{1,0:T(8,128)(2,1)S(1)} collective-permute-done((bf16[64,1536]{1,0:T(8,128)(2,1)S(1)}, bf16[64,1536]{1,0:T(8,128)(2,1)S(1)}, u32[]{:S(2)}, u32[]{:S(2)}) %collective-permute-start.4) | collective-permute-done | bytes 196640 | tf_op jit(solution)/shard_map/ppermute | solution.py:562
  30.3 2.1 %prepare.1 = (f32[512,512]{1,0:T(8,128)S(1)}, bf16[512,512]{1,0:T(8,128)(2,1)S(1)}, f32[64,384]{1,0:T(8,128)S(1)}, s32[512,128]{1,0:T(8,128)S(1)}, s32[512,128]{1,0:T(8,128)S(1)}, /*index=5*/s32[64,128]{1,0:T(8,128)S(1)}) custom-call(bf16[512,512]{1,0:T(8,128)(2,1)S(1)} %bitcast.57, s32[8,64]{1,0:T(8,128)S(1)} %copy-done.7, s32[8,64]{1,0:T(8,128)S(1)} %copy-done.8, ...), custom_call_target="tpu_custom_call" | custom-call | flops 3449999872 | tf_op jit(solution)/shard_map/prepare/pallas_call | solution.py:99
  32.8 3.6 %collective-permute-done.7 = bf16[128,1536]{1,0:T(8,128)(2,1)S(1)} collective-permute-done((bf16[128,1536]{1,0:T(8,128)(2,1)S(1)}, bf16[128,1536]{1,0:T(8,128)(2,1)S(1)}, u32[]{:S(2)}, u32[]{:S(2)}) %collective-permute-start.7) | collective-permute-done | bytes 393248 | tf_op jit(solution)/shard_map/ppermute | solution.py:562
  38.8 2.8 %layer_0_attention.1 = (bf16[512,1536]{1,0:T(8,128)(2,1)S(1)}, bf16[512,1152]{1,0:T(8,128)(2,1)S(1)}, f32[512,384]{1,0:T(8,128)S(1)}, bf16[512,384]{1,0:T(8,128)...) custom-call(s32[4]{0:T(128)S(1)} %pad_add_fusion.refs_0_.place_ref, ...), custom_call_target="tpu_custom_call" | custom-call | flops 11500000256 | tf_op jit(solution)/shard_map/layer_0_attention/pallas_call | solution.py:99
  41.8 3.2 %layer_0_ff.1 = (bf16[2,512,1024]{2,1,0:T(8,128)(2,1)S(1)}, bf16[2,512,512]{2,1,0:T(8,128)(2,1)S(1)}, f32[512,512]{1,0:T(8,128)S(1)}, bf16[512,512]{1,0:T(8,128)(2,1)S(1)}) custom-call(s32[4]{0:T(128)S(1)} %pad_add_fusion.refs_0_.place_ref, f32[512,512]{1,0:T(8,128)S(1)} %get-tuple-element.140.refs_1_.refs_4_, ...), custom_call_target="tpu_custom_call" | custom-call | flops 3449999872 | tf_op jit(solution)/shard_map/layer_0_ff/pallas_call | solution.py:99
  45.0 3.3 %collective-permute-done.14 = bf16[3,128,512]{2,1,0:T(8,128)(2,1)S(1)} collective-permute-done((bf16[3,128,512]{2,1,0:T(8,128)(2,1)S(1)}, bf16[3,128,512]{2,1,0:T(8,128)(2,1)S(1)}, u32[]{:S(2)}, u32[]{:S(2)}) %collective-permute-start.14) | collective-permute-done | bytes 393248 | tf_op jit(solution)/shard_map/ppermute | solution.py:562
  48.4 2.8 %layer_1_attention.1 = (bf16[512,1536]{1,0:T(8,128)(2,1)S(1)}, bf16[512,1152]{1,0:T(8,128)(2,1)S(1)}, f32[512,384]{1,0:T(8,128)S(1)}, bf16[512,384]{1,0:T(8,128)...) custom-call(s32[4]{0:T(128)S(1)} %pad_add_fusion.refs_0_.place_ref, ...), custom_call_target="tpu_custom_call" | custom-call | flops 115000000 | tf_op jit(solution)/shard_map/layer_1_attention/pallas_call | solution.py:99
  51.2 7.3 %layer_1_ff.1 = (bf16[16,64,768]{2,1,0:T(8,128)(2,1)S(1)}, bf16[16,64,768]{2,1,0:T(8,128)(2,1)S(1)}, f32[8,1536]{1,0:T(8,128)S(1)}, f32[512,512]{1,0:T(8,128)S(1...) custom-call(s32[4]{0:T(128)S(1)} %pad_add_fusion.refs_0_.place_ref, bf16[512,512]{1,0:T(8,128)(2,1)S(1)} %bitcast.58, ...), custom_call_target="tpu_custom_call" | custom-call | flops 9200000000 | tf_op jit(solution)/shard_map/layer_1_ff/pallas_call | solution.py:99
  59.1 4.6 %layer_1_attention_backward.1 = (bf16[16,16,1536]{2,1,0:T(8,128)(2,1)S(1)}, bf16[16,16,1536]{2,1,0:T(8,128)(2,1)S(1)}, f32[8,1536]{1,0:T(8,128)S(1)}, f32[512,512]{1,0:T(8,128)S(1)}, f32[64,384]{1,0:T(8,128)S(1)}) custom-call(s32[4]{0:T(128)S(1)} %pad_add_fusion.refs_0_.place_ref, f32[8,1536]{1,0:T(8,128)S(1)} %get-tuple-element.151.refs_1_, ...), custom_call_target="tpu_custom_call" | custom-call | flops 6899999744 | tf_op jit(solution)/shard_map/layer_1_attention_backward/pallas_call | solution.py:99
  66.9 7.1 %layer_0_ff_backward.1 = (bf16[16,64,768]{2,1,0:T(8,128)(2,1)S(1)}, bf16[16,64,768]{2,1,0:T(8,128)(2,1)S(1)}, f32[8,1536]{1,0:T(8,128)S(1)}, f32[512,512]{1,0:T(8,128)S(1)}, bf16[512,512]{1,0:T(8,128)(2,1)S(1)}) custom-call(s32[4]{0:T(128)S(1)} %pad_add_fusion.refs_0_.place_ref, f32[512,512]{1,0:T(8,128)S(1)} %get-tuple-element.161.refs_1_, ...), custom_call_target="tpu_custom_call" | custom-call | flops 9200000000 | tf_op jit(solution)/shard_map/layer_0_ff_backward/pallas_call | solution.py:99
  83.3 6.1 %layer_0_attention_backward.1 = (bf16[16,16,1536]{2,1,0:T(8,128)(2,1)S(1)}, bf16[17,16,1536]{2,1,0:T(8,128)(2,1)S(1)}, f32[8,1536]{1,0:T(8,128)S(1)}, f32[512,512]{1,0:T(8,128)}) custom-call(s32[4]{0:T(128)S(1)} %pad_add_fusion.refs_0_.place_ref, f32[64,384]{1,0:T(8,128)S(1)} %get-tuple-element.158.refs_1_, s32[512,128]{1,0:T(8,128)S(1)} %get-tuple-element.159.refs_2_, ...), custom_call_target="tpu_custom_call" | custom-call | flops 8049999872 | tf_op jit(solution)/shard_map/layer_0_attention_backward/pallas_call | solution.py:99
  97.5 2.2 %collective-permute-start.28 = (bf16[1,64,1536]{2,1,0:T(8,128)(2,1)S(1)}, bf16[1,64,1536]{2,1,0:T(8,128)(2,1)S(1)}, u32[]{:S(2)}, u32[]{:S(2)}) collective-permute-start(bf16[1,64,1536]{2,1,0:T(8,128)(2,1)S(1)} %add_convert_fusion.21), channel_id=1, source_target_pairs={{0,16},{1,17},{2,18},{3,19},{4,20},{5,21},{6,22},{7,23},{8,24},{9,... | collective-permute-start | bytes 589832 | tf_op jit(solution)/shard_map/ppermute | solution.py:562
  100.0 2.4 %collective-permute-done.29 = bf16[2,64,768]{2,1,0:T(8,128)(2,1)S(1)} collective-permute-done((bf16[2,64,768]{2,1,0:T(8,128)(2,1)S(1)}, bf16[2,64,768]{2,1,0:T(8,128)(2,1)S(1)}, u32[]{:S(2)}, u32[]{:S(2)}) %collective-permute-start.29) | collective-permute-done | bytes 196640 | tf_op jit(solution)/shard_map/ppermute | solution.py:562
  104.2 5.0 %collective-permute-done.28 = bf16[1,64,1536]{2,1,0:T(8,128)(2,1)S(1)} collective-permute-done((bf16[1,64,1536]{2,1,0:T(8,128)(2,1)S(1)}, bf16[1,64,1536]{2,1,0:T(8,128)(2,1)S(1)}, u32[]{:S(2)}, u32[]{:S(2)}) %collective-permute-start.28) | collective-permute-done | bytes 196640 | tf_op jit(solution)/shard_map/ppermute | solution.py:562
  109.3 2.9 %collective-permute-start.35 = (bf16[1,64,1536]{2,1,0:T(8,128)(2,1)S(1)}, bf16[1,64,1536]{2,1,0:T(8,128)(2,1)S(1)}, u32[]{:S(2)}, u32[]{:S(2)}) collective-permute-start(bf16[1,64,1536]{2,1,0:T(8,128)(2,1)S(1)} %add_convert_fusion.18), channel_id=1, source_target_pairs={{0,8},{1,9},{2,10},{3,11},{4,12},{5,13},{6,14},{7,15},{8,0},{9,1},... | collective-permute-start | bytes 589832 | tf_op jit(solution)/shard_map/ppermute | solution.py:562
  114.4 1.9 %collective-permute-start.34 = (bf16[1,64,1536]{2,1,0:T(8,128)(2,1)S(1)}, bf16[1,64,1536]{2,1,0:T(8,128)(2,1)S(1)}, u32[]{:S(2)}, u32[]{:S(2)}) collective-permute-start(bf16[1,64,1536]{2,1,0:T(8,128)(2,1)S(1)} %add_convert_fusion.15), channel_id=1, source_target_pairs={{0,16},{1,17},{2,18},{3,19},{4,20},{5,21},{6,22},{7,23},{8,24},{9,... | collective-permute-start | bytes 589832 | tf_op jit(solution)/shard_map/ppermute | solution.py:562
  116.3 2.9 %collective-permute-done.31 = bf16[5,16,1536]{2,1,0:T(8,128)(2,1)S(1)} collective-permute-done((bf16[5,16,1536]{2,1,0:T(8,128)(2,1)S(1)}, bf16[5,16,1536]{2,1,0:T(8,128)(2,1)S(1)}, u32[]{:S(2)}, u32[]{:S(2)}) %collective-permute-start.31) | collective-permute-done | bytes 245792 | tf_op jit(solution)/shard_map/ppermute | solution.py:562
  122.0 3.8 %collective-permute-done.34 = bf16[1,64,1536]{2,1,0:T(8,128)(2,1)S(1)} collective-permute-done((bf16[1,64,1536]{2,1,0:T(8,128)(2,1)S(1)}, bf16[1,64,1536]{2,1,0:T(8,128)(2,1)S(1)}, u32[]{:S(2)}, u32[]{:S(2)}) %collective-permute-start.34) | collective-permute-done | bytes 196640 | tf_op jit(solution)/shard_map/ppermute | solution.py:562
  126.6 2.9 %collective-permute-start.37 = (bf16[2,16,1536]{2,1,0:T(8,128)(2,1)S(1)}, bf16[2,16,1536]{2,1,0:T(8,128)(2,1)S(1)}, u32[]{:S(2)}, u32[]{:S(2)}) collective-permute-start(bf16[2,16,1536]{2,1,0:T(8,128)(2,1)S(1)} %maximum_maximum_fusion.3), channel_id=1, source_target_pairs={{0,16},{1,17},{2,18},{3,19},{4,20},{5,21},{6,22},{7,23},{8,24},{9,... | collective-permute-start | bytes 294920 | tf_op jit(solution)/shard_map/ppermute | solution.py:562
  130.2 3.0 %collective-permute-done.38 = bf16[2,64,1536]{2,1,0:T(8,128)(2,1)S(1)} collective-permute-done((bf16[2,64,1536]{2,1,0:T(8,128)(2,1)S(1)}, bf16[2,64,1536]{2,1,0:T(8,128)(2,1)S(1)}, u32[]{:S(2)}, u32[]{:S(2)}) %collective-permute-start.38) | collective-permute-done | bytes 393248 | tf_op jit(solution)/shard_map/ppermute | solution.py:562
  (172 shorter events, 58.4 us)
Async XLA Ops:
  8.3 10.3 %collective-permute-start.3 = (bf16[3,128,512]{2,1,0:T(8,128)(2,1)S(1)}, bf16[3,128,512]{2,1,0:T(8,128)(2,1)S(1)}, u32[]{:S(2)}, u32[]{:S(2)}) collective-permute-start(bf16[3,128,512]{2,1,0:T(8,128)(2,1)S(1)} %get-tuple-element.132), channel_id=1, source_target_pairs={{0,1},{1,0},{2,3},{3,2},{4,5},{5,4},{6,7},{7,6},{8,9},{9,8},{10,11... | collective-permute-start | bytes 1179656 | tf_op jit(solution)/shard_map/ppermute | solution.py:562
  9.7 9.7 %collective-permute-start.2 = (bf16[32,1536]{1,0:T(8,128)(2,1)S(1)}, bf16[32,1536]{1,0:T(8,128)(2,1)S(1)}, u32[]{:S(2)}, u32[]{:S(2)}) collective-permute-start(bf16[32,1536]{1,0:T(8,128)(2,1)S(1)} %get-tuple-element.299), channel_id=1, source_target_pairs={{0,16},{1,17},{2,18},{3,19},{4,20},{5,21},{6,22},{7,23},{8,24},{9,... | collective-permute-start | bytes 294920 | tf_op jit(solution)/shard_map/ppermute | solution.py:562
  12.4 8.6 %collective-permute-start.5 = (bf16[32,1536]{1,0:T(8,128)(2,1)S(1)}, bf16[32,1536]{1,0:T(8,128)(2,1)S(1)}, u32[]{:S(2)}, u32[]{:S(2)}) collective-permute-start(bf16[32,1536]{1,0:T(8,128)(2,1)S(1)} %get-tuple-element.293), channel_id=1, source_target_pairs={{0,4},{1,5},{2,6},{3,7},{4,0},{5,1},{6,2},{7,3},{8,12},{9,13},{10,... | collective-permute-start | bytes 294920 | tf_op jit(solution)/shard_map/ppermute | solution.py:562
  18.6 13.9 %collective-permute-start.9 = (bf16[3,128,512]{2,1,0:T(8,128)(2,1)S(1)}, bf16[3,128,512]{2,1,0:T(8,128)(2,1)S(1)}, u32[]{:S(2)}, u32[]{:S(2)}) collective-permute-start(bf16[3,128,512]{2,1,0:T(8,128)(2,1)S(1)} %get-tuple-element.138), channel_id=1, source_target_pairs={{0,1},{1,0},{2,3},{3,2},{4,5},{5,4},{6,7},{7,6},{8,9},{9,8},{10,11... | collective-permute-start | bytes 1179656 | tf_op jit(solution)/shard_map/ppermute | solution.py:562
  22.7 10.1 %collective-permute-start.8 = (bf16[3,128,512]{2,1,0:T(8,128)(2,1)S(1)}, bf16[3,128,512]{2,1,0:T(8,128)(2,1)S(1)}, u32[]{:S(2)}, u32[]{:S(2)}) collective-permute-start(bf16[3,128,512]{2,1,0:T(8,128)(2,1)S(1)} %collective-permute-done.3), channel_id=1, source_target_pairs={{0,4},{1,5},{2,6},{3,7},{4,0},{5,1},{6,2},{7,3},{8,12},{9,13},{10,... | collective-permute-start | bytes 1179656 | tf_op jit(solution)/shard_map/ppermute | solution.py:562
  27.3 9.1 %collective-permute-start.10 = (bf16[128,1536]{1,0:T(8,128)(2,1)S(1)}, bf16[128,1536]{1,0:T(8,128)(2,1)S(1)}, u32[]{:S(2)}, u32[]{:S(2)}) collective-permute-start(bf16[128,1536]{1,0:T(8,128)(2,1)S(1)} %get-tuple-element.286), channel_id=1, source_target_pairs={{0,1},{1,0},{2,3},{3,2},{4,5},{5,4},{6,7},{7,6},{8,9},{9,8},{10,11... | collective-permute-start | bytes 1179656 | tf_op jit(solution)/shard_map/ppermute | solution.py:562
  37.2 11.1 %collective-permute-start.14 = (bf16[3,128,512]{2,1,0:T(8,128)(2,1)S(1)}, bf16[3,128,512]{2,1,0:T(8,128)(2,1)S(1)}, u32[]{:S(2)}, u32[]{:S(2)}) collective-permute-start(bf16[3,128,512]{2,1,0:T(8,128)(2,1)S(1)} %collective-permute-done.9), channel_id=1, source_target_pairs={{0,4},{1,5},{2,6},{3,7},{4,0},{5,1},{6,2},{7,3},{8,12},{9,13},{10,... | collective-permute-start | bytes 1179656 | tf_op jit(solution)/shard_map/ppermute | solution.py:562
  64.2 11.6 %collective-permute-start.19 = (bf16[4,64,768]{2,1,0:T(8,128)(2,1)S(1)}, bf16[4,64,768]{2,1,0:T(8,128)(2,1)S(1)}, u32[]{:S(2)}, u32[]{:S(2)}) collective-permute-start(bf16[4,64,768]{2,1,0:T(8,128)(2,1)S(1)} %get-tuple-element.251), channel_id=1, source_target_pairs={{0,1},{1,0},{2,3},{3,2},{4,5},{5,4},{6,7},{7,6},{8,9},{9,8},{10,11... | collective-permute-start | bytes 1179656 | tf_op jit(solution)/shard_map/ppermute | solution.py:562
  65.0 11.2 %collective-permute-start.18 = (bf16[4,64,768]{2,1,0:T(8,128)(2,1)S(1)}, bf16[4,64,768]{2,1,0:T(8,128)(2,1)S(1)}, u32[]{:S(2)}, u32[]{:S(2)}) collective-permute-start(bf16[4,64,768]{2,1,0:T(8,128)(2,1)S(1)} %get-tuple-element.252), channel_id=1, source_target_pairs={{0,4},{1,5},{2,6},{3,7},{4,0},{5,1},{6,2},{7,3},{8,12},{9,13},{10,... | collective-permute-start | bytes 1179656 | tf_op jit(solution)/shard_map/ppermute | solution.py:562
  76.5 13.0 %collective-permute-start.25 = (bf16[2,64,768]{2,1,0:T(8,128)(2,1)S(1)}, bf16[2,64,768]{2,1,0:T(8,128)(2,1)S(1)}, u32[]{:S(2)}, u32[]{:S(2)}) collective-permute-start(bf16[2,64,768]{2,1,0:T(8,128)(2,1)S(1)} %get-tuple-element.266), channel_id=1, source_target_pairs={{0,4},{1,5},{2,6},{3,7},{4,0},{5,1},{6,2},{7,3},{8,12},{9,13},{10,... | collective-permute-start | bytes 589832 | tf_op jit(solution)/shard_map/ppermute | solution.py:562
  78.2 11.3 %collective-permute-start.24 = (bf16[2,64,768]{2,1,0:T(8,128)(2,1)S(1)}, bf16[2,64,768]{2,1,0:T(8,128)(2,1)S(1)}, u32[]{:S(2)}, u32[]{:S(2)}) collective-permute-start(bf16[2,64,768]{2,1,0:T(8,128)(2,1)S(1)} %get-tuple-element.268), channel_id=1, source_target_pairs={{0,1},{1,0},{2,3},{3,2},{4,5},{5,4},{6,7},{7,6},{8,9},{9,8},{10,11... | collective-permute-start | bytes 589832 | tf_op jit(solution)/shard_map/ppermute | solution.py:562
  80.4 13.2 %collective-permute-start.23 = (bf16[4,64,768]{2,1,0:T(8,128)(2,1)S(1)}, bf16[4,64,768]{2,1,0:T(8,128)(2,1)S(1)}, u32[]{:S(2)}, u32[]{:S(2)}) collective-permute-start(bf16[4,64,768]{2,1,0:T(8,128)(2,1)S(1)} %get-tuple-element.247.refs_15_), channel_id=1, source_target_pairs={{0,1},{1,0},{2,3},{3,2},{4,5},{5,4},{6,7},{7,6},{8,9},{9,8},{10,11... | collective-permute-start | bytes 1179656 | tf_op jit(solution)/shard_map/ppermute | solution.py:562
  81.7 11.9 %collective-permute-start.22 = (bf16[4,64,768]{2,1,0:T(8,128)(2,1)S(1)}, bf16[4,64,768]{2,1,0:T(8,128)(2,1)S(1)}, u32[]{:S(2)}, u32[]{:S(2)}) collective-permute-start(bf16[4,64,768]{2,1,0:T(8,128)(2,1)S(1)} %get-tuple-element.248.refs_14_), channel_id=1, source_target_pairs={{0,4},{1,5},{2,6},{3,7},{4,0},{5,1},{6,2},{7,3},{8,12},{9,13},{10,... | collective-permute-start | bytes 1179656 | tf_op jit(solution)/shard_map/ppermute | solution.py:562
  91.4 28.4 %collective-permute-start.36 = (bf16[8,16,1536]{2,1,0:T(8,128)(2,1)S(1)}, bf16[8,16,1536]{2,1,0:T(8,128)(2,1)S(1)}, u32[]{:S(2)}, u32[]{:S(2)}) collective-permute-start(bf16[8,16,1536]{2,1,0:T(8,128)(2,1)S(1)} %get-tuple-element.200.refs_8_), channel_id=1, source_target_pairs={{0,8},{1,9},{2,10},{3,11},{4,12},{5,13},{6,14},{7,15},{8,0},{9,1},... | collective-permute-start | bytes 1179656 | tf_op jit(solution)/shard_map/ppermute | solution.py:562
  96.0 16.1 %collective-permute-start.26 = (bf16[9,16,1536]{2,1,0:T(8,128)(2,1)S(1)}, bf16[9,16,1536]{2,1,0:T(8,128)(2,1)S(1)}, u32[]{:S(2)}, u32[]{:S(2)}) collective-permute-start(bf16[9,16,1536]{2,1,0:T(8,128)(2,1)S(1)} %maximum_maximum_fusion), channel_id=1, source_target_pairs={{0,1},{1,0},{2,3},{3,2},{4,5},{5,4},{6,7},{7,6},{8,9},{9,8},{10,11... | collective-permute-start | bytes 1327112 | tf_op jit(solution)/shard_map/ppermute | solution.py:562
  97.5 11.7 %collective-permute-start.28 = (bf16[1,64,1536]{2,1,0:T(8,128)(2,1)S(1)}, bf16[1,64,1536]{2,1,0:T(8,128)(2,1)S(1)}, u32[]{:S(2)}, u32[]{:S(2)}) collective-permute-start(bf16[1,64,1536]{2,1,0:T(8,128)(2,1)S(1)} %add_convert_fusion.21), channel_id=1, source_target_pairs={{0,16},{1,17},{2,18},{3,19},{4,20},{5,21},{6,22},{7,23},{8,24},{9,... | collective-permute-start | bytes 589832 | tf_op jit(solution)/shard_map/ppermute | solution.py:562
  102.5 11.8 %collective-permute-start.32 = (bf16[1,64,1536]{2,1,0:T(8,128)(2,1)S(1)}, bf16[1,64,1536]{2,1,0:T(8,128)(2,1)S(1)}, u32[]{:S(2)}, u32[]{:S(2)}) collective-permute-start(bf16[1,64,1536]{2,1,0:T(8,128)(2,1)S(1)} %pad_maximum_fusion.6), channel_id=1, source_target_pairs={{0,8},{1,9},{2,10},{3,11},{4,12},{5,13},{6,14},{7,15},{8,0},{9,1},... | collective-permute-start | bytes 589832 | tf_op jit(solution)/shard_map/ppermute | solution.py:562
  109.3 11.4 %collective-permute-start.35 = (bf16[1,64,1536]{2,1,0:T(8,128)(2,1)S(1)}, bf16[1,64,1536]{2,1,0:T(8,128)(2,1)S(1)}, u32[]{:S(2)}, u32[]{:S(2)}) collective-permute-start(bf16[1,64,1536]{2,1,0:T(8,128)(2,1)S(1)} %add_convert_fusion.18), channel_id=1, source_target_pairs={{0,8},{1,9},{2,10},{3,11},{4,12},{5,13},{6,14},{7,15},{8,0},{9,1},... | collective-permute-start | bytes 589832 | tf_op jit(solution)/shard_map/ppermute | solution.py:562
  114.4 11.4 %collective-permute-start.34 = (bf16[1,64,1536]{2,1,0:T(8,128)(2,1)S(1)}, bf16[1,64,1536]{2,1,0:T(8,128)(2,1)S(1)}, u32[]{:S(2)}, u32[]{:S(2)}) collective-permute-start(bf16[1,64,1536]{2,1,0:T(8,128)(2,1)S(1)} %add_convert_fusion.15), channel_id=1, source_target_pairs={{0,16},{1,17},{2,18},{3,19},{4,20},{5,21},{6,22},{7,23},{8,24},{9,... | collective-permute-start | bytes 589832 | tf_op jit(solution)/shard_map/ppermute | solution.py:562
  119.8 9.7 %collective-permute-start.39 = (bf16[4,16,1536]{2,1,0:T(8,128)(2,1)S(1)}, bf16[4,16,1536]{2,1,0:T(8,128)(2,1)S(1)}, u32[]{:S(2)}, u32[]{:S(2)}) collective-permute-start(bf16[4,16,1536]{2,1,0:T(8,128)(2,1)S(1)} %get-tuple-element.260), channel_id=1, source_target_pairs={{0,4},{1,5},{2,6},{3,7},{4,0},{5,1},{6,2},{7,3},{8,12},{9,13},{10,... | collective-permute-start | bytes 589832 | tf_op jit(solution)/shard_map/ppermute | solution.py:562
  120.7 12.5 %collective-permute-start.38 = (bf16[2,64,1536]{2,1,0:T(8,128)(2,1)S(1)}, bf16[2,64,1536]{2,1,0:T(8,128)(2,1)S(1)}, u32[]{:S(2)}, u32[]{:S(2)}) collective-permute-start(bf16[2,64,1536]{2,1,0:T(8,128)(2,1)S(1)} %pad_maximum_fusion.2), channel_id=1, source_target_pairs={{0,4},{1,5},{2,6},{3,7},{4,0},{5,1},{6,2},{7,3},{8,12},{9,13},{10,... | collective-permute-start | bytes 1179656 | tf_op jit(solution)/shard_map/ppermute | solution.py:562
  126.6 10.5 %collective-permute-start.37 = (bf16[2,16,1536]{2,1,0:T(8,128)(2,1)S(1)}, bf16[2,16,1536]{2,1,0:T(8,128)(2,1)S(1)}, u32[]{:S(2)}, u32[]{:S(2)}) collective-permute-start(bf16[2,16,1536]{2,1,0:T(8,128)(2,1)S(1)} %maximum_maximum_fusion.3), channel_id=1, source_target_pairs={{0,16},{1,17},{2,18},{3,19},{4,20},{5,21},{6,22},{7,23},{8,24},{9,... | collective-permute-start | bytes 294920 | tf_op jit(solution)/shard_map/ppermute | solution.py:562
  129.6 8.6 %collective-permute-start.41 = (bf16[2,16,1536]{2,1,0:T(8,128)(2,1)S(1)}, bf16[2,16,1536]{2,1,0:T(8,128)(2,1)S(1)}, u32[]{:S(2)}, u32[]{:S(2)}) collective-permute-start(bf16[2,16,1536]{2,1,0:T(8,128)(2,1)S(1)} %get-tuple-element.272), channel_id=1, source_target_pairs={{0,16},{1,17},{2,18},{3,19},{4,20},{5,21},{6,22},{7,23},{8,24},{9,... | collective-permute-start | bytes 294920 | tf_op jit(solution)/shard_map/ppermute | solution.py:562
  133.4 9.0 %collective-permute-start.43 = (bf16[2,64,1536]{2,1,0:T(8,128)(2,1)S(1)}, bf16[2,64,1536]{2,1,0:T(8,128)(2,1)S(1)}, u32[]{:S(2)}, u32[]{:S(2)}) collective-permute-start(bf16[2,64,1536]{2,1,0:T(8,128)(2,1)S(1)} %pad_maximum_fusion.3), channel_id=1, source_target_pairs={{0,4},{1,5},{2,6},{3,7},{4,0},{5,1},{6,2},{7,3},{8,12},{9,13},{10,... | collective-permute-start | bytes 1179656 | tf_op jit(solution)/shard_map/ppermute | solution.py:562
  (34 other events, 314.6 us)
